TPU v7x, 32 devices: a whole 2x2x4 slice. The times are simulated.
32 devices in a mesh: dp: 4 (over y, core), fsdp: 8 (over z, x).
Axes of the slice: x: 2, y: 2, z: 4, core: 2. Of those that a mesh axis runs over, the one named last changes fastest.
Arguments:
- layer_input: bfloat16 [8192, 4096], P(('dp', 'fsdp')), may hold values from -6 to 6
- query_states: bfloat16 [8192, 2048], P(('dp', 'fsdp')), may hold values from -120 to 120
- key_states: bfloat16 [8192, 512], P(('dp', 'fsdp')), may hold values from -6 to 6
- output_grad: bfloat16 [8192, 2048], P(('dp', 'fsdp')), may hold values from -0.0625 to 0.0625
- document_ids: int32 [8192], P(('dp', 'fsdp')), may hold values from 0 to 255, as said below
- weight_index: int32 [8192], P(('dp', 'fsdp')), may hold values from 0 to 15, as said below
- loss_weights: float32 [16], replicated, may hold values from 0.25 to 4
- scale_exponent: int32 [32], P(('dp', 'fsdp')), may hold values from 0 to 3
- swap_start: int32 [32, 2], P(('dp', 'fsdp')), may hold values from 128 to 224, as said below
- swap_rows: int32 [32, 2], P(('dp', 'fsdp')), may hold values from 16 to 32, as said below
Outputs:
- grad_value: float32 [4096, 512], P('fsdp')
- value_grad: bfloat16 [8192, 512], P(('dp', 'fsdp'))
Inputs may be any that keep to these rules, and one draw needn't show every extreme that they name: `document_ids`: each row holds the index, within its device's 256 rows, of its document's first row; a document lies inside one device, either within its first 128 rows or within one of its last 8 aligned blocks of 16 rows. `weight_index`: equal on all rows of a document. `swap_start`: 128 plus a multiple of 16. `swap_rows`: 16 or 32; equal on the two devices whose dp indices differ in bit level.
All inputs are finite; a program needn't handle non-finite values.
Results may differ from a plain program's by a relative error of at most 0.0065.
Values may be sent and summed in bfloat16 or wider, within the bound.
No kernel may reach another device: no remote copies, remote signals or barrier semaphores. Data moves between devices by JAX's collectives and lax.ppermute only.
A program may use at most 64 MiB of HBM per device.

v0:
```python
import jax
import jax.numpy as jnp
from jax import lax
from jax.sharding import PartitionSpec as P

D = 4096
HD = 128
CAP = 32


def swapped(block, axis, distance):
    count = lax.axis_size(axis)
    route = []
    for low in range(count):
        high = low | 1 << distance
        if high != low and high < count:
            route += [(low, high), (high, low)]
    return lax.ppermute(block, axis, route)


def cut_rows(item, offset):
    return lax.dynamic_slice_in_dim(item, offset, CAP, 0)


def blend_rows(item, incoming, offset, extent):
    inside = jnp.arange(CAP) < extent
    shaped = inside.reshape((CAP,) + (1,) * (item.ndim - 1))
    chosen = jnp.where(shaped, incoming, lax.dynamic_slice_in_dim(item, offset, CAP, 0))
    return lax.dynamic_update_slice_in_dim(item, chosen, offset, 0)


def attend(query_rows, key_rows, grad_rows, doc_rows):
    tokens = query_rows.shape[0]
    groups = key_rows.shape[1] // HD
    per_group = query_rows.shape[1] // HD // groups
    q_four = query_rows.reshape(tokens, groups, per_group, HD)
    k_three = key_rows.reshape(tokens, groups, HD)
    scores = jnp.einsum(
        "ignd,jgd->gnij", q_four, k_three, preferred_element_type=jnp.float32
    ) * HD ** (-0.5)
    positions = jnp.arange(tokens)
    allowed = (doc_rows[:, None] == doc_rows[None, :]) & (positions[None, :] <= positions[:, None])
    scores = jnp.where(allowed, scores, -1e30)
    highest = jnp.max(scores, axis=-1, keepdims=True)
    expo = jnp.exp(scores - highest)
    probs = (expo / jnp.sum(expo, axis=-1, keepdims=True)).astype(jnp.bfloat16)
    g_four = grad_rows.reshape(tokens, groups, per_group, HD)
    values = jnp.einsum("gnij,ignd->jgd", probs, g_four, preferred_element_type=jnp.float32)
    return values.reshape(tokens, groups * HD).astype(jnp.bfloat16)


def on_device(
    layer_input,
    query_states,
    key_states,
    output_grad,
    document_ids,
    weight_index,
    loss_weights,
    scale_exponent,
    swap_start,
    swap_rows,
):
    onehot = (weight_index[:, None] == jnp.arange(loss_weights.shape[0])[None, :]).astype(
        jnp.float32
    )
    unscale = jnp.exp2(-scale_exponent[0].astype(jnp.float32))
    factor = jnp.sum(onehot * loss_weights[None, :], axis=1) * unscale
    weighted = (output_grad.astype(jnp.float32) * factor[:, None]).astype(jnp.bfloat16)
    rounds = lax.axis_size("dp").bit_length() - 1
    tokens = layer_input.shape[0]
    device = lax.axis_index("dp") * lax.axis_size("fsdp") + lax.axis_index("fsdp")
    query_rows = query_states
    key_rows = key_states
    grad_rows = weighted
    doc_rows = document_ids + device * tokens
    input_rows = layer_input
    for level in range(rounds):
        offset = swap_start[0, level]
        extent = swap_rows[0, level]
        arrived = swapped(
            (
                cut_rows(query_rows, offset),
                cut_rows(key_rows, offset),
                cut_rows(grad_rows, offset),
                cut_rows(doc_rows, offset),
                cut_rows(input_rows, offset),
            ),
            "dp",
            level,
        )
        query_rows = blend_rows(query_rows, arrived[0], offset, extent)
        key_rows = blend_rows(key_rows, arrived[1], offset, extent)
        grad_rows = blend_rows(grad_rows, arrived[2], offset, extent)
        doc_rows = blend_rows(doc_rows, arrived[3], offset, extent)
        input_rows = blend_rows(input_rows, arrived[4], offset, extent)
    values_grad = attend(query_rows, key_rows, grad_rows, doc_rows)
    owners = lax.axis_size("fsdp")
    owned = (D + owners - 1) // owners
    padded = jnp.pad(input_rows, ((0, 0), (0, owned * owners - D)))
    arranged = lax.all_to_all(
        padded.reshape(tokens, owners, owned), "fsdp", split_axis=1, concat_axis=0, tiled=True
    )
    feature_rows = arranged.reshape(-1, owned)
    owned_block = lax.dot_general(
        feature_rows,
        lax.all_gather(values_grad, "fsdp", axis=0, tiled=True),
        (((0,), (0,)), ((), ())),
        preferred_element_type=jnp.float32,
    )
    return (lax.psum(owned_block, "dp"), values_grad)


def solution(mesh):
    return jax.shard_map(
        on_device,
        mesh=mesh,
        in_specs=(
            P(("dp", "fsdp"), None),
            P(("dp", "fsdp"), None),
            P(("dp", "fsdp"), None),
            P(("dp", "fsdp"), None),
            P(("dp", "fsdp")),
            P(("dp", "fsdp")),
            P(),
            P(("dp", "fsdp")),
            P(("dp", "fsdp"), None),
            P(("dp", "fsdp"), None),
        ),
        out_specs=(P("fsdp", None), P(("dp", "fsdp"), None)),
        check_vma=False,
    )
```

profile of v0, /device:TPU:0, one launch (start us, length us, event | category | flops | bytes accessed | tf_op | source)
XLA Modules:
  0.0 213.5 jit_solution(12625540188040302319)
XLA Ops:
  7.2 1.3 copy.78
  8.6 0.6 fusion.15
  12.3 0.5 collective-permute-start.2
  12.8 0.7 constant_dynamic-slice_fusion.1
  13.5 0.6 constant_dynamic-slice_fusion.3
  14.6 0.6 dynamic_slice.44
  15.3 4.1 %copy.45 = bf16[256,4096]{0,1:T(8,128)(2,1)} copy(bf16[256,4096]{1,0:T(8,128)(2,1)} %param.10) | data formatting | bytes 4194304 | tf_op args[0]
  19.4 1.6 constant_dynamic-slice_fusion.7
  21.0 1.0 copy.43
  22.5 0.6 fusion.14
  23.1 0.6 iota_compare_fusion.3
  25.8 0.8 select_dynamic-update-slice_fusion.1
  26.7 2.5 %collective-permute-start.5 = (s32[32]{0:T(128)S(1)}, s32[32]{0:T(128)S(1)}, u32[]{:S(2)}, u32[]{:S(2)}) collective-permute-start(s32[32]{0:T(128)S(1)} %dynamic_slice.45), channel_id=1, source_target_pairs={{0,16},{16,0},{8,24},{24,8},{1,17},{17,1},{9,25},{25,9},{2,18},{18... | collective-permute-start | bytes 392 | tf_op jit(solution)/shard_map/ppermute | solution.py:18
  29.2 0.7 iota_compare_fusion.2
  29.9 0.8 collective-permute-done.5
  30.7 0.8 select_dynamic-update-slice_fusion
  31.5 0.7 fusion.11
  32.3 0.8 broadcast_select_fusion.7
  33.4 2.1 %collective-permute-start.7 = (bf16[32,512]{1,0:T(8,128)(2,1)S(1)}, bf16[32,512]{1,0:T(8,128)(2,1)S(1)}, u32[]{:S(2)}, u32[]{:S(2)}) collective-permute-start(bf16[32,512]{1,0:T(8,128)(2,1)S(1)} %constant_dynamic-slice_fusion.2), channel_id=1, source_target_pairs={{0,16},{16,0},{8,24},{24,8},{1,17},{17,1},{9,25},{25,9},{2,18},{18... | collective-permute-start | bytes 98312 | tf_op jit(solution)/shard_map/ppermute | solution.py:18
  35.5 1.1 broadcast_select_fusion.4
  36.6 0.8 dynamic_update_slice.32
  37.7 0.7 dynamic_update_slice.38
  38.5 2.1 collective-permute-start.9
  40.9 0.8 reshape.55
  41.6 2.1 %collective-permute-done.3 = bf16[32,2048]{1,0:T(8,128)(2,1)S(1)} collective-permute-done((bf16[32,2048]{1,0:T(8,128)(2,1)S(1)}, bf16[32,2048]{1,0:T(8,128)(2,1)S(1)}, u32[]{:S(2)}, u32[]{:S(2)}) %collective-permute-start.3) | collective-permute-done | bytes 131104 | tf_op jit(solution)/shard_map/ppermute | solution.py:18
  43.8 1.4 collective-permute-done.9
  45.3 0.8 dynamic_update_slice.39
  46.1 0.8 reshape.56
  46.9 0.8 dynamic_update_slice.33
  47.6 1.3 copy.57
  48.9 1.4 copy.44
  50.4 1.7 broadcast_select_fusion.1
  52.1 11.0 %dynamic_update_slice.30 = bf16[256,4096]{0,1:T(8,128)(2,1)} dynamic-update-slice(bf16[256,4096]{0,1:T(8,128)(2,1)} %copy.45, bf16[32,4096]{0,1:T(8,128)(2,1)S(1)} %broadcast_select_fusion.1, s32[]{:T(128)S(6)} %select_n.72, s32[]{:T(128)} %constant.10.clone.1) | dynamic-update-slice | bytes 524292 | tf_op jit(solution)/shard_map/dynamic_update_slice | solution.py:29
  63.2 1.7 constant_dynamic-slice_fusion.6
  65.6 0.7 fusion.8
  66.4 3.1 %fusion.16 = (f32[4,4,256]{2,1,0:T(4,128)S(1)}, f32[4,4,256,256]{2,3,1,0:T(8,128)}) fusion(f32[4,256,256,4]{2,1,3,0:T(8,128)S(1)} %fusion.8, pred[256,256]{0,1:T(8,128)(4,1)S(1)} %copy-done.5), kind=kOutput, calls=%fused_computation.45 | output fusion | flops 6291711 | bytes 8470528 | tf_op jit(solution)/shard_map/sub | solution.py:45
  69.5 2.1 collective-permute-done.1
  72.1 1.7 broadcast_select_fusion
  73.8 11.0 %dynamic_update_slice.31 = bf16[256,4096]{0,1:T(8,128)(2,1)} dynamic-update-slice(bf16[256,4096]{0,1:T(8,128)(2,1)} %dynamic_update_slice.30, bf16[32,4096]{0,1:T(8,128)(2,1)S(1)} %broadcast_select_fusion, s32[]{:T(128)S(6)} %select_n.74, s32[]{:T(128)} %constant.10.clone.1) | dynamic-update-slice | bytes 524292 | tf_op jit(solution)/shard_map/dynamic_update_slice | solution.py:29
  84.8 6.8 %all-to-all-start = ((bf16[256,8,512]{0,2,1:T(8,128)(2,1)}), bf16[256,8,512]{0,2,1:T(8,128)(2,1)S(1)}, u32[]{:S(2)}, u32[]{:S(2)}) async-start(bf16[256,8,512]{0,2,1:T(8,128)(2,1)} %bitcast.4), calls=%async_computation | async-start | bytes 4194304 | tf_op jit(solution)/shard_map/all_to_all | solution.py:101
  91.7 3.7 %fusion.7 = bf16[4,128,256]{2,1,0:T(8,128)(2,1)} fusion(bf16[256,4,4,128]{0,3,2,1:T(8,128)(2,1)S(1)} %bitcast.36, f32[4,4,256,256]{2,3,1,0:T(8,128)} %get-tuple-element.21, f32[4,4,256]{2,1,0:T(4,128)S(1)} %get-tuple-element.20), kind=kOutput, calls=%fused_computation.11 | convolution fusion | flops 270663680 | bytes 5521408 | tf_op jit(solution)/shard_map/gnij,ignd->jgd/dot_general | solution.py:48
  95.5 50.8 %all-to-all-done = bf16[256,8,512]{0,2,1:T(8,128)(2,1)S(1)} async-done(((bf16[256,8,512]{0,2,1:T(8,128)(2,1)}), bf16[256,8,512]{0,2,1:T(8,128)(2,1)S(1)}, u32[]{:S(2)}, u32[]{:S(2)}) %all-to-all-start) | async-done | bytes 2097184 | tf_op jit(solution)/shard_map/all_to_all | solution.py:101
  146.4 2.4 %copy.48 = bf16[8,256,1,512]{3,1,0,2:T(8,128)(2,1)} copy(bf16[8,256,1,512]{1,3,0,2:T(8,128)(2,1)S(1)} %bitcast.34) | data formatting | bytes 4194304 | tf_op jit(solution)/shard_map/all_to_all | solution.py:101
  148.7 16.4 %all-gather.2.cloned.1.call-done = bf16[2048,512]{0,1:T(8,128)(2,1)} async-done(((bf16[256,512]{0,1:T(8,128)(2,1)}), bf16[2048,512]{0,1:T(8,128)(2,1)}) %all-gather.2.cloned.1.call-update) | async-done | bytes 2097168 | tf_op jit(solution)/shard_map/all_gather | solution.py:107
  165.2 4.5 %fusion.17 = f32[512,512]{1,0:T(8,128)} fusion(bf16[2048,512]{1,0:T(8,128)(2,1)} %bitcast.35, bf16[2048,512]{0,1:T(8,128)(2,1)} %all-gather.2.cloned.1.call-done), kind=kOutput, calls=%fused_computation.46 | convolution fusion | flops 1073741824 | bytes 5242880 | tf_op jit(solution)/shard_map/dot_general | solution.py:105
  169.7 0.8 copy.53
  170.6 33.8 %all-reduce.2.cloned.1.call-done = f32[512,512]{1,0:T(8,128)} async-done(((f32[512,512]{1,0:T(8,128)}), f32[512,512]{1,0:T(8,128)}) %all-reduce.2.cloned.1.call-update) | async-done | bytes 1048592 | tf_op jit(solution)/shard_map/psum | solution.py:111
  204.4 2.3 %copy.80 = f32[512,512]{1,0:T(8,128)} copy(f32[512,512]{1,0:T(8,128)} %all-reduce.2.cloned.1.call-done) | data formatting | bytes 2097152
  (54 shorter events, 4.1 us)
Async XLA Ops:
  7.2 1.4 copy-start.4
  7.2 4.8 %copy-start.2 = (bf16[256,2048]{1,0:T(8,128)(2,1)S(1)}, bf16[256,2048]{1,0:T(8,128)(2,1)}, u32[]{:S(2)}) copy-start(bf16[256,2048]{1,0:T(8,128)(2,1)} %param.13) | copy-start | bytes 3145732
  7.2 4.7 %copy-start.8 = (s32[256]{0:T(256)S(1)}, s32[256]{0:T(256)}, u32[]{:S(2)}) copy-start(s32[256]{0:T(256)} %param.15) | copy-start | bytes 3076
  7.2 4.7 %copy-start.10 = (f32[16]{0:T(128)S(1)}, f32[16]{0:T(128)}, u32[]{:S(2)}) copy-start(f32[16]{0:T(128)} %param.16) | copy-start | bytes 196
  7.2 1.4 copy-start.6
  8.5 6.1 %copy-start.9 = (s32[256]{0:T(256)S(1)}, s32[256]{0:T(256)}, u32[]{:S(2)}) copy-start(s32[256]{0:T(256)} %param.14) | copy-start | bytes 3076
  12.3 23.2 %collective-permute-start.2 = (bf16[32,2048]{1,0:T(8,128)(2,1)S(1)}, bf16[32,2048]{1,0:T(8,128)(2,1)}, u32[]{:S(2)}, u32[]{:S(2)}) collective-permute-start(bf16[32,2048]{1,0:T(8,128)(2,1)S(1)} %constant_dynamic-slice_fusion.5), channel_id=1, source_target_pairs={{0,8},{8,0},{16,24},{24,16},{1,9},{9,1},{17,25},{25,17},{2,10},{10... | collective-permute-start | bytes 393224 | tf_op jit(solution)/shard_map/ppermute | solution.py:18
  13.5 22.0 %collective-permute-start.8 = (bf16[32,2048]{1,0:T(8,128)(2,1)}, bf16[32,2048]{1,0:T(8,128)(2,1)}, u32[]{:S(2)}, u32[]{:S(2)}) collective-permute-start(bf16[32,2048]{1,0:T(8,128)(2,1)} %constant_dynamic-slice_fusion.1), channel_id=1, source_target_pairs={{0,8},{8,0},{16,24},{24,16},{1,9},{9,1},{17,25},{25,17},{2,10},{10... | collective-permute-start | bytes 393224 | tf_op jit(solution)/shard_map/ppermute | solution.py:18
  14.2 18.1 %collective-permute-start.6 = (bf16[32,512]{1,0:T(8,128)(2,1)}, bf16[32,512]{1,0:T(8,128)(2,1)}, u32[]{:S(2)}, u32[]{:S(2)}) collective-permute-start(bf16[32,512]{1,0:T(8,128)(2,1)} %constant_dynamic-slice_fusion.3), channel_id=1, source_target_pairs={{0,8},{8,0},{16,24},{24,16},{1,9},{9,1},{17,25},{25,17},{2,10},{10... | collective-permute-start | bytes 98312 | tf_op jit(solution)/shard_map/ppermute | solution.py:18
  15.2 10.5 %collective-permute-start.4 = (s32[32]{0:T(128)}, s32[32]{0:T(128)S(1)}, u32[]{:S(2)}, u32[]{:S(2)}) collective-permute-start(s32[32]{0:T(128)} %dynamic_slice.44), channel_id=1, source_target_pairs={{0,8},{8,0},{16,24},{24,16},{1,9},{9,1},{17,25},{25,17},{2,10},{10... | collective-permute-start | bytes 392 | tf_op jit(solution)/shard_map/ppermute | solution.py:18
  19.4 3.1 %copy-start.7 = (s32[1,2]{1,0:T(1,128)S(1)}, s32[1,2]{1,0:T(1,128)}, u32[]{:S(2)}) copy-start(s32[1,2]{1,0:T(1,128)} %param.19) | copy-start | bytes 28
  22.0 26.9 %collective-permute-start = (bf16[32,4096]{1,0:T(8,128)(2,1)}, bf16[32,4096]{1,0:T(8,128)(2,1)}, u32[]{:S(2)}, u32[]{:S(2)}) collective-permute-start(bf16[32,4096]{1,0:T(8,128)(2,1)} %copy.43), channel_id=1, source_target_pairs={{0,8},{8,0},{16,24},{24,16},{1,9},{9,1},{17,25},{25,17},{2,10},{10... | collective-permute-start | bytes 786440 | tf_op jit(solution)/shard_map/ppermute | solution.py:18
  26.7 4.1 %collective-permute-start.5 = (s32[32]{0:T(128)S(1)}, s32[32]{0:T(128)S(1)}, u32[]{:S(2)}, u32[]{:S(2)}) collective-permute-start(s32[32]{0:T(128)S(1)} %dynamic_slice.45), channel_id=1, source_target_pairs={{0,16},{16,0},{8,24},{24,8},{1,17},{17,1},{9,25},{25,9},{2,18},{18... | collective-permute-start | bytes 392 | tf_op jit(solution)/shard_map/ppermute | solution.py:18
  33.4 7.2 %collective-permute-start.7 = (bf16[32,512]{1,0:T(8,128)(2,1)S(1)}, bf16[32,512]{1,0:T(8,128)(2,1)S(1)}, u32[]{:S(2)}, u32[]{:S(2)}) collective-permute-start(bf16[32,512]{1,0:T(8,128)(2,1)S(1)} %constant_dynamic-slice_fusion.2), channel_id=1, source_target_pairs={{0,16},{16,0},{8,24},{24,8},{1,17},{17,1},{9,25},{25,9},{2,18},{18... | collective-permute-start | bytes 98312 | tf_op jit(solution)/shard_map/ppermute | solution.py:18
  37.4 6.3 %collective-permute-start.3 = (bf16[32,2048]{1,0:T(8,128)(2,1)S(1)}, bf16[32,2048]{1,0:T(8,128)(2,1)S(1)}, u32[]{:S(2)}, u32[]{:S(2)}) collective-permute-start(bf16[32,2048]{1,0:T(8,128)(2,1)S(1)} %constant_dynamic-slice_fusion.4), channel_id=1, source_target_pairs={{0,16},{16,0},{8,24},{24,8},{1,17},{17,1},{9,25},{25,9},{2,18},{18... | collective-permute-start | bytes 393224 | tf_op jit(solution)/shard_map/ppermute | solution.py:18
  38.5 6.7 %collective-permute-start.9 = (bf16[32,2048]{1,0:T(8,128)(2,1)S(1)}, bf16[32,2048]{1,0:T(8,128)(2,1)S(1)}, u32[]{:S(2)}, u32[]{:S(2)}) collective-permute-start(bf16[32,2048]{1,0:T(8,128)(2,1)S(1)} %constant_dynamic-slice_fusion), channel_id=1, source_target_pairs={{0,16},{16,0},{8,24},{24,8},{1,17},{17,1},{9,25},{25,9},{2,18},{18... | collective-permute-start | bytes 393224 | tf_op jit(solution)/shard_map/ppermute | solution.py:18
  63.2 2.4 %copy-start.3 = (bf16[256,4,128]{2,1,0:T(4,128)(2,1)S(1)}, bf16[256,4,128]{2,1,0:T(4,128)(2,1)}, u32[]{:S(2)}) copy-start(bf16[256,4,128]{2,1,0:T(4,128)(2,1)} %reshape.55) | copy-start | bytes 786436
  65.1 6.4 %collective-permute-start.1 = (bf16[32,4096]{1,0:T(8,128)(2,1)S(1)}, bf16[32,4096]{1,0:T(8,128)(2,1)S(1)}, u32[]{:S(2)}, u32[]{:S(2)}) collective-permute-start(bf16[32,4096]{1,0:T(8,128)(2,1)S(1)} %copy.46), channel_id=1, source_target_pairs={{0,16},{16,0},{8,24},{24,8},{1,17},{17,1},{9,25},{25,9},{2,18},{18... | collective-permute-start | bytes 786440 | tf_op jit(solution)/shard_map/ppermute | solution.py:18
  65.5 0.8 copy-start.5
  84.8 6.9 %copy-start = (bf16[256,2048]{0,1:T(8,128)(2,1)S(1)}, bf16[256,2048]{0,1:T(8,128)(2,1)}, u32[]{:S(2)}) copy-start(bf16[256,2048]{0,1:T(8,128)(2,1)} %copy.57) | copy-start | bytes 3145732
  84.8 61.5 %all-to-all-start = ((bf16[256,8,512]{0,2,1:T(8,128)(2,1)}), bf16[256,8,512]{0,2,1:T(8,128)(2,1)S(1)}, u32[]{:S(2)}, u32[]{:S(2)}) async-start(bf16[256,8,512]{0,2,1:T(8,128)(2,1)} %bitcast.4), calls=%async_computation | async-start | bytes 4194304 | tf_op jit(solution)/shard_map/all_to_all | solution.py:101
  91.7 73.5 %all-gather.2.cloned.1.call-start = ((), (), s32[]{:S(2)}) async-start(), calls=%async_computation.1 | async-start | bytes 2359296 | tf_op jit(solution)/shard_map/all_gather | solution.py:107
  95.5 108.9 %all-reduce.2.cloned.1.call-start = ((), (), s32[]{:S(2)}) async-start(), calls=%async_computation.2 | async-start | bytes 2097152 | tf_op jit(solution)/shard_map/psum | solution.py:111
  165.2 4.6 %copy-start.1 = (bf16[4,128,256]{2,1,0:T(8,128)(2,1)S(1)}, bf16[4,128,256]{2,1,0:T(8,128)(2,1)}, u32[]{:S(2)}) copy-start(bf16[4,128,256]{2,1,0:T(8,128)(2,1)} %fusion.7) | copy-start | bytes 786436
Sparse Core Ops, SparseCore 0:
  95.6 69.5 all-gather.1
  169.9 34.5 all-reduce.1
where the time goes:
time: 214 us
  waiting for transfers between devices  108 us (50%)
  local copies, waits for them, and re-layouts  49.4 us (23%)
  between operations  19 us (9%)
  starting transfers between devices  15.9 us (7%)
  other arithmetic  12.7 us (6%)
  matrix products  8.97 us (4%)
    all_to_all x1, waiting for transfers between devices, on_device(): lax.all_to_all(padded.reshape(tokens, owners, owned), 'fsdp', split_axis=...  50.8 us
    psum x1, waiting for transfers between devices, on_device(): return (lax.psum(owned_block, 'dp'), values_grad)  33.8 us
    dynamic_update_slice x8, local copies, waits for them, and re-layouts, blend_rows(): return lax.dynamic_update_slice_in_dim(item, chosen, offset, 0)  25.5 us
    all_gather x1, waiting for transfers between devices, on_device(): lax.all_gather(values_grad, 'fsdp', axis=0, tiled=True)  16.4 us
    ppermute x10, starting transfers between devices, swapped(): return lax.ppermute(block, axis, route)  8.98 us
    unnamed x27, local copies, waits for them, and re-layouts  8.68 us
    all_to_all x1, starting transfers between devices, on_device(): lax.all_to_all(padded.reshape(tokens, owners, owned), 'fsdp', split_axis=...  6.85 us
    dynamic_slice x12, local copies, waits for them, and re-layouts, cut_rows(): return lax.dynamic_slice_in_dim(item, offset, CAP, 0)  6.78 us
  transfers between devices with their start and end apart: 13, of which 7 were waited for; matrix products, arithmetic and copies ran while one was open for 15% of the time, Pallas kernels for 0%

commit v1 on v0

v1 whole, which is shorter than its diff:
```python
import functools

import jax
import jax.numpy as jnp
from jax import lax
from jax.experimental import pallas as pl
from jax.experimental.pallas import tpu as pltpu
from jax.sharding import PartitionSpec as P

D = 4096
HD = 128
CAP = 32
HALF = 128
LANE = 128
INFO = 16
MIB = 1 << 20
BF16 = jnp.bfloat16
F32 = jnp.float32

VMEM = pl.BlockSpec(memory_space=pltpu.VMEM)
SMEM = pl.BlockSpec(memory_space=pltpu.SMEM)
ANY = pl.BlockSpec(memory_space=pl.ANY)


def attend_kernel(per_group, loss_ref, exponent_ref, start_ref, rows_ref, q_ref, k_ref, g_ref, doc_ref, index_ref, v_ref):
    exponent = exponent_ref[0]
    unscale = jnp.float32(1.0)
    for bit in range(5):
        unscale = unscale * jnp.where((exponent >> bit) & 1 == 1, jnp.float32(2.0 ** -(1 << bit)), 1.0)
    row = lax.broadcasted_iota(jnp.int32, (HALF, HALF), 0)
    col = lax.broadcasted_iota(jnp.int32, (HALF, HALF), 1)
    for half in range(2):
        span = pl.ds(half * HALF, HALF)
        doc_i = jnp.broadcast_to(doc_ref[:, span], (HALF, HALF))
        allowed = (doc_i == doc_i.T) & (row <= col)
        index = index_ref[:, span]
        factor = jnp.zeros((1, HALF), F32)
        for entry in range(loss_ref.shape[0]):
            factor = jnp.where(index == entry, loss_ref[entry], factor)
        factor = jnp.broadcast_to(factor * unscale, (HALF, HALF)).T
        q_all = jnp.concatenate([q_ref[span, pl.ds(n * HD, HD)] for n in range(per_group)], axis=0)
        scores = lax.dot_general(
            k_ref[span, :], q_all, (((1,), (1,)), ((), ())), preferred_element_type=F32
        ) * HD ** (-0.5)
        probs = []
        weighted = []
        for n in range(per_group):
            own = jnp.where(allowed, scores[:, n * HALF:(n + 1) * HALF], -1e30)
            expo = jnp.exp(own - jnp.max(own, axis=0, keepdims=True))
            probs.append((expo / jnp.sum(expo, axis=0, keepdims=True)).astype(BF16))
            weighted.append((g_ref[span, pl.ds(n * HD, HD)].astype(F32) * factor).astype(BF16))
        values = jnp.dot(
            jnp.concatenate(probs, axis=1), jnp.concatenate(weighted, axis=0), preferred_element_type=F32
        )
        v_ref[span, :] = values.astype(BF16)
    info_row = lax.broadcasted_iota(jnp.int32, (INFO, HD), 0)
    info = jnp.zeros((INFO, HD), jnp.int32)
    for level in range(min(start_ref.shape[1], INFO // 2)):
        info = jnp.where(info_row == 2 * level, start_ref[0, level], info)
        info = jnp.where(info_row == 2 * level + 1, rows_ref[0, level], info)
    v_ref[pl.ds(2 * HALF, INFO), :] = info.astype(F32).astype(BF16)


def attend(query, key, grad, ids, index, loss, exponent, start, rows):
    tokens, key_width = key.shape
    groups = key_width // HD
    per_group = query.shape[1] // key_width
    wide = per_group * HD
    return pl.pallas_call(
        functools.partial(attend_kernel, per_group),
        grid=(groups,),
        in_specs=[SMEM] * 4 + [
            pl.BlockSpec((tokens, wide), lambda g: (0, g)),
            pl.BlockSpec((tokens, HD), lambda g: (0, g)),
            pl.BlockSpec((tokens, wide), lambda g: (0, g)),
            pl.BlockSpec((1, tokens), lambda g: (0, 0)),
            pl.BlockSpec((1, tokens), lambda g: (0, 0)),
        ],
        out_specs=pl.BlockSpec((tokens + INFO, HD), lambda g: (0, g)),
        out_shape=jax.ShapeDtypeStruct((tokens + INFO, key_width), BF16),
        compiler_params=pltpu.CompilerParams(vmem_limit_bytes=32 * MIB),
        cost_estimate=pl.CostEstimate(flops=600_000_000, bytes_accessed=3 * MIB, transcendentals=500_000),
        name="attend",
    )(loss, exponent, start, rows, query, key, grad, ids.reshape(1, tokens), index.reshape(1, tokens))


CORE, Y, X = 8, 16, 1


def xor_permute(value, mask):
    count = lax.axis_size("dp") * lax.axis_size("fsdp")
    return lax.ppermute(value, ("dp", "fsdp"), [(i, i ^ mask) for i in range(count)])


def pieces_kernel(x_ref, near_ref, a2_ref, a3_ref, b2_ref, b3_ref, own_ref, sems):
    dp = lax.axis_index("dp")
    fsdp = lax.axis_index("fsdp")

    def column(dp_flip, fsdp_flip):
        owner = fsdp ^ fsdp_flip
        return pl.multiple_of(owner * 512 + (dp ^ dp_flip) * LANE, LANE)

    copies = []

    def put(target, at, dp_flip, fsdp_flip):
        copy = pltpu.make_async_copy(
            x_ref.at[:, pl.ds(column(dp_flip, fsdp_flip), LANE)], target.at[:, pl.ds(at, LANE)], sems.at[len(copies)]
        )
        copy.start()
        copies.append(copy)

    a_targets = {3: a3_ref, 2: a2_ref, 1: near_ref.at[0], 0: own_ref.at[0]}
    b_targets = {3: b3_ref, 2: b2_ref, 1: near_ref.at[1], 0: own_ref.at[1]}
    for m in (2, 3, 1, 0):
        for far in range(2):
            for z in range(2):
                at = (far * 2 + z) * LANE
                put(a_targets[m], at, m, (z << 1) | far)
                put(b_targets[m], at, (m & 1) | (far << 1), ((2 + z) << 1) | (m >> 1))
    for copy in copies:
        copy.wait()


def make_pieces(layer_input):
    tokens = layer_input.shape[0]
    one = jax.ShapeDtypeStruct((tokens, 512), BF16)
    two = jax.ShapeDtypeStruct((2, tokens, 512), BF16)
    return pl.pallas_call(
        pieces_kernel,
        in_specs=[ANY],
        out_specs=[ANY] * 6,
        out_shape=[two, one, one, one, one, two],
        scratch_shapes=[pltpu.SemaphoreType.DMA((32,))],
        cost_estimate=pl.CostEstimate(flops=0, bytes_accessed=4 * MIB, transcendentals=0),
        name="pieces",
    )(layer_input)


def partial_kernel(which, own_ref, near_ref, far_ref, diagonal_ref, v0_ref, v1_ref, v2_ref, v3_ref, keep_ref, send_ref):
    total = None
    tokens = far_ref.shape[0]
    for x, v in (
        (own_ref[which], v0_ref), (near_ref[which], v1_ref), (far_ref[...], v2_ref), (diagonal_ref[...], v3_ref)
    ):
        term = lax.dot_general(x, v[:tokens, :], (((0,), (0,)), ((), ())), preferred_element_type=F32)
        total = term if total is None else total + term
    keep_ref[...] = total[:256]
    send_ref[...] = total[256:].astype(BF16)


def partial_sums(which, own, near, far, diagonal, values):
    return pl.pallas_call(
        functools.partial(partial_kernel, which),
        in_specs=[VMEM] * 8,
        out_specs=[VMEM] * 2,
        out_shape=[jax.ShapeDtypeStruct((256, 512), F32), jax.ShapeDtypeStruct((256, 512), BF16)],
        compiler_params=pltpu.CompilerParams(vmem_limit_bytes=32 * MIB),
        cost_estimate=pl.CostEstimate(flops=540_000_000, bytes_accessed=4 * MIB, transcendentals=0),
        name="partial_sums",
    )(own, near, far, diagonal, *values)


def balance_kernel(v0_ref, v1_ref, v2_ref, v3_ref, out_ref):
    refs = (v0_ref, v1_ref, v2_ref, v3_ref)
    tokens = out_ref.shape[0]
    infos = [ref[pl.ds(tokens, INFO), pl.ds(0, HALF)].astype(F32).astype(jnp.int32) for ref in refs]

    def table(device, entry):
        return jnp.broadcast_to(infos[device][entry:entry + 1, :], (HALF, HALF))

    place = lax.broadcasted_iota(jnp.int32, (HALF, HALF), 0) + HALF
    inner = lax.broadcasted_iota(jnp.int32, (HALF, HALF), 1) + HALF

    def source(device, at):
        first = table(device, 0)
        swapped = (at >= first) & (at < first + table(device, 1))
        return swapped, jnp.where(swapped, table(device ^ 1, 0) + at - first, at)

    first = table(0, 2)
    outer = (place >= first) & (place < first + table(0, 3))
    swapped_here, here = source(0, place)
    swapped_there, there = source(2, table(2, 2) + place - first)
    position = jnp.where(outer, there, here)
    device = jnp.where(outer, jnp.where(swapped_there, 3, 2), jnp.where(swapped_here, 1, 0))
    total = None
    for number, ref in enumerate(refs):
        pick = jnp.where((device == number) & (position == inner), 1.0, 0.0).astype(BF16)
        term = jnp.dot(pick, ref[pl.ds(HALF, HALF), :], preferred_element_type=F32)
        total = term if total is None else total + term
    out_ref[pl.ds(0, HALF), :] = v0_ref[pl.ds(0, HALF), :]
    out_ref[pl.ds(HALF, HALF), :] = total.astype(BF16)


def balance(values):
    return pl.pallas_call(
        balance_kernel,
        in_specs=[VMEM] * 4,
        out_specs=VMEM,
        out_shape=jax.ShapeDtypeStruct((2 * HALF, values[0].shape[1]), BF16),
        compiler_params=pltpu.CompilerParams(vmem_limit_bytes=32 * MIB),
        cost_estimate=pl.CostEstimate(flops=70_000_000, bytes_accessed=MIB, transcendentals=0),
        name="balance",
    )(*values)


def place_kernel(pair_ref, near_ref, out_ref):
    dp = lax.axis_index("dp")
    for ref, core in ((pair_ref, 0), (near_ref, 1)):
        for y in range(2):
            quarter = dp ^ (core | y << 1)
            out_ref[pl.ds(pl.multiple_of(quarter * LANE, LANE), LANE), :] = ref[y].astype(F32)


def place(pair, near):
    return pl.pallas_call(
        place_kernel,
        in_specs=[VMEM] * 2,
        out_specs=VMEM,
        out_shape=jax.ShapeDtypeStruct((512, pair.shape[2]), F32),
        cost_estimate=pl.CostEstimate(flops=0, bytes_accessed=2 * MIB, transcendentals=0),
        name="place",
    )(pair, near)


def reduce_by_axis(layer_input, values):
    near, a2, a3, b2, b3, own = make_pieces(layer_input)
    a2 = xor_permute(a2, Y)
    b2 = xor_permute(b2, X)
    a3 = xor_permute(a3, Y | CORE)
    b3 = xor_permute(b3, X | CORE)
    near = xor_permute(near, CORE)
    values = values()
    v_core = xor_permute(values, CORE)
    v_y = xor_permute(values, Y)
    v_x = xor_permute(values, X)
    v_y_core = xor_permute(v_y, CORE)
    v_x_core = xor_permute(v_x, CORE)
    b_keep, b_send = partial_sums(1, own, near, b2, b3, (values, v_core, v_x, v_x_core))
    a_keep, a_send = partial_sums(0, own, near, a2, a3, (values, v_core, v_y, v_y_core))
    b_total = b_keep + xor_permute(b_send, Y).astype(F32)
    a_total = a_keep + xor_permute(a_send, X).astype(F32)
    z2 = xor_permute(b_total[:LANE].astype(BF16), 4)
    z3 = xor_permute(b_total[LANE:].astype(BF16), 6)
    z1 = xor_permute(a_total[LANE:].astype(BF16), 2)
    mine = (a_total[:LANE] + z1.astype(F32) + (z2.astype(F32) + z3.astype(F32))).astype(BF16)
    pair = jnp.stack([mine, xor_permute(mine, Y)])
    grad_value = place(pair, xor_permute(pair, CORE))
    return grad_value, balance((values, v_core, v_y, v_y_core))


def swapped(block, axis, distance):
    count = lax.axis_size(axis)
    route = []
    for low in range(count):
        high = low | 1 << distance
        if high != low and high < count:
            route += [(low, high), (high, low)]
    return lax.ppermute(block, axis, route)


def blend_rows(item, incoming, offset, extent):
    inside = (jnp.arange(CAP) < extent)[:, None]
    chosen = jnp.where(inside, incoming, lax.dynamic_slice_in_dim(item, offset, CAP, 0))
    return lax.dynamic_update_slice_in_dim(item, chosen, offset, 0)


def reduce_by_owner(layer_input, values, swap_start, swap_rows):
    tokens = layer_input.shape[0]
    values = values()[:tokens]
    balanced = values
    for level in range(lax.axis_size("dp").bit_length() - 1):
        offset = swap_start[0, level]
        window = lax.dynamic_slice_in_dim(balanced, offset, CAP, 0)
        balanced = blend_rows(balanced, swapped(window, "dp", level), offset, swap_rows[0, level])
    owners = lax.axis_size("fsdp")
    owned = (D + owners - 1) // owners
    padded = jnp.pad(layer_input, ((0, 0), (0, owned * owners - D)))
    arranged = lax.all_to_all(
        padded.reshape(tokens, owners, owned), "fsdp", split_axis=1, concat_axis=0, tiled=True
    )
    block = lax.dot_general(
        arranged.reshape(-1, owned),
        lax.all_gather(values, "fsdp", axis=0, tiled=True),
        (((0,), (0,)), ((), ())),
        preferred_element_type=F32,
    )
    return lax.psum(block, "dp"), balanced


def on_device(
    layer_input,
    query_states,
    key_states,
    output_grad,
    document_ids,
    weight_index,
    loss_weights,
    scale_exponent,
    swap_start,
    swap_rows,
):
    def values():
        return attend(
            query_states, key_states, output_grad, document_ids, weight_index,
            loss_weights, scale_exponent, swap_start, swap_rows,
        )

    if lax.axis_size("dp") == 4 and lax.axis_size("fsdp") == 8:
        return reduce_by_axis(layer_input, values)
    return reduce_by_owner(layer_input, values, swap_start, swap_rows)


def solution(mesh):
    return jax.shard_map(
        on_device,
        mesh=mesh,
        in_specs=(
            P(("dp", "fsdp"), None),
            P(("dp", "fsdp"), None),
            P(("dp", "fsdp"), None),
            P(("dp", "fsdp"), None),
            P(("dp", "fsdp")),
            P(("dp", "fsdp")),
            P(),
            P(("dp", "fsdp")),
            P(("dp", "fsdp"), None),
            P(("dp", "fsdp"), None),
        ),
        out_specs=(P("fsdp", None), P(("dp", "fsdp"), None)),
        check_vma=False,
    )
```

time: 214 us -> 139 us (0.65)
  Pallas kernels: 0 us -> 73.1 us
  waiting for transfers between devices: 108 us -> 36.7 us
  local copies, waits for them, and re-layouts: 49.4 us -> 8.5 us
  between operations: 19 us -> 1.42 us
  other arithmetic: 12.7 us -> 0.23 us
  matrix products: 8.97 us -> 0 us
    pallas_call x0 -> x6, Pallas kernels: none -> 73.1 us  [the longest x1 64.9 us: make_pieces(): pl.pallas_call(pieces_kernel, in_specs=[ANY], out_specs=[ANY] * 6, out_sh...]
    all_to_all x1 -> x0, waiting for transfers between devices: 50.8 us -> none  [on_device(): lax.all_to_all(padded.reshape(tokens, owners, owned), 'fsdp', split_axis=...]
    psum x1 -> x0, waiting for transfers between devices: 33.8 us -> none  [on_device(): return (lax.psum(owned_block, 'dp'), values_grad)]
    ppermute x10 -> x17, waiting for transfers between devices: 6.48 us -> 36.7 us  [xor_permute(): lax.ppermute(value, ('dp', 'fsdp'), [(i, i ^ mask) for i in range(count)])]
    dynamic_update_slice x8 -> x0, local copies, waits for them, and re-layouts: 25.5 us -> none  [blend_rows(): return lax.dynamic_update_slice_in_dim(item, chosen, offset, 0)]
    all_gather x1 -> x0, waiting for transfers between devices: 16.4 us -> none  [on_device(): lax.all_gather(values_grad, 'fsdp', axis=0, tiled=True)]
    dot_general x3 -> x0, matrix products: 8.97 us -> none  [the longest x1 4.53 us: on_device(): lax.dot_general(feature_rows, lax.all_gather(values_grad, 'fsdp', axis=0,...]
    ppermute x10 -> x17, starting transfers between devices: 8.98 us -> 16.8 us  [xor_permute(): lax.ppermute(value, ('dp', 'fsdp'), [(i, i ^ mask) for i in range(count)])]
  transfers between devices with their start and end apart: 13 -> 17, of which waited for: 7 -> 11; matrix products, arithmetic and copies ran while one was open for 15% -> 0% of each run, Pallas kernels for 0% -> 49%
where the time goes in v1:
time: 139 us; the launch traced here: 137 us
  Pallas kernels  73.1 us (53%)
  waiting for transfers between devices  36.7 us (26%)
  starting transfers between devices  16.8 us (12%)
  local copies, waits for them, and re-layouts  8.5 us (6%)
  between operations  1.42 us (1%)
    pallas_call x1, Pallas kernels, make_pieces(): pl.pallas_call(pieces_kernel, in_specs=[ANY], out_specs=[ANY] * 6, out_sh...  64.9 us
    ppermute x17, waiting for transfers between devices, xor_permute(): lax.ppermute(value, ('dp', 'fsdp'), [(i, i ^ mask) for i in range(count)])  36.7 us
    ppermute x17, starting transfers between devices, xor_permute(): lax.ppermute(value, ('dp', 'fsdp'), [(i, i ^ mask) for i in range(count)])  16.8 us
    unnamed x22, local copies, waits for them, and re-layouts  8.46 us
    pallas_call x1, Pallas kernels, attend(): pl.pallas_call(functools.partial(attend_kernel, per_group), grid=(groups,...  3.59 us
  transfers between devices with their start and end apart: 17, of which 11 were waited for; matrix products, arithmetic and copies ran while one was open for 0% of the time, Pallas kernels for 49%

profile of v1, /device:TPU:0, one launch (start us, length us, event | category | flops | bytes accessed | tf_op | source)
XLA Modules:
  0.0 136.7 jit_solution(18034760858964787808)
XLA Ops:
  1.3 1.2 copy-done.1
  2.5 1.2 copy-done.2
  3.7 0.9 copy-done.3
  4.7 0.7 copy-done.4
  5.4 0.7 copy-done.5
  6.0 0.7 copy-done.6
  6.7 0.7 copy-done.7
  7.4 0.7 copy-done.8
  8.0 3.6 %attend.1.v0_ref = bf16[272,512]{1,0:T(8,128)(2,1)S(1)} custom-call(f32[16]{0:T(128)S(1)} %copy-done.6, s32[1]{0:T(128)S(6)} %copy.12.exponent_ref, s32[1,2]{1,0:T(1,128)S(1)} %copy-done.7, s32[1,2]{1,0:T(1,128)S(1)} %copy-done.8, bf16[256,2048]{1,0:T(8,128)(2,1)S(1)} %copy-done.1, bf16[256,512]{1,0:T(8,128)(2,1)S(1)} %copy-done.3, ...), custom_call_target="tpu_custom_call" | custom-call | flops 600000000 | bytes 3145728 | tf_op jit(solution)/shard_map/attend/pallas_call | solution.py:69
  11.6 3.0 %collective-permute-start.10 = (bf16[272,512]{1,0:T(8,128)(2,1)S(1)}, bf16[272,512]{1,0:T(8,128)(2,1)S(1)}, u32[]{:S(2)}, u32[]{:S(2)}) collective-permute-start(bf16[272,512]{1,0:T(8,128)(2,1)S(1)} %attend.1.v0_ref), channel_id=1, source_target_pairs={{0,1},{1,0},{2,3},{3,2},{4,5},{5,4},{6,7},{7,6},{8,9},{9,8},{10,11... | collective-permute-start | bytes 835592 | tf_op jit(solution)/shard_map/ppermute | solution.py:92
  14.6 64.9 %pieces.1 = (bf16[2,256,512]{2,1,0:T(8,128)(2,1)}, bf16[256,512]{1,0:T(8,128)(2,1)}, bf16[256,512]{1,0:T(8,128)(2,1)}, bf16[256,512]{1,0:T(8,128)(2,1)}, bf16[25...) custom-call(bf16[256,4096]{1,0:T(8,128)(2,1)} %x_ref.1), custom_call_target="tpu_custom_call" | custom-call | bytes 4194304 | tf_op jit(solution)/shard_map/pieces/pallas_call | solution.py:128
  79.5 0.1 collective-permute-start.8
  79.6 0.1 collective-permute-start
  79.7 2.0 %collective-permute-start.4 = (bf16[272,512]{1,0:T(8,128)(2,1)S(1)}, bf16[272,512]{1,0:T(8,128)(2,1)S(1)}, u32[]{:S(2)}, u32[]{:S(2)}) collective-permute-start(bf16[272,512]{1,0:T(8,128)(2,1)S(1)} %attend.1.v0_ref), channel_id=1, source_target_pairs={{0,16},{1,17},{2,18},{3,19},{4,20},{5,21},{6,22},{7,23},{8,24},{9,... | collective-permute-start | bytes 835592 | tf_op jit(solution)/shard_map/ppermute | solution.py:92
  81.7 0.2 collective-permute-start.3
  81.9 0.0 collective-permute-done.10.v2_ref
  81.9 0.3 collective-permute-start.11
  82.2 5.4 %collective-permute-done.8.far_ref = bf16[256,512]{1,0:T(8,128)(2,1)S(1)} collective-permute-done((bf16[256,512]{1,0:T(8,128)(2,1)}, bf16[256,512]{1,0:T(8,128)(2,1)S(1)}, u32[]{:S(2)}, u32[]{:S(2)}) %collective-permute-start.8) | collective-permute-done | bytes 262176 | tf_op jit(solution)/shard_map/ppermute | solution.py:92
  87.6 1.4 %collective-permute-done.4.v2_ref = bf16[272,512]{1,0:T(8,128)(2,1)S(1)} collective-permute-done((bf16[272,512]{1,0:T(8,128)(2,1)S(1)}, bf16[272,512]{1,0:T(8,128)(2,1)S(1)}, u32[]{:S(2)}, u32[]{:S(2)}) %collective-permute-start.4) | collective-permute-done | bytes 278560 | tf_op jit(solution)/shard_map/ppermute | solution.py:92
  89.0 0.0 collective-permute-start.5
  89.0 6.3 %collective-permute-done.9.diagonal_ref = bf16[256,512]{1,0:T(8,128)(2,1)S(1)} collective-permute-done((bf16[256,512]{1,0:T(8,128)(2,1)}, bf16[256,512]{1,0:T(8,128)(2,1)S(1)}, u32[]{:S(2)}, u32[]{:S(2)}) %collective-permute-start.9) | collective-permute-done | bytes 262176 | tf_op jit(solution)/shard_map/ppermute | solution.py:92
  95.3 1.7 %collective-permute-start.1 = (bf16[256,512]{1,0:T(8,128)(2,1)}, bf16[256,512]{1,0:T(8,128)(2,1)S(1)}, u32[]{:S(2)}, u32[]{:S(2)}) collective-permute-start(bf16[256,512]{1,0:T(8,128)(2,1)} %get-tuple-element.14), channel_id=1, source_target_pairs={{0,16},{1,17},{2,18},{3,19},{4,20},{5,21},{6,22},{7,23},{8,24},{9,... | collective-permute-start | bytes 786440 | tf_op jit(solution)/shard_map/ppermute | solution.py:92
  97.0 0.0 collective-permute-done.3.v1_ref
  97.0 0.0 collective-permute-done.11.v3_ref
  97.0 1.0 copy-done
  98.1 0.7 partial_sums.3
  98.8 0.6 collective-permute-start.12
  99.4 5.3 %collective-permute-done.1.far_ref = bf16[256,512]{1,0:T(8,128)(2,1)S(1)} collective-permute-done((bf16[256,512]{1,0:T(8,128)(2,1)}, bf16[256,512]{1,0:T(8,128)(2,1)S(1)}, u32[]{:S(2)}, u32[]{:S(2)}) %collective-permute-start.1) | collective-permute-done | bytes 262176 | tf_op jit(solution)/shard_map/ppermute | solution.py:92
  104.7 5.0 %collective-permute-done.2.diagonal_ref = bf16[256,512]{1,0:T(8,128)(2,1)S(1)} collective-permute-done((bf16[256,512]{1,0:T(8,128)(2,1)}, bf16[256,512]{1,0:T(8,128)(2,1)S(1)}, u32[]{:S(2)}, u32[]{:S(2)}) %collective-permute-start.2) | collective-permute-done | bytes 262176 | tf_op jit(solution)/shard_map/ppermute | solution.py:92
  109.7 0.7 partial_sums.2
  110.4 1.4 collective-permute-start.6
  111.8 2.3 %collective-permute-done.12 = bf16[256,512]{1,0:T(8,128)(2,1)S(1)} collective-permute-done((bf16[256,512]{1,0:T(8,128)(2,1)S(1)}, bf16[256,512]{1,0:T(8,128)(2,1)S(1)}, u32[]{:S(2)}, u32[]{:S(2)}) %collective-permute-start.12) | collective-permute-done | bytes 262176 | tf_op jit(solution)/shard_map/ppermute | solution.py:92
  114.1 0.1 add_convert_fusion
  114.2 2.9 %collective-permute-start.13 = (bf16[128,512]{1,0:T(8,128)(2,1)S(1)}, bf16[128,512]{1,0:T(8,128)(2,1)S(1)}, u32[]{:S(2)}, u32[]{:S(2)}) collective-permute-start(bf16[128,512]{1,0:T(8,128)(2,1)S(1)} %get-tuple-element.22), channel_id=1, source_target_pairs={{0,4},{1,5},{2,6},{3,7},{4,0},{5,1},{6,2},{7,3},{8,12},{9,13},{10,... | collective-permute-start | bytes 393224 | tf_op jit(solution)/shard_map/ppermute | solution.py:92
  117.1 1.3 collective-permute-start.14
  118.5 0.7 collective-permute-done.6
  119.2 0.1 convert_add_fusion
  119.3 1.9 %collective-permute-start.7 = (bf16[128,512]{1,0:T(8,128)(2,1)S(1)}, bf16[128,512]{1,0:T(8,128)(2,1)S(1)}, u32[]{:S(2)}, u32[]{:S(2)}) collective-permute-start(bf16[128,512]{1,0:T(8,128)(2,1)S(1)} %slice.29), channel_id=1, source_target_pairs={{0,2},{1,3},{2,0},{3,1},{4,6},{5,7},{6,4},{7,5},{8,10},{9,11},{10,... | collective-permute-start | bytes 393224 | tf_op jit(solution)/shard_map/ppermute | solution.py:92
  121.1 4.8 %collective-permute-done.13 = bf16[128,512]{1,0:T(8,128)(2,1)S(1)} collective-permute-done((bf16[128,512]{1,0:T(8,128)(2,1)S(1)}, bf16[128,512]{1,0:T(8,128)(2,1)S(1)}, u32[]{:S(2)}, u32[]{:S(2)}) %collective-permute-start.13) | collective-permute-done | bytes 131104 | tf_op jit(solution)/shard_map/ppermute | solution.py:92
  126.0 1.2 collective-permute-done.7
  127.2 0.1 fusion.1
  127.2 1.3 collective-permute-start.15
  128.5 3.7 %collective-permute-done.15 = bf16[128,512]{1,0:T(8,128)(2,1)S(1)} collective-permute-done((bf16[128,512]{1,0:T(8,128)(2,1)S(1)}, bf16[128,512]{1,0:T(8,128)(2,1)S(1)}, u32[]{:S(2)}, u32[]{:S(2)}) %collective-permute-start.15) | collective-permute-done | bytes 131104 | tf_op jit(solution)/shard_map/ppermute | solution.py:92
  132.3 0.1 collective-permute-start.16
  132.4 1.0 balance.1
  133.4 0.5 collective-permute-done.16.near_ref
  133.9 0.7 copy-done.10
  134.6 2.1 %place.1 = f32[512,512]{1,0:T(8,128)} custom-call(bf16[2,128,512]{2,1,0:T(8,128)(2,1)} %copy-done.9, bf16[2,128,512]{2,1,0:T(8,128)(2,1)} %copy-done.10), custom_call_target="tpu_custom_call" | custom-call | bytes 2097152 | tf_op jit(solution)/shard_map/place/pallas_call | solution.py:215
  (20 shorter events, 0.1 us)
Async XLA Ops:
  1.3 1.2 copy-start.1
  2.5 1.2 copy-start.2
  3.7 0.9 copy-start.3
  4.7 0.7 copy-start.4
  5.4 0.7 copy-start.5
  6.0 0.7 copy-start.6
  6.7 0.7 copy-start.7
  7.4 0.7 copy-start.8
  11.6 70.3 %collective-permute-start.10 = (bf16[272,512]{1,0:T(8,128)(2,1)S(1)}, bf16[272,512]{1,0:T(8,128)(2,1)S(1)}, u32[]{:S(2)}, u32[]{:S(2)}) collective-permute-start(bf16[272,512]{1,0:T(8,128)(2,1)S(1)} %attend.1.v0_ref), channel_id=1, source_target_pairs={{0,1},{1,0},{2,3},{3,2},{4,5},{5,4},{6,7},{7,6},{8,9},{9,8},{10,11... | collective-permute-start | bytes 835592 | tf_op jit(solution)/shard_map/ppermute | solution.py:92
  79.5 8.0 %collective-permute-start.8 = (bf16[256,512]{1,0:T(8,128)(2,1)}, bf16[256,512]{1,0:T(8,128)(2,1)S(1)}, u32[]{:S(2)}, u32[]{:S(2)}) collective-permute-start(bf16[256,512]{1,0:T(8,128)(2,1)} %get-tuple-element.18), channel_id=1, source_target_pairs={{0,1},{1,0},{2,3},{3,2},{4,5},{5,4},{6,7},{7,6},{8,9},{9,8},{10,11... | collective-permute-start | bytes 786440 | tf_op jit(solution)/shard_map/ppermute | solution.py:92
  79.6 17.4 %collective-permute-start = (bf16[2,256,512]{2,1,0:T(8,128)(2,1)}, bf16[2,256,512]{2,1,0:T(8,128)(2,1)S(1)}, u32[]{:S(2)}, u32[]{:S(2)}) collective-permute-start(bf16[2,256,512]{2,1,0:T(8,128)(2,1)} %get-tuple-element.13), channel_id=1, source_target_pairs={{0,8},{1,9},{2,10},{3,11},{4,12},{5,13},{6,14},{7,15},{8,0},{9,1},... | collective-permute-start | bytes 1572872 | tf_op jit(solution)/shard_map/ppermute | solution.py:92
  79.7 9.3 %collective-permute-start.4 = (bf16[272,512]{1,0:T(8,128)(2,1)S(1)}, bf16[272,512]{1,0:T(8,128)(2,1)S(1)}, u32[]{:S(2)}, u32[]{:S(2)}) collective-permute-start(bf16[272,512]{1,0:T(8,128)(2,1)S(1)} %attend.1.v0_ref), channel_id=1, source_target_pairs={{0,16},{1,17},{2,18},{3,19},{4,20},{5,21},{6,22},{7,23},{8,24},{9,... | collective-permute-start | bytes 835592 | tf_op jit(solution)/shard_map/ppermute | solution.py:92
  81.7 15.3 %collective-permute-start.3 = (bf16[272,512]{1,0:T(8,128)(2,1)S(1)}, bf16[272,512]{1,0:T(8,128)(2,1)S(1)}, u32[]{:S(2)}, u32[]{:S(2)}) collective-permute-start(bf16[272,512]{1,0:T(8,128)(2,1)S(1)} %attend.1.v0_ref), channel_id=1, source_target_pairs={{0,8},{1,9},{2,10},{3,11},{4,12},{5,13},{6,14},{7,15},{8,0},{9,1},... | collective-permute-start | bytes 835592 | tf_op jit(solution)/shard_map/ppermute | solution.py:92
  81.9 15.1 %collective-permute-start.11 = (bf16[272,512]{1,0:T(8,128)(2,1)S(1)}, bf16[272,512]{1,0:T(8,128)(2,1)S(1)}, u32[]{:S(2)}, u32[]{:S(2)}) collective-permute-start(bf16[272,512]{1,0:T(8,128)(2,1)S(1)} %collective-permute-done.10.v2_ref), channel_id=1, source_target_pairs={{0,8},{1,9},{2,10},{3,11},{4,12},{5,13},{6,14},{7,15},{8,0},{9,1},... | collective-permute-start | bytes 835592 | tf_op jit(solution)/shard_map/ppermute | solution.py:92
  87.6 7.7 %collective-permute-start.9 = (bf16[256,512]{1,0:T(8,128)(2,1)}, bf16[256,512]{1,0:T(8,128)(2,1)S(1)}, u32[]{:S(2)}, u32[]{:S(2)}) collective-permute-start(bf16[256,512]{1,0:T(8,128)(2,1)} %get-tuple-element.19), channel_id=1, source_target_pairs={{0,9},{1,8},{2,11},{3,10},{4,13},{5,12},{6,15},{7,14},{8,1},{9,0},... | collective-permute-start | bytes 786440 | tf_op jit(solution)/shard_map/ppermute | solution.py:92
  89.0 20.7 %collective-permute-start.5 = (bf16[272,512]{1,0:T(8,128)(2,1)S(1)}, bf16[272,512]{1,0:T(8,128)(2,1)S(1)}, u32[]{:S(2)}, u32[]{:S(2)}) collective-permute-start(bf16[272,512]{1,0:T(8,128)(2,1)S(1)} %collective-permute-done.4.v2_ref), channel_id=1, source_target_pairs={{0,8},{1,9},{2,10},{3,11},{4,12},{5,13},{6,14},{7,15},{8,0},{9,1},... | collective-permute-start | bytes 835592 | tf_op jit(solution)/shard_map/ppermute | solution.py:92
  95.3 9.5 %collective-permute-start.1 = (bf16[256,512]{1,0:T(8,128)(2,1)}, bf16[256,512]{1,0:T(8,128)(2,1)S(1)}, u32[]{:S(2)}, u32[]{:S(2)}) collective-permute-start(bf16[256,512]{1,0:T(8,128)(2,1)} %get-tuple-element.14), channel_id=1, source_target_pairs={{0,16},{1,17},{2,18},{3,19},{4,20},{5,21},{6,22},{7,23},{8,24},{9,... | collective-permute-start | bytes 786440 | tf_op jit(solution)/shard_map/ppermute | solution.py:92
  97.0 12.7 %collective-permute-start.2 = (bf16[256,512]{1,0:T(8,128)(2,1)}, bf16[256,512]{1,0:T(8,128)(2,1)S(1)}, u32[]{:S(2)}, u32[]{:S(2)}) collective-permute-start(bf16[256,512]{1,0:T(8,128)(2,1)} %get-tuple-element.15), channel_id=1, source_target_pairs={{0,24},{1,25},{2,26},{3,27},{4,28},{5,29},{6,30},{7,31},{8,16},{9,... | collective-permute-start | bytes 786440 | tf_op jit(solution)/shard_map/ppermute | solution.py:92
  97.0 1.0 copy-start
  98.8 15.3 %collective-permute-start.12 = (bf16[256,512]{1,0:T(8,128)(2,1)S(1)}, bf16[256,512]{1,0:T(8,128)(2,1)S(1)}, u32[]{:S(2)}, u32[]{:S(2)}) collective-permute-start(bf16[256,512]{1,0:T(8,128)(2,1)S(1)} %get-tuple-element.21), channel_id=1, source_target_pairs={{0,16},{1,17},{2,18},{3,19},{4,20},{5,21},{6,22},{7,23},{8,24},{9,... | collective-permute-start | bytes 786440 | tf_op jit(solution)/shard_map/ppermute | solution.py:92
  110.4 8.7 %collective-permute-start.6 = (bf16[256,512]{1,0:T(8,128)(2,1)S(1)}, bf16[256,512]{1,0:T(8,128)(2,1)S(1)}, u32[]{:S(2)}, u32[]{:S(2)}) collective-permute-start(bf16[256,512]{1,0:T(8,128)(2,1)S(1)} %get-tuple-element.17), channel_id=1, source_target_pairs={{0,1},{1,0},{2,3},{3,2},{4,5},{5,4},{6,7},{7,6},{8,9},{9,8},{10,11... | collective-permute-start | bytes 786440 | tf_op jit(solution)/shard_map/ppermute | solution.py:92
  114.2 11.7 %collective-permute-start.13 = (bf16[128,512]{1,0:T(8,128)(2,1)S(1)}, bf16[128,512]{1,0:T(8,128)(2,1)S(1)}, u32[]{:S(2)}, u32[]{:S(2)}) collective-permute-start(bf16[128,512]{1,0:T(8,128)(2,1)S(1)} %get-tuple-element.22), channel_id=1, source_target_pairs={{0,4},{1,5},{2,6},{3,7},{4,0},{5,1},{6,2},{7,3},{8,12},{9,13},{10,... | collective-permute-start | bytes 393224 | tf_op jit(solution)/shard_map/ppermute | solution.py:92
  117.1 8.8 %collective-permute-start.14 = (bf16[128,512]{1,0:T(8,128)(2,1)S(1)}, bf16[128,512]{1,0:T(8,128)(2,1)S(1)}, u32[]{:S(2)}, u32[]{:S(2)}) collective-permute-start(bf16[128,512]{1,0:T(8,128)(2,1)S(1)} %get-tuple-element.23), channel_id=1, source_target_pairs={{0,6},{1,7},{2,4},{3,5},{4,2},{5,3},{6,0},{7,1},{8,14},{9,15},{10,... | collective-permute-start | bytes 393224 | tf_op jit(solution)/shard_map/ppermute | solution.py:92
  119.3 7.9 %collective-permute-start.7 = (bf16[128,512]{1,0:T(8,128)(2,1)S(1)}, bf16[128,512]{1,0:T(8,128)(2,1)S(1)}, u32[]{:S(2)}, u32[]{:S(2)}) collective-permute-start(bf16[128,512]{1,0:T(8,128)(2,1)S(1)} %slice.29), channel_id=1, source_target_pairs={{0,2},{1,3},{2,0},{3,1},{4,6},{5,7},{6,4},{7,5},{8,10},{9,11},{10,... | collective-permute-start | bytes 393224 | tf_op jit(solution)/shard_map/ppermute | solution.py:92
  127.2 5.0 %collective-permute-start.15 = (bf16[128,512]{1,0:T(8,128)(2,1)S(1)}, bf16[128,512]{1,0:T(8,128)(2,1)S(1)}, u32[]{:S(2)}, u32[]{:S(2)}) collective-permute-start(bf16[128,512]{1,0:T(8,128)(2,1)S(1)} %fusion.1), channel_id=1, source_target_pairs={{0,16},{1,17},{2,18},{3,19},{4,20},{5,21},{6,22},{7,23},{8,24},{9,... | collective-permute-start | bytes 393224 | tf_op jit(solution)/shard_map/ppermute | solution.py:92
  132.3 1.6 %copy-start.9 = (bf16[2,128,512]{2,1,0:T(8,128)(2,1)}, bf16[2,128,512]{2,1,0:T(8,128)(2,1)S(1)}, u32[]{:S(2)}) copy-start(bf16[2,128,512]{2,1,0:T(8,128)(2,1)S(1)} %pad_maximum_fusion.pair_ref) | copy-start | bytes 786436
  132.3 1.6 %collective-permute-start.16 = (bf16[2,128,512]{2,1,0:T(8,128)(2,1)S(1)}, bf16[2,128,512]{2,1,0:T(8,128)(2,1)S(1)}, u32[]{:S(2)}, u32[]{:S(2)}) collective-permute-start(bf16[2,128,512]{2,1,0:T(8,128)(2,1)S(1)} %pad_maximum_fusion.pair_ref), channel_id=1, source_target_pairs={{0,8},{1,9},{2,10},{3,11},{4,12},{5,13},{6,14},{7,15},{8,0},{9,1},... | collective-permute-start | bytes 786440 | tf_op jit(solution)/shard_map/ppermute | solution.py:92
  133.9 0.7 copy-start.10

commit v2 on v1

v2 whole, which is shorter than its diff:
```python
import functools

import jax
import jax.numpy as jnp
from jax import lax
from jax.experimental import pallas as pl
from jax.experimental.pallas import tpu as pltpu
from jax.sharding import PartitionSpec as P

D = 4096
HD = 128
CAP = 32
HALF = 128
LANE = 128
INFO = 16
MIB = 1 << 20
BF16 = jnp.bfloat16
F32 = jnp.float32

VMEM = pl.BlockSpec(memory_space=pltpu.VMEM)
HBM = pl.BlockSpec(memory_space=pltpu.HBM)


def attend_group(per_group, span, q, k, g, allowed, factor):
    q_all = jnp.concatenate([q[span, n * HD:(n + 1) * HD] for n in range(per_group)], axis=0)
    scores = lax.dot_general(
        k[span, :], q_all, (((1,), (1,)), ((), ())), preferred_element_type=F32
    ) * HD ** (-0.5)
    probs = []
    weighted = []
    for n in range(per_group):
        own = jnp.where(allowed, scores[:, n * HALF:(n + 1) * HALF], -1e30)
        expo = jnp.exp(own - jnp.max(own, axis=0, keepdims=True))
        probs.append((expo / jnp.sum(expo, axis=0, keepdims=True)).astype(BF16))
        weighted.append((g[span, n * HD:(n + 1) * HD].astype(F32) * factor).astype(BF16))
    return jnp.dot(
        jnp.concatenate(probs, axis=1), jnp.concatenate(weighted, axis=0), preferred_element_type=F32
    ).astype(BF16)


def mask_and_factor(span, loss_ref, exponent_ref, ids_ref, index_ref):
    exponent = exponent_ref[0]
    unscale = jnp.float32(1.0)
    for bit in range(5):
        unscale = unscale * jnp.where((exponent >> bit) & 1 == 1, jnp.float32(2.0 ** -(1 << bit)), 1.0)
    row = lax.broadcasted_iota(jnp.int32, (HALF, HALF), 0)
    col = lax.broadcasted_iota(jnp.int32, (HALF, HALF), 1)
    doc_i = jnp.broadcast_to(ids_ref[:, span], (HALF, HALF))
    allowed = (doc_i == doc_i.T) & (row <= col)
    index = index_ref[:, span]
    factor = jnp.zeros((1, HALF), F32)
    for entry in range(loss_ref.shape[0]):
        factor = jnp.where(index == entry, loss_ref[entry], factor)
    return allowed, jnp.broadcast_to(factor * unscale, (HALF, HALF)).T


def front_kernel(
    split, per_group, loss_hbm, exponent_hbm, start_hbm, rows_hbm, q_hbm, k_hbm, g_hbm, ids_hbm, index_hbm, *rest
):
    if split:
        x_hbm, own_ref, near_ref, y1_ref, x1_ref, *pieces = rest[:11]
        rest = rest[11:]
        v_refs = (own_ref, near_ref, y1_ref, x1_ref)
    else:
        v_refs = rest[:1]
        rest = rest[1:]
    loss_ref, exponent_ref, start_ref, rows_ref, q_ref, k_ref, g_ref, ids_ref, index_ref, sems = rest
    count = 0

    def begin(source, target):
        nonlocal count
        copy = pltpu.make_async_copy(source, target, sems.at[count])
        copy.start()
        count += 1
        return copy

    small = [
        begin(source, target)
        for source, target in (
            (ids_hbm, ids_ref), (index_hbm, index_ref), (loss_hbm, loss_ref), (exponent_hbm, exponent_ref),
            (start_hbm, start_ref), (rows_hbm, rows_ref),
        )
    ]
    groups = k_ref.shape[1] // HD
    wide = per_group * HD
    loads = []
    for group in range(groups):
        some = pl.ds(group * wide, wide)
        one = pl.ds(group * HD, HD)
        loads.append([
            begin(q_hbm.at[:, some], q_ref.at[:, some]),
            begin(k_hbm.at[:, one], k_ref.at[:, one]),
            begin(g_hbm.at[:, some], g_ref.at[:, some]),
        ])
    cuts = []
    if split:
        dp = lax.axis_index("dp")
        fsdp = lax.axis_index("fsdp")

        def cut(target, row, dp_flips, fsdp_flips):
            for far in range(2):
                owner = fsdp ^ fsdp_flips[far]
                column = pl.multiple_of(owner * (4 * LANE) + (dp ^ dp_flips[far]) * LANE, LANE)
                cuts.append(begin(
                    x_hbm.at[:, pl.ds(column, LANE)],
                    target.at[pl.ds(row, 2 * HALF), pl.ds(far * LANE, LANE)],
                ))

        def cut_a(target, row, m, z):
            cut(target, row, (m, m), (z << 1, z << 1 | 1))

        def cut_b(target, row, m, z):
            cut(target, row, (m & 1, m & 1 | 2), (z << 1 | m >> 1, z << 1 | m >> 1))

        a3_1, b3_1, a2_2, a3_2, b2_2, b3_2 = pieces
        cut_a(y1_ref, VROWS, 2, 2)
        cut_b(x1_ref, VROWS, 2, 3)
        cut_a(a3_1, 0, 3, 2)
        cut_b(b3_1, 0, 3, 3)
        for m, ref in ((1, near_ref), (0, own_ref)):
            cut_a(ref, VROWS, m, 2)
            cut_b(ref, VROWS + 256, m, 3)
            cut_a(ref, VROWS + 512, m, 0)
            cut_b(ref, VROWS + 768, m, 1)
        cut_a(a2_2, 0, 2, 0)
        cut_b(b2_2, 0, 2, 1)
        cut_a(a3_2, 0, 3, 0)
        cut_b(b3_2, 0, 3, 1)
    for copy in small:
        copy.wait()
    masks = [
        mask_and_factor(pl.ds(half * HALF, HALF), loss_ref, exponent_ref, ids_ref, index_ref) for half in range(2)
    ]

    def put(group, row, value):
        for ref in v_refs:
            ref[pl.ds((group // 2) * (2 * HALF + INFO) + row, value.shape[0]), pl.ds(group % 2 * HD, HD)] = value

    info_row = lax.broadcasted_iota(jnp.int32, (INFO, HD), 0)
    info = jnp.zeros((INFO, HD), jnp.int32)
    for level in range(min(start_ref.shape[1], INFO // 2)):
        info = jnp.where(info_row == 2 * level, start_ref[0, level], info)
        info = jnp.where(info_row == 2 * level + 1, rows_ref[0, level], info)
    info = info.astype(F32).astype(BF16)
    for group in range(groups):
        for copy in loads[group]:
            copy.wait()
        some = pl.ds(group * wide, wide)
        for half in range(2):
            span = pl.ds(half * HALF, HALF)
            value = attend_group(
                per_group, slice(None), q_ref[span, some], k_ref[span, pl.ds(group * HD, HD)], g_ref[span, some],
                *masks[half],
            )
            put(group, half * HALF, value)
        put(group, 2 * HALF, info)
    for copy in cuts:
        copy.wait()


def front(split, layer_input, query, key, grad, ids, index, loss, exponent, start, rows):
    tokens, key_width = key.shape
    per_group = query.shape[1] // key_width
    groups = key_width // HD
    v_rows = (tokens + INFO) * (groups // 2)
    heights = [v_rows + 4 * tokens, v_rows + 4 * tokens, v_rows + tokens, v_rows + tokens] + [tokens] * 6
    args = [
        loss, exponent, start, rows, query, key, grad, ids.reshape(1, tokens), index.reshape(1, tokens)
    ]
    return pl.pallas_call(
        functools.partial(front_kernel, split, per_group),
        in_specs=[HBM] * (10 if split else 9),
        out_specs=[VMEM] * (10 if split else 1),
        out_shape=[jax.ShapeDtypeStruct((height, 2 * HD), BF16) for height in (heights if split else [v_rows])],
        scratch_shapes=[
            pltpu.SMEM(loss.shape, F32), pltpu.SMEM(exponent.shape, jnp.int32),
            pltpu.SMEM(start.shape, jnp.int32), pltpu.SMEM(rows.shape, jnp.int32),
            pltpu.VMEM(query.shape, BF16), pltpu.VMEM(key.shape, BF16), pltpu.VMEM(grad.shape, BF16),
            pltpu.VMEM((1, tokens), jnp.int32), pltpu.VMEM((1, tokens), jnp.int32),
            pltpu.SemaphoreType.DMA((6 + 3 * groups + 32,)),
        ],
        compiler_params=pltpu.CompilerParams(vmem_limit_bytes=32 * MIB),
        cost_estimate=pl.CostEstimate(flops=600_000_000, bytes_accessed=8 * MIB, transcendentals=500_000),
        name="front",
    )(*(args + [layer_input] if split else args))


CORE, Y, X = 8, 16, 1
VROWS = 2 * (2 * HALF + INFO)


def xor_permute(value, mask):
    count = lax.axis_size("dp") * lax.axis_size("fsdp")
    return lax.ppermute(value, ("dp", "fsdp"), [(i, i ^ mask) for i in range(count)])


def partial_kernel(number, own_ref, near_ref, v2_ref, v3_ref, *rest):
    *far_refs, diagonal_ref, keep_ref, send_ref = rest
    row = VROWS + 256 * number
    far = far_refs[0][...] if far_refs else v2_ref[pl.ds(VROWS, 256), :]
    x = jnp.concatenate([own_ref[pl.ds(row, 256), :], near_ref[pl.ds(row, 256), :], far, diagonal_ref[...]], axis=0)
    for part in range(2):
        v = jnp.concatenate(
            [ref[pl.ds(part * (256 + INFO), 256), :] for ref in (own_ref, near_ref, v2_ref, v3_ref)], axis=0
        )
        total = lax.dot_general(x, v, (((0,), (0,)), ((), ())), preferred_element_type=F32)
        keep_ref[:, pl.ds(256 * part, 256)] = total[:LANE]
        send_ref[:, pl.ds(256 * part, 256)] = total[LANE:].astype(BF16)


def partial_sums(number, *args):
    return pl.pallas_call(
        functools.partial(partial_kernel, number),
        in_specs=[VMEM] * len(args),
        out_specs=[VMEM] * 2,
        out_shape=[jax.ShapeDtypeStruct((LANE, 512), F32), jax.ShapeDtypeStruct((LANE, 512), BF16)],
        compiler_params=pltpu.CompilerParams(vmem_limit_bytes=32 * MIB),
        cost_estimate=pl.CostEstimate(flops=270_000_000, bytes_accessed=2 * MIB, transcendentals=0),
        name="partial_sums",
    )(*args)


def balance_kernel(v0_ref, v1_ref, v2_ref, v3_ref, out_ref):
    refs = (v0_ref, v1_ref, v2_ref, v3_ref)
    tokens = out_ref.shape[0]
    infos = [ref[pl.ds(tokens, INFO), pl.ds(0, HALF)].astype(F32).astype(jnp.int32) for ref in refs]

    def table(device, entry):
        return jnp.broadcast_to(infos[device][entry:entry + 1, :], (HALF, HALF))

    place = lax.broadcasted_iota(jnp.int32, (HALF, HALF), 0) + HALF
    inner = lax.broadcasted_iota(jnp.int32, (HALF, HALF), 1) + HALF

    def source(device, at):
        first = table(device, 0)
        swapped = (at >= first) & (at < first + table(device, 1))
        return swapped, jnp.where(swapped, table(device ^ 1, 0) + at - first, at)

    first = table(0, 2)
    outer = (place >= first) & (place < first + table(0, 3))
    swapped_here, here = source(0, place)
    swapped_there, there = source(2, table(2, 2) + place - first)
    position = jnp.where(outer, there, here)
    device = jnp.where(outer, jnp.where(swapped_there, 3, 2), jnp.where(swapped_here, 1, 0))
    for part in range(2):
        base = part * (tokens + INFO)
        some = pl.ds(256 * part, 256)
        total = None
        for number, ref in enumerate(refs):
            pick = jnp.where((device == number) & (position == inner), 1.0, 0.0).astype(BF16)
            term = jnp.dot(pick, ref[pl.ds(base + HALF, HALF), :], preferred_element_type=F32)
            total = term if total is None else total + term
        out_ref[pl.ds(0, HALF), some] = v0_ref[pl.ds(base, HALF), :]
        out_ref[pl.ds(HALF, HALF), some] = total.astype(BF16)


def balance(values):
    return pl.pallas_call(
        balance_kernel,
        in_specs=[VMEM] * 4,
        out_specs=VMEM,
        out_shape=jax.ShapeDtypeStruct((2 * HALF, 512), BF16),
        compiler_params=pltpu.CompilerParams(vmem_limit_bytes=32 * MIB),
        cost_estimate=pl.CostEstimate(flops=70_000_000, bytes_accessed=MIB, transcendentals=0),
        name="balance",
    )(*values)


def place_kernel(mine_ref, y_ref, near_ref, out_ref):
    dp = lax.axis_index("dp")
    for flip, block in ((0, mine_ref), (2, y_ref), (1, near_ref.at[0]), (3, near_ref.at[1])):
        out_ref[pl.ds(pl.multiple_of((dp ^ flip) * LANE, LANE), LANE), :] = block[...].astype(F32)


def place(mine, from_y, near):
    return pl.pallas_call(
        place_kernel,
        in_specs=[VMEM] * 3,
        out_specs=VMEM,
        out_shape=jax.ShapeDtypeStruct((512, 512), F32),
        compiler_params=pltpu.CompilerParams(vmem_limit_bytes=8 * MIB),
        cost_estimate=pl.CostEstimate(flops=0, bytes_accessed=2 * MIB, transcendentals=0),
        name="place",
    )(mine, from_y, near)


def reduce_by_axis(*args):
    own, near, y1, x1, a3_1, b3_1, a2_2, a3_2, b2_2, b3_2 = front(True, *args)
    y1 = xor_permute(y1, Y)
    x1 = xor_permute(x1, X)
    near = xor_permute(near, CORE)
    a3_1 = xor_permute(a3_1, Y | CORE)
    b3_1 = xor_permute(b3_1, X | CORE)
    a2_2 = xor_permute(a2_2, Y)
    b2_2 = xor_permute(b2_2, X)
    a3_2 = xor_permute(a3_2, Y | CORE)
    b3_2 = xor_permute(b3_2, X | CORE)
    y_core = xor_permute(y1[:VROWS], CORE)
    x_core = xor_permute(x1[:VROWS], CORE)
    keep_a1, send_a1 = partial_sums(0, own, near, y1, y_core, a3_1)
    keep_b1, send_b1 = partial_sums(1, own, near, x1, x_core, b3_1)
    keep_a2, send_a2 = partial_sums(2, own, near, y1, y_core, a2_2, a3_2)
    keep_b2, send_b2 = partial_sums(3, own, near, x1, x_core, b2_2, b3_2)
    z2 = xor_permute((keep_a1 + xor_permute(send_a1, X).astype(F32)).astype(BF16), 4)
    z3 = xor_permute((keep_b1 + xor_permute(send_b1, Y).astype(F32)).astype(BF16), 6)
    total = keep_a2 + xor_permute(send_a2, X).astype(F32)
    z1 = xor_permute((keep_b2 + xor_permute(send_b2, Y).astype(F32)).astype(BF16), 2)
    mine = (total + z1.astype(F32) + (z2.astype(F32) + z3.astype(F32))).astype(BF16)
    from_y = xor_permute(mine, Y)
    grad_value = place(mine, from_y, xor_permute(jnp.stack([mine, from_y]), CORE))
    return grad_value, balance((own, near, y1, y_core))


def swapped(block, axis, distance):
    count = lax.axis_size(axis)
    route = []
    for low in range(count):
        high = low | 1 << distance
        if high != low and high < count:
            route += [(low, high), (high, low)]
    return lax.ppermute(block, axis, route)


def blend_rows(item, incoming, offset, extent):
    inside = (jnp.arange(CAP) < extent)[:, None]
    chosen = jnp.where(inside, incoming, lax.dynamic_slice_in_dim(item, offset, CAP, 0))
    return lax.dynamic_update_slice_in_dim(item, chosen, offset, 0)


def reduce_by_owner(layer_input, *args):
    swap_start, swap_rows = args[-2:]
    tokens = layer_input.shape[0]
    halves = front(False, layer_input, *args)[0].reshape(2, tokens + INFO, 2 * HD)[:, :tokens]
    values = jnp.concatenate([halves[0], halves[1]], axis=1)
    balanced = values
    for level in range(lax.axis_size("dp").bit_length() - 1):
        offset = swap_start[0, level]
        window = lax.dynamic_slice_in_dim(balanced, offset, CAP, 0)
        balanced = blend_rows(balanced, swapped(window, "dp", level), offset, swap_rows[0, level])
    owners = lax.axis_size("fsdp")
    owned = (D + owners - 1) // owners
    padded = jnp.pad(layer_input, ((0, 0), (0, owned * owners - D)))
    arranged = lax.all_to_all(
        padded.reshape(tokens, owners, owned), "fsdp", split_axis=1, concat_axis=0, tiled=True
    )
    block = lax.dot_general(
        arranged.reshape(-1, owned),
        lax.all_gather(values, "fsdp", axis=0, tiled=True),
        (((0,), (0,)), ((), ())),
        preferred_element_type=F32,
    )
    return lax.psum(block, "dp"), balanced


def on_device(layer_input, *args):
    if lax.axis_size("dp") == 4 and lax.axis_size("fsdp") == 8:
        return reduce_by_axis(layer_input, *args)
    return reduce_by_owner(layer_input, *args)


def solution(mesh):
    return jax.shard_map(
        on_device,
        mesh=mesh,
        in_specs=(
            P(("dp", "fsdp"), None),
            P(("dp", "fsdp"), None),
            P(("dp", "fsdp"), None),
            P(("dp", "fsdp"), None),
            P(("dp", "fsdp")),
            P(("dp", "fsdp")),
            P(),
            P(("dp", "fsdp")),
            P(("dp", "fsdp"), None),
            P(("dp", "fsdp"), None),
        ),
        out_specs=(P("fsdp", None), P(("dp", "fsdp"), None)),
        check_vma=False,
    )
```

time: 139 us -> 70.7 us (0.51); the launches traced: 137 us -> 70.4 us
  Pallas kernels: 73.1 us -> 8.22 us
  waiting for transfers between devices: 36.7 us -> 28.6 us
  starting transfers between devices: 16.8 us -> 23.6 us
    pallas_call x5 -> x6, Pallas kernels: 72 us -> 7.21 us  [the longest x1 4.33 us: front(): pl.pallas_call(functools.partial(front_kernel, split, per_group), in_spec...]
    ppermute x17 -> x20, waiting for transfers between devices: 36.7 us -> 28.6 us  [xor_permute(): lax.ppermute(value, ('dp', 'fsdp'), [(i, i ^ mask) for i in range(count)])]
    ppermute x17 -> x20, starting transfers between devices: 16.8 us -> 23.6 us  [xor_permute(): lax.ppermute(value, ('dp', 'fsdp'), [(i, i ^ mask) for i in range(count)])]
    unnamed x22 -> x18, local copies, waits for them, and re-layouts: 8.46 us -> 8.3 us
  transfers between devices with their start and end apart: 17 -> 20, of which waited for: 11 -> 9; matrix products, arithmetic and copies ran while one was open for 0% -> 0% of each run, Pallas kernels for 49% -> 4%
where the time goes in v2:
time: 70.7 us; the launch traced here: 70.4 us
  waiting for transfers between devices  28.6 us (40%)
  starting transfers between devices  23.6 us (33%)
  local copies, waits for them, and re-layouts  8.34 us (12%)
  Pallas kernels  8.22 us (12%)
  between operations  1.41 us (2%)
    ppermute x20, waiting for transfers between devices, xor_permute(): lax.ppermute(value, ('dp', 'fsdp'), [(i, i ^ mask) for i in range(count)])  28.6 us
    ppermute x20, starting transfers between devices, xor_permute(): lax.ppermute(value, ('dp', 'fsdp'), [(i, i ^ mask) for i in range(count)])  23.6 us
    unnamed x18, local copies, waits for them, and re-layouts  8.3 us
    pallas_call x1, Pallas kernels, front(): pl.pallas_call(functools.partial(front_kernel, split, per_group), in_spec...  4.33 us
    pallas_call x4, Pallas kernels, partial_sums(): pl.pallas_call(functools.partial(partial_kernel, number), in_specs=[VMEM]...  1.83 us
  transfers between devices with their start and end apart: 20, of which 9 were waited for; matrix products, arithmetic and copies ran while one was open for 0% of the time, Pallas kernels for 4%

profile of v2, /device:TPU:0, one launch (start us, length us, event | category | flops | bytes accessed | tf_op | source)
XLA Modules:
  0.0 70.4 jit_solution(10147162013480479643)
XLA Ops:
  1.3 1.6 %copy-done = bf16[256,4096]{1,0:T(8,128)(2,1)S(1)} copy-done((bf16[256,4096]{1,0:T(8,128)(2,1)S(1)}, bf16[256,4096]{1,0:T(8,128)(2,1)}, u32[]{:S(2)}) %copy-start) | copy-done | bytes 2097176
  2.9 1.2 %copy-done.1 = bf16[256,2048]{1,0:T(8,128)(2,1)S(1)} copy-done((bf16[256,2048]{1,0:T(8,128)(2,1)S(1)}, bf16[256,2048]{1,0:T(8,128)(2,1)}, u32[]{:S(2)}) %copy-start.1) | copy-done | bytes 1048600
  4.1 1.2 %copy-done.2 = bf16[256,2048]{1,0:T(8,128)(2,1)S(1)} copy-done((bf16[256,2048]{1,0:T(8,128)(2,1)S(1)}, bf16[256,2048]{1,0:T(8,128)(2,1)}, u32[]{:S(2)}) %copy-start.2) | copy-done | bytes 1048600
  5.3 0.9 %copy-done.3 = bf16[256,512]{1,0:T(8,128)(2,1)S(1)} copy-done((bf16[256,512]{1,0:T(8,128)(2,1)S(1)}, bf16[256,512]{1,0:T(8,128)(2,1)}, u32[]{:S(2)}) %copy-start.3) | copy-done | bytes 262168
  6.3 0.7 copy-done.4
  7.0 0.7 copy-done.5
  7.6 0.7 copy-done.6
  8.3 0.7 copy-done.7
  8.9 0.7 copy-done.8
  9.6 4.3 %front.1 = (bf16[1568,256]{1,0:T(8,128)(2,1)S(1)}, bf16[1568,256]{1,0:T(8,128)(2,1)S(1)}, bf16[800,256]{1,0:T(8,128)(2,1)S(1)}, bf16[800,256]{1,0:T(8,128)(2,1)S...) custom-call(f32[16]{0:T(128)S(1)} %copy-done.6, ...), custom_call_target="tpu_custom_call" | custom-call | flops 600000000 | bytes 8388608 | tf_op jit(solution)/shard_map/front/pallas_call | solution.py:170
  13.9 0.5 collective-permute-start
  14.5 2.6 %collective-permute-start.6 = (bf16[800,256]{1,0:T(8,128)(2,1)S(1)}, bf16[800,256]{1,0:T(8,128)(2,1)S(1)}, u32[]{:S(2)}, u32[]{:S(2)}) collective-permute-start(bf16[800,256]{1,0:T(8,128)(2,1)S(1)} %get-tuple-element.27), channel_id=1, source_target_pairs={{0,1},{1,0},{2,3},{3,2},{4,5},{5,4},{6,7},{7,6},{8,9},{9,8},{10,11... | collective-permute-start | bytes 1228808 | tf_op jit(solution)/shard_map/ppermute | solution.py:194
  17.0 1.5 %collective-permute-start.1 = (bf16[800,256]{1,0:T(8,128)(2,1)S(1)}, bf16[800,256]{1,0:T(8,128)(2,1)S(1)}, u32[]{:S(2)}, u32[]{:S(2)}) collective-permute-start(bf16[800,256]{1,0:T(8,128)(2,1)S(1)} %get-tuple-element.22), channel_id=1, source_target_pairs={{0,16},{1,17},{2,18},{3,19},{4,20},{5,21},{6,22},{7,23},{8,24},{9,... | collective-permute-start | bytes 1228808 | tf_op jit(solution)/shard_map/ppermute | solution.py:194
  18.5 8.5 %collective-permute-done.6.v2_ref = bf16[800,256]{1,0:T(8,128)(2,1)S(1)} collective-permute-done((bf16[800,256]{1,0:T(8,128)(2,1)S(1)}, bf16[800,256]{1,0:T(8,128)(2,1)S(1)}, u32[]{:S(2)}, u32[]{:S(2)}) %collective-permute-start.6) | collective-permute-done | bytes 409632 | tf_op jit(solution)/shard_map/ppermute | solution.py:194
  27.1 0.1 collective-permute-start.7
  27.2 1.8 %collective-permute-start.8 = (bf16[256,256]{1,0:T(8,128)(2,1)S(1)}, bf16[256,256]{1,0:T(8,128)(2,1)S(1)}, u32[]{:S(2)}, u32[]{:S(2)}) collective-permute-start(bf16[256,256]{1,0:T(8,128)(2,1)S(1)} %get-tuple-element.28), channel_id=1, source_target_pairs={{0,1},{1,0},{2,3},{3,2},{4,5},{5,4},{6,7},{7,6},{8,9},{9,8},{10,11... | collective-permute-start | bytes 393224 | tf_op jit(solution)/shard_map/ppermute | solution.py:194
  29.0 0.2 collective-permute-start.2
  29.3 0.2 collective-permute-start.9
  29.5 4.1 %collective-permute-done.8.rest_0_ = bf16[256,256]{1,0:T(8,128)(2,1)S(1)} collective-permute-done((bf16[256,256]{1,0:T(8,128)(2,1)S(1)}, bf16[256,256]{1,0:T(8,128)(2,1)S(1)}, u32[]{:S(2)}, u32[]{:S(2)}) %collective-permute-start.8) | collective-permute-done | bytes 131104 | tf_op jit(solution)/shard_map/ppermute | solution.py:194
  33.5 0.6 collective-permute-start.12
  34.1 1.3 %collective-permute-done.9.rest_1_ = bf16[256,256]{1,0:T(8,128)(2,1)S(1)} collective-permute-done((bf16[256,256]{1,0:T(8,128)(2,1)S(1)}, bf16[256,256]{1,0:T(8,128)(2,1)S(1)}, u32[]{:S(2)}, u32[]{:S(2)}) %collective-permute-start.9) | collective-permute-done | bytes 131104 | tf_op jit(solution)/shard_map/ppermute | solution.py:194
  35.4 1.6 %collective-permute-start.15 = (bf16[256,256]{1,0:T(8,128)(2,1)S(1)}, bf16[256,256]{1,0:T(8,128)(2,1)S(1)}, u32[]{:S(2)}, u32[]{:S(2)}) collective-permute-start(bf16[256,256]{1,0:T(8,128)(2,1)S(1)} %get-tuple-element.35), channel_id=1, source_target_pairs={{0,9},{1,8},{2,11},{3,10},{4,13},{5,12},{6,15},{7,14},{8,1},{9,0},... | collective-permute-start | bytes 393224 | tf_op jit(solution)/shard_map/ppermute | solution.py:194
  37.1 0.0 collective-permute-done.7.v3_ref
  37.1 1.5 %collective-permute-start.3 = (bf16[256,256]{1,0:T(8,128)(2,1)S(1)}, bf16[256,256]{1,0:T(8,128)(2,1)S(1)}, u32[]{:S(2)}, u32[]{:S(2)}) collective-permute-start(bf16[256,256]{1,0:T(8,128)(2,1)S(1)} %get-tuple-element.23), channel_id=1, source_target_pairs={{0,16},{1,17},{2,18},{3,19},{4,20},{5,21},{6,22},{7,23},{8,24},{9,... | collective-permute-start | bytes 393224 | tf_op jit(solution)/shard_map/ppermute | solution.py:194
  38.6 0.1 collective-permute-start.4
  38.7 0.5 partial_sums.5
  39.2 1.6 %collective-permute-start.10 = (bf16[128,512]{1,0:T(8,128)(2,1)S(1)}, bf16[128,512]{1,0:T(8,128)(2,1)S(1)}, u32[]{:S(2)}, u32[]{:S(2)}) collective-permute-start(bf16[128,512]{1,0:T(8,128)(2,1)S(1)} %get-tuple-element.31), channel_id=1, source_target_pairs={{0,16},{1,17},{2,18},{3,19},{4,20},{5,21},{6,22},{7,23},{8,24},{9,... | collective-permute-start | bytes 393224 | tf_op jit(solution)/shard_map/ppermute | solution.py:194
  40.7 0.5 partial_sums.6
  41.2 1.3 %collective-permute-start.13 = (bf16[128,512]{1,0:T(8,128)(2,1)S(1)}, bf16[128,512]{1,0:T(8,128)(2,1)S(1)}, u32[]{:S(2)}, u32[]{:S(2)}) collective-permute-start(bf16[128,512]{1,0:T(8,128)(2,1)S(1)} %get-tuple-element.34), channel_id=1, source_target_pairs={{0,1},{1,0},{2,3},{3,2},{4,5},{5,4},{6,7},{7,6},{8,9},{9,8},{10,11... | collective-permute-start | bytes 393224 | tf_op jit(solution)/shard_map/ppermute | solution.py:194
  42.5 0.0 collective-permute-done.15.rest_0_
  42.5 0.5 partial_sums.7
  43.0 1.1 %collective-permute-start.16 = (bf16[128,512]{1,0:T(8,128)(2,1)S(1)}, bf16[128,512]{1,0:T(8,128)(2,1)S(1)}, u32[]{:S(2)}, u32[]{:S(2)}) collective-permute-start(bf16[128,512]{1,0:T(8,128)(2,1)S(1)} %get-tuple-element.37), channel_id=1, source_target_pairs={{0,16},{1,17},{2,18},{3,19},{4,20},{5,21},{6,22},{7,23},{8,24},{9,... | collective-permute-start | bytes 393224 | tf_op jit(solution)/shard_map/ppermute | solution.py:194
  44.1 1.1 %collective-permute-done.4.rest_1_ = bf16[256,256]{1,0:T(8,128)(2,1)S(1)} collective-permute-done((bf16[256,256]{1,0:T(8,128)(2,1)S(1)}, bf16[256,256]{1,0:T(8,128)(2,1)S(1)}, u32[]{:S(2)}, u32[]{:S(2)}) %collective-permute-start.4) | collective-permute-done | bytes 131104 | tf_op jit(solution)/shard_map/ppermute | solution.py:194
  45.3 0.5 partial_sums.4
  45.7 1.4 %collective-permute-start.5 = (bf16[128,512]{1,0:T(8,128)(2,1)S(1)}, bf16[128,512]{1,0:T(8,128)(2,1)S(1)}, u32[]{:S(2)}, u32[]{:S(2)}) collective-permute-start(bf16[128,512]{1,0:T(8,128)(2,1)S(1)} %get-tuple-element.26), channel_id=1, source_target_pairs={{0,1},{1,0},{2,3},{3,2},{4,5},{5,4},{6,7},{7,6},{8,9},{9,8},{10,11... | collective-permute-start | bytes 393224 | tf_op jit(solution)/shard_map/ppermute | solution.py:194
  47.2 1.9 %collective-permute-done.10 = bf16[128,512]{1,0:T(8,128)(2,1)S(1)} collective-permute-done((bf16[128,512]{1,0:T(8,128)(2,1)S(1)}, bf16[128,512]{1,0:T(8,128)(2,1)S(1)}, u32[]{:S(2)}, u32[]{:S(2)}) %collective-permute-start.10) | collective-permute-done | bytes 131104 | tf_op jit(solution)/shard_map/ppermute | solution.py:194
  49.1 1.6 %collective-permute-start.11 = (bf16[128,512]{1,0:T(8,128)(2,1)S(1)}, bf16[128,512]{1,0:T(8,128)(2,1)S(1)}, u32[]{:S(2)}, u32[]{:S(2)}) collective-permute-start(bf16[128,512]{1,0:T(8,128)(2,1)S(1)} %add_convert_fusion.3), channel_id=1, source_target_pairs={{0,2},{1,3},{2,0},{3,1},{4,6},{5,7},{6,4},{7,5},{8,10},{9,11},{10,... | collective-permute-start | bytes 393224 | tf_op jit(solution)/shard_map/ppermute | solution.py:194
  50.7 2.7 %collective-permute-start.14 = (bf16[128,512]{1,0:T(8,128)(2,1)S(1)}, bf16[128,512]{1,0:T(8,128)(2,1)S(1)}, u32[]{:S(2)}, u32[]{:S(2)}) collective-permute-start(bf16[128,512]{1,0:T(8,128)(2,1)S(1)} %add_convert_fusion.2), channel_id=1, source_target_pairs={{0,4},{1,5},{2,6},{3,7},{4,0},{5,1},{6,2},{7,3},{8,12},{9,13},{10,... | collective-permute-start | bytes 393224 | tf_op jit(solution)/shard_map/ppermute | solution.py:194
  53.4 1.4 %collective-permute-start.17 = (bf16[128,512]{1,0:T(8,128)(2,1)S(1)}, bf16[128,512]{1,0:T(8,128)(2,1)S(1)}, u32[]{:S(2)}, u32[]{:S(2)}) collective-permute-start(bf16[128,512]{1,0:T(8,128)(2,1)S(1)} %add_convert_fusion.1), channel_id=1, source_target_pairs={{0,6},{1,7},{2,4},{3,5},{4,2},{5,3},{6,0},{7,1},{8,14},{9,15},{10,... | collective-permute-start | bytes 393224 | tf_op jit(solution)/shard_map/ppermute | solution.py:194
  54.9 0.7 collective-permute-done.11
  55.5 7.1 %collective-permute-done.14 = bf16[128,512]{1,0:T(8,128)(2,1)S(1)} collective-permute-done((bf16[128,512]{1,0:T(8,128)(2,1)S(1)}, bf16[128,512]{1,0:T(8,128)(2,1)S(1)}, u32[]{:S(2)}, u32[]{:S(2)}) %collective-permute-start.14) | collective-permute-done | bytes 131104 | tf_op jit(solution)/shard_map/ppermute | solution.py:194
  62.6 0.1 add_convert_fusion.mine_ref
  62.7 1.6 %collective-permute-start.18 = (bf16[128,512]{1,0:T(8,128)(2,1)S(1)}, bf16[128,512]{1,0:T(8,128)(2,1)S(1)}, u32[]{:S(2)}, u32[]{:S(2)}) collective-permute-start(bf16[128,512]{1,0:T(8,128)(2,1)S(1)} %add_convert_fusion.mine_ref), channel_id=1, source_target_pairs={{0,16},{1,17},{2,18},{3,19},{4,20},{5,21},{6,22},{7,23},{8,24},{9,... | collective-permute-start | bytes 393224 | tf_op jit(solution)/shard_map/ppermute | solution.py:194
  64.3 3.4 %collective-permute-done.18.y_ref = bf16[128,512]{1,0:T(8,128)(2,1)S(1)} collective-permute-done((bf16[128,512]{1,0:T(8,128)(2,1)S(1)}, bf16[128,512]{1,0:T(8,128)(2,1)S(1)}, u32[]{:S(2)}, u32[]{:S(2)}) %collective-permute-start.18) | collective-permute-done | bytes 131104 | tf_op jit(solution)/shard_map/ppermute | solution.py:194
  67.8 0.1 collective-permute-start.19
  67.8 1.0 %balance.1 = bf16[256,512]{1,0:T(8,128)(2,1)} custom-call(bf16[1568,256]{1,0:T(8,128)(2,1)S(1)} %get-tuple-element.20.own_ref.v0_ref, bf16[1568,256]{1,0:T(8,128)(2,1)S(1)} %collective-permute-done.near_ref.v1_ref, bf16[800,256]{1,0:T(8,128)(2,1)S(1)} %collective-permute-done.1.v2_ref, bf16[544,256]{1,0:T(8,128)(2,1)S(1)} %collective-permute-done.2.v3_ref), custom_call_target="tpu_custom_call" | custom-call | flops 70000000 | bytes 1048576 | tf_op jit(solution)/shard_map/balance/pallas_call | solution.py:258
  68.9 0.5 collective-permute-done.19.near_ref
  69.4 1.0 %place.1 = f32[512,512]{1,0:T(8,128)} custom-call(bf16[128,512]{1,0:T(8,128)(2,1)S(1)} %add_convert_fusion.mine_ref, bf16[128,512]{1,0:T(8,128)(2,1)S(1)} %collective-permute-done.18.y_ref, bf16[2,128,512]{2,1,0:T(8,128)(2,1)S(1)} %collective-permute-done.19.near_ref), custom_call_target="tpu_custom_call" | custom-call | bytes 2097152 | tf_op jit(solution)/shard_map/place/pallas_call | solution.py:276
  (24 shorter events, 0.2 us)
Async XLA Ops:
  1.3 1.6 %copy-start = (bf16[256,4096]{1,0:T(8,128)(2,1)S(1)}, bf16[256,4096]{1,0:T(8,128)(2,1)}, u32[]{:S(2)}) copy-start(bf16[256,4096]{1,0:T(8,128)(2,1)} %rest_0_.1) | copy-start | bytes 6291460
  2.9 1.2 %copy-start.1 = (bf16[256,2048]{1,0:T(8,128)(2,1)S(1)}, bf16[256,2048]{1,0:T(8,128)(2,1)}, u32[]{:S(2)}) copy-start(bf16[256,2048]{1,0:T(8,128)(2,1)} %q_hbm.1) | copy-start | bytes 3145732
  4.1 1.2 %copy-start.2 = (bf16[256,2048]{1,0:T(8,128)(2,1)S(1)}, bf16[256,2048]{1,0:T(8,128)(2,1)}, u32[]{:S(2)}) copy-start(bf16[256,2048]{1,0:T(8,128)(2,1)} %g_hbm.1) | copy-start | bytes 3145732
  5.3 0.9 %copy-start.3 = (bf16[256,512]{1,0:T(8,128)(2,1)S(1)}, bf16[256,512]{1,0:T(8,128)(2,1)}, u32[]{:S(2)}) copy-start(bf16[256,512]{1,0:T(8,128)(2,1)} %k_hbm.1) | copy-start | bytes 786436
  6.3 0.7 copy-start.4
  7.0 0.7 copy-start.5
  7.6 0.7 copy-start.6
  8.3 0.7 copy-start.7
  8.9 0.7 copy-start.8
  13.9 24.7 %collective-permute-start = (bf16[1568,256]{1,0:T(8,128)(2,1)S(1)}, bf16[1568,256]{1,0:T(8,128)(2,1)S(1)}, u32[]{:S(2)}, u32[]{:S(2)}) collective-permute-start(bf16[1568,256]{1,0:T(8,128)(2,1)S(1)} %get-tuple-element.21), channel_id=1, source_target_pairs={{0,8},{1,9},{2,10},{3,11},{4,12},{5,13},{6,14},{7,15},{8,0},{9,1},... | collective-permute-start | bytes 2408456 | tf_op jit(solution)/shard_map/ppermute | solution.py:194
  14.5 12.6 %collective-permute-start.6 = (bf16[800,256]{1,0:T(8,128)(2,1)S(1)}, bf16[800,256]{1,0:T(8,128)(2,1)S(1)}, u32[]{:S(2)}, u32[]{:S(2)}) collective-permute-start(bf16[800,256]{1,0:T(8,128)(2,1)S(1)} %get-tuple-element.27), channel_id=1, source_target_pairs={{0,1},{1,0},{2,3},{3,2},{4,5},{5,4},{6,7},{7,6},{8,9},{9,8},{10,11... | collective-permute-start | bytes 1228808 | tf_op jit(solution)/shard_map/ppermute | solution.py:194
  17.0 12.0 %collective-permute-start.1 = (bf16[800,256]{1,0:T(8,128)(2,1)S(1)}, bf16[800,256]{1,0:T(8,128)(2,1)S(1)}, u32[]{:S(2)}, u32[]{:S(2)}) collective-permute-start(bf16[800,256]{1,0:T(8,128)(2,1)S(1)} %get-tuple-element.22), channel_id=1, source_target_pairs={{0,16},{1,17},{2,18},{3,19},{4,20},{5,21},{6,22},{7,23},{8,24},{9,... | collective-permute-start | bytes 1228808 | tf_op jit(solution)/shard_map/ppermute | solution.py:194
  27.1 10.0 %collective-permute-start.7 = (bf16[544,256]{1,0:T(8,128)(2,1)S(1)}, bf16[544,256]{1,0:T(8,128)(2,1)S(1)}, u32[]{:S(2)}, u32[]{:S(2)}) collective-permute-start(bf16[544,256]{1,0:T(8,128)(2,1)S(1)} %slice.9), channel_id=1, source_target_pairs={{0,8},{1,9},{2,10},{3,11},{4,12},{5,13},{6,14},{7,15},{8,0},{9,1},... | collective-permute-start | bytes 835592 | tf_op jit(solution)/shard_map/ppermute | solution.py:194
  27.2 6.4 %collective-permute-start.8 = (bf16[256,256]{1,0:T(8,128)(2,1)S(1)}, bf16[256,256]{1,0:T(8,128)(2,1)S(1)}, u32[]{:S(2)}, u32[]{:S(2)}) collective-permute-start(bf16[256,256]{1,0:T(8,128)(2,1)S(1)} %get-tuple-element.28), channel_id=1, source_target_pairs={{0,1},{1,0},{2,3},{3,2},{4,5},{5,4},{6,7},{7,6},{8,9},{9,8},{10,11... | collective-permute-start | bytes 393224 | tf_op jit(solution)/shard_map/ppermute | solution.py:194
  29.0 11.7 %collective-permute-start.2 = (bf16[544,256]{1,0:T(8,128)(2,1)S(1)}, bf16[544,256]{1,0:T(8,128)(2,1)S(1)}, u32[]{:S(2)}, u32[]{:S(2)}) collective-permute-start(bf16[544,256]{1,0:T(8,128)(2,1)S(1)} %slice.8), channel_id=1, source_target_pairs={{0,8},{1,9},{2,10},{3,11},{4,12},{5,13},{6,14},{7,15},{8,0},{9,1},... | collective-permute-start | bytes 835592 | tf_op jit(solution)/shard_map/ppermute | solution.py:194
  29.3 6.2 %collective-permute-start.9 = (bf16[256,256]{1,0:T(8,128)(2,1)S(1)}, bf16[256,256]{1,0:T(8,128)(2,1)S(1)}, u32[]{:S(2)}, u32[]{:S(2)}) collective-permute-start(bf16[256,256]{1,0:T(8,128)(2,1)S(1)} %get-tuple-element.29), channel_id=1, source_target_pairs={{0,9},{1,8},{2,11},{3,10},{4,13},{5,12},{6,15},{7,14},{8,1},{9,0},... | collective-permute-start | bytes 393224 | tf_op jit(solution)/shard_map/ppermute | solution.py:194
  33.5 5.6 %collective-permute-start.12 = (bf16[256,256]{1,0:T(8,128)(2,1)S(1)}, bf16[256,256]{1,0:T(8,128)(2,1)S(1)}, u32[]{:S(2)}, u32[]{:S(2)}) collective-permute-start(bf16[256,256]{1,0:T(8,128)(2,1)S(1)} %get-tuple-element.32), channel_id=1, source_target_pairs={{0,24},{1,25},{2,26},{3,27},{4,28},{5,29},{6,30},{7,31},{8,16},{9,... | collective-permute-start | bytes 393224 | tf_op jit(solution)/shard_map/ppermute | solution.py:194
  35.4 7.1 %collective-permute-start.15 = (bf16[256,256]{1,0:T(8,128)(2,1)S(1)}, bf16[256,256]{1,0:T(8,128)(2,1)S(1)}, u32[]{:S(2)}, u32[]{:S(2)}) collective-permute-start(bf16[256,256]{1,0:T(8,128)(2,1)S(1)} %get-tuple-element.35), channel_id=1, source_target_pairs={{0,9},{1,8},{2,11},{3,10},{4,13},{5,12},{6,15},{7,14},{8,1},{9,0},... | collective-permute-start | bytes 393224 | tf_op jit(solution)/shard_map/ppermute | solution.py:194
  37.1 7.0 %collective-permute-start.3 = (bf16[256,256]{1,0:T(8,128)(2,1)S(1)}, bf16[256,256]{1,0:T(8,128)(2,1)S(1)}, u32[]{:S(2)}, u32[]{:S(2)}) collective-permute-start(bf16[256,256]{1,0:T(8,128)(2,1)S(1)} %get-tuple-element.23), channel_id=1, source_target_pairs={{0,16},{1,17},{2,18},{3,19},{4,20},{5,21},{6,22},{7,23},{8,24},{9,... | collective-permute-start | bytes 393224 | tf_op jit(solution)/shard_map/ppermute | solution.py:194
  38.6 6.7 %collective-permute-start.4 = (bf16[256,256]{1,0:T(8,128)(2,1)S(1)}, bf16[256,256]{1,0:T(8,128)(2,1)S(1)}, u32[]{:S(2)}, u32[]{:S(2)}) collective-permute-start(bf16[256,256]{1,0:T(8,128)(2,1)S(1)} %get-tuple-element.24), channel_id=1, source_target_pairs={{0,24},{1,25},{2,26},{3,27},{4,28},{5,29},{6,30},{7,31},{8,16},{9,... | collective-permute-start | bytes 393224 | tf_op jit(solution)/shard_map/ppermute | solution.py:194
  39.2 9.9 %collective-permute-start.10 = (bf16[128,512]{1,0:T(8,128)(2,1)S(1)}, bf16[128,512]{1,0:T(8,128)(2,1)S(1)}, u32[]{:S(2)}, u32[]{:S(2)}) collective-permute-start(bf16[128,512]{1,0:T(8,128)(2,1)S(1)} %get-tuple-element.31), channel_id=1, source_target_pairs={{0,16},{1,17},{2,18},{3,19},{4,20},{5,21},{6,22},{7,23},{8,24},{9,... | collective-permute-start | bytes 393224 | tf_op jit(solution)/shard_map/ppermute | solution.py:194
  41.2 9.5 %collective-permute-start.13 = (bf16[128,512]{1,0:T(8,128)(2,1)S(1)}, bf16[128,512]{1,0:T(8,128)(2,1)S(1)}, u32[]{:S(2)}, u32[]{:S(2)}) collective-permute-start(bf16[128,512]{1,0:T(8,128)(2,1)S(1)} %get-tuple-element.34), channel_id=1, source_target_pairs={{0,1},{1,0},{2,3},{3,2},{4,5},{5,4},{6,7},{7,6},{8,9},{9,8},{10,11... | collective-permute-start | bytes 393224 | tf_op jit(solution)/shard_map/ppermute | solution.py:194
  43.0 10.4 %collective-permute-start.16 = (bf16[128,512]{1,0:T(8,128)(2,1)S(1)}, bf16[128,512]{1,0:T(8,128)(2,1)S(1)}, u32[]{:S(2)}, u32[]{:S(2)}) collective-permute-start(bf16[128,512]{1,0:T(8,128)(2,1)S(1)} %get-tuple-element.37), channel_id=1, source_target_pairs={{0,16},{1,17},{2,18},{3,19},{4,20},{5,21},{6,22},{7,23},{8,24},{9,... | collective-permute-start | bytes 393224 | tf_op jit(solution)/shard_map/ppermute | solution.py:194
  45.7 9.1 %collective-permute-start.5 = (bf16[128,512]{1,0:T(8,128)(2,1)S(1)}, bf16[128,512]{1,0:T(8,128)(2,1)S(1)}, u32[]{:S(2)}, u32[]{:S(2)}) collective-permute-start(bf16[128,512]{1,0:T(8,128)(2,1)S(1)} %get-tuple-element.26), channel_id=1, source_target_pairs={{0,1},{1,0},{2,3},{3,2},{4,5},{5,4},{6,7},{7,6},{8,9},{9,8},{10,11... | collective-permute-start | bytes 393224 | tf_op jit(solution)/shard_map/ppermute | solution.py:194
  49.1 6.5 %collective-permute-start.11 = (bf16[128,512]{1,0:T(8,128)(2,1)S(1)}, bf16[128,512]{1,0:T(8,128)(2,1)S(1)}, u32[]{:S(2)}, u32[]{:S(2)}) collective-permute-start(bf16[128,512]{1,0:T(8,128)(2,1)S(1)} %add_convert_fusion.3), channel_id=1, source_target_pairs={{0,2},{1,3},{2,0},{3,1},{4,6},{5,7},{6,4},{7,5},{8,10},{9,11},{10,... | collective-permute-start | bytes 393224 | tf_op jit(solution)/shard_map/ppermute | solution.py:194
  50.7 11.9 %collective-permute-start.14 = (bf16[128,512]{1,0:T(8,128)(2,1)S(1)}, bf16[128,512]{1,0:T(8,128)(2,1)S(1)}, u32[]{:S(2)}, u32[]{:S(2)}) collective-permute-start(bf16[128,512]{1,0:T(8,128)(2,1)S(1)} %add_convert_fusion.2), channel_id=1, source_target_pairs={{0,4},{1,5},{2,6},{3,7},{4,0},{5,1},{6,2},{7,3},{8,12},{9,13},{10,... | collective-permute-start | bytes 393224 | tf_op jit(solution)/shard_map/ppermute | solution.py:194
  53.4 9.2 %collective-permute-start.17 = (bf16[128,512]{1,0:T(8,128)(2,1)S(1)}, bf16[128,512]{1,0:T(8,128)(2,1)S(1)}, u32[]{:S(2)}, u32[]{:S(2)}) collective-permute-start(bf16[128,512]{1,0:T(8,128)(2,1)S(1)} %add_convert_fusion.1), channel_id=1, source_target_pairs={{0,6},{1,7},{2,4},{3,5},{4,2},{5,3},{6,0},{7,1},{8,14},{9,15},{10,... | collective-permute-start | bytes 393224 | tf_op jit(solution)/shard_map/ppermute | solution.py:194
  62.7 5.0 %collective-permute-start.18 = (bf16[128,512]{1,0:T(8,128)(2,1)S(1)}, bf16[128,512]{1,0:T(8,128)(2,1)S(1)}, u32[]{:S(2)}, u32[]{:S(2)}) collective-permute-start(bf16[128,512]{1,0:T(8,128)(2,1)S(1)} %add_convert_fusion.mine_ref), channel_id=1, source_target_pairs={{0,16},{1,17},{2,18},{3,19},{4,20},{5,21},{6,22},{7,23},{8,24},{9,... | collective-permute-start | bytes 393224 | tf_op jit(solution)/shard_map/ppermute | solution.py:194
  67.8 1.6 %collective-permute-start.19 = (bf16[2,128,512]{2,1,0:T(8,128)(2,1)S(1)}, bf16[2,128,512]{2,1,0:T(8,128)(2,1)S(1)}, u32[]{:S(2)}, u32[]{:S(2)}) collective-permute-start(bf16[2,128,512]{2,1,0:T(8,128)(2,1)S(1)} %pad_maximum_fusion), channel_id=1, source_target_pairs={{0,8},{1,9},{2,10},{3,11},{4,12},{5,13},{6,14},{7,15},{8,0},{9,1},... | collective-permute-start | bytes 786440 | tf_op jit(solution)/shard_map/ppermute | solution.py:194

commit v3 on v2

--- a/solution.py
+++ b/solution.py
@@ -14,6 +14,7 @@
 LANE = 128
 INFO = 16
 MIB = 1 << 20
+FREE = pl.CostEstimate(flops=0, bytes_accessed=0, transcendentals=0)
 BF16 = jnp.bfloat16
 F32 = jnp.float32
 
@@ -58,9 +59,9 @@
     split, per_group, loss_hbm, exponent_hbm, start_hbm, rows_hbm, q_hbm, k_hbm, g_hbm, ids_hbm, index_hbm, *rest
 ):
     if split:
-        x_hbm, own_ref, near_ref, y1_ref, x1_ref, *pieces = rest[:11]
-        rest = rest[11:]
-        v_refs = (own_ref, near_ref, y1_ref, x1_ref)
+        x_hbm, own1_ref, near1_ref, own2_ref, near2_ref = rest[:5]
+        rest = rest[5:]
+        v_refs = (own1_ref, near1_ref)
     else:
         v_refs = rest[:1]
         rest = rest[1:]
@@ -97,35 +98,22 @@
         dp = lax.axis_index("dp")
         fsdp = lax.axis_index("fsdp")
 
-        def cut(target, row, dp_flips, fsdp_flips):
-            for far in range(2):
-                owner = fsdp ^ fsdp_flips[far]
-                column = pl.multiple_of(owner * (4 * LANE) + (dp ^ dp_flips[far]) * LANE, LANE)
+        def cut(target, row, core, z, flips):
+            for at, (y, x) in enumerate(flips):
+                owner = fsdp ^ (z << 1 | x)
+                column = pl.multiple_of(owner * (4 * LANE) + (dp ^ (y << 1 | core)) * LANE, LANE)
                 cuts.append(begin(
                     x_hbm.at[:, pl.ds(column, LANE)],
-                    target.at[pl.ds(row, 2 * HALF), pl.ds(far * LANE, LANE)],
+                    target.at[pl.ds(row, 2 * HALF), pl.ds(at * LANE, LANE)],
                 ))
 
-        def cut_a(target, row, m, z):
-            cut(target, row, (m, m), (z << 1, z << 1 | 1))
-
-        def cut_b(target, row, m, z):
-            cut(target, row, (m & 1, m & 1 | 2), (z << 1 | m >> 1, z << 1 | m >> 1))
-
-        a3_1, b3_1, a2_2, a3_2, b2_2, b3_2 = pieces
-        cut_a(y1_ref, VROWS, 2, 2)
-        cut_b(x1_ref, VROWS, 2, 3)
-        cut_a(a3_1, 0, 3, 2)
-        cut_b(b3_1, 0, 3, 3)
-        for m, ref in ((1, near_ref), (0, own_ref)):
-            cut_a(ref, VROWS, m, 2)
-            cut_b(ref, VROWS + 256, m, 3)
-            cut_a(ref, VROWS + 512, m, 0)
-            cut_b(ref, VROWS + 768, m, 1)
-        cut_a(a2_2, 0, 2, 0)
-        cut_b(b2_2, 0, 2, 1)
-        cut_a(a3_2, 0, 3, 0)
-        cut_b(b3_2, 0, 3, 1)
+        for core, row, z_a, z_b, target in (
+            (1, VROWS, 2, 3, near1_ref), (0, VROWS, 2, 3, own1_ref), (1, 0, 0, 1, near2_ref), (0, 0, 0, 1, own2_ref)
+        ):
+            cut(target, row, core, z_a, ((1, 1), (1, 0)))
+            cut(target, row + 256, core, z_b, ((1, 1), (0, 1)))
+            cut(target, row + 512, core, z_a, ((0, 1), (0, 0)))
+            cut(target, row + 768, core, z_b, ((1, 0), (0, 0)))
     for copy in small:
         copy.wait()
     masks = [
@@ -163,14 +151,14 @@
     per_group = query.shape[1] // key_width
     groups = key_width // HD
     v_rows = (tokens + INFO) * (groups // 2)
-    heights = [v_rows + 4 * tokens, v_rows + 4 * tokens, v_rows + tokens, v_rows + tokens] + [tokens] * 6
+    heights = [v_rows + 4 * tokens, v_rows + 4 * tokens, 4 * tokens, 4 * tokens]
     args = [
         loss, exponent, start, rows, query, key, grad, ids.reshape(1, tokens), index.reshape(1, tokens)
     ]
     return pl.pallas_call(
         functools.partial(front_kernel, split, per_group),
         in_specs=[HBM] * (10 if split else 9),
-        out_specs=[VMEM] * (10 if split else 1),
+        out_specs=[VMEM] * (4 if split else 1),
         out_shape=[jax.ShapeDtypeStruct((height, 2 * HD), BF16) for height in (heights if split else [v_rows])],
         scratch_shapes=[
             pltpu.SMEM(loss.shape, F32), pltpu.SMEM(exponent.shape, jnp.int32),
@@ -180,9 +168,12 @@
             pltpu.SemaphoreType.DMA((6 + 3 * groups + 32,)),
         ],
         compiler_params=pltpu.CompilerParams(vmem_limit_bytes=32 * MIB),
-        cost_estimate=pl.CostEstimate(flops=600_000_000, bytes_accessed=8 * MIB, transcendentals=500_000),
+        cost_estimate=FREE,
         name="front",
-    )(*(args + [layer_input] if split else args))
+    )(*[
+        arg if arg is exponent else pltpu.with_memory_space_constraint(arg, pltpu.HBM)
+        for arg in (args + [layer_input] if split else args)
+    ])
 
 
 CORE, Y, X = 8, 16, 1
@@ -194,76 +185,93 @@
     return lax.ppermute(value, ("dp", "fsdp"), [(i, i ^ mask) for i in range(count)])
 
 
-def partial_kernel(number, own_ref, near_ref, v2_ref, v3_ref, *rest):
-    *far_refs, diagonal_ref, keep_ref, send_ref = rest
-    row = VROWS + 256 * number
-    far = far_refs[0][...] if far_refs else v2_ref[pl.ds(VROWS, 256), :]
-    x = jnp.concatenate([own_ref[pl.ds(row, 256), :], near_ref[pl.ds(row, 256), :], far, diagonal_ref[...]], axis=0)
-    for part in range(2):
-        v = jnp.concatenate(
-            [ref[pl.ds(part * (256 + INFO), 256), :] for ref in (own_ref, near_ref, v2_ref, v3_ref)], axis=0
-        )
-        total = lax.dot_general(x, v, (((0,), (0,)), ((), ())), preferred_element_type=F32)
-        keep_ref[:, pl.ds(256 * part, 256)] = total[:LANE]
-        send_ref[:, pl.ds(256 * part, 256)] = total[LANE:].astype(BF16)
-
-
-def partial_sums(number, *args):
-    return pl.pallas_call(
-        functools.partial(partial_kernel, number),
-        in_specs=[VMEM] * len(args),
+def partial_kernel(row, own_ref, near_ref, v0_ref, v1_ref, a_ref, b_ref):
+    for number, out_ref in enumerate((a_ref, b_ref)):
+        some = pl.ds(row + 256 * number, 256)
+        x = jnp.concatenate([own_ref[some, :], near_ref[some, :]], axis=0)
+        for part in range(2):
+            v = jnp.concatenate([ref[pl.ds(part * (256 + INFO), 256), :] for ref in (v0_ref, v1_ref)], axis=0)
+            total = lax.dot_general(x, v, (((0,), (0,)), ((), ())), preferred_element_type=F32)
+            out_ref[:, pl.ds(256 * part, 256)] = total.astype(out_ref.dtype)
+
+
+def partial_sums(row, dtype, own, near, v0, v1):
+    return pl.pallas_call(
+        functools.partial(partial_kernel, row),
+        in_specs=[VMEM] * 4,
         out_specs=[VMEM] * 2,
-        out_shape=[jax.ShapeDtypeStruct((LANE, 512), F32), jax.ShapeDtypeStruct((LANE, 512), BF16)],
+        out_shape=[jax.ShapeDtypeStruct((256, 512), dtype)] * 2,
         compiler_params=pltpu.CompilerParams(vmem_limit_bytes=32 * MIB),
-        cost_estimate=pl.CostEstimate(flops=270_000_000, bytes_accessed=2 * MIB, transcendentals=0),
+        cost_estimate=FREE,
         name="partial_sums",
-    )(*args)
-
-
-def balance_kernel(v0_ref, v1_ref, v2_ref, v3_ref, out_ref):
-    refs = (v0_ref, v1_ref, v2_ref, v3_ref)
+    )(own, near, v0, v1)
+
+
+def inner_swap_kernel(v0_ref, v1_ref, out_ref, window_ref):
     tokens = out_ref.shape[0]
-    infos = [ref[pl.ds(tokens, INFO), pl.ds(0, HALF)].astype(F32).astype(jnp.int32) for ref in refs]
+    infos = [ref[pl.ds(tokens, INFO), pl.ds(0, HALF)].astype(F32).astype(jnp.int32) for ref in (v0_ref, v1_ref)]
 
     def table(device, entry):
         return jnp.broadcast_to(infos[device][entry:entry + 1, :], (HALF, HALF))
 
     place = lax.broadcasted_iota(jnp.int32, (HALF, HALF), 0) + HALF
     inner = lax.broadcasted_iota(jnp.int32, (HALF, HALF), 1) + HALF
-
-    def source(device, at):
-        first = table(device, 0)
-        swapped = (at >= first) & (at < first + table(device, 1))
-        return swapped, jnp.where(swapped, table(device ^ 1, 0) + at - first, at)
-
-    first = table(0, 2)
-    outer = (place >= first) & (place < first + table(0, 3))
-    swapped_here, here = source(0, place)
-    swapped_there, there = source(2, table(2, 2) + place - first)
-    position = jnp.where(outer, there, here)
-    device = jnp.where(outer, jnp.where(swapped_there, 3, 2), jnp.where(swapped_here, 1, 0))
+    first = table(0, 0)
+    moved = (place >= first) & (place < first + table(0, 1))
+    stays = jnp.where(~moved & (place == inner), 1.0, 0.0).astype(BF16)
+    comes = jnp.where(moved & (place + table(1, 0) - first == inner), 1.0, 0.0).astype(BF16)
+    taken = jnp.where(place - HALF + table(0, 2) == inner, 1.0, 0.0).astype(BF16)[:CAP]
     for part in range(2):
         base = part * (tokens + INFO)
         some = pl.ds(256 * part, 256)
-        total = None
-        for number, ref in enumerate(refs):
-            pick = jnp.where((device == number) & (position == inner), 1.0, 0.0).astype(BF16)
-            term = jnp.dot(pick, ref[pl.ds(base + HALF, HALF), :], preferred_element_type=F32)
-            total = term if total is None else total + term
+        rows = (
+            jnp.dot(stays, v0_ref[pl.ds(base + HALF, HALF), :], preferred_element_type=F32)
+            + jnp.dot(comes, v1_ref[pl.ds(base + HALF, HALF), :], preferred_element_type=F32)
+        ).astype(BF16)
         out_ref[pl.ds(0, HALF), some] = v0_ref[pl.ds(base, HALF), :]
-        out_ref[pl.ds(HALF, HALF), some] = total.astype(BF16)
-
-
-def balance(values):
-    return pl.pallas_call(
-        balance_kernel,
-        in_specs=[VMEM] * 4,
+        out_ref[pl.ds(HALF, HALF), some] = rows
+        window_ref[:, some] = jnp.dot(taken, rows, preferred_element_type=F32).astype(BF16)
+
+
+def inner_swap(v0, v1):
+    return pl.pallas_call(
+        inner_swap_kernel,
+        in_specs=[VMEM] * 2,
+        out_specs=[VMEM] * 2,
+        out_shape=[jax.ShapeDtypeStruct((2 * HALF, 512), BF16), jax.ShapeDtypeStruct((CAP, 512), BF16)],
+        compiler_params=pltpu.CompilerParams(vmem_limit_bytes=8 * MIB),
+        cost_estimate=FREE,
+        name="inner_swap",
+    )(v0, v1)
+
+
+def outer_swap_kernel(v0_ref, rows_ref, window_ref, out_ref):
+    tokens = out_ref.shape[0]
+    info = v0_ref[pl.ds(tokens, INFO), pl.ds(0, HALF)].astype(F32).astype(jnp.int32)
+    first = jnp.broadcast_to(info[2:3, :], (HALF, HALF))
+    extent = jnp.broadcast_to(info[3:4, :], (HALF, HALF))
+    place = lax.broadcasted_iota(jnp.int32, (HALF, HALF), 0) + HALF
+    inner = lax.broadcasted_iota(jnp.int32, (HALF, HALF), 1)
+    moved = (place >= first) & (place < first + extent)
+    stays = jnp.where(~moved & (place == inner + HALF), 1.0, 0.0).astype(BF16)
+    comes = jnp.where(moved & (place - first == inner), 1.0, 0.0).astype(BF16)[:, :CAP]
+    out_ref[pl.ds(0, HALF), :] = rows_ref[pl.ds(0, HALF), :]
+    out_ref[pl.ds(HALF, HALF), :] = (
+        jnp.dot(stays, rows_ref[pl.ds(HALF, HALF), :], preferred_element_type=F32)
+        + jnp.dot(comes, window_ref[...], preferred_element_type=F32)
+    ).astype(BF16)
+
+
+def outer_swap(v0, rows, window):
+    return pl.pallas_call(
+        outer_swap_kernel,
+        in_specs=[VMEM] * 3,
         out_specs=VMEM,
-        out_shape=jax.ShapeDtypeStruct((2 * HALF, 512), BF16),
-        compiler_params=pltpu.CompilerParams(vmem_limit_bytes=32 * MIB),
-        cost_estimate=pl.CostEstimate(flops=70_000_000, bytes_accessed=MIB, transcendentals=0),
-        name="balance",
-    )(*values)
+        out_shape=jax.ShapeDtypeStruct(rows.shape, BF16),
+        compiler_params=pltpu.CompilerParams(vmem_limit_bytes=8 * MIB),
+        cost_estimate=FREE,
+        name="outer_swap",
+    )(v0, rows, window)
 
 
 def place_kernel(mine_ref, y_ref, near_ref, out_ref):
@@ -279,36 +287,38 @@
         out_specs=VMEM,
         out_shape=jax.ShapeDtypeStruct((512, 512), F32),
         compiler_params=pltpu.CompilerParams(vmem_limit_bytes=8 * MIB),
-        cost_estimate=pl.CostEstimate(flops=0, bytes_accessed=2 * MIB, transcendentals=0),
+        cost_estimate=FREE,
         name="place",
     )(mine, from_y, near)
 
 
 def reduce_by_axis(*args):
-    own, near, y1, x1, a3_1, b3_1, a2_2, a3_2, b2_2, b3_2 = front(True, *args)
-    y1 = xor_permute(y1, Y)
-    x1 = xor_permute(x1, X)
-    near = xor_permute(near, CORE)
-    a3_1 = xor_permute(a3_1, Y | CORE)
-    b3_1 = xor_permute(b3_1, X | CORE)
-    a2_2 = xor_permute(a2_2, Y)
-    b2_2 = xor_permute(b2_2, X)
-    a3_2 = xor_permute(a3_2, Y | CORE)
-    b3_2 = xor_permute(b3_2, X | CORE)
-    y_core = xor_permute(y1[:VROWS], CORE)
-    x_core = xor_permute(x1[:VROWS], CORE)
-    keep_a1, send_a1 = partial_sums(0, own, near, y1, y_core, a3_1)
-    keep_b1, send_b1 = partial_sums(1, own, near, x1, x_core, b3_1)
-    keep_a2, send_a2 = partial_sums(2, own, near, y1, y_core, a2_2, a3_2)
-    keep_b2, send_b2 = partial_sums(3, own, near, x1, x_core, b2_2, b3_2)
-    z2 = xor_permute((keep_a1 + xor_permute(send_a1, X).astype(F32)).astype(BF16), 4)
-    z3 = xor_permute((keep_b1 + xor_permute(send_b1, Y).astype(F32)).astype(BF16), 6)
-    total = keep_a2 + xor_permute(send_a2, X).astype(F32)
-    z1 = xor_permute((keep_b2 + xor_permute(send_b2, Y).astype(F32)).astype(BF16), 2)
-    mine = (total + z1.astype(F32) + (z2.astype(F32) + z3.astype(F32))).astype(BF16)
+    own1, near1, own2, near2 = front(True, *args)
+    near1 = xor_permute(near1, CORE)
+    near2 = xor_permute(near2, CORE)
+    send_a1, send_b1 = partial_sums(VROWS, BF16, own1, near1, own1, near1)
+    send_a2, send_b2 = partial_sums(0, BF16, own2, near2, own1, near1)
+    keep_a1, keep_b1 = partial_sums(VROWS + 512, F32, own1, near1, own1, near1)
+    keep_a2, keep_b2 = partial_sums(512, F32, own2, near2, own1, near1)
+    half_a1 = keep_a1 + xor_permute(send_a1, Y).astype(F32)
+    half_b1 = keep_b1 + xor_permute(send_b1, X).astype(F32)
+    half_a2 = keep_a2 + xor_permute(send_a2, Y).astype(F32)
+    half_b2 = keep_b2 + xor_permute(send_b2, X).astype(F32)
+
+    def other(half, mask):
+        return half[LANE:] + xor_permute(half[:LANE].astype(BF16), mask).astype(F32)
+
+    z2 = xor_permute(other(half_a1, X).astype(BF16), 4)
+    z3 = xor_permute(other(half_b1, Y).astype(BF16), 6)
+    z1 = xor_permute(other(half_b2, Y).astype(BF16), 2)
+    z0 = other(half_a2, X)
+    rows, window = inner_swap(own1, near1)
+    value_grad = outer_swap(own1, rows, xor_permute(window, Y))
+    z1, value_grad = lax.optimization_barrier((z1, value_grad))
+    mine = (z0 + z1.astype(F32) + (z2.astype(F32) + z3.astype(F32))).astype(BF16)
     from_y = xor_permute(mine, Y)
     grad_value = place(mine, from_y, xor_permute(jnp.stack([mine, from_y]), CORE))
-    return grad_value, balance((own, near, y1, y_core))
+    return grad_value, value_grad
 
 
 def swapped(block, axis, distance):

time: 70.7 us -> 51.1 us (0.72)
  waiting for transfers between devices: 28.6 us -> 19.4 us
  local copies, waits for them, and re-layouts: 8.34 us -> 0.08 us
  starting transfers between devices: 23.6 us -> 20.9 us
    ppermute x20 -> x16, waiting for transfers between devices: 28.6 us -> 19.4 us  [xor_permute(): lax.ppermute(value, ('dp', 'fsdp'), [(i, i ^ mask) for i in range(count)])]
    unnamed x18 -> x0, local copies, waits for them, and re-layouts: 8.3 us -> none
    ppermute x20 -> x16, starting transfers between devices: 23.6 us -> 20.9 us  [xor_permute(): lax.ppermute(value, ('dp', 'fsdp'), [(i, i ^ mask) for i in range(count)])]
    pallas_call x5 -> x6, Pallas kernels: 2.84 us -> 3.25 us  [the longest x4 1.83 us: partial_sums(): pl.pallas_call(functools.partial(partial_kernel, row), in_specs=[VMEM] *...]
  transfers between devices with their start and end apart: 20 -> 16, of which waited for: 9 -> 10; matrix products, arithmetic and copies ran while one was open for 0% -> 1% of each run, Pallas kernels for 4% -> 5%
where the time goes in v3:
time: 51.1 us; the launch traced here: 50.9 us
  starting transfers between devices  20.9 us (41%)
  waiting for transfers between devices  19.4 us (38%)
  Pallas kernels  8.68 us (17%)
  between operations  1.42 us (3%)
    ppermute x16, starting transfers between devices, xor_permute(): lax.ppermute(value, ('dp', 'fsdp'), [(i, i ^ mask) for i in range(count)])  20.9 us
    ppermute x16, waiting for transfers between devices, xor_permute(): lax.ppermute(value, ('dp', 'fsdp'), [(i, i ^ mask) for i in range(count)])  19.4 us
    pallas_call x1, Pallas kernels, front(): pl.pallas_call(functools.partial(front_kernel, split, per_group), in_spec...  4.39 us
    pallas_call x4, Pallas kernels, partial_sums(): pl.pallas_call(functools.partial(partial_kernel, row), in_specs=[VMEM] *...  1.83 us
    pallas_call x1, Pallas kernels, place(): pl.pallas_call(place_kernel, in_specs=[VMEM] * 3, out_specs=VMEM, out_sha...  1.05 us
  transfers between devices with their start and end apart: 16, of which 10 were waited for; matrix products, arithmetic and copies ran while one was open for 1% of the time, Pallas kernels for 5%

profile of v3, /device:TPU:0, one launch (start us, length us, event | category | flops | bytes accessed | tf_op | source)
XLA Modules:
  0.0 50.9 jit_solution(8930572275069227318)
XLA Ops:
  1.3 4.4 %front.1 = (bf16[1568,256]{1,0:T(8,128)(2,1)S(1)}, bf16[1568,256]{1,0:T(8,128)(2,1)S(1)}, bf16[1024,256]{1,0:T(8,128)(2,1)S(1)}, bf16[1024,256]{1,0:T(8,128)(2,1)S(1)}) custom-call(f32[16]{0:T(128)} %loss_hbm.1, s32[1]{0:T(128)S(6)} %copy.12.exponent_hbm, s32[1,2]{1,0:T(1,128)} %start_hbm.1, s32[1,2]{1,0:T(1,128)} %rows_hbm.1, bf16[256,2048]{1,0:T(8,128)(2,1)} %q_hbm.1, ...), custom_call_target="tpu_custom_call" | custom-call | tf_op jit(solution)/shard_map/front/pallas_call | solution.py:158
  5.7 0.5 %collective-permute-start.1 = (bf16[1568,256]{1,0:T(8,128)(2,1)S(1)}, bf16[1568,256]{1,0:T(8,128)(2,1)S(1)}, u32[]{:S(2)}, u32[]{:S(2)}) collective-permute-start(bf16[1568,256]{1,0:T(8,128)(2,1)S(1)} %get-tuple-element.21), channel_id=1, source_target_pairs={{0,8},{1,9},{2,10},{3,11},{4,12},{5,13},{6,14},{7,15},{8,0},{9,1},... | collective-permute-start | bytes 2408456 | tf_op jit(solution)/shard_map/ppermute | solution.py:185
  6.2 0.1 collective-permute-start
  6.3 2.6 %collective-permute-done.near_ref = bf16[1024,256]{1,0:T(8,128)(2,1)S(1)} collective-permute-done((bf16[1024,256]{1,0:T(8,128)(2,1)S(1)}, bf16[1024,256]{1,0:T(8,128)(2,1)S(1)}, u32[]{:S(2)}, u32[]{:S(2)}) %collective-permute-start) | collective-permute-done | bytes 524320 | tf_op jit(solution)/shard_map/ppermute | solution.py:185
  8.9 0.0 collective-permute-done.1.v1_ref.near_ref
  8.9 0.5 partial_sums.5
  9.3 2.9 %collective-permute-start.4 = (bf16[256,512]{1,0:T(8,128)(2,1)S(1)}, bf16[256,512]{1,0:T(8,128)(2,1)S(1)}, u32[]{:S(2)}, u32[]{:S(2)}) collective-permute-start(bf16[256,512]{1,0:T(8,128)(2,1)S(1)} %get-tuple-element.25), channel_id=1, source_target_pairs={{0,1},{1,0},{2,3},{3,2},{4,5},{5,4},{6,7},{7,6},{8,9},{9,8},{10,11... | collective-permute-start | bytes 786440 | tf_op jit(solution)/shard_map/ppermute | solution.py:185
  12.3 0.5 partial_sums.7
  12.7 1.6 %collective-permute-start.8 = (bf16[256,512]{1,0:T(8,128)(2,1)S(1)}, bf16[256,512]{1,0:T(8,128)(2,1)S(1)}, u32[]{:S(2)}, u32[]{:S(2)}) collective-permute-start(bf16[256,512]{1,0:T(8,128)(2,1)S(1)} %get-tuple-element.30), channel_id=1, source_target_pairs={{0,16},{1,17},{2,18},{3,19},{4,20},{5,21},{6,22},{7,23},{8,24},{9,... | collective-permute-start | bytes 786440 | tf_op jit(solution)/shard_map/ppermute | solution.py:185
  14.3 0.5 %collective-permute-start.11 = (bf16[256,512]{1,0:T(8,128)(2,1)S(1)}, bf16[256,512]{1,0:T(8,128)(2,1)S(1)}, u32[]{:S(2)}, u32[]{:S(2)}) collective-permute-start(bf16[256,512]{1,0:T(8,128)(2,1)S(1)} %get-tuple-element.32), channel_id=1, source_target_pairs={{0,1},{1,0},{2,3},{3,2},{4,5},{5,4},{6,7},{7,6},{8,9},{9,8},{10,11... | collective-permute-start | bytes 786440 | tf_op jit(solution)/shard_map/ppermute | solution.py:185
  14.9 0.1 collective-permute-start.2
  14.9 0.5 partial_sums.4
  15.4 0.5 partial_sums.6
  15.9 3.5 %collective-permute-done.4 = bf16[256,512]{1,0:T(8,128)(2,1)S(1)} collective-permute-done((bf16[256,512]{1,0:T(8,128)(2,1)S(1)}, bf16[256,512]{1,0:T(8,128)(2,1)S(1)}, u32[]{:S(2)}, u32[]{:S(2)}) %collective-permute-start.4) | collective-permute-done | bytes 262176 | tf_op jit(solution)/shard_map/ppermute | solution.py:185
  19.4 0.1 convert_add_fusion.2
  19.5 2.2 %collective-permute-start.5 = (bf16[128,512]{1,0:T(8,128)(2,1)S(1)}, bf16[128,512]{1,0:T(8,128)(2,1)S(1)}, u32[]{:S(2)}, u32[]{:S(2)}) collective-permute-start(bf16[128,512]{1,0:T(8,128)(2,1)S(1)} %slice.66), channel_id=1, source_target_pairs={{0,16},{1,17},{2,18},{3,19},{4,20},{5,21},{6,22},{7,23},{8,24},{9,... | collective-permute-start | bytes 393224 | tf_op jit(solution)/shard_map/ppermute | solution.py:185
  21.6 0.4 collective-permute-done.8
  22.0 0.1 convert_add_fusion.1
  22.1 1.2 %collective-permute-start.9 = (bf16[128,512]{1,0:T(8,128)(2,1)S(1)}, bf16[128,512]{1,0:T(8,128)(2,1)S(1)}, u32[]{:S(2)}, u32[]{:S(2)}) collective-permute-start(bf16[128,512]{1,0:T(8,128)(2,1)S(1)} %slice.65), channel_id=1, source_target_pairs={{0,1},{1,0},{2,3},{3,2},{4,5},{5,4},{6,7},{7,6},{8,9},{9,8},{10,11... | collective-permute-start | bytes 393224 | tf_op jit(solution)/shard_map/ppermute | solution.py:185
  23.3 1.7 %collective-permute-done.11 = bf16[256,512]{1,0:T(8,128)(2,1)S(1)} collective-permute-done((bf16[256,512]{1,0:T(8,128)(2,1)S(1)}, bf16[256,512]{1,0:T(8,128)(2,1)S(1)}, u32[]{:S(2)}, u32[]{:S(2)}) %collective-permute-start.11) | collective-permute-done | bytes 262176 | tf_op jit(solution)/shard_map/ppermute | solution.py:185
  25.0 0.1 convert_add_fusion
  25.1 2.2 %collective-permute-start.12 = (bf16[128,512]{1,0:T(8,128)(2,1)S(1)}, bf16[128,512]{1,0:T(8,128)(2,1)S(1)}, u32[]{:S(2)}, u32[]{:S(2)}) collective-permute-start(bf16[128,512]{1,0:T(8,128)(2,1)S(1)} %slice.64), channel_id=1, source_target_pairs={{0,16},{1,17},{2,18},{3,19},{4,20},{5,21},{6,22},{7,23},{8,24},{9,... | collective-permute-start | bytes 393224 | tf_op jit(solution)/shard_map/ppermute | solution.py:185
  27.2 0.4 collective-permute-done.2
  27.6 0.1 convert_add_fusion.3
  27.7 1.2 %collective-permute-start.3 = (bf16[128,512]{1,0:T(8,128)(2,1)S(1)}, bf16[128,512]{1,0:T(8,128)(2,1)S(1)}, u32[]{:S(2)}, u32[]{:S(2)}) collective-permute-start(bf16[128,512]{1,0:T(8,128)(2,1)S(1)} %slice.67), channel_id=1, source_target_pairs={{0,1},{1,0},{2,3},{3,2},{4,5},{5,4},{6,7},{7,6},{8,9},{9,8},{10,11... | collective-permute-start | bytes 393224 | tf_op jit(solution)/shard_map/ppermute | solution.py:185
  28.9 1.5 %collective-permute-done.5 = bf16[128,512]{1,0:T(8,128)(2,1)S(1)} collective-permute-done((bf16[128,512]{1,0:T(8,128)(2,1)S(1)}, bf16[128,512]{1,0:T(8,128)(2,1)S(1)}, u32[]{:S(2)}, u32[]{:S(2)}) %collective-permute-start.5) | collective-permute-done | bytes 131104 | tf_op jit(solution)/shard_map/ppermute | solution.py:185
  30.5 1.6 %collective-permute-start.6 = (bf16[128,512]{1,0:T(8,128)(2,1)S(1)}, bf16[128,512]{1,0:T(8,128)(2,1)S(1)}, u32[]{:S(2)}, u32[]{:S(2)}) collective-permute-start(bf16[128,512]{1,0:T(8,128)(2,1)S(1)} %fusion.2), channel_id=1, source_target_pairs={{0,2},{1,3},{2,0},{3,1},{4,6},{5,7},{6,4},{7,5},{8,10},{9,11},{10,... | collective-permute-start | bytes 393224 | tf_op jit(solution)/shard_map/ppermute | solution.py:185
  32.1 0.0 collective-permute-done.9
  32.1 2.7 %collective-permute-start.10 = (bf16[128,512]{1,0:T(8,128)(2,1)S(1)}, bf16[128,512]{1,0:T(8,128)(2,1)S(1)}, u32[]{:S(2)}, u32[]{:S(2)}) collective-permute-start(bf16[128,512]{1,0:T(8,128)(2,1)S(1)} %fusion.1), channel_id=1, source_target_pairs={{0,4},{1,5},{2,6},{3,7},{4,0},{5,1},{6,2},{7,3},{8,12},{9,13},{10,... | collective-permute-start | bytes 393224 | tf_op jit(solution)/shard_map/ppermute | solution.py:185
  34.8 0.0 collective-permute-done.12
  34.8 1.0 %collective-permute-start.13 = (bf16[128,512]{1,0:T(8,128)(2,1)S(1)}, bf16[128,512]{1,0:T(8,128)(2,1)S(1)}, u32[]{:S(2)}, u32[]{:S(2)}) collective-permute-start(bf16[128,512]{1,0:T(8,128)(2,1)S(1)} %fusion), channel_id=1, source_target_pairs={{0,6},{1,7},{2,4},{3,5},{4,2},{5,3},{6,0},{7,1},{8,14},{9,15},{10,... | collective-permute-start | bytes 393224 | tf_op jit(solution)/shard_map/ppermute | solution.py:185
  35.8 0.5 inner_swap.1
  36.3 1.5 %collective-permute-start.7 = (bf16[32,512]{1,0:T(8,128)(2,1)S(1)}, bf16[32,512]{1,0:T(8,128)(2,1)S(1)}, u32[]{:S(2)}, u32[]{:S(2)}) collective-permute-start(bf16[32,512]{1,0:T(8,128)(2,1)S(1)} %get-tuple-element.27), channel_id=1, source_target_pairs={{0,16},{1,17},{2,18},{3,19},{4,20},{5,21},{6,22},{7,23},{8,24},{9,... | collective-permute-start | bytes 98312 | tf_op jit(solution)/shard_map/ppermute | solution.py:185
  37.9 2.4 %collective-permute-done.7.window_ref = bf16[32,512]{1,0:T(8,128)(2,1)S(1)} collective-permute-done((bf16[32,512]{1,0:T(8,128)(2,1)S(1)}, bf16[32,512]{1,0:T(8,128)(2,1)S(1)}, u32[]{:S(2)}, u32[]{:S(2)}) %collective-permute-start.7) | collective-permute-done | bytes 32800 | tf_op jit(solution)/shard_map/ppermute | solution.py:185
  40.2 0.9 %outer_swap.1 = bf16[256,512]{1,0:T(8,128)(2,1)} custom-call(bf16[1568,256]{1,0:T(8,128)(2,1)S(1)} %get-tuple-element.20.v0_ref.own_ref, bf16[256,512]{1,0:T(8,128)(2,1)S(1)} %get-tuple-element.26.rows_ref, bf16[32,512]{1,0:T(8,128)(2,1)S(1)} %collective-permute-done.7.window_ref), custom_call_target="tpu_custom_call" | custom-call | tf_op jit(solution)/shard_map/outer_swap/pallas_call | solution.py:266
  41.2 0.0 collective-permute-done.6
  41.2 0.0 collective-permute-done.3
  41.2 1.9 %collective-permute-done.10 = bf16[128,512]{1,0:T(8,128)(2,1)S(1)} collective-permute-done((bf16[128,512]{1,0:T(8,128)(2,1)S(1)}, bf16[128,512]{1,0:T(8,128)(2,1)S(1)}, u32[]{:S(2)}, u32[]{:S(2)}) %collective-permute-start.10) | collective-permute-done | bytes 131104 | tf_op jit(solution)/shard_map/ppermute | solution.py:185
  43.1 0.0 collective-permute-done.13
  43.1 0.1 fusion.5.mine_ref
  43.2 1.6 %collective-permute-start.14 = (bf16[128,512]{1,0:T(8,128)(2,1)S(1)}, bf16[128,512]{1,0:T(8,128)(2,1)S(1)}, u32[]{:S(2)}, u32[]{:S(2)}) collective-permute-start(bf16[128,512]{1,0:T(8,128)(2,1)S(1)} %fusion.5.mine_ref), channel_id=1, source_target_pairs={{0,16},{1,17},{2,18},{3,19},{4,20},{5,21},{6,22},{7,23},{8,24},{9,... | collective-permute-start | bytes 393224 | tf_op jit(solution)/shard_map/ppermute | solution.py:185
  44.8 3.4 %collective-permute-done.14.y_ref = bf16[128,512]{1,0:T(8,128)(2,1)S(1)} collective-permute-done((bf16[128,512]{1,0:T(8,128)(2,1)S(1)}, bf16[128,512]{1,0:T(8,128)(2,1)S(1)}, u32[]{:S(2)}, u32[]{:S(2)}) %collective-permute-start.14) | collective-permute-done | bytes 131104 | tf_op jit(solution)/shard_map/ppermute | solution.py:185
  48.3 0.1 collective-permute-start.15
  48.3 1.5 %collective-permute-done.15.near_ref = bf16[2,128,512]{2,1,0:T(8,128)(2,1)S(1)} collective-permute-done((bf16[2,128,512]{2,1,0:T(8,128)(2,1)S(1)}, bf16[2,128,512]{2,1,0:T(8,128)(2,1)S(1)}, u32[]{:S(2)}, u32[]{:S(2)}) %collective-permute-start.15) | collective-permute-done | bytes 262176 | tf_op jit(solution)/shard_map/ppermute | solution.py:185
  49.9 1.0 %place.1 = f32[512,512]{1,0:T(8,128)} custom-call(bf16[128,512]{1,0:T(8,128)(2,1)S(1)} %fusion.5.mine_ref, bf16[128,512]{1,0:T(8,128)(2,1)S(1)} %collective-permute-done.14.y_ref, bf16[2,128,512]{2,1,0:T(8,128)(2,1)S(1)} %collective-permute-done.15.near_ref), custom_call_target="tpu_custom_call" | custom-call | tf_op jit(solution)/shard_map/place/pallas_call | solution.py:284
  (8 shorter events, 0.2 us)
Async XLA Ops:
  5.7 3.2 %collective-permute-start.1 = (bf16[1568,256]{1,0:T(8,128)(2,1)S(1)}, bf16[1568,256]{1,0:T(8,128)(2,1)S(1)}, u32[]{:S(2)}, u32[]{:S(2)}) collective-permute-start(bf16[1568,256]{1,0:T(8,128)(2,1)S(1)} %get-tuple-element.21), channel_id=1, source_target_pairs={{0,8},{1,9},{2,10},{3,11},{4,12},{5,13},{6,14},{7,15},{8,0},{9,1},... | collective-permute-start | bytes 2408456 | tf_op jit(solution)/shard_map/ppermute | solution.py:185
  6.2 2.7 %collective-permute-start = (bf16[1024,256]{1,0:T(8,128)(2,1)S(1)}, bf16[1024,256]{1,0:T(8,128)(2,1)S(1)}, u32[]{:S(2)}, u32[]{:S(2)}) collective-permute-start(bf16[1024,256]{1,0:T(8,128)(2,1)S(1)} %get-tuple-element.19), channel_id=1, source_target_pairs={{0,8},{1,9},{2,10},{3,11},{4,12},{5,13},{6,14},{7,15},{8,0},{9,1},... | collective-permute-start | bytes 1572872 | tf_op jit(solution)/shard_map/ppermute | solution.py:185
  9.3 10.0 %collective-permute-start.4 = (bf16[256,512]{1,0:T(8,128)(2,1)S(1)}, bf16[256,512]{1,0:T(8,128)(2,1)S(1)}, u32[]{:S(2)}, u32[]{:S(2)}) collective-permute-start(bf16[256,512]{1,0:T(8,128)(2,1)S(1)} %get-tuple-element.25), channel_id=1, source_target_pairs={{0,1},{1,0},{2,3},{3,2},{4,5},{5,4},{6,7},{7,6},{8,9},{9,8},{10,11... | collective-permute-start | bytes 786440 | tf_op jit(solution)/shard_map/ppermute | solution.py:185
  12.7 9.3 %collective-permute-start.8 = (bf16[256,512]{1,0:T(8,128)(2,1)S(1)}, bf16[256,512]{1,0:T(8,128)(2,1)S(1)}, u32[]{:S(2)}, u32[]{:S(2)}) collective-permute-start(bf16[256,512]{1,0:T(8,128)(2,1)S(1)} %get-tuple-element.30), channel_id=1, source_target_pairs={{0,16},{1,17},{2,18},{3,19},{4,20},{5,21},{6,22},{7,23},{8,24},{9,... | collective-permute-start | bytes 786440 | tf_op jit(solution)/shard_map/ppermute | solution.py:185
  14.3 10.7 %collective-permute-start.11 = (bf16[256,512]{1,0:T(8,128)(2,1)S(1)}, bf16[256,512]{1,0:T(8,128)(2,1)S(1)}, u32[]{:S(2)}, u32[]{:S(2)}) collective-permute-start(bf16[256,512]{1,0:T(8,128)(2,1)S(1)} %get-tuple-element.32), channel_id=1, source_target_pairs={{0,1},{1,0},{2,3},{3,2},{4,5},{5,4},{6,7},{7,6},{8,9},{9,8},{10,11... | collective-permute-start | bytes 786440 | tf_op jit(solution)/shard_map/ppermute | solution.py:185
  14.9 12.7 %collective-permute-start.2 = (bf16[256,512]{1,0:T(8,128)(2,1)S(1)}, bf16[256,512]{1,0:T(8,128)(2,1)S(1)}, u32[]{:S(2)}, u32[]{:S(2)}) collective-permute-start(bf16[256,512]{1,0:T(8,128)(2,1)S(1)} %get-tuple-element.23), channel_id=1, source_target_pairs={{0,16},{1,17},{2,18},{3,19},{4,20},{5,21},{6,22},{7,23},{8,24},{9,... | collective-permute-start | bytes 786440 | tf_op jit(solution)/shard_map/ppermute | solution.py:185
  19.5 10.9 %collective-permute-start.5 = (bf16[128,512]{1,0:T(8,128)(2,1)S(1)}, bf16[128,512]{1,0:T(8,128)(2,1)S(1)}, u32[]{:S(2)}, u32[]{:S(2)}) collective-permute-start(bf16[128,512]{1,0:T(8,128)(2,1)S(1)} %slice.66), channel_id=1, source_target_pairs={{0,16},{1,17},{2,18},{3,19},{4,20},{5,21},{6,22},{7,23},{8,24},{9,... | collective-permute-start | bytes 393224 | tf_op jit(solution)/shard_map/ppermute | solution.py:185
  22.1 10.0 %collective-permute-start.9 = (bf16[128,512]{1,0:T(8,128)(2,1)S(1)}, bf16[128,512]{1,0:T(8,128)(2,1)S(1)}, u32[]{:S(2)}, u32[]{:S(2)}) collective-permute-start(bf16[128,512]{1,0:T(8,128)(2,1)S(1)} %slice.65), channel_id=1, source_target_pairs={{0,1},{1,0},{2,3},{3,2},{4,5},{5,4},{6,7},{7,6},{8,9},{9,8},{10,11... | collective-permute-start | bytes 393224 | tf_op jit(solution)/shard_map/ppermute | solution.py:185
  25.1 9.7 %collective-permute-start.12 = (bf16[128,512]{1,0:T(8,128)(2,1)S(1)}, bf16[128,512]{1,0:T(8,128)(2,1)S(1)}, u32[]{:S(2)}, u32[]{:S(2)}) collective-permute-start(bf16[128,512]{1,0:T(8,128)(2,1)S(1)} %slice.64), channel_id=1, source_target_pairs={{0,16},{1,17},{2,18},{3,19},{4,20},{5,21},{6,22},{7,23},{8,24},{9,... | collective-permute-start | bytes 393224 | tf_op jit(solution)/shard_map/ppermute | solution.py:185
  27.7 13.5 %collective-permute-start.3 = (bf16[128,512]{1,0:T(8,128)(2,1)S(1)}, bf16[128,512]{1,0:T(8,128)(2,1)S(1)}, u32[]{:S(2)}, u32[]{:S(2)}) collective-permute-start(bf16[128,512]{1,0:T(8,128)(2,1)S(1)} %slice.67), channel_id=1, source_target_pairs={{0,1},{1,0},{2,3},{3,2},{4,5},{5,4},{6,7},{7,6},{8,9},{9,8},{10,11... | collective-permute-start | bytes 393224 | tf_op jit(solution)/shard_map/ppermute | solution.py:185
  30.5 10.7 %collective-permute-start.6 = (bf16[128,512]{1,0:T(8,128)(2,1)S(1)}, bf16[128,512]{1,0:T(8,128)(2,1)S(1)}, u32[]{:S(2)}, u32[]{:S(2)}) collective-permute-start(bf16[128,512]{1,0:T(8,128)(2,1)S(1)} %fusion.2), channel_id=1, source_target_pairs={{0,2},{1,3},{2,0},{3,1},{4,6},{5,7},{6,4},{7,5},{8,10},{9,11},{10,... | collective-permute-start | bytes 393224 | tf_op jit(solution)/shard_map/ppermute | solution.py:185
  32.1 11.0 %collective-permute-start.10 = (bf16[128,512]{1,0:T(8,128)(2,1)S(1)}, bf16[128,512]{1,0:T(8,128)(2,1)S(1)}, u32[]{:S(2)}, u32[]{:S(2)}) collective-permute-start(bf16[128,512]{1,0:T(8,128)(2,1)S(1)} %fusion.1), channel_id=1, source_target_pairs={{0,4},{1,5},{2,6},{3,7},{4,0},{5,1},{6,2},{7,3},{8,12},{9,13},{10,... | collective-permute-start | bytes 393224 | tf_op jit(solution)/shard_map/ppermute | solution.py:185
  34.8 8.3 %collective-permute-start.13 = (bf16[128,512]{1,0:T(8,128)(2,1)S(1)}, bf16[128,512]{1,0:T(8,128)(2,1)S(1)}, u32[]{:S(2)}, u32[]{:S(2)}) collective-permute-start(bf16[128,512]{1,0:T(8,128)(2,1)S(1)} %fusion), channel_id=1, source_target_pairs={{0,6},{1,7},{2,4},{3,5},{4,2},{5,3},{6,0},{7,1},{8,14},{9,15},{10,... | collective-permute-start | bytes 393224 | tf_op jit(solution)/shard_map/ppermute | solution.py:185
  36.3 3.9 %collective-permute-start.7 = (bf16[32,512]{1,0:T(8,128)(2,1)S(1)}, bf16[32,512]{1,0:T(8,128)(2,1)S(1)}, u32[]{:S(2)}, u32[]{:S(2)}) collective-permute-start(bf16[32,512]{1,0:T(8,128)(2,1)S(1)} %get-tuple-element.27), channel_id=1, source_target_pairs={{0,16},{1,17},{2,18},{3,19},{4,20},{5,21},{6,22},{7,23},{8,24},{9,... | collective-permute-start | bytes 98312 | tf_op jit(solution)/shard_map/ppermute | solution.py:185
  43.2 5.0 %collective-permute-start.14 = (bf16[128,512]{1,0:T(8,128)(2,1)S(1)}, bf16[128,512]{1,0:T(8,128)(2,1)S(1)}, u32[]{:S(2)}, u32[]{:S(2)}) collective-permute-start(bf16[128,512]{1,0:T(8,128)(2,1)S(1)} %fusion.5.mine_ref), channel_id=1, source_target_pairs={{0,16},{1,17},{2,18},{3,19},{4,20},{5,21},{6,22},{7,23},{8,24},{9,... | collective-permute-start | bytes 393224 | tf_op jit(solution)/shard_map/ppermute | solution.py:185
  48.3 1.6 %collective-permute-start.15 = (bf16[2,128,512]{2,1,0:T(8,128)(2,1)S(1)}, bf16[2,128,512]{2,1,0:T(8,128)(2,1)S(1)}, u32[]{:S(2)}, u32[]{:S(2)}) collective-permute-start(bf16[2,128,512]{2,1,0:T(8,128)(2,1)S(1)} %pad_maximum_fusion), channel_id=1, source_target_pairs={{0,8},{1,9},{2,10},{3,11},{4,12},{5,13},{6,14},{7,15},{8,0},{9,1},... | collective-permute-start | bytes 786440 | tf_op jit(solution)/shard_map/ppermute | solution.py:185

commit v4 on v3

--- a/solution.py
+++ b/solution.py
@@ -56,16 +56,9 @@
 
 
 def front_kernel(
-    split, per_group, loss_hbm, exponent_hbm, start_hbm, rows_hbm, q_hbm, k_hbm, g_hbm, ids_hbm, index_hbm, *rest
+    per_group, loss_hbm, exponent_hbm, start_hbm, rows_hbm, q_hbm, k_hbm, g_hbm, ids_hbm, index_hbm, *rest
 ):
-    if split:
-        x_hbm, own1_ref, near1_ref, own2_ref, near2_ref = rest[:5]
-        rest = rest[5:]
-        v_refs = (own1_ref, near1_ref)
-    else:
-        v_refs = rest[:1]
-        rest = rest[1:]
-    loss_ref, exponent_ref, start_ref, rows_ref, q_ref, k_ref, g_ref, ids_ref, index_ref, sems = rest
+    v_ref, loss_ref, exponent_ref, start_ref, rows_ref, q_ref, k_ref, g_ref, ids_ref, index_ref, sems = rest
     count = 0
 
     def begin(source, target):
@@ -93,27 +86,6 @@
             begin(k_hbm.at[:, one], k_ref.at[:, one]),
             begin(g_hbm.at[:, some], g_ref.at[:, some]),
         ])
-    cuts = []
-    if split:
-        dp = lax.axis_index("dp")
-        fsdp = lax.axis_index("fsdp")
-
-        def cut(target, row, core, z, flips):
-            for at, (y, x) in enumerate(flips):
-                owner = fsdp ^ (z << 1 | x)
-                column = pl.multiple_of(owner * (4 * LANE) + (dp ^ (y << 1 | core)) * LANE, LANE)
-                cuts.append(begin(
-                    x_hbm.at[:, pl.ds(column, LANE)],
-                    target.at[pl.ds(row, 2 * HALF), pl.ds(at * LANE, LANE)],
-                ))
-
-        for core, row, z_a, z_b, target in (
-            (1, VROWS, 2, 3, near1_ref), (0, VROWS, 2, 3, own1_ref), (1, 0, 0, 1, near2_ref), (0, 0, 0, 1, own2_ref)
-        ):
-            cut(target, row, core, z_a, ((1, 1), (1, 0)))
-            cut(target, row + 256, core, z_b, ((1, 1), (0, 1)))
-            cut(target, row + 512, core, z_a, ((0, 1), (0, 0)))
-            cut(target, row + 768, core, z_b, ((1, 0), (0, 0)))
     for copy in small:
         copy.wait()
     masks = [
@@ -121,8 +93,7 @@
     ]
 
     def put(group, row, value):
-        for ref in v_refs:
-            ref[pl.ds((group // 2) * (2 * HALF + INFO) + row, value.shape[0]), pl.ds(group % 2 * HD, HD)] = value
+        v_ref[pl.ds(row, value.shape[0]), pl.ds(group * HD, HD)] = value
 
     info_row = lax.broadcasted_iota(jnp.int32, (INFO, HD), 0)
     info = jnp.zeros((INFO, HD), jnp.int32)
@@ -142,42 +113,34 @@
             )
             put(group, half * HALF, value)
         put(group, 2 * HALF, info)
-    for copy in cuts:
-        copy.wait()
-
-
-def front(split, layer_input, query, key, grad, ids, index, loss, exponent, start, rows):
+
+
+def front(query, key, grad, ids, index, loss, exponent, start, rows):
     tokens, key_width = key.shape
     per_group = query.shape[1] // key_width
     groups = key_width // HD
-    v_rows = (tokens + INFO) * (groups // 2)
-    heights = [v_rows + 4 * tokens, v_rows + 4 * tokens, 4 * tokens, 4 * tokens]
     args = [
         loss, exponent, start, rows, query, key, grad, ids.reshape(1, tokens), index.reshape(1, tokens)
     ]
     return pl.pallas_call(
-        functools.partial(front_kernel, split, per_group),
-        in_specs=[HBM] * (10 if split else 9),
-        out_specs=[VMEM] * (4 if split else 1),
-        out_shape=[jax.ShapeDtypeStruct((height, 2 * HD), BF16) for height in (heights if split else [v_rows])],
+        functools.partial(front_kernel, per_group),
+        in_specs=[HBM] * 9,
+        out_specs=VMEM,
+        out_shape=jax.ShapeDtypeStruct((tokens + INFO, key_width), BF16),
         scratch_shapes=[
             pltpu.SMEM(loss.shape, F32), pltpu.SMEM(exponent.shape, jnp.int32),
             pltpu.SMEM(start.shape, jnp.int32), pltpu.SMEM(rows.shape, jnp.int32),
             pltpu.VMEM(query.shape, BF16), pltpu.VMEM(key.shape, BF16), pltpu.VMEM(grad.shape, BF16),
             pltpu.VMEM((1, tokens), jnp.int32), pltpu.VMEM((1, tokens), jnp.int32),
-            pltpu.SemaphoreType.DMA((6 + 3 * groups + 32,)),
+            pltpu.SemaphoreType.DMA((6 + 3 * groups,)),
         ],
-        compiler_params=pltpu.CompilerParams(vmem_limit_bytes=32 * MIB),
+        compiler_params=pltpu.CompilerParams(vmem_limit_bytes=24 * MIB),
         cost_estimate=FREE,
         name="front",
-    )(*[
-        arg if arg is exponent else pltpu.with_memory_space_constraint(arg, pltpu.HBM)
-        for arg in (args + [layer_input] if split else args)
-    ])
+    )(*[arg if arg is exponent else pltpu.with_memory_space_constraint(arg, pltpu.HBM) for arg in args])
 
 
 CORE, Y, X = 8, 16, 1
-VROWS = 2 * (2 * HALF + INFO)
 
 
 def xor_permute(value, mask):
@@ -185,23 +148,29 @@
     return lax.ppermute(value, ("dp", "fsdp"), [(i, i ^ mask) for i in range(count)])
 
 
-def partial_kernel(row, own_ref, near_ref, v0_ref, v1_ref, a_ref, b_ref):
-    for number, out_ref in enumerate((a_ref, b_ref)):
-        some = pl.ds(row + 256 * number, 256)
-        x = jnp.concatenate([own_ref[some, :], near_ref[some, :]], axis=0)
-        for part in range(2):
-            v = jnp.concatenate([ref[pl.ds(part * (256 + INFO), 256), :] for ref in (v0_ref, v1_ref)], axis=0)
-            total = lax.dot_general(x, v, (((0,), (0,)), ((), ())), preferred_element_type=F32)
-            out_ref[:, pl.ds(256 * part, 256)] = total.astype(out_ref.dtype)
-
-
-def partial_sums(row, dtype, own, near, v0, v1):
-    return pl.pallas_call(
-        functools.partial(partial_kernel, row),
+def partial_kernel(parts, own_ref, near_ref, v0_ref, v1_ref, *out_refs):
+    dp = lax.axis_index("dp")
+    fsdp = lax.axis_index("fsdp")
+    v = jnp.concatenate([ref[pl.ds(0, 2 * HALF), :] for ref in (v0_ref, v1_ref)], axis=0)
+    for blocks, out_ref in zip(parts, out_refs):
+        columns = []
+        for z, y, x in blocks:
+            owner = fsdp ^ (z << 1 | x)
+            column = pl.multiple_of(owner * (4 * LANE) + (dp ^ (y << 1)) * LANE, LANE)
+            columns.append(jnp.concatenate([ref[:, pl.ds(column, LANE)] for ref in (own_ref, near_ref)], axis=0))
+        total = lax.dot_general(
+            jnp.concatenate(columns, axis=1), v, (((0,), (0,)), ((), ())), preferred_element_type=F32
+        )
+        out_ref[...] = total.astype(out_ref.dtype)
+
+
+def partial_sums(parts, dtype, own, near, v0, v1):
+    return pl.pallas_call(
+        functools.partial(partial_kernel, parts),
         in_specs=[VMEM] * 4,
-        out_specs=[VMEM] * 2,
-        out_shape=[jax.ShapeDtypeStruct((256, 512), dtype)] * 2,
-        compiler_params=pltpu.CompilerParams(vmem_limit_bytes=32 * MIB),
+        out_specs=[VMEM] * len(parts),
+        out_shape=[jax.ShapeDtypeStruct((len(blocks) * LANE, 512), dtype) for blocks in parts],
+        compiler_params=pltpu.CompilerParams(vmem_limit_bytes=24 * MIB),
         cost_estimate=FREE,
         name="partial_sums",
     )(own, near, v0, v1)
@@ -221,16 +190,13 @@
     stays = jnp.where(~moved & (place == inner), 1.0, 0.0).astype(BF16)
     comes = jnp.where(moved & (place + table(1, 0) - first == inner), 1.0, 0.0).astype(BF16)
     taken = jnp.where(place - HALF + table(0, 2) == inner, 1.0, 0.0).astype(BF16)[:CAP]
-    for part in range(2):
-        base = part * (tokens + INFO)
-        some = pl.ds(256 * part, 256)
-        rows = (
-            jnp.dot(stays, v0_ref[pl.ds(base + HALF, HALF), :], preferred_element_type=F32)
-            + jnp.dot(comes, v1_ref[pl.ds(base + HALF, HALF), :], preferred_element_type=F32)
-        ).astype(BF16)
-        out_ref[pl.ds(0, HALF), some] = v0_ref[pl.ds(base, HALF), :]
-        out_ref[pl.ds(HALF, HALF), some] = rows
-        window_ref[:, some] = jnp.dot(taken, rows, preferred_element_type=F32).astype(BF16)
+    rows = (
+        jnp.dot(stays, v0_ref[pl.ds(HALF, HALF), :], preferred_element_type=F32)
+        + jnp.dot(comes, v1_ref[pl.ds(HALF, HALF), :], preferred_element_type=F32)
+    ).astype(BF16)
+    out_ref[pl.ds(0, HALF), :] = v0_ref[pl.ds(0, HALF), :]
+    out_ref[pl.ds(HALF, HALF), :] = rows
+    window_ref[...] = jnp.dot(taken, rows, preferred_element_type=F32).astype(BF16)
 
 
 def inner_swap(v0, v1):
@@ -292,33 +258,46 @@
     )(mine, from_y, near)
 
 
-def reduce_by_axis(*args):
-    own1, near1, own2, near2 = front(True, *args)
-    near1 = xor_permute(near1, CORE)
-    near2 = xor_permute(near2, CORE)
-    send_a1, send_b1 = partial_sums(VROWS, BF16, own1, near1, own1, near1)
-    send_a2, send_b2 = partial_sums(0, BF16, own2, near2, own1, near1)
-    keep_a1, keep_b1 = partial_sums(VROWS + 512, F32, own1, near1, own1, near1)
-    keep_a2, keep_b2 = partial_sums(512, F32, own2, near2, own1, near1)
-    half_a1 = keep_a1 + xor_permute(send_a1, Y).astype(F32)
-    half_b1 = keep_b1 + xor_permute(send_b1, X).astype(F32)
-    half_a2 = keep_a2 + xor_permute(send_a2, Y).astype(F32)
-    half_b2 = keep_b2 + xor_permute(send_b2, X).astype(F32)
-
-    def other(half, mask):
-        return half[LANE:] + xor_permute(half[:LANE].astype(BF16), mask).astype(F32)
-
-    z2 = xor_permute(other(half_a1, X).astype(BF16), 4)
-    z3 = xor_permute(other(half_b1, Y).astype(BF16), 6)
-    z1 = xor_permute(other(half_b2, Y).astype(BF16), 2)
-    z0 = other(half_a2, X)
-    rows, window = inner_swap(own1, near1)
-    value_grad = outer_swap(own1, rows, xor_permute(window, Y))
+def reduce_by_axis(layer_input, *args):
+    near = xor_permute(layer_input, CORE)
+    v0 = front(*args)
+    v1 = xor_permute(v0, CORE)
+
+    def sums(parts, dtype):
+        return partial_sums(parts, dtype, layer_input, near, v0, v1)
+
+    far_a, far_b = sums((((2, 1, 1),), ((3, 1, 1),)), BF16)
+    side_a, side_b = sums((((2, 1, 0),), ((3, 0, 1),)), BF16)
+    late_a, late_b = sums((((0, 1, 1), (0, 1, 0)), ((1, 1, 1), (1, 0, 1))), BF16)
+    keep_far_a, keep_far_b = sums((((2, 0, 1),), ((3, 1, 0),)), F32)
+    keep_a, keep_b = sums((((2, 0, 0),), ((3, 0, 0),)), F32)
+    keep_late_a, keep_late_b = sums((((0, 0, 1), (0, 0, 0)), ((1, 1, 0), (1, 0, 0))), F32)
+
+    far_a = xor_permute(far_a, Y)
+    far_b = xor_permute(far_b, X)
+    side_a = xor_permute(side_a, Y)
+    side_b = xor_permute(side_b, X)
+    on_a = (keep_far_a + far_a.astype(F32)).astype(BF16)
+    on_b = (keep_far_b + far_b.astype(F32)).astype(BF16)
+    on_a, on_b, late_a, late_b = lax.optimization_barrier((on_a, on_b, late_a, late_b))
+    on_a = xor_permute(on_a, X)
+    on_b = xor_permute(on_b, Y)
+    late_a = xor_permute(late_a, Y)
+    late_b = xor_permute(late_b, X)
+    z2 = xor_permute((keep_a + side_a.astype(F32) + on_a.astype(F32)).astype(BF16), 4)
+    z3 = xor_permute((keep_b + side_b.astype(F32) + on_b.astype(F32)).astype(BF16), 6)
+    half_a = keep_late_a + late_a.astype(F32)
+    half_b = keep_late_b + late_b.astype(F32)
+    on_late_a = xor_permute(half_a[:LANE].astype(BF16), X)
+    on_late_b = xor_permute(half_b[:LANE].astype(BF16), Y)
+    z0 = half_a[LANE:] + on_late_a.astype(F32)
+    z1 = xor_permute((half_b[LANE:] + on_late_b.astype(F32)).astype(BF16), 2)
+    rows, window = inner_swap(v0, v1)
+    value_grad = outer_swap(v0, rows, xor_permute(window, Y))
     z1, value_grad = lax.optimization_barrier((z1, value_grad))
     mine = (z0 + z1.astype(F32) + (z2.astype(F32) + z3.astype(F32))).astype(BF16)
     from_y = xor_permute(mine, Y)
-    grad_value = place(mine, from_y, xor_permute(jnp.stack([mine, from_y]), CORE))
-    return grad_value, value_grad
+    return place(mine, from_y, xor_permute(jnp.stack([mine, from_y]), CORE)), value_grad
 
 
 def swapped(block, axis, distance):
@@ -340,8 +319,7 @@
 def reduce_by_owner(layer_input, *args):
     swap_start, swap_rows = args[-2:]
     tokens = layer_input.shape[0]
-    halves = front(False, layer_input, *args)[0].reshape(2, tokens + INFO, 2 * HD)[:, :tokens]
-    values = jnp.concatenate([halves[0], halves[1]], axis=1)
+    values = front(*args)[:tokens]
     balanced = values
     for level in range(lax.axis_size("dp").bit_length() - 1):
         offset = swap_start[0, level]

time: 51.1 us -> 48.9 us (0.957)
  waiting for transfers between devices: 19.4 us -> 15.2 us
  starting transfers between devices: 20.9 us -> 22.8 us
    ppermute x16 -> x18, waiting for transfers between devices: 19.4 us -> 15.2 us  [xor_permute(): lax.ppermute(value, ('dp', 'fsdp'), [(i, i ^ mask) for i in range(count)])]
    ppermute x16 -> x18, starting transfers between devices: 20.9 us -> 22.8 us  [xor_permute(): lax.ppermute(value, ('dp', 'fsdp'), [(i, i ^ mask) for i in range(count)])]
    pallas_call x5 -> x7, Pallas kernels: 6.21 us -> 6.42 us  [the longest x1 4.05 us: front(): pl.pallas_call(functools.partial(front_kernel, per_group), in_specs=[HBM]...]
  transfers between devices with their start and end apart: 16 -> 18, of which waited for: 10 -> 8; matrix products, arithmetic and copies ran while one was open for 1% -> 1% of each run, Pallas kernels for 5% -> 15%
where the time goes in v4:
time: 48.9 us; the launch traced here: 48.7 us
  starting transfers between devices  22.8 us (47%)
  waiting for transfers between devices  15.2 us (31%)
  Pallas kernels  8.71 us (18%)
  between operations  1.55 us (3%)
    ppermute x18, starting transfers between devices, xor_permute(): lax.ppermute(value, ('dp', 'fsdp'), [(i, i ^ mask) for i in range(count)])  22.8 us
    ppermute x18, waiting for transfers between devices, xor_permute(): lax.ppermute(value, ('dp', 'fsdp'), [(i, i ^ mask) for i in range(count)])  15.2 us
    pallas_call x1, Pallas kernels, front(): pl.pallas_call(functools.partial(front_kernel, per_group), in_specs=[HBM]...  4.05 us
    pallas_call x6, Pallas kernels, partial_sums(): pl.pallas_call(functools.partial(partial_kernel, parts), in_specs=[VMEM]...  2.37 us
    pallas_call x1, Pallas kernels, place(): pl.pallas_call(place_kernel, in_specs=[VMEM] * 3, out_specs=VMEM, out_sha...  1.05 us
  transfers between devices with their start and end apart: 18, of which 8 were waited for; matrix products, arithmetic and copies ran while one was open for 1% of the time, Pallas kernels for 15%

profile of v4, /device:TPU:0, one launch (start us, length us, event | category | flops | bytes accessed | tf_op | source)
XLA Modules:
  0.0 48.7 jit_solution(1257550788707038720)
XLA Ops:
  0.6 0.5 %collective-permute-start = (bf16[256,4096]{1,0:T(8,128)(2,1)}, bf16[256,4096]{1,0:T(8,128)(2,1)S(1)}, u32[]{:S(2)}, u32[]{:S(2)}) collective-permute-start(bf16[256,4096]{1,0:T(8,128)(2,1)} %own_ref.11), channel_id=1, source_target_pairs={{0,8},{1,9},{2,10},{3,11},{4,12},{5,13},{6,14},{7,15},{8,0},{9,1},... | collective-permute-start | bytes 6291464 | tf_op jit(solution)/shard_map/ppermute | solution.py:148
  1.9 4.1 %front.1.v0_ref = bf16[272,512]{1,0:T(8,128)(2,1)S(1)} custom-call(f32[16]{0:T(128)} %loss_hbm.1, s32[1]{0:T(128)S(6)} %copy.12.exponent_hbm, s32[1,2]{1,0:T(1,128)} %start_hbm.1, s32[1,2]{1,0:T(1,128)} %rows_hbm.1, bf16[256,2048]{1,0:T(8,128)(2,1)} %q_hbm.1, bf16[256,512]{1,0:T(8,128)(2,1)} %k_hbm.1, bf16[256,2048]{1,0:T(8,128)(2,1)} %g_hbm.1, ...), custom_call_target="tpu_custom_call" | custom-call | tf_op jit(solution)/shard_map/front/pallas_call | solution.py:125
  6.0 0.1 collective-permute-start.1
  6.1 1.5 %collective-permute-done.1.v1_ref = bf16[272,512]{1,0:T(8,128)(2,1)S(1)} collective-permute-done((bf16[272,512]{1,0:T(8,128)(2,1)S(1)}, bf16[272,512]{1,0:T(8,128)(2,1)S(1)}, u32[]{:S(2)}, u32[]{:S(2)}) %collective-permute-start.1) | collective-permute-done | bytes 278560 | tf_op jit(solution)/shard_map/ppermute | solution.py:148
  7.6 0.0 collective-permute-done.near_ref
  7.6 0.3 partial_sums.8
  8.0 2.6 %collective-permute-start.3 = (bf16[128,512]{1,0:T(8,128)(2,1)S(1)}, bf16[128,512]{1,0:T(8,128)(2,1)S(1)}, u32[]{:S(2)}, u32[]{:S(2)}) collective-permute-start(bf16[128,512]{1,0:T(8,128)(2,1)S(1)} %get-tuple-element.26), channel_id=1, source_target_pairs={{0,1},{1,0},{2,3},{3,2},{4,5},{5,4},{6,7},{7,6},{8,9},{9,8},{10,11... | collective-permute-start | bytes 393224 | tf_op jit(solution)/shard_map/ppermute | solution.py:148
  10.6 1.5 %collective-permute-start.2 = (bf16[128,512]{1,0:T(8,128)(2,1)S(1)}, bf16[128,512]{1,0:T(8,128)(2,1)S(1)}, u32[]{:S(2)}, u32[]{:S(2)}) collective-permute-start(bf16[128,512]{1,0:T(8,128)(2,1)S(1)} %get-tuple-element.24), channel_id=1, source_target_pairs={{0,16},{1,17},{2,18},{3,19},{4,20},{5,21},{6,22},{7,23},{8,24},{9,... | collective-permute-start | bytes 393224 | tf_op jit(solution)/shard_map/ppermute | solution.py:148
  12.1 0.3 partial_sums.11
  12.4 0.6 %collective-permute-start.10 = (bf16[128,512]{1,0:T(8,128)(2,1)S(1)}, bf16[128,512]{1,0:T(8,128)(2,1)S(1)}, u32[]{:S(2)}, u32[]{:S(2)}) collective-permute-start(bf16[128,512]{1,0:T(8,128)(2,1)S(1)} %get-tuple-element.36), channel_id=1, source_target_pairs={{0,16},{1,17},{2,18},{3,19},{4,20},{5,21},{6,22},{7,23},{8,24},{9,... | collective-permute-start | bytes 393224 | tf_op jit(solution)/shard_map/ppermute | solution.py:148
  13.0 0.3 partial_sums.7
  13.4 0.5 %partial_sums.9 = (bf16[256,512]{1,0:T(8,128)(2,1)S(1)}, bf16[256,512]{1,0:T(8,128)(2,1)S(1)}) custom-call(bf16[256,4096]{1,0:T(8,128)(2,1)S(1)} %copy-done, bf16[256,4096]{1,0:T(8,128)(2,1)S(1)} %collective-permute-done.near_ref, bf16[272,512]{1,0:T(8,128)(2,1)S(1)} %front.1.v0_ref, bf16[272,512]{1,0:T(8,128)(2,1)S(1)} %collective-permute-done.1.v1_ref), custom_call_target="tpu_custom_call" | custom-call | tf_op jit(solution)/shard_map/partial_sums/pallas_call | solution.py:168
  13.9 0.7 %collective-permute-done.3 = bf16[128,512]{1,0:T(8,128)(2,1)S(1)} collective-permute-done((bf16[128,512]{1,0:T(8,128)(2,1)S(1)}, bf16[128,512]{1,0:T(8,128)(2,1)S(1)}, u32[]{:S(2)}, u32[]{:S(2)}) %collective-permute-start.3) | collective-permute-done | bytes 131104 | tf_op jit(solution)/shard_map/ppermute | solution.py:148
  14.6 2.3 %collective-permute-done.2 = bf16[128,512]{1,0:T(8,128)(2,1)S(1)} collective-permute-done((bf16[128,512]{1,0:T(8,128)(2,1)S(1)}, bf16[128,512]{1,0:T(8,128)(2,1)S(1)}, u32[]{:S(2)}, u32[]{:S(2)}) %collective-permute-start.2) | collective-permute-done | bytes 131104 | tf_op jit(solution)/shard_map/ppermute | solution.py:148
  17.0 0.1 collective-permute-start.11
  17.1 2.0 %collective-permute-start.6 = (bf16[256,512]{1,0:T(8,128)(2,1)S(1)}, bf16[256,512]{1,0:T(8,128)(2,1)S(1)}, u32[]{:S(2)}, u32[]{:S(2)}) collective-permute-start(bf16[256,512]{1,0:T(8,128)(2,1)S(1)} %get-tuple-element.31), channel_id=1, source_target_pairs={{0,1},{1,0},{2,3},{3,2},{4,5},{5,4},{6,7},{7,6},{8,9},{9,8},{10,11... | collective-permute-start | bytes 786440 | tf_op jit(solution)/shard_map/ppermute | solution.py:148
  19.0 0.1 collective-permute-start.13
  19.1 0.5 partial_sums.6
  19.6 0.3 partial_sums.10
  20.0 2.1 %collective-permute-start.14 = (bf16[128,512]{1,0:T(8,128)(2,1)S(1)}, bf16[128,512]{1,0:T(8,128)(2,1)S(1)}, u32[]{:S(2)}, u32[]{:S(2)}) collective-permute-start(bf16[128,512]{1,0:T(8,128)(2,1)S(1)} %add_convert_fusion.2), channel_id=1, source_target_pairs={{0,16},{1,17},{2,18},{3,19},{4,20},{5,21},{6,22},{7,23},{8,24},{9,... | collective-permute-start | bytes 393224 | tf_op jit(solution)/shard_map/ppermute | solution.py:148
  22.0 0.0 collective-permute-done.10
  22.0 0.1 collective-permute-start.4
  22.1 1.3 %collective-permute-done.11 = bf16[128,512]{1,0:T(8,128)(2,1)S(1)} collective-permute-done((bf16[128,512]{1,0:T(8,128)(2,1)S(1)}, bf16[128,512]{1,0:T(8,128)(2,1)S(1)}, u32[]{:S(2)}, u32[]{:S(2)}) %collective-permute-start.11) | collective-permute-done | bytes 131104 | tf_op jit(solution)/shard_map/ppermute | solution.py:148
  23.5 2.7 %collective-permute-start.12 = (bf16[128,512]{1,0:T(8,128)(2,1)S(1)}, bf16[128,512]{1,0:T(8,128)(2,1)S(1)}, u32[]{:S(2)}, u32[]{:S(2)}) collective-permute-start(bf16[128,512]{1,0:T(8,128)(2,1)S(1)} %add_convert_fusion.1), channel_id=1, source_target_pairs={{0,4},{1,5},{2,6},{3,7},{4,0},{5,1},{6,2},{7,3},{8,12},{9,13},{10,... | collective-permute-start | bytes 393224 | tf_op jit(solution)/shard_map/ppermute | solution.py:148
  26.2 1.6 %collective-permute-done.6 = bf16[256,512]{1,0:T(8,128)(2,1)S(1)} collective-permute-done((bf16[256,512]{1,0:T(8,128)(2,1)S(1)}, bf16[256,512]{1,0:T(8,128)(2,1)S(1)}, u32[]{:S(2)}, u32[]{:S(2)}) %collective-permute-start.6) | collective-permute-done | bytes 262176 | tf_op jit(solution)/shard_map/ppermute | solution.py:148
  27.8 0.1 convert_add_fusion
  27.9 1.6 %collective-permute-start.7 = (bf16[128,512]{1,0:T(8,128)(2,1)S(1)}, bf16[128,512]{1,0:T(8,128)(2,1)S(1)}, u32[]{:S(2)}, u32[]{:S(2)}) collective-permute-start(bf16[128,512]{1,0:T(8,128)(2,1)S(1)} %slice.34), channel_id=1, source_target_pairs={{0,16},{1,17},{2,18},{3,19},{4,20},{5,21},{6,22},{7,23},{8,24},{9,... | collective-permute-start | bytes 393224 | tf_op jit(solution)/shard_map/ppermute | solution.py:148
  29.5 0.0 collective-permute-done.13
  29.5 0.0 collective-permute-done.14
  29.5 3.7 %collective-permute-start.15 = (bf16[128,512]{1,0:T(8,128)(2,1)S(1)}, bf16[128,512]{1,0:T(8,128)(2,1)S(1)}, u32[]{:S(2)}, u32[]{:S(2)}) collective-permute-start(bf16[128,512]{1,0:T(8,128)(2,1)S(1)} %add_convert_fusion), channel_id=1, source_target_pairs={{0,6},{1,7},{2,4},{3,5},{4,2},{5,3},{6,0},{7,1},{8,14},{9,15},{10,... | collective-permute-start | bytes 393224 | tf_op jit(solution)/shard_map/ppermute | solution.py:148
  33.2 0.0 collective-permute-done.7
  33.3 1.4 %collective-permute-start.8 = (bf16[128,512]{1,0:T(8,128)(2,1)S(1)}, bf16[128,512]{1,0:T(8,128)(2,1)S(1)}, u32[]{:S(2)}, u32[]{:S(2)}) collective-permute-start(bf16[128,512]{1,0:T(8,128)(2,1)S(1)} %fusion), channel_id=1, source_target_pairs={{0,2},{1,3},{2,0},{3,1},{4,6},{5,7},{6,4},{7,5},{8,10},{9,11},{10,... | collective-permute-start | bytes 393224 | tf_op jit(solution)/shard_map/ppermute | solution.py:148
  34.6 0.0 collective-permute-done.4
  34.6 0.1 convert_add_fusion.1
  34.7 0.7 %collective-permute-start.5 = (bf16[128,512]{1,0:T(8,128)(2,1)S(1)}, bf16[128,512]{1,0:T(8,128)(2,1)S(1)}, u32[]{:S(2)}, u32[]{:S(2)}) collective-permute-start(bf16[128,512]{1,0:T(8,128)(2,1)S(1)} %slice.35), channel_id=1, source_target_pairs={{0,1},{1,0},{2,3},{3,2},{4,5},{5,4},{6,7},{7,6},{8,9},{9,8},{10,11... | collective-permute-start | bytes 393224 | tf_op jit(solution)/shard_map/ppermute | solution.py:148
  35.4 0.3 inner_swap.1
  35.8 1.5 %collective-permute-start.9 = (bf16[32,512]{1,0:T(8,128)(2,1)S(1)}, bf16[32,512]{1,0:T(8,128)(2,1)S(1)}, u32[]{:S(2)}, u32[]{:S(2)}) collective-permute-start(bf16[32,512]{1,0:T(8,128)(2,1)S(1)} %get-tuple-element.33), channel_id=1, source_target_pairs={{0,16},{1,17},{2,18},{3,19},{4,20},{5,21},{6,22},{7,23},{8,24},{9,... | collective-permute-start | bytes 98312 | tf_op jit(solution)/shard_map/ppermute | solution.py:148
  37.3 2.7 %collective-permute-done.9.window_ref = bf16[32,512]{1,0:T(8,128)(2,1)S(1)} collective-permute-done((bf16[32,512]{1,0:T(8,128)(2,1)S(1)}, bf16[32,512]{1,0:T(8,128)(2,1)S(1)}, u32[]{:S(2)}, u32[]{:S(2)}) %collective-permute-start.9) | collective-permute-done | bytes 32800 | tf_op jit(solution)/shard_map/ppermute | solution.py:148
  40.0 0.9 %outer_swap.1 = bf16[256,512]{1,0:T(8,128)(2,1)} custom-call(bf16[272,512]{1,0:T(8,128)(2,1)S(1)} %front.1.v0_ref, bf16[256,512]{1,0:T(8,128)(2,1)S(1)} %get-tuple-element.32.rows_ref, bf16[32,512]{1,0:T(8,128)(2,1)S(1)} %collective-permute-done.9.window_ref), custom_call_target="tpu_custom_call" | custom-call | tf_op jit(solution)/shard_map/outer_swap/pallas_call | solution.py:232
  40.9 0.0 collective-permute-done.8
  40.9 0.0 collective-permute-done.12
  40.9 0.0 collective-permute-done.5
  40.9 0.1 fusion.3.mine_ref
  41.0 1.5 %collective-permute-start.16 = (bf16[128,512]{1,0:T(8,128)(2,1)S(1)}, bf16[128,512]{1,0:T(8,128)(2,1)S(1)}, u32[]{:S(2)}, u32[]{:S(2)}) collective-permute-start(bf16[128,512]{1,0:T(8,128)(2,1)S(1)} %fusion.3.mine_ref), channel_id=1, source_target_pairs={{0,16},{1,17},{2,18},{3,19},{4,20},{5,21},{6,22},{7,23},{8,24},{9,... | collective-permute-start | bytes 393224 | tf_op jit(solution)/shard_map/ppermute | solution.py:148
  42.6 3.5 %collective-permute-done.16.y_ref = bf16[128,512]{1,0:T(8,128)(2,1)S(1)} collective-permute-done((bf16[128,512]{1,0:T(8,128)(2,1)S(1)}, bf16[128,512]{1,0:T(8,128)(2,1)S(1)}, u32[]{:S(2)}, u32[]{:S(2)}) %collective-permute-start.16) | collective-permute-done | bytes 131104 | tf_op jit(solution)/shard_map/ppermute | solution.py:148
  46.1 0.1 collective-permute-start.17
  46.2 1.5 %collective-permute-done.17.near_ref = bf16[2,128,512]{2,1,0:T(8,128)(2,1)S(1)} collective-permute-done((bf16[2,128,512]{2,1,0:T(8,128)(2,1)S(1)}, bf16[2,128,512]{2,1,0:T(8,128)(2,1)S(1)}, u32[]{:S(2)}, u32[]{:S(2)}) %collective-permute-start.17) | collective-permute-done | bytes 262176 | tf_op jit(solution)/shard_map/ppermute | solution.py:148
  47.7 1.0 %place.1 = f32[512,512]{1,0:T(8,128)} custom-call(bf16[128,512]{1,0:T(8,128)(2,1)S(1)} %fusion.3.mine_ref, bf16[128,512]{1,0:T(8,128)(2,1)S(1)} %collective-permute-done.16.y_ref, bf16[2,128,512]{2,1,0:T(8,128)(2,1)S(1)} %collective-permute-done.17.near_ref), custom_call_target="tpu_custom_call" | custom-call | tf_op jit(solution)/shard_map/place/pallas_call | solution.py:250
  (11 shorter events, 0.2 us)
Async XLA Ops:
  0.6 7.0 %copy-start = (bf16[256,4096]{1,0:T(8,128)(2,1)S(1)}, bf16[256,4096]{1,0:T(8,128)(2,1)}, u32[]{:S(2)}) copy-start(bf16[256,4096]{1,0:T(8,128)(2,1)} %own_ref.11) | copy-start | bytes 6291460
  0.6 7.0 %collective-permute-start = (bf16[256,4096]{1,0:T(8,128)(2,1)}, bf16[256,4096]{1,0:T(8,128)(2,1)S(1)}, u32[]{:S(2)}, u32[]{:S(2)}) collective-permute-start(bf16[256,4096]{1,0:T(8,128)(2,1)} %own_ref.11), channel_id=1, source_target_pairs={{0,8},{1,9},{2,10},{3,11},{4,12},{5,13},{6,14},{7,15},{8,0},{9,1},... | collective-permute-start | bytes 6291464 | tf_op jit(solution)/shard_map/ppermute | solution.py:148
  6.0 1.6 %collective-permute-start.1 = (bf16[272,512]{1,0:T(8,128)(2,1)S(1)}, bf16[272,512]{1,0:T(8,128)(2,1)S(1)}, u32[]{:S(2)}, u32[]{:S(2)}) collective-permute-start(bf16[272,512]{1,0:T(8,128)(2,1)S(1)} %front.1.v0_ref), channel_id=1, source_target_pairs={{0,8},{1,9},{2,10},{3,11},{4,12},{5,13},{6,14},{7,15},{8,0},{9,1},... | collective-permute-start | bytes 835592 | tf_op jit(solution)/shard_map/ppermute | solution.py:148
  8.0 6.6 %collective-permute-start.3 = (bf16[128,512]{1,0:T(8,128)(2,1)S(1)}, bf16[128,512]{1,0:T(8,128)(2,1)S(1)}, u32[]{:S(2)}, u32[]{:S(2)}) collective-permute-start(bf16[128,512]{1,0:T(8,128)(2,1)S(1)} %get-tuple-element.26), channel_id=1, source_target_pairs={{0,1},{1,0},{2,3},{3,2},{4,5},{5,4},{6,7},{7,6},{8,9},{9,8},{10,11... | collective-permute-start | bytes 393224 | tf_op jit(solution)/shard_map/ppermute | solution.py:148
  10.6 6.4 %collective-permute-start.2 = (bf16[128,512]{1,0:T(8,128)(2,1)S(1)}, bf16[128,512]{1,0:T(8,128)(2,1)S(1)}, u32[]{:S(2)}, u32[]{:S(2)}) collective-permute-start(bf16[128,512]{1,0:T(8,128)(2,1)S(1)} %get-tuple-element.24), channel_id=1, source_target_pairs={{0,16},{1,17},{2,18},{3,19},{4,20},{5,21},{6,22},{7,23},{8,24},{9,... | collective-permute-start | bytes 393224 | tf_op jit(solution)/shard_map/ppermute | solution.py:148
  12.4 9.6 %collective-permute-start.10 = (bf16[128,512]{1,0:T(8,128)(2,1)S(1)}, bf16[128,512]{1,0:T(8,128)(2,1)S(1)}, u32[]{:S(2)}, u32[]{:S(2)}) collective-permute-start(bf16[128,512]{1,0:T(8,128)(2,1)S(1)} %get-tuple-element.36), channel_id=1, source_target_pairs={{0,16},{1,17},{2,18},{3,19},{4,20},{5,21},{6,22},{7,23},{8,24},{9,... | collective-permute-start | bytes 393224 | tf_op jit(solution)/shard_map/ppermute | solution.py:148
  17.0 6.5 %collective-permute-start.11 = (bf16[128,512]{1,0:T(8,128)(2,1)S(1)}, bf16[128,512]{1,0:T(8,128)(2,1)S(1)}, u32[]{:S(2)}, u32[]{:S(2)}) collective-permute-start(bf16[128,512]{1,0:T(8,128)(2,1)S(1)} %add_convert_fusion.3), channel_id=1, source_target_pairs={{0,1},{1,0},{2,3},{3,2},{4,5},{5,4},{6,7},{7,6},{8,9},{9,8},{10,11... | collective-permute-start | bytes 393224 | tf_op jit(solution)/shard_map/ppermute | solution.py:148
  17.1 10.7 %collective-permute-start.6 = (bf16[256,512]{1,0:T(8,128)(2,1)S(1)}, bf16[256,512]{1,0:T(8,128)(2,1)S(1)}, u32[]{:S(2)}, u32[]{:S(2)}) collective-permute-start(bf16[256,512]{1,0:T(8,128)(2,1)S(1)} %get-tuple-element.31), channel_id=1, source_target_pairs={{0,1},{1,0},{2,3},{3,2},{4,5},{5,4},{6,7},{7,6},{8,9},{9,8},{10,11... | collective-permute-start | bytes 786440 | tf_op jit(solution)/shard_map/ppermute | solution.py:148
  19.0 10.4 %collective-permute-start.13 = (bf16[128,512]{1,0:T(8,128)(2,1)S(1)}, bf16[128,512]{1,0:T(8,128)(2,1)S(1)}, u32[]{:S(2)}, u32[]{:S(2)}) collective-permute-start(bf16[128,512]{1,0:T(8,128)(2,1)S(1)} %get-tuple-element.39), channel_id=1, source_target_pairs={{0,1},{1,0},{2,3},{3,2},{4,5},{5,4},{6,7},{7,6},{8,9},{9,8},{10,11... | collective-permute-start | bytes 393224 | tf_op jit(solution)/shard_map/ppermute | solution.py:148
  20.0 9.5 %collective-permute-start.14 = (bf16[128,512]{1,0:T(8,128)(2,1)S(1)}, bf16[128,512]{1,0:T(8,128)(2,1)S(1)}, u32[]{:S(2)}, u32[]{:S(2)}) collective-permute-start(bf16[128,512]{1,0:T(8,128)(2,1)S(1)} %add_convert_fusion.2), channel_id=1, source_target_pairs={{0,16},{1,17},{2,18},{3,19},{4,20},{5,21},{6,22},{7,23},{8,24},{9,... | collective-permute-start | bytes 393224 | tf_op jit(solution)/shard_map/ppermute | solution.py:148
  22.0 12.6 %collective-permute-start.4 = (bf16[256,512]{1,0:T(8,128)(2,1)S(1)}, bf16[256,512]{1,0:T(8,128)(2,1)S(1)}, u32[]{:S(2)}, u32[]{:S(2)}) collective-permute-start(bf16[256,512]{1,0:T(8,128)(2,1)S(1)} %get-tuple-element.29), channel_id=1, source_target_pairs={{0,16},{1,17},{2,18},{3,19},{4,20},{5,21},{6,22},{7,23},{8,24},{9,... | collective-permute-start | bytes 786440 | tf_op jit(solution)/shard_map/ppermute | solution.py:148
  23.5 17.4 %collective-permute-start.12 = (bf16[128,512]{1,0:T(8,128)(2,1)S(1)}, bf16[128,512]{1,0:T(8,128)(2,1)S(1)}, u32[]{:S(2)}, u32[]{:S(2)}) collective-permute-start(bf16[128,512]{1,0:T(8,128)(2,1)S(1)} %add_convert_fusion.1), channel_id=1, source_target_pairs={{0,4},{1,5},{2,6},{3,7},{4,0},{5,1},{6,2},{7,3},{8,12},{9,13},{10,... | collective-permute-start | bytes 393224 | tf_op jit(solution)/shard_map/ppermute | solution.py:148
  27.9 5.3 %collective-permute-start.7 = (bf16[128,512]{1,0:T(8,128)(2,1)S(1)}, bf16[128,512]{1,0:T(8,128)(2,1)S(1)}, u32[]{:S(2)}, u32[]{:S(2)}) collective-permute-start(bf16[128,512]{1,0:T(8,128)(2,1)S(1)} %slice.34), channel_id=1, source_target_pairs={{0,16},{1,17},{2,18},{3,19},{4,20},{5,21},{6,22},{7,23},{8,24},{9,... | collective-permute-start | bytes 393224 | tf_op jit(solution)/shard_map/ppermute | solution.py:148
  29.5 11.4 %collective-permute-start.15 = (bf16[128,512]{1,0:T(8,128)(2,1)S(1)}, bf16[128,512]{1,0:T(8,128)(2,1)S(1)}, u32[]{:S(2)}, u32[]{:S(2)}) collective-permute-start(bf16[128,512]{1,0:T(8,128)(2,1)S(1)} %add_convert_fusion), channel_id=1, source_target_pairs={{0,6},{1,7},{2,4},{3,5},{4,2},{5,3},{6,0},{7,1},{8,14},{9,15},{10,... | collective-permute-start | bytes 393224 | tf_op jit(solution)/shard_map/ppermute | solution.py:148
  33.3 7.7 %collective-permute-start.8 = (bf16[128,512]{1,0:T(8,128)(2,1)S(1)}, bf16[128,512]{1,0:T(8,128)(2,1)S(1)}, u32[]{:S(2)}, u32[]{:S(2)}) collective-permute-start(bf16[128,512]{1,0:T(8,128)(2,1)S(1)} %fusion), channel_id=1, source_target_pairs={{0,2},{1,3},{2,0},{3,1},{4,6},{5,7},{6,4},{7,5},{8,10},{9,11},{10,... | collective-permute-start | bytes 393224 | tf_op jit(solution)/shard_map/ppermute | solution.py:148
  34.7 6.2 %collective-permute-start.5 = (bf16[128,512]{1,0:T(8,128)(2,1)S(1)}, bf16[128,512]{1,0:T(8,128)(2,1)S(1)}, u32[]{:S(2)}, u32[]{:S(2)}) collective-permute-start(bf16[128,512]{1,0:T(8,128)(2,1)S(1)} %slice.35), channel_id=1, source_target_pairs={{0,1},{1,0},{2,3},{3,2},{4,5},{5,4},{6,7},{7,6},{8,9},{9,8},{10,11... | collective-permute-start | bytes 393224 | tf_op jit(solution)/shard_map/ppermute | solution.py:148
  35.8 4.3 %collective-permute-start.9 = (bf16[32,512]{1,0:T(8,128)(2,1)S(1)}, bf16[32,512]{1,0:T(8,128)(2,1)S(1)}, u32[]{:S(2)}, u32[]{:S(2)}) collective-permute-start(bf16[32,512]{1,0:T(8,128)(2,1)S(1)} %get-tuple-element.33), channel_id=1, source_target_pairs={{0,16},{1,17},{2,18},{3,19},{4,20},{5,21},{6,22},{7,23},{8,24},{9,... | collective-permute-start | bytes 98312 | tf_op jit(solution)/shard_map/ppermute | solution.py:148
  41.0 5.0 %collective-permute-start.16 = (bf16[128,512]{1,0:T(8,128)(2,1)S(1)}, bf16[128,512]{1,0:T(8,128)(2,1)S(1)}, u32[]{:S(2)}, u32[]{:S(2)}) collective-permute-start(bf16[128,512]{1,0:T(8,128)(2,1)S(1)} %fusion.3.mine_ref), channel_id=1, source_target_pairs={{0,16},{1,17},{2,18},{3,19},{4,20},{5,21},{6,22},{7,23},{8,24},{9,... | collective-permute-start | bytes 393224 | tf_op jit(solution)/shard_map/ppermute | solution.py:148
  46.1 1.6 %collective-permute-start.17 = (bf16[2,128,512]{2,1,0:T(8,128)(2,1)S(1)}, bf16[2,128,512]{2,1,0:T(8,128)(2,1)S(1)}, u32[]{:S(2)}, u32[]{:S(2)}) collective-permute-start(bf16[2,128,512]{2,1,0:T(8,128)(2,1)S(1)} %pad_maximum_fusion), channel_id=1, source_target_pairs={{0,8},{1,9},{2,10},{3,11},{4,12},{5,13},{6,14},{7,15},{8,0},{9,1},... | collective-permute-start | bytes 786440 | tf_op jit(solution)/shard_map/ppermute | solution.py:148

commit v5 on v4

--- a/solution.py
+++ b/solution.py
@@ -140,7 +140,7 @@
     )(*[arg if arg is exponent else pltpu.with_memory_space_constraint(arg, pltpu.HBM) for arg in args])
 
 
-CORE, Y, X = 8, 16, 1
+CORE, Y, X, Z1, Z2 = 8, 16, 1, 2, 4
 
 
 def xor_permute(value, mask):
@@ -258,6 +258,22 @@
     )(mine, from_y, near)
 
 
+def fold_kernel(base_ref, arrived_ref, out_ref):
+    out_ref[...] = base_ref[...] + arrived_ref[...].astype(F32)
+
+
+def fold(base, arrived):
+    return pl.pallas_call(
+        fold_kernel,
+        in_specs=[VMEM] * 2,
+        out_specs=VMEM,
+        out_shape=jax.ShapeDtypeStruct(base.shape, F32),
+        compiler_params=pltpu.CompilerParams(vmem_limit_bytes=8 * MIB),
+        cost_estimate=pl.CostEstimate(flops=6_000_000_000, bytes_accessed=0, transcendentals=0),
+        name="fold",
+    )(base, arrived)
+
+
 def reduce_by_axis(layer_input, *args):
     near = xor_permute(layer_input, CORE)
     v0 = front(*args)
@@ -266,36 +282,50 @@
     def sums(parts, dtype):
         return partial_sums(parts, dtype, layer_input, near, v0, v1)
 
-    far_a, far_b = sums((((2, 1, 1),), ((3, 1, 1),)), BF16)
-    side_a, side_b = sums((((2, 1, 0),), ((3, 0, 1),)), BF16)
-    late_a, late_b = sums((((0, 1, 1), (0, 1, 0)), ((1, 1, 1), (1, 0, 1))), BF16)
-    keep_far_a, keep_far_b = sums((((2, 0, 1),), ((3, 1, 0),)), F32)
-    keep_a, keep_b = sums((((2, 0, 0),), ((3, 0, 0),)), F32)
-    keep_late_a, keep_late_b = sums((((0, 0, 1), (0, 0, 0)), ((1, 1, 0), (1, 0, 0))), F32)
-
+    def after_all(*values):
+        return lax.optimization_barrier(values)
+
+    def add(*terms):
+        total = terms[0]
+        for term in terms[1:]:
+            total = total + term.astype(F32)
+        return total
+
+    far_b, far_a = sums((((3, 1, 1),), ((2, 1, 1),)), BF16)
+    side_b, side_a = sums((((3, 0, 1),), ((2, 1, 0),)), BF16)
+    pair, = sums((((1, 1, 1), (1, 1, 0), (1, 0, 1), (1, 0, 0)),), BF16)
+    keep_far_b, keep_far_a = sums((((3, 1, 0),), ((2, 0, 1),)), F32)
+    keep_b, keep_a = sums((((3, 0, 0),), ((2, 0, 0),)), F32)
+    own, = sums((((0, 1, 1), (0, 1, 0), (0, 0, 1), (0, 0, 0)),), F32)
+    far_b = xor_permute(far_b, X)
     far_a = xor_permute(far_a, Y)
-    far_b = xor_permute(far_b, X)
+    side_b = xor_permute(side_b, X)
+    pair = xor_permute(pair, Z1)
+    on_b = add(keep_far_b, far_b).astype(BF16)
+    rows, window = inner_swap(v0, v1)
+    side_a = after_all(jnp.concatenate([side_a, window]), on_b)[0]
+    on_b = xor_permute(on_b, Y)
     side_a = xor_permute(side_a, Y)
-    side_b = xor_permute(side_b, X)
-    on_a = (keep_far_a + far_a.astype(F32)).astype(BF16)
-    on_b = (keep_far_b + far_b.astype(F32)).astype(BF16)
-    on_a, on_b, late_a, late_b = lax.optimization_barrier((on_a, on_b, late_a, late_b))
-    on_a = xor_permute(on_a, X)
-    on_b = xor_permute(on_b, Y)
-    late_a = xor_permute(late_a, Y)
-    late_b = xor_permute(late_b, X)
-    z2 = xor_permute((keep_a + side_a.astype(F32) + on_a.astype(F32)).astype(BF16), 4)
-    z3 = xor_permute((keep_b + side_b.astype(F32) + on_b.astype(F32)).astype(BF16), 6)
-    half_a = keep_late_a + late_a.astype(F32)
-    half_b = keep_late_b + late_b.astype(F32)
-    on_late_a = xor_permute(half_a[:LANE].astype(BF16), X)
-    on_late_b = xor_permute(half_b[:LANE].astype(BF16), Y)
-    z0 = half_a[LANE:] + on_late_a.astype(F32)
-    z1 = xor_permute((half_b[LANE:] + on_late_b.astype(F32)).astype(BF16), 2)
-    rows, window = inner_swap(v0, v1)
-    value_grad = outer_swap(v0, rows, xor_permute(window, Y))
-    z1, value_grad = lax.optimization_barrier((z1, value_grad))
-    mine = (z0 + z1.astype(F32) + (z2.astype(F32) + z3.astype(F32))).astype(BF16)
+    side_a, window = side_a[:LANE], side_a[LANE:]
+    on_a = xor_permute(add(keep_far_a, far_a).astype(BF16), X)
+    z3 = add(keep_b, side_b, on_b).astype(BF16)
+    pair, window = after_all(pair, window, z3)[:2]
+    z3 = xor_permute(z3, Z1)
+    value_grad = outer_swap(v0, rows, window)
+    on_a, value_grad = after_all(on_a, value_grad)
+    z2 = add(keep_a, side_a, on_a, z3).astype(BF16)
+
+    total = add(own, pair)
+    some, rest = total[:, :256], total[:, 256:]
+    rest_far, rest_y, rest_x, rest_own = (rest[row:row + LANE] for row in range(0, 4 * LANE, LANE))
+    some_in = xor_permute(some[:2 * LANE].astype(BF16), Y)
+    rest_in = xor_permute(jnp.concatenate([rest_far, rest_x]).astype(BF16), X)
+    some_in, rest_in = after_all(some_in, rest_in, z2)[:2]
+    z2 = xor_permute(z2, Z2)
+    some_on = xor_permute(add(some[2 * LANE:3 * LANE], some_in[:LANE]).astype(BF16), X)
+    rest_on = xor_permute(add(rest_y, rest_in[:LANE]).astype(BF16), Y)
+    base = jnp.concatenate([add(some[3 * LANE:], some_in[LANE:]), add(rest_own, rest_in[LANE:])], axis=1)
+    mine = add(fold(base, z2), jnp.concatenate([some_on, rest_on], axis=1)).astype(BF16)
     from_y = xor_permute(mine, Y)
     return place(mine, from_y, xor_permute(jnp.stack([mine, from_y]), CORE)), value_grad
 

time: 48.9 us -> 48.4 us (0.990)
  starting transfers between devices: 22.8 us -> 20.9 us
  waiting for transfers between devices: 15.2 us -> 16.5 us
    ppermute x18 -> x17, starting transfers between devices: 22.8 us -> 20.9 us  [xor_permute(): lax.ppermute(value, ('dp', 'fsdp'), [(i, i ^ mask) for i in range(count)])]
    ppermute x18 -> x17, waiting for transfers between devices: 15.2 us -> 16.5 us  [xor_permute(): lax.ppermute(value, ('dp', 'fsdp'), [(i, i ^ mask) for i in range(count)])]
  transfers between devices with their start and end apart: 18 -> 17, of which waited for: 8 -> 11; matrix products, arithmetic and copies ran while one was open for 1% -> 1% of each run, Pallas kernels for 15% -> 15%
where the time goes in v5:
time: 48.4 us; the launch traced here: 48.2 us
  starting transfers between devices  20.9 us (43%)
  waiting for transfers between devices  16.5 us (34%)
  Pallas kernels  8.74 us (18%)
  between operations  1.56 us (3%)
  other arithmetic  0.5 us (1%)
    ppermute x17, starting transfers between devices, xor_permute(): lax.ppermute(value, ('dp', 'fsdp'), [(i, i ^ mask) for i in range(count)])  20.9 us
    ppermute x17, waiting for transfers between devices, xor_permute(): lax.ppermute(value, ('dp', 'fsdp'), [(i, i ^ mask) for i in range(count)])  16.5 us
    pallas_call x1, Pallas kernels, front(): pl.pallas_call(functools.partial(front_kernel, per_group), in_specs=[HBM]...  4.05 us
    pallas_call x6, Pallas kernels, partial_sums(): pl.pallas_call(functools.partial(partial_kernel, parts), in_specs=[VMEM]...  2.37 us
    pallas_call x1, Pallas kernels, place(): pl.pallas_call(place_kernel, in_specs=[VMEM] * 3, out_specs=VMEM, out_sha...  1.05 us
  transfers between devices with their start and end apart: 17, of which 11 were waited for; matrix products, arithmetic and copies ran while one was open for 1% of the time, Pallas kernels for 15%

profile of v5, /device:TPU:0, one launch (start us, length us, event | category | flops | bytes accessed | tf_op | source)
XLA Modules:
  0.0 48.2 jit_solution(2054564639181555344)
XLA Ops:
  0.6 0.0 copy-start
  0.6 0.5 %collective-permute-start = (bf16[256,4096]{1,0:T(8,128)(2,1)}, bf16[256,4096]{1,0:T(8,128)(2,1)S(1)}, u32[]{:S(2)}, u32[]{:S(2)}) collective-permute-start(bf16[256,4096]{1,0:T(8,128)(2,1)} %own_ref.11), channel_id=1, source_target_pairs={{0,8},{1,9},{2,10},{3,11},{4,12},{5,13},{6,14},{7,15},{8,0},{9,1},... | collective-permute-start | bytes 6291464 | tf_op jit(solution)/shard_map/ppermute | solution.py:148
  1.9 4.1 %front.1.v0_ref = bf16[272,512]{1,0:T(8,128)(2,1)S(1)} custom-call(f32[16]{0:T(128)} %loss_hbm.1, s32[1]{0:T(128)S(6)} %copy.12.exponent_hbm, s32[1,2]{1,0:T(1,128)} %start_hbm.1, s32[1,2]{1,0:T(1,128)} %rows_hbm.1, bf16[256,2048]{1,0:T(8,128)(2,1)} %q_hbm.1, bf16[256,512]{1,0:T(8,128)(2,1)} %k_hbm.1, bf16[256,2048]{1,0:T(8,128)(2,1)} %g_hbm.1, ...), custom_call_target="tpu_custom_call" | custom-call | tf_op jit(solution)/shard_map/front/pallas_call | solution.py:125
  6.0 0.1 collective-permute-start.1
  6.1 1.5 %collective-permute-done.1.v1_ref = bf16[272,512]{1,0:T(8,128)(2,1)S(1)} collective-permute-done((bf16[272,512]{1,0:T(8,128)(2,1)S(1)}, bf16[272,512]{1,0:T(8,128)(2,1)S(1)}, u32[]{:S(2)}, u32[]{:S(2)}) %collective-permute-start.1) | collective-permute-done | bytes 278560 | tf_op jit(solution)/shard_map/ppermute | solution.py:148
  7.6 0.0 collective-permute-done.near_ref
  7.6 0.3 partial_sums.10
  8.0 2.6 %collective-permute-start.3 = (bf16[128,512]{1,0:T(8,128)(2,1)S(1)}, bf16[128,512]{1,0:T(8,128)(2,1)S(1)}, u32[]{:S(2)}, u32[]{:S(2)}) collective-permute-start(bf16[128,512]{1,0:T(8,128)(2,1)S(1)} %get-tuple-element.22), channel_id=1, source_target_pairs={{0,1},{1,0},{2,3},{3,2},{4,5},{5,4},{6,7},{7,6},{8,9},{9,8},{10,11... | collective-permute-start | bytes 393224 | tf_op jit(solution)/shard_map/ppermute | solution.py:148
  10.6 0.3 inner_swap.1
  10.9 0.4 partial_sums.8
  11.3 0.1 collective-permute-start.5
  11.3 0.5 %partial_sums.7 = bf16[512,512]{1,0:T(8,128)(2,1)S(1)} custom-call(bf16[256,4096]{1,0:T(8,128)(2,1)S(1)} %copy-done, bf16[256,4096]{1,0:T(8,128)(2,1)S(1)} %collective-permute-done.near_ref, bf16[272,512]{1,0:T(8,128)(2,1)S(1)} %front.1.v0_ref, bf16[272,512]{1,0:T(8,128)(2,1)S(1)} %collective-permute-done.1.v1_ref), custom_call_target="tpu_custom_call" | custom-call | tf_op jit(solution)/shard_map/partial_sums/pallas_call | solution.py:168
  11.8 2.2 %collective-permute-start.2 = (bf16[512,512]{1,0:T(8,128)(2,1)S(1)}, bf16[512,512]{1,0:T(8,128)(2,1)S(1)}, u32[]{:S(2)}, u32[]{:S(2)}) collective-permute-start(bf16[512,512]{1,0:T(8,128)(2,1)S(1)} %partial_sums.7), channel_id=1, source_target_pairs={{0,2},{1,3},{2,0},{3,1},{4,6},{5,7},{6,4},{7,5},{8,10},{9,11},{10,... | collective-permute-start | bytes 1572872 | tf_op jit(solution)/shard_map/ppermute | solution.py:148
  14.0 1.5 %collective-permute-start.9 = (bf16[128,512]{1,0:T(8,128)(2,1)S(1)}, bf16[128,512]{1,0:T(8,128)(2,1)S(1)}, u32[]{:S(2)}, u32[]{:S(2)}) collective-permute-start(bf16[128,512]{1,0:T(8,128)(2,1)S(1)} %get-tuple-element.29), channel_id=1, source_target_pairs={{0,16},{1,17},{2,18},{3,19},{4,20},{5,21},{6,22},{7,23},{8,24},{9,... | collective-permute-start | bytes 393224 | tf_op jit(solution)/shard_map/ppermute | solution.py:148
  15.5 0.3 partial_sums.9
  15.9 0.3 partial_sums.11
  16.2 0.5 %partial_sums.6 = f32[512,512]{1,0:T(8,128)S(1)} custom-call(bf16[256,4096]{1,0:T(8,128)(2,1)S(1)} %copy-done, bf16[256,4096]{1,0:T(8,128)(2,1)S(1)} %collective-permute-done.near_ref, bf16[272,512]{1,0:T(8,128)(2,1)S(1)} %front.1.v0_ref, bf16[272,512]{1,0:T(8,128)(2,1)S(1)} %collective-permute-done.1.v1_ref), custom_call_target="tpu_custom_call" | custom-call | tf_op jit(solution)/shard_map/partial_sums/pallas_call | solution.py:168
  16.7 0.0 collective-permute-done.3
  16.8 0.6 %collective-permute-start.6 = (bf16[128,512]{1,0:T(8,128)(2,1)S(1)}, bf16[128,512]{1,0:T(8,128)(2,1)S(1)}, u32[]{:S(2)}, u32[]{:S(2)}) collective-permute-start(bf16[128,512]{1,0:T(8,128)(2,1)S(1)} %add_convert_fusion.4), channel_id=1, source_target_pairs={{0,16},{1,17},{2,18},{3,19},{4,20},{5,21},{6,22},{7,23},{8,24},{9,... | collective-permute-start | bytes 393224 | tf_op jit(solution)/shard_map/ppermute | solution.py:148
  17.4 1.5 %collective-permute-start.4 = (bf16[160,512]{1,0:T(8,128)(2,1)S(1)}, bf16[160,512]{1,0:T(8,128)(2,1)S(1)}, u32[]{:S(2)}, u32[]{:S(2)}) collective-permute-start(bf16[160,512]{1,0:T(8,128)(2,1)S(1)} %pad_maximum_fusion.2), channel_id=1, source_target_pairs={{0,16},{1,17},{2,18},{3,19},{4,20},{5,21},{6,22},{7,23},{8,24},{9,... | collective-permute-start | bytes 491528 | tf_op jit(solution)/shard_map/ppermute | solution.py:148
  18.9 0.4 collective-permute-done.9
  19.3 1.6 %collective-permute-start.10 = (bf16[128,512]{1,0:T(8,128)(2,1)S(1)}, bf16[128,512]{1,0:T(8,128)(2,1)S(1)}, u32[]{:S(2)}, u32[]{:S(2)}) collective-permute-start(bf16[128,512]{1,0:T(8,128)(2,1)S(1)} %add_convert_fusion.2), channel_id=1, source_target_pairs={{0,1},{1,0},{2,3},{3,2},{4,5},{5,4},{6,7},{7,6},{8,9},{9,8},{10,11... | collective-permute-start | bytes 393224 | tf_op jit(solution)/shard_map/ppermute | solution.py:148
  20.9 0.0 collective-permute-done.5
  20.9 2.4 %collective-permute-done.6 = bf16[128,512]{1,0:T(8,128)(2,1)S(1)} collective-permute-done((bf16[128,512]{1,0:T(8,128)(2,1)S(1)}, bf16[128,512]{1,0:T(8,128)(2,1)S(1)}, u32[]{:S(2)}, u32[]{:S(2)}) %collective-permute-start.6) | collective-permute-done | bytes 131104 | tf_op jit(solution)/shard_map/ppermute | solution.py:148
  23.3 0.5 %collective-permute-start.11 = (bf16[128,512]{1,0:T(8,128)(2,1)S(1)}, bf16[128,512]{1,0:T(8,128)(2,1)S(1)}, u32[]{:S(2)}, u32[]{:S(2)}) collective-permute-start(bf16[128,512]{1,0:T(8,128)(2,1)S(1)} %add_convert_fusion.3), channel_id=1, source_target_pairs={{0,2},{1,3},{2,0},{3,1},{4,6},{5,7},{6,4},{7,5},{8,10},{9,11},{10,... | collective-permute-start | bytes 393224 | tf_op jit(solution)/shard_map/ppermute | solution.py:148
  23.9 1.4 %collective-permute-done.4 = bf16[160,512]{1,0:T(8,128)(2,1)S(1)} collective-permute-done((bf16[160,512]{1,0:T(8,128)(2,1)S(1)}, bf16[160,512]{1,0:T(8,128)(2,1)S(1)}, u32[]{:S(2)}, u32[]{:S(2)}) %collective-permute-start.4) | collective-permute-done | bytes 163872 | tf_op jit(solution)/shard_map/ppermute | solution.py:148
  25.3 1.5 %collective-permute-done.2 = bf16[512,512]{1,0:T(8,128)(2,1)S(1)} collective-permute-done((bf16[512,512]{1,0:T(8,128)(2,1)S(1)}, bf16[512,512]{1,0:T(8,128)(2,1)S(1)}, u32[]{:S(2)}, u32[]{:S(2)}) %collective-permute-start.2) | collective-permute-done | bytes 524320 | tf_op jit(solution)/shard_map/ppermute | solution.py:148
  26.8 0.2 fusion.2
  27.0 0.9 %outer_swap.1 = bf16[256,512]{1,0:T(8,128)(2,1)} custom-call(bf16[272,512]{1,0:T(8,128)(2,1)S(1)} %front.1.v0_ref, bf16[256,512]{1,0:T(8,128)(2,1)S(1)} %get-tuple-element.30.rows_ref, bf16[32,512]{1,0:T(8,128)(2,1)S(1)} %slice.64.window_ref), custom_call_target="tpu_custom_call" | custom-call | tf_op jit(solution)/shard_map/outer_swap/pallas_call | solution.py:232
  27.9 0.0 collective-permute-done.10
  27.9 2.0 %collective-permute-start.8 = (bf16[256,256]{1,0:T(8,128)(2,1)S(1)}, bf16[256,256]{1,0:T(8,128)(2,1)S(1)}, u32[]{:S(2)}, u32[]{:S(2)}) collective-permute-start(bf16[256,256]{1,0:T(8,128)(2,1)S(1)} %pad_maximum_fusion.3), channel_id=1, source_target_pairs={{0,1},{1,0},{2,3},{3,2},{4,5},{5,4},{6,7},{7,6},{8,9},{9,8},{10,11... | collective-permute-start | bytes 393224 | tf_op jit(solution)/shard_map/ppermute | solution.py:148
  30.0 1.5 %collective-permute-start.7 = (bf16[256,256]{1,0:T(8,128)(2,1)S(1)}, bf16[256,256]{1,0:T(8,128)(2,1)S(1)}, u32[]{:S(2)}, u32[]{:S(2)}) collective-permute-start(bf16[256,256]{1,0:T(8,128)(2,1)S(1)} %slice.66), channel_id=1, source_target_pairs={{0,16},{1,17},{2,18},{3,19},{4,20},{5,21},{6,22},{7,23},{8,24},{9,... | collective-permute-start | bytes 393224 | tf_op jit(solution)/shard_map/ppermute | solution.py:148
  31.5 0.0 collective-permute-done.11
  31.5 0.1 add_convert_fusion.1
  31.6 2.7 %collective-permute-start.12 = (bf16[128,512]{1,0:T(8,128)(2,1)S(1)}, bf16[128,512]{1,0:T(8,128)(2,1)S(1)}, u32[]{:S(2)}, u32[]{:S(2)}) collective-permute-start(bf16[128,512]{1,0:T(8,128)(2,1)S(1)} %add_convert_fusion.1), channel_id=1, source_target_pairs={{0,4},{1,5},{2,6},{3,7},{4,0},{5,1},{6,2},{7,3},{8,12},{9,13},{10,... | collective-permute-start | bytes 393224 | tf_op jit(solution)/shard_map/ppermute | solution.py:148
  34.2 0.0 collective-permute-done.8
  34.2 1.3 %collective-permute-done.7 = bf16[256,256]{1,0:T(8,128)(2,1)S(1)} collective-permute-done((bf16[256,256]{1,0:T(8,128)(2,1)S(1)}, bf16[256,256]{1,0:T(8,128)(2,1)S(1)}, u32[]{:S(2)}, u32[]{:S(2)}) %collective-permute-start.7) | collective-permute-done | bytes 131104 | tf_op jit(solution)/shard_map/ppermute | solution.py:148
  35.5 0.1 fusion.1
  35.6 0.1 collective-permute-start.13
  35.7 1.7 %collective-permute-start.14 = (bf16[128,256]{1,0:T(8,128)(2,1)S(1)}, bf16[128,256]{1,0:T(8,128)(2,1)S(1)}, u32[]{:S(2)}, u32[]{:S(2)}) collective-permute-start(bf16[128,256]{1,0:T(8,128)(2,1)S(1)} %get-tuple-element.43), channel_id=1, source_target_pairs={{0,16},{1,17},{2,18},{3,19},{4,20},{5,21},{6,22},{7,23},{8,24},{9,... | collective-permute-start | bytes 196616 | tf_op jit(solution)/shard_map/ppermute | solution.py:148
  37.4 1.5 %collective-permute-done.12.arrived_ref = bf16[128,512]{1,0:T(8,128)(2,1)S(1)} collective-permute-done((bf16[128,512]{1,0:T(8,128)(2,1)S(1)}, bf16[128,512]{1,0:T(8,128)(2,1)S(1)}, u32[]{:S(2)}, u32[]{:S(2)}) %collective-permute-start.12) | collective-permute-done | bytes 131104 | tf_op jit(solution)/shard_map/ppermute | solution.py:148
  38.9 1.0 %collective-permute-done.13 = bf16[128,256]{1,0:T(8,128)(2,1)S(1)} collective-permute-done((bf16[128,256]{1,0:T(8,128)(2,1)S(1)}, bf16[128,256]{1,0:T(8,128)(2,1)S(1)}, u32[]{:S(2)}, u32[]{:S(2)}) %collective-permute-start.13) | collective-permute-done | bytes 65568 | tf_op jit(solution)/shard_map/ppermute | solution.py:148
  39.9 0.5 %collective-permute-done.14 = bf16[128,256]{1,0:T(8,128)(2,1)S(1)} collective-permute-done((bf16[128,256]{1,0:T(8,128)(2,1)S(1)}, bf16[128,256]{1,0:T(8,128)(2,1)S(1)}, u32[]{:S(2)}, u32[]{:S(2)}) %collective-permute-start.14) | collective-permute-done | bytes 65568 | tf_op jit(solution)/shard_map/ppermute | solution.py:148
  40.5 1.6 %collective-permute-start.15 = (bf16[128,512]{1,0:T(8,128)(2,1)S(1)}, bf16[128,512]{1,0:T(8,128)(2,1)S(1)}, u32[]{:S(2)}, u32[]{:S(2)}) collective-permute-start(bf16[128,512]{1,0:T(8,128)(2,1)S(1)} %add_convert_fusion.mine_ref), channel_id=1, source_target_pairs={{0,16},{1,17},{2,18},{3,19},{4,20},{5,21},{6,22},{7,23},{8,24},{9,... | collective-permute-start | bytes 393224 | tf_op jit(solution)/shard_map/ppermute | solution.py:148
  42.1 3.4 %collective-permute-done.15.y_ref = bf16[128,512]{1,0:T(8,128)(2,1)S(1)} collective-permute-done((bf16[128,512]{1,0:T(8,128)(2,1)S(1)}, bf16[128,512]{1,0:T(8,128)(2,1)S(1)}, u32[]{:S(2)}, u32[]{:S(2)}) %collective-permute-start.15) | collective-permute-done | bytes 131104 | tf_op jit(solution)/shard_map/ppermute | solution.py:148
  45.5 0.1 collective-permute-start.16
  45.6 1.5 %collective-permute-done.16.near_ref = bf16[2,128,512]{2,1,0:T(8,128)(2,1)S(1)} collective-permute-done((bf16[2,128,512]{2,1,0:T(8,128)(2,1)S(1)}, bf16[2,128,512]{2,1,0:T(8,128)(2,1)S(1)}, u32[]{:S(2)}, u32[]{:S(2)}) %collective-permute-start.16) | collective-permute-done | bytes 262176 | tf_op jit(solution)/shard_map/ppermute | solution.py:148
  47.1 1.0 %place.1 = f32[512,512]{1,0:T(8,128)} custom-call(bf16[128,512]{1,0:T(8,128)(2,1)S(1)} %add_convert_fusion.mine_ref, bf16[128,512]{1,0:T(8,128)(2,1)S(1)} %collective-permute-done.15.y_ref, bf16[2,128,512]{2,1,0:T(8,128)(2,1)S(1)} %collective-permute-done.16.near_ref), custom_call_target="tpu_custom_call" | custom-call | tf_op jit(solution)/shard_map/place/pallas_call | solution.py:250
  (13 shorter events, 0.2 us)
Async XLA Ops:
  0.6 7.0 %copy-start = (bf16[256,4096]{1,0:T(8,128)(2,1)S(1)}, bf16[256,4096]{1,0:T(8,128)(2,1)}, u32[]{:S(2)}) copy-start(bf16[256,4096]{1,0:T(8,128)(2,1)} %own_ref.11) | copy-start | bytes 6291460
  0.6 7.0 %collective-permute-start = (bf16[256,4096]{1,0:T(8,128)(2,1)}, bf16[256,4096]{1,0:T(8,128)(2,1)S(1)}, u32[]{:S(2)}, u32[]{:S(2)}) collective-permute-start(bf16[256,4096]{1,0:T(8,128)(2,1)} %own_ref.11), channel_id=1, source_target_pairs={{0,8},{1,9},{2,10},{3,11},{4,12},{5,13},{6,14},{7,15},{8,0},{9,1},... | collective-permute-start | bytes 6291464 | tf_op jit(solution)/shard_map/ppermute | solution.py:148
  6.0 1.6 %collective-permute-start.1 = (bf16[272,512]{1,0:T(8,128)(2,1)S(1)}, bf16[272,512]{1,0:T(8,128)(2,1)S(1)}, u32[]{:S(2)}, u32[]{:S(2)}) collective-permute-start(bf16[272,512]{1,0:T(8,128)(2,1)S(1)} %front.1.v0_ref), channel_id=1, source_target_pairs={{0,8},{1,9},{2,10},{3,11},{4,12},{5,13},{6,14},{7,15},{8,0},{9,1},... | collective-permute-start | bytes 835592 | tf_op jit(solution)/shard_map/ppermute | solution.py:148
  8.0 8.8 %collective-permute-start.3 = (bf16[128,512]{1,0:T(8,128)(2,1)S(1)}, bf16[128,512]{1,0:T(8,128)(2,1)S(1)}, u32[]{:S(2)}, u32[]{:S(2)}) collective-permute-start(bf16[128,512]{1,0:T(8,128)(2,1)S(1)} %get-tuple-element.22), channel_id=1, source_target_pairs={{0,1},{1,0},{2,3},{3,2},{4,5},{5,4},{6,7},{7,6},{8,9},{9,8},{10,11... | collective-permute-start | bytes 393224 | tf_op jit(solution)/shard_map/ppermute | solution.py:148
  11.3 9.6 %collective-permute-start.5 = (bf16[128,512]{1,0:T(8,128)(2,1)S(1)}, bf16[128,512]{1,0:T(8,128)(2,1)S(1)}, u32[]{:S(2)}, u32[]{:S(2)}) collective-permute-start(bf16[128,512]{1,0:T(8,128)(2,1)S(1)} %get-tuple-element.25), channel_id=1, source_target_pairs={{0,1},{1,0},{2,3},{3,2},{4,5},{5,4},{6,7},{7,6},{8,9},{9,8},{10,11... | collective-permute-start | bytes 393224 | tf_op jit(solution)/shard_map/ppermute | solution.py:148
  11.8 14.9 %collective-permute-start.2 = (bf16[512,512]{1,0:T(8,128)(2,1)S(1)}, bf16[512,512]{1,0:T(8,128)(2,1)S(1)}, u32[]{:S(2)}, u32[]{:S(2)}) collective-permute-start(bf16[512,512]{1,0:T(8,128)(2,1)S(1)} %partial_sums.7), channel_id=1, source_target_pairs={{0,2},{1,3},{2,0},{3,1},{4,6},{5,7},{6,4},{7,5},{8,10},{9,11},{10,... | collective-permute-start | bytes 1572872 | tf_op jit(solution)/shard_map/ppermute | solution.py:148
  14.0 5.3 %collective-permute-start.9 = (bf16[128,512]{1,0:T(8,128)(2,1)S(1)}, bf16[128,512]{1,0:T(8,128)(2,1)S(1)}, u32[]{:S(2)}, u32[]{:S(2)}) collective-permute-start(bf16[128,512]{1,0:T(8,128)(2,1)S(1)} %get-tuple-element.29), channel_id=1, source_target_pairs={{0,16},{1,17},{2,18},{3,19},{4,20},{5,21},{6,22},{7,23},{8,24},{9,... | collective-permute-start | bytes 393224 | tf_op jit(solution)/shard_map/ppermute | solution.py:148
  16.8 6.5 %collective-permute-start.6 = (bf16[128,512]{1,0:T(8,128)(2,1)S(1)}, bf16[128,512]{1,0:T(8,128)(2,1)S(1)}, u32[]{:S(2)}, u32[]{:S(2)}) collective-permute-start(bf16[128,512]{1,0:T(8,128)(2,1)S(1)} %add_convert_fusion.4), channel_id=1, source_target_pairs={{0,16},{1,17},{2,18},{3,19},{4,20},{5,21},{6,22},{7,23},{8,24},{9,... | collective-permute-start | bytes 393224 | tf_op jit(solution)/shard_map/ppermute | solution.py:148
  17.4 7.9 %collective-permute-start.4 = (bf16[160,512]{1,0:T(8,128)(2,1)S(1)}, bf16[160,512]{1,0:T(8,128)(2,1)S(1)}, u32[]{:S(2)}, u32[]{:S(2)}) collective-permute-start(bf16[160,512]{1,0:T(8,128)(2,1)S(1)} %pad_maximum_fusion.2), channel_id=1, source_target_pairs={{0,16},{1,17},{2,18},{3,19},{4,20},{5,21},{6,22},{7,23},{8,24},{9,... | collective-permute-start | bytes 491528 | tf_op jit(solution)/shard_map/ppermute | solution.py:148
  19.3 8.6 %collective-permute-start.10 = (bf16[128,512]{1,0:T(8,128)(2,1)S(1)}, bf16[128,512]{1,0:T(8,128)(2,1)S(1)}, u32[]{:S(2)}, u32[]{:S(2)}) collective-permute-start(bf16[128,512]{1,0:T(8,128)(2,1)S(1)} %add_convert_fusion.2), channel_id=1, source_target_pairs={{0,1},{1,0},{2,3},{3,2},{4,5},{5,4},{6,7},{7,6},{8,9},{9,8},{10,11... | collective-permute-start | bytes 393224 | tf_op jit(solution)/shard_map/ppermute | solution.py:148
  23.3 8.2 %collective-permute-start.11 = (bf16[128,512]{1,0:T(8,128)(2,1)S(1)}, bf16[128,512]{1,0:T(8,128)(2,1)S(1)}, u32[]{:S(2)}, u32[]{:S(2)}) collective-permute-start(bf16[128,512]{1,0:T(8,128)(2,1)S(1)} %add_convert_fusion.3), channel_id=1, source_target_pairs={{0,2},{1,3},{2,0},{3,1},{4,6},{5,7},{6,4},{7,5},{8,10},{9,11},{10,... | collective-permute-start | bytes 393224 | tf_op jit(solution)/shard_map/ppermute | solution.py:148
  27.9 6.3 %collective-permute-start.8 = (bf16[256,256]{1,0:T(8,128)(2,1)S(1)}, bf16[256,256]{1,0:T(8,128)(2,1)S(1)}, u32[]{:S(2)}, u32[]{:S(2)}) collective-permute-start(bf16[256,256]{1,0:T(8,128)(2,1)S(1)} %pad_maximum_fusion.3), channel_id=1, source_target_pairs={{0,1},{1,0},{2,3},{3,2},{4,5},{5,4},{6,7},{7,6},{8,9},{9,8},{10,11... | collective-permute-start | bytes 393224 | tf_op jit(solution)/shard_map/ppermute | solution.py:148
  30.0 5.6 %collective-permute-start.7 = (bf16[256,256]{1,0:T(8,128)(2,1)S(1)}, bf16[256,256]{1,0:T(8,128)(2,1)S(1)}, u32[]{:S(2)}, u32[]{:S(2)}) collective-permute-start(bf16[256,256]{1,0:T(8,128)(2,1)S(1)} %slice.66), channel_id=1, source_target_pairs={{0,16},{1,17},{2,18},{3,19},{4,20},{5,21},{6,22},{7,23},{8,24},{9,... | collective-permute-start | bytes 393224 | tf_op jit(solution)/shard_map/ppermute | solution.py:148
  31.6 7.3 %collective-permute-start.12 = (bf16[128,512]{1,0:T(8,128)(2,1)S(1)}, bf16[128,512]{1,0:T(8,128)(2,1)S(1)}, u32[]{:S(2)}, u32[]{:S(2)}) collective-permute-start(bf16[128,512]{1,0:T(8,128)(2,1)S(1)} %add_convert_fusion.1), channel_id=1, source_target_pairs={{0,4},{1,5},{2,6},{3,7},{4,0},{5,1},{6,2},{7,3},{8,12},{9,13},{10,... | collective-permute-start | bytes 393224 | tf_op jit(solution)/shard_map/ppermute | solution.py:148
  35.6 4.3 %collective-permute-start.13 = (bf16[128,256]{1,0:T(8,128)(2,1)S(1)}, bf16[128,256]{1,0:T(8,128)(2,1)S(1)}, u32[]{:S(2)}, u32[]{:S(2)}) collective-permute-start(bf16[128,256]{1,0:T(8,128)(2,1)S(1)} %get-tuple-element.38), channel_id=1, source_target_pairs={{0,1},{1,0},{2,3},{3,2},{4,5},{5,4},{6,7},{7,6},{8,9},{9,8},{10,11... | collective-permute-start | bytes 196616 | tf_op jit(solution)/shard_map/ppermute | solution.py:148
  35.7 4.8 %collective-permute-start.14 = (bf16[128,256]{1,0:T(8,128)(2,1)S(1)}, bf16[128,256]{1,0:T(8,128)(2,1)S(1)}, u32[]{:S(2)}, u32[]{:S(2)}) collective-permute-start(bf16[128,256]{1,0:T(8,128)(2,1)S(1)} %get-tuple-element.43), channel_id=1, source_target_pairs={{0,16},{1,17},{2,18},{3,19},{4,20},{5,21},{6,22},{7,23},{8,24},{9,... | collective-permute-start | bytes 196616 | tf_op jit(solution)/shard_map/ppermute | solution.py:148
  40.5 5.0 %collective-permute-start.15 = (bf16[128,512]{1,0:T(8,128)(2,1)S(1)}, bf16[128,512]{1,0:T(8,128)(2,1)S(1)}, u32[]{:S(2)}, u32[]{:S(2)}) collective-permute-start(bf16[128,512]{1,0:T(8,128)(2,1)S(1)} %add_convert_fusion.mine_ref), channel_id=1, source_target_pairs={{0,16},{1,17},{2,18},{3,19},{4,20},{5,21},{6,22},{7,23},{8,24},{9,... | collective-permute-start | bytes 393224 | tf_op jit(solution)/shard_map/ppermute | solution.py:148
  45.5 1.6 %collective-permute-start.16 = (bf16[2,128,512]{2,1,0:T(8,128)(2,1)S(1)}, bf16[2,128,512]{2,1,0:T(8,128)(2,1)S(1)}, u32[]{:S(2)}, u32[]{:S(2)}) collective-permute-start(bf16[2,128,512]{2,1,0:T(8,128)(2,1)S(1)} %pad_maximum_fusion.1), channel_id=1, source_target_pairs={{0,8},{1,9},{2,10},{3,11},{4,12},{5,13},{6,14},{7,15},{8,0},{9,1},... | collective-permute-start | bytes 786440 | tf_op jit(solution)/shard_map/ppermute | solution.py:148

commit v6 on v5

--- a/solution.py
+++ b/solution.py
@@ -291,40 +291,33 @@
             total = total + term.astype(F32)
         return total
 
-    far_b, far_a = sums((((3, 1, 1),), ((2, 1, 1),)), BF16)
-    side_b, side_a = sums((((3, 0, 1),), ((2, 1, 0),)), BF16)
+    first_b, first_a = sums((((3, 1, 1), (3, 0, 1)), ((2, 1, 1), (2, 1, 0))), BF16)
+    rows, window = inner_swap(v0, v1)
     pair, = sums((((1, 1, 1), (1, 1, 0), (1, 0, 1), (1, 0, 0)),), BF16)
-    keep_far_b, keep_far_a = sums((((3, 1, 0),), ((2, 0, 1),)), F32)
-    keep_b, keep_a = sums((((3, 0, 0),), ((2, 0, 0),)), F32)
+    keep_b, keep_a = sums((((3, 1, 0), (3, 0, 0)), ((2, 0, 1), (2, 0, 0))), F32)
     own, = sums((((0, 1, 1), (0, 1, 0), (0, 0, 1), (0, 0, 0)),), F32)
-    far_b = xor_permute(far_b, X)
-    far_a = xor_permute(far_a, Y)
-    side_b = xor_permute(side_b, X)
+    first_b = xor_permute(first_b, X)
+    first_a = xor_permute(jnp.concatenate([first_a, window]), Y)
     pair = xor_permute(pair, Z1)
-    on_b = add(keep_far_b, far_b).astype(BF16)
-    rows, window = inner_swap(v0, v1)
-    side_a = after_all(jnp.concatenate([side_a, window]), on_b)[0]
-    on_b = xor_permute(on_b, Y)
-    side_a = xor_permute(side_a, Y)
-    side_a, window = side_a[:LANE], side_a[LANE:]
-    on_a = xor_permute(add(keep_far_a, far_a).astype(BF16), X)
-    z3 = add(keep_b, side_b, on_b).astype(BF16)
-    pair, window = after_all(pair, window, z3)[:2]
+    on_b = xor_permute(add(keep_b[:LANE], first_b[:LANE]).astype(BF16), Y)
+    on_a = xor_permute(add(keep_a[:LANE], first_a[:LANE]).astype(BF16), X)
+    z3 = add(keep_b[LANE:], first_b[LANE:], on_b).astype(BF16)
+    pair = after_all(pair, z3)[0]
     z3 = xor_permute(z3, Z1)
-    value_grad = outer_swap(v0, rows, window)
-    on_a, value_grad = after_all(on_a, value_grad)
-    z2 = add(keep_a, side_a, on_a, z3).astype(BF16)
+    z2 = add(keep_a[LANE:], first_a[LANE:2 * LANE], on_a, z3).astype(BF16)
 
     total = add(own, pair)
     some, rest = total[:, :256], total[:, 256:]
     rest_far, rest_y, rest_x, rest_own = (rest[row:row + LANE] for row in range(0, 4 * LANE, LANE))
     some_in = xor_permute(some[:2 * LANE].astype(BF16), Y)
     rest_in = xor_permute(jnp.concatenate([rest_far, rest_x]).astype(BF16), X)
-    some_in, rest_in = after_all(some_in, rest_in, z2)[:2]
+    some_in, rest_in, window = after_all(some_in, rest_in, first_a[2 * LANE:], z2)[:3]
     z2 = xor_permute(z2, Z2)
     some_on = xor_permute(add(some[2 * LANE:3 * LANE], some_in[:LANE]).astype(BF16), X)
     rest_on = xor_permute(add(rest_y, rest_in[:LANE]).astype(BF16), Y)
+    value_grad = outer_swap(v0, rows, window)
     base = jnp.concatenate([add(some[3 * LANE:], some_in[LANE:]), add(rest_own, rest_in[LANE:])], axis=1)
+    base, value_grad = after_all(base, value_grad)
     mine = add(fold(base, z2), jnp.concatenate([some_on, rest_on], axis=1)).astype(BF16)
     from_y = xor_permute(mine, Y)
     return place(mine, from_y, xor_permute(jnp.stack([mine, from_y]), CORE)), value_grad

time: 48.4 us -> 48.6 us (level)
  waiting for transfers between devices: 16.5 us -> 21.2 us
  starting transfers between devices: 20.9 us -> 16.8 us
    ppermute x17 -> x15, waiting for transfers between devices: 16.5 us -> 21.2 us  [xor_permute(): lax.ppermute(value, ('dp', 'fsdp'), [(i, i ^ mask) for i in range(count)])]
    ppermute x17 -> x15, starting transfers between devices: 20.9 us -> 16.8 us  [xor_permute(): lax.ppermute(value, ('dp', 'fsdp'), [(i, i ^ mask) for i in range(count)])]
    pallas_call x6 -> x4, Pallas kernels: 2.37 us -> 1.93 us  [partial_sums(): pl.pallas_call(functools.partial(partial_kernel, parts), in_specs=[VMEM]...]
  transfers between devices with their start and end apart: 17 -> 15, of which waited for: 11 -> 13; matrix products, arithmetic and copies ran while one was open for 1% -> 1% of each run, Pallas kernels for 15% -> 14%
where the time goes in v6:
time: 48.6 us; the launch traced here: 48.4 us
  waiting for transfers between devices  21.2 us (44%)
  starting transfers between devices  16.8 us (35%)
  Pallas kernels  8.3 us (17%)
  between operations  1.53 us (3%)
  other arithmetic  0.51 us (1%)
    ppermute x15, waiting for transfers between devices, xor_permute(): lax.ppermute(value, ('dp', 'fsdp'), [(i, i ^ mask) for i in range(count)])  21.2 us
    ppermute x15, starting transfers between devices, xor_permute(): lax.ppermute(value, ('dp', 'fsdp'), [(i, i ^ mask) for i in range(count)])  16.8 us
    pallas_call x1, Pallas kernels, front(): pl.pallas_call(functools.partial(front_kernel, per_group), in_specs=[HBM]...  4.05 us
    pallas_call x4, Pallas kernels, partial_sums(): pl.pallas_call(functools.partial(partial_kernel, parts), in_specs=[VMEM]...  1.93 us
    pallas_call x1, Pallas kernels, place(): pl.pallas_call(place_kernel, in_specs=[VMEM] * 3, out_specs=VMEM, out_sha...  1.05 us
  transfers between devices with their start and end apart: 15, of which 13 were waited for; matrix products, arithmetic and copies ran while one was open for 1% of the time, Pallas kernels for 14%

profile of v6, /device:TPU:0, one launch (start us, length us, event | category | flops | bytes accessed | tf_op | source)
XLA Modules:
  0.0 48.4 jit_solution(8648186029578752593)
XLA Ops:
  0.6 0.0 copy-start
  0.6 0.5 %collective-permute-start = (bf16[256,4096]{1,0:T(8,128)(2,1)}, bf16[256,4096]{1,0:T(8,128)(2,1)S(1)}, u32[]{:S(2)}, u32[]{:S(2)}) collective-permute-start(bf16[256,4096]{1,0:T(8,128)(2,1)} %own_ref.7), channel_id=1, source_target_pairs={{0,8},{1,9},{2,10},{3,11},{4,12},{5,13},{6,14},{7,15},{8,0},{9,1},... | collective-permute-start | bytes 6291464 | tf_op jit(solution)/shard_map/ppermute | solution.py:148
  1.9 4.1 %front.1.v0_ref = bf16[272,512]{1,0:T(8,128)(2,1)S(1)} custom-call(f32[16]{0:T(128)} %loss_hbm.1, s32[1]{0:T(128)S(6)} %copy.12.exponent_hbm, s32[1,2]{1,0:T(1,128)} %start_hbm.1, s32[1,2]{1,0:T(1,128)} %rows_hbm.1, bf16[256,2048]{1,0:T(8,128)(2,1)} %q_hbm.1, bf16[256,512]{1,0:T(8,128)(2,1)} %k_hbm.1, bf16[256,2048]{1,0:T(8,128)(2,1)} %g_hbm.1, ...), custom_call_target="tpu_custom_call" | custom-call | tf_op jit(solution)/shard_map/front/pallas_call | solution.py:125
  6.0 0.1 collective-permute-start.1
  6.1 1.5 %collective-permute-done.1.v1_ref = bf16[272,512]{1,0:T(8,128)(2,1)S(1)} collective-permute-done((bf16[272,512]{1,0:T(8,128)(2,1)S(1)}, bf16[272,512]{1,0:T(8,128)(2,1)S(1)}, u32[]{:S(2)}, u32[]{:S(2)}) %collective-permute-start.1) | collective-permute-done | bytes 278560 | tf_op jit(solution)/shard_map/ppermute | solution.py:148
  7.6 0.0 collective-permute-done.near_ref
  7.6 0.0 copy-done
  7.6 0.5 %partial_sums.7 = (bf16[256,512]{1,0:T(8,128)(2,1)S(1)}, bf16[256,512]{1,0:T(8,128)(2,1)S(1)}) custom-call(bf16[256,4096]{1,0:T(8,128)(2,1)S(1)} %copy-done, bf16[256,4096]{1,0:T(8,128)(2,1)S(1)} %collective-permute-done.near_ref, bf16[272,512]{1,0:T(8,128)(2,1)S(1)} %front.1.v0_ref, bf16[272,512]{1,0:T(8,128)(2,1)S(1)} %collective-permute-done.1.v1_ref), custom_call_target="tpu_custom_call" | custom-call | tf_op jit(solution)/shard_map/partial_sums/pallas_call | solution.py:168
  8.1 2.6 %collective-permute-start.3 = (bf16[256,512]{1,0:T(8,128)(2,1)S(1)}, bf16[256,512]{1,0:T(8,128)(2,1)S(1)}, u32[]{:S(2)}, u32[]{:S(2)}) collective-permute-start(bf16[256,512]{1,0:T(8,128)(2,1)S(1)} %get-tuple-element.15), channel_id=1, source_target_pairs={{0,1},{1,0},{2,3},{3,2},{4,5},{5,4},{6,7},{7,6},{8,9},{9,8},{10,11... | collective-permute-start | bytes 786440 | tf_op jit(solution)/shard_map/ppermute | solution.py:148
  10.7 0.3 inner_swap.1
  11.1 1.6 %collective-permute-start.7 = (bf16[288,512]{1,0:T(8,128)(2,1)S(1)}, bf16[288,512]{1,0:T(8,128)(2,1)S(1)}, u32[]{:S(2)}, u32[]{:S(2)}) collective-permute-start(bf16[288,512]{1,0:T(8,128)(2,1)S(1)} %pad_maximum_fusion), channel_id=1, source_target_pairs={{0,16},{1,17},{2,18},{3,19},{4,20},{5,21},{6,22},{7,23},{8,24},{9,... | collective-permute-start | bytes 884744 | tf_op jit(solution)/shard_map/ppermute | solution.py:148
  12.6 0.5 partial_sums.5
  13.1 1.6 %collective-permute-start.2 = (bf16[512,512]{1,0:T(8,128)(2,1)S(1)}, bf16[512,512]{1,0:T(8,128)(2,1)S(1)}, u32[]{:S(2)}, u32[]{:S(2)}) collective-permute-start(bf16[512,512]{1,0:T(8,128)(2,1)S(1)} %partial_sums.5), channel_id=1, source_target_pairs={{0,2},{1,3},{2,0},{3,1},{4,6},{5,7},{6,4},{7,5},{8,10},{9,11},{10,... | collective-permute-start | bytes 1572872 | tf_op jit(solution)/shard_map/ppermute | solution.py:148
  14.8 0.5 partial_sums.6
  15.3 0.5 partial_sums.4
  15.8 1.8 %collective-permute-done.3 = bf16[256,512]{1,0:T(8,128)(2,1)S(1)} collective-permute-done((bf16[256,512]{1,0:T(8,128)(2,1)S(1)}, bf16[256,512]{1,0:T(8,128)(2,1)S(1)}, u32[]{:S(2)}, u32[]{:S(2)}) %collective-permute-start.3) | collective-permute-done | bytes 262176 | tf_op jit(solution)/shard_map/ppermute | solution.py:148
  17.6 1.8 %collective-permute-start.4 = (bf16[128,512]{1,0:T(8,128)(2,1)S(1)}, bf16[128,512]{1,0:T(8,128)(2,1)S(1)}, u32[]{:S(2)}, u32[]{:S(2)}) collective-permute-start(bf16[128,512]{1,0:T(8,128)(2,1)S(1)} %add_convert_fusion.4), channel_id=1, source_target_pairs={{0,16},{1,17},{2,18},{3,19},{4,20},{5,21},{6,22},{7,23},{8,24},{9,... | collective-permute-start | bytes 393224 | tf_op jit(solution)/shard_map/ppermute | solution.py:148
  19.4 0.8 %collective-permute-done.7 = bf16[288,512]{1,0:T(8,128)(2,1)S(1)} collective-permute-done((bf16[288,512]{1,0:T(8,128)(2,1)S(1)}, bf16[288,512]{1,0:T(8,128)(2,1)S(1)}, u32[]{:S(2)}, u32[]{:S(2)}) %collective-permute-start.7) | collective-permute-done | bytes 294944 | tf_op jit(solution)/shard_map/ppermute | solution.py:148
  20.2 0.8 %collective-permute-start.8 = (bf16[128,512]{1,0:T(8,128)(2,1)S(1)}, bf16[128,512]{1,0:T(8,128)(2,1)S(1)}, u32[]{:S(2)}, u32[]{:S(2)}) collective-permute-start(bf16[128,512]{1,0:T(8,128)(2,1)S(1)} %add_convert_fusion.2), channel_id=1, source_target_pairs={{0,1},{1,0},{2,3},{3,2},{4,5},{5,4},{6,7},{7,6},{8,9},{9,8},{10,11... | collective-permute-start | bytes 393224 | tf_op jit(solution)/shard_map/ppermute | solution.py:148
  21.0 1.9 %collective-permute-done.4 = bf16[128,512]{1,0:T(8,128)(2,1)S(1)} collective-permute-done((bf16[128,512]{1,0:T(8,128)(2,1)S(1)}, bf16[128,512]{1,0:T(8,128)(2,1)S(1)}, u32[]{:S(2)}, u32[]{:S(2)}) %collective-permute-start.4) | collective-permute-done | bytes 131104 | tf_op jit(solution)/shard_map/ppermute | solution.py:148
  23.0 1.6 %collective-permute-start.9 = (bf16[128,512]{1,0:T(8,128)(2,1)S(1)}, bf16[128,512]{1,0:T(8,128)(2,1)S(1)}, u32[]{:S(2)}, u32[]{:S(2)}) collective-permute-start(bf16[128,512]{1,0:T(8,128)(2,1)S(1)} %add_convert_fusion.3), channel_id=1, source_target_pairs={{0,2},{1,3},{2,0},{3,1},{4,6},{5,7},{6,4},{7,5},{8,10},{9,11},{10,... | collective-permute-start | bytes 393224 | tf_op jit(solution)/shard_map/ppermute | solution.py:148
  24.6 3.4 %collective-permute-done.2 = bf16[512,512]{1,0:T(8,128)(2,1)S(1)} collective-permute-done((bf16[512,512]{1,0:T(8,128)(2,1)S(1)}, bf16[512,512]{1,0:T(8,128)(2,1)S(1)}, u32[]{:S(2)}, u32[]{:S(2)}) %collective-permute-start.2) | collective-permute-done | bytes 524320 | tf_op jit(solution)/shard_map/ppermute | solution.py:148
  28.0 0.2 fusion.2
  28.3 0.6 %collective-permute-start.6 = (bf16[256,256]{1,0:T(8,128)(2,1)S(1)}, bf16[256,256]{1,0:T(8,128)(2,1)S(1)}, u32[]{:S(2)}, u32[]{:S(2)}) collective-permute-start(bf16[256,256]{1,0:T(8,128)(2,1)S(1)} %pad_maximum_fusion.3), channel_id=1, source_target_pairs={{0,1},{1,0},{2,3},{3,2},{4,5},{5,4},{6,7},{7,6},{8,9},{9,8},{10,11... | collective-permute-start | bytes 393224 | tf_op jit(solution)/shard_map/ppermute | solution.py:148
  28.9 0.1 collective-permute-start.5
  28.9 0.0 collective-permute-done.8
  28.9 0.7 %collective-permute-done.9 = bf16[128,512]{1,0:T(8,128)(2,1)S(1)} collective-permute-done((bf16[128,512]{1,0:T(8,128)(2,1)S(1)}, bf16[128,512]{1,0:T(8,128)(2,1)S(1)}, u32[]{:S(2)}, u32[]{:S(2)}) %collective-permute-start.9) | collective-permute-done | bytes 131104 | tf_op jit(solution)/shard_map/ppermute | solution.py:148
  29.6 0.1 add_convert_fusion.1
  29.7 2.7 %collective-permute-start.10 = (bf16[128,512]{1,0:T(8,128)(2,1)S(1)}, bf16[128,512]{1,0:T(8,128)(2,1)S(1)}, u32[]{:S(2)}, u32[]{:S(2)}) collective-permute-start(bf16[128,512]{1,0:T(8,128)(2,1)S(1)} %add_convert_fusion.1), channel_id=1, source_target_pairs={{0,4},{1,5},{2,6},{3,7},{4,0},{5,1},{6,2},{7,3},{8,12},{9,13},{10,... | collective-permute-start | bytes 393224 | tf_op jit(solution)/shard_map/ppermute | solution.py:148
  32.4 0.9 %collective-permute-done.6 = bf16[256,256]{1,0:T(8,128)(2,1)S(1)} collective-permute-done((bf16[256,256]{1,0:T(8,128)(2,1)S(1)}, bf16[256,256]{1,0:T(8,128)(2,1)S(1)}, u32[]{:S(2)}, u32[]{:S(2)}) %collective-permute-start.6) | collective-permute-done | bytes 131104 | tf_op jit(solution)/shard_map/ppermute | solution.py:148
  33.3 0.5 %collective-permute-done.5 = bf16[256,256]{1,0:T(8,128)(2,1)S(1)} collective-permute-done((bf16[256,256]{1,0:T(8,128)(2,1)S(1)}, bf16[256,256]{1,0:T(8,128)(2,1)S(1)}, u32[]{:S(2)}, u32[]{:S(2)}) %collective-permute-start.5) | collective-permute-done | bytes 131104 | tf_op jit(solution)/shard_map/ppermute | solution.py:148
  33.8 0.1 fusion.1
  33.9 0.9 %outer_swap.1 = bf16[256,512]{1,0:T(8,128)(2,1)} custom-call(bf16[272,512]{1,0:T(8,128)(2,1)S(1)} %front.1.v0_ref, bf16[256,512]{1,0:T(8,128)(2,1)S(1)} %get-tuple-element.22.rows_ref, bf16[32,512]{1,0:T(8,128)(2,1)S(1)} %slice.98.window_ref), custom_call_target="tpu_custom_call" | custom-call | tf_op jit(solution)/shard_map/outer_swap/pallas_call | solution.py:232
  34.8 1.6 %collective-permute-start.11 = (bf16[128,256]{1,0:T(8,128)(2,1)S(1)}, bf16[128,256]{1,0:T(8,128)(2,1)S(1)}, u32[]{:S(2)}, u32[]{:S(2)}) collective-permute-start(bf16[128,256]{1,0:T(8,128)(2,1)S(1)} %get-tuple-element.28), channel_id=1, source_target_pairs={{0,1},{1,0},{2,3},{3,2},{4,5},{5,4},{6,7},{7,6},{8,9},{9,8},{10,11... | collective-permute-start | bytes 196616 | tf_op jit(solution)/shard_map/ppermute | solution.py:148
  36.4 0.5 %collective-permute-start.12 = (bf16[128,256]{1,0:T(8,128)(2,1)S(1)}, bf16[128,256]{1,0:T(8,128)(2,1)S(1)}, u32[]{:S(2)}, u32[]{:S(2)}) collective-permute-start(bf16[128,256]{1,0:T(8,128)(2,1)S(1)} %get-tuple-element.33), channel_id=1, source_target_pairs={{0,16},{1,17},{2,18},{3,19},{4,20},{5,21},{6,22},{7,23},{8,24},{9,... | collective-permute-start | bytes 196616 | tf_op jit(solution)/shard_map/ppermute | solution.py:148
  36.9 0.9 %collective-permute-done.10.arrived_ref = bf16[128,512]{1,0:T(8,128)(2,1)S(1)} collective-permute-done((bf16[128,512]{1,0:T(8,128)(2,1)S(1)}, bf16[128,512]{1,0:T(8,128)(2,1)S(1)}, u32[]{:S(2)}, u32[]{:S(2)}) %collective-permute-start.10) | collective-permute-done | bytes 131104 | tf_op jit(solution)/shard_map/ppermute | solution.py:148
  37.8 1.3 %collective-permute-done.11 = bf16[128,256]{1,0:T(8,128)(2,1)S(1)} collective-permute-done((bf16[128,256]{1,0:T(8,128)(2,1)S(1)}, bf16[128,256]{1,0:T(8,128)(2,1)S(1)}, u32[]{:S(2)}, u32[]{:S(2)}) %collective-permute-start.11) | collective-permute-done | bytes 65568 | tf_op jit(solution)/shard_map/ppermute | solution.py:148
  39.2 1.5 %collective-permute-done.12 = bf16[128,256]{1,0:T(8,128)(2,1)S(1)} collective-permute-done((bf16[128,256]{1,0:T(8,128)(2,1)S(1)}, bf16[128,256]{1,0:T(8,128)(2,1)S(1)}, u32[]{:S(2)}, u32[]{:S(2)}) %collective-permute-start.12) | collective-permute-done | bytes 65568 | tf_op jit(solution)/shard_map/ppermute | solution.py:148
  40.7 0.6 %collective-permute-start.13 = (bf16[128,512]{1,0:T(8,128)(2,1)S(1)}, bf16[128,512]{1,0:T(8,128)(2,1)S(1)}, u32[]{:S(2)}, u32[]{:S(2)}) collective-permute-start(bf16[128,512]{1,0:T(8,128)(2,1)S(1)} %add_convert_fusion.mine_ref), channel_id=1, source_target_pairs={{0,16},{1,17},{2,18},{3,19},{4,20},{5,21},{6,22},{7,23},{8,24},{9,... | collective-permute-start | bytes 393224 | tf_op jit(solution)/shard_map/ppermute | solution.py:148
  41.3 4.5 %collective-permute-done.13.y_ref = bf16[128,512]{1,0:T(8,128)(2,1)S(1)} collective-permute-done((bf16[128,512]{1,0:T(8,128)(2,1)S(1)}, bf16[128,512]{1,0:T(8,128)(2,1)S(1)}, u32[]{:S(2)}, u32[]{:S(2)}) %collective-permute-start.13) | collective-permute-done | bytes 131104 | tf_op jit(solution)/shard_map/ppermute | solution.py:148
  45.8 0.1 collective-permute-start.14
  45.8 1.5 %collective-permute-done.14.near_ref = bf16[2,128,512]{2,1,0:T(8,128)(2,1)S(1)} collective-permute-done((bf16[2,128,512]{2,1,0:T(8,128)(2,1)S(1)}, bf16[2,128,512]{2,1,0:T(8,128)(2,1)S(1)}, u32[]{:S(2)}, u32[]{:S(2)}) %collective-permute-start.14) | collective-permute-done | bytes 262176 | tf_op jit(solution)/shard_map/ppermute | solution.py:148
  47.4 1.0 %place.1 = f32[512,512]{1,0:T(8,128)} custom-call(bf16[128,512]{1,0:T(8,128)(2,1)S(1)} %add_convert_fusion.mine_ref, bf16[128,512]{1,0:T(8,128)(2,1)S(1)} %collective-permute-done.13.y_ref, bf16[2,128,512]{2,1,0:T(8,128)(2,1)S(1)} %collective-permute-done.14.near_ref), custom_call_target="tpu_custom_call" | custom-call | tf_op jit(solution)/shard_map/place/pallas_call | solution.py:250
  (12 shorter events, 0.3 us)
Async XLA Ops:
  0.6 7.0 %copy-start = (bf16[256,4096]{1,0:T(8,128)(2,1)S(1)}, bf16[256,4096]{1,0:T(8,128)(2,1)}, u32[]{:S(2)}) copy-start(bf16[256,4096]{1,0:T(8,128)(2,1)} %own_ref.7) | copy-start | bytes 6291460
  0.6 7.0 %collective-permute-start = (bf16[256,4096]{1,0:T(8,128)(2,1)}, bf16[256,4096]{1,0:T(8,128)(2,1)S(1)}, u32[]{:S(2)}, u32[]{:S(2)}) collective-permute-start(bf16[256,4096]{1,0:T(8,128)(2,1)} %own_ref.7), channel_id=1, source_target_pairs={{0,8},{1,9},{2,10},{3,11},{4,12},{5,13},{6,14},{7,15},{8,0},{9,1},... | collective-permute-start | bytes 6291464 | tf_op jit(solution)/shard_map/ppermute | solution.py:148
  6.0 1.6 %collective-permute-start.1 = (bf16[272,512]{1,0:T(8,128)(2,1)S(1)}, bf16[272,512]{1,0:T(8,128)(2,1)S(1)}, u32[]{:S(2)}, u32[]{:S(2)}) collective-permute-start(bf16[272,512]{1,0:T(8,128)(2,1)S(1)} %front.1.v0_ref), channel_id=1, source_target_pairs={{0,8},{1,9},{2,10},{3,11},{4,12},{5,13},{6,14},{7,15},{8,0},{9,1},... | collective-permute-start | bytes 835592 | tf_op jit(solution)/shard_map/ppermute | solution.py:148
  8.1 9.4 %collective-permute-start.3 = (bf16[256,512]{1,0:T(8,128)(2,1)S(1)}, bf16[256,512]{1,0:T(8,128)(2,1)S(1)}, u32[]{:S(2)}, u32[]{:S(2)}) collective-permute-start(bf16[256,512]{1,0:T(8,128)(2,1)S(1)} %get-tuple-element.15), channel_id=1, source_target_pairs={{0,1},{1,0},{2,3},{3,2},{4,5},{5,4},{6,7},{7,6},{8,9},{9,8},{10,11... | collective-permute-start | bytes 786440 | tf_op jit(solution)/shard_map/ppermute | solution.py:148
  11.1 9.1 %collective-permute-start.7 = (bf16[288,512]{1,0:T(8,128)(2,1)S(1)}, bf16[288,512]{1,0:T(8,128)(2,1)S(1)}, u32[]{:S(2)}, u32[]{:S(2)}) collective-permute-start(bf16[288,512]{1,0:T(8,128)(2,1)S(1)} %pad_maximum_fusion), channel_id=1, source_target_pairs={{0,16},{1,17},{2,18},{3,19},{4,20},{5,21},{6,22},{7,23},{8,24},{9,... | collective-permute-start | bytes 884744 | tf_op jit(solution)/shard_map/ppermute | solution.py:148
  13.1 14.9 %collective-permute-start.2 = (bf16[512,512]{1,0:T(8,128)(2,1)S(1)}, bf16[512,512]{1,0:T(8,128)(2,1)S(1)}, u32[]{:S(2)}, u32[]{:S(2)}) collective-permute-start(bf16[512,512]{1,0:T(8,128)(2,1)S(1)} %partial_sums.5), channel_id=1, source_target_pairs={{0,2},{1,3},{2,0},{3,1},{4,6},{5,7},{6,4},{7,5},{8,10},{9,11},{10,... | collective-permute-start | bytes 1572872 | tf_op jit(solution)/shard_map/ppermute | solution.py:148
  17.6 5.4 %collective-permute-start.4 = (bf16[128,512]{1,0:T(8,128)(2,1)S(1)}, bf16[128,512]{1,0:T(8,128)(2,1)S(1)}, u32[]{:S(2)}, u32[]{:S(2)}) collective-permute-start(bf16[128,512]{1,0:T(8,128)(2,1)S(1)} %add_convert_fusion.4), channel_id=1, source_target_pairs={{0,16},{1,17},{2,18},{3,19},{4,20},{5,21},{6,22},{7,23},{8,24},{9,... | collective-permute-start | bytes 393224 | tf_op jit(solution)/shard_map/ppermute | solution.py:148
  20.2 8.7 %collective-permute-start.8 = (bf16[128,512]{1,0:T(8,128)(2,1)S(1)}, bf16[128,512]{1,0:T(8,128)(2,1)S(1)}, u32[]{:S(2)}, u32[]{:S(2)}) collective-permute-start(bf16[128,512]{1,0:T(8,128)(2,1)S(1)} %add_convert_fusion.2), channel_id=1, source_target_pairs={{0,1},{1,0},{2,3},{3,2},{4,5},{5,4},{6,7},{7,6},{8,9},{9,8},{10,11... | collective-permute-start | bytes 393224 | tf_op jit(solution)/shard_map/ppermute | solution.py:148
  23.0 6.7 %collective-permute-start.9 = (bf16[128,512]{1,0:T(8,128)(2,1)S(1)}, bf16[128,512]{1,0:T(8,128)(2,1)S(1)}, u32[]{:S(2)}, u32[]{:S(2)}) collective-permute-start(bf16[128,512]{1,0:T(8,128)(2,1)S(1)} %add_convert_fusion.3), channel_id=1, source_target_pairs={{0,2},{1,3},{2,0},{3,1},{4,6},{5,7},{6,4},{7,5},{8,10},{9,11},{10,... | collective-permute-start | bytes 393224 | tf_op jit(solution)/shard_map/ppermute | solution.py:148
  28.3 5.0 %collective-permute-start.6 = (bf16[256,256]{1,0:T(8,128)(2,1)S(1)}, bf16[256,256]{1,0:T(8,128)(2,1)S(1)}, u32[]{:S(2)}, u32[]{:S(2)}) collective-permute-start(bf16[256,256]{1,0:T(8,128)(2,1)S(1)} %pad_maximum_fusion.3), channel_id=1, source_target_pairs={{0,1},{1,0},{2,3},{3,2},{4,5},{5,4},{6,7},{7,6},{8,9},{9,8},{10,11... | collective-permute-start | bytes 393224 | tf_op jit(solution)/shard_map/ppermute | solution.py:148
  28.9 5.0 %collective-permute-start.5 = (bf16[256,256]{1,0:T(8,128)(2,1)S(1)}, bf16[256,256]{1,0:T(8,128)(2,1)S(1)}, u32[]{:S(2)}, u32[]{:S(2)}) collective-permute-start(bf16[256,256]{1,0:T(8,128)(2,1)S(1)} %slice.95), channel_id=1, source_target_pairs={{0,16},{1,17},{2,18},{3,19},{4,20},{5,21},{6,22},{7,23},{8,24},{9,... | collective-permute-start | bytes 393224 | tf_op jit(solution)/shard_map/ppermute | solution.py:148
  29.7 8.1 %collective-permute-start.10 = (bf16[128,512]{1,0:T(8,128)(2,1)S(1)}, bf16[128,512]{1,0:T(8,128)(2,1)S(1)}, u32[]{:S(2)}, u32[]{:S(2)}) collective-permute-start(bf16[128,512]{1,0:T(8,128)(2,1)S(1)} %add_convert_fusion.1), channel_id=1, source_target_pairs={{0,4},{1,5},{2,6},{3,7},{4,0},{5,1},{6,2},{7,3},{8,12},{9,13},{10,... | collective-permute-start | bytes 393224 | tf_op jit(solution)/shard_map/ppermute | solution.py:148
  34.8 4.3 %collective-permute-start.11 = (bf16[128,256]{1,0:T(8,128)(2,1)S(1)}, bf16[128,256]{1,0:T(8,128)(2,1)S(1)}, u32[]{:S(2)}, u32[]{:S(2)}) collective-permute-start(bf16[128,256]{1,0:T(8,128)(2,1)S(1)} %get-tuple-element.28), channel_id=1, source_target_pairs={{0,1},{1,0},{2,3},{3,2},{4,5},{5,4},{6,7},{7,6},{8,9},{9,8},{10,11... | collective-permute-start | bytes 196616 | tf_op jit(solution)/shard_map/ppermute | solution.py:148
  36.4 4.3 %collective-permute-start.12 = (bf16[128,256]{1,0:T(8,128)(2,1)S(1)}, bf16[128,256]{1,0:T(8,128)(2,1)S(1)}, u32[]{:S(2)}, u32[]{:S(2)}) collective-permute-start(bf16[128,256]{1,0:T(8,128)(2,1)S(1)} %get-tuple-element.33), channel_id=1, source_target_pairs={{0,16},{1,17},{2,18},{3,19},{4,20},{5,21},{6,22},{7,23},{8,24},{9,... | collective-permute-start | bytes 196616 | tf_op jit(solution)/shard_map/ppermute | solution.py:148
  40.7 5.0 %collective-permute-start.13 = (bf16[128,512]{1,0:T(8,128)(2,1)S(1)}, bf16[128,512]{1,0:T(8,128)(2,1)S(1)}, u32[]{:S(2)}, u32[]{:S(2)}) collective-permute-start(bf16[128,512]{1,0:T(8,128)(2,1)S(1)} %add_convert_fusion.mine_ref), channel_id=1, source_target_pairs={{0,16},{1,17},{2,18},{3,19},{4,20},{5,21},{6,22},{7,23},{8,24},{9,... | collective-permute-start | bytes 393224 | tf_op jit(solution)/shard_map/ppermute | solution.py:148
  45.8 1.6 %collective-permute-start.14 = (bf16[2,128,512]{2,1,0:T(8,128)(2,1)S(1)}, bf16[2,128,512]{2,1,0:T(8,128)(2,1)S(1)}, u32[]{:S(2)}, u32[]{:S(2)}) collective-permute-start(bf16[2,128,512]{2,1,0:T(8,128)(2,1)S(1)} %pad_maximum_fusion.2), channel_id=1, source_target_pairs={{0,8},{1,9},{2,10},{3,11},{4,12},{5,13},{6,14},{7,15},{8,0},{9,1},... | collective-permute-start | bytes 786440 | tf_op jit(solution)/shard_map/ppermute | solution.py:148

commit v7 on v6

--- a/solution.py
+++ b/solution.py
@@ -1,4 +1,5 @@
 import functools
+import math
 
 import jax
 import jax.numpy as jnp
@@ -11,6 +12,7 @@
 HD = 128
 CAP = 32
 HALF = 128
+SEG = 16
 LANE = 128
 INFO = 16
 MIB = 1 << 20
@@ -22,24 +24,57 @@
 HBM = pl.BlockSpec(memory_space=pltpu.HBM)
 
 
-def attend_group(per_group, span, q, k, g, allowed, factor):
-    q_all = jnp.concatenate([q[span, n * HD:(n + 1) * HD] for n in range(per_group)], axis=0)
-    scores = lax.dot_general(
-        k[span, :], q_all, (((1,), (1,)), ((), ())), preferred_element_type=F32
-    ) * HD ** (-0.5)
+def attend_half(per_group, folded, span, q_ref, k_ref, g_ref, allowed, factor):
+    heads = q_ref.shape[1] // HD
+    groups = heads // per_group
+    scores = [
+        lax.dot_general(
+            k_ref[span, pl.ds(group * HD, HD)],
+            jnp.concatenate(
+                [q_ref[span, pl.ds((group * per_group + n) * HD, HD)] for n in range(per_group)], axis=0
+            ),
+            (((1,), (1,)), ((), ())),
+            preferred_element_type=F32,
+        )
+        for group in range(groups)
+    ]
+    weighted = [
+        (g_ref[span, pl.ds(head * HD, HD)].astype(F32) * factor).astype(BF16) for head in range(heads)
+    ]
+    if folded:
+        block = lax.broadcasted_iota(jnp.int32, (SEG, HALF), 1) // SEG
     probs = []
-    weighted = []
-    for n in range(per_group):
-        own = jnp.where(allowed, scores[:, n * HALF:(n + 1) * HALF], -1e30)
-        expo = jnp.exp(own - jnp.max(own, axis=0, keepdims=True))
-        probs.append((expo / jnp.sum(expo, axis=0, keepdims=True)).astype(BF16))
-        weighted.append((g[span, n * HD:(n + 1) * HD].astype(F32) * factor).astype(BF16))
-    return jnp.dot(
-        jnp.concatenate(probs, axis=1), jnp.concatenate(weighted, axis=0), preferred_element_type=F32
-    ).astype(BF16)
-
-
-def mask_and_factor(span, loss_ref, exponent_ref, ids_ref, index_ref):
+    for head in range(heads):
+        n = head % per_group
+        own = scores[head // per_group][:, n * HALF:(n + 1) * HALF]
+        if folded:
+            own = fold_blocks(own, block)
+        own = jnp.where(allowed, own, -1e30)
+        expo = jnp.exp2((own - jnp.max(own, axis=0, keepdims=True)) * (HD ** (-0.5) * math.log2(math.e)))
+        prob = (expo * (1.0 / jnp.sum(expo, axis=0, keepdims=True))).astype(BF16)
+        if folded:
+            prob = jnp.concatenate(
+                [jnp.where(block == b, prob, jnp.zeros_like(prob)) for b in range(HALF // SEG)], axis=0
+            )
+        probs.append(prob)
+    return [
+        jnp.dot(
+            jnp.concatenate(probs[head:head + per_group], axis=1),
+            jnp.concatenate(weighted[head:head + per_group], axis=0),
+            preferred_element_type=F32,
+        ).astype(BF16)
+        for head in range(0, heads, per_group)
+    ]
+
+
+def fold_blocks(square, block):
+    total = square[:SEG]
+    for b in range(1, HALF // SEG):
+        total = jnp.where(block == b, square[b * SEG:(b + 1) * SEG], total)
+    return total
+
+
+def mask_and_factor(folded, span, loss_ref, exponent_ref, ids_ref, index_ref):
     exponent = exponent_ref[0]
     unscale = jnp.float32(1.0)
     for bit in range(5):
@@ -48,6 +83,10 @@
     col = lax.broadcasted_iota(jnp.int32, (HALF, HALF), 1)
     doc_i = jnp.broadcast_to(ids_ref[:, span], (HALF, HALF))
     allowed = (doc_i == doc_i.T) & (row <= col)
+    if folded:
+        allowed = fold_blocks(
+            jnp.where(allowed, 1, 0), lax.broadcasted_iota(jnp.int32, (SEG, HALF), 1) // SEG
+        ) == 1
     index = index_ref[:, span]
     factor = jnp.zeros((1, HALF), F32)
     for entry in range(loss_ref.shape[0]):
@@ -78,47 +117,36 @@
     groups = k_ref.shape[1] // HD
     wide = per_group * HD
     loads = []
-    for group in range(groups):
-        some = pl.ds(group * wide, wide)
-        one = pl.ds(group * HD, HD)
+    for half in range(2):
+        span = pl.ds(half * HALF, HALF)
         loads.append([
-            begin(q_hbm.at[:, some], q_ref.at[:, some]),
-            begin(k_hbm.at[:, one], k_ref.at[:, one]),
-            begin(g_hbm.at[:, some], g_ref.at[:, some]),
+            begin(source.at[span, :], target.at[span, :])
+            for source, target in ((q_hbm, q_ref), (k_hbm, k_ref), (g_hbm, g_ref))
         ])
     for copy in small:
         copy.wait()
     masks = [
-        mask_and_factor(pl.ds(half * HALF, HALF), loss_ref, exponent_ref, ids_ref, index_ref) for half in range(2)
-    ]
-
-    def put(group, row, value):
-        v_ref[pl.ds(row, value.shape[0]), pl.ds(group * HD, HD)] = value
-
-    info_row = lax.broadcasted_iota(jnp.int32, (INFO, HD), 0)
-    info = jnp.zeros((INFO, HD), jnp.int32)
+        mask_and_factor(half == 1, pl.ds(half * HALF, HALF), loss_ref, exponent_ref, ids_ref, index_ref)
+        for half in range(2)
+    ]
+    info_row = lax.broadcasted_iota(jnp.int32, (INFO, k_ref.shape[1]), 0)
+    info = jnp.zeros(info_row.shape, jnp.int32)
     for level in range(min(start_ref.shape[1], INFO // 2)):
         info = jnp.where(info_row == 2 * level, start_ref[0, level], info)
         info = jnp.where(info_row == 2 * level + 1, rows_ref[0, level], info)
-    info = info.astype(F32).astype(BF16)
-    for group in range(groups):
-        for copy in loads[group]:
+    v_ref[pl.ds(2 * HALF, INFO), :] = info.astype(F32).astype(BF16)
+    for half in range(2):
+        for copy in loads[half]:
             copy.wait()
-        some = pl.ds(group * wide, wide)
-        for half in range(2):
-            span = pl.ds(half * HALF, HALF)
-            value = attend_group(
-                per_group, slice(None), q_ref[span, some], k_ref[span, pl.ds(group * HD, HD)], g_ref[span, some],
-                *masks[half],
-            )
-            put(group, half * HALF, value)
-        put(group, 2 * HALF, info)
+        span = pl.ds(half * HALF, HALF)
+        values = attend_half(per_group, half == 1, span, q_ref, k_ref, g_ref, *masks[half])
+        for group, value in enumerate(values):
+            v_ref[span, pl.ds(group * HD, HD)] = value
 
 
 def front(query, key, grad, ids, index, loss, exponent, start, rows):
     tokens, key_width = key.shape
     per_group = query.shape[1] // key_width
-    groups = key_width // HD
     args = [
         loss, exponent, start, rows, query, key, grad, ids.reshape(1, tokens), index.reshape(1, tokens)
     ]
@@ -132,7 +160,7 @@
             pltpu.SMEM(start.shape, jnp.int32), pltpu.SMEM(rows.shape, jnp.int32),
             pltpu.VMEM(query.shape, BF16), pltpu.VMEM(key.shape, BF16), pltpu.VMEM(grad.shape, BF16),
             pltpu.VMEM((1, tokens), jnp.int32), pltpu.VMEM((1, tokens), jnp.int32),
-            pltpu.SemaphoreType.DMA((6 + 3 * groups,)),
+            pltpu.SemaphoreType.DMA((12,)),
         ],
         compiler_params=pltpu.CompilerParams(vmem_limit_bytes=24 * MIB),
         cost_estimate=FREE,
@@ -292,34 +320,35 @@
         return total
 
     first_b, first_a = sums((((3, 1, 1), (3, 0, 1)), ((2, 1, 1), (2, 1, 0))), BF16)
-    rows, window = inner_swap(v0, v1)
     pair, = sums((((1, 1, 1), (1, 1, 0), (1, 0, 1), (1, 0, 0)),), BF16)
     keep_b, keep_a = sums((((3, 1, 0), (3, 0, 0)), ((2, 0, 1), (2, 0, 0))), F32)
     own, = sums((((0, 1, 1), (0, 1, 0), (0, 0, 1), (0, 0, 0)),), F32)
     first_b = xor_permute(first_b, X)
-    first_a = xor_permute(jnp.concatenate([first_a, window]), Y)
+    first_a = xor_permute(first_a, Y)
     pair = xor_permute(pair, Z1)
-    on_b = xor_permute(add(keep_b[:LANE], first_b[:LANE]).astype(BF16), Y)
+    on_b = add(keep_b[:LANE], first_b[:LANE]).astype(BF16)
+    rows, window = inner_swap(after_all(v0, own)[0], v1)
+    window = xor_permute(after_all(window, on_b)[0], Y)
+    on_b = xor_permute(on_b, Y)
     on_a = xor_permute(add(keep_a[:LANE], first_a[:LANE]).astype(BF16), X)
     z3 = add(keep_b[LANE:], first_b[LANE:], on_b).astype(BF16)
-    pair = after_all(pair, z3)[0]
+    pair, window = after_all(pair, window, z3)[:2]
     z3 = xor_permute(z3, Z1)
-    z2 = add(keep_a[LANE:], first_a[LANE:2 * LANE], on_a, z3).astype(BF16)
+    z2 = add(keep_a[LANE:], first_a[LANE:], on_a, z3).astype(BF16)
 
     total = add(own, pair)
     some, rest = total[:, :256], total[:, 256:]
     rest_far, rest_y, rest_x, rest_own = (rest[row:row + LANE] for row in range(0, 4 * LANE, LANE))
     some_in = xor_permute(some[:2 * LANE].astype(BF16), Y)
     rest_in = xor_permute(jnp.concatenate([rest_far, rest_x]).astype(BF16), X)
-    some_in, rest_in, window = after_all(some_in, rest_in, first_a[2 * LANE:], z2)[:3]
+    some_in, rest_in = after_all(some_in, rest_in, z2)[:2]
     z2 = xor_permute(z2, Z2)
     some_on = xor_permute(add(some[2 * LANE:3 * LANE], some_in[:LANE]).astype(BF16), X)
     rest_on = xor_permute(add(rest_y, rest_in[:LANE]).astype(BF16), Y)
-    value_grad = outer_swap(v0, rows, window)
     base = jnp.concatenate([add(some[3 * LANE:], some_in[LANE:]), add(rest_own, rest_in[LANE:])], axis=1)
-    base, value_grad = after_all(base, value_grad)
     mine = add(fold(base, z2), jnp.concatenate([some_on, rest_on], axis=1)).astype(BF16)
     from_y = xor_permute(mine, Y)
+    value_grad = outer_swap(v0, rows, after_all(window, from_y)[0])
     return place(mine, from_y, xor_permute(jnp.stack([mine, from_y]), CORE)), value_grad
 
 

time: 48.6 us -> 46.8 us (0.963)
  Pallas kernels: 8.3 us -> 6.89 us
  waiting for transfers between devices: 21.2 us -> 19.8 us
  starting transfers between devices: 16.8 us -> 17.9 us
    ppermute x15 -> x16, waiting for transfers between devices: 21.2 us -> 19.8 us  [xor_permute(): lax.ppermute(value, ('dp', 'fsdp'), [(i, i ^ mask) for i in range(count)])]
    pallas_call x1, Pallas kernels: 4.05 us -> 2.64 us  [front(): pl.pallas_call(functools.partial(front_kernel, per_group), in_specs=[HBM]...]
    ppermute x15 -> x16, starting transfers between devices: 16.8 us -> 17.9 us  [xor_permute(): lax.ppermute(value, ('dp', 'fsdp'), [(i, i ^ mask) for i in range(count)])]
  transfers between devices with their start and end apart: 15 -> 16, of which waited for: 13 -> 13; matrix products, arithmetic and copies ran while one was open for 1% -> 1% of each run, Pallas kernels for 14% -> 11%
where the time goes in v7:
time: 46.8 us; the launch traced here: 46.6 us
  waiting for transfers between devices  19.8 us (42%)
  starting transfers between devices  17.9 us (38%)
  Pallas kernels  6.89 us (15%)
  between operations  1.53 us (3%)
  other arithmetic  0.48 us (1%)
    ppermute x16, waiting for transfers between devices, xor_permute(): lax.ppermute(value, ('dp', 'fsdp'), [(i, i ^ mask) for i in range(count)])  19.8 us
    ppermute x16, starting transfers between devices, xor_permute(): lax.ppermute(value, ('dp', 'fsdp'), [(i, i ^ mask) for i in range(count)])  17.9 us
    pallas_call x1, Pallas kernels, front(): pl.pallas_call(functools.partial(front_kernel, per_group), in_specs=[HBM]...  2.64 us
    pallas_call x4, Pallas kernels, partial_sums(): pl.pallas_call(functools.partial(partial_kernel, parts), in_specs=[VMEM]...  1.94 us
    pallas_call x1, Pallas kernels, place(): pl.pallas_call(place_kernel, in_specs=[VMEM] * 3, out_specs=VMEM, out_sha...  1.05 us
  transfers between devices with their start and end apart: 16, of which 13 were waited for; matrix products, arithmetic and copies ran while one was open for 1% of the time, Pallas kernels for 11%

profile of v7, /device:TPU:0, one launch (start us, length us, event | category | flops | bytes accessed | tf_op | source)
XLA Modules:
  0.0 46.6 jit_solution(11992257369953977887)
XLA Ops:
  0.6 0.0 copy-start
  0.6 0.5 %collective-permute-start = (bf16[256,4096]{1,0:T(8,128)(2,1)}, bf16[256,4096]{1,0:T(8,128)(2,1)S(1)}, u32[]{:S(2)}, u32[]{:S(2)}) collective-permute-start(bf16[256,4096]{1,0:T(8,128)(2,1)} %own_ref.7), channel_id=1, source_target_pairs={{0,8},{1,9},{2,10},{3,11},{4,12},{5,13},{6,14},{7,15},{8,0},{9,1},... | collective-permute-start | bytes 6291464 | tf_op jit(solution)/shard_map/ppermute | solution.py:176
  1.9 2.6 %front.1.v0_ref = bf16[272,512]{1,0:T(8,128)(2,1)S(1)} custom-call(f32[16]{0:T(128)} %loss_hbm.1, s32[1]{0:T(128)S(6)} %copy.12.exponent_hbm, s32[1,2]{1,0:T(1,128)} %start_hbm.1, s32[1,2]{1,0:T(1,128)} %rows_hbm.1, bf16[256,2048]{1,0:T(8,128)(2,1)} %q_hbm.1, bf16[256,512]{1,0:T(8,128)(2,1)} %k_hbm.1, bf16[256,2048]{1,0:T(8,128)(2,1)} %g_hbm.1, ...), custom_call_target="tpu_custom_call" | custom-call | tf_op jit(solution)/shard_map/front/pallas_call | solution.py:153
  4.6 0.1 collective-permute-start.1
  4.7 1.5 %collective-permute-done.1.v1_ref = bf16[272,512]{1,0:T(8,128)(2,1)S(1)} collective-permute-done((bf16[272,512]{1,0:T(8,128)(2,1)S(1)}, bf16[272,512]{1,0:T(8,128)(2,1)S(1)}, u32[]{:S(2)}, u32[]{:S(2)}) %collective-permute-start.1) | collective-permute-done | bytes 278560 | tf_op jit(solution)/shard_map/ppermute | solution.py:176
  6.2 0.0 collective-permute-done.near_ref
  6.2 0.0 copy-done
  6.2 0.5 %partial_sums.7 = (bf16[256,512]{1,0:T(8,128)(2,1)S(1)}, bf16[256,512]{1,0:T(8,128)(2,1)S(1)}) custom-call(bf16[256,4096]{1,0:T(8,128)(2,1)S(1)} %copy-done, bf16[256,4096]{1,0:T(8,128)(2,1)S(1)} %collective-permute-done.near_ref, bf16[272,512]{1,0:T(8,128)(2,1)S(1)} %front.1.v0_ref, bf16[272,512]{1,0:T(8,128)(2,1)S(1)} %collective-permute-done.1.v1_ref), custom_call_target="tpu_custom_call" | custom-call | tf_op jit(solution)/shard_map/partial_sums/pallas_call | solution.py:196
  6.7 2.6 %collective-permute-start.3 = (bf16[256,512]{1,0:T(8,128)(2,1)S(1)}, bf16[256,512]{1,0:T(8,128)(2,1)S(1)}, u32[]{:S(2)}, u32[]{:S(2)}) collective-permute-start(bf16[256,512]{1,0:T(8,128)(2,1)S(1)} %get-tuple-element.18), channel_id=1, source_target_pairs={{0,1},{1,0},{2,3},{3,2},{4,5},{5,4},{6,7},{7,6},{8,9},{9,8},{10,11... | collective-permute-start | bytes 786440 | tf_op jit(solution)/shard_map/ppermute | solution.py:176
  9.3 1.5 %collective-permute-start.8 = (bf16[256,512]{1,0:T(8,128)(2,1)S(1)}, bf16[256,512]{1,0:T(8,128)(2,1)S(1)}, u32[]{:S(2)}, u32[]{:S(2)}) collective-permute-start(bf16[256,512]{1,0:T(8,128)(2,1)S(1)} %get-tuple-element.22), channel_id=1, source_target_pairs={{0,16},{1,17},{2,18},{3,19},{4,20},{5,21},{6,22},{7,23},{8,24},{9,... | collective-permute-start | bytes 786440 | tf_op jit(solution)/shard_map/ppermute | solution.py:176
  10.8 0.5 %partial_sums.4 = f32[512,512]{1,0:T(8,128)S(1)} custom-call(bf16[256,4096]{1,0:T(8,128)(2,1)S(1)} %copy-done, bf16[256,4096]{1,0:T(8,128)(2,1)S(1)} %collective-permute-done.near_ref, bf16[272,512]{1,0:T(8,128)(2,1)S(1)} %front.1.v0_ref, bf16[272,512]{1,0:T(8,128)(2,1)S(1)} %collective-permute-done.1.v1_ref), custom_call_target="tpu_custom_call" | custom-call | tf_op jit(solution)/shard_map/partial_sums/pallas_call | solution.py:196
  11.3 0.5 %partial_sums.5 = bf16[512,512]{1,0:T(8,128)(2,1)S(1)} custom-call(bf16[256,4096]{1,0:T(8,128)(2,1)S(1)} %copy-done, bf16[256,4096]{1,0:T(8,128)(2,1)S(1)} %collective-permute-done.near_ref, bf16[272,512]{1,0:T(8,128)(2,1)S(1)} %front.1.v0_ref, bf16[272,512]{1,0:T(8,128)(2,1)S(1)} %collective-permute-done.1.v1_ref), custom_call_target="tpu_custom_call" | custom-call | tf_op jit(solution)/shard_map/partial_sums/pallas_call | solution.py:196
  11.8 1.6 %collective-permute-start.2 = (bf16[512,512]{1,0:T(8,128)(2,1)S(1)}, bf16[512,512]{1,0:T(8,128)(2,1)S(1)}, u32[]{:S(2)}, u32[]{:S(2)}) collective-permute-start(bf16[512,512]{1,0:T(8,128)(2,1)S(1)} %partial_sums.5), channel_id=1, source_target_pairs={{0,2},{1,3},{2,0},{3,1},{4,6},{5,7},{6,4},{7,5},{8,10},{9,11},{10,... | collective-permute-start | bytes 1572872 | tf_op jit(solution)/shard_map/ppermute | solution.py:176
  13.4 0.5 %partial_sums.6 = (f32[256,512]{1,0:T(8,128)S(1)}, f32[256,512]{1,0:T(8,128)S(1)}) custom-call(bf16[256,4096]{1,0:T(8,128)(2,1)S(1)} %copy-done, bf16[256,4096]{1,0:T(8,128)(2,1)S(1)} %collective-permute-done.near_ref, bf16[272,512]{1,0:T(8,128)(2,1)S(1)} %front.1.v0_ref, bf16[272,512]{1,0:T(8,128)(2,1)S(1)} %collective-permute-done.1.v1_ref), custom_call_target="tpu_custom_call" | custom-call | tf_op jit(solution)/shard_map/partial_sums/pallas_call | solution.py:196
  13.9 0.3 inner_swap.1
  14.2 1.9 %collective-permute-done.3 = bf16[256,512]{1,0:T(8,128)(2,1)S(1)} collective-permute-done((bf16[256,512]{1,0:T(8,128)(2,1)S(1)}, bf16[256,512]{1,0:T(8,128)(2,1)S(1)}, u32[]{:S(2)}, u32[]{:S(2)}) %collective-permute-start.3) | collective-permute-done | bytes 262176 | tf_op jit(solution)/shard_map/ppermute | solution.py:176
  16.1 1.8 %collective-permute-start.5 = (bf16[128,512]{1,0:T(8,128)(2,1)S(1)}, bf16[128,512]{1,0:T(8,128)(2,1)S(1)}, u32[]{:S(2)}, u32[]{:S(2)}) collective-permute-start(bf16[128,512]{1,0:T(8,128)(2,1)S(1)} %add_convert_fusion.4), channel_id=1, source_target_pairs={{0,16},{1,17},{2,18},{3,19},{4,20},{5,21},{6,22},{7,23},{8,24},{9,... | collective-permute-start | bytes 393224 | tf_op jit(solution)/shard_map/ppermute | solution.py:176
  18.0 0.0 collective-permute-done.8
  18.0 1.6 %collective-permute-start.9 = (bf16[128,512]{1,0:T(8,128)(2,1)S(1)}, bf16[128,512]{1,0:T(8,128)(2,1)S(1)}, u32[]{:S(2)}, u32[]{:S(2)}) collective-permute-start(bf16[128,512]{1,0:T(8,128)(2,1)S(1)} %add_convert_fusion.2), channel_id=1, source_target_pairs={{0,1},{1,0},{2,3},{3,2},{4,5},{5,4},{6,7},{7,6},{8,9},{9,8},{10,11... | collective-permute-start | bytes 393224 | tf_op jit(solution)/shard_map/ppermute | solution.py:176
  19.6 0.5 %collective-permute-start.4 = (bf16[32,512]{1,0:T(8,128)(2,1)S(1)}, bf16[32,512]{1,0:T(8,128)(2,1)S(1)}, u32[]{:S(2)}, u32[]{:S(2)}) collective-permute-start(bf16[32,512]{1,0:T(8,128)(2,1)S(1)} %get-tuple-element.19), channel_id=1, source_target_pairs={{0,16},{1,17},{2,18},{3,19},{4,20},{5,21},{6,22},{7,23},{8,24},{9,... | collective-permute-start | bytes 98312 | tf_op jit(solution)/shard_map/ppermute | solution.py:176
  20.1 1.5 %collective-permute-done.5 = bf16[128,512]{1,0:T(8,128)(2,1)S(1)} collective-permute-done((bf16[128,512]{1,0:T(8,128)(2,1)S(1)}, bf16[128,512]{1,0:T(8,128)(2,1)S(1)}, u32[]{:S(2)}, u32[]{:S(2)}) %collective-permute-start.5) | collective-permute-done | bytes 131104 | tf_op jit(solution)/shard_map/ppermute | solution.py:176
  21.6 1.7 %collective-permute-start.10 = (bf16[128,512]{1,0:T(8,128)(2,1)S(1)}, bf16[128,512]{1,0:T(8,128)(2,1)S(1)}, u32[]{:S(2)}, u32[]{:S(2)}) collective-permute-start(bf16[128,512]{1,0:T(8,128)(2,1)S(1)} %add_convert_fusion.3), channel_id=1, source_target_pairs={{0,2},{1,3},{2,0},{3,1},{4,6},{5,7},{6,4},{7,5},{8,10},{9,11},{10,... | collective-permute-start | bytes 393224 | tf_op jit(solution)/shard_map/ppermute | solution.py:176
  23.4 0.1 collective-permute-done.4.window_ref
  23.5 3.2 %collective-permute-done.2 = bf16[512,512]{1,0:T(8,128)(2,1)S(1)} collective-permute-done((bf16[512,512]{1,0:T(8,128)(2,1)S(1)}, bf16[512,512]{1,0:T(8,128)(2,1)S(1)}, u32[]{:S(2)}, u32[]{:S(2)}) %collective-permute-start.2) | collective-permute-done | bytes 524320 | tf_op jit(solution)/shard_map/ppermute | solution.py:176
  26.7 0.2 fusion.2
  26.9 0.6 %collective-permute-start.7 = (bf16[256,256]{1,0:T(8,128)(2,1)S(1)}, bf16[256,256]{1,0:T(8,128)(2,1)S(1)}, u32[]{:S(2)}, u32[]{:S(2)}) collective-permute-start(bf16[256,256]{1,0:T(8,128)(2,1)S(1)} %pad_maximum_fusion.2), channel_id=1, source_target_pairs={{0,1},{1,0},{2,3},{3,2},{4,5},{5,4},{6,7},{7,6},{8,9},{9,8},{10,11... | collective-permute-start | bytes 393224 | tf_op jit(solution)/shard_map/ppermute | solution.py:176
  27.5 0.1 collective-permute-start.6
  27.6 0.0 collective-permute-done.9
  27.6 0.7 %collective-permute-done.10 = bf16[128,512]{1,0:T(8,128)(2,1)S(1)} collective-permute-done((bf16[128,512]{1,0:T(8,128)(2,1)S(1)}, bf16[128,512]{1,0:T(8,128)(2,1)S(1)}, u32[]{:S(2)}, u32[]{:S(2)}) %collective-permute-start.10) | collective-permute-done | bytes 131104 | tf_op jit(solution)/shard_map/ppermute | solution.py:176
  28.3 0.1 add_convert_fusion.1
  28.4 2.7 %collective-permute-start.11 = (bf16[128,512]{1,0:T(8,128)(2,1)S(1)}, bf16[128,512]{1,0:T(8,128)(2,1)S(1)}, u32[]{:S(2)}, u32[]{:S(2)}) collective-permute-start(bf16[128,512]{1,0:T(8,128)(2,1)S(1)} %add_convert_fusion.1), channel_id=1, source_target_pairs={{0,4},{1,5},{2,6},{3,7},{4,0},{5,1},{6,2},{7,3},{8,12},{9,13},{10,... | collective-permute-start | bytes 393224 | tf_op jit(solution)/shard_map/ppermute | solution.py:176
  31.0 0.9 %collective-permute-done.7 = bf16[256,256]{1,0:T(8,128)(2,1)S(1)} collective-permute-done((bf16[256,256]{1,0:T(8,128)(2,1)S(1)}, bf16[256,256]{1,0:T(8,128)(2,1)S(1)}, u32[]{:S(2)}, u32[]{:S(2)}) %collective-permute-start.7) | collective-permute-done | bytes 131104 | tf_op jit(solution)/shard_map/ppermute | solution.py:176
  32.0 0.5 %collective-permute-done.6 = bf16[256,256]{1,0:T(8,128)(2,1)S(1)} collective-permute-done((bf16[256,256]{1,0:T(8,128)(2,1)S(1)}, bf16[256,256]{1,0:T(8,128)(2,1)S(1)}, u32[]{:S(2)}, u32[]{:S(2)}) %collective-permute-start.6) | collective-permute-done | bytes 131104 | tf_op jit(solution)/shard_map/ppermute | solution.py:176
  32.5 0.1 fusion.1
  32.5 1.6 %collective-permute-start.12 = (bf16[128,256]{1,0:T(8,128)(2,1)S(1)}, bf16[128,256]{1,0:T(8,128)(2,1)S(1)}, u32[]{:S(2)}, u32[]{:S(2)}) collective-permute-start(bf16[128,256]{1,0:T(8,128)(2,1)S(1)} %get-tuple-element.30), channel_id=1, source_target_pairs={{0,1},{1,0},{2,3},{3,2},{4,5},{5,4},{6,7},{7,6},{8,9},{9,8},{10,11... | collective-permute-start | bytes 196616 | tf_op jit(solution)/shard_map/ppermute | solution.py:176
  34.1 0.5 %collective-permute-start.13 = (bf16[128,256]{1,0:T(8,128)(2,1)S(1)}, bf16[128,256]{1,0:T(8,128)(2,1)S(1)}, u32[]{:S(2)}, u32[]{:S(2)}) collective-permute-start(bf16[128,256]{1,0:T(8,128)(2,1)S(1)} %get-tuple-element.35), channel_id=1, source_target_pairs={{0,16},{1,17},{2,18},{3,19},{4,20},{5,21},{6,22},{7,23},{8,24},{9,... | collective-permute-start | bytes 196616 | tf_op jit(solution)/shard_map/ppermute | solution.py:176
  34.7 1.8 %collective-permute-done.11.arrived_ref = bf16[128,512]{1,0:T(8,128)(2,1)S(1)} collective-permute-done((bf16[128,512]{1,0:T(8,128)(2,1)S(1)}, bf16[128,512]{1,0:T(8,128)(2,1)S(1)}, u32[]{:S(2)}, u32[]{:S(2)}) %collective-permute-start.11) | collective-permute-done | bytes 131104 | tf_op jit(solution)/shard_map/ppermute | solution.py:176
  36.5 0.4 collective-permute-done.12
  36.9 2.0 %collective-permute-done.13 = bf16[128,256]{1,0:T(8,128)(2,1)S(1)} collective-permute-done((bf16[128,256]{1,0:T(8,128)(2,1)S(1)}, bf16[128,256]{1,0:T(8,128)(2,1)S(1)}, u32[]{:S(2)}, u32[]{:S(2)}) %collective-permute-start.13) | collective-permute-done | bytes 65568 | tf_op jit(solution)/shard_map/ppermute | solution.py:176
  38.9 0.4 collective-permute-start.14
  39.2 4.7 %collective-permute-done.14.y_ref = bf16[128,512]{1,0:T(8,128)(2,1)S(1)} collective-permute-done((bf16[128,512]{1,0:T(8,128)(2,1)S(1)}, bf16[128,512]{1,0:T(8,128)(2,1)S(1)}, u32[]{:S(2)}, u32[]{:S(2)}) %collective-permute-start.14) | collective-permute-done | bytes 131104 | tf_op jit(solution)/shard_map/ppermute | solution.py:176
  43.9 0.1 collective-permute-start.15
  44.0 0.9 %outer_swap.1 = bf16[256,512]{1,0:T(8,128)(2,1)} custom-call(bf16[272,512]{1,0:T(8,128)(2,1)S(1)} %front.1.v0_ref, bf16[256,512]{1,0:T(8,128)(2,1)S(1)} %get-tuple-element.25.rows_ref, bf16[32,512]{1,0:T(8,128)(2,1)S(1)} %collective-permute-done.4.window_ref), custom_call_target="tpu_custom_call" | custom-call | tf_op jit(solution)/shard_map/outer_swap/pallas_call | solution.py:260
  44.9 0.6 %collective-permute-done.15.near_ref = bf16[2,128,512]{2,1,0:T(8,128)(2,1)S(1)} collective-permute-done((bf16[2,128,512]{2,1,0:T(8,128)(2,1)S(1)}, bf16[2,128,512]{2,1,0:T(8,128)(2,1)S(1)}, u32[]{:S(2)}, u32[]{:S(2)}) %collective-permute-start.15) | collective-permute-done | bytes 262176 | tf_op jit(solution)/shard_map/ppermute | solution.py:176
  45.5 1.0 %place.1 = f32[512,512]{1,0:T(8,128)} custom-call(bf16[128,512]{1,0:T(8,128)(2,1)S(1)} %add_convert_fusion.mine_ref, bf16[128,512]{1,0:T(8,128)(2,1)S(1)} %collective-permute-done.14.y_ref, bf16[2,128,512]{2,1,0:T(8,128)(2,1)S(1)} %collective-permute-done.15.near_ref), custom_call_target="tpu_custom_call" | custom-call | tf_op jit(solution)/shard_map/place/pallas_call | solution.py:278
  (10 shorter events, 0.2 us)
Async XLA Ops:
  0.6 5.6 %copy-start = (bf16[256,4096]{1,0:T(8,128)(2,1)S(1)}, bf16[256,4096]{1,0:T(8,128)(2,1)}, u32[]{:S(2)}) copy-start(bf16[256,4096]{1,0:T(8,128)(2,1)} %own_ref.7) | copy-start | bytes 6291460
  0.6 5.5 %collective-permute-start = (bf16[256,4096]{1,0:T(8,128)(2,1)}, bf16[256,4096]{1,0:T(8,128)(2,1)S(1)}, u32[]{:S(2)}, u32[]{:S(2)}) collective-permute-start(bf16[256,4096]{1,0:T(8,128)(2,1)} %own_ref.7), channel_id=1, source_target_pairs={{0,8},{1,9},{2,10},{3,11},{4,12},{5,13},{6,14},{7,15},{8,0},{9,1},... | collective-permute-start | bytes 6291464 | tf_op jit(solution)/shard_map/ppermute | solution.py:176
  4.6 1.6 %collective-permute-start.1 = (bf16[272,512]{1,0:T(8,128)(2,1)S(1)}, bf16[272,512]{1,0:T(8,128)(2,1)S(1)}, u32[]{:S(2)}, u32[]{:S(2)}) collective-permute-start(bf16[272,512]{1,0:T(8,128)(2,1)S(1)} %front.1.v0_ref), channel_id=1, source_target_pairs={{0,8},{1,9},{2,10},{3,11},{4,12},{5,13},{6,14},{7,15},{8,0},{9,1},... | collective-permute-start | bytes 835592 | tf_op jit(solution)/shard_map/ppermute | solution.py:176
  6.7 9.4 %collective-permute-start.3 = (bf16[256,512]{1,0:T(8,128)(2,1)S(1)}, bf16[256,512]{1,0:T(8,128)(2,1)S(1)}, u32[]{:S(2)}, u32[]{:S(2)}) collective-permute-start(bf16[256,512]{1,0:T(8,128)(2,1)S(1)} %get-tuple-element.18), channel_id=1, source_target_pairs={{0,1},{1,0},{2,3},{3,2},{4,5},{5,4},{6,7},{7,6},{8,9},{9,8},{10,11... | collective-permute-start | bytes 786440 | tf_op jit(solution)/shard_map/ppermute | solution.py:176
  9.3 8.7 %collective-permute-start.8 = (bf16[256,512]{1,0:T(8,128)(2,1)S(1)}, bf16[256,512]{1,0:T(8,128)(2,1)S(1)}, u32[]{:S(2)}, u32[]{:S(2)}) collective-permute-start(bf16[256,512]{1,0:T(8,128)(2,1)S(1)} %get-tuple-element.22), channel_id=1, source_target_pairs={{0,16},{1,17},{2,18},{3,19},{4,20},{5,21},{6,22},{7,23},{8,24},{9,... | collective-permute-start | bytes 786440 | tf_op jit(solution)/shard_map/ppermute | solution.py:176
  11.8 14.9 %collective-permute-start.2 = (bf16[512,512]{1,0:T(8,128)(2,1)S(1)}, bf16[512,512]{1,0:T(8,128)(2,1)S(1)}, u32[]{:S(2)}, u32[]{:S(2)}) collective-permute-start(bf16[512,512]{1,0:T(8,128)(2,1)S(1)} %partial_sums.5), channel_id=1, source_target_pairs={{0,2},{1,3},{2,0},{3,1},{4,6},{5,7},{6,4},{7,5},{8,10},{9,11},{10,... | collective-permute-start | bytes 1572872 | tf_op jit(solution)/shard_map/ppermute | solution.py:176
  16.1 5.5 %collective-permute-start.5 = (bf16[128,512]{1,0:T(8,128)(2,1)S(1)}, bf16[128,512]{1,0:T(8,128)(2,1)S(1)}, u32[]{:S(2)}, u32[]{:S(2)}) collective-permute-start(bf16[128,512]{1,0:T(8,128)(2,1)S(1)} %add_convert_fusion.4), channel_id=1, source_target_pairs={{0,16},{1,17},{2,18},{3,19},{4,20},{5,21},{6,22},{7,23},{8,24},{9,... | collective-permute-start | bytes 393224 | tf_op jit(solution)/shard_map/ppermute | solution.py:176
  18.0 9.6 %collective-permute-start.9 = (bf16[128,512]{1,0:T(8,128)(2,1)S(1)}, bf16[128,512]{1,0:T(8,128)(2,1)S(1)}, u32[]{:S(2)}, u32[]{:S(2)}) collective-permute-start(bf16[128,512]{1,0:T(8,128)(2,1)S(1)} %add_convert_fusion.2), channel_id=1, source_target_pairs={{0,1},{1,0},{2,3},{3,2},{4,5},{5,4},{6,7},{7,6},{8,9},{9,8},{10,11... | collective-permute-start | bytes 393224 | tf_op jit(solution)/shard_map/ppermute | solution.py:176
  19.6 3.9 %collective-permute-start.4 = (bf16[32,512]{1,0:T(8,128)(2,1)S(1)}, bf16[32,512]{1,0:T(8,128)(2,1)S(1)}, u32[]{:S(2)}, u32[]{:S(2)}) collective-permute-start(bf16[32,512]{1,0:T(8,128)(2,1)S(1)} %get-tuple-element.19), channel_id=1, source_target_pairs={{0,16},{1,17},{2,18},{3,19},{4,20},{5,21},{6,22},{7,23},{8,24},{9,... | collective-permute-start | bytes 98312 | tf_op jit(solution)/shard_map/ppermute | solution.py:176
  21.6 6.7 %collective-permute-start.10 = (bf16[128,512]{1,0:T(8,128)(2,1)S(1)}, bf16[128,512]{1,0:T(8,128)(2,1)S(1)}, u32[]{:S(2)}, u32[]{:S(2)}) collective-permute-start(bf16[128,512]{1,0:T(8,128)(2,1)S(1)} %add_convert_fusion.3), channel_id=1, source_target_pairs={{0,2},{1,3},{2,0},{3,1},{4,6},{5,7},{6,4},{7,5},{8,10},{9,11},{10,... | collective-permute-start | bytes 393224 | tf_op jit(solution)/shard_map/ppermute | solution.py:176
  26.9 5.0 %collective-permute-start.7 = (bf16[256,256]{1,0:T(8,128)(2,1)S(1)}, bf16[256,256]{1,0:T(8,128)(2,1)S(1)}, u32[]{:S(2)}, u32[]{:S(2)}) collective-permute-start(bf16[256,256]{1,0:T(8,128)(2,1)S(1)} %pad_maximum_fusion.2), channel_id=1, source_target_pairs={{0,1},{1,0},{2,3},{3,2},{4,5},{5,4},{6,7},{7,6},{8,9},{9,8},{10,11... | collective-permute-start | bytes 393224 | tf_op jit(solution)/shard_map/ppermute | solution.py:176
  27.5 5.0 %collective-permute-start.6 = (bf16[256,256]{1,0:T(8,128)(2,1)S(1)}, bf16[256,256]{1,0:T(8,128)(2,1)S(1)}, u32[]{:S(2)}, u32[]{:S(2)}) collective-permute-start(bf16[256,256]{1,0:T(8,128)(2,1)S(1)} %slice.91), channel_id=1, source_target_pairs={{0,16},{1,17},{2,18},{3,19},{4,20},{5,21},{6,22},{7,23},{8,24},{9,... | collective-permute-start | bytes 393224 | tf_op jit(solution)/shard_map/ppermute | solution.py:176
  28.4 8.1 %collective-permute-start.11 = (bf16[128,512]{1,0:T(8,128)(2,1)S(1)}, bf16[128,512]{1,0:T(8,128)(2,1)S(1)}, u32[]{:S(2)}, u32[]{:S(2)}) collective-permute-start(bf16[128,512]{1,0:T(8,128)(2,1)S(1)} %add_convert_fusion.1), channel_id=1, source_target_pairs={{0,4},{1,5},{2,6},{3,7},{4,0},{5,1},{6,2},{7,3},{8,12},{9,13},{10,... | collective-permute-start | bytes 393224 | tf_op jit(solution)/shard_map/ppermute | solution.py:176
  32.5 4.3 %collective-permute-start.12 = (bf16[128,256]{1,0:T(8,128)(2,1)S(1)}, bf16[128,256]{1,0:T(8,128)(2,1)S(1)}, u32[]{:S(2)}, u32[]{:S(2)}) collective-permute-start(bf16[128,256]{1,0:T(8,128)(2,1)S(1)} %get-tuple-element.30), channel_id=1, source_target_pairs={{0,1},{1,0},{2,3},{3,2},{4,5},{5,4},{6,7},{7,6},{8,9},{9,8},{10,11... | collective-permute-start | bytes 196616 | tf_op jit(solution)/shard_map/ppermute | solution.py:176
  34.1 4.7 %collective-permute-start.13 = (bf16[128,256]{1,0:T(8,128)(2,1)S(1)}, bf16[128,256]{1,0:T(8,128)(2,1)S(1)}, u32[]{:S(2)}, u32[]{:S(2)}) collective-permute-start(bf16[128,256]{1,0:T(8,128)(2,1)S(1)} %get-tuple-element.35), channel_id=1, source_target_pairs={{0,16},{1,17},{2,18},{3,19},{4,20},{5,21},{6,22},{7,23},{8,24},{9,... | collective-permute-start | bytes 196616 | tf_op jit(solution)/shard_map/ppermute | solution.py:176
  38.9 5.0 %collective-permute-start.14 = (bf16[128,512]{1,0:T(8,128)(2,1)S(1)}, bf16[128,512]{1,0:T(8,128)(2,1)S(1)}, u32[]{:S(2)}, u32[]{:S(2)}) collective-permute-start(bf16[128,512]{1,0:T(8,128)(2,1)S(1)} %add_convert_fusion.mine_ref), channel_id=1, source_target_pairs={{0,16},{1,17},{2,18},{3,19},{4,20},{5,21},{6,22},{7,23},{8,24},{9,... | collective-permute-start | bytes 393224 | tf_op jit(solution)/shard_map/ppermute | solution.py:176
  43.9 1.6 %collective-permute-start.15 = (bf16[2,128,512]{2,1,0:T(8,128)(2,1)S(1)}, bf16[2,128,512]{2,1,0:T(8,128)(2,1)S(1)}, u32[]{:S(2)}, u32[]{:S(2)}) collective-permute-start(bf16[2,128,512]{2,1,0:T(8,128)(2,1)S(1)} %pad_maximum_fusion.1), channel_id=1, source_target_pairs={{0,8},{1,9},{2,10},{3,11},{4,12},{5,13},{6,14},{7,15},{8,0},{9,1},... | collective-permute-start | bytes 786440 | tf_op jit(solution)/shard_map/ppermute | solution.py:176

commit v8 on v7

--- a/solution.py
+++ b/solution.py
@@ -320,33 +320,31 @@
         return total
 
     first_b, first_a = sums((((3, 1, 1), (3, 0, 1)), ((2, 1, 1), (2, 1, 0))), BF16)
-    pair, = sums((((1, 1, 1), (1, 1, 0), (1, 0, 1), (1, 0, 0)),), BF16)
+    late_b, late_a = sums((((1, 1, 1), (1, 0, 1)), ((0, 1, 1), (0, 1, 0))), BF16)
     keep_b, keep_a = sums((((3, 1, 0), (3, 0, 0)), ((2, 0, 1), (2, 0, 0))), F32)
-    own, = sums((((0, 1, 1), (0, 1, 0), (0, 0, 1), (0, 0, 0)),), F32)
+    rest_b, rest_a = sums((((1, 1, 0), (1, 0, 0)), ((0, 0, 1), (0, 0, 0))), F32)
+    rows, window = inner_swap(after_all(v0, rest_b)[0], v1)
     first_b = xor_permute(first_b, X)
     first_a = xor_permute(first_a, Y)
-    pair = xor_permute(pair, Z1)
+    late_b = xor_permute(late_b, X)
     on_b = add(keep_b[:LANE], first_b[:LANE]).astype(BF16)
-    rows, window = inner_swap(after_all(v0, own)[0], v1)
-    window = xor_permute(after_all(window, on_b)[0], Y)
+    window, late_a = after_all(window, late_a, on_b)[:2]
     on_b = xor_permute(on_b, Y)
     on_a = xor_permute(add(keep_a[:LANE], first_a[:LANE]).astype(BF16), X)
+    late_a = xor_permute(late_a, Y)
+    window = xor_permute(window, Y)
     z3 = add(keep_b[LANE:], first_b[LANE:], on_b).astype(BF16)
-    pair, window = after_all(pair, window, z3)[:2]
+    late_b = after_all(late_b, z3)[0]
     z3 = xor_permute(z3, Z1)
     z2 = add(keep_a[LANE:], first_a[LANE:], on_a, z3).astype(BF16)
-
-    total = add(own, pair)
-    some, rest = total[:, :256], total[:, 256:]
-    rest_far, rest_y, rest_x, rest_own = (rest[row:row + LANE] for row in range(0, 4 * LANE, LANE))
-    some_in = xor_permute(some[:2 * LANE].astype(BF16), Y)
-    rest_in = xor_permute(jnp.concatenate([rest_far, rest_x]).astype(BF16), X)
-    some_in, rest_in = after_all(some_in, rest_in, z2)[:2]
+    late_a = after_all(late_a, z2)[0]
     z2 = xor_permute(z2, Z2)
-    some_on = xor_permute(add(some[2 * LANE:3 * LANE], some_in[:LANE]).astype(BF16), X)
-    rest_on = xor_permute(add(rest_y, rest_in[:LANE]).astype(BF16), Y)
-    base = jnp.concatenate([add(some[3 * LANE:], some_in[LANE:]), add(rest_own, rest_in[LANE:])], axis=1)
-    mine = add(fold(base, z2), jnp.concatenate([some_on, rest_on], axis=1)).astype(BF16)
+    late_on_b = xor_permute(add(rest_b[:LANE], late_b[:LANE]).astype(BF16), Y)
+    late_on_a = xor_permute(add(rest_a[:LANE], late_a[:LANE]).astype(BF16), X)
+    z1 = add(rest_b[LANE:], late_b[LANE:], late_on_b).astype(BF16)
+    z1, window = after_all(z1, window)
+    z1 = xor_permute(z1, Z1)
+    mine = add(fold(add(rest_a[LANE:], late_a[LANE:], late_on_a), z2), z1).astype(BF16)
     from_y = xor_permute(mine, Y)
     value_grad = outer_swap(v0, rows, after_all(window, from_y)[0])
     return place(mine, from_y, xor_permute(jnp.stack([mine, from_y]), CORE)), value_grad

time: 46.8 us -> 47.1 us (level)
  starting transfers between devices: 17.9 us -> 23.8 us
  waiting for transfers between devices: 19.8 us -> 14.3 us
    ppermute x16, starting transfers between devices: 17.9 us -> 23.8 us  [xor_permute(): lax.ppermute(value, ('dp', 'fsdp'), [(i, i ^ mask) for i in range(count)])]
    ppermute x16, waiting for transfers between devices: 19.8 us -> 14.3 us  [xor_permute(): lax.ppermute(value, ('dp', 'fsdp'), [(i, i ^ mask) for i in range(count)])]
  transfers between devices with their start and end apart: 16 -> 16, of which waited for: 13 -> 7; matrix products, arithmetic and copies ran while one was open for 1% -> 1% of each run, Pallas kernels for 11% -> 11%
where the time goes in v8:
time: 47.1 us; the launch traced here: 46.9 us
  starting transfers between devices  23.8 us (51%)
  waiting for transfers between devices  14.3 us (30%)
  Pallas kernels  6.89 us (15%)
  between operations  1.52 us (3%)
    ppermute x16, starting transfers between devices, xor_permute(): lax.ppermute(value, ('dp', 'fsdp'), [(i, i ^ mask) for i in range(count)])  23.8 us
    ppermute x16, waiting for transfers between devices, xor_permute(): lax.ppermute(value, ('dp', 'fsdp'), [(i, i ^ mask) for i in range(count)])  14.3 us
    pallas_call x1, Pallas kernels, front(): pl.pallas_call(functools.partial(front_kernel, per_group), in_specs=[HBM]...  2.64 us
    pallas_call x4, Pallas kernels, partial_sums(): pl.pallas_call(functools.partial(partial_kernel, parts), in_specs=[VMEM]...  1.93 us
    pallas_call x1, Pallas kernels, place(): pl.pallas_call(place_kernel, in_specs=[VMEM] * 3, out_specs=VMEM, out_sha...  1.05 us
  transfers between devices with their start and end apart: 16, of which 7 were waited for; matrix products, arithmetic and copies ran while one was open for 1% of the time, Pallas kernels for 11%

profile of v8, /device:TPU:0, one launch (start us, length us, event | category | flops | bytes accessed | tf_op | source)
XLA Modules:
  0.0 46.9 jit_solution(5295711766473384468)
XLA Ops:
  0.6 0.0 copy-start
  0.6 0.5 %collective-permute-start = (bf16[256,4096]{1,0:T(8,128)(2,1)}, bf16[256,4096]{1,0:T(8,128)(2,1)S(1)}, u32[]{:S(2)}, u32[]{:S(2)}) collective-permute-start(bf16[256,4096]{1,0:T(8,128)(2,1)} %own_ref.7), channel_id=1, source_target_pairs={{0,8},{1,9},{2,10},{3,11},{4,12},{5,13},{6,14},{7,15},{8,0},{9,1},... | collective-permute-start | bytes 6291464 | tf_op jit(solution)/shard_map/ppermute | solution.py:176
  1.9 2.6 %front.1.v0_ref = bf16[272,512]{1,0:T(8,128)(2,1)S(1)} custom-call(f32[16]{0:T(128)} %loss_hbm.1, s32[1]{0:T(128)S(6)} %copy.12.exponent_hbm, s32[1,2]{1,0:T(1,128)} %start_hbm.1, s32[1,2]{1,0:T(1,128)} %rows_hbm.1, bf16[256,2048]{1,0:T(8,128)(2,1)} %q_hbm.1, bf16[256,512]{1,0:T(8,128)(2,1)} %k_hbm.1, bf16[256,2048]{1,0:T(8,128)(2,1)} %g_hbm.1, ...), custom_call_target="tpu_custom_call" | custom-call | tf_op jit(solution)/shard_map/front/pallas_call | solution.py:153
  4.6 0.1 collective-permute-start.1
  4.7 1.5 %collective-permute-done.1.v1_ref = bf16[272,512]{1,0:T(8,128)(2,1)S(1)} collective-permute-done((bf16[272,512]{1,0:T(8,128)(2,1)S(1)}, bf16[272,512]{1,0:T(8,128)(2,1)S(1)}, u32[]{:S(2)}, u32[]{:S(2)}) %collective-permute-start.1) | collective-permute-done | bytes 278560 | tf_op jit(solution)/shard_map/ppermute | solution.py:176
  6.2 0.0 collective-permute-done.near_ref
  6.2 0.0 copy-done
  6.2 0.5 %partial_sums.7 = (bf16[256,512]{1,0:T(8,128)(2,1)S(1)}, bf16[256,512]{1,0:T(8,128)(2,1)S(1)}) custom-call(bf16[256,4096]{1,0:T(8,128)(2,1)S(1)} %copy-done, bf16[256,4096]{1,0:T(8,128)(2,1)S(1)} %collective-permute-done.near_ref, bf16[272,512]{1,0:T(8,128)(2,1)S(1)} %front.1.v0_ref, bf16[272,512]{1,0:T(8,128)(2,1)S(1)} %collective-permute-done.1.v1_ref), custom_call_target="tpu_custom_call" | custom-call | tf_op jit(solution)/shard_map/partial_sums/pallas_call | solution.py:196
  6.7 2.6 %collective-permute-start.2 = (bf16[256,512]{1,0:T(8,128)(2,1)S(1)}, bf16[256,512]{1,0:T(8,128)(2,1)S(1)}, u32[]{:S(2)}, u32[]{:S(2)}) collective-permute-start(bf16[256,512]{1,0:T(8,128)(2,1)S(1)} %get-tuple-element.26), channel_id=1, source_target_pairs={{0,1},{1,0},{2,3},{3,2},{4,5},{5,4},{6,7},{7,6},{8,9},{9,8},{10,11... | collective-permute-start | bytes 786440 | tf_op jit(solution)/shard_map/ppermute | solution.py:176
  9.3 1.5 %collective-permute-start.4 = (bf16[256,512]{1,0:T(8,128)(2,1)S(1)}, bf16[256,512]{1,0:T(8,128)(2,1)S(1)}, u32[]{:S(2)}, u32[]{:S(2)}) collective-permute-start(bf16[256,512]{1,0:T(8,128)(2,1)S(1)} %get-tuple-element.29), channel_id=1, source_target_pairs={{0,16},{1,17},{2,18},{3,19},{4,20},{5,21},{6,22},{7,23},{8,24},{9,... | collective-permute-start | bytes 786440 | tf_op jit(solution)/shard_map/ppermute | solution.py:176
  10.8 0.5 %partial_sums.5 = (bf16[256,512]{1,0:T(8,128)(2,1)S(1)}, bf16[256,512]{1,0:T(8,128)(2,1)S(1)}) custom-call(bf16[256,4096]{1,0:T(8,128)(2,1)S(1)} %copy-done, bf16[256,4096]{1,0:T(8,128)(2,1)S(1)} %collective-permute-done.near_ref, bf16[272,512]{1,0:T(8,128)(2,1)S(1)} %front.1.v0_ref, bf16[272,512]{1,0:T(8,128)(2,1)S(1)} %collective-permute-done.1.v1_ref), custom_call_target="tpu_custom_call" | custom-call | tf_op jit(solution)/shard_map/partial_sums/pallas_call | solution.py:196
  11.3 0.6 %collective-permute-start.10 = (bf16[256,512]{1,0:T(8,128)(2,1)S(1)}, bf16[256,512]{1,0:T(8,128)(2,1)S(1)}, u32[]{:S(2)}, u32[]{:S(2)}) collective-permute-start(bf16[256,512]{1,0:T(8,128)(2,1)S(1)} %get-tuple-element.31), channel_id=1, source_target_pairs={{0,1},{1,0},{2,3},{3,2},{4,5},{5,4},{6,7},{7,6},{8,9},{9,8},{10,11... | collective-permute-start | bytes 786440 | tf_op jit(solution)/shard_map/ppermute | solution.py:176
  11.9 0.5 %partial_sums.4 = (f32[256,512]{1,0:T(8,128)S(1)}, f32[256,512]{1,0:T(8,128)S(1)}) custom-call(bf16[256,4096]{1,0:T(8,128)(2,1)S(1)} %copy-done, bf16[256,4096]{1,0:T(8,128)(2,1)S(1)} %collective-permute-done.near_ref, bf16[272,512]{1,0:T(8,128)(2,1)S(1)} %front.1.v0_ref, bf16[272,512]{1,0:T(8,128)(2,1)S(1)} %collective-permute-done.1.v1_ref), custom_call_target="tpu_custom_call" | custom-call | tf_op jit(solution)/shard_map/partial_sums/pallas_call | solution.py:196
  12.4 0.5 %partial_sums.6 = (f32[256,512]{1,0:T(8,128)S(1)}, f32[256,512]{1,0:T(8,128)S(1)}) custom-call(bf16[256,4096]{1,0:T(8,128)(2,1)S(1)} %copy-done, bf16[256,4096]{1,0:T(8,128)(2,1)S(1)} %collective-permute-done.near_ref, bf16[272,512]{1,0:T(8,128)(2,1)S(1)} %front.1.v0_ref, bf16[272,512]{1,0:T(8,128)(2,1)S(1)} %collective-permute-done.1.v1_ref), custom_call_target="tpu_custom_call" | custom-call | tf_op jit(solution)/shard_map/partial_sums/pallas_call | solution.py:196
  12.9 0.3 inner_swap.1
  13.2 3.2 %collective-permute-done.2 = bf16[256,512]{1,0:T(8,128)(2,1)S(1)} collective-permute-done((bf16[256,512]{1,0:T(8,128)(2,1)S(1)}, bf16[256,512]{1,0:T(8,128)(2,1)S(1)}, u32[]{:S(2)}, u32[]{:S(2)}) %collective-permute-start.2) | collective-permute-done | bytes 262176 | tf_op jit(solution)/shard_map/ppermute | solution.py:176
  16.5 2.1 %collective-permute-start.6 = (bf16[128,512]{1,0:T(8,128)(2,1)S(1)}, bf16[128,512]{1,0:T(8,128)(2,1)S(1)}, u32[]{:S(2)}, u32[]{:S(2)}) collective-permute-start(bf16[128,512]{1,0:T(8,128)(2,1)S(1)} %add_convert_fusion.7), channel_id=1, source_target_pairs={{0,16},{1,17},{2,18},{3,19},{4,20},{5,21},{6,22},{7,23},{8,24},{9,... | collective-permute-start | bytes 393224 | tf_op jit(solution)/shard_map/ppermute | solution.py:176
  18.5 0.1 collective-permute-start.12
  18.6 0.0 collective-permute-done.4
  18.6 2.0 %collective-permute-start.5 = (bf16[128,512]{1,0:T(8,128)(2,1)S(1)}, bf16[128,512]{1,0:T(8,128)(2,1)S(1)}, u32[]{:S(2)}, u32[]{:S(2)}) collective-permute-start(bf16[128,512]{1,0:T(8,128)(2,1)S(1)} %add_convert_fusion.6), channel_id=1, source_target_pairs={{0,1},{1,0},{2,3},{3,2},{4,5},{5,4},{6,7},{7,6},{8,9},{9,8},{10,11... | collective-permute-start | bytes 393224 | tf_op jit(solution)/shard_map/ppermute | solution.py:176
  20.6 1.5 %collective-permute-start.3 = (bf16[256,512]{1,0:T(8,128)(2,1)S(1)}, bf16[256,512]{1,0:T(8,128)(2,1)S(1)}, u32[]{:S(2)}, u32[]{:S(2)}) collective-permute-start(bf16[256,512]{1,0:T(8,128)(2,1)S(1)} %get-tuple-element.27), channel_id=1, source_target_pairs={{0,16},{1,17},{2,18},{3,19},{4,20},{5,21},{6,22},{7,23},{8,24},{9,... | collective-permute-start | bytes 786440 | tf_op jit(solution)/shard_map/ppermute | solution.py:176
  22.2 0.0 collective-permute-done.6
  22.2 2.1 %collective-permute-start.7 = (bf16[128,512]{1,0:T(8,128)(2,1)S(1)}, bf16[128,512]{1,0:T(8,128)(2,1)S(1)}, u32[]{:S(2)}, u32[]{:S(2)}) collective-permute-start(bf16[128,512]{1,0:T(8,128)(2,1)S(1)} %add_convert_fusion.5), channel_id=1, source_target_pairs={{0,2},{1,3},{2,0},{3,1},{4,6},{5,7},{6,4},{7,5},{8,10},{9,11},{10,... | collective-permute-start | bytes 393224 | tf_op jit(solution)/shard_map/ppermute | solution.py:176
  24.3 0.0 collective-permute-done.10
  24.3 1.6 %collective-permute-start.11 = (bf16[128,512]{1,0:T(8,128)(2,1)S(1)}, bf16[128,512]{1,0:T(8,128)(2,1)S(1)}, u32[]{:S(2)}, u32[]{:S(2)}) collective-permute-start(bf16[128,512]{1,0:T(8,128)(2,1)S(1)} %add_convert_fusion.2), channel_id=1, source_target_pairs={{0,16},{1,17},{2,18},{3,19},{4,20},{5,21},{6,22},{7,23},{8,24},{9,... | collective-permute-start | bytes 393224 | tf_op jit(solution)/shard_map/ppermute | solution.py:176
  25.9 0.0 collective-permute-done.5
  25.9 1.3 %collective-permute-done.7 = bf16[128,512]{1,0:T(8,128)(2,1)S(1)} collective-permute-done((bf16[128,512]{1,0:T(8,128)(2,1)S(1)}, bf16[128,512]{1,0:T(8,128)(2,1)S(1)}, u32[]{:S(2)}, u32[]{:S(2)}) %collective-permute-start.7) | collective-permute-done | bytes 131104 | tf_op jit(solution)/shard_map/ppermute | solution.py:176
  27.2 0.1 add_convert_fusion.4
  27.3 3.9 %collective-permute-start.9 = (bf16[128,512]{1,0:T(8,128)(2,1)S(1)}, bf16[128,512]{1,0:T(8,128)(2,1)S(1)}, u32[]{:S(2)}, u32[]{:S(2)}) collective-permute-start(bf16[128,512]{1,0:T(8,128)(2,1)S(1)} %add_convert_fusion.4), channel_id=1, source_target_pairs={{0,4},{1,5},{2,6},{3,7},{4,0},{5,1},{6,2},{7,3},{8,12},{9,13},{10,... | collective-permute-start | bytes 393224 | tf_op jit(solution)/shard_map/ppermute | solution.py:176
  31.2 0.0 collective-permute-done.3
  31.2 2.9 %collective-permute-start.8 = (bf16[128,512]{1,0:T(8,128)(2,1)S(1)}, bf16[128,512]{1,0:T(8,128)(2,1)S(1)}, u32[]{:S(2)}, u32[]{:S(2)}) collective-permute-start(bf16[128,512]{1,0:T(8,128)(2,1)S(1)} %add_convert_fusion.3), channel_id=1, source_target_pairs={{0,1},{1,0},{2,3},{3,2},{4,5},{5,4},{6,7},{7,6},{8,9},{9,8},{10,11... | collective-permute-start | bytes 393224 | tf_op jit(solution)/shard_map/ppermute | solution.py:176
  34.1 0.0 collective-permute-done.11
  34.1 0.0 collective-permute-done.12.window_ref
  34.2 0.7 %collective-permute-start.13 = (bf16[128,512]{1,0:T(8,128)(2,1)S(1)}, bf16[128,512]{1,0:T(8,128)(2,1)S(1)}, u32[]{:S(2)}, u32[]{:S(2)}) collective-permute-start(bf16[128,512]{1,0:T(8,128)(2,1)S(1)} %add_convert_fusion.1), channel_id=1, source_target_pairs={{0,2},{1,3},{2,0},{3,1},{4,6},{5,7},{6,4},{7,5},{8,10},{9,11},{10,... | collective-permute-start | bytes 393224 | tf_op jit(solution)/shard_map/ppermute | solution.py:176
  34.9 2.1 %collective-permute-done.8 = bf16[128,512]{1,0:T(8,128)(2,1)S(1)} collective-permute-done((bf16[128,512]{1,0:T(8,128)(2,1)S(1)}, bf16[128,512]{1,0:T(8,128)(2,1)S(1)}, u32[]{:S(2)}, u32[]{:S(2)}) %collective-permute-start.8) | collective-permute-done | bytes 131104 | tf_op jit(solution)/shard_map/ppermute | solution.py:176
  37.1 0.0 collective-permute-done.9.arrived_ref
  37.1 2.1 %collective-permute-done.13 = bf16[128,512]{1,0:T(8,128)(2,1)S(1)} collective-permute-done((bf16[128,512]{1,0:T(8,128)(2,1)S(1)}, bf16[128,512]{1,0:T(8,128)(2,1)S(1)}, u32[]{:S(2)}, u32[]{:S(2)}) %collective-permute-start.13) | collective-permute-done | bytes 131104 | tf_op jit(solution)/shard_map/ppermute | solution.py:176
  39.2 1.6 %collective-permute-start.14 = (bf16[128,512]{1,0:T(8,128)(2,1)S(1)}, bf16[128,512]{1,0:T(8,128)(2,1)S(1)}, u32[]{:S(2)}, u32[]{:S(2)}) collective-permute-start(bf16[128,512]{1,0:T(8,128)(2,1)S(1)} %add_convert_fusion.mine_ref), channel_id=1, source_target_pairs={{0,16},{1,17},{2,18},{3,19},{4,20},{5,21},{6,22},{7,23},{8,24},{9,... | collective-permute-start | bytes 393224 | tf_op jit(solution)/shard_map/ppermute | solution.py:176
  40.8 3.4 %collective-permute-done.14.y_ref = bf16[128,512]{1,0:T(8,128)(2,1)S(1)} collective-permute-done((bf16[128,512]{1,0:T(8,128)(2,1)S(1)}, bf16[128,512]{1,0:T(8,128)(2,1)S(1)}, u32[]{:S(2)}, u32[]{:S(2)}) %collective-permute-start.14) | collective-permute-done | bytes 131104 | tf_op jit(solution)/shard_map/ppermute | solution.py:176
  44.3 0.1 collective-permute-start.15
  44.4 0.9 %outer_swap.1 = bf16[256,512]{1,0:T(8,128)(2,1)} custom-call(bf16[272,512]{1,0:T(8,128)(2,1)S(1)} %front.1.v0_ref, bf16[256,512]{1,0:T(8,128)(2,1)S(1)} %get-tuple-element.35.rows_ref, bf16[32,512]{1,0:T(8,128)(2,1)S(1)} %collective-permute-done.12.window_ref), custom_call_target="tpu_custom_call" | custom-call | tf_op jit(solution)/shard_map/outer_swap/pallas_call | solution.py:260
  45.3 0.6 %collective-permute-done.15.near_ref = bf16[2,128,512]{2,1,0:T(8,128)(2,1)S(1)} collective-permute-done((bf16[2,128,512]{2,1,0:T(8,128)(2,1)S(1)}, bf16[2,128,512]{2,1,0:T(8,128)(2,1)S(1)}, u32[]{:S(2)}, u32[]{:S(2)}) %collective-permute-start.15) | collective-permute-done | bytes 262176 | tf_op jit(solution)/shard_map/ppermute | solution.py:176
  45.9 1.0 %place.1 = f32[512,512]{1,0:T(8,128)} custom-call(bf16[128,512]{1,0:T(8,128)(2,1)S(1)} %add_convert_fusion.mine_ref, bf16[128,512]{1,0:T(8,128)(2,1)S(1)} %collective-permute-done.14.y_ref, bf16[2,128,512]{2,1,0:T(8,128)(2,1)S(1)} %collective-permute-done.15.near_ref), custom_call_target="tpu_custom_call" | custom-call | tf_op jit(solution)/shard_map/place/pallas_call | solution.py:278
  (10 shorter events, 0.3 us)
Async XLA Ops:
  0.6 5.6 %copy-start = (bf16[256,4096]{1,0:T(8,128)(2,1)S(1)}, bf16[256,4096]{1,0:T(8,128)(2,1)}, u32[]{:S(2)}) copy-start(bf16[256,4096]{1,0:T(8,128)(2,1)} %own_ref.7) | copy-start | bytes 6291460
  0.6 5.5 %collective-permute-start = (bf16[256,4096]{1,0:T(8,128)(2,1)}, bf16[256,4096]{1,0:T(8,128)(2,1)S(1)}, u32[]{:S(2)}, u32[]{:S(2)}) collective-permute-start(bf16[256,4096]{1,0:T(8,128)(2,1)} %own_ref.7), channel_id=1, source_target_pairs={{0,8},{1,9},{2,10},{3,11},{4,12},{5,13},{6,14},{7,15},{8,0},{9,1},... | collective-permute-start | bytes 6291464 | tf_op jit(solution)/shard_map/ppermute | solution.py:176
  4.6 1.6 %collective-permute-start.1 = (bf16[272,512]{1,0:T(8,128)(2,1)S(1)}, bf16[272,512]{1,0:T(8,128)(2,1)S(1)}, u32[]{:S(2)}, u32[]{:S(2)}) collective-permute-start(bf16[272,512]{1,0:T(8,128)(2,1)S(1)} %front.1.v0_ref), channel_id=1, source_target_pairs={{0,8},{1,9},{2,10},{3,11},{4,12},{5,13},{6,14},{7,15},{8,0},{9,1},... | collective-permute-start | bytes 835592 | tf_op jit(solution)/shard_map/ppermute | solution.py:176
  6.7 9.7 %collective-permute-start.2 = (bf16[256,512]{1,0:T(8,128)(2,1)S(1)}, bf16[256,512]{1,0:T(8,128)(2,1)S(1)}, u32[]{:S(2)}, u32[]{:S(2)}) collective-permute-start(bf16[256,512]{1,0:T(8,128)(2,1)S(1)} %get-tuple-element.26), channel_id=1, source_target_pairs={{0,1},{1,0},{2,3},{3,2},{4,5},{5,4},{6,7},{7,6},{8,9},{9,8},{10,11... | collective-permute-start | bytes 786440 | tf_op jit(solution)/shard_map/ppermute | solution.py:176
  9.3 9.3 %collective-permute-start.4 = (bf16[256,512]{1,0:T(8,128)(2,1)S(1)}, bf16[256,512]{1,0:T(8,128)(2,1)S(1)}, u32[]{:S(2)}, u32[]{:S(2)}) collective-permute-start(bf16[256,512]{1,0:T(8,128)(2,1)S(1)} %get-tuple-element.29), channel_id=1, source_target_pairs={{0,16},{1,17},{2,18},{3,19},{4,20},{5,21},{6,22},{7,23},{8,24},{9,... | collective-permute-start | bytes 786440 | tf_op jit(solution)/shard_map/ppermute | solution.py:176
  11.3 13.0 %collective-permute-start.10 = (bf16[256,512]{1,0:T(8,128)(2,1)S(1)}, bf16[256,512]{1,0:T(8,128)(2,1)S(1)}, u32[]{:S(2)}, u32[]{:S(2)}) collective-permute-start(bf16[256,512]{1,0:T(8,128)(2,1)S(1)} %get-tuple-element.31), channel_id=1, source_target_pairs={{0,1},{1,0},{2,3},{3,2},{4,5},{5,4},{6,7},{7,6},{8,9},{9,8},{10,11... | collective-permute-start | bytes 786440 | tf_op jit(solution)/shard_map/ppermute | solution.py:176
  16.5 5.7 %collective-permute-start.6 = (bf16[128,512]{1,0:T(8,128)(2,1)S(1)}, bf16[128,512]{1,0:T(8,128)(2,1)S(1)}, u32[]{:S(2)}, u32[]{:S(2)}) collective-permute-start(bf16[128,512]{1,0:T(8,128)(2,1)S(1)} %add_convert_fusion.7), channel_id=1, source_target_pairs={{0,16},{1,17},{2,18},{3,19},{4,20},{5,21},{6,22},{7,23},{8,24},{9,... | collective-permute-start | bytes 393224 | tf_op jit(solution)/shard_map/ppermute | solution.py:176
  18.5 15.6 %collective-permute-start.12 = (bf16[32,512]{1,0:T(8,128)(2,1)S(1)}, bf16[32,512]{1,0:T(8,128)(2,1)S(1)}, u32[]{:S(2)}, u32[]{:S(2)}) collective-permute-start(bf16[32,512]{1,0:T(8,128)(2,1)S(1)} %get-tuple-element.33), channel_id=1, source_target_pairs={{0,16},{1,17},{2,18},{3,19},{4,20},{5,21},{6,22},{7,23},{8,24},{9,... | collective-permute-start | bytes 98312 | tf_op jit(solution)/shard_map/ppermute | solution.py:176
  18.6 7.3 %collective-permute-start.5 = (bf16[128,512]{1,0:T(8,128)(2,1)S(1)}, bf16[128,512]{1,0:T(8,128)(2,1)S(1)}, u32[]{:S(2)}, u32[]{:S(2)}) collective-permute-start(bf16[128,512]{1,0:T(8,128)(2,1)S(1)} %add_convert_fusion.6), channel_id=1, source_target_pairs={{0,1},{1,0},{2,3},{3,2},{4,5},{5,4},{6,7},{7,6},{8,9},{9,8},{10,11... | collective-permute-start | bytes 393224 | tf_op jit(solution)/shard_map/ppermute | solution.py:176
  20.6 10.6 %collective-permute-start.3 = (bf16[256,512]{1,0:T(8,128)(2,1)S(1)}, bf16[256,512]{1,0:T(8,128)(2,1)S(1)}, u32[]{:S(2)}, u32[]{:S(2)}) collective-permute-start(bf16[256,512]{1,0:T(8,128)(2,1)S(1)} %get-tuple-element.27), channel_id=1, source_target_pairs={{0,16},{1,17},{2,18},{3,19},{4,20},{5,21},{6,22},{7,23},{8,24},{9,... | collective-permute-start | bytes 786440 | tf_op jit(solution)/shard_map/ppermute | solution.py:176
  22.2 5.0 %collective-permute-start.7 = (bf16[128,512]{1,0:T(8,128)(2,1)S(1)}, bf16[128,512]{1,0:T(8,128)(2,1)S(1)}, u32[]{:S(2)}, u32[]{:S(2)}) collective-permute-start(bf16[128,512]{1,0:T(8,128)(2,1)S(1)} %add_convert_fusion.5), channel_id=1, source_target_pairs={{0,2},{1,3},{2,0},{3,1},{4,6},{5,7},{6,4},{7,5},{8,10},{9,11},{10,... | collective-permute-start | bytes 393224 | tf_op jit(solution)/shard_map/ppermute | solution.py:176
  24.3 9.8 %collective-permute-start.11 = (bf16[128,512]{1,0:T(8,128)(2,1)S(1)}, bf16[128,512]{1,0:T(8,128)(2,1)S(1)}, u32[]{:S(2)}, u32[]{:S(2)}) collective-permute-start(bf16[128,512]{1,0:T(8,128)(2,1)S(1)} %add_convert_fusion.2), channel_id=1, source_target_pairs={{0,16},{1,17},{2,18},{3,19},{4,20},{5,21},{6,22},{7,23},{8,24},{9,... | collective-permute-start | bytes 393224 | tf_op jit(solution)/shard_map/ppermute | solution.py:176
  27.3 9.8 %collective-permute-start.9 = (bf16[128,512]{1,0:T(8,128)(2,1)S(1)}, bf16[128,512]{1,0:T(8,128)(2,1)S(1)}, u32[]{:S(2)}, u32[]{:S(2)}) collective-permute-start(bf16[128,512]{1,0:T(8,128)(2,1)S(1)} %add_convert_fusion.4), channel_id=1, source_target_pairs={{0,4},{1,5},{2,6},{3,7},{4,0},{5,1},{6,2},{7,3},{8,12},{9,13},{10,... | collective-permute-start | bytes 393224 | tf_op jit(solution)/shard_map/ppermute | solution.py:176
  31.2 5.8 %collective-permute-start.8 = (bf16[128,512]{1,0:T(8,128)(2,1)S(1)}, bf16[128,512]{1,0:T(8,128)(2,1)S(1)}, u32[]{:S(2)}, u32[]{:S(2)}) collective-permute-start(bf16[128,512]{1,0:T(8,128)(2,1)S(1)} %add_convert_fusion.3), channel_id=1, source_target_pairs={{0,1},{1,0},{2,3},{3,2},{4,5},{5,4},{6,7},{7,6},{8,9},{9,8},{10,11... | collective-permute-start | bytes 393224 | tf_op jit(solution)/shard_map/ppermute | solution.py:176
  34.2 5.0 %collective-permute-start.13 = (bf16[128,512]{1,0:T(8,128)(2,1)S(1)}, bf16[128,512]{1,0:T(8,128)(2,1)S(1)}, u32[]{:S(2)}, u32[]{:S(2)}) collective-permute-start(bf16[128,512]{1,0:T(8,128)(2,1)S(1)} %add_convert_fusion.1), channel_id=1, source_target_pairs={{0,2},{1,3},{2,0},{3,1},{4,6},{5,7},{6,4},{7,5},{8,10},{9,11},{10,... | collective-permute-start | bytes 393224 | tf_op jit(solution)/shard_map/ppermute | solution.py:176
  39.2 5.0 %collective-permute-start.14 = (bf16[128,512]{1,0:T(8,128)(2,1)S(1)}, bf16[128,512]{1,0:T(8,128)(2,1)S(1)}, u32[]{:S(2)}, u32[]{:S(2)}) collective-permute-start(bf16[128,512]{1,0:T(8,128)(2,1)S(1)} %add_convert_fusion.mine_ref), channel_id=1, source_target_pairs={{0,16},{1,17},{2,18},{3,19},{4,20},{5,21},{6,22},{7,23},{8,24},{9,... | collective-permute-start | bytes 393224 | tf_op jit(solution)/shard_map/ppermute | solution.py:176
  44.3 1.6 %collective-permute-start.15 = (bf16[2,128,512]{2,1,0:T(8,128)(2,1)S(1)}, bf16[2,128,512]{2,1,0:T(8,128)(2,1)S(1)}, u32[]{:S(2)}, u32[]{:S(2)}) collective-permute-start(bf16[2,128,512]{2,1,0:T(8,128)(2,1)S(1)} %pad_maximum_fusion), channel_id=1, source_target_pairs={{0,8},{1,9},{2,10},{3,11},{4,12},{5,13},{6,14},{7,15},{8,0},{9,1},... | collective-permute-start | bytes 786440 | tf_op jit(solution)/shard_map/ppermute | solution.py:176

commit v9 on v7

--- a/solution.py
+++ b/solution.py
@@ -179,15 +179,20 @@
 def partial_kernel(parts, own_ref, near_ref, v0_ref, v1_ref, *out_refs):
     dp = lax.axis_index("dp")
     fsdp = lax.axis_index("fsdp")
-    v = jnp.concatenate([ref[pl.ds(0, 2 * HALF), :] for ref in (v0_ref, v1_ref)], axis=0)
-    for blocks, out_ref in zip(parts, out_refs):
-        columns = []
-        for z, y, x in blocks:
+    loaded = {}
+
+    def block(z, y, x):
+        if (z, y, x) not in loaded:
             owner = fsdp ^ (z << 1 | x)
             column = pl.multiple_of(owner * (4 * LANE) + (dp ^ (y << 1)) * LANE, LANE)
-            columns.append(jnp.concatenate([ref[:, pl.ds(column, LANE)] for ref in (own_ref, near_ref)], axis=0))
+            loaded[z, y, x] = jnp.concatenate([ref[:, pl.ds(column, LANE)] for ref in (own_ref, near_ref)], axis=0)
+        return loaded[z, y, x]
+
+    for (blocks, start, width), out_ref in zip(parts, out_refs):
+        v = jnp.concatenate([ref[pl.ds(0, 2 * HALF), pl.ds(start, width)] for ref in (v0_ref, v1_ref)], axis=0)
         total = lax.dot_general(
-            jnp.concatenate(columns, axis=1), v, (((0,), (0,)), ((), ())), preferred_element_type=F32
+            jnp.concatenate([block(*place) for place in blocks], axis=1), v, (((0,), (0,)), ((), ())),
+            preferred_element_type=F32,
         )
         out_ref[...] = total.astype(out_ref.dtype)
 
@@ -197,7 +202,7 @@
         functools.partial(partial_kernel, parts),
         in_specs=[VMEM] * 4,
         out_specs=[VMEM] * len(parts),
-        out_shape=[jax.ShapeDtypeStruct((len(blocks) * LANE, 512), dtype) for blocks in parts],
+        out_shape=[jax.ShapeDtypeStruct((len(blocks) * LANE, width), dtype) for blocks, _, width in parts],
         compiler_params=pltpu.CompilerParams(vmem_limit_bytes=24 * MIB),
         cost_estimate=FREE,
         name="partial_sums",
@@ -319,31 +324,36 @@
             total = total + term.astype(F32)
         return total
 
-    first_b, first_a = sums((((3, 1, 1), (3, 0, 1)), ((2, 1, 1), (2, 1, 0))), BF16)
-    pair, = sums((((1, 1, 1), (1, 1, 0), (1, 0, 1), (1, 0, 0)),), BF16)
-    keep_b, keep_a = sums((((3, 1, 0), (3, 0, 0)), ((2, 0, 1), (2, 0, 0))), F32)
-    own, = sums((((0, 1, 1), (0, 1, 0), (0, 0, 1), (0, 0, 0)),), F32)
+    first_b, first_a = sums([(((3, 1, 1), (3, 0, 1)), 0, 512), (((2, 1, 1), (2, 1, 0)), 0, 512)], BF16)
+    every = ((1, 1), (1, 0), (0, 1), (0, 0))
+    pair_some, pair_rest = sums([(tuple((1, *at) for at in every), start, 256) for start in (0, 256)], BF16)
+    keep_b, keep_a = sums([(((3, 1, 0), (3, 0, 0)), 0, 512), (((2, 0, 1), (2, 0, 0)), 0, 512)], F32)
+    own_some, own_rest = sums([(tuple((0, *at) for at in every), start, 256) for start in (0, 256)], F32)
     first_b = xor_permute(first_b, X)
     first_a = xor_permute(first_a, Y)
-    pair = xor_permute(pair, Z1)
+    pair_sent = pair_rest
+    pair_some = xor_permute(pair_some, Z1)
+    pair_rest = xor_permute(pair_rest, Z1)
     on_b = add(keep_b[:LANE], first_b[:LANE]).astype(BF16)
-    rows, window = inner_swap(after_all(v0, own)[0], v1)
+    rows, window = inner_swap(after_all(v0, pair_sent)[0], v1)
     window = xor_permute(after_all(window, on_b)[0], Y)
     on_b = xor_permute(on_b, Y)
     on_a = xor_permute(add(keep_a[:LANE], first_a[:LANE]).astype(BF16), X)
     z3 = add(keep_b[LANE:], first_b[LANE:], on_b).astype(BF16)
-    pair, window = after_all(pair, window, z3)[:2]
+    pair_some, window = after_all(pair_some, window, z3)[:2]
     z3 = xor_permute(z3, Z1)
     z2 = add(keep_a[LANE:], first_a[LANE:], on_a, z3).astype(BF16)
 
-    total = add(own, pair)
-    some, rest = total[:, :256], total[:, 256:]
+    some = add(own_some, pair_some)
+    some_in = xor_permute(some[:2 * LANE].astype(BF16), Y)
+    rest = add(own_rest, after_all(pair_rest, some)[0])
     rest_far, rest_y, rest_x, rest_own = (rest[row:row + LANE] for row in range(0, 4 * LANE, LANE))
-    some_in = xor_permute(some[:2 * LANE].astype(BF16), Y)
     rest_in = xor_permute(jnp.concatenate([rest_far, rest_x]).astype(BF16), X)
-    some_in, rest_in = after_all(some_in, rest_in, z2)[:2]
+    some_in = after_all(some_in, z2)[0]
     z2 = xor_permute(z2, Z2)
-    some_on = xor_permute(add(some[2 * LANE:3 * LANE], some_in[:LANE]).astype(BF16), X)
+    some_on = add(some[2 * LANE:3 * LANE], some_in[:LANE]).astype(BF16)
+    rest_in = after_all(rest_in, some_on)[0]
+    some_on = xor_permute(some_on, X)
     rest_on = xor_permute(add(rest_y, rest_in[:LANE]).astype(BF16), Y)
     base = jnp.concatenate([add(some[3 * LANE:], some_in[LANE:]), add(rest_own, rest_in[LANE:])], axis=1)
     mine = add(fold(base, z2), jnp.concatenate([some_on, rest_on], axis=1)).astype(BF16)

time: 46.8 us -> 44.5 us (0.951)
  waiting for transfers between devices: 19.8 us -> 14.7 us
  starting transfers between devices: 17.9 us -> 20.8 us
    ppermute x16 -> x17, waiting for transfers between devices: 19.8 us -> 14.7 us  [xor_permute(): lax.ppermute(value, ('dp', 'fsdp'), [(i, i ^ mask) for i in range(count)])]
    ppermute x16 -> x17, starting transfers between devices: 17.9 us -> 20.8 us  [xor_permute(): lax.ppermute(value, ('dp', 'fsdp'), [(i, i ^ mask) for i in range(count)])]
  transfers between devices with their start and end apart: 16 -> 17, of which waited for: 13 -> 10; matrix products, arithmetic and copies ran while one was open for 1% -> 1% of each run, Pallas kernels for 11% -> 12%
where the time goes in v9:
time: 44.5 us; the launch traced here: 44.4 us
  starting transfers between devices  20.8 us (47%)
  waiting for transfers between devices  14.7 us (33%)
  Pallas kernels  6.89 us (15%)
  between operations  1.53 us (3%)
    ppermute x17, starting transfers between devices, xor_permute(): lax.ppermute(value, ('dp', 'fsdp'), [(i, i ^ mask) for i in range(count)])  20.8 us
    ppermute x17, waiting for transfers between devices, xor_permute(): lax.ppermute(value, ('dp', 'fsdp'), [(i, i ^ mask) for i in range(count)])  14.7 us
    pallas_call x1, Pallas kernels, front(): pl.pallas_call(functools.partial(front_kernel, per_group), in_specs=[HBM]...  2.64 us
    pallas_call x4, Pallas kernels, partial_sums(): pl.pallas_call(functools.partial(partial_kernel, parts), in_specs=[VMEM]...  1.94 us
    pallas_call x1, Pallas kernels, place(): pl.pallas_call(place_kernel, in_specs=[VMEM] * 3, out_specs=VMEM, out_sha...  1.05 us
    pallas_call x1, Pallas kernels, outer_swap(): pl.pallas_call(outer_swap_kernel, in_specs=[VMEM] * 3, out_specs=VMEM, ou...  0.91 us
  transfers between devices with their start and end apart: 17, of which 10 were waited for; matrix products, arithmetic and copies ran while one was open for 1% of the time, Pallas kernels for 12%

profile of v9, /device:TPU:0, one launch (start us, length us, event | category | flops | bytes accessed | tf_op | source)
XLA Modules:
  0.0 44.4 jit_solution(13772651664909462192)
XLA Ops:
  0.6 0.0 copy-start
  0.6 0.5 %collective-permute-start = (bf16[256,4096]{1,0:T(8,128)(2,1)}, bf16[256,4096]{1,0:T(8,128)(2,1)S(1)}, u32[]{:S(2)}, u32[]{:S(2)}) collective-permute-start(bf16[256,4096]{1,0:T(8,128)(2,1)} %own_ref.7), channel_id=1, source_target_pairs={{0,8},{1,9},{2,10},{3,11},{4,12},{5,13},{6,14},{7,15},{8,0},{9,1},... | collective-permute-start | bytes 6291464 | tf_op jit(solution)/shard_map/ppermute | solution.py:176
  1.9 2.6 %front.1.v0_ref = bf16[272,512]{1,0:T(8,128)(2,1)S(1)} custom-call(f32[16]{0:T(128)} %loss_hbm.1, s32[1]{0:T(128)S(6)} %copy.12.exponent_hbm, s32[1,2]{1,0:T(1,128)} %start_hbm.1, s32[1,2]{1,0:T(1,128)} %rows_hbm.1, bf16[256,2048]{1,0:T(8,128)(2,1)} %q_hbm.1, bf16[256,512]{1,0:T(8,128)(2,1)} %k_hbm.1, bf16[256,2048]{1,0:T(8,128)(2,1)} %g_hbm.1, ...), custom_call_target="tpu_custom_call" | custom-call | tf_op jit(solution)/shard_map/front/pallas_call | solution.py:153
  4.6 0.1 collective-permute-start.1
  4.7 1.5 %collective-permute-done.1.v1_ref = bf16[272,512]{1,0:T(8,128)(2,1)S(1)} collective-permute-done((bf16[272,512]{1,0:T(8,128)(2,1)S(1)}, bf16[272,512]{1,0:T(8,128)(2,1)S(1)}, u32[]{:S(2)}, u32[]{:S(2)}) %collective-permute-start.1) | collective-permute-done | bytes 278560 | tf_op jit(solution)/shard_map/ppermute | solution.py:176
  6.2 0.0 collective-permute-done.near_ref
  6.2 0.0 copy-done
  6.2 0.5 %partial_sums.7 = (bf16[256,512]{1,0:T(8,128)(2,1)S(1)}, bf16[256,512]{1,0:T(8,128)(2,1)S(1)}) custom-call(bf16[256,4096]{1,0:T(8,128)(2,1)S(1)} %copy-done, bf16[256,4096]{1,0:T(8,128)(2,1)S(1)} %collective-permute-done.near_ref, bf16[272,512]{1,0:T(8,128)(2,1)S(1)} %front.1.v0_ref, bf16[272,512]{1,0:T(8,128)(2,1)S(1)} %collective-permute-done.1.v1_ref), custom_call_target="tpu_custom_call" | custom-call | tf_op jit(solution)/shard_map/partial_sums/pallas_call | solution.py:201
  6.7 2.6 %collective-permute-start.3 = (bf16[256,512]{1,0:T(8,128)(2,1)S(1)}, bf16[256,512]{1,0:T(8,128)(2,1)S(1)}, u32[]{:S(2)}, u32[]{:S(2)}) collective-permute-start(bf16[256,512]{1,0:T(8,128)(2,1)S(1)} %get-tuple-element.26), channel_id=1, source_target_pairs={{0,1},{1,0},{2,3},{3,2},{4,5},{5,4},{6,7},{7,6},{8,9},{9,8},{10,11... | collective-permute-start | bytes 786440 | tf_op jit(solution)/shard_map/ppermute | solution.py:176
  9.3 1.5 %collective-permute-start.7 = (bf16[256,512]{1,0:T(8,128)(2,1)S(1)}, bf16[256,512]{1,0:T(8,128)(2,1)S(1)}, u32[]{:S(2)}, u32[]{:S(2)}) collective-permute-start(bf16[256,512]{1,0:T(8,128)(2,1)S(1)} %get-tuple-element.30), channel_id=1, source_target_pairs={{0,16},{1,17},{2,18},{3,19},{4,20},{5,21},{6,22},{7,23},{8,24},{9,... | collective-permute-start | bytes 786440 | tf_op jit(solution)/shard_map/ppermute | solution.py:176
  10.8 0.5 %partial_sums.5 = (bf16[512,256]{1,0:T(8,128)(2,1)S(1)}, bf16[512,256]{1,0:T(8,128)(2,1)S(1)}) custom-call(bf16[256,4096]{1,0:T(8,128)(2,1)S(1)} %copy-done, bf16[256,4096]{1,0:T(8,128)(2,1)S(1)} %collective-permute-done.near_ref, bf16[272,512]{1,0:T(8,128)(2,1)S(1)} %front.1.v0_ref, bf16[272,512]{1,0:T(8,128)(2,1)S(1)} %collective-permute-done.1.v1_ref), custom_call_target="tpu_custom_call" | custom-call | tf_op jit(solution)/shard_map/partial_sums/pallas_call | solution.py:201
  11.3 1.6 %collective-permute-start.10 = (bf16[512,256]{1,0:T(8,128)(2,1)S(1)}, bf16[512,256]{1,0:T(8,128)(2,1)S(1)}, u32[]{:S(2)}, u32[]{:S(2)}) collective-permute-start(bf16[512,256]{1,0:T(8,128)(2,1)S(1)} %get-tuple-element.22), channel_id=1, source_target_pairs={{0,2},{1,3},{2,0},{3,1},{4,6},{5,7},{6,4},{7,5},{8,10},{9,11},{10,... | collective-permute-start | bytes 786440 | tf_op jit(solution)/shard_map/ppermute | solution.py:176
  12.9 0.4 %collective-permute-start.2 = (bf16[512,256]{1,0:T(8,128)(2,1)S(1)}, bf16[512,256]{1,0:T(8,128)(2,1)S(1)}, u32[]{:S(2)}, u32[]{:S(2)}) collective-permute-start(bf16[512,256]{1,0:T(8,128)(2,1)S(1)} %get-tuple-element.21), channel_id=1, source_target_pairs={{0,2},{1,3},{2,0},{3,1},{4,6},{5,7},{6,4},{7,5},{8,10},{9,11},{10,... | collective-permute-start | bytes 786440 | tf_op jit(solution)/shard_map/ppermute | solution.py:176
  13.4 0.5 %partial_sums.6 = (f32[256,512]{1,0:T(8,128)S(1)}, f32[256,512]{1,0:T(8,128)S(1)}) custom-call(bf16[256,4096]{1,0:T(8,128)(2,1)S(1)} %copy-done, bf16[256,4096]{1,0:T(8,128)(2,1)S(1)} %collective-permute-done.near_ref, bf16[272,512]{1,0:T(8,128)(2,1)S(1)} %front.1.v0_ref, bf16[272,512]{1,0:T(8,128)(2,1)S(1)} %collective-permute-done.1.v1_ref), custom_call_target="tpu_custom_call" | custom-call | tf_op jit(solution)/shard_map/partial_sums/pallas_call | solution.py:201
  13.9 0.5 %partial_sums.4 = (f32[512,256]{1,0:T(8,128)S(1)}, f32[512,256]{1,0:T(8,128)S(1)}) custom-call(bf16[256,4096]{1,0:T(8,128)(2,1)S(1)} %copy-done, bf16[256,4096]{1,0:T(8,128)(2,1)S(1)} %collective-permute-done.near_ref, bf16[272,512]{1,0:T(8,128)(2,1)S(1)} %front.1.v0_ref, bf16[272,512]{1,0:T(8,128)(2,1)S(1)} %collective-permute-done.1.v1_ref), custom_call_target="tpu_custom_call" | custom-call | tf_op jit(solution)/shard_map/partial_sums/pallas_call | solution.py:201
  14.4 0.3 inner_swap.1
  14.7 1.4 %collective-permute-done.3 = bf16[256,512]{1,0:T(8,128)(2,1)S(1)} collective-permute-done((bf16[256,512]{1,0:T(8,128)(2,1)S(1)}, bf16[256,512]{1,0:T(8,128)(2,1)S(1)}, u32[]{:S(2)}, u32[]{:S(2)}) %collective-permute-start.3) | collective-permute-done | bytes 262176 | tf_op jit(solution)/shard_map/ppermute | solution.py:176
  16.1 1.8 %collective-permute-start.5 = (bf16[128,512]{1,0:T(8,128)(2,1)S(1)}, bf16[128,512]{1,0:T(8,128)(2,1)S(1)}, u32[]{:S(2)}, u32[]{:S(2)}) collective-permute-start(bf16[128,512]{1,0:T(8,128)(2,1)S(1)} %add_convert_fusion.4), channel_id=1, source_target_pairs={{0,16},{1,17},{2,18},{3,19},{4,20},{5,21},{6,22},{7,23},{8,24},{9,... | collective-permute-start | bytes 393224 | tf_op jit(solution)/shard_map/ppermute | solution.py:176
  18.0 0.0 collective-permute-done.7
  18.0 1.6 %collective-permute-start.8 = (bf16[128,512]{1,0:T(8,128)(2,1)S(1)}, bf16[128,512]{1,0:T(8,128)(2,1)S(1)}, u32[]{:S(2)}, u32[]{:S(2)}) collective-permute-start(bf16[128,512]{1,0:T(8,128)(2,1)S(1)} %add_convert_fusion.2), channel_id=1, source_target_pairs={{0,1},{1,0},{2,3},{3,2},{4,5},{5,4},{6,7},{7,6},{8,9},{9,8},{10,11... | collective-permute-start | bytes 393224 | tf_op jit(solution)/shard_map/ppermute | solution.py:176
  19.6 0.5 %collective-permute-start.4 = (bf16[32,512]{1,0:T(8,128)(2,1)S(1)}, bf16[32,512]{1,0:T(8,128)(2,1)S(1)}, u32[]{:S(2)}, u32[]{:S(2)}) collective-permute-start(bf16[32,512]{1,0:T(8,128)(2,1)S(1)} %get-tuple-element.27), channel_id=1, source_target_pairs={{0,16},{1,17},{2,18},{3,19},{4,20},{5,21},{6,22},{7,23},{8,24},{9,... | collective-permute-start | bytes 98312 | tf_op jit(solution)/shard_map/ppermute | solution.py:176
  20.1 1.5 %collective-permute-done.5 = bf16[128,512]{1,0:T(8,128)(2,1)S(1)} collective-permute-done((bf16[128,512]{1,0:T(8,128)(2,1)S(1)}, bf16[128,512]{1,0:T(8,128)(2,1)S(1)}, u32[]{:S(2)}, u32[]{:S(2)}) %collective-permute-start.5) | collective-permute-done | bytes 131104 | tf_op jit(solution)/shard_map/ppermute | solution.py:176
  21.7 1.7 %collective-permute-start.9 = (bf16[128,512]{1,0:T(8,128)(2,1)S(1)}, bf16[128,512]{1,0:T(8,128)(2,1)S(1)}, u32[]{:S(2)}, u32[]{:S(2)}) collective-permute-start(bf16[128,512]{1,0:T(8,128)(2,1)S(1)} %add_convert_fusion.3), channel_id=1, source_target_pairs={{0,2},{1,3},{2,0},{3,1},{4,6},{5,7},{6,4},{7,5},{8,10},{9,11},{10,... | collective-permute-start | bytes 393224 | tf_op jit(solution)/shard_map/ppermute | solution.py:176
  23.4 2.8 %collective-permute-done.2 = bf16[512,256]{1,0:T(8,128)(2,1)S(1)} collective-permute-done((bf16[512,256]{1,0:T(8,128)(2,1)S(1)}, bf16[512,256]{1,0:T(8,128)(2,1)S(1)}, u32[]{:S(2)}, u32[]{:S(2)}) %collective-permute-start.2) | collective-permute-done | bytes 262176 | tf_op jit(solution)/shard_map/ppermute | solution.py:176
  26.2 0.0 collective-permute-done.4.window_ref
  26.2 0.1 convert_add_fusion.1
  26.3 0.5 %collective-permute-start.6 = (bf16[256,256]{1,0:T(8,128)(2,1)S(1)}, bf16[256,256]{1,0:T(8,128)(2,1)S(1)}, u32[]{:S(2)}, u32[]{:S(2)}) collective-permute-start(bf16[256,256]{1,0:T(8,128)(2,1)S(1)} %slice.111), channel_id=1, source_target_pairs={{0,16},{1,17},{2,18},{3,19},{4,20},{5,21},{6,22},{7,23},{8,24},{9,... | collective-permute-start | bytes 393224 | tf_op jit(solution)/shard_map/ppermute | solution.py:176
  26.7 0.0 collective-permute-done.10
  26.7 0.1 fusion.2
  26.8 0.2 collective-permute-start.11
  27.0 0.0 collective-permute-done.8
  27.0 0.8 %collective-permute-done.9 = bf16[128,512]{1,0:T(8,128)(2,1)S(1)} collective-permute-done((bf16[128,512]{1,0:T(8,128)(2,1)S(1)}, bf16[128,512]{1,0:T(8,128)(2,1)S(1)}, u32[]{:S(2)}, u32[]{:S(2)}) %collective-permute-start.9) | collective-permute-done | bytes 131104 | tf_op jit(solution)/shard_map/ppermute | solution.py:176
  27.8 0.1 add_convert_fusion.1
  27.9 2.7 %collective-permute-start.12 = (bf16[128,512]{1,0:T(8,128)(2,1)S(1)}, bf16[128,512]{1,0:T(8,128)(2,1)S(1)}, u32[]{:S(2)}, u32[]{:S(2)}) collective-permute-start(bf16[128,512]{1,0:T(8,128)(2,1)S(1)} %add_convert_fusion.1), channel_id=1, source_target_pairs={{0,4},{1,5},{2,6},{3,7},{4,0},{5,1},{6,2},{7,3},{8,12},{9,13},{10,... | collective-permute-start | bytes 393224 | tf_op jit(solution)/shard_map/ppermute | solution.py:176
  30.5 0.8 %collective-permute-done.6 = bf16[256,256]{1,0:T(8,128)(2,1)S(1)} collective-permute-done((bf16[256,256]{1,0:T(8,128)(2,1)S(1)}, bf16[256,256]{1,0:T(8,128)(2,1)S(1)}, u32[]{:S(2)}, u32[]{:S(2)}) %collective-permute-start.6) | collective-permute-done | bytes 131104 | tf_op jit(solution)/shard_map/ppermute | solution.py:176
  31.3 0.5 %collective-permute-start.13 = (bf16[128,256]{1,0:T(8,128)(2,1)S(1)}, bf16[128,256]{1,0:T(8,128)(2,1)S(1)}, u32[]{:S(2)}, u32[]{:S(2)}) collective-permute-start(bf16[128,256]{1,0:T(8,128)(2,1)S(1)} %get-tuple-element.43), channel_id=1, source_target_pairs={{0,1},{1,0},{2,3},{3,2},{4,5},{5,4},{6,7},{7,6},{8,9},{9,8},{10,11... | collective-permute-start | bytes 196616 | tf_op jit(solution)/shard_map/ppermute | solution.py:176
  31.9 0.0 collective-permute-done.11
  31.9 2.2 %collective-permute-start.14 = (bf16[128,256]{1,0:T(8,128)(2,1)S(1)}, bf16[128,256]{1,0:T(8,128)(2,1)S(1)}, u32[]{:S(2)}, u32[]{:S(2)}) collective-permute-start(bf16[128,256]{1,0:T(8,128)(2,1)S(1)} %get-tuple-element.40), channel_id=1, source_target_pairs={{0,16},{1,17},{2,18},{3,19},{4,20},{5,21},{6,22},{7,23},{8,24},{9,... | collective-permute-start | bytes 196616 | tf_op jit(solution)/shard_map/ppermute | solution.py:176
  34.1 1.9 %collective-permute-done.12.arrived_ref = bf16[128,512]{1,0:T(8,128)(2,1)S(1)} collective-permute-done((bf16[128,512]{1,0:T(8,128)(2,1)S(1)}, bf16[128,512]{1,0:T(8,128)(2,1)S(1)}, u32[]{:S(2)}, u32[]{:S(2)}) %collective-permute-start.12) | collective-permute-done | bytes 131104 | tf_op jit(solution)/shard_map/ppermute | solution.py:176
  36.0 0.4 collective-permute-done.14
  36.4 0.0 collective-permute-done.13
  36.5 2.3 %collective-permute-start.15 = (bf16[128,512]{1,0:T(8,128)(2,1)S(1)}, bf16[128,512]{1,0:T(8,128)(2,1)S(1)}, u32[]{:S(2)}, u32[]{:S(2)}) collective-permute-start(bf16[128,512]{1,0:T(8,128)(2,1)S(1)} %add_convert_fusion.mine_ref), channel_id=1, source_target_pairs={{0,16},{1,17},{2,18},{3,19},{4,20},{5,21},{6,22},{7,23},{8,24},{9,... | collective-permute-start | bytes 393224 | tf_op jit(solution)/shard_map/ppermute | solution.py:176
  38.7 2.9 %collective-permute-done.15.y_ref = bf16[128,512]{1,0:T(8,128)(2,1)S(1)} collective-permute-done((bf16[128,512]{1,0:T(8,128)(2,1)S(1)}, bf16[128,512]{1,0:T(8,128)(2,1)S(1)}, u32[]{:S(2)}, u32[]{:S(2)}) %collective-permute-start.15) | collective-permute-done | bytes 131104 | tf_op jit(solution)/shard_map/ppermute | solution.py:176
  41.7 0.1 collective-permute-start.16
  41.8 0.9 %outer_swap.1 = bf16[256,512]{1,0:T(8,128)(2,1)} custom-call(bf16[272,512]{1,0:T(8,128)(2,1)S(1)} %front.1.v0_ref, bf16[256,512]{1,0:T(8,128)(2,1)S(1)} %get-tuple-element.35.rows_ref, bf16[32,512]{1,0:T(8,128)(2,1)S(1)} %collective-permute-done.4.window_ref), custom_call_target="tpu_custom_call" | custom-call | tf_op jit(solution)/shard_map/outer_swap/pallas_call | solution.py:265
  42.7 0.6 %collective-permute-done.16.near_ref = bf16[2,128,512]{2,1,0:T(8,128)(2,1)S(1)} collective-permute-done((bf16[2,128,512]{2,1,0:T(8,128)(2,1)S(1)}, bf16[2,128,512]{2,1,0:T(8,128)(2,1)S(1)}, u32[]{:S(2)}, u32[]{:S(2)}) %collective-permute-start.16) | collective-permute-done | bytes 262176 | tf_op jit(solution)/shard_map/ppermute | solution.py:176
  43.3 1.0 %place.1 = f32[512,512]{1,0:T(8,128)} custom-call(bf16[128,512]{1,0:T(8,128)(2,1)S(1)} %add_convert_fusion.mine_ref, bf16[128,512]{1,0:T(8,128)(2,1)S(1)} %collective-permute-done.15.y_ref, bf16[2,128,512]{2,1,0:T(8,128)(2,1)S(1)} %collective-permute-done.16.near_ref), custom_call_target="tpu_custom_call" | custom-call | tf_op jit(solution)/shard_map/place/pallas_call | solution.py:283
  (12 shorter events, 0.3 us)
Async XLA Ops:
  0.6 5.6 %copy-start = (bf16[256,4096]{1,0:T(8,128)(2,1)S(1)}, bf16[256,4096]{1,0:T(8,128)(2,1)}, u32[]{:S(2)}) copy-start(bf16[256,4096]{1,0:T(8,128)(2,1)} %own_ref.7) | copy-start | bytes 6291460
  0.6 5.5 %collective-permute-start = (bf16[256,4096]{1,0:T(8,128)(2,1)}, bf16[256,4096]{1,0:T(8,128)(2,1)S(1)}, u32[]{:S(2)}, u32[]{:S(2)}) collective-permute-start(bf16[256,4096]{1,0:T(8,128)(2,1)} %own_ref.7), channel_id=1, source_target_pairs={{0,8},{1,9},{2,10},{3,11},{4,12},{5,13},{6,14},{7,15},{8,0},{9,1},... | collective-permute-start | bytes 6291464 | tf_op jit(solution)/shard_map/ppermute | solution.py:176
  4.6 1.6 %collective-permute-start.1 = (bf16[272,512]{1,0:T(8,128)(2,1)S(1)}, bf16[272,512]{1,0:T(8,128)(2,1)S(1)}, u32[]{:S(2)}, u32[]{:S(2)}) collective-permute-start(bf16[272,512]{1,0:T(8,128)(2,1)S(1)} %front.1.v0_ref), channel_id=1, source_target_pairs={{0,8},{1,9},{2,10},{3,11},{4,12},{5,13},{6,14},{7,15},{8,0},{9,1},... | collective-permute-start | bytes 835592 | tf_op jit(solution)/shard_map/ppermute | solution.py:176
  6.7 9.4 %collective-permute-start.3 = (bf16[256,512]{1,0:T(8,128)(2,1)S(1)}, bf16[256,512]{1,0:T(8,128)(2,1)S(1)}, u32[]{:S(2)}, u32[]{:S(2)}) collective-permute-start(bf16[256,512]{1,0:T(8,128)(2,1)S(1)} %get-tuple-element.26), channel_id=1, source_target_pairs={{0,1},{1,0},{2,3},{3,2},{4,5},{5,4},{6,7},{7,6},{8,9},{9,8},{10,11... | collective-permute-start | bytes 786440 | tf_op jit(solution)/shard_map/ppermute | solution.py:176
  9.3 8.7 %collective-permute-start.7 = (bf16[256,512]{1,0:T(8,128)(2,1)S(1)}, bf16[256,512]{1,0:T(8,128)(2,1)S(1)}, u32[]{:S(2)}, u32[]{:S(2)}) collective-permute-start(bf16[256,512]{1,0:T(8,128)(2,1)S(1)} %get-tuple-element.30), channel_id=1, source_target_pairs={{0,16},{1,17},{2,18},{3,19},{4,20},{5,21},{6,22},{7,23},{8,24},{9,... | collective-permute-start | bytes 786440 | tf_op jit(solution)/shard_map/ppermute | solution.py:176
  11.3 15.4 %collective-permute-start.10 = (bf16[512,256]{1,0:T(8,128)(2,1)S(1)}, bf16[512,256]{1,0:T(8,128)(2,1)S(1)}, u32[]{:S(2)}, u32[]{:S(2)}) collective-permute-start(bf16[512,256]{1,0:T(8,128)(2,1)S(1)} %get-tuple-element.22), channel_id=1, source_target_pairs={{0,2},{1,3},{2,0},{3,1},{4,6},{5,7},{6,4},{7,5},{8,10},{9,11},{10,... | collective-permute-start | bytes 786440 | tf_op jit(solution)/shard_map/ppermute | solution.py:176
  12.9 13.2 %collective-permute-start.2 = (bf16[512,256]{1,0:T(8,128)(2,1)S(1)}, bf16[512,256]{1,0:T(8,128)(2,1)S(1)}, u32[]{:S(2)}, u32[]{:S(2)}) collective-permute-start(bf16[512,256]{1,0:T(8,128)(2,1)S(1)} %get-tuple-element.21), channel_id=1, source_target_pairs={{0,2},{1,3},{2,0},{3,1},{4,6},{5,7},{6,4},{7,5},{8,10},{9,11},{10,... | collective-permute-start | bytes 786440 | tf_op jit(solution)/shard_map/ppermute | solution.py:176
  16.1 5.5 %collective-permute-start.5 = (bf16[128,512]{1,0:T(8,128)(2,1)S(1)}, bf16[128,512]{1,0:T(8,128)(2,1)S(1)}, u32[]{:S(2)}, u32[]{:S(2)}) collective-permute-start(bf16[128,512]{1,0:T(8,128)(2,1)S(1)} %add_convert_fusion.4), channel_id=1, source_target_pairs={{0,16},{1,17},{2,18},{3,19},{4,20},{5,21},{6,22},{7,23},{8,24},{9,... | collective-permute-start | bytes 393224 | tf_op jit(solution)/shard_map/ppermute | solution.py:176
  18.0 9.0 %collective-permute-start.8 = (bf16[128,512]{1,0:T(8,128)(2,1)S(1)}, bf16[128,512]{1,0:T(8,128)(2,1)S(1)}, u32[]{:S(2)}, u32[]{:S(2)}) collective-permute-start(bf16[128,512]{1,0:T(8,128)(2,1)S(1)} %add_convert_fusion.2), channel_id=1, source_target_pairs={{0,1},{1,0},{2,3},{3,2},{4,5},{5,4},{6,7},{7,6},{8,9},{9,8},{10,11... | collective-permute-start | bytes 393224 | tf_op jit(solution)/shard_map/ppermute | solution.py:176
  19.6 6.6 %collective-permute-start.4 = (bf16[32,512]{1,0:T(8,128)(2,1)S(1)}, bf16[32,512]{1,0:T(8,128)(2,1)S(1)}, u32[]{:S(2)}, u32[]{:S(2)}) collective-permute-start(bf16[32,512]{1,0:T(8,128)(2,1)S(1)} %get-tuple-element.27), channel_id=1, source_target_pairs={{0,16},{1,17},{2,18},{3,19},{4,20},{5,21},{6,22},{7,23},{8,24},{9,... | collective-permute-start | bytes 98312 | tf_op jit(solution)/shard_map/ppermute | solution.py:176
  21.7 6.1 %collective-permute-start.9 = (bf16[128,512]{1,0:T(8,128)(2,1)S(1)}, bf16[128,512]{1,0:T(8,128)(2,1)S(1)}, u32[]{:S(2)}, u32[]{:S(2)}) collective-permute-start(bf16[128,512]{1,0:T(8,128)(2,1)S(1)} %add_convert_fusion.3), channel_id=1, source_target_pairs={{0,2},{1,3},{2,0},{3,1},{4,6},{5,7},{6,4},{7,5},{8,10},{9,11},{10,... | collective-permute-start | bytes 393224 | tf_op jit(solution)/shard_map/ppermute | solution.py:176
  26.3 5.0 %collective-permute-start.6 = (bf16[256,256]{1,0:T(8,128)(2,1)S(1)}, bf16[256,256]{1,0:T(8,128)(2,1)S(1)}, u32[]{:S(2)}, u32[]{:S(2)}) collective-permute-start(bf16[256,256]{1,0:T(8,128)(2,1)S(1)} %slice.111), channel_id=1, source_target_pairs={{0,16},{1,17},{2,18},{3,19},{4,20},{5,21},{6,22},{7,23},{8,24},{9,... | collective-permute-start | bytes 393224 | tf_op jit(solution)/shard_map/ppermute | solution.py:176
  26.8 5.0 %collective-permute-start.11 = (bf16[256,256]{1,0:T(8,128)(2,1)S(1)}, bf16[256,256]{1,0:T(8,128)(2,1)S(1)}, u32[]{:S(2)}, u32[]{:S(2)}) collective-permute-start(bf16[256,256]{1,0:T(8,128)(2,1)S(1)} %pad_maximum_fusion.2), channel_id=1, source_target_pairs={{0,1},{1,0},{2,3},{3,2},{4,5},{5,4},{6,7},{7,6},{8,9},{9,8},{10,11... | collective-permute-start | bytes 393224 | tf_op jit(solution)/shard_map/ppermute | solution.py:176
  27.9 8.1 %collective-permute-start.12 = (bf16[128,512]{1,0:T(8,128)(2,1)S(1)}, bf16[128,512]{1,0:T(8,128)(2,1)S(1)}, u32[]{:S(2)}, u32[]{:S(2)}) collective-permute-start(bf16[128,512]{1,0:T(8,128)(2,1)S(1)} %add_convert_fusion.1), channel_id=1, source_target_pairs={{0,4},{1,5},{2,6},{3,7},{4,0},{5,1},{6,2},{7,3},{8,12},{9,13},{10,... | collective-permute-start | bytes 393224 | tf_op jit(solution)/shard_map/ppermute | solution.py:176
  31.3 5.1 %collective-permute-start.13 = (bf16[128,256]{1,0:T(8,128)(2,1)S(1)}, bf16[128,256]{1,0:T(8,128)(2,1)S(1)}, u32[]{:S(2)}, u32[]{:S(2)}) collective-permute-start(bf16[128,256]{1,0:T(8,128)(2,1)S(1)} %get-tuple-element.43), channel_id=1, source_target_pairs={{0,1},{1,0},{2,3},{3,2},{4,5},{5,4},{6,7},{7,6},{8,9},{9,8},{10,11... | collective-permute-start | bytes 196616 | tf_op jit(solution)/shard_map/ppermute | solution.py:176
  31.9 4.5 %collective-permute-start.14 = (bf16[128,256]{1,0:T(8,128)(2,1)S(1)}, bf16[128,256]{1,0:T(8,128)(2,1)S(1)}, u32[]{:S(2)}, u32[]{:S(2)}) collective-permute-start(bf16[128,256]{1,0:T(8,128)(2,1)S(1)} %get-tuple-element.40), channel_id=1, source_target_pairs={{0,16},{1,17},{2,18},{3,19},{4,20},{5,21},{6,22},{7,23},{8,24},{9,... | collective-permute-start | bytes 196616 | tf_op jit(solution)/shard_map/ppermute | solution.py:176
  36.5 5.2 %collective-permute-start.15 = (bf16[128,512]{1,0:T(8,128)(2,1)S(1)}, bf16[128,512]{1,0:T(8,128)(2,1)S(1)}, u32[]{:S(2)}, u32[]{:S(2)}) collective-permute-start(bf16[128,512]{1,0:T(8,128)(2,1)S(1)} %add_convert_fusion.mine_ref), channel_id=1, source_target_pairs={{0,16},{1,17},{2,18},{3,19},{4,20},{5,21},{6,22},{7,23},{8,24},{9,... | collective-permute-start | bytes 393224 | tf_op jit(solution)/shard_map/ppermute | solution.py:176
  41.7 1.6 %collective-permute-start.16 = (bf16[2,128,512]{2,1,0:T(8,128)(2,1)S(1)}, bf16[2,128,512]{2,1,0:T(8,128)(2,1)S(1)}, u32[]{:S(2)}, u32[]{:S(2)}) collective-permute-start(bf16[2,128,512]{2,1,0:T(8,128)(2,1)S(1)} %pad_maximum_fusion.1), channel_id=1, source_target_pairs={{0,8},{1,9},{2,10},{3,11},{4,12},{5,13},{6,14},{7,15},{8,0},{9,1},... | collective-permute-start | bytes 786440 | tf_op jit(solution)/shard_map/ppermute | solution.py:176

commit v10 on v8

--- a/solution.py
+++ b/solution.py
@@ -171,25 +171,40 @@
 CORE, Y, X, Z1, Z2 = 8, 16, 1, 2, 4
 
 
+def routed(value, odd, even):
+    owners = lax.axis_size("fsdp")
+    count = lax.axis_size("dp") * owners
+    return lax.ppermute(
+        value, ("dp", "fsdp"), [(i, i ^ (odd if i // owners % 2 else even)) for i in range(count)]
+    )
+
+
 def xor_permute(value, mask):
-    count = lax.axis_size("dp") * lax.axis_size("fsdp")
-    return lax.ppermute(value, ("dp", "fsdp"), [(i, i ^ mask) for i in range(count)])
+    return routed(value, mask, mask)
 
 
 def partial_kernel(parts, own_ref, near_ref, v0_ref, v1_ref, *out_refs):
     dp = lax.axis_index("dp")
     fsdp = lax.axis_index("fsdp")
-    v = jnp.concatenate([ref[pl.ds(0, 2 * HALF), :] for ref in (v0_ref, v1_ref)], axis=0)
-    for blocks, out_ref in zip(parts, out_refs):
-        columns = []
-        for z, y, x in blocks:
-            owner = fsdp ^ (z << 1 | x)
-            column = pl.multiple_of(owner * (4 * LANE) + (dp ^ (y << 1)) * LANE, LANE)
-            columns.append(jnp.concatenate([ref[:, pl.ds(column, LANE)] for ref in (own_ref, near_ref)], axis=0))
-        total = lax.dot_general(
-            jnp.concatenate(columns, axis=1), v, (((0,), (0,)), ((), ())), preferred_element_type=F32
-        )
-        out_ref[...] = total.astype(out_ref.dtype)
+    odd = dp & 1
+
+    def pick(choices):
+        return choices[0] + odd * (choices[1] - choices[0])
+
+    for units, out_ref in zip(parts, out_refs):
+        for number, (odd_unit, even_unit) in enumerate(units):
+            z, y, x, part = (pick(pair) for pair in zip(even_unit, odd_unit))
+            owner = fsdp ^ (z * 2 + x)
+            quarter = (dp - odd) ^ (y * 2)
+            column = pl.ds(pl.multiple_of(owner * (4 * LANE) + quarter * LANE, 2 * LANE), 2 * LANE)
+            some = pl.ds(pl.multiple_of(part * (2 * LANE), 2 * LANE), 2 * LANE)
+            total = lax.dot_general(
+                jnp.concatenate([own_ref[:, column], near_ref[:, column]], axis=0),
+                jnp.concatenate([ref[pl.ds(0, 2 * HALF), some] for ref in (v0_ref, v1_ref)], axis=0),
+                (((0,), (0,)), ((), ())),
+                preferred_element_type=F32,
+            )
+            out_ref[pl.ds(number * (2 * LANE), 2 * LANE), :] = total.astype(out_ref.dtype)
 
 
 def partial_sums(parts, dtype, own, near, v0, v1):
@@ -197,7 +212,7 @@
         functools.partial(partial_kernel, parts),
         in_specs=[VMEM] * 4,
         out_specs=[VMEM] * len(parts),
-        out_shape=[jax.ShapeDtypeStruct((len(blocks) * LANE, 512), dtype) for blocks in parts],
+        out_shape=[jax.ShapeDtypeStruct((2 * HALF * len(units), 2 * HALF), dtype) for units in parts],
         compiler_params=pltpu.CompilerParams(vmem_limit_bytes=24 * MIB),
         cost_estimate=FREE,
         name="partial_sums",
@@ -268,44 +283,33 @@
     )(v0, rows, window)
 
 
-def place_kernel(mine_ref, y_ref, near_ref, out_ref):
+def place_kernel(pair_ref, near_ref, out_ref):
     dp = lax.axis_index("dp")
-    for flip, block in ((0, mine_ref), (2, y_ref), (1, near_ref.at[0]), (3, near_ref.at[1])):
-        out_ref[pl.ds(pl.multiple_of((dp ^ flip) * LANE, LANE), LANE), :] = block[...].astype(F32)
-
-
-def place(mine, from_y, near):
+    for ref, part in ((pair_ref, dp & 1), (near_ref, 1 - (dp & 1))):
+        some = pl.ds(pl.multiple_of(part * (2 * LANE), 2 * LANE), 2 * LANE)
+        for flip in range(2):
+            rows = pl.ds(pl.multiple_of(((dp >> 1) ^ flip) * (2 * LANE), 2 * LANE), 2 * LANE)
+            out_ref[rows, some] = ref[flip].astype(F32)
+
+
+def place(pair, near):
     return pl.pallas_call(
         place_kernel,
-        in_specs=[VMEM] * 3,
+        in_specs=[VMEM] * 2,
         out_specs=VMEM,
         out_shape=jax.ShapeDtypeStruct((512, 512), F32),
         compiler_params=pltpu.CompilerParams(vmem_limit_bytes=8 * MIB),
         cost_estimate=FREE,
         name="place",
-    )(mine, from_y, near)
-
-
-def fold_kernel(base_ref, arrived_ref, out_ref):
-    out_ref[...] = base_ref[...] + arrived_ref[...].astype(F32)
-
-
-def fold(base, arrived):
-    return pl.pallas_call(
-        fold_kernel,
-        in_specs=[VMEM] * 2,
-        out_specs=VMEM,
-        out_shape=jax.ShapeDtypeStruct(base.shape, F32),
-        compiler_params=pltpu.CompilerParams(vmem_limit_bytes=8 * MIB),
-        cost_estimate=pl.CostEstimate(flops=6_000_000_000, bytes_accessed=0, transcendentals=0),
-        name="fold",
-    )(base, arrived)
+    )(pair, near)
 
 
 def reduce_by_axis(layer_input, *args):
     near = xor_permute(layer_input, CORE)
     v0 = front(*args)
     v1 = xor_permute(v0, CORE)
+    odd = (lax.axis_index("dp") & 1) == 1
+    both = 2 * LANE
 
     def sums(parts, dtype):
         return partial_sums(parts, dtype, layer_input, near, v0, v1)
@@ -319,35 +323,48 @@
             total = total + term.astype(F32)
         return total
 
-    first_b, first_a = sums((((3, 1, 1), (3, 0, 1)), ((2, 1, 1), (2, 1, 0))), BF16)
-    late_b, late_a = sums((((1, 1, 1), (1, 0, 1)), ((0, 1, 1), (0, 1, 0))), BF16)
-    keep_b, keep_a = sums((((3, 1, 0), (3, 0, 0)), ((2, 0, 1), (2, 0, 0))), F32)
-    rest_b, rest_a = sums((((1, 1, 0), (1, 0, 0)), ((0, 0, 1), (0, 0, 0))), F32)
-    rows, window = inner_swap(after_all(v0, rest_b)[0], v1)
-    first_b = xor_permute(first_b, X)
-    first_a = xor_permute(first_a, Y)
-    late_b = xor_permute(late_b, X)
-    on_b = add(keep_b[:LANE], first_b[:LANE]).astype(BF16)
-    window, late_a = after_all(window, late_a, on_b)[:2]
-    on_b = xor_permute(on_b, Y)
-    on_a = xor_permute(add(keep_a[:LANE], first_a[:LANE]).astype(BF16), X)
-    late_a = xor_permute(late_a, Y)
-    window = xor_permute(window, Y)
-    z3 = add(keep_b[LANE:], first_b[LANE:], on_b).astype(BF16)
-    late_b = after_all(late_b, z3)[0]
-    z3 = xor_permute(z3, Z1)
-    z2 = add(keep_a[LANE:], first_a[LANE:], on_a, z3).astype(BF16)
-    late_a = after_all(late_a, z2)[0]
-    z2 = xor_permute(z2, Z2)
-    late_on_b = xor_permute(add(rest_b[:LANE], late_b[:LANE]).astype(BF16), Y)
-    late_on_a = xor_permute(add(rest_a[:LANE], late_a[:LANE]).astype(BF16), X)
-    z1 = add(rest_b[LANE:], late_b[LANE:], late_on_b).astype(BF16)
-    z1, window = after_all(z1, window)
-    z1 = xor_permute(z1, Z1)
-    mine = add(fold(add(rest_a[LANE:], late_a[LANE:], late_on_a), z2), z1).astype(BF16)
+    def chain(z, y, x):
+        return ((z, y, x, 0), (z, y, x, 1))
+
+    def own(z, y, part):
+        return ((z, y, 1, part), (z, y, 0, part))
+
+    def parts(*pairs):
+        return [tuple(zip(*pair)) for pair in pairs]
+
+    first, second = sums(parts((chain(3, 1, 1), own(1, 1, 0)), (chain(2, 1, 1), own(1, 0, 0))), BF16)
+    third, fourth = sums(parts((chain(3, 0, 1), own(1, 1, 1)), (chain(2, 1, 0), own(1, 0, 1))), BF16)
+    keep1, keep2 = sums(parts((chain(3, 1, 0), own(0, 1, 0)), (chain(2, 0, 1), own(0, 0, 0))), F32)
+    keep3, keep4 = sums(parts((chain(3, 0, 0), own(0, 1, 1)), (chain(2, 0, 0), own(0, 0, 1))), F32)
+    side = fourth
+    first = routed(first, X, Z1)
+    second = routed(second, Y, Z1)
+    third = routed(third, X, Z1)
+    total1 = add(keep1, first)
+    fourth = routed(jnp.where(odd, total1.astype(BF16), fourth), Y, Z1)
+    total2 = add(keep2, second)
+    fifth = jnp.where(odd, total2, total1).astype(BF16)
+    rows, window = inner_swap(after_all(v0, third)[0], v1)
+    side = after_all(side, fifth)[0]
+    fifth = routed(fifth, X, Y)
+    side = routed(side, Y, 0)
+    total3 = add(keep3, third)
+    sixth = jnp.where(odd, add(total3, fourth), total3).astype(BF16)
+    window = xor_permute(after_all(window, sixth)[0], Y)
+    sixth = routed(sixth, Z1, Y)
+    some = add(total2, fifth)
+    rest = add(keep4, jnp.where(odd, side, fourth), sixth)
+    last = jnp.where(odd, add(rest, fifth), jnp.concatenate([some[:both], rest[:both]])).astype(BF16)
+    last, window = after_all(last, window)
+    last = routed(last, Z2, X)
+    base = jnp.concatenate([add(some[both:], last[:both]), add(rest[both:], last[both:])])
+    mine = jnp.where(odd, last.astype(F32), base)
+    crossed = xor_permute(jnp.where(odd, last[:both], base[both:].astype(BF16)), CORE)
+    mine = add(jnp.where(odd, mine[both:], mine[:both]), crossed).astype(BF16)
     from_y = xor_permute(mine, Y)
     value_grad = outer_swap(v0, rows, after_all(window, from_y)[0])
-    return place(mine, from_y, xor_permute(jnp.stack([mine, from_y]), CORE)), value_grad
+    pair = jnp.stack([mine, from_y])
+    return place(pair, xor_permute(pair, CORE)), value_grad
 
 
 def swapped(block, axis, distance):

time: 47.1 us -> 48.8 us (1.036)
  starting transfers between devices: 23.8 us -> 16.3 us
  waiting for transfers between devices: 14.3 us -> 18.5 us
  local copies, waits for them, and re-layouts: 0.01 us -> 2.41 us
  other arithmetic: 0.35 us -> 2.64 us
    ppermute x16 -> x14, starting transfers between devices: 23.8 us -> 16.3 us  [routed(): lax.ppermute(value, ('dp', 'fsdp'), [(i, i ^ (odd if i // owners % 2 else...]
    ppermute x16 -> x14, waiting for transfers between devices: 14.3 us -> 18.5 us  [routed(): lax.ppermute(value, ('dp', 'fsdp'), [(i, i ^ (odd if i // owners % 2 else...]
    unnamed x2 -> x6, local copies, waits for them, and re-layouts: 0.01 us -> 2.37 us
    add x1 -> x3, other arithmetic: 0.04 us -> 1.16 us  [add(): total = total + term.astype(F32)]
    convert_element_type x8 -> x4, other arithmetic: 0.29 us -> 1.28 us  [the longest x1 1.06 us: reduce_by_axis(): fifth = jnp.where(odd, total2, total1).astype(BF16)]
    pallas_call x2 -> x1, Pallas kernels: 1.07 us -> 1.05 us  [place(): pl.pallas_call(place_kernel, in_specs=[VMEM] * 2, out_specs=VMEM, out_sha...]
  transfers between devices with their start and end apart: 16 -> 14, of which waited for: 7 -> 10; matrix products, arithmetic and copies ran while one was open for 1% -> 5% of each run, Pallas kernels for 11% -> 11%
where the time goes in v10:
time: 48.8 us; the launch traced here: 48.5 us
  waiting for transfers between devices  18.5 us (38%)
  starting transfers between devices  16.3 us (33%)
  Pallas kernels  7.07 us (14%)
  other arithmetic  2.64 us (5%)
  local copies, waits for them, and re-layouts  2.41 us (5%)
  between operations  1.55 us (3%)
    ppermute x14, waiting for transfers between devices, routed(): lax.ppermute(value, ('dp', 'fsdp'), [(i, i ^ (odd if i // owners % 2 else...  18.5 us
    ppermute x14, starting transfers between devices, routed(): lax.ppermute(value, ('dp', 'fsdp'), [(i, i ^ (odd if i // owners % 2 else...  16.3 us
    pallas_call x1, Pallas kernels, front(): pl.pallas_call(functools.partial(front_kernel, per_group), in_specs=[HBM]...  2.64 us
    unnamed x6, local copies, waits for them, and re-layouts  2.37 us
    pallas_call x4, Pallas kernels, partial_sums(): pl.pallas_call(functools.partial(partial_kernel, parts), in_specs=[VMEM]...  2.14 us
    add x3, other arithmetic, add(): total = total + term.astype(F32)  1.16 us
    convert_element_type x1, other arithmetic, reduce_by_axis(): fifth = jnp.where(odd, total2, total1).astype(BF16)  1.06 us
    pallas_call x1, Pallas kernels, place(): pl.pallas_call(place_kernel, in_specs=[VMEM] * 2, out_specs=VMEM, out_sha...  1.05 us
  transfers between devices with their start and end apart: 14, of which 10 were waited for; matrix products, arithmetic and copies ran while one was open for 5% of the time, Pallas kernels for 11%

profile of v10, /device:TPU:0, one launch (start us, length us, event | category | flops | bytes accessed | tf_op | source)
XLA Modules:
  0.0 48.5 jit_solution(2836178636565384677)
XLA Ops:
  0.6 0.0 copy-start
  0.6 0.5 %collective-permute-start = (bf16[256,4096]{1,0:T(8,128)(2,1)}, bf16[256,4096]{1,0:T(8,128)(2,1)S(1)}, u32[]{:S(2)}, u32[]{:S(2)}) collective-permute-start(bf16[256,4096]{1,0:T(8,128)(2,1)} %own_ref.7), channel_id=1, source_target_pairs={{0,8},{1,9},{2,10},{3,11},{4,12},{5,13},{6,14},{7,15},{8,0},{9,1},... | collective-permute-start | bytes 6291464 | tf_op jit(solution)/shard_map/ppermute | solution.py:177
  1.9 2.6 %front.1.v0_ref = bf16[272,512]{1,0:T(8,128)(2,1)S(1)} custom-call(f32[16]{0:T(128)} %loss_hbm.1, s32[1]{0:T(128)S(6)} %copy.12.exponent_hbm, s32[1,2]{1,0:T(1,128)} %start_hbm.1, s32[1,2]{1,0:T(1,128)} %rows_hbm.1, bf16[256,2048]{1,0:T(8,128)(2,1)} %q_hbm.1, bf16[256,512]{1,0:T(8,128)(2,1)} %k_hbm.1, bf16[256,2048]{1,0:T(8,128)(2,1)} %g_hbm.1, ...), custom_call_target="tpu_custom_call" | custom-call | tf_op jit(solution)/shard_map/front/pallas_call | solution.py:153
  4.6 0.1 collective-permute-start.1
  4.7 1.5 %collective-permute-done.1.v1_ref = bf16[272,512]{1,0:T(8,128)(2,1)S(1)} collective-permute-done((bf16[272,512]{1,0:T(8,128)(2,1)S(1)}, bf16[272,512]{1,0:T(8,128)(2,1)S(1)}, u32[]{:S(2)}, u32[]{:S(2)}) %collective-permute-start.1) | collective-permute-done | bytes 278560 | tf_op jit(solution)/shard_map/ppermute | solution.py:177
  6.2 0.0 collective-permute-done.near_ref
  6.2 0.0 copy-done
  6.2 0.0 copy-start.1
  6.2 0.5 %partial_sums.7 = (bf16[512,256]{1,0:T(8,128)(2,1)S(1)}, bf16[512,256]{1,0:T(8,128)(2,1)S(1)}) custom-call(bf16[256,4096]{1,0:T(8,128)(2,1)S(1)} %copy-done, bf16[256,4096]{1,0:T(8,128)(2,1)S(1)} %collective-permute-done.near_ref, bf16[272,512]{1,0:T(8,128)(2,1)S(1)} %front.1.v0_ref, bf16[272,512]{1,0:T(8,128)(2,1)S(1)} %collective-permute-done.1.v1_ref), custom_call_target="tpu_custom_call" | custom-call | tf_op jit(solution)/shard_map/partial_sums/pallas_call | solution.py:211
  6.7 0.8 %copy-done.1 = bf16[256,4096]{1,0:T(8,128)(2,1)} copy-done((bf16[256,4096]{1,0:T(8,128)(2,1)}, bf16[256,4096]{1,0:T(8,128)(2,1)S(1)}, u32[]{:S(2)}) %copy-start.1) | copy-done | bytes 2097176
  7.5 2.6 %collective-permute-start.3 = (bf16[512,256]{1,0:T(8,128)(2,1)S(1)}, bf16[512,256]{1,0:T(8,128)(2,1)S(1)}, u32[]{:S(2)}, u32[]{:S(2)}) collective-permute-start(bf16[512,256]{1,0:T(8,128)(2,1)S(1)} %get-tuple-element.23), channel_id=1, source_target_pairs={{0,2},{1,3},{2,0},{3,1},{4,6},{5,7},{6,4},{7,5},{8,9},{9,8},{10,11... | collective-permute-start | bytes 786440 | tf_op jit(solution)/shard_map/ppermute | solution.py:177
  10.1 0.0 collective-permute-start.2
  10.2 1.6 %copy-done.2 = bf16[256,4096]{1,0:T(8,128)(2,1)S(1)} copy-done((bf16[256,4096]{1,0:T(8,128)(2,1)S(1)}, bf16[256,4096]{1,0:T(8,128)(2,1)}, u32[]{:S(2)}) %copy-start.2) | copy-done | bytes 2097176
  11.8 0.5 %partial_sums.5 = (bf16[512,256]{1,0:T(8,128)(2,1)S(1)}, bf16[512,256]{1,0:T(8,128)(2,1)S(1)}) custom-call(bf16[256,4096]{1,0:T(8,128)(2,1)S(1)} %copy-done, bf16[256,4096]{1,0:T(8,128)(2,1)S(1)} %copy-done.2, bf16[272,512]{1,0:T(8,128)(2,1)S(1)} %front.1.v0_ref, bf16[272,512]{1,0:T(8,128)(2,1)S(1)} %collective-permute-done.1.v1_ref), custom_call_target="tpu_custom_call" | custom-call | tf_op jit(solution)/shard_map/partial_sums/pallas_call | solution.py:211
  12.3 2.1 %collective-permute-start.6 = (bf16[512,256]{1,0:T(8,128)(2,1)S(1)}, bf16[512,256]{1,0:T(8,128)(2,1)S(1)}, u32[]{:S(2)}, u32[]{:S(2)}) collective-permute-start(bf16[512,256]{1,0:T(8,128)(2,1)S(1)} %get-tuple-element.26), channel_id=1, source_target_pairs={{0,2},{1,3},{2,0},{3,1},{4,6},{5,7},{6,4},{7,5},{8,9},{9,8},{10,11... | collective-permute-start | bytes 786440 | tf_op jit(solution)/shard_map/ppermute | solution.py:177
  14.4 0.5 %partial_sums.6 = (f32[512,256]{1,0:T(8,128)S(1)}, f32[512,256]{1,0:T(8,128)S(1)}) custom-call(bf16[256,4096]{1,0:T(8,128)(2,1)S(1)} %copy-done, bf16[256,4096]{1,0:T(8,128)(2,1)S(1)} %copy-done.2, bf16[272,512]{1,0:T(8,128)(2,1)S(1)} %front.1.v0_ref, bf16[272,512]{1,0:T(8,128)(2,1)S(1)} %collective-permute-done.1.v1_ref), custom_call_target="tpu_custom_call" | custom-call | tf_op jit(solution)/shard_map/partial_sums/pallas_call | solution.py:211
  14.9 0.0 collective-permute-done.3
  14.9 0.1 fusion.4
  15.0 1.7 %collective-permute-start.5 = (bf16[512,256]{1,0:T(8,128)(2,1)S(1)}, bf16[512,256]{1,0:T(8,128)(2,1)S(1)}, u32[]{:S(2)}, u32[]{:S(2)}) collective-permute-start(bf16[512,256]{1,0:T(8,128)(2,1)S(1)} %fusion.4), channel_id=1, source_target_pairs={{0,2},{1,3},{2,0},{3,1},{4,6},{5,7},{6,4},{7,5},{8,24},{9,25},{10,... | collective-permute-start | bytes 786440 | tf_op jit(solution)/shard_map/ppermute | solution.py:177
  16.7 0.7 %collective-permute-done.2 = bf16[512,256]{1,0:T(8,128)(2,1)} collective-permute-done((bf16[512,256]{1,0:T(8,128)(2,1)S(1)}, bf16[512,256]{1,0:T(8,128)(2,1)}, u32[]{:S(2)}, u32[]{:S(2)}) %collective-permute-start.2) | collective-permute-done | bytes 262176 | tf_op jit(solution)/shard_map/ppermute | solution.py:177
  17.4 1.1 %select_convert_fusion = bf16[512,256]{1,0:T(8,128)(2,1)S(1)} fusion(f32[512,256]{1,0:T(8,128)S(1)} %get-tuple-element.20, bf16[512,256]{1,0:T(8,128)(2,1)} %collective-permute-done.2, f32[512,256]{1,0:T(8,128)S(1)} %get-tuple-element.22, bf16[512,256]{1,0:T(8,128)(2,1)S(1)} %collective-permute-done.3, pred[]{:T(512)S(6)} %eq.3), kind=kLoop, calls=%fused_computation.8 | loop fusion | flops 786432 | bytes 1835009 | tf_op jit(solution)/shard_map/convert_element_type | solution.py:346
  18.5 2.0 %collective-permute-start.8 = (bf16[512,256]{1,0:T(8,128)(2,1)S(1)}, bf16[512,256]{1,0:T(8,128)(2,1)S(1)}, u32[]{:S(2)}, u32[]{:S(2)}) collective-permute-start(bf16[512,256]{1,0:T(8,128)(2,1)S(1)} %select_convert_fusion), channel_id=1, source_target_pairs={{0,16},{1,17},{2,18},{3,19},{4,20},{5,21},{6,22},{7,23},{8,9},{9,8... | collective-permute-start | bytes 786440 | tf_op jit(solution)/shard_map/ppermute | solution.py:177
  20.5 0.5 %partial_sums.4 = (f32[512,256]{1,0:T(8,128)S(1)}, f32[512,256]{1,0:T(8,128)S(1)}) custom-call(bf16[256,4096]{1,0:T(8,128)(2,1)S(1)} %copy-done, bf16[256,4096]{1,0:T(8,128)(2,1)S(1)} %copy-done.2, bf16[272,512]{1,0:T(8,128)(2,1)S(1)} %front.1.v0_ref, bf16[272,512]{1,0:T(8,128)(2,1)S(1)} %collective-permute-done.1.v1_ref), custom_call_target="tpu_custom_call" | custom-call | tf_op jit(solution)/shard_map/partial_sums/pallas_call | solution.py:211
  21.0 0.0 collective-permute-done.6
  21.1 0.7 %collective-permute-start.4 = (bf16[512,256]{1,0:T(8,128)(2,1)S(1)}, bf16[512,256]{1,0:T(8,128)(2,1)S(1)}, u32[]{:S(2)}, u32[]{:S(2)}) collective-permute-start(bf16[512,256]{1,0:T(8,128)(2,1)S(1)} %get-tuple-element.24), channel_id=1, source_target_pairs={{0,0},{1,1},{2,2},{3,3},{4,4},{5,5},{6,6},{7,7},{8,24},{9,25},{10,... | collective-permute-start | bytes 786440 | tf_op jit(solution)/shard_map/ppermute | solution.py:177
  21.7 0.3 inner_swap.1
  22.1 0.8 %collective-permute-done.5 = bf16[512,256]{1,0:T(8,128)(2,1)S(1)} collective-permute-done((bf16[512,256]{1,0:T(8,128)(2,1)S(1)}, bf16[512,256]{1,0:T(8,128)(2,1)S(1)}, u32[]{:S(2)}, u32[]{:S(2)}) %collective-permute-start.5) | collective-permute-done | bytes 262176 | tf_op jit(solution)/shard_map/ppermute | solution.py:177
  22.9 0.1 fusion.2
  23.0 2.0 %collective-permute-start.7 = (bf16[512,256]{1,0:T(8,128)(2,1)S(1)}, bf16[512,256]{1,0:T(8,128)(2,1)S(1)}, u32[]{:S(2)}, u32[]{:S(2)}) collective-permute-start(bf16[512,256]{1,0:T(8,128)(2,1)S(1)} %fusion.2), channel_id=1, source_target_pairs={{0,16},{1,17},{2,18},{3,19},{4,20},{5,21},{6,22},{7,23},{8,10},{9,... | collective-permute-start | bytes 786440 | tf_op jit(solution)/shard_map/ppermute | solution.py:177
  25.0 0.1 collective-permute-start.9
  25.1 2.1 %collective-permute-done.8 = bf16[512,256]{1,0:T(8,128)(2,1)S(1)} collective-permute-done((bf16[512,256]{1,0:T(8,128)(2,1)S(1)}, bf16[512,256]{1,0:T(8,128)(2,1)S(1)}, u32[]{:S(2)}, u32[]{:S(2)}) %collective-permute-start.8) | collective-permute-done | bytes 262176 | tf_op jit(solution)/shard_map/ppermute | solution.py:177
  27.2 1.0 %convert_add_fusion = f32[512,256]{1,0:T(8,128)S(1)} fusion(bf16[512,256]{1,0:T(8,128)(2,1)S(1)} %collective-permute-done.8, f32[512,256]{1,0:T(8,128)S(1)} %get-tuple-element.20, bf16[512,256]{1,0:T(8,128)(2,1)} %collective-permute-done.2), kind=kLoop, calls=%fused_computation.1 | loop fusion | flops 524288 | bytes 1572864 | tf_op jit(solution)/shard_map/add | solution.py:323
  28.2 0.0 collective-permute-done.4
  28.3 2.6 %collective-permute-done.7 = bf16[512,256]{1,0:T(8,128)(2,1)S(1)} collective-permute-done((bf16[512,256]{1,0:T(8,128)(2,1)S(1)}, bf16[512,256]{1,0:T(8,128)(2,1)S(1)}, u32[]{:S(2)}, u32[]{:S(2)}) %collective-permute-start.7) | collective-permute-done | bytes 262176 | tf_op jit(solution)/shard_map/ppermute | solution.py:177
  30.9 0.1 convert_add_fusion.2
  31.0 0.1 fusion.1
  31.1 0.1 collective-permute-done.9.window_ref
  31.2 1.9 %collective-permute-start.10 = (bf16[512,256]{1,0:T(8,128)(2,1)S(1)}, bf16[512,256]{1,0:T(8,128)(2,1)S(1)}, u32[]{:S(2)}, u32[]{:S(2)}) collective-permute-start(bf16[512,256]{1,0:T(8,128)(2,1)S(1)} %fusion.1), channel_id=1, source_target_pairs={{0,1},{1,0},{2,3},{3,2},{4,5},{5,4},{6,7},{7,6},{8,12},{9,13},{10,... | collective-permute-start | bytes 786440 | tf_op jit(solution)/shard_map/ppermute | solution.py:177
  33.1 4.4 %collective-permute-done.10 = bf16[512,256]{1,0:T(8,128)(2,1)S(1)} collective-permute-done((bf16[512,256]{1,0:T(8,128)(2,1)S(1)}, bf16[512,256]{1,0:T(8,128)(2,1)S(1)}, u32[]{:S(2)}, u32[]{:S(2)}) %collective-permute-start.10) | collective-permute-done | bytes 262176 | tf_op jit(solution)/shard_map/ppermute | solution.py:177
  37.6 1.4 %collective-permute-start.11 = (bf16[256,256]{1,0:T(8,128)(2,1)S(1)}, bf16[256,256]{1,0:T(8,128)(2,1)S(1)}, u32[]{:S(2)}, u32[]{:S(2)}) collective-permute-start(bf16[256,256]{1,0:T(8,128)(2,1)S(1)} %get-tuple-element.34), channel_id=1, source_target_pairs={{0,8},{1,9},{2,10},{3,11},{4,12},{5,13},{6,14},{7,15},{8,0},{9,1},... | collective-permute-start | bytes 393224 | tf_op jit(solution)/shard_map/ppermute | solution.py:177
  39.0 0.1 maximum_select_fusion
  39.1 0.9 %collective-permute-done.11 = bf16[256,256]{1,0:T(8,128)(2,1)S(1)} collective-permute-done((bf16[256,256]{1,0:T(8,128)(2,1)S(1)}, bf16[256,256]{1,0:T(8,128)(2,1)S(1)}, u32[]{:S(2)}, u32[]{:S(2)}) %collective-permute-start.11) | collective-permute-done | bytes 131104 | tf_op jit(solution)/shard_map/ppermute | solution.py:177
  40.0 1.1 %collective-permute-start.12 = (bf16[256,256]{1,0:T(8,128)(2,1)S(1)}, bf16[256,256]{1,0:T(8,128)(2,1)S(1)}, u32[]{:S(2)}, u32[]{:S(2)}) collective-permute-start(bf16[256,256]{1,0:T(8,128)(2,1)S(1)} %fusion.6), channel_id=1, source_target_pairs={{0,16},{1,17},{2,18},{3,19},{4,20},{5,21},{6,22},{7,23},{8,24},{9,... | collective-permute-start | bytes 393224 | tf_op jit(solution)/shard_map/ppermute | solution.py:177
  41.1 4.7 %collective-permute-done.12 = bf16[256,256]{1,0:T(8,128)(2,1)S(1)} collective-permute-done((bf16[256,256]{1,0:T(8,128)(2,1)S(1)}, bf16[256,256]{1,0:T(8,128)(2,1)S(1)}, u32[]{:S(2)}, u32[]{:S(2)}) %collective-permute-start.12) | collective-permute-done | bytes 131104 | tf_op jit(solution)/shard_map/ppermute | solution.py:177
  45.9 0.1 collective-permute-start.13
  46.0 0.9 %outer_swap.1 = bf16[256,512]{1,0:T(8,128)(2,1)} custom-call(bf16[272,512]{1,0:T(8,128)(2,1)S(1)} %front.1.v0_ref, bf16[256,512]{1,0:T(8,128)(2,1)S(1)} %get-tuple-element.31.rows_ref, bf16[32,512]{1,0:T(8,128)(2,1)S(1)} %collective-permute-done.9.window_ref), custom_call_target="tpu_custom_call" | custom-call | tf_op jit(solution)/shard_map/outer_swap/pallas_call | solution.py:275
  46.9 0.6 %collective-permute-done.13.near_ref = bf16[2,256,256]{2,1,0:T(8,128)(2,1)S(1)} collective-permute-done((bf16[2,256,256]{2,1,0:T(8,128)(2,1)S(1)}, bf16[2,256,256]{2,1,0:T(8,128)(2,1)S(1)}, u32[]{:S(2)}, u32[]{:S(2)}) %collective-permute-start.13) | collective-permute-done | bytes 262176 | tf_op jit(solution)/shard_map/ppermute | solution.py:177
  47.5 1.1 %place.1 = f32[512,512]{1,0:T(8,128)} custom-call(bf16[2,256,256]{2,1,0:T(8,128)(2,1)S(1)} %pad_maximum_fusion.pair_ref, bf16[2,256,256]{2,1,0:T(8,128)(2,1)S(1)} %collective-permute-done.13.near_ref), custom_call_target="tpu_custom_call" | custom-call | tf_op jit(solution)/shard_map/place/pallas_call | solution.py:296
  (7 shorter events, 0.2 us)
Async XLA Ops:
  0.6 5.6 %copy-start = (bf16[256,4096]{1,0:T(8,128)(2,1)S(1)}, bf16[256,4096]{1,0:T(8,128)(2,1)}, u32[]{:S(2)}) copy-start(bf16[256,4096]{1,0:T(8,128)(2,1)} %own_ref.7) | copy-start | bytes 6291460
  0.6 5.5 %collective-permute-start = (bf16[256,4096]{1,0:T(8,128)(2,1)}, bf16[256,4096]{1,0:T(8,128)(2,1)S(1)}, u32[]{:S(2)}, u32[]{:S(2)}) collective-permute-start(bf16[256,4096]{1,0:T(8,128)(2,1)} %own_ref.7), channel_id=1, source_target_pairs={{0,8},{1,9},{2,10},{3,11},{4,12},{5,13},{6,14},{7,15},{8,0},{9,1},... | collective-permute-start | bytes 6291464 | tf_op jit(solution)/shard_map/ppermute | solution.py:177
  4.6 1.6 %collective-permute-start.1 = (bf16[272,512]{1,0:T(8,128)(2,1)S(1)}, bf16[272,512]{1,0:T(8,128)(2,1)S(1)}, u32[]{:S(2)}, u32[]{:S(2)}) collective-permute-start(bf16[272,512]{1,0:T(8,128)(2,1)S(1)} %front.1.v0_ref), channel_id=1, source_target_pairs={{0,8},{1,9},{2,10},{3,11},{4,12},{5,13},{6,14},{7,15},{8,0},{9,1},... | collective-permute-start | bytes 835592 | tf_op jit(solution)/shard_map/ppermute | solution.py:177
  6.2 1.3 %copy-start.1 = (bf16[256,4096]{1,0:T(8,128)(2,1)}, bf16[256,4096]{1,0:T(8,128)(2,1)S(1)}, u32[]{:S(2)}) copy-start(bf16[256,4096]{1,0:T(8,128)(2,1)S(1)} %collective-permute-done.near_ref) | copy-start | bytes 6291460
  7.5 7.4 %collective-permute-start.3 = (bf16[512,256]{1,0:T(8,128)(2,1)S(1)}, bf16[512,256]{1,0:T(8,128)(2,1)S(1)}, u32[]{:S(2)}, u32[]{:S(2)}) collective-permute-start(bf16[512,256]{1,0:T(8,128)(2,1)S(1)} %get-tuple-element.23), channel_id=1, source_target_pairs={{0,2},{1,3},{2,0},{3,1},{4,6},{5,7},{6,4},{7,5},{8,9},{9,8},{10,11... | collective-permute-start | bytes 786440 | tf_op jit(solution)/shard_map/ppermute | solution.py:177
  10.1 7.3 %collective-permute-start.2 = (bf16[512,256]{1,0:T(8,128)(2,1)S(1)}, bf16[512,256]{1,0:T(8,128)(2,1)}, u32[]{:S(2)}, u32[]{:S(2)}) collective-permute-start(bf16[512,256]{1,0:T(8,128)(2,1)S(1)} %get-tuple-element.21), channel_id=1, source_target_pairs={{0,2},{1,3},{2,0},{3,1},{4,6},{5,7},{6,4},{7,5},{8,24},{9,25},{10,... | collective-permute-start | bytes 786440 | tf_op jit(solution)/shard_map/ppermute | solution.py:177
  10.2 1.6 %copy-start.2 = (bf16[256,4096]{1,0:T(8,128)(2,1)S(1)}, bf16[256,4096]{1,0:T(8,128)(2,1)}, u32[]{:S(2)}) copy-start(bf16[256,4096]{1,0:T(8,128)(2,1)} %copy-done.1) | copy-start | bytes 6291460
  12.3 8.8 %collective-permute-start.6 = (bf16[512,256]{1,0:T(8,128)(2,1)S(1)}, bf16[512,256]{1,0:T(8,128)(2,1)S(1)}, u32[]{:S(2)}, u32[]{:S(2)}) collective-permute-start(bf16[512,256]{1,0:T(8,128)(2,1)S(1)} %get-tuple-element.26), channel_id=1, source_target_pairs={{0,2},{1,3},{2,0},{3,1},{4,6},{5,7},{6,4},{7,5},{8,9},{9,8},{10,11... | collective-permute-start | bytes 786440 | tf_op jit(solution)/shard_map/ppermute | solution.py:177
  15.0 7.9 %collective-permute-start.5 = (bf16[512,256]{1,0:T(8,128)(2,1)S(1)}, bf16[512,256]{1,0:T(8,128)(2,1)S(1)}, u32[]{:S(2)}, u32[]{:S(2)}) collective-permute-start(bf16[512,256]{1,0:T(8,128)(2,1)S(1)} %fusion.4), channel_id=1, source_target_pairs={{0,2},{1,3},{2,0},{3,1},{4,6},{5,7},{6,4},{7,5},{8,24},{9,25},{10,... | collective-permute-start | bytes 786440 | tf_op jit(solution)/shard_map/ppermute | solution.py:177
  18.5 8.7 %collective-permute-start.8 = (bf16[512,256]{1,0:T(8,128)(2,1)S(1)}, bf16[512,256]{1,0:T(8,128)(2,1)S(1)}, u32[]{:S(2)}, u32[]{:S(2)}) collective-permute-start(bf16[512,256]{1,0:T(8,128)(2,1)S(1)} %select_convert_fusion), channel_id=1, source_target_pairs={{0,16},{1,17},{2,18},{3,19},{4,20},{5,21},{6,22},{7,23},{8,9},{9,8... | collective-permute-start | bytes 786440 | tf_op jit(solution)/shard_map/ppermute | solution.py:177
  21.1 7.2 %collective-permute-start.4 = (bf16[512,256]{1,0:T(8,128)(2,1)S(1)}, bf16[512,256]{1,0:T(8,128)(2,1)S(1)}, u32[]{:S(2)}, u32[]{:S(2)}) collective-permute-start(bf16[512,256]{1,0:T(8,128)(2,1)S(1)} %get-tuple-element.24), channel_id=1, source_target_pairs={{0,0},{1,1},{2,2},{3,3},{4,4},{5,5},{6,6},{7,7},{8,24},{9,25},{10,... | collective-permute-start | bytes 786440 | tf_op jit(solution)/shard_map/ppermute | solution.py:177
  23.0 7.9 %collective-permute-start.7 = (bf16[512,256]{1,0:T(8,128)(2,1)S(1)}, bf16[512,256]{1,0:T(8,128)(2,1)S(1)}, u32[]{:S(2)}, u32[]{:S(2)}) collective-permute-start(bf16[512,256]{1,0:T(8,128)(2,1)S(1)} %fusion.2), channel_id=1, source_target_pairs={{0,16},{1,17},{2,18},{3,19},{4,20},{5,21},{6,22},{7,23},{8,10},{9,... | collective-permute-start | bytes 786440 | tf_op jit(solution)/shard_map/ppermute | solution.py:177
  25.0 6.2 %collective-permute-start.9 = (bf16[32,512]{1,0:T(8,128)(2,1)S(1)}, bf16[32,512]{1,0:T(8,128)(2,1)S(1)}, u32[]{:S(2)}, u32[]{:S(2)}) collective-permute-start(bf16[32,512]{1,0:T(8,128)(2,1)S(1)} %get-tuple-element.29), channel_id=1, source_target_pairs={{0,16},{1,17},{2,18},{3,19},{4,20},{5,21},{6,22},{7,23},{8,24},{9,... | collective-permute-start | bytes 98312 | tf_op jit(solution)/shard_map/ppermute | solution.py:177
  31.2 6.4 %collective-permute-start.10 = (bf16[512,256]{1,0:T(8,128)(2,1)S(1)}, bf16[512,256]{1,0:T(8,128)(2,1)S(1)}, u32[]{:S(2)}, u32[]{:S(2)}) collective-permute-start(bf16[512,256]{1,0:T(8,128)(2,1)S(1)} %fusion.1), channel_id=1, source_target_pairs={{0,1},{1,0},{2,3},{3,2},{4,5},{5,4},{6,7},{7,6},{8,12},{9,13},{10,... | collective-permute-start | bytes 786440 | tf_op jit(solution)/shard_map/ppermute | solution.py:177
  37.6 2.3 %collective-permute-start.11 = (bf16[256,256]{1,0:T(8,128)(2,1)S(1)}, bf16[256,256]{1,0:T(8,128)(2,1)S(1)}, u32[]{:S(2)}, u32[]{:S(2)}) collective-permute-start(bf16[256,256]{1,0:T(8,128)(2,1)S(1)} %get-tuple-element.34), channel_id=1, source_target_pairs={{0,8},{1,9},{2,10},{3,11},{4,12},{5,13},{6,14},{7,15},{8,0},{9,1},... | collective-permute-start | bytes 393224 | tf_op jit(solution)/shard_map/ppermute | solution.py:177
  40.0 5.8 %collective-permute-start.12 = (bf16[256,256]{1,0:T(8,128)(2,1)S(1)}, bf16[256,256]{1,0:T(8,128)(2,1)S(1)}, u32[]{:S(2)}, u32[]{:S(2)}) collective-permute-start(bf16[256,256]{1,0:T(8,128)(2,1)S(1)} %fusion.6), channel_id=1, source_target_pairs={{0,16},{1,17},{2,18},{3,19},{4,20},{5,21},{6,22},{7,23},{8,24},{9,... | collective-permute-start | bytes 393224 | tf_op jit(solution)/shard_map/ppermute | solution.py:177
  45.9 1.6 %collective-permute-start.13 = (bf16[2,256,256]{2,1,0:T(8,128)(2,1)S(1)}, bf16[2,256,256]{2,1,0:T(8,128)(2,1)S(1)}, u32[]{:S(2)}, u32[]{:S(2)}) collective-permute-start(bf16[2,256,256]{2,1,0:T(8,128)(2,1)S(1)} %pad_maximum_fusion.pair_ref), channel_id=1, source_target_pairs={{0,8},{1,9},{2,10},{3,11},{4,12},{5,13},{6,14},{7,15},{8,0},{9,1},... | collective-permute-start | bytes 786440 | tf_op jit(solution)/shard_map/ppermute | solution.py:177

commit v11 on v10

--- a/solution.py
+++ b/solution.py
@@ -97,7 +97,7 @@
 def front_kernel(
     per_group, loss_hbm, exponent_hbm, start_hbm, rows_hbm, q_hbm, k_hbm, g_hbm, ids_hbm, index_hbm, *rest
 ):
-    v_ref, loss_ref, exponent_ref, start_ref, rows_ref, q_ref, k_ref, g_ref, ids_ref, index_ref, sems = rest
+    v_ref, odd_ref, loss_ref, exponent_ref, start_ref, rows_ref, q_ref, k_ref, g_ref, ids_ref, index_ref, sems = rest
     count = 0
 
     def begin(source, target):
@@ -123,6 +123,7 @@
             begin(source.at[span, :], target.at[span, :])
             for source, target in ((q_hbm, q_ref), (k_hbm, k_ref), (g_hbm, g_ref))
         ])
+    odd_ref[...] = jnp.broadcast_to((lax.axis_index("dp") & 1).astype(F32), odd_ref.shape)
     for copy in small:
         copy.wait()
     masks = [
@@ -153,8 +154,10 @@
     return pl.pallas_call(
         functools.partial(front_kernel, per_group),
         in_specs=[HBM] * 9,
-        out_specs=VMEM,
-        out_shape=jax.ShapeDtypeStruct((tokens + INFO, key_width), BF16),
+        out_specs=[VMEM] * 2,
+        out_shape=[
+            jax.ShapeDtypeStruct((tokens + INFO, key_width), BF16), jax.ShapeDtypeStruct((8, 2 * HALF), F32)
+        ],
         scratch_shapes=[
             pltpu.SMEM(loss.shape, F32), pltpu.SMEM(exponent.shape, jnp.int32),
             pltpu.SMEM(start.shape, jnp.int32), pltpu.SMEM(rows.shape, jnp.int32),
@@ -306,9 +309,9 @@
 
 def reduce_by_axis(layer_input, *args):
     near = xor_permute(layer_input, CORE)
-    v0 = front(*args)
+    v0, odd = front(*args)
+    odd = odd[:1] > 0.5
     v1 = xor_permute(v0, CORE)
-    odd = (lax.axis_index("dp") & 1) == 1
     both = 2 * LANE
 
     def sums(parts, dtype):
@@ -341,19 +344,26 @@
     second = routed(second, Y, Z1)
     third = routed(third, X, Z1)
     total1 = add(keep1, first)
-    fourth = routed(jnp.where(odd, total1.astype(BF16), fourth), Y, Z1)
+    fourth = jnp.where(odd, total1.astype(BF16), fourth)
+    second = after_all(second, fourth)[0]
+    fourth = routed(fourth, Y, Z1)
     total2 = add(keep2, second)
     fifth = jnp.where(odd, total2, total1).astype(BF16)
     rows, window = inner_swap(after_all(v0, third)[0], v1)
+    fifth_sent = fifth
     side = after_all(side, fifth)[0]
     fifth = routed(fifth, X, Y)
     side = routed(side, Y, 0)
+    third, fourth = after_all(third, fourth, fifth_sent)[:2]
     total3 = add(keep3, third)
     sixth = jnp.where(odd, add(total3, fourth), total3).astype(BF16)
-    window = xor_permute(after_all(window, sixth)[0], Y)
+    window, side, fifth = after_all(window, side, fifth, sixth)[:3]
+    window = xor_permute(window, Y)
     sixth = routed(sixth, Z1, Y)
     some = add(total2, fifth)
-    rest = add(keep4, jnp.where(odd, side, fourth), sixth)
+    rest = add(keep4, jnp.where(odd, side, fourth))
+    rest, sixth = after_all(rest, sixth)
+    rest = add(rest, sixth)
     last = jnp.where(odd, add(rest, fifth), jnp.concatenate([some[:both], rest[:both]])).astype(BF16)
     last, window = after_all(last, window)
     last = routed(last, Z2, X)
@@ -386,7 +396,7 @@
 def reduce_by_owner(layer_input, *args):
     swap_start, swap_rows = args[-2:]
     tokens = layer_input.shape[0]
-    values = front(*args)[:tokens]
+    values = front(*args)[0][:tokens]
     balanced = values
     for level in range(lax.axis_size("dp").bit_length() - 1):
         offset = swap_start[0, level]

time: 48.8 us -> 46.6 us (0.955)
  local copies, waits for them, and re-layouts: 2.41 us -> 0.04 us
  other arithmetic: 2.64 us -> 0.9 us
  starting transfers between devices: 16.3 us -> 17.9 us
    unnamed x6 -> x2, local copies, waits for them, and re-layouts: 2.37 us -> 0.01 us
    ppermute x14, starting transfers between devices: 16.3 us -> 17.9 us  [routed(): lax.ppermute(value, ('dp', 'fsdp'), [(i, i ^ (odd if i // owners % 2 else...]
    convert_element_type x1, other arithmetic: 1.06 us -> 0.13 us  [reduce_by_axis(): fifth = jnp.where(odd, total2, total1).astype(BF16)]
    add x3 -> x4, other arithmetic: 1.16 us -> 0.24 us  [add(): total = total + term.astype(F32)]
  transfers between devices with their start and end apart: 14 -> 14, of which waited for: 10 -> 11; matrix products, arithmetic and copies ran while one was open for 5% -> 2% of each run, Pallas kernels for 11% -> 12%
where the time goes in v11:
time: 46.6 us; the launch traced here: 46.4 us
  waiting for transfers between devices  18.9 us (41%)
  starting transfers between devices  17.9 us (38%)
  Pallas kernels  7.06 us (15%)
  between operations  1.53 us (3%)
  other arithmetic  0.9 us (2%)
    ppermute x14, waiting for transfers between devices, routed(): lax.ppermute(value, ('dp', 'fsdp'), [(i, i ^ (odd if i // owners % 2 else...  18.9 us
    ppermute x14, starting transfers between devices, routed(): lax.ppermute(value, ('dp', 'fsdp'), [(i, i ^ (odd if i // owners % 2 else...  17.9 us
    pallas_call x1, Pallas kernels, front(): pl.pallas_call(functools.partial(front_kernel, per_group), in_specs=[HBM]...  2.64 us
    pallas_call x4, Pallas kernels, partial_sums(): pl.pallas_call(functools.partial(partial_kernel, parts), in_specs=[VMEM]...  2.13 us
    pallas_call x1, Pallas kernels, place(): pl.pallas_call(place_kernel, in_specs=[VMEM] * 2, out_specs=VMEM, out_sha...  1.05 us
  transfers between devices with their start and end apart: 14, of which 11 were waited for; matrix products, arithmetic and copies ran while one was open for 2% of the time, Pallas kernels for 12%

profile of v11, /device:TPU:0, one launch (start us, length us, event | category | flops | bytes accessed | tf_op | source)
XLA Modules:
  0.0 46.4 jit_solution(5740785002639626879)
XLA Ops:
  0.6 0.0 copy-start
  0.6 0.5 %collective-permute-start = (bf16[256,4096]{1,0:T(8,128)(2,1)}, bf16[256,4096]{1,0:T(8,128)(2,1)S(1)}, u32[]{:S(2)}, u32[]{:S(2)}) collective-permute-start(bf16[256,4096]{1,0:T(8,128)(2,1)} %own_ref.7), channel_id=1, source_target_pairs={{0,8},{1,9},{2,10},{3,11},{4,12},{5,13},{6,14},{7,15},{8,0},{9,1},... | collective-permute-start | bytes 6291464 | tf_op jit(solution)/shard_map/ppermute | solution.py:180
  1.9 2.6 %front.1 = (bf16[272,512]{1,0:T(8,128)(2,1)S(1)}, f32[8,256]{1,0:T(8,128)S(1)}) custom-call(f32[16]{0:T(128)} %loss_hbm.1, s32[1]{0:T(128)S(6)} %copy.12.exponent_hbm, s32[1,2]{1,0:T(1,128)} %start_hbm.1, s32[1,2]{1,0:T(1,128)} %rows_hbm.1, bf16[256,2048]{1,0:T(8,128)(2,1)} %q_hbm.1, bf16[256,512]{1,0:T(8,128)(2,1)} %k_hbm.1, bf16[256,2048]{1,0:T(8,128)(2,1)} %g_hbm.1, ...), custom_call_target="tpu_custom_call" | custom-call | tf_op jit(solution)/shard_map/front/pallas_call | solution.py:154
  4.6 0.1 collective-permute-start.1
  4.7 1.5 %collective-permute-done.1.v1_ref = bf16[272,512]{1,0:T(8,128)(2,1)S(1)} collective-permute-done((bf16[272,512]{1,0:T(8,128)(2,1)S(1)}, bf16[272,512]{1,0:T(8,128)(2,1)S(1)}, u32[]{:S(2)}, u32[]{:S(2)}) %collective-permute-start.1) | collective-permute-done | bytes 278560 | tf_op jit(solution)/shard_map/ppermute | solution.py:180
  6.2 0.0 collective-permute-done.near_ref
  6.2 0.0 copy-done
  6.2 0.5 %partial_sums.7 = (bf16[512,256]{1,0:T(8,128)(2,1)S(1)}, bf16[512,256]{1,0:T(8,128)(2,1)S(1)}) custom-call(bf16[256,4096]{1,0:T(8,128)(2,1)S(1)} %copy-done, bf16[256,4096]{1,0:T(8,128)(2,1)S(1)} %collective-permute-done.near_ref, bf16[272,512]{1,0:T(8,128)(2,1)S(1)} %get-tuple-element.31.v0_ref, bf16[272,512]{1,0:T(8,128)(2,1)S(1)} %collective-permute-done.1.v1_ref), custom_call_target="tpu_custom_call" | custom-call | tf_op jit(solution)/shard_map/partial_sums/pallas_call | solution.py:214
  6.7 2.7 %collective-permute-start.4 = (bf16[512,256]{1,0:T(8,128)(2,1)S(1)}, bf16[512,256]{1,0:T(8,128)(2,1)S(1)}, u32[]{:S(2)}, u32[]{:S(2)}) collective-permute-start(bf16[512,256]{1,0:T(8,128)(2,1)S(1)} %get-tuple-element.37), channel_id=1, source_target_pairs={{0,2},{1,3},{2,0},{3,1},{4,6},{5,7},{6,4},{7,5},{8,9},{9,8},{10,11... | collective-permute-start | bytes 786440 | tf_op jit(solution)/shard_map/ppermute | solution.py:180
  9.4 0.1 collective-permute-start.3
  9.5 0.5 %partial_sums.5 = (bf16[512,256]{1,0:T(8,128)(2,1)S(1)}, bf16[512,256]{1,0:T(8,128)(2,1)S(1)}) custom-call(bf16[256,4096]{1,0:T(8,128)(2,1)S(1)} %copy-done, bf16[256,4096]{1,0:T(8,128)(2,1)S(1)} %collective-permute-done.near_ref, bf16[272,512]{1,0:T(8,128)(2,1)S(1)} %get-tuple-element.31.v0_ref, bf16[272,512]{1,0:T(8,128)(2,1)S(1)} %collective-permute-done.1.v1_ref), custom_call_target="tpu_custom_call" | custom-call | tf_op jit(solution)/shard_map/partial_sums/pallas_call | solution.py:214
  10.0 2.0 %collective-permute-start.2 = (bf16[512,256]{1,0:T(8,128)(2,1)S(1)}, bf16[512,256]{1,0:T(8,128)(2,1)S(1)}, u32[]{:S(2)}, u32[]{:S(2)}) collective-permute-start(bf16[512,256]{1,0:T(8,128)(2,1)S(1)} %get-tuple-element.30), channel_id=1, source_target_pairs={{0,2},{1,3},{2,0},{3,1},{4,6},{5,7},{6,4},{7,5},{8,9},{9,8},{10,11... | collective-permute-start | bytes 786440 | tf_op jit(solution)/shard_map/ppermute | solution.py:180
  12.1 0.5 %partial_sums.6 = (f32[512,256]{1,0:T(8,128)S(1)}, f32[512,256]{1,0:T(8,128)S(1)}) custom-call(bf16[256,4096]{1,0:T(8,128)(2,1)S(1)} %copy-done, bf16[256,4096]{1,0:T(8,128)(2,1)S(1)} %collective-permute-done.near_ref, bf16[272,512]{1,0:T(8,128)(2,1)S(1)} %get-tuple-element.31.v0_ref, bf16[272,512]{1,0:T(8,128)(2,1)S(1)} %collective-permute-done.1.v1_ref), custom_call_target="tpu_custom_call" | custom-call | tf_op jit(solution)/shard_map/partial_sums/pallas_call | solution.py:214
  12.6 1.2 %collective-permute-done.4 = bf16[512,256]{1,0:T(8,128)(2,1)S(1)} collective-permute-done((bf16[512,256]{1,0:T(8,128)(2,1)S(1)}, bf16[512,256]{1,0:T(8,128)(2,1)S(1)}, u32[]{:S(2)}, u32[]{:S(2)}) %collective-permute-start.4) | collective-permute-done | bytes 262176 | tf_op jit(solution)/shard_map/ppermute | solution.py:180
  13.8 0.1 fusion.4
  13.9 2.1 %collective-permute-start.7 = (bf16[512,256]{1,0:T(8,128)(2,1)S(1)}, bf16[512,256]{1,0:T(8,128)(2,1)S(1)}, u32[]{:S(2)}, u32[]{:S(2)}) collective-permute-start(bf16[512,256]{1,0:T(8,128)(2,1)S(1)} %fusion.4), channel_id=1, source_target_pairs={{0,2},{1,3},{2,0},{3,1},{4,6},{5,7},{6,4},{7,5},{8,24},{9,25},{10,... | collective-permute-start | bytes 786440 | tf_op jit(solution)/shard_map/ppermute | solution.py:180
  16.0 0.6 %collective-permute-done.3 = bf16[512,256]{1,0:T(8,128)(2,1)S(1)} collective-permute-done((bf16[512,256]{1,0:T(8,128)(2,1)S(1)}, bf16[512,256]{1,0:T(8,128)(2,1)S(1)}, u32[]{:S(2)}, u32[]{:S(2)}) %collective-permute-start.3) | collective-permute-done | bytes 262176 | tf_op jit(solution)/shard_map/ppermute | solution.py:180
  16.6 0.1 select_convert_fusion
  16.7 0.7 %collective-permute-start.5 = (bf16[512,256]{1,0:T(8,128)(2,1)S(1)}, bf16[512,256]{1,0:T(8,128)(2,1)S(1)}, u32[]{:S(2)}, u32[]{:S(2)}) collective-permute-start(bf16[512,256]{1,0:T(8,128)(2,1)S(1)} %get-tuple-element.39), channel_id=1, source_target_pairs={{0,0},{1,1},{2,2},{3,3},{4,4},{5,5},{6,6},{7,7},{8,24},{9,25},{10,... | collective-permute-start | bytes 786440 | tf_op jit(solution)/shard_map/ppermute | solution.py:180
  17.4 2.0 %collective-permute-start.6 = (bf16[512,256]{1,0:T(8,128)(2,1)S(1)}, bf16[512,256]{1,0:T(8,128)(2,1)S(1)}, u32[]{:S(2)}, u32[]{:S(2)}) collective-permute-start(bf16[512,256]{1,0:T(8,128)(2,1)S(1)} %select_convert_fusion), channel_id=1, source_target_pairs={{0,16},{1,17},{2,18},{3,19},{4,20},{5,21},{6,22},{7,23},{8,9},{9,8... | collective-permute-start | bytes 786440 | tf_op jit(solution)/shard_map/ppermute | solution.py:180
  19.4 0.5 %partial_sums.4 = (f32[512,256]{1,0:T(8,128)S(1)}, f32[512,256]{1,0:T(8,128)S(1)}) custom-call(bf16[256,4096]{1,0:T(8,128)(2,1)S(1)} %copy-done, bf16[256,4096]{1,0:T(8,128)(2,1)S(1)} %collective-permute-done.near_ref, bf16[272,512]{1,0:T(8,128)(2,1)S(1)} %get-tuple-element.31.v0_ref, bf16[272,512]{1,0:T(8,128)(2,1)S(1)} %collective-permute-done.1.v1_ref), custom_call_target="tpu_custom_call" | custom-call | tf_op jit(solution)/shard_map/partial_sums/pallas_call | solution.py:214
  20.0 0.0 collective-permute-done.2
  20.0 0.3 inner_swap.1
  20.3 1.9 %collective-permute-done.7 = bf16[512,256]{1,0:T(8,128)(2,1)S(1)} collective-permute-done((bf16[512,256]{1,0:T(8,128)(2,1)S(1)}, bf16[512,256]{1,0:T(8,128)(2,1)S(1)}, u32[]{:S(2)}, u32[]{:S(2)}) %collective-permute-start.7) | collective-permute-done | bytes 262176 | tf_op jit(solution)/shard_map/ppermute | solution.py:180
  22.2 0.1 fusion.2
  22.3 2.2 %collective-permute-start.8 = (bf16[512,256]{1,0:T(8,128)(2,1)S(1)}, bf16[512,256]{1,0:T(8,128)(2,1)S(1)}, u32[]{:S(2)}, u32[]{:S(2)}) collective-permute-start(bf16[512,256]{1,0:T(8,128)(2,1)S(1)} %fusion.2), channel_id=1, source_target_pairs={{0,16},{1,17},{2,18},{3,19},{4,20},{5,21},{6,22},{7,23},{8,10},{9,... | collective-permute-start | bytes 786440 | tf_op jit(solution)/shard_map/ppermute | solution.py:180
  24.5 0.0 collective-permute-done.5
  24.6 0.8 %collective-permute-done.6 = bf16[512,256]{1,0:T(8,128)(2,1)S(1)} collective-permute-done((bf16[512,256]{1,0:T(8,128)(2,1)S(1)}, bf16[512,256]{1,0:T(8,128)(2,1)S(1)}, u32[]{:S(2)}, u32[]{:S(2)}) %collective-permute-start.6) | collective-permute-done | bytes 262176 | tf_op jit(solution)/shard_map/ppermute | solution.py:180
  25.4 0.1 convert_add_fusion
  25.5 1.4 %collective-permute-start.9 = (bf16[32,512]{1,0:T(8,128)(2,1)S(1)}, bf16[32,512]{1,0:T(8,128)(2,1)S(1)}, u32[]{:S(2)}, u32[]{:S(2)}) collective-permute-start(bf16[32,512]{1,0:T(8,128)(2,1)S(1)} %get-tuple-element.47), channel_id=1, source_target_pairs={{0,16},{1,17},{2,18},{3,19},{4,20},{5,21},{6,22},{7,23},{8,24},{9,... | collective-permute-start | bytes 98312 | tf_op jit(solution)/shard_map/ppermute | solution.py:180
  26.8 0.1 convert_add_fusion.3
  26.9 2.3 %collective-permute-done.8 = bf16[512,256]{1,0:T(8,128)(2,1)S(1)} collective-permute-done((bf16[512,256]{1,0:T(8,128)(2,1)S(1)}, bf16[512,256]{1,0:T(8,128)(2,1)S(1)}, u32[]{:S(2)}, u32[]{:S(2)}) %collective-permute-start.8) | collective-permute-done | bytes 262176 | tf_op jit(solution)/shard_map/ppermute | solution.py:180
  29.3 0.1 convert_add_fusion.2
  29.3 0.1 fusion.1
  29.5 0.1 collective-permute-done.9.window_ref
  29.6 1.9 %collective-permute-start.10 = (bf16[512,256]{1,0:T(8,128)(2,1)S(1)}, bf16[512,256]{1,0:T(8,128)(2,1)S(1)}, u32[]{:S(2)}, u32[]{:S(2)}) collective-permute-start(bf16[512,256]{1,0:T(8,128)(2,1)S(1)} %fusion.1), channel_id=1, source_target_pairs={{0,1},{1,0},{2,3},{3,2},{4,5},{5,4},{6,7},{7,6},{8,12},{9,13},{10,... | collective-permute-start | bytes 786440 | tf_op jit(solution)/shard_map/ppermute | solution.py:180
  31.5 4.5 %collective-permute-done.10 = bf16[512,256]{1,0:T(8,128)(2,1)S(1)} collective-permute-done((bf16[512,256]{1,0:T(8,128)(2,1)S(1)}, bf16[512,256]{1,0:T(8,128)(2,1)S(1)}, u32[]{:S(2)}, u32[]{:S(2)}) %collective-permute-start.10) | collective-permute-done | bytes 262176 | tf_op jit(solution)/shard_map/ppermute | solution.py:180
  36.0 0.1 convert_select_fusion
  36.0 0.8 %collective-permute-start.11 = (bf16[256,256]{1,0:T(8,128)(2,1)S(1)}, bf16[256,256]{1,0:T(8,128)(2,1)S(1)}, u32[]{:S(2)}, u32[]{:S(2)}) collective-permute-start(bf16[256,256]{1,0:T(8,128)(2,1)S(1)} %get-tuple-element.52), channel_id=1, source_target_pairs={{0,8},{1,9},{2,10},{3,11},{4,12},{5,13},{6,14},{7,15},{8,0},{9,1},... | collective-permute-start | bytes 393224 | tf_op jit(solution)/shard_map/ppermute | solution.py:180
  36.9 0.1 maximum_select_fusion
  36.9 0.9 %collective-permute-done.11 = bf16[256,256]{1,0:T(8,128)(2,1)S(1)} collective-permute-done((bf16[256,256]{1,0:T(8,128)(2,1)S(1)}, bf16[256,256]{1,0:T(8,128)(2,1)S(1)}, u32[]{:S(2)}, u32[]{:S(2)}) %collective-permute-start.11) | collective-permute-done | bytes 131104 | tf_op jit(solution)/shard_map/ppermute | solution.py:180
  37.9 1.4 %collective-permute-start.12 = (bf16[256,256]{1,0:T(8,128)(2,1)S(1)}, bf16[256,256]{1,0:T(8,128)(2,1)S(1)}, u32[]{:S(2)}, u32[]{:S(2)}) collective-permute-start(bf16[256,256]{1,0:T(8,128)(2,1)S(1)} %fusion.6), channel_id=1, source_target_pairs={{0,16},{1,17},{2,18},{3,19},{4,20},{5,21},{6,22},{7,23},{8,24},{9,... | collective-permute-start | bytes 393224 | tf_op jit(solution)/shard_map/ppermute | solution.py:180
  39.2 4.5 %collective-permute-done.12 = bf16[256,256]{1,0:T(8,128)(2,1)S(1)} collective-permute-done((bf16[256,256]{1,0:T(8,128)(2,1)S(1)}, bf16[256,256]{1,0:T(8,128)(2,1)S(1)}, u32[]{:S(2)}, u32[]{:S(2)}) %collective-permute-start.12) | collective-permute-done | bytes 131104 | tf_op jit(solution)/shard_map/ppermute | solution.py:180
  43.7 0.1 collective-permute-start.13
  43.8 0.9 %outer_swap.1 = bf16[256,512]{1,0:T(8,128)(2,1)} custom-call(bf16[272,512]{1,0:T(8,128)(2,1)S(1)} %get-tuple-element.31.v0_ref, bf16[256,512]{1,0:T(8,128)(2,1)S(1)} %get-tuple-element.49.rows_ref, bf16[32,512]{1,0:T(8,128)(2,1)S(1)} %collective-permute-done.9.window_ref), custom_call_target="tpu_custom_call" | custom-call | tf_op jit(solution)/shard_map/outer_swap/pallas_call | solution.py:278
  44.7 0.6 %collective-permute-done.13.near_ref = bf16[2,256,256]{2,1,0:T(8,128)(2,1)S(1)} collective-permute-done((bf16[2,256,256]{2,1,0:T(8,128)(2,1)S(1)}, bf16[2,256,256]{2,1,0:T(8,128)(2,1)S(1)}, u32[]{:S(2)}, u32[]{:S(2)}) %collective-permute-start.13) | collective-permute-done | bytes 262176 | tf_op jit(solution)/shard_map/ppermute | solution.py:180
  45.3 1.1 %place.1 = f32[512,512]{1,0:T(8,128)} custom-call(bf16[2,256,256]{2,1,0:T(8,128)(2,1)S(1)} %pad_maximum_fusion.pair_ref, bf16[2,256,256]{2,1,0:T(8,128)(2,1)S(1)} %collective-permute-done.13.near_ref), custom_call_target="tpu_custom_call" | custom-call | tf_op jit(solution)/shard_map/place/pallas_call | solution.py:299
  (6 shorter events, 0.2 us)
Async XLA Ops:
  0.6 5.6 %copy-start = (bf16[256,4096]{1,0:T(8,128)(2,1)S(1)}, bf16[256,4096]{1,0:T(8,128)(2,1)}, u32[]{:S(2)}) copy-start(bf16[256,4096]{1,0:T(8,128)(2,1)} %own_ref.7) | copy-start | bytes 6291460
  0.6 5.5 %collective-permute-start = (bf16[256,4096]{1,0:T(8,128)(2,1)}, bf16[256,4096]{1,0:T(8,128)(2,1)S(1)}, u32[]{:S(2)}, u32[]{:S(2)}) collective-permute-start(bf16[256,4096]{1,0:T(8,128)(2,1)} %own_ref.7), channel_id=1, source_target_pairs={{0,8},{1,9},{2,10},{3,11},{4,12},{5,13},{6,14},{7,15},{8,0},{9,1},... | collective-permute-start | bytes 6291464 | tf_op jit(solution)/shard_map/ppermute | solution.py:180
  4.6 1.6 %collective-permute-start.1 = (bf16[272,512]{1,0:T(8,128)(2,1)S(1)}, bf16[272,512]{1,0:T(8,128)(2,1)S(1)}, u32[]{:S(2)}, u32[]{:S(2)}) collective-permute-start(bf16[272,512]{1,0:T(8,128)(2,1)S(1)} %get-tuple-element.31.v0_ref), channel_id=1, source_target_pairs={{0,8},{1,9},{2,10},{3,11},{4,12},{5,13},{6,14},{7,15},{8,0},{9,1},... | collective-permute-start | bytes 835592 | tf_op jit(solution)/shard_map/ppermute | solution.py:180
  6.7 7.0 %collective-permute-start.4 = (bf16[512,256]{1,0:T(8,128)(2,1)S(1)}, bf16[512,256]{1,0:T(8,128)(2,1)S(1)}, u32[]{:S(2)}, u32[]{:S(2)}) collective-permute-start(bf16[512,256]{1,0:T(8,128)(2,1)S(1)} %get-tuple-element.37), channel_id=1, source_target_pairs={{0,2},{1,3},{2,0},{3,1},{4,6},{5,7},{6,4},{7,5},{8,9},{9,8},{10,11... | collective-permute-start | bytes 786440 | tf_op jit(solution)/shard_map/ppermute | solution.py:180
  9.4 7.2 %collective-permute-start.3 = (bf16[512,256]{1,0:T(8,128)(2,1)S(1)}, bf16[512,256]{1,0:T(8,128)(2,1)S(1)}, u32[]{:S(2)}, u32[]{:S(2)}) collective-permute-start(bf16[512,256]{1,0:T(8,128)(2,1)S(1)} %get-tuple-element.35), channel_id=1, source_target_pairs={{0,2},{1,3},{2,0},{3,1},{4,6},{5,7},{6,4},{7,5},{8,24},{9,25},{10,... | collective-permute-start | bytes 786440 | tf_op jit(solution)/shard_map/ppermute | solution.py:180
  10.0 9.9 %collective-permute-start.2 = (bf16[512,256]{1,0:T(8,128)(2,1)S(1)}, bf16[512,256]{1,0:T(8,128)(2,1)S(1)}, u32[]{:S(2)}, u32[]{:S(2)}) collective-permute-start(bf16[512,256]{1,0:T(8,128)(2,1)S(1)} %get-tuple-element.30), channel_id=1, source_target_pairs={{0,2},{1,3},{2,0},{3,1},{4,6},{5,7},{6,4},{7,5},{8,9},{9,8},{10,11... | collective-permute-start | bytes 786440 | tf_op jit(solution)/shard_map/ppermute | solution.py:180
  13.9 8.3 %collective-permute-start.7 = (bf16[512,256]{1,0:T(8,128)(2,1)S(1)}, bf16[512,256]{1,0:T(8,128)(2,1)S(1)}, u32[]{:S(2)}, u32[]{:S(2)}) collective-permute-start(bf16[512,256]{1,0:T(8,128)(2,1)S(1)} %fusion.4), channel_id=1, source_target_pairs={{0,2},{1,3},{2,0},{3,1},{4,6},{5,7},{6,4},{7,5},{8,24},{9,25},{10,... | collective-permute-start | bytes 786440 | tf_op jit(solution)/shard_map/ppermute | solution.py:180
  16.7 7.9 %collective-permute-start.5 = (bf16[512,256]{1,0:T(8,128)(2,1)S(1)}, bf16[512,256]{1,0:T(8,128)(2,1)S(1)}, u32[]{:S(2)}, u32[]{:S(2)}) collective-permute-start(bf16[512,256]{1,0:T(8,128)(2,1)S(1)} %get-tuple-element.39), channel_id=1, source_target_pairs={{0,0},{1,1},{2,2},{3,3},{4,4},{5,5},{6,6},{7,7},{8,24},{9,25},{10,... | collective-permute-start | bytes 786440 | tf_op jit(solution)/shard_map/ppermute | solution.py:180
  17.4 8.0 %collective-permute-start.6 = (bf16[512,256]{1,0:T(8,128)(2,1)S(1)}, bf16[512,256]{1,0:T(8,128)(2,1)S(1)}, u32[]{:S(2)}, u32[]{:S(2)}) collective-permute-start(bf16[512,256]{1,0:T(8,128)(2,1)S(1)} %select_convert_fusion), channel_id=1, source_target_pairs={{0,16},{1,17},{2,18},{3,19},{4,20},{5,21},{6,22},{7,23},{8,9},{9,8... | collective-permute-start | bytes 786440 | tf_op jit(solution)/shard_map/ppermute | solution.py:180
  22.3 6.9 %collective-permute-start.8 = (bf16[512,256]{1,0:T(8,128)(2,1)S(1)}, bf16[512,256]{1,0:T(8,128)(2,1)S(1)}, u32[]{:S(2)}, u32[]{:S(2)}) collective-permute-start(bf16[512,256]{1,0:T(8,128)(2,1)S(1)} %fusion.2), channel_id=1, source_target_pairs={{0,16},{1,17},{2,18},{3,19},{4,20},{5,21},{6,22},{7,23},{8,10},{9,... | collective-permute-start | bytes 786440 | tf_op jit(solution)/shard_map/ppermute | solution.py:180
  25.5 4.1 %collective-permute-start.9 = (bf16[32,512]{1,0:T(8,128)(2,1)S(1)}, bf16[32,512]{1,0:T(8,128)(2,1)S(1)}, u32[]{:S(2)}, u32[]{:S(2)}) collective-permute-start(bf16[32,512]{1,0:T(8,128)(2,1)S(1)} %get-tuple-element.47), channel_id=1, source_target_pairs={{0,16},{1,17},{2,18},{3,19},{4,20},{5,21},{6,22},{7,23},{8,24},{9,... | collective-permute-start | bytes 98312 | tf_op jit(solution)/shard_map/ppermute | solution.py:180
  29.6 6.4 %collective-permute-start.10 = (bf16[512,256]{1,0:T(8,128)(2,1)S(1)}, bf16[512,256]{1,0:T(8,128)(2,1)S(1)}, u32[]{:S(2)}, u32[]{:S(2)}) collective-permute-start(bf16[512,256]{1,0:T(8,128)(2,1)S(1)} %fusion.1), channel_id=1, source_target_pairs={{0,1},{1,0},{2,3},{3,2},{4,5},{5,4},{6,7},{7,6},{8,12},{9,13},{10,... | collective-permute-start | bytes 786440 | tf_op jit(solution)/shard_map/ppermute | solution.py:180
  36.0 1.8 %collective-permute-start.11 = (bf16[256,256]{1,0:T(8,128)(2,1)S(1)}, bf16[256,256]{1,0:T(8,128)(2,1)S(1)}, u32[]{:S(2)}, u32[]{:S(2)}) collective-permute-start(bf16[256,256]{1,0:T(8,128)(2,1)S(1)} %get-tuple-element.52), channel_id=1, source_target_pairs={{0,8},{1,9},{2,10},{3,11},{4,12},{5,13},{6,14},{7,15},{8,0},{9,1},... | collective-permute-start | bytes 393224 | tf_op jit(solution)/shard_map/ppermute | solution.py:180
  37.9 5.8 %collective-permute-start.12 = (bf16[256,256]{1,0:T(8,128)(2,1)S(1)}, bf16[256,256]{1,0:T(8,128)(2,1)S(1)}, u32[]{:S(2)}, u32[]{:S(2)}) collective-permute-start(bf16[256,256]{1,0:T(8,128)(2,1)S(1)} %fusion.6), channel_id=1, source_target_pairs={{0,16},{1,17},{2,18},{3,19},{4,20},{5,21},{6,22},{7,23},{8,24},{9,... | collective-permute-start | bytes 393224 | tf_op jit(solution)/shard_map/ppermute | solution.py:180
  43.7 1.6 %collective-permute-start.13 = (bf16[2,256,256]{2,1,0:T(8,128)(2,1)S(1)}, bf16[2,256,256]{2,1,0:T(8,128)(2,1)S(1)}, u32[]{:S(2)}, u32[]{:S(2)}) collective-permute-start(bf16[2,256,256]{2,1,0:T(8,128)(2,1)S(1)} %pad_maximum_fusion.pair_ref), channel_id=1, source_target_pairs={{0,8},{1,9},{2,10},{3,11},{4,12},{5,13},{6,14},{7,15},{8,0},{9,1},... | collective-permute-start | bytes 786440 | tf_op jit(solution)/shard_map/ppermute | solution.py:180

commit v12 on v11

--- a/solution.py
+++ b/solution.py
@@ -307,6 +307,22 @@
     )(pair, near)
 
 
+def fold_kernel(base_ref, arrived_ref, out_ref):
+    out_ref[...] = base_ref[...] + arrived_ref[...].astype(F32)
+
+
+def fold(base, arrived):
+    return pl.pallas_call(
+        fold_kernel,
+        in_specs=[VMEM] * 2,
+        out_specs=VMEM,
+        out_shape=jax.ShapeDtypeStruct(base.shape, F32),
+        compiler_params=pltpu.CompilerParams(vmem_limit_bytes=8 * MIB),
+        cost_estimate=pl.CostEstimate(flops=8_000_000_000, bytes_accessed=0, transcendentals=0),
+        name="fold",
+    )(base, arrived)
+
+
 def reduce_by_axis(layer_input, *args):
     near = xor_permute(layer_input, CORE)
     v0, odd = front(*args)
@@ -335,42 +351,39 @@
     def parts(*pairs):
         return [tuple(zip(*pair)) for pair in pairs]
 
-    first, second = sums(parts((chain(3, 1, 1), own(1, 1, 0)), (chain(2, 1, 1), own(1, 0, 0))), BF16)
-    third, fourth = sums(parts((chain(3, 0, 1), own(1, 1, 1)), (chain(2, 1, 0), own(1, 0, 1))), BF16)
-    keep1, keep2 = sums(parts((chain(3, 1, 0), own(0, 1, 0)), (chain(2, 0, 1), own(0, 0, 0))), F32)
-    keep3, keep4 = sums(parts((chain(3, 0, 0), own(0, 1, 1)), (chain(2, 0, 0), own(0, 0, 1))), F32)
-    side = fourth
+    first, second = sums(parts((chain(3, 1, 1), own(1, 1, 0)), (chain(2, 1, 1), own(1, 1, 1))), BF16)
+    third, spare = sums(parts((chain(3, 0, 1), own(1, 0, 0)), (chain(2, 1, 0), own(1, 0, 1))), BF16)
+    keep1, keep2 = sums(parts((chain(3, 1, 0), own(0, 1, 0)), (chain(2, 0, 1), own(0, 1, 1))), F32)
+    keep3, keep4 = sums(parts((chain(3, 0, 0), own(0, 0, 0)), (chain(2, 0, 0), own(0, 0, 1))), F32)
     first = routed(first, X, Z1)
     second = routed(second, Y, Z1)
     third = routed(third, X, Z1)
     total1 = add(keep1, first)
-    fourth = jnp.where(odd, total1.astype(BF16), fourth)
+    fourth = jnp.where(odd, total1.astype(BF16), spare)
     second = after_all(second, fourth)[0]
     fourth = routed(fourth, Y, Z1)
     total2 = add(keep2, second)
-    fifth = jnp.where(odd, total2, total1).astype(BF16)
-    rows, window = inner_swap(after_all(v0, third)[0], v1)
-    fifth_sent = fifth
-    side = after_all(side, fifth)[0]
-    fifth = routed(fifth, X, Y)
-    side = routed(side, Y, 0)
-    third, fourth = after_all(third, fourth, fifth_sent)[:2]
+    fifth = jnp.where(odd, spare, total2.astype(BF16))
+    sixth = jnp.where(odd, total2, total1).astype(BF16)
+    rows, window = inner_swap(after_all(v0, spare)[0], v1)
+    third, fourth, window = after_all(third, fourth, window, fifth, sixth)[:3]
+    fifth = routed(fifth, Y, Y)
+    sixth = routed(sixth, X, Y)
     total3 = add(keep3, third)
-    sixth = jnp.where(odd, add(total3, fourth), total3).astype(BF16)
-    window, side, fifth = after_all(window, side, fifth, sixth)[:3]
-    window = xor_permute(window, Y)
-    sixth = routed(sixth, Z1, Y)
-    some = add(total2, fifth)
-    rest = add(keep4, jnp.where(odd, side, fourth))
-    rest, sixth = after_all(rest, sixth)
-    rest = add(rest, sixth)
-    last = jnp.where(odd, add(rest, fifth), jnp.concatenate([some[:both], rest[:both]])).astype(BF16)
-    last, window = after_all(last, window)
-    last = routed(last, Z2, X)
-    base = jnp.concatenate([add(some[both:], last[:both]), add(rest[both:], last[both:])])
-    mine = jnp.where(odd, last.astype(F32), base)
-    crossed = xor_permute(jnp.where(odd, last[:both], base[both:].astype(BF16)), CORE)
-    mine = add(jnp.where(odd, mine[both:], mine[:both]), crossed).astype(BF16)
+    joined = add(total3, fourth).astype(BF16)
+    fourth, fifth, sixth = after_all(fourth, fifth, sixth, joined)[:3]
+    joined = routed(joined, Z1, 0)
+    rest = add(keep4, fifth)
+    some = add(total3, sixth)
+    rest = jnp.where(odd, add(rest, sixth, joined), add(rest, fourth))
+    last1 = rest[:both].astype(BF16)
+    last2 = jnp.where(odd, rest[both:], some[:both]).astype(BF16)
+    window = xor_permute(after_all(window, last1, last2)[0], Y)
+    last1 = routed(last1, Z2, X)
+    last2 = routed(last2, Z2, X)
+    last1, window = after_all(last1, window)
+    crossed = xor_permute(jnp.where(odd, last1, add(rest[both:], last1).astype(BF16)), CORE)
+    mine = add(fold(jnp.where(odd, 0.0, some[both:]), last2), crossed).astype(BF16)
     from_y = xor_permute(mine, Y)
     value_grad = outer_swap(v0, rows, after_all(window, from_y)[0])
     pair = jnp.stack([mine, from_y])

time: 46.6 us -> 44.6 us (0.957)
  starting transfers between devices: 17.9 us -> 15.7 us
    ppermute x14 -> x15, starting transfers between devices: 17.9 us -> 15.7 us  [routed(): lax.ppermute(value, ('dp', 'fsdp'), [(i, i ^ (odd if i // owners % 2 else...]
    ppermute x14 -> x15, waiting for transfers between devices: 18.9 us -> 19.2 us  [routed(): lax.ppermute(value, ('dp', 'fsdp'), [(i, i ^ (odd if i // owners % 2 else...]
  transfers between devices with their start and end apart: 14 -> 15, of which waited for: 11 -> 12; matrix products, arithmetic and copies ran while one was open for 2% -> 1% of each run, Pallas kernels for 12% -> 12%
where the time goes in v12:
time: 44.6 us; the launch traced here: 44.4 us
  waiting for transfers between devices  19.2 us (43%)
  starting transfers between devices  15.7 us (35%)
  Pallas kernels  7.14 us (16%)
  between operations  1.52 us (3%)
  other arithmetic  0.83 us (2%)
    ppermute x15, waiting for transfers between devices, routed(): lax.ppermute(value, ('dp', 'fsdp'), [(i, i ^ (odd if i // owners % 2 else...  19.2 us
    ppermute x15, starting transfers between devices, routed(): lax.ppermute(value, ('dp', 'fsdp'), [(i, i ^ (odd if i // owners % 2 else...  15.7 us
    pallas_call x1, Pallas kernels, front(): pl.pallas_call(functools.partial(front_kernel, per_group), in_specs=[HBM]...  2.64 us
    pallas_call x4, Pallas kernels, partial_sums(): pl.pallas_call(functools.partial(partial_kernel, parts), in_specs=[VMEM]...  2.18 us
    pallas_call x1, Pallas kernels, place(): pl.pallas_call(place_kernel, in_specs=[VMEM] * 2, out_specs=VMEM, out_sha...  1.05 us
    pallas_call x1, Pallas kernels, outer_swap(): pl.pallas_call(outer_swap_kernel, in_specs=[VMEM] * 3, out_specs=VMEM, ou...  0.91 us
  transfers between devices with their start and end apart: 15, of which 12 were waited for; matrix products, arithmetic and copies ran while one was open for 1% of the time, Pallas kernels for 12%

profile of v12, /device:TPU:0, one launch (start us, length us, event | category | flops | bytes accessed | tf_op | source)
XLA Modules:
  0.0 44.4 jit_solution(15638435678783972663)
XLA Ops:
  0.6 0.0 copy-start
  0.6 0.5 %collective-permute-start = (bf16[256,4096]{1,0:T(8,128)(2,1)}, bf16[256,4096]{1,0:T(8,128)(2,1)S(1)}, u32[]{:S(2)}, u32[]{:S(2)}) collective-permute-start(bf16[256,4096]{1,0:T(8,128)(2,1)} %own_ref.7), channel_id=1, source_target_pairs={{0,8},{1,9},{2,10},{3,11},{4,12},{5,13},{6,14},{7,15},{8,0},{9,1},... | collective-permute-start | bytes 6291464 | tf_op jit(solution)/shard_map/ppermute | solution.py:180
  1.9 2.6 %front.1 = (bf16[272,512]{1,0:T(8,128)(2,1)S(1)}, f32[8,256]{1,0:T(8,128)S(1)}) custom-call(f32[16]{0:T(128)} %loss_hbm.1, s32[1]{0:T(128)S(6)} %copy.12.exponent_hbm, s32[1,2]{1,0:T(1,128)} %start_hbm.1, s32[1,2]{1,0:T(1,128)} %rows_hbm.1, bf16[256,2048]{1,0:T(8,128)(2,1)} %q_hbm.1, bf16[256,512]{1,0:T(8,128)(2,1)} %k_hbm.1, bf16[256,2048]{1,0:T(8,128)(2,1)} %g_hbm.1, ...), custom_call_target="tpu_custom_call" | custom-call | tf_op jit(solution)/shard_map/front/pallas_call | solution.py:154
  4.6 0.1 collective-permute-start.1
  4.7 1.5 %collective-permute-done.1.v1_ref = bf16[272,512]{1,0:T(8,128)(2,1)S(1)} collective-permute-done((bf16[272,512]{1,0:T(8,128)(2,1)S(1)}, bf16[272,512]{1,0:T(8,128)(2,1)S(1)}, u32[]{:S(2)}, u32[]{:S(2)}) %collective-permute-start.1) | collective-permute-done | bytes 278560 | tf_op jit(solution)/shard_map/ppermute | solution.py:180
  6.2 0.0 collective-permute-done.near_ref
  6.2 0.0 copy-done
  6.2 0.6 %partial_sums.7 = (bf16[512,256]{1,0:T(8,128)(2,1)S(1)}, bf16[512,256]{1,0:T(8,128)(2,1)S(1)}) custom-call(bf16[256,4096]{1,0:T(8,128)(2,1)S(1)} %copy-done, bf16[256,4096]{1,0:T(8,128)(2,1)S(1)} %collective-permute-done.near_ref, bf16[272,512]{1,0:T(8,128)(2,1)S(1)} %get-tuple-element.33.v0_ref, bf16[272,512]{1,0:T(8,128)(2,1)S(1)} %collective-permute-done.1.v1_ref), custom_call_target="tpu_custom_call" | custom-call | tf_op jit(solution)/shard_map/partial_sums/pallas_call | solution.py:214
  6.8 2.7 %collective-permute-start.3 = (bf16[512,256]{1,0:T(8,128)(2,1)S(1)}, bf16[512,256]{1,0:T(8,128)(2,1)S(1)}, u32[]{:S(2)}, u32[]{:S(2)}) collective-permute-start(bf16[512,256]{1,0:T(8,128)(2,1)S(1)} %get-tuple-element.31), channel_id=1, source_target_pairs={{0,2},{1,3},{2,0},{3,1},{4,6},{5,7},{6,4},{7,5},{8,9},{9,8},{10,11... | collective-permute-start | bytes 786440 | tf_op jit(solution)/shard_map/ppermute | solution.py:180
  9.4 0.1 collective-permute-start.5
  9.5 0.5 %partial_sums.5 = (bf16[512,256]{1,0:T(8,128)(2,1)S(1)}, bf16[512,256]{1,0:T(8,128)(2,1)S(1)}) custom-call(bf16[256,4096]{1,0:T(8,128)(2,1)S(1)} %copy-done, bf16[256,4096]{1,0:T(8,128)(2,1)S(1)} %collective-permute-done.near_ref, bf16[272,512]{1,0:T(8,128)(2,1)S(1)} %get-tuple-element.33.v0_ref, bf16[272,512]{1,0:T(8,128)(2,1)S(1)} %collective-permute-done.1.v1_ref), custom_call_target="tpu_custom_call" | custom-call | tf_op jit(solution)/shard_map/partial_sums/pallas_call | solution.py:214
  10.1 2.0 %collective-permute-start.2 = (bf16[512,256]{1,0:T(8,128)(2,1)S(1)}, bf16[512,256]{1,0:T(8,128)(2,1)S(1)}, u32[]{:S(2)}, u32[]{:S(2)}) collective-permute-start(bf16[512,256]{1,0:T(8,128)(2,1)S(1)} %get-tuple-element.29), channel_id=1, source_target_pairs={{0,2},{1,3},{2,0},{3,1},{4,6},{5,7},{6,4},{7,5},{8,9},{9,8},{10,11... | collective-permute-start | bytes 786440 | tf_op jit(solution)/shard_map/ppermute | solution.py:180
  12.1 0.5 %partial_sums.6 = (f32[512,256]{1,0:T(8,128)S(1)}, f32[512,256]{1,0:T(8,128)S(1)}) custom-call(bf16[256,4096]{1,0:T(8,128)(2,1)S(1)} %copy-done, bf16[256,4096]{1,0:T(8,128)(2,1)S(1)} %collective-permute-done.near_ref, bf16[272,512]{1,0:T(8,128)(2,1)S(1)} %get-tuple-element.33.v0_ref, bf16[272,512]{1,0:T(8,128)(2,1)S(1)} %collective-permute-done.1.v1_ref), custom_call_target="tpu_custom_call" | custom-call | tf_op jit(solution)/shard_map/partial_sums/pallas_call | solution.py:214
  12.6 0.5 %partial_sums.4 = (f32[512,256]{1,0:T(8,128)S(1)}, f32[512,256]{1,0:T(8,128)S(1)}) custom-call(bf16[256,4096]{1,0:T(8,128)(2,1)S(1)} %copy-done, bf16[256,4096]{1,0:T(8,128)(2,1)S(1)} %collective-permute-done.near_ref, bf16[272,512]{1,0:T(8,128)(2,1)S(1)} %get-tuple-element.33.v0_ref, bf16[272,512]{1,0:T(8,128)(2,1)S(1)} %collective-permute-done.1.v1_ref), custom_call_target="tpu_custom_call" | custom-call | tf_op jit(solution)/shard_map/partial_sums/pallas_call | solution.py:214
  13.2 0.3 inner_swap.1
  13.5 0.3 collective-permute-done.3
  13.8 0.1 fusion.5
  13.9 2.1 %collective-permute-start.4 = (bf16[512,256]{1,0:T(8,128)(2,1)S(1)}, bf16[512,256]{1,0:T(8,128)(2,1)S(1)}, u32[]{:S(2)}, u32[]{:S(2)}) collective-permute-start(bf16[512,256]{1,0:T(8,128)(2,1)S(1)} %fusion.5), channel_id=1, source_target_pairs={{0,2},{1,3},{2,0},{3,1},{4,6},{5,7},{6,4},{7,5},{8,24},{9,25},{10,... | collective-permute-start | bytes 786440 | tf_op jit(solution)/shard_map/ppermute | solution.py:180
  16.0 0.6 %collective-permute-done.5 = bf16[512,256]{1,0:T(8,128)(2,1)S(1)} collective-permute-done((bf16[512,256]{1,0:T(8,128)(2,1)S(1)}, bf16[512,256]{1,0:T(8,128)(2,1)S(1)}, u32[]{:S(2)}, u32[]{:S(2)}) %collective-permute-start.5) | collective-permute-done | bytes 262176 | tf_op jit(solution)/shard_map/ppermute | solution.py:180
  16.6 0.1 select_convert_fusion
  16.7 2.0 %collective-permute-start.7 = (bf16[512,256]{1,0:T(8,128)(2,1)S(1)}, bf16[512,256]{1,0:T(8,128)(2,1)S(1)}, u32[]{:S(2)}, u32[]{:S(2)}) collective-permute-start(bf16[512,256]{1,0:T(8,128)(2,1)S(1)} %select_convert_fusion), channel_id=1, source_target_pairs={{0,16},{1,17},{2,18},{3,19},{4,20},{5,21},{6,22},{7,23},{8,9},{9,8... | collective-permute-start | bytes 786440 | tf_op jit(solution)/shard_map/ppermute | solution.py:180
  18.7 0.1 fusion.4
  18.8 0.1 collective-permute-start.6
  19.0 0.4 collective-permute-done.2
  19.4 2.8 %collective-permute-done.4 = bf16[512,256]{1,0:T(8,128)(2,1)S(1)} collective-permute-done((bf16[512,256]{1,0:T(8,128)(2,1)S(1)}, bf16[512,256]{1,0:T(8,128)(2,1)S(1)}, u32[]{:S(2)}, u32[]{:S(2)}) %collective-permute-start.4) | collective-permute-done | bytes 262176 | tf_op jit(solution)/shard_map/ppermute | solution.py:180
  22.2 0.1 add_convert_fusion
  22.3 0.7 %collective-permute-start.8 = (bf16[512,256]{1,0:T(8,128)(2,1)S(1)}, bf16[512,256]{1,0:T(8,128)(2,1)S(1)}, u32[]{:S(2)}, u32[]{:S(2)}) collective-permute-start(bf16[512,256]{1,0:T(8,128)(2,1)S(1)} %add_convert_fusion), channel_id=1, source_target_pairs={{0,0},{1,1},{2,2},{3,3},{4,4},{5,5},{6,6},{7,7},{8,10},{9,11},{10,... | collective-permute-start | bytes 786440 | tf_op jit(solution)/shard_map/ppermute | solution.py:180
  23.0 1.9 %collective-permute-done.7 = bf16[512,256]{1,0:T(8,128)(2,1)S(1)} collective-permute-done((bf16[512,256]{1,0:T(8,128)(2,1)S(1)}, bf16[512,256]{1,0:T(8,128)(2,1)S(1)}, u32[]{:S(2)}, u32[]{:S(2)}) %collective-permute-start.7) | collective-permute-done | bytes 262176 | tf_op jit(solution)/shard_map/ppermute | solution.py:180
  24.9 2.8 %collective-permute-done.6 = bf16[512,256]{1,0:T(8,128)(2,1)S(1)} collective-permute-done((bf16[512,256]{1,0:T(8,128)(2,1)S(1)}, bf16[512,256]{1,0:T(8,128)(2,1)S(1)}, u32[]{:S(2)}, u32[]{:S(2)}) %collective-permute-start.6) | collective-permute-done | bytes 262176 | tf_op jit(solution)/shard_map/ppermute | solution.py:180
  27.7 0.0 collective-permute-done.8
  27.7 0.2 fusion.1
  28.0 1.6 %collective-permute-start.10 = (bf16[256,256]{1,0:T(8,128)(2,1)S(1)}, bf16[256,256]{1,0:T(8,128)(2,1)S(1)}, u32[]{:S(2)}, u32[]{:S(2)}) collective-permute-start(bf16[256,256]{1,0:T(8,128)(2,1)S(1)} %get-tuple-element.50), channel_id=1, source_target_pairs={{0,1},{1,0},{2,3},{3,2},{4,5},{5,4},{6,7},{7,6},{8,12},{9,13},{10,... | collective-permute-start | bytes 393224 | tf_op jit(solution)/shard_map/ppermute | solution.py:180
  29.6 0.5 %collective-permute-start.9 = (bf16[256,256]{1,0:T(8,128)(2,1)S(1)}, bf16[256,256]{1,0:T(8,128)(2,1)S(1)}, u32[]{:S(2)}, u32[]{:S(2)}) collective-permute-start(bf16[256,256]{1,0:T(8,128)(2,1)S(1)} %get-tuple-element.51), channel_id=1, source_target_pairs={{0,1},{1,0},{2,3},{3,2},{4,5},{5,4},{6,7},{7,6},{8,12},{9,13},{10,... | collective-permute-start | bytes 393224 | tf_op jit(solution)/shard_map/ppermute | solution.py:180
  30.1 1.5 %collective-permute-start.11 = (bf16[32,512]{1,0:T(8,128)(2,1)S(1)}, bf16[32,512]{1,0:T(8,128)(2,1)S(1)}, u32[]{:S(2)}, u32[]{:S(2)}) collective-permute-start(bf16[32,512]{1,0:T(8,128)(2,1)S(1)} %get-tuple-element.45), channel_id=1, source_target_pairs={{0,16},{1,17},{2,18},{3,19},{4,20},{5,21},{6,22},{7,23},{8,24},{9,... | collective-permute-start | bytes 98312 | tf_op jit(solution)/shard_map/ppermute | solution.py:180
  31.7 2.4 %collective-permute-done.11.window_ref = bf16[32,512]{1,0:T(8,128)(2,1)S(1)} collective-permute-done((bf16[32,512]{1,0:T(8,128)(2,1)S(1)}, bf16[32,512]{1,0:T(8,128)(2,1)S(1)}, u32[]{:S(2)}, u32[]{:S(2)}) %collective-permute-start.11) | collective-permute-done | bytes 32800 | tf_op jit(solution)/shard_map/ppermute | solution.py:180
  34.0 0.0 collective-permute-done.10
  34.1 0.1 collective-permute-start.12
  34.2 0.4 collective-permute-done.9.arrived_ref
  34.6 0.9 %collective-permute-done.12 = bf16[256,256]{1,0:T(8,128)(2,1)S(1)} collective-permute-done((bf16[256,256]{1,0:T(8,128)(2,1)S(1)}, bf16[256,256]{1,0:T(8,128)(2,1)S(1)}, u32[]{:S(2)}, u32[]{:S(2)}) %collective-permute-start.12) | collective-permute-done | bytes 131104 | tf_op jit(solution)/shard_map/ppermute | solution.py:180
  35.5 1.6 %collective-permute-start.13 = (bf16[256,256]{1,0:T(8,128)(2,1)S(1)}, bf16[256,256]{1,0:T(8,128)(2,1)S(1)}, u32[]{:S(2)}, u32[]{:S(2)}) collective-permute-start(bf16[256,256]{1,0:T(8,128)(2,1)S(1)} %add_convert_fusion.1), channel_id=1, source_target_pairs={{0,16},{1,17},{2,18},{3,19},{4,20},{5,21},{6,22},{7,23},{8,24},{9,... | collective-permute-start | bytes 393224 | tf_op jit(solution)/shard_map/ppermute | solution.py:180
  37.1 4.6 %collective-permute-done.13 = bf16[256,256]{1,0:T(8,128)(2,1)S(1)} collective-permute-done((bf16[256,256]{1,0:T(8,128)(2,1)S(1)}, bf16[256,256]{1,0:T(8,128)(2,1)S(1)}, u32[]{:S(2)}, u32[]{:S(2)}) %collective-permute-start.13) | collective-permute-done | bytes 131104 | tf_op jit(solution)/shard_map/ppermute | solution.py:180
  41.7 0.1 collective-permute-start.14
  41.8 0.9 %outer_swap.1 = bf16[256,512]{1,0:T(8,128)(2,1)} custom-call(bf16[272,512]{1,0:T(8,128)(2,1)S(1)} %get-tuple-element.33.v0_ref, bf16[256,512]{1,0:T(8,128)(2,1)S(1)} %get-tuple-element.47.rows_ref, bf16[32,512]{1,0:T(8,128)(2,1)S(1)} %collective-permute-done.11.window_ref), custom_call_target="tpu_custom_call" | custom-call | tf_op jit(solution)/shard_map/outer_swap/pallas_call | solution.py:278
  42.7 0.6 %collective-permute-done.14.near_ref = bf16[2,256,256]{2,1,0:T(8,128)(2,1)S(1)} collective-permute-done((bf16[2,256,256]{2,1,0:T(8,128)(2,1)S(1)}, bf16[2,256,256]{2,1,0:T(8,128)(2,1)S(1)}, u32[]{:S(2)}, u32[]{:S(2)}) %collective-permute-start.14) | collective-permute-done | bytes 262176 | tf_op jit(solution)/shard_map/ppermute | solution.py:180
  43.3 1.1 %place.1 = f32[512,512]{1,0:T(8,128)} custom-call(bf16[2,256,256]{2,1,0:T(8,128)(2,1)S(1)} %pad_maximum_fusion.pair_ref, bf16[2,256,256]{2,1,0:T(8,128)(2,1)S(1)} %collective-permute-done.14.near_ref), custom_call_target="tpu_custom_call" | custom-call | tf_op jit(solution)/shard_map/place/pallas_call | solution.py:299
  (7 shorter events, 0.2 us)
Async XLA Ops:
  0.6 5.6 %copy-start = (bf16[256,4096]{1,0:T(8,128)(2,1)S(1)}, bf16[256,4096]{1,0:T(8,128)(2,1)}, u32[]{:S(2)}) copy-start(bf16[256,4096]{1,0:T(8,128)(2,1)} %own_ref.7) | copy-start | bytes 6291460
  0.6 5.5 %collective-permute-start = (bf16[256,4096]{1,0:T(8,128)(2,1)}, bf16[256,4096]{1,0:T(8,128)(2,1)S(1)}, u32[]{:S(2)}, u32[]{:S(2)}) collective-permute-start(bf16[256,4096]{1,0:T(8,128)(2,1)} %own_ref.7), channel_id=1, source_target_pairs={{0,8},{1,9},{2,10},{3,11},{4,12},{5,13},{6,14},{7,15},{8,0},{9,1},... | collective-permute-start | bytes 6291464 | tf_op jit(solution)/shard_map/ppermute | solution.py:180
  4.6 1.6 %collective-permute-start.1 = (bf16[272,512]{1,0:T(8,128)(2,1)S(1)}, bf16[272,512]{1,0:T(8,128)(2,1)S(1)}, u32[]{:S(2)}, u32[]{:S(2)}) collective-permute-start(bf16[272,512]{1,0:T(8,128)(2,1)S(1)} %get-tuple-element.33.v0_ref), channel_id=1, source_target_pairs={{0,8},{1,9},{2,10},{3,11},{4,12},{5,13},{6,14},{7,15},{8,0},{9,1},... | collective-permute-start | bytes 835592 | tf_op jit(solution)/shard_map/ppermute | solution.py:180
  6.8 7.0 %collective-permute-start.3 = (bf16[512,256]{1,0:T(8,128)(2,1)S(1)}, bf16[512,256]{1,0:T(8,128)(2,1)S(1)}, u32[]{:S(2)}, u32[]{:S(2)}) collective-permute-start(bf16[512,256]{1,0:T(8,128)(2,1)S(1)} %get-tuple-element.31), channel_id=1, source_target_pairs={{0,2},{1,3},{2,0},{3,1},{4,6},{5,7},{6,4},{7,5},{8,9},{9,8},{10,11... | collective-permute-start | bytes 786440 | tf_op jit(solution)/shard_map/ppermute | solution.py:180
  9.4 7.2 %collective-permute-start.5 = (bf16[512,256]{1,0:T(8,128)(2,1)S(1)}, bf16[512,256]{1,0:T(8,128)(2,1)S(1)}, u32[]{:S(2)}, u32[]{:S(2)}) collective-permute-start(bf16[512,256]{1,0:T(8,128)(2,1)S(1)} %get-tuple-element.36), channel_id=1, source_target_pairs={{0,2},{1,3},{2,0},{3,1},{4,6},{5,7},{6,4},{7,5},{8,24},{9,25},{10,... | collective-permute-start | bytes 786440 | tf_op jit(solution)/shard_map/ppermute | solution.py:180
  10.1 9.3 %collective-permute-start.2 = (bf16[512,256]{1,0:T(8,128)(2,1)S(1)}, bf16[512,256]{1,0:T(8,128)(2,1)S(1)}, u32[]{:S(2)}, u32[]{:S(2)}) collective-permute-start(bf16[512,256]{1,0:T(8,128)(2,1)S(1)} %get-tuple-element.29), channel_id=1, source_target_pairs={{0,2},{1,3},{2,0},{3,1},{4,6},{5,7},{6,4},{7,5},{8,9},{9,8},{10,11... | collective-permute-start | bytes 786440 | tf_op jit(solution)/shard_map/ppermute | solution.py:180
  13.9 8.3 %collective-permute-start.4 = (bf16[512,256]{1,0:T(8,128)(2,1)S(1)}, bf16[512,256]{1,0:T(8,128)(2,1)S(1)}, u32[]{:S(2)}, u32[]{:S(2)}) collective-permute-start(bf16[512,256]{1,0:T(8,128)(2,1)S(1)} %fusion.5), channel_id=1, source_target_pairs={{0,2},{1,3},{2,0},{3,1},{4,6},{5,7},{6,4},{7,5},{8,24},{9,25},{10,... | collective-permute-start | bytes 786440 | tf_op jit(solution)/shard_map/ppermute | solution.py:180
  16.7 8.2 %collective-permute-start.7 = (bf16[512,256]{1,0:T(8,128)(2,1)S(1)}, bf16[512,256]{1,0:T(8,128)(2,1)S(1)}, u32[]{:S(2)}, u32[]{:S(2)}) collective-permute-start(bf16[512,256]{1,0:T(8,128)(2,1)S(1)} %select_convert_fusion), channel_id=1, source_target_pairs={{0,16},{1,17},{2,18},{3,19},{4,20},{5,21},{6,22},{7,23},{8,9},{9,8... | collective-permute-start | bytes 786440 | tf_op jit(solution)/shard_map/ppermute | solution.py:180
  18.8 8.9 %collective-permute-start.6 = (bf16[512,256]{1,0:T(8,128)(2,1)S(1)}, bf16[512,256]{1,0:T(8,128)(2,1)S(1)}, u32[]{:S(2)}, u32[]{:S(2)}) collective-permute-start(bf16[512,256]{1,0:T(8,128)(2,1)S(1)} %fusion.4), channel_id=1, source_target_pairs={{0,16},{1,17},{2,18},{3,19},{4,20},{5,21},{6,22},{7,23},{8,24},{9,... | collective-permute-start | bytes 786440 | tf_op jit(solution)/shard_map/ppermute | solution.py:180
  22.3 5.4 %collective-permute-start.8 = (bf16[512,256]{1,0:T(8,128)(2,1)S(1)}, bf16[512,256]{1,0:T(8,128)(2,1)S(1)}, u32[]{:S(2)}, u32[]{:S(2)}) collective-permute-start(bf16[512,256]{1,0:T(8,128)(2,1)S(1)} %add_convert_fusion), channel_id=1, source_target_pairs={{0,0},{1,1},{2,2},{3,3},{4,4},{5,5},{6,6},{7,7},{8,10},{9,11},{10,... | collective-permute-start | bytes 786440 | tf_op jit(solution)/shard_map/ppermute | solution.py:180
  28.0 6.0 %collective-permute-start.10 = (bf16[256,256]{1,0:T(8,128)(2,1)S(1)}, bf16[256,256]{1,0:T(8,128)(2,1)S(1)}, u32[]{:S(2)}, u32[]{:S(2)}) collective-permute-start(bf16[256,256]{1,0:T(8,128)(2,1)S(1)} %get-tuple-element.50), channel_id=1, source_target_pairs={{0,1},{1,0},{2,3},{3,2},{4,5},{5,4},{6,7},{7,6},{8,12},{9,13},{10,... | collective-permute-start | bytes 393224 | tf_op jit(solution)/shard_map/ppermute | solution.py:180
  29.6 5.0 %collective-permute-start.9 = (bf16[256,256]{1,0:T(8,128)(2,1)S(1)}, bf16[256,256]{1,0:T(8,128)(2,1)S(1)}, u32[]{:S(2)}, u32[]{:S(2)}) collective-permute-start(bf16[256,256]{1,0:T(8,128)(2,1)S(1)} %get-tuple-element.51), channel_id=1, source_target_pairs={{0,1},{1,0},{2,3},{3,2},{4,5},{5,4},{6,7},{7,6},{8,12},{9,13},{10,... | collective-permute-start | bytes 393224 | tf_op jit(solution)/shard_map/ppermute | solution.py:180
  30.1 3.9 %collective-permute-start.11 = (bf16[32,512]{1,0:T(8,128)(2,1)S(1)}, bf16[32,512]{1,0:T(8,128)(2,1)S(1)}, u32[]{:S(2)}, u32[]{:S(2)}) collective-permute-start(bf16[32,512]{1,0:T(8,128)(2,1)S(1)} %get-tuple-element.45), channel_id=1, source_target_pairs={{0,16},{1,17},{2,18},{3,19},{4,20},{5,21},{6,22},{7,23},{8,24},{9,... | collective-permute-start | bytes 98312 | tf_op jit(solution)/shard_map/ppermute | solution.py:180
  34.1 1.4 %collective-permute-start.12 = (bf16[256,256]{1,0:T(8,128)(2,1)S(1)}, bf16[256,256]{1,0:T(8,128)(2,1)S(1)}, u32[]{:S(2)}, u32[]{:S(2)}) collective-permute-start(bf16[256,256]{1,0:T(8,128)(2,1)S(1)} %fusion.7), channel_id=1, source_target_pairs={{0,8},{1,9},{2,10},{3,11},{4,12},{5,13},{6,14},{7,15},{8,0},{9,1},... | collective-permute-start | bytes 393224 | tf_op jit(solution)/shard_map/ppermute | solution.py:180
  35.5 6.2 %collective-permute-start.13 = (bf16[256,256]{1,0:T(8,128)(2,1)S(1)}, bf16[256,256]{1,0:T(8,128)(2,1)S(1)}, u32[]{:S(2)}, u32[]{:S(2)}) collective-permute-start(bf16[256,256]{1,0:T(8,128)(2,1)S(1)} %add_convert_fusion.1), channel_id=1, source_target_pairs={{0,16},{1,17},{2,18},{3,19},{4,20},{5,21},{6,22},{7,23},{8,24},{9,... | collective-permute-start | bytes 393224 | tf_op jit(solution)/shard_map/ppermute | solution.py:180
  41.7 1.6 %collective-permute-start.14 = (bf16[2,256,256]{2,1,0:T(8,128)(2,1)S(1)}, bf16[2,256,256]{2,1,0:T(8,128)(2,1)S(1)}, u32[]{:S(2)}, u32[]{:S(2)}) collective-permute-start(bf16[2,256,256]{2,1,0:T(8,128)(2,1)S(1)} %pad_maximum_fusion.pair_ref), channel_id=1, source_target_pairs={{0,8},{1,9},{2,10},{3,11},{4,12},{5,13},{6,14},{7,15},{8,0},{9,1},... | collective-permute-start | bytes 786440 | tf_op jit(solution)/shard_map/ppermute | solution.py:180

commit v13 on v12

--- a/solution.py
+++ b/solution.py
@@ -345,8 +345,8 @@
     def chain(z, y, x):
         return ((z, y, x, 0), (z, y, x, 1))
 
-    def own(z, y, part):
-        return ((z, y, 1, part), (z, y, 0, part))
+    def own(z, far, part):
+        return ((z, far, 1, part), (z, far, 0, part)) if part == 0 else ((z, 1, far, part), (z, 0, far, part))
 
     def parts(*pairs):
         return [tuple(zip(*pair)) for pair in pairs]
@@ -367,19 +367,19 @@
     sixth = jnp.where(odd, total2, total1).astype(BF16)
     rows, window = inner_swap(after_all(v0, spare)[0], v1)
     third, fourth, window = after_all(third, fourth, window, fifth, sixth)[:3]
-    fifth = routed(fifth, Y, Y)
+    fifth = routed(fifth, Y, X)
     sixth = routed(sixth, X, Y)
     total3 = add(keep3, third)
     joined = add(total3, fourth).astype(BF16)
     fourth, fifth, sixth = after_all(fourth, fifth, sixth, joined)[:3]
-    joined = routed(joined, Z1, 0)
+    joined = routed(joined, Z1, X)
     rest = add(keep4, fifth)
     some = add(total3, sixth)
     rest = jnp.where(odd, add(rest, sixth, joined), add(rest, fourth))
     last1 = rest[:both].astype(BF16)
     last2 = jnp.where(odd, rest[both:], some[:both]).astype(BF16)
     window = xor_permute(after_all(window, last1, last2)[0], Y)
-    last1 = routed(last1, Z2, X)
+    last1 = routed(last1, Z2, Y)
     last2 = routed(last2, Z2, X)
     last1, window = after_all(last1, window)
     crossed = xor_permute(jnp.where(odd, last1, add(rest[both:], last1).astype(BF16)), CORE)

time: 44.6 us -> 46.8 us (1.049)
  starting transfers between devices: 15.7 us -> 18.2 us
    ppermute x15, starting transfers between devices: 15.7 us -> 18.2 us  [routed(): lax.ppermute(value, ('dp', 'fsdp'), [(i, i ^ (odd if i // owners % 2 else...]
  transfers between devices with their start and end apart: 15 -> 15, of which waited for: 12 -> 11; matrix products, arithmetic and copies ran while one was open for 1% -> 1% of each run, Pallas kernels for 12% -> 12%
where the time goes in v13:
time: 46.8 us; the launch traced here: 46.7 us
  waiting for transfers between devices  19 us (41%)
  starting transfers between devices  18.2 us (39%)
  Pallas kernels  7.13 us (15%)
  between operations  1.52 us (3%)
  other arithmetic  0.83 us (2%)
    ppermute x15, waiting for transfers between devices, routed(): lax.ppermute(value, ('dp', 'fsdp'), [(i, i ^ (odd if i // owners % 2 else...  19 us
    ppermute x15, starting transfers between devices, routed(): lax.ppermute(value, ('dp', 'fsdp'), [(i, i ^ (odd if i // owners % 2 else...  18.2 us
    pallas_call x1, Pallas kernels, front(): pl.pallas_call(functools.partial(front_kernel, per_group), in_specs=[HBM]...  2.64 us
    pallas_call x4, Pallas kernels, partial_sums(): pl.pallas_call(functools.partial(partial_kernel, parts), in_specs=[VMEM]...  2.17 us
    pallas_call x1, Pallas kernels, place(): pl.pallas_call(place_kernel, in_specs=[VMEM] * 2, out_specs=VMEM, out_sha...  1.05 us
  transfers between devices with their start and end apart: 15, of which 11 were waited for; matrix products, arithmetic and copies ran while one was open for 1% of the time, Pallas kernels for 12%

profile of v13, /device:TPU:0, one launch (start us, length us, event | category | flops | bytes accessed | tf_op | source)
XLA Modules:
  0.0 46.7 jit_solution(1949136253980888636)
XLA Ops:
  0.6 0.0 copy-start
  0.6 0.5 %collective-permute-start = (bf16[256,4096]{1,0:T(8,128)(2,1)}, bf16[256,4096]{1,0:T(8,128)(2,1)S(1)}, u32[]{:S(2)}, u32[]{:S(2)}) collective-permute-start(bf16[256,4096]{1,0:T(8,128)(2,1)} %own_ref.7), channel_id=1, source_target_pairs={{0,8},{1,9},{2,10},{3,11},{4,12},{5,13},{6,14},{7,15},{8,0},{9,1},... | collective-permute-start | bytes 6291464 | tf_op jit(solution)/shard_map/ppermute | solution.py:180
  1.9 2.6 %front.1 = (bf16[272,512]{1,0:T(8,128)(2,1)S(1)}, f32[8,256]{1,0:T(8,128)S(1)}) custom-call(f32[16]{0:T(128)} %loss_hbm.1, s32[1]{0:T(128)S(6)} %copy.12.exponent_hbm, s32[1,2]{1,0:T(1,128)} %start_hbm.1, s32[1,2]{1,0:T(1,128)} %rows_hbm.1, bf16[256,2048]{1,0:T(8,128)(2,1)} %q_hbm.1, bf16[256,512]{1,0:T(8,128)(2,1)} %k_hbm.1, bf16[256,2048]{1,0:T(8,128)(2,1)} %g_hbm.1, ...), custom_call_target="tpu_custom_call" | custom-call | tf_op jit(solution)/shard_map/front/pallas_call | solution.py:154
  4.6 0.1 collective-permute-start.1
  4.7 1.5 %collective-permute-done.1.v1_ref = bf16[272,512]{1,0:T(8,128)(2,1)S(1)} collective-permute-done((bf16[272,512]{1,0:T(8,128)(2,1)S(1)}, bf16[272,512]{1,0:T(8,128)(2,1)S(1)}, u32[]{:S(2)}, u32[]{:S(2)}) %collective-permute-start.1) | collective-permute-done | bytes 278560 | tf_op jit(solution)/shard_map/ppermute | solution.py:180
  6.2 0.0 collective-permute-done.near_ref
  6.2 0.0 copy-done
  6.2 0.5 %partial_sums.7 = (bf16[512,256]{1,0:T(8,128)(2,1)S(1)}, bf16[512,256]{1,0:T(8,128)(2,1)S(1)}) custom-call(bf16[256,4096]{1,0:T(8,128)(2,1)S(1)} %copy-done, bf16[256,4096]{1,0:T(8,128)(2,1)S(1)} %collective-permute-done.near_ref, bf16[272,512]{1,0:T(8,128)(2,1)S(1)} %get-tuple-element.33.v0_ref, bf16[272,512]{1,0:T(8,128)(2,1)S(1)} %collective-permute-done.1.v1_ref), custom_call_target="tpu_custom_call" | custom-call | tf_op jit(solution)/shard_map/partial_sums/pallas_call | solution.py:214
  6.8 2.7 %collective-permute-start.3 = (bf16[512,256]{1,0:T(8,128)(2,1)S(1)}, bf16[512,256]{1,0:T(8,128)(2,1)S(1)}, u32[]{:S(2)}, u32[]{:S(2)}) collective-permute-start(bf16[512,256]{1,0:T(8,128)(2,1)S(1)} %get-tuple-element.31), channel_id=1, source_target_pairs={{0,2},{1,3},{2,0},{3,1},{4,6},{5,7},{6,4},{7,5},{8,9},{9,8},{10,11... | collective-permute-start | bytes 786440 | tf_op jit(solution)/shard_map/ppermute | solution.py:180
  9.4 0.1 collective-permute-start.5
  9.5 0.5 %partial_sums.5 = (bf16[512,256]{1,0:T(8,128)(2,1)S(1)}, bf16[512,256]{1,0:T(8,128)(2,1)S(1)}) custom-call(bf16[256,4096]{1,0:T(8,128)(2,1)S(1)} %copy-done, bf16[256,4096]{1,0:T(8,128)(2,1)S(1)} %collective-permute-done.near_ref, bf16[272,512]{1,0:T(8,128)(2,1)S(1)} %get-tuple-element.33.v0_ref, bf16[272,512]{1,0:T(8,128)(2,1)S(1)} %collective-permute-done.1.v1_ref), custom_call_target="tpu_custom_call" | custom-call | tf_op jit(solution)/shard_map/partial_sums/pallas_call | solution.py:214
  10.1 2.0 %collective-permute-start.2 = (bf16[512,256]{1,0:T(8,128)(2,1)S(1)}, bf16[512,256]{1,0:T(8,128)(2,1)S(1)}, u32[]{:S(2)}, u32[]{:S(2)}) collective-permute-start(bf16[512,256]{1,0:T(8,128)(2,1)S(1)} %get-tuple-element.29), channel_id=1, source_target_pairs={{0,2},{1,3},{2,0},{3,1},{4,6},{5,7},{6,4},{7,5},{8,9},{9,8},{10,11... | collective-permute-start | bytes 786440 | tf_op jit(solution)/shard_map/ppermute | solution.py:180
  12.1 0.5 %partial_sums.6 = (f32[512,256]{1,0:T(8,128)S(1)}, f32[512,256]{1,0:T(8,128)S(1)}) custom-call(bf16[256,4096]{1,0:T(8,128)(2,1)S(1)} %copy-done, bf16[256,4096]{1,0:T(8,128)(2,1)S(1)} %collective-permute-done.near_ref, bf16[272,512]{1,0:T(8,128)(2,1)S(1)} %get-tuple-element.33.v0_ref, bf16[272,512]{1,0:T(8,128)(2,1)S(1)} %collective-permute-done.1.v1_ref), custom_call_target="tpu_custom_call" | custom-call | tf_op jit(solution)/shard_map/partial_sums/pallas_call | solution.py:214
  12.6 0.5 %partial_sums.4 = (f32[512,256]{1,0:T(8,128)S(1)}, f32[512,256]{1,0:T(8,128)S(1)}) custom-call(bf16[256,4096]{1,0:T(8,128)(2,1)S(1)} %copy-done, bf16[256,4096]{1,0:T(8,128)(2,1)S(1)} %collective-permute-done.near_ref, bf16[272,512]{1,0:T(8,128)(2,1)S(1)} %get-tuple-element.33.v0_ref, bf16[272,512]{1,0:T(8,128)(2,1)S(1)} %collective-permute-done.1.v1_ref), custom_call_target="tpu_custom_call" | custom-call | tf_op jit(solution)/shard_map/partial_sums/pallas_call | solution.py:214
  13.2 0.3 inner_swap.1
  13.5 0.3 collective-permute-done.3
  13.8 0.1 fusion.5
  13.9 2.1 %collective-permute-start.4 = (bf16[512,256]{1,0:T(8,128)(2,1)S(1)}, bf16[512,256]{1,0:T(8,128)(2,1)S(1)}, u32[]{:S(2)}, u32[]{:S(2)}) collective-permute-start(bf16[512,256]{1,0:T(8,128)(2,1)S(1)} %fusion.5), channel_id=1, source_target_pairs={{0,2},{1,3},{2,0},{3,1},{4,6},{5,7},{6,4},{7,5},{8,24},{9,25},{10,... | collective-permute-start | bytes 786440 | tf_op jit(solution)/shard_map/ppermute | solution.py:180
  16.0 0.6 %collective-permute-done.5 = bf16[512,256]{1,0:T(8,128)(2,1)S(1)} collective-permute-done((bf16[512,256]{1,0:T(8,128)(2,1)S(1)}, bf16[512,256]{1,0:T(8,128)(2,1)S(1)}, u32[]{:S(2)}, u32[]{:S(2)}) %collective-permute-start.5) | collective-permute-done | bytes 262176 | tf_op jit(solution)/shard_map/ppermute | solution.py:180
  16.6 0.1 select_convert_fusion
  16.7 2.0 %collective-permute-start.7 = (bf16[512,256]{1,0:T(8,128)(2,1)S(1)}, bf16[512,256]{1,0:T(8,128)(2,1)S(1)}, u32[]{:S(2)}, u32[]{:S(2)}) collective-permute-start(bf16[512,256]{1,0:T(8,128)(2,1)S(1)} %select_convert_fusion), channel_id=1, source_target_pairs={{0,16},{1,17},{2,18},{3,19},{4,20},{5,21},{6,22},{7,23},{8,9},{9,8... | collective-permute-start | bytes 786440 | tf_op jit(solution)/shard_map/ppermute | solution.py:180
  18.7 0.1 fusion.4
  18.8 1.6 %collective-permute-start.6 = (bf16[512,256]{1,0:T(8,128)(2,1)S(1)}, bf16[512,256]{1,0:T(8,128)(2,1)S(1)}, u32[]{:S(2)}, u32[]{:S(2)}) collective-permute-start(bf16[512,256]{1,0:T(8,128)(2,1)S(1)} %fusion.4), channel_id=1, source_target_pairs={{0,1},{1,0},{2,3},{3,2},{4,5},{5,4},{6,7},{7,6},{8,24},{9,25},{10,... | collective-permute-start | bytes 786440 | tf_op jit(solution)/shard_map/ppermute | solution.py:180
  20.4 0.0 collective-permute-done.2
  20.4 1.9 %collective-permute-done.4 = bf16[512,256]{1,0:T(8,128)(2,1)S(1)} collective-permute-done((bf16[512,256]{1,0:T(8,128)(2,1)S(1)}, bf16[512,256]{1,0:T(8,128)(2,1)S(1)}, u32[]{:S(2)}, u32[]{:S(2)}) %collective-permute-start.4) | collective-permute-done | bytes 262176 | tf_op jit(solution)/shard_map/ppermute | solution.py:180
  22.3 0.1 add_convert_fusion
  22.4 2.3 %collective-permute-start.8 = (bf16[512,256]{1,0:T(8,128)(2,1)S(1)}, bf16[512,256]{1,0:T(8,128)(2,1)S(1)}, u32[]{:S(2)}, u32[]{:S(2)}) collective-permute-start(bf16[512,256]{1,0:T(8,128)(2,1)S(1)} %add_convert_fusion), channel_id=1, source_target_pairs={{0,1},{1,0},{2,3},{3,2},{4,5},{5,4},{6,7},{7,6},{8,10},{9,11},{10,... | collective-permute-start | bytes 786440 | tf_op jit(solution)/shard_map/ppermute | solution.py:180
  24.7 0.2 collective-permute-done.7
  24.9 0.4 collective-permute-done.6
  25.3 3.8 %collective-permute-done.8 = bf16[512,256]{1,0:T(8,128)(2,1)S(1)} collective-permute-done((bf16[512,256]{1,0:T(8,128)(2,1)S(1)}, bf16[512,256]{1,0:T(8,128)(2,1)S(1)}, u32[]{:S(2)}, u32[]{:S(2)}) %collective-permute-start.8) | collective-permute-done | bytes 262176 | tf_op jit(solution)/shard_map/ppermute | solution.py:180
  29.0 0.2 fusion.1
  29.3 2.1 %collective-permute-start.10 = (bf16[256,256]{1,0:T(8,128)(2,1)S(1)}, bf16[256,256]{1,0:T(8,128)(2,1)S(1)}, u32[]{:S(2)}, u32[]{:S(2)}) collective-permute-start(bf16[256,256]{1,0:T(8,128)(2,1)S(1)} %get-tuple-element.50), channel_id=1, source_target_pairs={{0,16},{1,17},{2,18},{3,19},{4,20},{5,21},{6,22},{7,23},{8,12},{9,... | collective-permute-start | bytes 393224 | tf_op jit(solution)/shard_map/ppermute | solution.py:180
  31.5 1.5 %collective-permute-start.9 = (bf16[256,256]{1,0:T(8,128)(2,1)S(1)}, bf16[256,256]{1,0:T(8,128)(2,1)S(1)}, u32[]{:S(2)}, u32[]{:S(2)}) collective-permute-start(bf16[256,256]{1,0:T(8,128)(2,1)S(1)} %get-tuple-element.51), channel_id=1, source_target_pairs={{0,1},{1,0},{2,3},{3,2},{4,5},{5,4},{6,7},{7,6},{8,12},{9,13},{10,... | collective-permute-start | bytes 393224 | tf_op jit(solution)/shard_map/ppermute | solution.py:180
  33.0 0.5 %collective-permute-start.11 = (bf16[32,512]{1,0:T(8,128)(2,1)S(1)}, bf16[32,512]{1,0:T(8,128)(2,1)S(1)}, u32[]{:S(2)}, u32[]{:S(2)}) collective-permute-start(bf16[32,512]{1,0:T(8,128)(2,1)S(1)} %get-tuple-element.45), channel_id=1, source_target_pairs={{0,16},{1,17},{2,18},{3,19},{4,20},{5,21},{6,22},{7,23},{8,24},{9,... | collective-permute-start | bytes 98312 | tf_op jit(solution)/shard_map/ppermute | solution.py:180
  33.5 3.4 %collective-permute-done.11.window_ref = bf16[32,512]{1,0:T(8,128)(2,1)S(1)} collective-permute-done((bf16[32,512]{1,0:T(8,128)(2,1)S(1)}, bf16[32,512]{1,0:T(8,128)(2,1)S(1)}, u32[]{:S(2)}, u32[]{:S(2)}) %collective-permute-start.11) | collective-permute-done | bytes 32800 | tf_op jit(solution)/shard_map/ppermute | solution.py:180
  36.9 0.0 collective-permute-done.10
  36.9 0.1 collective-permute-start.12
  37.0 0.0 collective-permute-done.9.arrived_ref
  37.1 1.3 %collective-permute-done.12 = bf16[256,256]{1,0:T(8,128)(2,1)S(1)} collective-permute-done((bf16[256,256]{1,0:T(8,128)(2,1)S(1)}, bf16[256,256]{1,0:T(8,128)(2,1)S(1)}, u32[]{:S(2)}, u32[]{:S(2)}) %collective-permute-start.12) | collective-permute-done | bytes 131104 | tf_op jit(solution)/shard_map/ppermute | solution.py:180
  38.4 0.5 %collective-permute-start.13 = (bf16[256,256]{1,0:T(8,128)(2,1)S(1)}, bf16[256,256]{1,0:T(8,128)(2,1)S(1)}, u32[]{:S(2)}, u32[]{:S(2)}) collective-permute-start(bf16[256,256]{1,0:T(8,128)(2,1)S(1)} %add_convert_fusion.1), channel_id=1, source_target_pairs={{0,16},{1,17},{2,18},{3,19},{4,20},{5,21},{6,22},{7,23},{8,24},{9,... | collective-permute-start | bytes 393224 | tf_op jit(solution)/shard_map/ppermute | solution.py:180
  38.9 5.1 %collective-permute-done.13 = bf16[256,256]{1,0:T(8,128)(2,1)S(1)} collective-permute-done((bf16[256,256]{1,0:T(8,128)(2,1)S(1)}, bf16[256,256]{1,0:T(8,128)(2,1)S(1)}, u32[]{:S(2)}, u32[]{:S(2)}) %collective-permute-start.13) | collective-permute-done | bytes 131104 | tf_op jit(solution)/shard_map/ppermute | solution.py:180
  44.0 0.1 collective-permute-start.14
  44.1 0.9 %outer_swap.1 = bf16[256,512]{1,0:T(8,128)(2,1)} custom-call(bf16[272,512]{1,0:T(8,128)(2,1)S(1)} %get-tuple-element.33.v0_ref, bf16[256,512]{1,0:T(8,128)(2,1)S(1)} %get-tuple-element.47.rows_ref, bf16[32,512]{1,0:T(8,128)(2,1)S(1)} %collective-permute-done.11.window_ref), custom_call_target="tpu_custom_call" | custom-call | tf_op jit(solution)/shard_map/outer_swap/pallas_call | solution.py:278
  45.0 0.6 %collective-permute-done.14.near_ref = bf16[2,256,256]{2,1,0:T(8,128)(2,1)S(1)} collective-permute-done((bf16[2,256,256]{2,1,0:T(8,128)(2,1)S(1)}, bf16[2,256,256]{2,1,0:T(8,128)(2,1)S(1)}, u32[]{:S(2)}, u32[]{:S(2)}) %collective-permute-start.14) | collective-permute-done | bytes 262176 | tf_op jit(solution)/shard_map/ppermute | solution.py:180
  45.6 1.1 %place.1 = f32[512,512]{1,0:T(8,128)} custom-call(bf16[2,256,256]{2,1,0:T(8,128)(2,1)S(1)} %pad_maximum_fusion.pair_ref, bf16[2,256,256]{2,1,0:T(8,128)(2,1)S(1)} %collective-permute-done.14.near_ref), custom_call_target="tpu_custom_call" | custom-call | tf_op jit(solution)/shard_map/place/pallas_call | solution.py:299
  (7 shorter events, 0.2 us)
Async XLA Ops:
  0.6 5.6 %copy-start = (bf16[256,4096]{1,0:T(8,128)(2,1)S(1)}, bf16[256,4096]{1,0:T(8,128)(2,1)}, u32[]{:S(2)}) copy-start(bf16[256,4096]{1,0:T(8,128)(2,1)} %own_ref.7) | copy-start | bytes 6291460
  0.6 5.5 %collective-permute-start = (bf16[256,4096]{1,0:T(8,128)(2,1)}, bf16[256,4096]{1,0:T(8,128)(2,1)S(1)}, u32[]{:S(2)}, u32[]{:S(2)}) collective-permute-start(bf16[256,4096]{1,0:T(8,128)(2,1)} %own_ref.7), channel_id=1, source_target_pairs={{0,8},{1,9},{2,10},{3,11},{4,12},{5,13},{6,14},{7,15},{8,0},{9,1},... | collective-permute-start | bytes 6291464 | tf_op jit(solution)/shard_map/ppermute | solution.py:180
  4.6 1.6 %collective-permute-start.1 = (bf16[272,512]{1,0:T(8,128)(2,1)S(1)}, bf16[272,512]{1,0:T(8,128)(2,1)S(1)}, u32[]{:S(2)}, u32[]{:S(2)}) collective-permute-start(bf16[272,512]{1,0:T(8,128)(2,1)S(1)} %get-tuple-element.33.v0_ref), channel_id=1, source_target_pairs={{0,8},{1,9},{2,10},{3,11},{4,12},{5,13},{6,14},{7,15},{8,0},{9,1},... | collective-permute-start | bytes 835592 | tf_op jit(solution)/shard_map/ppermute | solution.py:180
  6.8 7.0 %collective-permute-start.3 = (bf16[512,256]{1,0:T(8,128)(2,1)S(1)}, bf16[512,256]{1,0:T(8,128)(2,1)S(1)}, u32[]{:S(2)}, u32[]{:S(2)}) collective-permute-start(bf16[512,256]{1,0:T(8,128)(2,1)S(1)} %get-tuple-element.31), channel_id=1, source_target_pairs={{0,2},{1,3},{2,0},{3,1},{4,6},{5,7},{6,4},{7,5},{8,9},{9,8},{10,11... | collective-permute-start | bytes 786440 | tf_op jit(solution)/shard_map/ppermute | solution.py:180
  9.4 7.2 %collective-permute-start.5 = (bf16[512,256]{1,0:T(8,128)(2,1)S(1)}, bf16[512,256]{1,0:T(8,128)(2,1)S(1)}, u32[]{:S(2)}, u32[]{:S(2)}) collective-permute-start(bf16[512,256]{1,0:T(8,128)(2,1)S(1)} %get-tuple-element.36), channel_id=1, source_target_pairs={{0,2},{1,3},{2,0},{3,1},{4,6},{5,7},{6,4},{7,5},{8,24},{9,25},{10,... | collective-permute-start | bytes 786440 | tf_op jit(solution)/shard_map/ppermute | solution.py:180
  10.1 10.3 %collective-permute-start.2 = (bf16[512,256]{1,0:T(8,128)(2,1)S(1)}, bf16[512,256]{1,0:T(8,128)(2,1)S(1)}, u32[]{:S(2)}, u32[]{:S(2)}) collective-permute-start(bf16[512,256]{1,0:T(8,128)(2,1)S(1)} %get-tuple-element.29), channel_id=1, source_target_pairs={{0,2},{1,3},{2,0},{3,1},{4,6},{5,7},{6,4},{7,5},{8,9},{9,8},{10,11... | collective-permute-start | bytes 786440 | tf_op jit(solution)/shard_map/ppermute | solution.py:180
  13.9 8.5 %collective-permute-start.4 = (bf16[512,256]{1,0:T(8,128)(2,1)S(1)}, bf16[512,256]{1,0:T(8,128)(2,1)S(1)}, u32[]{:S(2)}, u32[]{:S(2)}) collective-permute-start(bf16[512,256]{1,0:T(8,128)(2,1)S(1)} %fusion.5), channel_id=1, source_target_pairs={{0,2},{1,3},{2,0},{3,1},{4,6},{5,7},{6,4},{7,5},{8,24},{9,25},{10,... | collective-permute-start | bytes 786440 | tf_op jit(solution)/shard_map/ppermute | solution.py:180
  16.7 8.2 %collective-permute-start.7 = (bf16[512,256]{1,0:T(8,128)(2,1)S(1)}, bf16[512,256]{1,0:T(8,128)(2,1)S(1)}, u32[]{:S(2)}, u32[]{:S(2)}) collective-permute-start(bf16[512,256]{1,0:T(8,128)(2,1)S(1)} %select_convert_fusion), channel_id=1, source_target_pairs={{0,16},{1,17},{2,18},{3,19},{4,20},{5,21},{6,22},{7,23},{8,9},{9,8... | collective-permute-start | bytes 786440 | tf_op jit(solution)/shard_map/ppermute | solution.py:180
  18.8 6.4 %collective-permute-start.6 = (bf16[512,256]{1,0:T(8,128)(2,1)S(1)}, bf16[512,256]{1,0:T(8,128)(2,1)S(1)}, u32[]{:S(2)}, u32[]{:S(2)}) collective-permute-start(bf16[512,256]{1,0:T(8,128)(2,1)S(1)} %fusion.4), channel_id=1, source_target_pairs={{0,1},{1,0},{2,3},{3,2},{4,5},{5,4},{6,7},{7,6},{8,24},{9,25},{10,... | collective-permute-start | bytes 786440 | tf_op jit(solution)/shard_map/ppermute | solution.py:180
  22.4 6.6 %collective-permute-start.8 = (bf16[512,256]{1,0:T(8,128)(2,1)S(1)}, bf16[512,256]{1,0:T(8,128)(2,1)S(1)}, u32[]{:S(2)}, u32[]{:S(2)}) collective-permute-start(bf16[512,256]{1,0:T(8,128)(2,1)S(1)} %add_convert_fusion), channel_id=1, source_target_pairs={{0,1},{1,0},{2,3},{3,2},{4,5},{5,4},{6,7},{7,6},{8,10},{9,11},{10,... | collective-permute-start | bytes 786440 | tf_op jit(solution)/shard_map/ppermute | solution.py:180
  29.3 7.6 %collective-permute-start.10 = (bf16[256,256]{1,0:T(8,128)(2,1)S(1)}, bf16[256,256]{1,0:T(8,128)(2,1)S(1)}, u32[]{:S(2)}, u32[]{:S(2)}) collective-permute-start(bf16[256,256]{1,0:T(8,128)(2,1)S(1)} %get-tuple-element.50), channel_id=1, source_target_pairs={{0,16},{1,17},{2,18},{3,19},{4,20},{5,21},{6,22},{7,23},{8,12},{9,... | collective-permute-start | bytes 393224 | tf_op jit(solution)/shard_map/ppermute | solution.py:180
  31.5 5.5 %collective-permute-start.9 = (bf16[256,256]{1,0:T(8,128)(2,1)S(1)}, bf16[256,256]{1,0:T(8,128)(2,1)S(1)}, u32[]{:S(2)}, u32[]{:S(2)}) collective-permute-start(bf16[256,256]{1,0:T(8,128)(2,1)S(1)} %get-tuple-element.51), channel_id=1, source_target_pairs={{0,1},{1,0},{2,3},{3,2},{4,5},{5,4},{6,7},{7,6},{8,12},{9,13},{10,... | collective-permute-start | bytes 393224 | tf_op jit(solution)/shard_map/ppermute | solution.py:180
  33.0 3.9 %collective-permute-start.11 = (bf16[32,512]{1,0:T(8,128)(2,1)S(1)}, bf16[32,512]{1,0:T(8,128)(2,1)S(1)}, u32[]{:S(2)}, u32[]{:S(2)}) collective-permute-start(bf16[32,512]{1,0:T(8,128)(2,1)S(1)} %get-tuple-element.45), channel_id=1, source_target_pairs={{0,16},{1,17},{2,18},{3,19},{4,20},{5,21},{6,22},{7,23},{8,24},{9,... | collective-permute-start | bytes 98312 | tf_op jit(solution)/shard_map/ppermute | solution.py:180
  36.9 1.4 %collective-permute-start.12 = (bf16[256,256]{1,0:T(8,128)(2,1)S(1)}, bf16[256,256]{1,0:T(8,128)(2,1)S(1)}, u32[]{:S(2)}, u32[]{:S(2)}) collective-permute-start(bf16[256,256]{1,0:T(8,128)(2,1)S(1)} %fusion.7), channel_id=1, source_target_pairs={{0,8},{1,9},{2,10},{3,11},{4,12},{5,13},{6,14},{7,15},{8,0},{9,1},... | collective-permute-start | bytes 393224 | tf_op jit(solution)/shard_map/ppermute | solution.py:180
  38.4 5.6 %collective-permute-start.13 = (bf16[256,256]{1,0:T(8,128)(2,1)S(1)}, bf16[256,256]{1,0:T(8,128)(2,1)S(1)}, u32[]{:S(2)}, u32[]{:S(2)}) collective-permute-start(bf16[256,256]{1,0:T(8,128)(2,1)S(1)} %add_convert_fusion.1), channel_id=1, source_target_pairs={{0,16},{1,17},{2,18},{3,19},{4,20},{5,21},{6,22},{7,23},{8,24},{9,... | collective-permute-start | bytes 393224 | tf_op jit(solution)/shard_map/ppermute | solution.py:180
  44.0 1.6 %collective-permute-start.14 = (bf16[2,256,256]{2,1,0:T(8,128)(2,1)S(1)}, bf16[2,256,256]{2,1,0:T(8,128)(2,1)S(1)}, u32[]{:S(2)}, u32[]{:S(2)}) collective-permute-start(bf16[2,256,256]{2,1,0:T(8,128)(2,1)S(1)} %pad_maximum_fusion.pair_ref), channel_id=1, source_target_pairs={{0,8},{1,9},{2,10},{3,11},{4,12},{5,13},{6,14},{7,15},{8,0},{9,1},... | collective-permute-start | bytes 786440 | tf_op jit(solution)/shard_map/ppermute | solution.py:180

commit v14 on v13

--- a/solution.py
+++ b/solution.py
@@ -307,26 +307,26 @@
     )(pair, near)
 
 
-def fold_kernel(base_ref, arrived_ref, out_ref):
-    out_ref[...] = base_ref[...] + arrived_ref[...].astype(F32)
-
-
-def fold(base, arrived):
+def fold_kernel(base_ref, arrived_ref, odd_ref, out_ref):
+    out_ref[...] = jnp.where(odd_ref[:1, :] > 0.5, arrived_ref[...].astype(F32), base_ref[...])
+
+
+def fold(base, arrived, odd):
     return pl.pallas_call(
         fold_kernel,
-        in_specs=[VMEM] * 2,
+        in_specs=[VMEM] * 3,
         out_specs=VMEM,
         out_shape=jax.ShapeDtypeStruct(base.shape, F32),
         compiler_params=pltpu.CompilerParams(vmem_limit_bytes=8 * MIB),
         cost_estimate=pl.CostEstimate(flops=8_000_000_000, bytes_accessed=0, transcendentals=0),
         name="fold",
-    )(base, arrived)
+    )(base, arrived, odd)
 
 
 def reduce_by_axis(layer_input, *args):
     near = xor_permute(layer_input, CORE)
-    v0, odd = front(*args)
-    odd = odd[:1] > 0.5
+    v0, odd_row = front(*args)
+    odd = odd_row[:1] > 0.5
     v1 = xor_permute(v0, CORE)
     both = 2 * LANE
 
@@ -358,32 +358,30 @@
     first = routed(first, X, Z1)
     second = routed(second, Y, Z1)
     third = routed(third, X, Z1)
-    total1 = add(keep1, first)
-    fourth = jnp.where(odd, total1.astype(BF16), spare)
+    fourth = add(keep1, first).astype(BF16)
     second = after_all(second, fourth)[0]
-    fourth = routed(fourth, Y, Z1)
-    total2 = add(keep2, second)
-    fifth = jnp.where(odd, spare, total2.astype(BF16))
-    sixth = jnp.where(odd, total2, total1).astype(BF16)
+    sixth = add(keep2, second).astype(BF16)
+    fifth, sixth = after_all(spare, sixth)
     rows, window = inner_swap(after_all(v0, spare)[0], v1)
-    third, fourth, window = after_all(third, fourth, window, fifth, sixth)[:3]
-    fifth = routed(fifth, Y, X)
-    sixth = routed(sixth, X, Y)
-    total3 = add(keep3, third)
-    joined = add(total3, fourth).astype(BF16)
-    fourth, fifth, sixth = after_all(fourth, fifth, sixth, joined)[:3]
+    fourth = routed(fourth, Y, Y)
+    fifth = routed(fifth, Y, Z1)
+    third, fourth, window = after_all(third, fourth, window, sixth)[:3]
+    sixth = routed(sixth, X, X)
+    some = add(keep3, third, fourth)
+    joined = some.astype(BF16)
+    fifth, sixth = after_all(fifth, sixth, joined)[:2]
     joined = routed(joined, Z1, X)
-    rest = add(keep4, fifth)
-    some = add(total3, sixth)
-    rest = jnp.where(odd, add(rest, sixth, joined), add(rest, fourth))
-    last1 = rest[:both].astype(BF16)
-    last2 = jnp.where(odd, rest[both:], some[:both]).astype(BF16)
+    rest = add(keep4, fifth, sixth)
+    crossing = add(rest, joined)
+    last1 = jnp.where(odd, crossing[:both], rest[:both]).astype(BF16)
+    last2 = crossing[both:].astype(BF16)
     window = xor_permute(after_all(window, last1, last2)[0], Y)
     last1 = routed(last1, Z2, Y)
     last2 = routed(last2, Z2, X)
     last1, window = after_all(last1, window)
     crossed = xor_permute(jnp.where(odd, last1, add(rest[both:], last1).astype(BF16)), CORE)
-    mine = add(fold(jnp.where(odd, 0.0, some[both:]), last2), crossed).astype(BF16)
+    base = fold(add(some[both:], joined[:both]), last2, odd_row)
+    mine = add(base, crossed).astype(BF16)
     from_y = xor_permute(mine, Y)
     value_grad = outer_swap(v0, rows, after_all(window, from_y)[0])
     pair = jnp.stack([mine, from_y])

time: 46.8 us -> 47.2 us (level)
  waiting for transfers between devices: 19 us -> 20.3 us
  starting transfers between devices: 18.2 us -> 17.6 us
    ppermute x15, waiting for transfers between devices: 19 us -> 20.3 us  [routed(): lax.ppermute(value, ('dp', 'fsdp'), [(i, i ^ (odd if i // owners % 2 else...]
    ppermute x15, starting transfers between devices: 18.2 us -> 17.6 us  [routed(): lax.ppermute(value, ('dp', 'fsdp'), [(i, i ^ (odd if i // owners % 2 else...]
  transfers between devices with their start and end apart: 15 -> 15, of which waited for: 11 -> 8; matrix products, arithmetic and copies ran while one was open for 1% -> 1% of each run, Pallas kernels for 12% -> 12%
where the time goes in v14:
time: 47.2 us; the launch traced here: 47.1 us
  waiting for transfers between devices  20.3 us (43%)
  starting transfers between devices  17.6 us (37%)
  Pallas kernels  7.13 us (15%)
  between operations  1.52 us (3%)
  other arithmetic  0.51 us (1%)
    ppermute x15, waiting for transfers between devices, routed(): lax.ppermute(value, ('dp', 'fsdp'), [(i, i ^ (odd if i // owners % 2 else...  20.3 us
    ppermute x15, starting transfers between devices, routed(): lax.ppermute(value, ('dp', 'fsdp'), [(i, i ^ (odd if i // owners % 2 else...  17.6 us
    pallas_call x1, Pallas kernels, front(): pl.pallas_call(functools.partial(front_kernel, per_group), in_specs=[HBM]...  2.64 us
    pallas_call x4, Pallas kernels, partial_sums(): pl.pallas_call(functools.partial(partial_kernel, parts), in_specs=[VMEM]...  2.17 us
    pallas_call x1, Pallas kernels, place(): pl.pallas_call(place_kernel, in_specs=[VMEM] * 2, out_specs=VMEM, out_sha...  1.05 us
  transfers between devices with their start and end apart: 15, of which 8 were waited for; matrix products, arithmetic and copies ran while one was open for 1% of the time, Pallas kernels for 12%

profile of v14, /device:TPU:0, one launch (start us, length us, event | category | flops | bytes accessed | tf_op | source)
XLA Modules:
  0.0 47.1 jit_solution(2339091797233903149)
XLA Ops:
  0.6 0.0 copy-start
  0.6 0.5 %collective-permute-start = (bf16[256,4096]{1,0:T(8,128)(2,1)}, bf16[256,4096]{1,0:T(8,128)(2,1)S(1)}, u32[]{:S(2)}, u32[]{:S(2)}) collective-permute-start(bf16[256,4096]{1,0:T(8,128)(2,1)} %own_ref.7), channel_id=1, source_target_pairs={{0,8},{1,9},{2,10},{3,11},{4,12},{5,13},{6,14},{7,15},{8,0},{9,1},... | collective-permute-start | bytes 6291464 | tf_op jit(solution)/shard_map/ppermute | solution.py:180
  1.9 2.6 %front.1 = (bf16[272,512]{1,0:T(8,128)(2,1)S(1)}, f32[8,256]{1,0:T(8,128)S(1)}) custom-call(f32[16]{0:T(128)} %loss_hbm.1, s32[1]{0:T(128)S(6)} %copy.12.exponent_hbm, s32[1,2]{1,0:T(1,128)} %start_hbm.1, s32[1,2]{1,0:T(1,128)} %rows_hbm.1, bf16[256,2048]{1,0:T(8,128)(2,1)} %q_hbm.1, bf16[256,512]{1,0:T(8,128)(2,1)} %k_hbm.1, bf16[256,2048]{1,0:T(8,128)(2,1)} %g_hbm.1, ...), custom_call_target="tpu_custom_call" | custom-call | tf_op jit(solution)/shard_map/front/pallas_call | solution.py:154
  4.6 0.1 collective-permute-start.1
  4.7 1.5 %collective-permute-done.1.v1_ref = bf16[272,512]{1,0:T(8,128)(2,1)S(1)} collective-permute-done((bf16[272,512]{1,0:T(8,128)(2,1)S(1)}, bf16[272,512]{1,0:T(8,128)(2,1)S(1)}, u32[]{:S(2)}, u32[]{:S(2)}) %collective-permute-start.1) | collective-permute-done | bytes 278560 | tf_op jit(solution)/shard_map/ppermute | solution.py:180
  6.2 0.0 collective-permute-done.near_ref
  6.2 0.0 copy-done
  6.2 0.5 %partial_sums.7 = (bf16[512,256]{1,0:T(8,128)(2,1)S(1)}, bf16[512,256]{1,0:T(8,128)(2,1)S(1)}) custom-call(bf16[256,4096]{1,0:T(8,128)(2,1)S(1)} %copy-done, bf16[256,4096]{1,0:T(8,128)(2,1)S(1)} %collective-permute-done.near_ref, bf16[272,512]{1,0:T(8,128)(2,1)S(1)} %get-tuple-element.33.v0_ref, bf16[272,512]{1,0:T(8,128)(2,1)S(1)} %collective-permute-done.1.v1_ref), custom_call_target="tpu_custom_call" | custom-call | tf_op jit(solution)/shard_map/partial_sums/pallas_call | solution.py:214
  6.8 2.7 %collective-permute-start.3 = (bf16[512,256]{1,0:T(8,128)(2,1)S(1)}, bf16[512,256]{1,0:T(8,128)(2,1)S(1)}, u32[]{:S(2)}, u32[]{:S(2)}) collective-permute-start(bf16[512,256]{1,0:T(8,128)(2,1)S(1)} %get-tuple-element.31), channel_id=1, source_target_pairs={{0,2},{1,3},{2,0},{3,1},{4,6},{5,7},{6,4},{7,5},{8,9},{9,8},{10,11... | collective-permute-start | bytes 786440 | tf_op jit(solution)/shard_map/ppermute | solution.py:180
  9.4 0.1 collective-permute-start.5
  9.5 0.5 %partial_sums.5 = (bf16[512,256]{1,0:T(8,128)(2,1)S(1)}, bf16[512,256]{1,0:T(8,128)(2,1)S(1)}) custom-call(bf16[256,4096]{1,0:T(8,128)(2,1)S(1)} %copy-done, bf16[256,4096]{1,0:T(8,128)(2,1)S(1)} %collective-permute-done.near_ref, bf16[272,512]{1,0:T(8,128)(2,1)S(1)} %get-tuple-element.33.v0_ref, bf16[272,512]{1,0:T(8,128)(2,1)S(1)} %collective-permute-done.1.v1_ref), custom_call_target="tpu_custom_call" | custom-call | tf_op jit(solution)/shard_map/partial_sums/pallas_call | solution.py:214
  10.1 2.0 %collective-permute-start.2 = (bf16[512,256]{1,0:T(8,128)(2,1)S(1)}, bf16[512,256]{1,0:T(8,128)(2,1)S(1)}, u32[]{:S(2)}, u32[]{:S(2)}) collective-permute-start(bf16[512,256]{1,0:T(8,128)(2,1)S(1)} %get-tuple-element.29), channel_id=1, source_target_pairs={{0,2},{1,3},{2,0},{3,1},{4,6},{5,7},{6,4},{7,5},{8,9},{9,8},{10,11... | collective-permute-start | bytes 786440 | tf_op jit(solution)/shard_map/ppermute | solution.py:180
  12.1 0.5 %partial_sums.6 = (f32[512,256]{1,0:T(8,128)S(1)}, f32[512,256]{1,0:T(8,128)S(1)}) custom-call(bf16[256,4096]{1,0:T(8,128)(2,1)S(1)} %copy-done, bf16[256,4096]{1,0:T(8,128)(2,1)S(1)} %collective-permute-done.near_ref, bf16[272,512]{1,0:T(8,128)(2,1)S(1)} %get-tuple-element.33.v0_ref, bf16[272,512]{1,0:T(8,128)(2,1)S(1)} %collective-permute-done.1.v1_ref), custom_call_target="tpu_custom_call" | custom-call | tf_op jit(solution)/shard_map/partial_sums/pallas_call | solution.py:214
  12.6 1.2 %collective-permute-done.3 = bf16[512,256]{1,0:T(8,128)(2,1)S(1)} collective-permute-done((bf16[512,256]{1,0:T(8,128)(2,1)S(1)}, bf16[512,256]{1,0:T(8,128)(2,1)S(1)}, u32[]{:S(2)}, u32[]{:S(2)}) %collective-permute-start.3) | collective-permute-done | bytes 262176 | tf_op jit(solution)/shard_map/ppermute | solution.py:180
  13.8 0.1 add_convert_fusion.1
  13.8 2.0 %collective-permute-start.4 = (bf16[512,256]{1,0:T(8,128)(2,1)S(1)}, bf16[512,256]{1,0:T(8,128)(2,1)S(1)}, u32[]{:S(2)}, u32[]{:S(2)}) collective-permute-start(bf16[512,256]{1,0:T(8,128)(2,1)S(1)} %add_convert_fusion.1), channel_id=1, source_target_pairs={{0,16},{1,17},{2,18},{3,19},{4,20},{5,21},{6,22},{7,23},{8,24},{9,... | collective-permute-start | bytes 786440 | tf_op jit(solution)/shard_map/ppermute | solution.py:180
  15.9 0.5 %partial_sums.4 = (f32[512,256]{1,0:T(8,128)S(1)}, f32[512,256]{1,0:T(8,128)S(1)}) custom-call(bf16[256,4096]{1,0:T(8,128)(2,1)S(1)} %copy-done, bf16[256,4096]{1,0:T(8,128)(2,1)S(1)} %collective-permute-done.near_ref, bf16[272,512]{1,0:T(8,128)(2,1)S(1)} %get-tuple-element.33.v0_ref, bf16[272,512]{1,0:T(8,128)(2,1)S(1)} %collective-permute-done.1.v1_ref), custom_call_target="tpu_custom_call" | custom-call | tf_op jit(solution)/shard_map/partial_sums/pallas_call | solution.py:214
  16.4 0.3 inner_swap.1
  16.7 0.0 collective-permute-done.5
  16.7 0.1 add_convert_fusion
  16.8 1.9 %collective-permute-start.7 = (bf16[512,256]{1,0:T(8,128)(2,1)S(1)}, bf16[512,256]{1,0:T(8,128)(2,1)S(1)}, u32[]{:S(2)}, u32[]{:S(2)}) collective-permute-start(bf16[512,256]{1,0:T(8,128)(2,1)S(1)} %get-tuple-element.42), channel_id=1, source_target_pairs={{0,2},{1,3},{2,0},{3,1},{4,6},{5,7},{6,4},{7,5},{8,24},{9,25},{10,... | collective-permute-start | bytes 786440 | tf_op jit(solution)/shard_map/ppermute | solution.py:180
  18.7 1.5 %collective-permute-start.8 = (bf16[512,256]{1,0:T(8,128)(2,1)S(1)}, bf16[512,256]{1,0:T(8,128)(2,1)S(1)}, u32[]{:S(2)}, u32[]{:S(2)}) collective-permute-start(bf16[512,256]{1,0:T(8,128)(2,1)S(1)} %add_convert_fusion), channel_id=1, source_target_pairs={{0,1},{1,0},{2,3},{3,2},{4,5},{5,4},{6,7},{7,6},{8,9},{9,8},{10,11... | collective-permute-start | bytes 786440 | tf_op jit(solution)/shard_map/ppermute | solution.py:180
  20.2 0.0 collective-permute-done.2
  20.2 2.9 %collective-permute-done.4 = bf16[512,256]{1,0:T(8,128)(2,1)S(1)} collective-permute-done((bf16[512,256]{1,0:T(8,128)(2,1)S(1)}, bf16[512,256]{1,0:T(8,128)(2,1)S(1)}, u32[]{:S(2)}, u32[]{:S(2)}) %collective-permute-start.4) | collective-permute-done | bytes 262176 | tf_op jit(solution)/shard_map/ppermute | solution.py:180
  23.1 0.1 fusion.3
  23.2 2.0 %collective-permute-start.6 = (bf16[512,256]{1,0:T(8,128)(2,1)S(1)}, bf16[512,256]{1,0:T(8,128)(2,1)S(1)}, u32[]{:S(2)}, u32[]{:S(2)}) collective-permute-start(bf16[512,256]{1,0:T(8,128)(2,1)S(1)} %get-tuple-element.54), channel_id=1, source_target_pairs={{0,1},{1,0},{2,3},{3,2},{4,5},{5,4},{6,7},{7,6},{8,10},{9,11},{10,... | collective-permute-start | bytes 786440 | tf_op jit(solution)/shard_map/ppermute | solution.py:180
  25.2 0.0 collective-permute-done.7
  25.2 0.0 collective-permute-done.8
  25.3 4.4 %collective-permute-done.6 = bf16[512,256]{1,0:T(8,128)(2,1)S(1)} collective-permute-done((bf16[512,256]{1,0:T(8,128)(2,1)S(1)}, bf16[512,256]{1,0:T(8,128)(2,1)S(1)}, u32[]{:S(2)}, u32[]{:S(2)}) %collective-permute-start.6) | collective-permute-done | bytes 262176 | tf_op jit(solution)/shard_map/ppermute | solution.py:180
  29.6 0.1 convert_add_fusion
  29.8 2.1 %collective-permute-start.10 = (bf16[256,256]{1,0:T(8,128)(2,1)S(1)}, bf16[256,256]{1,0:T(8,128)(2,1)S(1)}, u32[]{:S(2)}, u32[]{:S(2)}) collective-permute-start(bf16[256,256]{1,0:T(8,128)(2,1)S(1)} %get-tuple-element.56), channel_id=1, source_target_pairs={{0,16},{1,17},{2,18},{3,19},{4,20},{5,21},{6,22},{7,23},{8,12},{9,... | collective-permute-start | bytes 393224 | tf_op jit(solution)/shard_map/ppermute | solution.py:180
  31.9 1.5 %collective-permute-start.9 = (bf16[256,256]{1,0:T(8,128)(2,1)S(1)}, bf16[256,256]{1,0:T(8,128)(2,1)S(1)}, u32[]{:S(2)}, u32[]{:S(2)}) collective-permute-start(bf16[256,256]{1,0:T(8,128)(2,1)S(1)} %get-tuple-element.57), channel_id=1, source_target_pairs={{0,1},{1,0},{2,3},{3,2},{4,5},{5,4},{6,7},{7,6},{8,12},{9,13},{10,... | collective-permute-start | bytes 393224 | tf_op jit(solution)/shard_map/ppermute | solution.py:180
  33.4 0.5 %collective-permute-start.11 = (bf16[32,512]{1,0:T(8,128)(2,1)S(1)}, bf16[32,512]{1,0:T(8,128)(2,1)S(1)}, u32[]{:S(2)}, u32[]{:S(2)}) collective-permute-start(bf16[32,512]{1,0:T(8,128)(2,1)S(1)} %get-tuple-element.47), channel_id=1, source_target_pairs={{0,16},{1,17},{2,18},{3,19},{4,20},{5,21},{6,22},{7,23},{8,24},{9,... | collective-permute-start | bytes 98312 | tf_op jit(solution)/shard_map/ppermute | solution.py:180
  33.9 3.4 %collective-permute-done.11.window_ref = bf16[32,512]{1,0:T(8,128)(2,1)S(1)} collective-permute-done((bf16[32,512]{1,0:T(8,128)(2,1)S(1)}, bf16[32,512]{1,0:T(8,128)(2,1)S(1)}, u32[]{:S(2)}, u32[]{:S(2)}) %collective-permute-start.11) | collective-permute-done | bytes 32800 | tf_op jit(solution)/shard_map/ppermute | solution.py:180
  37.3 0.0 collective-permute-done.10
  37.3 0.1 collective-permute-start.12
  37.4 0.0 collective-permute-done.9.arrived_ref
  37.4 1.3 %collective-permute-done.12 = bf16[256,256]{1,0:T(8,128)(2,1)S(1)} collective-permute-done((bf16[256,256]{1,0:T(8,128)(2,1)S(1)}, bf16[256,256]{1,0:T(8,128)(2,1)S(1)}, u32[]{:S(2)}, u32[]{:S(2)}) %collective-permute-start.12) | collective-permute-done | bytes 131104 | tf_op jit(solution)/shard_map/ppermute | solution.py:180
  38.8 0.6 %collective-permute-start.13 = (bf16[256,256]{1,0:T(8,128)(2,1)S(1)}, bf16[256,256]{1,0:T(8,128)(2,1)S(1)}, u32[]{:S(2)}, u32[]{:S(2)}) collective-permute-start(bf16[256,256]{1,0:T(8,128)(2,1)S(1)} %add_convert_fusion.2), channel_id=1, source_target_pairs={{0,16},{1,17},{2,18},{3,19},{4,20},{5,21},{6,22},{7,23},{8,24},{9,... | collective-permute-start | bytes 393224 | tf_op jit(solution)/shard_map/ppermute | solution.py:180
  39.3 5.1 %collective-permute-done.13 = bf16[256,256]{1,0:T(8,128)(2,1)S(1)} collective-permute-done((bf16[256,256]{1,0:T(8,128)(2,1)S(1)}, bf16[256,256]{1,0:T(8,128)(2,1)S(1)}, u32[]{:S(2)}, u32[]{:S(2)}) %collective-permute-start.13) | collective-permute-done | bytes 131104 | tf_op jit(solution)/shard_map/ppermute | solution.py:180
  44.4 0.1 collective-permute-start.14
  44.5 0.9 %outer_swap.1 = bf16[256,512]{1,0:T(8,128)(2,1)} custom-call(bf16[272,512]{1,0:T(8,128)(2,1)S(1)} %get-tuple-element.33.v0_ref, bf16[256,512]{1,0:T(8,128)(2,1)S(1)} %get-tuple-element.49.rows_ref, bf16[32,512]{1,0:T(8,128)(2,1)S(1)} %collective-permute-done.11.window_ref), custom_call_target="tpu_custom_call" | custom-call | tf_op jit(solution)/shard_map/outer_swap/pallas_call | solution.py:278
  45.4 0.6 %collective-permute-done.14.near_ref = bf16[2,256,256]{2,1,0:T(8,128)(2,1)S(1)} collective-permute-done((bf16[2,256,256]{2,1,0:T(8,128)(2,1)S(1)}, bf16[2,256,256]{2,1,0:T(8,128)(2,1)S(1)}, u32[]{:S(2)}, u32[]{:S(2)}) %collective-permute-start.14) | collective-permute-done | bytes 262176 | tf_op jit(solution)/shard_map/ppermute | solution.py:180
  46.0 1.1 %place.1 = f32[512,512]{1,0:T(8,128)} custom-call(bf16[2,256,256]{2,1,0:T(8,128)(2,1)S(1)} %pad_maximum_fusion.pair_ref, bf16[2,256,256]{2,1,0:T(8,128)(2,1)S(1)} %collective-permute-done.14.near_ref), custom_call_target="tpu_custom_call" | custom-call | tf_op jit(solution)/shard_map/place/pallas_call | solution.py:299
  (7 shorter events, 0.2 us)
Async XLA Ops:
  0.6 5.6 %copy-start = (bf16[256,4096]{1,0:T(8,128)(2,1)S(1)}, bf16[256,4096]{1,0:T(8,128)(2,1)}, u32[]{:S(2)}) copy-start(bf16[256,4096]{1,0:T(8,128)(2,1)} %own_ref.7) | copy-start | bytes 6291460
  0.6 5.5 %collective-permute-start = (bf16[256,4096]{1,0:T(8,128)(2,1)}, bf16[256,4096]{1,0:T(8,128)(2,1)S(1)}, u32[]{:S(2)}, u32[]{:S(2)}) collective-permute-start(bf16[256,4096]{1,0:T(8,128)(2,1)} %own_ref.7), channel_id=1, source_target_pairs={{0,8},{1,9},{2,10},{3,11},{4,12},{5,13},{6,14},{7,15},{8,0},{9,1},... | collective-permute-start | bytes 6291464 | tf_op jit(solution)/shard_map/ppermute | solution.py:180
  4.6 1.6 %collective-permute-start.1 = (bf16[272,512]{1,0:T(8,128)(2,1)S(1)}, bf16[272,512]{1,0:T(8,128)(2,1)S(1)}, u32[]{:S(2)}, u32[]{:S(2)}) collective-permute-start(bf16[272,512]{1,0:T(8,128)(2,1)S(1)} %get-tuple-element.33.v0_ref), channel_id=1, source_target_pairs={{0,8},{1,9},{2,10},{3,11},{4,12},{5,13},{6,14},{7,15},{8,0},{9,1},... | collective-permute-start | bytes 835592 | tf_op jit(solution)/shard_map/ppermute | solution.py:180
  6.8 7.0 %collective-permute-start.3 = (bf16[512,256]{1,0:T(8,128)(2,1)S(1)}, bf16[512,256]{1,0:T(8,128)(2,1)S(1)}, u32[]{:S(2)}, u32[]{:S(2)}) collective-permute-start(bf16[512,256]{1,0:T(8,128)(2,1)S(1)} %get-tuple-element.31), channel_id=1, source_target_pairs={{0,2},{1,3},{2,0},{3,1},{4,6},{5,7},{6,4},{7,5},{8,9},{9,8},{10,11... | collective-permute-start | bytes 786440 | tf_op jit(solution)/shard_map/ppermute | solution.py:180
  9.4 7.3 %collective-permute-start.5 = (bf16[512,256]{1,0:T(8,128)(2,1)S(1)}, bf16[512,256]{1,0:T(8,128)(2,1)S(1)}, u32[]{:S(2)}, u32[]{:S(2)}) collective-permute-start(bf16[512,256]{1,0:T(8,128)(2,1)S(1)} %get-tuple-element.36), channel_id=1, source_target_pairs={{0,2},{1,3},{2,0},{3,1},{4,6},{5,7},{6,4},{7,5},{8,24},{9,25},{10,... | collective-permute-start | bytes 786440 | tf_op jit(solution)/shard_map/ppermute | solution.py:180
  10.1 10.2 %collective-permute-start.2 = (bf16[512,256]{1,0:T(8,128)(2,1)S(1)}, bf16[512,256]{1,0:T(8,128)(2,1)S(1)}, u32[]{:S(2)}, u32[]{:S(2)}) collective-permute-start(bf16[512,256]{1,0:T(8,128)(2,1)S(1)} %get-tuple-element.29), channel_id=1, source_target_pairs={{0,2},{1,3},{2,0},{3,1},{4,6},{5,7},{6,4},{7,5},{8,9},{9,8},{10,11... | collective-permute-start | bytes 786440 | tf_op jit(solution)/shard_map/ppermute | solution.py:180
  13.8 9.3 %collective-permute-start.4 = (bf16[512,256]{1,0:T(8,128)(2,1)S(1)}, bf16[512,256]{1,0:T(8,128)(2,1)S(1)}, u32[]{:S(2)}, u32[]{:S(2)}) collective-permute-start(bf16[512,256]{1,0:T(8,128)(2,1)S(1)} %add_convert_fusion.1), channel_id=1, source_target_pairs={{0,16},{1,17},{2,18},{3,19},{4,20},{5,21},{6,22},{7,23},{8,24},{9,... | collective-permute-start | bytes 786440 | tf_op jit(solution)/shard_map/ppermute | solution.py:180
  16.8 8.4 %collective-permute-start.7 = (bf16[512,256]{1,0:T(8,128)(2,1)S(1)}, bf16[512,256]{1,0:T(8,128)(2,1)S(1)}, u32[]{:S(2)}, u32[]{:S(2)}) collective-permute-start(bf16[512,256]{1,0:T(8,128)(2,1)S(1)} %get-tuple-element.42), channel_id=1, source_target_pairs={{0,2},{1,3},{2,0},{3,1},{4,6},{5,7},{6,4},{7,5},{8,24},{9,25},{10,... | collective-permute-start | bytes 786440 | tf_op jit(solution)/shard_map/ppermute | solution.py:180
  18.7 6.5 %collective-permute-start.8 = (bf16[512,256]{1,0:T(8,128)(2,1)S(1)}, bf16[512,256]{1,0:T(8,128)(2,1)S(1)}, u32[]{:S(2)}, u32[]{:S(2)}) collective-permute-start(bf16[512,256]{1,0:T(8,128)(2,1)S(1)} %add_convert_fusion), channel_id=1, source_target_pairs={{0,1},{1,0},{2,3},{3,2},{4,5},{5,4},{6,7},{7,6},{8,9},{9,8},{10,11... | collective-permute-start | bytes 786440 | tf_op jit(solution)/shard_map/ppermute | solution.py:180
  23.2 6.4 %collective-permute-start.6 = (bf16[512,256]{1,0:T(8,128)(2,1)S(1)}, bf16[512,256]{1,0:T(8,128)(2,1)S(1)}, u32[]{:S(2)}, u32[]{:S(2)}) collective-permute-start(bf16[512,256]{1,0:T(8,128)(2,1)S(1)} %get-tuple-element.54), channel_id=1, source_target_pairs={{0,1},{1,0},{2,3},{3,2},{4,5},{5,4},{6,7},{7,6},{8,10},{9,11},{10,... | collective-permute-start | bytes 786440 | tf_op jit(solution)/shard_map/ppermute | solution.py:180
  29.8 7.5 %collective-permute-start.10 = (bf16[256,256]{1,0:T(8,128)(2,1)S(1)}, bf16[256,256]{1,0:T(8,128)(2,1)S(1)}, u32[]{:S(2)}, u32[]{:S(2)}) collective-permute-start(bf16[256,256]{1,0:T(8,128)(2,1)S(1)} %get-tuple-element.56), channel_id=1, source_target_pairs={{0,16},{1,17},{2,18},{3,19},{4,20},{5,21},{6,22},{7,23},{8,12},{9,... | collective-permute-start | bytes 393224 | tf_op jit(solution)/shard_map/ppermute | solution.py:180
  31.9 5.5 %collective-permute-start.9 = (bf16[256,256]{1,0:T(8,128)(2,1)S(1)}, bf16[256,256]{1,0:T(8,128)(2,1)S(1)}, u32[]{:S(2)}, u32[]{:S(2)}) collective-permute-start(bf16[256,256]{1,0:T(8,128)(2,1)S(1)} %get-tuple-element.57), channel_id=1, source_target_pairs={{0,1},{1,0},{2,3},{3,2},{4,5},{5,4},{6,7},{7,6},{8,12},{9,13},{10,... | collective-permute-start | bytes 393224 | tf_op jit(solution)/shard_map/ppermute | solution.py:180
  33.4 3.9 %collective-permute-start.11 = (bf16[32,512]{1,0:T(8,128)(2,1)S(1)}, bf16[32,512]{1,0:T(8,128)(2,1)S(1)}, u32[]{:S(2)}, u32[]{:S(2)}) collective-permute-start(bf16[32,512]{1,0:T(8,128)(2,1)S(1)} %get-tuple-element.47), channel_id=1, source_target_pairs={{0,16},{1,17},{2,18},{3,19},{4,20},{5,21},{6,22},{7,23},{8,24},{9,... | collective-permute-start | bytes 98312 | tf_op jit(solution)/shard_map/ppermute | solution.py:180
  37.3 1.4 %collective-permute-start.12 = (bf16[256,256]{1,0:T(8,128)(2,1)S(1)}, bf16[256,256]{1,0:T(8,128)(2,1)S(1)}, u32[]{:S(2)}, u32[]{:S(2)}) collective-permute-start(bf16[256,256]{1,0:T(8,128)(2,1)S(1)} %fusion.2), channel_id=1, source_target_pairs={{0,8},{1,9},{2,10},{3,11},{4,12},{5,13},{6,14},{7,15},{8,0},{9,1},... | collective-permute-start | bytes 393224 | tf_op jit(solution)/shard_map/ppermute | solution.py:180
  38.8 5.6 %collective-permute-start.13 = (bf16[256,256]{1,0:T(8,128)(2,1)S(1)}, bf16[256,256]{1,0:T(8,128)(2,1)S(1)}, u32[]{:S(2)}, u32[]{:S(2)}) collective-permute-start(bf16[256,256]{1,0:T(8,128)(2,1)S(1)} %add_convert_fusion.2), channel_id=1, source_target_pairs={{0,16},{1,17},{2,18},{3,19},{4,20},{5,21},{6,22},{7,23},{8,24},{9,... | collective-permute-start | bytes 393224 | tf_op jit(solution)/shard_map/ppermute | solution.py:180
  44.4 1.6 %collective-permute-start.14 = (bf16[2,256,256]{2,1,0:T(8,128)(2,1)S(1)}, bf16[2,256,256]{2,1,0:T(8,128)(2,1)S(1)}, u32[]{:S(2)}, u32[]{:S(2)}) collective-permute-start(bf16[2,256,256]{2,1,0:T(8,128)(2,1)S(1)} %pad_maximum_fusion.pair_ref), channel_id=1, source_target_pairs={{0,8},{1,9},{2,10},{3,11},{4,12},{5,13},{6,14},{7,15},{8,0},{9,1},... | collective-permute-start | bytes 786440 | tf_op jit(solution)/shard_map/ppermute | solution.py:180

commit v15 on v14

--- a/solution.py
+++ b/solution.py
@@ -97,7 +97,7 @@
 def front_kernel(
     per_group, loss_hbm, exponent_hbm, start_hbm, rows_hbm, q_hbm, k_hbm, g_hbm, ids_hbm, index_hbm, *rest
 ):
-    v_ref, odd_ref, loss_ref, exponent_ref, start_ref, rows_ref, q_ref, k_ref, g_ref, ids_ref, index_ref, sems = rest
+    v_ref, lead_ref, loss_ref, exponent_ref, start_ref, rows_ref, q_ref, k_ref, g_ref, ids_ref, index_ref, sems = rest
     count = 0
 
     def begin(source, target):
@@ -123,7 +123,7 @@
             begin(source.at[span, :], target.at[span, :])
             for source, target in ((q_hbm, q_ref), (k_hbm, k_ref), (g_hbm, g_ref))
         ])
-    odd_ref[...] = jnp.broadcast_to((lax.axis_index("dp") & 1).astype(F32), odd_ref.shape)
+    lead_ref[...] = jnp.broadcast_to((1 - (lax.axis_index("dp") & 1)).astype(F32), lead_ref.shape)
     for copy in small:
         copy.wait()
     masks = [
@@ -174,11 +174,11 @@
 CORE, Y, X, Z1, Z2 = 8, 16, 1, 2, 4
 
 
-def routed(value, odd, even):
+def routed(value, lead, other):
     owners = lax.axis_size("fsdp")
     count = lax.axis_size("dp") * owners
     return lax.ppermute(
-        value, ("dp", "fsdp"), [(i, i ^ (odd if i // owners % 2 else even)) for i in range(count)]
+        value, ("dp", "fsdp"), [(i, i ^ (other if i // owners % 2 else lead)) for i in range(count)]
     )
 
 
@@ -189,16 +189,16 @@
 def partial_kernel(parts, own_ref, near_ref, v0_ref, v1_ref, *out_refs):
     dp = lax.axis_index("dp")
     fsdp = lax.axis_index("fsdp")
-    odd = dp & 1
+    core = dp & 1
 
     def pick(choices):
-        return choices[0] + odd * (choices[1] - choices[0])
+        return choices[0] + core * (choices[1] - choices[0])
 
     for units, out_ref in zip(parts, out_refs):
-        for number, (odd_unit, even_unit) in enumerate(units):
-            z, y, x, part = (pick(pair) for pair in zip(even_unit, odd_unit))
+        for number, (lead_unit, other_unit) in enumerate(units):
+            z, y, x, part = (pick(pair) for pair in zip(lead_unit, other_unit))
             owner = fsdp ^ (z * 2 + x)
-            quarter = (dp - odd) ^ (y * 2)
+            quarter = (dp - core) ^ (y * 2)
             column = pl.ds(pl.multiple_of(owner * (4 * LANE) + quarter * LANE, 2 * LANE), 2 * LANE)
             some = pl.ds(pl.multiple_of(part * (2 * LANE), 2 * LANE), 2 * LANE)
             total = lax.dot_general(
@@ -288,7 +288,7 @@
 
 def place_kernel(pair_ref, near_ref, out_ref):
     dp = lax.axis_index("dp")
-    for ref, part in ((pair_ref, dp & 1), (near_ref, 1 - (dp & 1))):
+    for ref, part in ((pair_ref, 1 - (dp & 1)), (near_ref, dp & 1)):
         some = pl.ds(pl.multiple_of(part * (2 * LANE), 2 * LANE), 2 * LANE)
         for flip in range(2):
             rows = pl.ds(pl.multiple_of(((dp >> 1) ^ flip) * (2 * LANE), 2 * LANE), 2 * LANE)
@@ -307,8 +307,8 @@
     )(pair, near)
 
 
-def fold_kernel(base_ref, arrived_ref, odd_ref, out_ref):
-    out_ref[...] = jnp.where(odd_ref[:1, :] > 0.5, arrived_ref[...].astype(F32), base_ref[...])
+def fold_kernel(base_ref, arrived_ref, lead_ref, out_ref):
+    out_ref[...] = jnp.where(lead_ref[:1, :] > 0.5, arrived_ref[...].astype(F32), base_ref[...])
 
 
 def fold(base, arrived, odd):
@@ -325,8 +325,8 @@
 
 def reduce_by_axis(layer_input, *args):
     near = xor_permute(layer_input, CORE)
-    v0, odd_row = front(*args)
-    odd = odd_row[:1] > 0.5
+    v0, lead_row = front(*args)
+    lead = lead_row[:1] > 0.5
     v1 = xor_permute(v0, CORE)
     both = 2 * LANE
 
@@ -373,14 +373,14 @@
     joined = routed(joined, Z1, X)
     rest = add(keep4, fifth, sixth)
     crossing = add(rest, joined)
-    last1 = jnp.where(odd, crossing[:both], rest[:both]).astype(BF16)
+    last1 = jnp.where(lead, crossing[:both], rest[:both]).astype(BF16)
     last2 = crossing[both:].astype(BF16)
     window = xor_permute(after_all(window, last1, last2)[0], Y)
     last1 = routed(last1, Z2, Y)
     last2 = routed(last2, Z2, X)
     last1, window = after_all(last1, window)
-    crossed = xor_permute(jnp.where(odd, last1, add(rest[both:], last1).astype(BF16)), CORE)
-    base = fold(add(some[both:], joined[:both]), last2, odd_row)
+    crossed = xor_permute(jnp.where(lead, last1, add(rest[both:], last1).astype(BF16)), CORE)
+    base = fold(add(some[both:], joined[:both]), last2, lead_row)
     mine = add(base, crossed).astype(BF16)
     from_y = xor_permute(mine, Y)
     value_grad = outer_swap(v0, rows, after_all(window, from_y)[0])

time: 47.2 us -> 46.7 us (0.989)
  waiting for transfers between devices: 20.3 us -> 19.5 us
    ppermute x15, waiting for transfers between devices: 20.3 us -> 19.5 us  [routed(): lax.ppermute(value, ('dp', 'fsdp'), [(i, i ^ (other if i // owners % 2 el...]
  transfers between devices with their start and end apart: 15 -> 15, of which waited for: 8 -> 11; matrix products, arithmetic and copies ran while one was open for 1% -> 1% of each run, Pallas kernels for 12% -> 12%
where the time goes in v15:
time: 46.7 us; the launch traced here: 46.5 us
  waiting for transfers between devices  19.5 us (42%)
  starting transfers between devices  17.9 us (38%)
  Pallas kernels  7.11 us (15%)
  between operations  1.51 us (3%)
  other arithmetic  0.51 us (1%)
    ppermute x15, waiting for transfers between devices, routed(): lax.ppermute(value, ('dp', 'fsdp'), [(i, i ^ (other if i // owners % 2 el...  19.5 us
    ppermute x15, starting transfers between devices, routed(): lax.ppermute(value, ('dp', 'fsdp'), [(i, i ^ (other if i // owners % 2 el...  17.9 us
    pallas_call x1, Pallas kernels, front(): pl.pallas_call(functools.partial(front_kernel, per_group), in_specs=[HBM]...  2.64 us
    pallas_call x4, Pallas kernels, partial_sums(): pl.pallas_call(functools.partial(partial_kernel, parts), in_specs=[VMEM]...  2.16 us
    pallas_call x1, Pallas kernels, place(): pl.pallas_call(place_kernel, in_specs=[VMEM] * 2, out_specs=VMEM, out_sha...  1.05 us
  transfers between devices with their start and end apart: 15, of which 11 were waited for; matrix products, arithmetic and copies ran while one was open for 1% of the time, Pallas kernels for 12%

profile of v15, /device:TPU:0, one launch (start us, length us, event | category | flops | bytes accessed | tf_op | source)
XLA Modules:
  0.0 46.5 jit_solution(13983432854376371749)
XLA Ops:
  0.6 0.0 copy-start
  0.6 0.5 %collective-permute-start = (bf16[256,4096]{1,0:T(8,128)(2,1)}, bf16[256,4096]{1,0:T(8,128)(2,1)S(1)}, u32[]{:S(2)}, u32[]{:S(2)}) collective-permute-start(bf16[256,4096]{1,0:T(8,128)(2,1)} %own_ref.7), channel_id=1, source_target_pairs={{0,8},{1,9},{2,10},{3,11},{4,12},{5,13},{6,14},{7,15},{8,0},{9,1},... | collective-permute-start | bytes 6291464 | tf_op jit(solution)/shard_map/ppermute | solution.py:180
  1.9 2.6 %front.1 = (bf16[272,512]{1,0:T(8,128)(2,1)S(1)}, f32[8,256]{1,0:T(8,128)S(1)}) custom-call(f32[16]{0:T(128)} %loss_hbm.1, s32[1]{0:T(128)S(6)} %copy.12.exponent_hbm, s32[1,2]{1,0:T(1,128)} %start_hbm.1, s32[1,2]{1,0:T(1,128)} %rows_hbm.1, bf16[256,2048]{1,0:T(8,128)(2,1)} %q_hbm.1, bf16[256,512]{1,0:T(8,128)(2,1)} %k_hbm.1, bf16[256,2048]{1,0:T(8,128)(2,1)} %g_hbm.1, ...), custom_call_target="tpu_custom_call" | custom-call | tf_op jit(solution)/shard_map/front/pallas_call | solution.py:154
  4.6 0.1 collective-permute-start.1
  4.7 1.5 %collective-permute-done.1.v1_ref = bf16[272,512]{1,0:T(8,128)(2,1)S(1)} collective-permute-done((bf16[272,512]{1,0:T(8,128)(2,1)S(1)}, bf16[272,512]{1,0:T(8,128)(2,1)S(1)}, u32[]{:S(2)}, u32[]{:S(2)}) %collective-permute-start.1) | collective-permute-done | bytes 278560 | tf_op jit(solution)/shard_map/ppermute | solution.py:180
  6.2 0.0 collective-permute-done.near_ref
  6.2 0.0 copy-done
  6.2 0.5 %partial_sums.7 = (bf16[512,256]{1,0:T(8,128)(2,1)S(1)}, bf16[512,256]{1,0:T(8,128)(2,1)S(1)}) custom-call(bf16[256,4096]{1,0:T(8,128)(2,1)S(1)} %copy-done, bf16[256,4096]{1,0:T(8,128)(2,1)S(1)} %collective-permute-done.near_ref, bf16[272,512]{1,0:T(8,128)(2,1)S(1)} %get-tuple-element.33.v0_ref, bf16[272,512]{1,0:T(8,128)(2,1)S(1)} %collective-permute-done.1.v1_ref), custom_call_target="tpu_custom_call" | custom-call | tf_op jit(solution)/shard_map/partial_sums/pallas_call | solution.py:214
  6.7 2.6 %collective-permute-start.3 = (bf16[512,256]{1,0:T(8,128)(2,1)S(1)}, bf16[512,256]{1,0:T(8,128)(2,1)S(1)}, u32[]{:S(2)}, u32[]{:S(2)}) collective-permute-start(bf16[512,256]{1,0:T(8,128)(2,1)S(1)} %get-tuple-element.31), channel_id=1, source_target_pairs={{0,1},{1,0},{2,3},{3,2},{4,5},{5,4},{6,7},{7,6},{8,10},{9,11},{10,... | collective-permute-start | bytes 786440 | tf_op jit(solution)/shard_map/ppermute | solution.py:180
  9.3 1.5 %collective-permute-start.5 = (bf16[512,256]{1,0:T(8,128)(2,1)S(1)}, bf16[512,256]{1,0:T(8,128)(2,1)S(1)}, u32[]{:S(2)}, u32[]{:S(2)}) collective-permute-start(bf16[512,256]{1,0:T(8,128)(2,1)S(1)} %get-tuple-element.36), channel_id=1, source_target_pairs={{0,16},{1,17},{2,18},{3,19},{4,20},{5,21},{6,22},{7,23},{8,10},{9,... | collective-permute-start | bytes 786440 | tf_op jit(solution)/shard_map/ppermute | solution.py:180
  10.8 0.5 %partial_sums.5 = (bf16[512,256]{1,0:T(8,128)(2,1)S(1)}, bf16[512,256]{1,0:T(8,128)(2,1)S(1)}) custom-call(bf16[256,4096]{1,0:T(8,128)(2,1)S(1)} %copy-done, bf16[256,4096]{1,0:T(8,128)(2,1)S(1)} %collective-permute-done.near_ref, bf16[272,512]{1,0:T(8,128)(2,1)S(1)} %get-tuple-element.33.v0_ref, bf16[272,512]{1,0:T(8,128)(2,1)S(1)} %collective-permute-done.1.v1_ref), custom_call_target="tpu_custom_call" | custom-call | tf_op jit(solution)/shard_map/partial_sums/pallas_call | solution.py:214
  11.4 0.6 %collective-permute-start.2 = (bf16[512,256]{1,0:T(8,128)(2,1)S(1)}, bf16[512,256]{1,0:T(8,128)(2,1)S(1)}, u32[]{:S(2)}, u32[]{:S(2)}) collective-permute-start(bf16[512,256]{1,0:T(8,128)(2,1)S(1)} %get-tuple-element.29), channel_id=1, source_target_pairs={{0,1},{1,0},{2,3},{3,2},{4,5},{5,4},{6,7},{7,6},{8,10},{9,11},{10,... | collective-permute-start | bytes 786440 | tf_op jit(solution)/shard_map/ppermute | solution.py:180
  12.0 0.5 %partial_sums.6 = (f32[512,256]{1,0:T(8,128)S(1)}, f32[512,256]{1,0:T(8,128)S(1)}) custom-call(bf16[256,4096]{1,0:T(8,128)(2,1)S(1)} %copy-done, bf16[256,4096]{1,0:T(8,128)(2,1)S(1)} %collective-permute-done.near_ref, bf16[272,512]{1,0:T(8,128)(2,1)S(1)} %get-tuple-element.33.v0_ref, bf16[272,512]{1,0:T(8,128)(2,1)S(1)} %collective-permute-done.1.v1_ref), custom_call_target="tpu_custom_call" | custom-call | tf_op jit(solution)/shard_map/partial_sums/pallas_call | solution.py:214
  12.5 1.2 %collective-permute-done.3 = bf16[512,256]{1,0:T(8,128)(2,1)S(1)} collective-permute-done((bf16[512,256]{1,0:T(8,128)(2,1)S(1)}, bf16[512,256]{1,0:T(8,128)(2,1)S(1)}, u32[]{:S(2)}, u32[]{:S(2)}) %collective-permute-start.3) | collective-permute-done | bytes 262176 | tf_op jit(solution)/shard_map/ppermute | solution.py:180
  13.7 0.1 add_convert_fusion.1
  13.7 2.1 %collective-permute-start.4 = (bf16[512,256]{1,0:T(8,128)(2,1)S(1)}, bf16[512,256]{1,0:T(8,128)(2,1)S(1)}, u32[]{:S(2)}, u32[]{:S(2)}) collective-permute-start(bf16[512,256]{1,0:T(8,128)(2,1)S(1)} %add_convert_fusion.1), channel_id=1, source_target_pairs={{0,16},{1,17},{2,18},{3,19},{4,20},{5,21},{6,22},{7,23},{8,24},{9,... | collective-permute-start | bytes 786440 | tf_op jit(solution)/shard_map/ppermute | solution.py:180
  15.8 0.5 %partial_sums.4 = (f32[512,256]{1,0:T(8,128)S(1)}, f32[512,256]{1,0:T(8,128)S(1)}) custom-call(bf16[256,4096]{1,0:T(8,128)(2,1)S(1)} %copy-done, bf16[256,4096]{1,0:T(8,128)(2,1)S(1)} %collective-permute-done.near_ref, bf16[272,512]{1,0:T(8,128)(2,1)S(1)} %get-tuple-element.33.v0_ref, bf16[272,512]{1,0:T(8,128)(2,1)S(1)} %collective-permute-done.1.v1_ref), custom_call_target="tpu_custom_call" | custom-call | tf_op jit(solution)/shard_map/partial_sums/pallas_call | solution.py:214
  16.4 0.3 inner_swap.1
  16.7 0.0 collective-permute-done.5
  16.7 0.1 add_convert_fusion
  16.8 0.6 %collective-permute-start.7 = (bf16[512,256]{1,0:T(8,128)(2,1)S(1)}, bf16[512,256]{1,0:T(8,128)(2,1)S(1)}, u32[]{:S(2)}, u32[]{:S(2)}) collective-permute-start(bf16[512,256]{1,0:T(8,128)(2,1)S(1)} %get-tuple-element.42), channel_id=1, source_target_pairs={{0,16},{1,17},{2,18},{3,19},{4,20},{5,21},{6,22},{7,23},{8,10},{9,... | collective-permute-start | bytes 786440 | tf_op jit(solution)/shard_map/ppermute | solution.py:180
  17.3 1.5 %collective-permute-start.8 = (bf16[512,256]{1,0:T(8,128)(2,1)S(1)}, bf16[512,256]{1,0:T(8,128)(2,1)S(1)}, u32[]{:S(2)}, u32[]{:S(2)}) collective-permute-start(bf16[512,256]{1,0:T(8,128)(2,1)S(1)} %add_convert_fusion), channel_id=1, source_target_pairs={{0,1},{1,0},{2,3},{3,2},{4,5},{5,4},{6,7},{7,6},{8,9},{9,8},{10,11... | collective-permute-start | bytes 786440 | tf_op jit(solution)/shard_map/ppermute | solution.py:180
  18.9 0.0 collective-permute-done.2
  18.9 3.0 %collective-permute-done.4 = bf16[512,256]{1,0:T(8,128)(2,1)S(1)} collective-permute-done((bf16[512,256]{1,0:T(8,128)(2,1)S(1)}, bf16[512,256]{1,0:T(8,128)(2,1)S(1)}, u32[]{:S(2)}, u32[]{:S(2)}) %collective-permute-start.4) | collective-permute-done | bytes 262176 | tf_op jit(solution)/shard_map/ppermute | solution.py:180
  21.9 0.1 fusion.3
  22.0 1.8 %collective-permute-start.6 = (bf16[512,256]{1,0:T(8,128)(2,1)S(1)}, bf16[512,256]{1,0:T(8,128)(2,1)S(1)}, u32[]{:S(2)}, u32[]{:S(2)}) collective-permute-start(bf16[512,256]{1,0:T(8,128)(2,1)S(1)} %get-tuple-element.54), channel_id=1, source_target_pairs={{0,2},{1,3},{2,0},{3,1},{4,6},{5,7},{6,4},{7,5},{8,9},{9,8},{10,11... | collective-permute-start | bytes 786440 | tf_op jit(solution)/shard_map/ppermute | solution.py:180
  23.8 0.9 %collective-permute-done.7 = bf16[512,256]{1,0:T(8,128)(2,1)S(1)} collective-permute-done((bf16[512,256]{1,0:T(8,128)(2,1)S(1)}, bf16[512,256]{1,0:T(8,128)(2,1)S(1)}, u32[]{:S(2)}, u32[]{:S(2)}) %collective-permute-start.7) | collective-permute-done | bytes 262176 | tf_op jit(solution)/shard_map/ppermute | solution.py:180
  24.7 1.7 %collective-permute-done.8 = bf16[512,256]{1,0:T(8,128)(2,1)S(1)} collective-permute-done((bf16[512,256]{1,0:T(8,128)(2,1)S(1)}, bf16[512,256]{1,0:T(8,128)(2,1)S(1)}, u32[]{:S(2)}, u32[]{:S(2)}) %collective-permute-start.8) | collective-permute-done | bytes 262176 | tf_op jit(solution)/shard_map/ppermute | solution.py:180
  26.4 2.0 %collective-permute-done.6 = bf16[512,256]{1,0:T(8,128)(2,1)S(1)} collective-permute-done((bf16[512,256]{1,0:T(8,128)(2,1)S(1)}, bf16[512,256]{1,0:T(8,128)(2,1)S(1)}, u32[]{:S(2)}, u32[]{:S(2)}) %collective-permute-start.6) | collective-permute-done | bytes 262176 | tf_op jit(solution)/shard_map/ppermute | solution.py:180
  28.4 0.1 convert_add_fusion
  28.6 2.8 %collective-permute-start.10 = (bf16[256,256]{1,0:T(8,128)(2,1)S(1)}, bf16[256,256]{1,0:T(8,128)(2,1)S(1)}, u32[]{:S(2)}, u32[]{:S(2)}) collective-permute-start(bf16[256,256]{1,0:T(8,128)(2,1)S(1)} %get-tuple-element.56), channel_id=1, source_target_pairs={{0,4},{1,5},{2,6},{3,7},{4,0},{5,1},{6,2},{7,3},{8,24},{9,25},{10,... | collective-permute-start | bytes 393224 | tf_op jit(solution)/shard_map/ppermute | solution.py:180
  31.4 0.2 collective-permute-start.9
  31.6 1.7 %collective-permute-start.11 = (bf16[32,512]{1,0:T(8,128)(2,1)S(1)}, bf16[32,512]{1,0:T(8,128)(2,1)S(1)}, u32[]{:S(2)}, u32[]{:S(2)}) collective-permute-start(bf16[32,512]{1,0:T(8,128)(2,1)S(1)} %get-tuple-element.47), channel_id=1, source_target_pairs={{0,16},{1,17},{2,18},{3,19},{4,20},{5,21},{6,22},{7,23},{8,24},{9,... | collective-permute-start | bytes 98312 | tf_op jit(solution)/shard_map/ppermute | solution.py:180
  33.3 2.2 %collective-permute-done.11.window_ref = bf16[32,512]{1,0:T(8,128)(2,1)S(1)} collective-permute-done((bf16[32,512]{1,0:T(8,128)(2,1)S(1)}, bf16[32,512]{1,0:T(8,128)(2,1)S(1)}, u32[]{:S(2)}, u32[]{:S(2)}) %collective-permute-start.11) | collective-permute-done | bytes 32800 | tf_op jit(solution)/shard_map/ppermute | solution.py:180
  35.5 0.4 collective-permute-done.10
  36.0 0.1 collective-permute-start.12
  36.0 2.7 %collective-permute-done.9.arrived_ref = bf16[256,256]{1,0:T(8,128)(2,1)S(1)} collective-permute-done((bf16[256,256]{1,0:T(8,128)(2,1)S(1)}, bf16[256,256]{1,0:T(8,128)(2,1)S(1)}, u32[]{:S(2)}, u32[]{:S(2)}) %collective-permute-start.9) | collective-permute-done | bytes 131104 | tf_op jit(solution)/shard_map/ppermute | solution.py:180
  38.8 0.0 collective-permute-done.12
  38.8 1.7 %collective-permute-start.13 = (bf16[256,256]{1,0:T(8,128)(2,1)S(1)}, bf16[256,256]{1,0:T(8,128)(2,1)S(1)}, u32[]{:S(2)}, u32[]{:S(2)}) collective-permute-start(bf16[256,256]{1,0:T(8,128)(2,1)S(1)} %add_convert_fusion.2), channel_id=1, source_target_pairs={{0,16},{1,17},{2,18},{3,19},{4,20},{5,21},{6,22},{7,23},{8,24},{9,... | collective-permute-start | bytes 393224 | tf_op jit(solution)/shard_map/ppermute | solution.py:180
  40.6 3.3 %collective-permute-done.13 = bf16[256,256]{1,0:T(8,128)(2,1)S(1)} collective-permute-done((bf16[256,256]{1,0:T(8,128)(2,1)S(1)}, bf16[256,256]{1,0:T(8,128)(2,1)S(1)}, u32[]{:S(2)}, u32[]{:S(2)}) %collective-permute-start.13) | collective-permute-done | bytes 131104 | tf_op jit(solution)/shard_map/ppermute | solution.py:180
  43.9 0.1 collective-permute-start.14
  44.0 0.9 %outer_swap.1 = bf16[256,512]{1,0:T(8,128)(2,1)} custom-call(bf16[272,512]{1,0:T(8,128)(2,1)S(1)} %get-tuple-element.33.v0_ref, bf16[256,512]{1,0:T(8,128)(2,1)S(1)} %get-tuple-element.49.rows_ref, bf16[32,512]{1,0:T(8,128)(2,1)S(1)} %collective-permute-done.11.window_ref), custom_call_target="tpu_custom_call" | custom-call | tf_op jit(solution)/shard_map/outer_swap/pallas_call | solution.py:278
  44.9 0.6 %collective-permute-done.14.near_ref = bf16[2,256,256]{2,1,0:T(8,128)(2,1)S(1)} collective-permute-done((bf16[2,256,256]{2,1,0:T(8,128)(2,1)S(1)}, bf16[2,256,256]{2,1,0:T(8,128)(2,1)S(1)}, u32[]{:S(2)}, u32[]{:S(2)}) %collective-permute-start.14) | collective-permute-done | bytes 262176 | tf_op jit(solution)/shard_map/ppermute | solution.py:180
  45.5 1.0 %place.1 = f32[512,512]{1,0:T(8,128)} custom-call(bf16[2,256,256]{2,1,0:T(8,128)(2,1)S(1)} %pad_maximum_fusion.pair_ref, bf16[2,256,256]{2,1,0:T(8,128)(2,1)S(1)} %collective-permute-done.14.near_ref), custom_call_target="tpu_custom_call" | custom-call | tf_op jit(solution)/shard_map/place/pallas_call | solution.py:299
  (7 shorter events, 0.2 us)
Async XLA Ops:
  0.6 5.6 %copy-start = (bf16[256,4096]{1,0:T(8,128)(2,1)S(1)}, bf16[256,4096]{1,0:T(8,128)(2,1)}, u32[]{:S(2)}) copy-start(bf16[256,4096]{1,0:T(8,128)(2,1)} %own_ref.7) | copy-start | bytes 6291460
  0.6 5.5 %collective-permute-start = (bf16[256,4096]{1,0:T(8,128)(2,1)}, bf16[256,4096]{1,0:T(8,128)(2,1)S(1)}, u32[]{:S(2)}, u32[]{:S(2)}) collective-permute-start(bf16[256,4096]{1,0:T(8,128)(2,1)} %own_ref.7), channel_id=1, source_target_pairs={{0,8},{1,9},{2,10},{3,11},{4,12},{5,13},{6,14},{7,15},{8,0},{9,1},... | collective-permute-start | bytes 6291464 | tf_op jit(solution)/shard_map/ppermute | solution.py:180
  4.6 1.6 %collective-permute-start.1 = (bf16[272,512]{1,0:T(8,128)(2,1)S(1)}, bf16[272,512]{1,0:T(8,128)(2,1)S(1)}, u32[]{:S(2)}, u32[]{:S(2)}) collective-permute-start(bf16[272,512]{1,0:T(8,128)(2,1)S(1)} %get-tuple-element.33.v0_ref), channel_id=1, source_target_pairs={{0,8},{1,9},{2,10},{3,11},{4,12},{5,13},{6,14},{7,15},{8,0},{9,1},... | collective-permute-start | bytes 835592 | tf_op jit(solution)/shard_map/ppermute | solution.py:180
  6.7 6.9 %collective-permute-start.3 = (bf16[512,256]{1,0:T(8,128)(2,1)S(1)}, bf16[512,256]{1,0:T(8,128)(2,1)S(1)}, u32[]{:S(2)}, u32[]{:S(2)}) collective-permute-start(bf16[512,256]{1,0:T(8,128)(2,1)S(1)} %get-tuple-element.31), channel_id=1, source_target_pairs={{0,1},{1,0},{2,3},{3,2},{4,5},{5,4},{6,7},{7,6},{8,10},{9,11},{10,... | collective-permute-start | bytes 786440 | tf_op jit(solution)/shard_map/ppermute | solution.py:180
  9.3 7.4 %collective-permute-start.5 = (bf16[512,256]{1,0:T(8,128)(2,1)S(1)}, bf16[512,256]{1,0:T(8,128)(2,1)S(1)}, u32[]{:S(2)}, u32[]{:S(2)}) collective-permute-start(bf16[512,256]{1,0:T(8,128)(2,1)S(1)} %get-tuple-element.36), channel_id=1, source_target_pairs={{0,16},{1,17},{2,18},{3,19},{4,20},{5,21},{6,22},{7,23},{8,10},{9,... | collective-permute-start | bytes 786440 | tf_op jit(solution)/shard_map/ppermute | solution.py:180
  11.4 7.5 %collective-permute-start.2 = (bf16[512,256]{1,0:T(8,128)(2,1)S(1)}, bf16[512,256]{1,0:T(8,128)(2,1)S(1)}, u32[]{:S(2)}, u32[]{:S(2)}) collective-permute-start(bf16[512,256]{1,0:T(8,128)(2,1)S(1)} %get-tuple-element.29), channel_id=1, source_target_pairs={{0,1},{1,0},{2,3},{3,2},{4,5},{5,4},{6,7},{7,6},{8,10},{9,11},{10,... | collective-permute-start | bytes 786440 | tf_op jit(solution)/shard_map/ppermute | solution.py:180
  13.7 8.2 %collective-permute-start.4 = (bf16[512,256]{1,0:T(8,128)(2,1)S(1)}, bf16[512,256]{1,0:T(8,128)(2,1)S(1)}, u32[]{:S(2)}, u32[]{:S(2)}) collective-permute-start(bf16[512,256]{1,0:T(8,128)(2,1)S(1)} %add_convert_fusion.1), channel_id=1, source_target_pairs={{0,16},{1,17},{2,18},{3,19},{4,20},{5,21},{6,22},{7,23},{8,24},{9,... | collective-permute-start | bytes 786440 | tf_op jit(solution)/shard_map/ppermute | solution.py:180
  16.8 7.9 %collective-permute-start.7 = (bf16[512,256]{1,0:T(8,128)(2,1)S(1)}, bf16[512,256]{1,0:T(8,128)(2,1)S(1)}, u32[]{:S(2)}, u32[]{:S(2)}) collective-permute-start(bf16[512,256]{1,0:T(8,128)(2,1)S(1)} %get-tuple-element.42), channel_id=1, source_target_pairs={{0,16},{1,17},{2,18},{3,19},{4,20},{5,21},{6,22},{7,23},{8,10},{9,... | collective-permute-start | bytes 786440 | tf_op jit(solution)/shard_map/ppermute | solution.py:180
  17.3 9.1 %collective-permute-start.8 = (bf16[512,256]{1,0:T(8,128)(2,1)S(1)}, bf16[512,256]{1,0:T(8,128)(2,1)S(1)}, u32[]{:S(2)}, u32[]{:S(2)}) collective-permute-start(bf16[512,256]{1,0:T(8,128)(2,1)S(1)} %add_convert_fusion), channel_id=1, source_target_pairs={{0,1},{1,0},{2,3},{3,2},{4,5},{5,4},{6,7},{7,6},{8,9},{9,8},{10,11... | collective-permute-start | bytes 786440 | tf_op jit(solution)/shard_map/ppermute | solution.py:180
  22.0 6.4 %collective-permute-start.6 = (bf16[512,256]{1,0:T(8,128)(2,1)S(1)}, bf16[512,256]{1,0:T(8,128)(2,1)S(1)}, u32[]{:S(2)}, u32[]{:S(2)}) collective-permute-start(bf16[512,256]{1,0:T(8,128)(2,1)S(1)} %get-tuple-element.54), channel_id=1, source_target_pairs={{0,2},{1,3},{2,0},{3,1},{4,6},{5,7},{6,4},{7,5},{8,9},{9,8},{10,11... | collective-permute-start | bytes 786440 | tf_op jit(solution)/shard_map/ppermute | solution.py:180
  28.6 7.3 %collective-permute-start.10 = (bf16[256,256]{1,0:T(8,128)(2,1)S(1)}, bf16[256,256]{1,0:T(8,128)(2,1)S(1)}, u32[]{:S(2)}, u32[]{:S(2)}) collective-permute-start(bf16[256,256]{1,0:T(8,128)(2,1)S(1)} %get-tuple-element.56), channel_id=1, source_target_pairs={{0,4},{1,5},{2,6},{3,7},{4,0},{5,1},{6,2},{7,3},{8,24},{9,25},{10,... | collective-permute-start | bytes 393224 | tf_op jit(solution)/shard_map/ppermute | solution.py:180
  31.4 7.3 %collective-permute-start.9 = (bf16[256,256]{1,0:T(8,128)(2,1)S(1)}, bf16[256,256]{1,0:T(8,128)(2,1)S(1)}, u32[]{:S(2)}, u32[]{:S(2)}) collective-permute-start(bf16[256,256]{1,0:T(8,128)(2,1)S(1)} %get-tuple-element.57), channel_id=1, source_target_pairs={{0,4},{1,5},{2,6},{3,7},{4,0},{5,1},{6,2},{7,3},{8,9},{9,8},{10,11... | collective-permute-start | bytes 393224 | tf_op jit(solution)/shard_map/ppermute | solution.py:180
  31.6 3.9 %collective-permute-start.11 = (bf16[32,512]{1,0:T(8,128)(2,1)S(1)}, bf16[32,512]{1,0:T(8,128)(2,1)S(1)}, u32[]{:S(2)}, u32[]{:S(2)}) collective-permute-start(bf16[32,512]{1,0:T(8,128)(2,1)S(1)} %get-tuple-element.47), channel_id=1, source_target_pairs={{0,16},{1,17},{2,18},{3,19},{4,20},{5,21},{6,22},{7,23},{8,24},{9,... | collective-permute-start | bytes 98312 | tf_op jit(solution)/shard_map/ppermute | solution.py:180
  36.0 2.8 %collective-permute-start.12 = (bf16[256,256]{1,0:T(8,128)(2,1)S(1)}, bf16[256,256]{1,0:T(8,128)(2,1)S(1)}, u32[]{:S(2)}, u32[]{:S(2)}) collective-permute-start(bf16[256,256]{1,0:T(8,128)(2,1)S(1)} %fusion.2), channel_id=1, source_target_pairs={{0,8},{1,9},{2,10},{3,11},{4,12},{5,13},{6,14},{7,15},{8,0},{9,1},... | collective-permute-start | bytes 393224 | tf_op jit(solution)/shard_map/ppermute | solution.py:180
  38.8 5.0 %collective-permute-start.13 = (bf16[256,256]{1,0:T(8,128)(2,1)S(1)}, bf16[256,256]{1,0:T(8,128)(2,1)S(1)}, u32[]{:S(2)}, u32[]{:S(2)}) collective-permute-start(bf16[256,256]{1,0:T(8,128)(2,1)S(1)} %add_convert_fusion.2), channel_id=1, source_target_pairs={{0,16},{1,17},{2,18},{3,19},{4,20},{5,21},{6,22},{7,23},{8,24},{9,... | collective-permute-start | bytes 393224 | tf_op jit(solution)/shard_map/ppermute | solution.py:180
  43.9 1.6 %collective-permute-start.14 = (bf16[2,256,256]{2,1,0:T(8,128)(2,1)S(1)}, bf16[2,256,256]{2,1,0:T(8,128)(2,1)S(1)}, u32[]{:S(2)}, u32[]{:S(2)}) collective-permute-start(bf16[2,256,256]{2,1,0:T(8,128)(2,1)S(1)} %pad_maximum_fusion.pair_ref), channel_id=1, source_target_pairs={{0,8},{1,9},{2,10},{3,11},{4,12},{5,13},{6,14},{7,15},{8,0},{9,1},... | collective-permute-start | bytes 786440 | tf_op jit(solution)/shard_map/ppermute | solution.py:180

commit v16 on v9

--- a/solution.py
+++ b/solution.py
@@ -273,22 +273,30 @@
     )(v0, rows, window)
 
 
-def place_kernel(mine_ref, y_ref, near_ref, out_ref):
-    dp = lax.axis_index("dp")
-    for flip, block in ((0, mine_ref), (2, y_ref), (1, near_ref.at[0]), (3, near_ref.at[1])):
-        out_ref[pl.ds(pl.multiple_of((dp ^ flip) * LANE, LANE), LANE), :] = block[...].astype(F32)
-
-
-def place(mine, from_y, near):
-    return pl.pallas_call(
-        place_kernel,
-        in_specs=[VMEM] * 3,
-        out_specs=VMEM,
+def place_kernel(core, pair_ref, *rest):
+    *_, out_ref, wide, sems = rest
+    copies = []
+    for y in range(2):
+        wide[y] = pair_ref[y].astype(F32)
+        row = pl.multiple_of((lax.axis_index("dp") ^ (y << 1 | core)) * LANE, LANE)
+        copies.append(pltpu.make_async_copy(wide.at[y], out_ref.at[pl.ds(row, LANE), :], sems.at[y]))
+        copies[-1].start()
+    for copy in copies:
+        copy.wait()
+
+
+def place(core, pair, *placed):
+    return pl.pallas_call(
+        functools.partial(place_kernel, core),
+        in_specs=[VMEM] + [HBM] * len(placed),
+        out_specs=HBM,
         out_shape=jax.ShapeDtypeStruct((512, 512), F32),
+        scratch_shapes=[pltpu.VMEM((2, LANE, 512), F32), pltpu.SemaphoreType.DMA((2,))],
+        input_output_aliases={1: 0} if placed else {},
         compiler_params=pltpu.CompilerParams(vmem_limit_bytes=8 * MIB),
         cost_estimate=FREE,
         name="place",
-    )(mine, from_y, near)
+    )(pair, *placed)
 
 
 def fold_kernel(base_ref, arrived_ref, out_ref):
@@ -312,8 +320,8 @@
     v0 = front(*args)
     v1 = xor_permute(v0, CORE)
 
-    def sums(parts, dtype):
-        return partial_sums(parts, dtype, layer_input, near, v0, v1)
+    def sums(parts, dtype, v=v0):
+        return partial_sums(parts, dtype, layer_input, near, v, v1)
 
     def after_all(*values):
         return lax.optimization_barrier(values)
@@ -324,9 +332,11 @@
             total = total + term.astype(F32)
         return total
 
-    first_b, first_a = sums([(((3, 1, 1), (3, 0, 1)), 0, 512), (((2, 1, 1), (2, 1, 0)), 0, 512)], BF16)
+    first_b, = sums([(((3, 1, 1), (3, 0, 1)), 0, 512)], BF16)
+    first_a, = sums([(((2, 1, 1), (2, 1, 0)), 0, 512)], BF16)
     every = ((1, 1), (1, 0), (0, 1), (0, 0))
-    pair_some, pair_rest = sums([(tuple((1, *at) for at in every), start, 256) for start in (0, 256)], BF16)
+    pair_some, = sums([(tuple((1, *at) for at in every), 0, 256)], BF16)
+    pair_rest, = sums([(tuple((1, *at) for at in every), 256, 256)], BF16, after_all(v0, pair_some)[0])
     keep_b, keep_a = sums([(((3, 1, 0), (3, 0, 0)), 0, 512), (((2, 0, 1), (2, 0, 0)), 0, 512)], F32)
     own_some, own_rest = sums([(tuple((0, *at) for at in every), start, 256) for start in (0, 256)], F32)
     first_b = xor_permute(first_b, X)
@@ -358,8 +368,13 @@
     base = jnp.concatenate([add(some[3 * LANE:], some_in[LANE:]), add(rest_own, rest_in[LANE:])], axis=1)
     mine = add(fold(base, z2), jnp.concatenate([some_on, rest_on], axis=1)).astype(BF16)
     from_y = xor_permute(mine, Y)
-    value_grad = outer_swap(v0, rows, after_all(window, from_y)[0])
-    return place(mine, from_y, xor_permute(jnp.stack([mine, from_y]), CORE)), value_grad
+    value_grad = outer_swap(v0, rows, after_all(window, mine)[0])
+    from_y, value_grad = after_all(from_y, value_grad)
+    pair = jnp.stack([mine, from_y])
+    near_pair = xor_permute(pair, CORE)
+    half = place(0, pair)
+    near_pair, half = after_all(near_pair, half)
+    return place(1, near_pair, half), value_grad
 
 
 def swapped(block, axis, distance):

time: 44.5 us -> 43.9 us (0.987)
  waiting for transfers between devices: 14.7 us -> 13.5 us
  Pallas kernels: 6.89 us -> 7.94 us
  starting transfers between devices: 20.8 us -> 20.3 us
    ppermute x17, waiting for transfers between devices: 14.7 us -> 13.5 us  [xor_permute(): lax.ppermute(value, ('dp', 'fsdp'), [(i, i ^ mask) for i in range(count)])]
    pallas_call x1 -> x2, Pallas kernels: 1.05 us -> 1.65 us  [place(): pl.pallas_call(functools.partial(place_kernel, core), in_specs=[VMEM] + [...]
    ppermute x17, starting transfers between devices: 20.8 us -> 20.3 us  [xor_permute(): lax.ppermute(value, ('dp', 'fsdp'), [(i, i ^ mask) for i in range(count)])]
    pallas_call x4 -> x6, Pallas kernels: 1.94 us -> 2.39 us  [partial_sums(): pl.pallas_call(functools.partial(partial_kernel, parts), in_specs=[VMEM]...]
  transfers between devices with their start and end apart: 17 -> 17, of which waited for: 10 -> 10; matrix products, arithmetic and copies ran while one was open for 1% -> 1% of each run, Pallas kernels for 12% -> 16%
where the time goes in v16:
time: 43.9 us; the launch traced here: 43.7 us
  starting transfers between devices  20.3 us (46%)
  waiting for transfers between devices  13.5 us (31%)
  Pallas kernels  7.94 us (18%)
  between operations  1.57 us (4%)
    ppermute x17, starting transfers between devices, xor_permute(): lax.ppermute(value, ('dp', 'fsdp'), [(i, i ^ mask) for i in range(count)])  20.3 us
    ppermute x17, waiting for transfers between devices, xor_permute(): lax.ppermute(value, ('dp', 'fsdp'), [(i, i ^ mask) for i in range(count)])  13.5 us
    pallas_call x1, Pallas kernels, front(): pl.pallas_call(functools.partial(front_kernel, per_group), in_specs=[HBM]...  2.64 us
    pallas_call x6, Pallas kernels, partial_sums(): pl.pallas_call(functools.partial(partial_kernel, parts), in_specs=[VMEM]...  2.39 us
    pallas_call x2, Pallas kernels, place(): pl.pallas_call(functools.partial(place_kernel, core), in_specs=[VMEM] + [...  1.65 us
    pallas_call x1, Pallas kernels, outer_swap(): pl.pallas_call(outer_swap_kernel, in_specs=[VMEM] * 3, out_specs=VMEM, ou...  0.91 us
  transfers between devices with their start and end apart: 17, of which 10 were waited for; matrix products, arithmetic and copies ran while one was open for 1% of the time, Pallas kernels for 16%

profile of v16, /device:TPU:0, one launch (start us, length us, event | category | flops | bytes accessed | tf_op | source)
XLA Modules:
  0.0 43.7 jit_solution(7615261298620597339)
XLA Ops:
  0.6 0.5 %collective-permute-start = (bf16[256,4096]{1,0:T(8,128)(2,1)}, bf16[256,4096]{1,0:T(8,128)(2,1)S(1)}, u32[]{:S(2)}, u32[]{:S(2)}) collective-permute-start(bf16[256,4096]{1,0:T(8,128)(2,1)} %own_ref.11), channel_id=1, source_target_pairs={{0,8},{1,9},{2,10},{3,11},{4,12},{5,13},{6,14},{7,15},{8,0},{9,1},... | collective-permute-start | bytes 6291464 | tf_op jit(solution)/shard_map/ppermute | solution.py:176
  1.9 2.6 %front.1.v0_ref = bf16[272,512]{1,0:T(8,128)(2,1)S(1)} custom-call(f32[16]{0:T(128)} %loss_hbm.1, s32[1]{0:T(128)S(6)} %copy.14.exponent_hbm, s32[1,2]{1,0:T(1,128)} %start_hbm.1, s32[1,2]{1,0:T(1,128)} %rows_hbm.1, bf16[256,2048]{1,0:T(8,128)(2,1)} %q_hbm.1, bf16[256,512]{1,0:T(8,128)(2,1)} %k_hbm.1, bf16[256,2048]{1,0:T(8,128)(2,1)} %g_hbm.1, ...), custom_call_target="tpu_custom_call" | custom-call | tf_op jit(solution)/shard_map/front/pallas_call | solution.py:153
  4.6 0.1 collective-permute-start.1
  4.7 1.5 %collective-permute-done.1.v1_ref = bf16[272,512]{1,0:T(8,128)(2,1)S(1)} collective-permute-done((bf16[272,512]{1,0:T(8,128)(2,1)S(1)}, bf16[272,512]{1,0:T(8,128)(2,1)S(1)}, u32[]{:S(2)}, u32[]{:S(2)}) %collective-permute-start.1) | collective-permute-done | bytes 278560 | tf_op jit(solution)/shard_map/ppermute | solution.py:176
  6.2 0.0 collective-permute-done.near_ref
  6.2 0.3 partial_sums.10
  6.5 2.6 %collective-permute-start.3 = (bf16[256,512]{1,0:T(8,128)(2,1)S(1)}, bf16[256,512]{1,0:T(8,128)(2,1)S(1)}, u32[]{:S(2)}, u32[]{:S(2)}) collective-permute-start(bf16[256,512]{1,0:T(8,128)(2,1)S(1)} %partial_sums.10), channel_id=1, source_target_pairs={{0,1},{1,0},{2,3},{3,2},{4,5},{5,4},{6,7},{7,6},{8,9},{9,8},{10,11... | collective-permute-start | bytes 786440 | tf_op jit(solution)/shard_map/ppermute | solution.py:176
  9.1 0.3 partial_sums.11
  9.5 1.6 %collective-permute-start.7 = (bf16[256,512]{1,0:T(8,128)(2,1)S(1)}, bf16[256,512]{1,0:T(8,128)(2,1)S(1)}, u32[]{:S(2)}, u32[]{:S(2)}) collective-permute-start(bf16[256,512]{1,0:T(8,128)(2,1)S(1)} %partial_sums.11), channel_id=1, source_target_pairs={{0,16},{1,17},{2,18},{3,19},{4,20},{5,21},{6,22},{7,23},{8,24},{9,... | collective-permute-start | bytes 786440 | tf_op jit(solution)/shard_map/ppermute | solution.py:176
  11.1 0.4 partial_sums.7
  11.5 1.6 %collective-permute-start.2 = (bf16[512,256]{1,0:T(8,128)(2,1)S(1)}, bf16[512,256]{1,0:T(8,128)(2,1)S(1)}, u32[]{:S(2)}, u32[]{:S(2)}) collective-permute-start(bf16[512,256]{1,0:T(8,128)(2,1)S(1)} %partial_sums.7), channel_id=1, source_target_pairs={{0,2},{1,3},{2,0},{3,1},{4,6},{5,7},{6,4},{7,5},{8,10},{9,11},{10,... | collective-permute-start | bytes 786440 | tf_op jit(solution)/shard_map/ppermute | solution.py:176
  13.1 0.4 partial_sums.8
  13.5 0.5 %collective-permute-start.10 = (bf16[512,256]{1,0:T(8,128)(2,1)S(1)}, bf16[512,256]{1,0:T(8,128)(2,1)S(1)}, u32[]{:S(2)}, u32[]{:S(2)}) collective-permute-start(bf16[512,256]{1,0:T(8,128)(2,1)S(1)} %partial_sums.8), channel_id=1, source_target_pairs={{0,2},{1,3},{2,0},{3,1},{4,6},{5,7},{6,4},{7,5},{8,10},{9,11},{10,... | collective-permute-start | bytes 786440 | tf_op jit(solution)/shard_map/ppermute | solution.py:176
  14.0 0.5 %partial_sums.9 = (f32[256,512]{1,0:T(8,128)S(1)}, f32[256,512]{1,0:T(8,128)S(1)}) custom-call(bf16[256,4096]{1,0:T(8,128)(2,1)S(1)} %copy-done, bf16[256,4096]{1,0:T(8,128)(2,1)S(1)} %collective-permute-done.near_ref, bf16[272,512]{1,0:T(8,128)(2,1)S(1)} %front.1.v0_ref, bf16[272,512]{1,0:T(8,128)(2,1)S(1)} %collective-permute-done.1.v1_ref), custom_call_target="tpu_custom_call" | custom-call | tf_op jit(solution)/shard_map/partial_sums/pallas_call | solution.py:201
  14.5 0.5 %partial_sums.6 = (f32[512,256]{1,0:T(8,128)S(1)}, f32[512,256]{1,0:T(8,128)S(1)}) custom-call(bf16[256,4096]{1,0:T(8,128)(2,1)S(1)} %copy-done, bf16[256,4096]{1,0:T(8,128)(2,1)S(1)} %collective-permute-done.near_ref, bf16[272,512]{1,0:T(8,128)(2,1)S(1)} %front.1.v0_ref, bf16[272,512]{1,0:T(8,128)(2,1)S(1)} %collective-permute-done.1.v1_ref), custom_call_target="tpu_custom_call" | custom-call | tf_op jit(solution)/shard_map/partial_sums/pallas_call | solution.py:201
  15.0 0.3 inner_swap.1
  15.3 0.7 %collective-permute-done.3 = bf16[256,512]{1,0:T(8,128)(2,1)S(1)} collective-permute-done((bf16[256,512]{1,0:T(8,128)(2,1)S(1)}, bf16[256,512]{1,0:T(8,128)(2,1)S(1)}, u32[]{:S(2)}, u32[]{:S(2)}) %collective-permute-start.3) | collective-permute-done | bytes 262176 | tf_op jit(solution)/shard_map/ppermute | solution.py:176
  16.0 1.8 %collective-permute-start.5 = (bf16[128,512]{1,0:T(8,128)(2,1)S(1)}, bf16[128,512]{1,0:T(8,128)(2,1)S(1)}, u32[]{:S(2)}, u32[]{:S(2)}) collective-permute-start(bf16[128,512]{1,0:T(8,128)(2,1)S(1)} %add_convert_fusion.4), channel_id=1, source_target_pairs={{0,16},{1,17},{2,18},{3,19},{4,20},{5,21},{6,22},{7,23},{8,24},{9,... | collective-permute-start | bytes 393224 | tf_op jit(solution)/shard_map/ppermute | solution.py:176
  17.8 0.0 collective-permute-done.7
  17.9 1.5 %collective-permute-start.8 = (bf16[128,512]{1,0:T(8,128)(2,1)S(1)}, bf16[128,512]{1,0:T(8,128)(2,1)S(1)}, u32[]{:S(2)}, u32[]{:S(2)}) collective-permute-start(bf16[128,512]{1,0:T(8,128)(2,1)S(1)} %add_convert_fusion.2), channel_id=1, source_target_pairs={{0,1},{1,0},{2,3},{3,2},{4,5},{5,4},{6,7},{7,6},{8,9},{9,8},{10,11... | collective-permute-start | bytes 393224 | tf_op jit(solution)/shard_map/ppermute | solution.py:176
  19.4 0.6 %collective-permute-start.4 = (bf16[32,512]{1,0:T(8,128)(2,1)S(1)}, bf16[32,512]{1,0:T(8,128)(2,1)S(1)}, u32[]{:S(2)}, u32[]{:S(2)}) collective-permute-start(bf16[32,512]{1,0:T(8,128)(2,1)S(1)} %get-tuple-element.26), channel_id=1, source_target_pairs={{0,16},{1,17},{2,18},{3,19},{4,20},{5,21},{6,22},{7,23},{8,24},{9,... | collective-permute-start | bytes 98312 | tf_op jit(solution)/shard_map/ppermute | solution.py:176
  20.0 1.5 %collective-permute-done.5 = bf16[128,512]{1,0:T(8,128)(2,1)S(1)} collective-permute-done((bf16[128,512]{1,0:T(8,128)(2,1)S(1)}, bf16[128,512]{1,0:T(8,128)(2,1)S(1)}, u32[]{:S(2)}, u32[]{:S(2)}) %collective-permute-start.5) | collective-permute-done | bytes 131104 | tf_op jit(solution)/shard_map/ppermute | solution.py:176
  21.5 1.7 %collective-permute-start.9 = (bf16[128,512]{1,0:T(8,128)(2,1)S(1)}, bf16[128,512]{1,0:T(8,128)(2,1)S(1)}, u32[]{:S(2)}, u32[]{:S(2)}) collective-permute-start(bf16[128,512]{1,0:T(8,128)(2,1)S(1)} %add_convert_fusion.3), channel_id=1, source_target_pairs={{0,2},{1,3},{2,0},{3,1},{4,6},{5,7},{6,4},{7,5},{8,10},{9,11},{10,... | collective-permute-start | bytes 393224 | tf_op jit(solution)/shard_map/ppermute | solution.py:176
  23.2 0.0 collective-permute-done.2
  23.2 0.1 collective-permute-done.4.window_ref
  23.3 0.1 convert_add_fusion.1
  23.4 1.6 %collective-permute-start.6 = (bf16[256,256]{1,0:T(8,128)(2,1)S(1)}, bf16[256,256]{1,0:T(8,128)(2,1)S(1)}, u32[]{:S(2)}, u32[]{:S(2)}) collective-permute-start(bf16[256,256]{1,0:T(8,128)(2,1)S(1)} %slice.111), channel_id=1, source_target_pairs={{0,16},{1,17},{2,18},{3,19},{4,20},{5,21},{6,22},{7,23},{8,24},{9,... | collective-permute-start | bytes 393224 | tf_op jit(solution)/shard_map/ppermute | solution.py:176
  25.0 1.3 %collective-permute-done.10 = bf16[512,256]{1,0:T(8,128)(2,1)S(1)} collective-permute-done((bf16[512,256]{1,0:T(8,128)(2,1)S(1)}, bf16[512,256]{1,0:T(8,128)(2,1)S(1)}, u32[]{:S(2)}, u32[]{:S(2)}) %collective-permute-start.10) | collective-permute-done | bytes 262176 | tf_op jit(solution)/shard_map/ppermute | solution.py:176
  26.3 0.1 fusion.2
  26.4 0.6 %collective-permute-start.11 = (bf16[256,256]{1,0:T(8,128)(2,1)S(1)}, bf16[256,256]{1,0:T(8,128)(2,1)S(1)}, u32[]{:S(2)}, u32[]{:S(2)}) collective-permute-start(bf16[256,256]{1,0:T(8,128)(2,1)S(1)} %pad_maximum_fusion.2), channel_id=1, source_target_pairs={{0,1},{1,0},{2,3},{3,2},{4,5},{5,4},{6,7},{7,6},{8,9},{9,8},{10,11... | collective-permute-start | bytes 393224 | tf_op jit(solution)/shard_map/ppermute | solution.py:176
  27.0 0.0 collective-permute-done.8
  27.0 0.9 %collective-permute-done.9 = bf16[128,512]{1,0:T(8,128)(2,1)S(1)} collective-permute-done((bf16[128,512]{1,0:T(8,128)(2,1)S(1)}, bf16[128,512]{1,0:T(8,128)(2,1)S(1)}, u32[]{:S(2)}, u32[]{:S(2)}) %collective-permute-start.9) | collective-permute-done | bytes 131104 | tf_op jit(solution)/shard_map/ppermute | solution.py:176
  28.0 0.1 add_convert_fusion.1
  28.0 2.7 %collective-permute-start.12 = (bf16[128,512]{1,0:T(8,128)(2,1)S(1)}, bf16[128,512]{1,0:T(8,128)(2,1)S(1)}, u32[]{:S(2)}, u32[]{:S(2)}) collective-permute-start(bf16[128,512]{1,0:T(8,128)(2,1)S(1)} %add_convert_fusion.1), channel_id=1, source_target_pairs={{0,4},{1,5},{2,6},{3,7},{4,0},{5,1},{6,2},{7,3},{8,12},{9,13},{10,... | collective-permute-start | bytes 393224 | tf_op jit(solution)/shard_map/ppermute | solution.py:176
  30.7 0.0 collective-permute-done.6
  30.7 0.6 %collective-permute-start.13 = (bf16[128,256]{1,0:T(8,128)(2,1)S(1)}, bf16[128,256]{1,0:T(8,128)(2,1)S(1)}, u32[]{:S(2)}, u32[]{:S(2)}) collective-permute-start(bf16[128,256]{1,0:T(8,128)(2,1)S(1)} %get-tuple-element.45), channel_id=1, source_target_pairs={{0,1},{1,0},{2,3},{3,2},{4,5},{5,4},{6,7},{7,6},{8,9},{9,8},{10,11... | collective-permute-start | bytes 196616 | tf_op jit(solution)/shard_map/ppermute | solution.py:176
  31.4 0.1 collective-permute-done.11
  31.5 1.2 %collective-permute-start.14 = (bf16[128,256]{1,0:T(8,128)(2,1)S(1)}, bf16[128,256]{1,0:T(8,128)(2,1)S(1)}, u32[]{:S(2)}, u32[]{:S(2)}) collective-permute-start(bf16[128,256]{1,0:T(8,128)(2,1)S(1)} %get-tuple-element.42), channel_id=1, source_target_pairs={{0,16},{1,17},{2,18},{3,19},{4,20},{5,21},{6,22},{7,23},{8,24},{9,... | collective-permute-start | bytes 196616 | tf_op jit(solution)/shard_map/ppermute | solution.py:176
  32.7 3.4 %collective-permute-done.12.arrived_ref = bf16[128,512]{1,0:T(8,128)(2,1)S(1)} collective-permute-done((bf16[128,512]{1,0:T(8,128)(2,1)S(1)}, bf16[128,512]{1,0:T(8,128)(2,1)S(1)}, u32[]{:S(2)}, u32[]{:S(2)}) %collective-permute-start.12) | collective-permute-done | bytes 131104 | tf_op jit(solution)/shard_map/ppermute | solution.py:176
  36.2 0.0 collective-permute-done.14
  36.2 0.0 collective-permute-done.13
  36.2 0.9 %collective-permute-start.15 = (bf16[128,512]{1,0:T(8,128)(2,1)S(1)}, bf16[128,512]{1,0:T(8,128)(2,1)S(1)}, u32[]{:S(2)}, u32[]{:S(2)}) collective-permute-start(bf16[128,512]{1,0:T(8,128)(2,1)S(1)} %add_convert_fusion), channel_id=1, source_target_pairs={{0,16},{1,17},{2,18},{3,19},{4,20},{5,21},{6,22},{7,23},{8,24},{9,... | collective-permute-start | bytes 393224 | tf_op jit(solution)/shard_map/ppermute | solution.py:176
  37.1 0.9 %outer_swap.1 = bf16[256,512]{1,0:T(8,128)(2,1)} custom-call(bf16[272,512]{1,0:T(8,128)(2,1)S(1)} %front.1.v0_ref, bf16[256,512]{1,0:T(8,128)(2,1)S(1)} %get-tuple-element.33.rows_ref, bf16[32,512]{1,0:T(8,128)(2,1)S(1)} %collective-permute-done.4.window_ref), custom_call_target="tpu_custom_call" | custom-call | tf_op jit(solution)/shard_map/outer_swap/pallas_call | solution.py:265
  38.0 3.2 %collective-permute-done.15 = bf16[128,512]{1,0:T(8,128)(2,1)S(1)} collective-permute-done((bf16[128,512]{1,0:T(8,128)(2,1)S(1)}, bf16[128,512]{1,0:T(8,128)(2,1)S(1)}, u32[]{:S(2)}, u32[]{:S(2)}) %collective-permute-start.15) | collective-permute-done | bytes 131104 | tf_op jit(solution)/shard_map/ppermute | solution.py:176
  41.3 0.1 collective-permute-start.16
  41.4 0.8 %place.2.rest_0_ = f32[512,512]{1,0:T(8,128)} custom-call(bf16[2,128,512]{2,1,0:T(8,128)(2,1)S(1)} %pad_maximum_fusion.1.pair_ref), custom_call_target="tpu_custom_call" | custom-call | tf_op jit(solution)/shard_map/place/pallas_call | solution.py:289
  42.2 0.7 %collective-permute-done.16.pair_ref = bf16[2,128,512]{2,1,0:T(8,128)(2,1)S(1)} collective-permute-done((bf16[2,128,512]{2,1,0:T(8,128)(2,1)S(1)}, bf16[2,128,512]{2,1,0:T(8,128)(2,1)S(1)}, u32[]{:S(2)}, u32[]{:S(2)}) %collective-permute-start.16) | collective-permute-done | bytes 262176 | tf_op jit(solution)/shard_map/ppermute | solution.py:176
  42.9 0.8 %place.3 = f32[512,512]{1,0:T(8,128)} custom-call(bf16[2,128,512]{2,1,0:T(8,128)(2,1)S(1)} %collective-permute-done.16.pair_ref, f32[512,512]{1,0:T(8,128)} %place.2.rest_0_), custom_call_target="tpu_custom_call", output_to_operand_aliasing={{}: (1, {})} | custom-call | tf_op jit(solution)/shard_map/place/pallas_call | solution.py:289
  (14 shorter events, 0.3 us)
Async XLA Ops:
  0.6 5.6 %copy-start = (bf16[256,4096]{1,0:T(8,128)(2,1)S(1)}, bf16[256,4096]{1,0:T(8,128)(2,1)}, u32[]{:S(2)}) copy-start(bf16[256,4096]{1,0:T(8,128)(2,1)} %own_ref.11) | copy-start | bytes 6291460
  0.6 5.5 %collective-permute-start = (bf16[256,4096]{1,0:T(8,128)(2,1)}, bf16[256,4096]{1,0:T(8,128)(2,1)S(1)}, u32[]{:S(2)}, u32[]{:S(2)}) collective-permute-start(bf16[256,4096]{1,0:T(8,128)(2,1)} %own_ref.11), channel_id=1, source_target_pairs={{0,8},{1,9},{2,10},{3,11},{4,12},{5,13},{6,14},{7,15},{8,0},{9,1},... | collective-permute-start | bytes 6291464 | tf_op jit(solution)/shard_map/ppermute | solution.py:176
  4.6 1.6 %collective-permute-start.1 = (bf16[272,512]{1,0:T(8,128)(2,1)S(1)}, bf16[272,512]{1,0:T(8,128)(2,1)S(1)}, u32[]{:S(2)}, u32[]{:S(2)}) collective-permute-start(bf16[272,512]{1,0:T(8,128)(2,1)S(1)} %front.1.v0_ref), channel_id=1, source_target_pairs={{0,8},{1,9},{2,10},{3,11},{4,12},{5,13},{6,14},{7,15},{8,0},{9,1},... | collective-permute-start | bytes 835592 | tf_op jit(solution)/shard_map/ppermute | solution.py:176
  6.5 9.4 %collective-permute-start.3 = (bf16[256,512]{1,0:T(8,128)(2,1)S(1)}, bf16[256,512]{1,0:T(8,128)(2,1)S(1)}, u32[]{:S(2)}, u32[]{:S(2)}) collective-permute-start(bf16[256,512]{1,0:T(8,128)(2,1)S(1)} %partial_sums.10), channel_id=1, source_target_pairs={{0,1},{1,0},{2,3},{3,2},{4,5},{5,4},{6,7},{7,6},{8,9},{9,8},{10,11... | collective-permute-start | bytes 786440 | tf_op jit(solution)/shard_map/ppermute | solution.py:176
  9.5 8.4 %collective-permute-start.7 = (bf16[256,512]{1,0:T(8,128)(2,1)S(1)}, bf16[256,512]{1,0:T(8,128)(2,1)S(1)}, u32[]{:S(2)}, u32[]{:S(2)}) collective-permute-start(bf16[256,512]{1,0:T(8,128)(2,1)S(1)} %partial_sums.11), channel_id=1, source_target_pairs={{0,16},{1,17},{2,18},{3,19},{4,20},{5,21},{6,22},{7,23},{8,24},{9,... | collective-permute-start | bytes 786440 | tf_op jit(solution)/shard_map/ppermute | solution.py:176
  11.5 11.8 %collective-permute-start.2 = (bf16[512,256]{1,0:T(8,128)(2,1)S(1)}, bf16[512,256]{1,0:T(8,128)(2,1)S(1)}, u32[]{:S(2)}, u32[]{:S(2)}) collective-permute-start(bf16[512,256]{1,0:T(8,128)(2,1)S(1)} %partial_sums.7), channel_id=1, source_target_pairs={{0,2},{1,3},{2,0},{3,1},{4,6},{5,7},{6,4},{7,5},{8,10},{9,11},{10,... | collective-permute-start | bytes 786440 | tf_op jit(solution)/shard_map/ppermute | solution.py:176
  13.5 12.9 %collective-permute-start.10 = (bf16[512,256]{1,0:T(8,128)(2,1)S(1)}, bf16[512,256]{1,0:T(8,128)(2,1)S(1)}, u32[]{:S(2)}, u32[]{:S(2)}) collective-permute-start(bf16[512,256]{1,0:T(8,128)(2,1)S(1)} %partial_sums.8), channel_id=1, source_target_pairs={{0,2},{1,3},{2,0},{3,1},{4,6},{5,7},{6,4},{7,5},{8,10},{9,11},{10,... | collective-permute-start | bytes 786440 | tf_op jit(solution)/shard_map/ppermute | solution.py:176
  16.0 5.5 %collective-permute-start.5 = (bf16[128,512]{1,0:T(8,128)(2,1)S(1)}, bf16[128,512]{1,0:T(8,128)(2,1)S(1)}, u32[]{:S(2)}, u32[]{:S(2)}) collective-permute-start(bf16[128,512]{1,0:T(8,128)(2,1)S(1)} %add_convert_fusion.4), channel_id=1, source_target_pairs={{0,16},{1,17},{2,18},{3,19},{4,20},{5,21},{6,22},{7,23},{8,24},{9,... | collective-permute-start | bytes 393224 | tf_op jit(solution)/shard_map/ppermute | solution.py:176
  17.9 9.2 %collective-permute-start.8 = (bf16[128,512]{1,0:T(8,128)(2,1)S(1)}, bf16[128,512]{1,0:T(8,128)(2,1)S(1)}, u32[]{:S(2)}, u32[]{:S(2)}) collective-permute-start(bf16[128,512]{1,0:T(8,128)(2,1)S(1)} %add_convert_fusion.2), channel_id=1, source_target_pairs={{0,1},{1,0},{2,3},{3,2},{4,5},{5,4},{6,7},{7,6},{8,9},{9,8},{10,11... | collective-permute-start | bytes 393224 | tf_op jit(solution)/shard_map/ppermute | solution.py:176
  19.4 3.9 %collective-permute-start.4 = (bf16[32,512]{1,0:T(8,128)(2,1)S(1)}, bf16[32,512]{1,0:T(8,128)(2,1)S(1)}, u32[]{:S(2)}, u32[]{:S(2)}) collective-permute-start(bf16[32,512]{1,0:T(8,128)(2,1)S(1)} %get-tuple-element.26), channel_id=1, source_target_pairs={{0,16},{1,17},{2,18},{3,19},{4,20},{5,21},{6,22},{7,23},{8,24},{9,... | collective-permute-start | bytes 98312 | tf_op jit(solution)/shard_map/ppermute | solution.py:176
  21.5 6.4 %collective-permute-start.9 = (bf16[128,512]{1,0:T(8,128)(2,1)S(1)}, bf16[128,512]{1,0:T(8,128)(2,1)S(1)}, u32[]{:S(2)}, u32[]{:S(2)}) collective-permute-start(bf16[128,512]{1,0:T(8,128)(2,1)S(1)} %add_convert_fusion.3), channel_id=1, source_target_pairs={{0,2},{1,3},{2,0},{3,1},{4,6},{5,7},{6,4},{7,5},{8,10},{9,11},{10,... | collective-permute-start | bytes 393224 | tf_op jit(solution)/shard_map/ppermute | solution.py:176
  23.4 7.3 %collective-permute-start.6 = (bf16[256,256]{1,0:T(8,128)(2,1)S(1)}, bf16[256,256]{1,0:T(8,128)(2,1)S(1)}, u32[]{:S(2)}, u32[]{:S(2)}) collective-permute-start(bf16[256,256]{1,0:T(8,128)(2,1)S(1)} %slice.111), channel_id=1, source_target_pairs={{0,16},{1,17},{2,18},{3,19},{4,20},{5,21},{6,22},{7,23},{8,24},{9,... | collective-permute-start | bytes 393224 | tf_op jit(solution)/shard_map/ppermute | solution.py:176
  26.4 5.0 %collective-permute-start.11 = (bf16[256,256]{1,0:T(8,128)(2,1)S(1)}, bf16[256,256]{1,0:T(8,128)(2,1)S(1)}, u32[]{:S(2)}, u32[]{:S(2)}) collective-permute-start(bf16[256,256]{1,0:T(8,128)(2,1)S(1)} %pad_maximum_fusion.2), channel_id=1, source_target_pairs={{0,1},{1,0},{2,3},{3,2},{4,5},{5,4},{6,7},{7,6},{8,9},{9,8},{10,11... | collective-permute-start | bytes 393224 | tf_op jit(solution)/shard_map/ppermute | solution.py:176
  28.0 8.1 %collective-permute-start.12 = (bf16[128,512]{1,0:T(8,128)(2,1)S(1)}, bf16[128,512]{1,0:T(8,128)(2,1)S(1)}, u32[]{:S(2)}, u32[]{:S(2)}) collective-permute-start(bf16[128,512]{1,0:T(8,128)(2,1)S(1)} %add_convert_fusion.1), channel_id=1, source_target_pairs={{0,4},{1,5},{2,6},{3,7},{4,0},{5,1},{6,2},{7,3},{8,12},{9,13},{10,... | collective-permute-start | bytes 393224 | tf_op jit(solution)/shard_map/ppermute | solution.py:176
  30.7 5.4 %collective-permute-start.13 = (bf16[128,256]{1,0:T(8,128)(2,1)S(1)}, bf16[128,256]{1,0:T(8,128)(2,1)S(1)}, u32[]{:S(2)}, u32[]{:S(2)}) collective-permute-start(bf16[128,256]{1,0:T(8,128)(2,1)S(1)} %get-tuple-element.45), channel_id=1, source_target_pairs={{0,1},{1,0},{2,3},{3,2},{4,5},{5,4},{6,7},{7,6},{8,9},{9,8},{10,11... | collective-permute-start | bytes 196616 | tf_op jit(solution)/shard_map/ppermute | solution.py:176
  31.5 4.7 %collective-permute-start.14 = (bf16[128,256]{1,0:T(8,128)(2,1)S(1)}, bf16[128,256]{1,0:T(8,128)(2,1)S(1)}, u32[]{:S(2)}, u32[]{:S(2)}) collective-permute-start(bf16[128,256]{1,0:T(8,128)(2,1)S(1)} %get-tuple-element.42), channel_id=1, source_target_pairs={{0,16},{1,17},{2,18},{3,19},{4,20},{5,21},{6,22},{7,23},{8,24},{9,... | collective-permute-start | bytes 196616 | tf_op jit(solution)/shard_map/ppermute | solution.py:176
  36.2 5.0 %collective-permute-start.15 = (bf16[128,512]{1,0:T(8,128)(2,1)S(1)}, bf16[128,512]{1,0:T(8,128)(2,1)S(1)}, u32[]{:S(2)}, u32[]{:S(2)}) collective-permute-start(bf16[128,512]{1,0:T(8,128)(2,1)S(1)} %add_convert_fusion), channel_id=1, source_target_pairs={{0,16},{1,17},{2,18},{3,19},{4,20},{5,21},{6,22},{7,23},{8,24},{9,... | collective-permute-start | bytes 393224 | tf_op jit(solution)/shard_map/ppermute | solution.py:176
  41.3 1.6 %collective-permute-start.16 = (bf16[2,128,512]{2,1,0:T(8,128)(2,1)S(1)}, bf16[2,128,512]{2,1,0:T(8,128)(2,1)S(1)}, u32[]{:S(2)}, u32[]{:S(2)}) collective-permute-start(bf16[2,128,512]{2,1,0:T(8,128)(2,1)S(1)} %pad_maximum_fusion.1.pair_ref), channel_id=1, source_target_pairs={{0,8},{1,9},{2,10},{3,11},{4,12},{5,13},{6,14},{7,15},{8,0},{9,1},... | collective-permute-start | bytes 786440 | tf_op jit(solution)/shard_map/ppermute | solution.py:176

commit v17 on v16

--- a/solution.py
+++ b/solution.py
@@ -332,40 +332,47 @@
             total = total + term.astype(F32)
         return total
 
-    first_b, = sums([(((3, 1, 1), (3, 0, 1)), 0, 512)], BF16)
+    far_b, = sums([(((3, 1, 1),), 0, 512)], BF16)
     first_a, = sums([(((2, 1, 1), (2, 1, 0)), 0, 512)], BF16)
     every = ((1, 1), (1, 0), (0, 1), (0, 0))
-    pair_some, = sums([(tuple((1, *at) for at in every), 0, 256)], BF16)
-    pair_rest, = sums([(tuple((1, *at) for at in every), 256, 256)], BF16, after_all(v0, pair_some)[0])
+    side_b, pair_some = sums([(((3, 0, 1),), 0, 512), (tuple((1, *at) for at in every[:3]), 0, 256)], BF16)
+    pair_rest, pair_own = sums(
+        [(tuple((1, *at) for at in every[:3]), 256, 256), (((1, 0, 0),), 0, 512)], BF16, after_all(v0, pair_some)[0]
+    )
     keep_b, keep_a = sums([(((3, 1, 0), (3, 0, 0)), 0, 512), (((2, 0, 1), (2, 0, 0)), 0, 512)], F32)
     own_some, own_rest = sums([(tuple((0, *at) for at in every), start, 256) for start in (0, 256)], F32)
-    first_b = xor_permute(first_b, X)
+    far_b = xor_permute(far_b, X)
+    side_b = xor_permute(side_b, X)
     first_a = xor_permute(first_a, Y)
     pair_sent = pair_rest
     pair_some = xor_permute(pair_some, Z1)
     pair_rest = xor_permute(pair_rest, Z1)
-    on_b = add(keep_b[:LANE], first_b[:LANE]).astype(BF16)
+    on_b = add(keep_b[:LANE], far_b).astype(BF16)
     rows, window = inner_swap(after_all(v0, pair_sent)[0], v1)
     window = xor_permute(after_all(window, on_b)[0], Y)
     on_b = xor_permute(on_b, Y)
     on_a = xor_permute(add(keep_a[:LANE], first_a[:LANE]).astype(BF16), X)
-    z3 = add(keep_b[LANE:], first_b[LANE:], on_b).astype(BF16)
-    pair_some, window = after_all(pair_some, window, z3)[:2]
+    z3 = add(keep_b[LANE:], side_b, on_b).astype(BF16)
+    pair_some, window, pair_own = after_all(pair_some, window, pair_own, z3)[:3]
     z3 = xor_permute(z3, Z1)
+    pair_own = xor_permute(pair_own, Z1)
     z2 = add(keep_a[LANE:], first_a[LANE:], on_a, z3).astype(BF16)
 
-    some = add(own_some, pair_some)
+    some = add(own_some[:3 * LANE], pair_some)
     some_in = xor_permute(some[:2 * LANE].astype(BF16), Y)
-    rest = add(own_rest, after_all(pair_rest, some)[0])
-    rest_far, rest_y, rest_x, rest_own = (rest[row:row + LANE] for row in range(0, 4 * LANE, LANE))
+    rest = add(own_rest[:3 * LANE], after_all(pair_rest, some)[0])
+    rest_far, rest_y, rest_x = (rest[row:row + LANE] for row in range(0, 3 * LANE, LANE))
     rest_in = xor_permute(jnp.concatenate([rest_far, rest_x]).astype(BF16), X)
     some_in = after_all(some_in, z2)[0]
     z2 = xor_permute(z2, Z2)
-    some_on = add(some[2 * LANE:3 * LANE], some_in[:LANE]).astype(BF16)
+    some_on = add(some[2 * LANE:], some_in[:LANE]).astype(BF16)
     rest_in = after_all(rest_in, some_on)[0]
     some_on = xor_permute(some_on, X)
     rest_on = xor_permute(add(rest_y, rest_in[:LANE]).astype(BF16), Y)
-    base = jnp.concatenate([add(some[3 * LANE:], some_in[LANE:]), add(rest_own, rest_in[LANE:])], axis=1)
+    base = jnp.concatenate([
+        add(own_some[3 * LANE:], pair_own[:, :256], some_in[LANE:]),
+        add(own_rest[3 * LANE:], pair_own[:, 256:], rest_in[LANE:]),
+    ], axis=1)
     mine = add(fold(base, z2), jnp.concatenate([some_on, rest_on], axis=1)).astype(BF16)
     from_y = xor_permute(mine, Y)
     value_grad = outer_swap(v0, rows, after_all(window, mine)[0])

time: 43.9 us -> 42.9 us (0.977)
  waiting for transfers between devices: 13.5 us -> 11.6 us
  starting transfers between devices: 20.3 us -> 21.2 us
    ppermute x17 -> x19, waiting for transfers between devices: 13.5 us -> 11.6 us  [xor_permute(): lax.ppermute(value, ('dp', 'fsdp'), [(i, i ^ mask) for i in range(count)])]
    ppermute x17 -> x19, starting transfers between devices: 20.3 us -> 21.2 us  [xor_permute(): lax.ppermute(value, ('dp', 'fsdp'), [(i, i ^ mask) for i in range(count)])]
  transfers between devices with their start and end apart: 17 -> 19, of which waited for: 10 -> 8; matrix products, arithmetic and copies ran while one was open for 1% -> 1% of each run, Pallas kernels for 16% -> 16%
where the time goes in v17:
time: 42.9 us; the launch traced here: 42.7 us
  starting transfers between devices  21.2 us (49%)
  waiting for transfers between devices  11.6 us (27%)
  Pallas kernels  7.92 us (18%)
  between operations  1.58 us (4%)
    ppermute x19, starting transfers between devices, xor_permute(): lax.ppermute(value, ('dp', 'fsdp'), [(i, i ^ mask) for i in range(count)])  21.2 us
    ppermute x19, waiting for transfers between devices, xor_permute(): lax.ppermute(value, ('dp', 'fsdp'), [(i, i ^ mask) for i in range(count)])  11.6 us
    pallas_call x1, Pallas kernels, front(): pl.pallas_call(functools.partial(front_kernel, per_group), in_specs=[HBM]...  2.64 us
    pallas_call x6, Pallas kernels, partial_sums(): pl.pallas_call(functools.partial(partial_kernel, parts), in_specs=[VMEM]...  2.37 us
    pallas_call x2, Pallas kernels, place(): pl.pallas_call(functools.partial(place_kernel, core), in_specs=[VMEM] + [...  1.65 us
    pallas_call x1, Pallas kernels, outer_swap(): pl.pallas_call(outer_swap_kernel, in_specs=[VMEM] * 3, out_specs=VMEM, ou...  0.91 us
  transfers between devices with their start and end apart: 19, of which 8 were waited for; matrix products, arithmetic and copies ran while one was open for 1% of the time, Pallas kernels for 16%

profile of v17, /device:TPU:0, one launch (start us, length us, event | category | flops | bytes accessed | tf_op | source)
XLA Modules:
  0.0 42.7 jit_solution(4775767879197037276)
XLA Ops:
  0.6 0.5 %collective-permute-start = (bf16[256,4096]{1,0:T(8,128)(2,1)}, bf16[256,4096]{1,0:T(8,128)(2,1)S(1)}, u32[]{:S(2)}, u32[]{:S(2)}) collective-permute-start(bf16[256,4096]{1,0:T(8,128)(2,1)} %own_ref.11), channel_id=1, source_target_pairs={{0,8},{1,9},{2,10},{3,11},{4,12},{5,13},{6,14},{7,15},{8,0},{9,1},... | collective-permute-start | bytes 6291464 | tf_op jit(solution)/shard_map/ppermute | solution.py:176
  1.9 2.6 %front.1.v0_ref = bf16[272,512]{1,0:T(8,128)(2,1)S(1)} custom-call(f32[16]{0:T(128)} %loss_hbm.1, s32[1]{0:T(128)S(6)} %copy.14.exponent_hbm, s32[1,2]{1,0:T(1,128)} %start_hbm.1, s32[1,2]{1,0:T(1,128)} %rows_hbm.1, bf16[256,2048]{1,0:T(8,128)(2,1)} %q_hbm.1, bf16[256,512]{1,0:T(8,128)(2,1)} %k_hbm.1, bf16[256,2048]{1,0:T(8,128)(2,1)} %g_hbm.1, ...), custom_call_target="tpu_custom_call" | custom-call | tf_op jit(solution)/shard_map/front/pallas_call | solution.py:153
  4.6 0.1 collective-permute-start.1
  4.7 1.5 %collective-permute-done.1.v1_ref = bf16[272,512]{1,0:T(8,128)(2,1)S(1)} collective-permute-done((bf16[272,512]{1,0:T(8,128)(2,1)S(1)}, bf16[272,512]{1,0:T(8,128)(2,1)S(1)}, u32[]{:S(2)}, u32[]{:S(2)}) %collective-permute-start.1) | collective-permute-done | bytes 278560 | tf_op jit(solution)/shard_map/ppermute | solution.py:176
  6.2 0.0 collective-permute-done.near_ref
  6.2 0.3 partial_sums.10
  6.5 2.6 %collective-permute-start.3 = (bf16[128,512]{1,0:T(8,128)(2,1)S(1)}, bf16[128,512]{1,0:T(8,128)(2,1)S(1)}, u32[]{:S(2)}, u32[]{:S(2)}) collective-permute-start(bf16[128,512]{1,0:T(8,128)(2,1)S(1)} %partial_sums.10), channel_id=1, source_target_pairs={{0,1},{1,0},{2,3},{3,2},{4,5},{5,4},{6,7},{7,6},{8,9},{9,8},{10,11... | collective-permute-start | bytes 393224 | tf_op jit(solution)/shard_map/ppermute | solution.py:176
  9.1 0.3 partial_sums.11
  9.4 1.6 %collective-permute-start.9 = (bf16[256,512]{1,0:T(8,128)(2,1)S(1)}, bf16[256,512]{1,0:T(8,128)(2,1)S(1)}, u32[]{:S(2)}, u32[]{:S(2)}) collective-permute-start(bf16[256,512]{1,0:T(8,128)(2,1)S(1)} %partial_sums.11), channel_id=1, source_target_pairs={{0,16},{1,17},{2,18},{3,19},{4,20},{5,21},{6,22},{7,23},{8,24},{9,... | collective-permute-start | bytes 786440 | tf_op jit(solution)/shard_map/ppermute | solution.py:176
  11.0 0.4 partial_sums.7
  11.4 1.6 %collective-permute-start.2 = (bf16[384,256]{1,0:T(8,128)(2,1)S(1)}, bf16[384,256]{1,0:T(8,128)(2,1)S(1)}, u32[]{:S(2)}, u32[]{:S(2)}) collective-permute-start(bf16[384,256]{1,0:T(8,128)(2,1)S(1)} %get-tuple-element.27), channel_id=1, source_target_pairs={{0,2},{1,3},{2,0},{3,1},{4,6},{5,7},{6,4},{7,5},{8,10},{9,11},{10,... | collective-permute-start | bytes 589832 | tf_op jit(solution)/shard_map/ppermute | solution.py:176
  13.0 0.4 partial_sums.8
  13.4 0.5 %collective-permute-start.12 = (bf16[384,256]{1,0:T(8,128)(2,1)S(1)}, bf16[384,256]{1,0:T(8,128)(2,1)S(1)}, u32[]{:S(2)}, u32[]{:S(2)}) collective-permute-start(bf16[384,256]{1,0:T(8,128)(2,1)S(1)} %get-tuple-element.29), channel_id=1, source_target_pairs={{0,2},{1,3},{2,0},{3,1},{4,6},{5,7},{6,4},{7,5},{8,10},{9,11},{10,... | collective-permute-start | bytes 589832 | tf_op jit(solution)/shard_map/ppermute | solution.py:176
  14.0 0.5 %collective-permute-start.5 = (bf16[128,512]{1,0:T(8,128)(2,1)S(1)}, bf16[128,512]{1,0:T(8,128)(2,1)S(1)}, u32[]{:S(2)}, u32[]{:S(2)}) collective-permute-start(bf16[128,512]{1,0:T(8,128)(2,1)S(1)} %get-tuple-element.35), channel_id=1, source_target_pairs={{0,1},{1,0},{2,3},{3,2},{4,5},{5,4},{6,7},{7,6},{8,9},{9,8},{10,11... | collective-permute-start | bytes 393224 | tf_op jit(solution)/shard_map/ppermute | solution.py:176
  14.5 0.5 %partial_sums.9 = (f32[256,512]{1,0:T(8,128)S(1)}, f32[256,512]{1,0:T(8,128)S(1)}) custom-call(bf16[256,4096]{1,0:T(8,128)(2,1)S(1)} %copy-done, bf16[256,4096]{1,0:T(8,128)(2,1)S(1)} %collective-permute-done.near_ref, bf16[272,512]{1,0:T(8,128)(2,1)S(1)} %front.1.v0_ref, bf16[272,512]{1,0:T(8,128)(2,1)S(1)} %collective-permute-done.1.v1_ref), custom_call_target="tpu_custom_call" | custom-call | tf_op jit(solution)/shard_map/partial_sums/pallas_call | solution.py:201
  15.0 0.5 %partial_sums.6 = (f32[512,256]{1,0:T(8,128)S(1)}, f32[512,256]{1,0:T(8,128)S(1)}) custom-call(bf16[256,4096]{1,0:T(8,128)(2,1)S(1)} %copy-done, bf16[256,4096]{1,0:T(8,128)(2,1)S(1)} %collective-permute-done.near_ref, bf16[272,512]{1,0:T(8,128)(2,1)S(1)} %front.1.v0_ref, bf16[272,512]{1,0:T(8,128)(2,1)S(1)} %collective-permute-done.1.v1_ref), custom_call_target="tpu_custom_call" | custom-call | tf_op jit(solution)/shard_map/partial_sums/pallas_call | solution.py:201
  15.5 0.3 inner_swap.1
  15.8 0.2 collective-permute-start.6
  16.0 2.0 %collective-permute-done.9 = bf16[256,512]{1,0:T(8,128)(2,1)S(1)} collective-permute-done((bf16[256,512]{1,0:T(8,128)(2,1)S(1)}, bf16[256,512]{1,0:T(8,128)(2,1)S(1)}, u32[]{:S(2)}, u32[]{:S(2)}) %collective-permute-start.9) | collective-permute-done | bytes 262176 | tf_op jit(solution)/shard_map/ppermute | solution.py:176
  18.0 2.1 %collective-permute-start.4 = (bf16[32,512]{1,0:T(8,128)(2,1)S(1)}, bf16[32,512]{1,0:T(8,128)(2,1)S(1)}, u32[]{:S(2)}, u32[]{:S(2)}) collective-permute-start(bf16[32,512]{1,0:T(8,128)(2,1)S(1)} %get-tuple-element.33), channel_id=1, source_target_pairs={{0,16},{1,17},{2,18},{3,19},{4,20},{5,21},{6,22},{7,23},{8,24},{9,... | collective-permute-start | bytes 98312 | tf_op jit(solution)/shard_map/ppermute | solution.py:176
  20.2 0.0 collective-permute-done.5
  20.2 0.1 collective-permute-start.10
  20.3 0.9 %collective-permute-done.6 = bf16[128,512]{1,0:T(8,128)(2,1)S(1)} collective-permute-done((bf16[128,512]{1,0:T(8,128)(2,1)S(1)}, bf16[128,512]{1,0:T(8,128)(2,1)S(1)}, u32[]{:S(2)}, u32[]{:S(2)}) %collective-permute-start.6) | collective-permute-done | bytes 131104 | tf_op jit(solution)/shard_map/ppermute | solution.py:176
  21.3 1.6 %collective-permute-start.11 = (bf16[128,512]{1,0:T(8,128)(2,1)S(1)}, bf16[128,512]{1,0:T(8,128)(2,1)S(1)}, u32[]{:S(2)}, u32[]{:S(2)}) collective-permute-start(bf16[128,512]{1,0:T(8,128)(2,1)S(1)} %add_convert_fusion.3), channel_id=1, source_target_pairs={{0,2},{1,3},{2,0},{3,1},{4,6},{5,7},{6,4},{7,5},{8,10},{9,11},{10,... | collective-permute-start | bytes 393224 | tf_op jit(solution)/shard_map/ppermute | solution.py:176
  22.9 0.0 collective-permute-done.4.window_ref
  22.9 0.0 collective-permute-done.2
  23.0 1.3 %collective-permute-start.8 = (bf16[256,256]{1,0:T(8,128)(2,1)S(1)}, bf16[256,256]{1,0:T(8,128)(2,1)S(1)}, u32[]{:S(2)}, u32[]{:S(2)}) collective-permute-start(bf16[256,256]{1,0:T(8,128)(2,1)S(1)} %slice.119), channel_id=1, source_target_pairs={{0,16},{1,17},{2,18},{3,19},{4,20},{5,21},{6,22},{7,23},{8,24},{9,... | collective-permute-start | bytes 393224 | tf_op jit(solution)/shard_map/ppermute | solution.py:176
  24.3 0.0 collective-permute-done.12
  24.4 0.8 %collective-permute-start.13 = (bf16[256,256]{1,0:T(8,128)(2,1)S(1)}, bf16[256,256]{1,0:T(8,128)(2,1)S(1)}, u32[]{:S(2)}, u32[]{:S(2)}) collective-permute-start(bf16[256,256]{1,0:T(8,128)(2,1)S(1)} %pad_maximum_fusion.2), channel_id=1, source_target_pairs={{0,1},{1,0},{2,3},{3,2},{4,5},{5,4},{6,7},{7,6},{8,9},{9,8},{10,11... | collective-permute-start | bytes 393224 | tf_op jit(solution)/shard_map/ppermute | solution.py:176
  25.2 0.8 %collective-permute-start.7 = (bf16[128,512]{1,0:T(8,128)(2,1)S(1)}, bf16[128,512]{1,0:T(8,128)(2,1)S(1)}, u32[]{:S(2)}, u32[]{:S(2)}) collective-permute-start(bf16[128,512]{1,0:T(8,128)(2,1)S(1)} %get-tuple-element.36), channel_id=1, source_target_pairs={{0,2},{1,3},{2,0},{3,1},{4,6},{5,7},{6,4},{7,5},{8,10},{9,11},{10,... | collective-permute-start | bytes 393224 | tf_op jit(solution)/shard_map/ppermute | solution.py:176
  26.0 0.0 collective-permute-done.10
  26.0 1.2 %collective-permute-done.11 = bf16[128,512]{1,0:T(8,128)(2,1)S(1)} collective-permute-done((bf16[128,512]{1,0:T(8,128)(2,1)S(1)}, bf16[128,512]{1,0:T(8,128)(2,1)S(1)}, u32[]{:S(2)}, u32[]{:S(2)}) %collective-permute-start.11) | collective-permute-done | bytes 131104 | tf_op jit(solution)/shard_map/ppermute | solution.py:176
  27.3 0.1 add_convert_fusion.1
  27.3 2.6 %collective-permute-start.14 = (bf16[128,512]{1,0:T(8,128)(2,1)S(1)}, bf16[128,512]{1,0:T(8,128)(2,1)S(1)}, u32[]{:S(2)}, u32[]{:S(2)}) collective-permute-start(bf16[128,512]{1,0:T(8,128)(2,1)S(1)} %add_convert_fusion.1), channel_id=1, source_target_pairs={{0,4},{1,5},{2,6},{3,7},{4,0},{5,1},{6,2},{7,3},{8,12},{9,13},{10,... | collective-permute-start | bytes 393224 | tf_op jit(solution)/shard_map/ppermute | solution.py:176
  30.0 0.0 collective-permute-done.8
  30.0 0.8 %collective-permute-start.15 = (bf16[128,256]{1,0:T(8,128)(2,1)S(1)}, bf16[128,256]{1,0:T(8,128)(2,1)S(1)}, u32[]{:S(2)}, u32[]{:S(2)}) collective-permute-start(bf16[128,256]{1,0:T(8,128)(2,1)S(1)} %fusion.1), channel_id=1, source_target_pairs={{0,1},{1,0},{2,3},{3,2},{4,5},{5,4},{6,7},{7,6},{8,9},{9,8},{10,11... | collective-permute-start | bytes 196616 | tf_op jit(solution)/shard_map/ppermute | solution.py:176
  30.8 0.0 collective-permute-done.13
  30.8 0.0 collective-permute-done.7
  30.8 1.4 %collective-permute-start.16 = (bf16[128,256]{1,0:T(8,128)(2,1)S(1)}, bf16[128,256]{1,0:T(8,128)(2,1)S(1)}, u32[]{:S(2)}, u32[]{:S(2)}) collective-permute-start(bf16[128,256]{1,0:T(8,128)(2,1)S(1)} %get-tuple-element.54), channel_id=1, source_target_pairs={{0,16},{1,17},{2,18},{3,19},{4,20},{5,21},{6,22},{7,23},{8,24},{9,... | collective-permute-start | bytes 196616 | tf_op jit(solution)/shard_map/ppermute | solution.py:176
  32.2 1.0 %collective-permute-done.14.arrived_ref = bf16[128,512]{1,0:T(8,128)(2,1)S(1)} collective-permute-done((bf16[128,512]{1,0:T(8,128)(2,1)S(1)}, bf16[128,512]{1,0:T(8,128)(2,1)S(1)}, u32[]{:S(2)}, u32[]{:S(2)}) %collective-permute-start.14) | collective-permute-done | bytes 131104 | tf_op jit(solution)/shard_map/ppermute | solution.py:176
  33.3 1.9 %collective-permute-done.16 = bf16[128,256]{1,0:T(8,128)(2,1)S(1)} collective-permute-done((bf16[128,256]{1,0:T(8,128)(2,1)S(1)}, bf16[128,256]{1,0:T(8,128)(2,1)S(1)}, u32[]{:S(2)}, u32[]{:S(2)}) %collective-permute-start.16) | collective-permute-done | bytes 65568 | tf_op jit(solution)/shard_map/ppermute | solution.py:176
  35.2 1.8 %collective-permute-start.17 = (bf16[128,512]{1,0:T(8,128)(2,1)S(1)}, bf16[128,512]{1,0:T(8,128)(2,1)S(1)}, u32[]{:S(2)}, u32[]{:S(2)}) collective-permute-start(bf16[128,512]{1,0:T(8,128)(2,1)S(1)} %add_convert_fusion), channel_id=1, source_target_pairs={{0,16},{1,17},{2,18},{3,19},{4,20},{5,21},{6,22},{7,23},{8,24},{9,... | collective-permute-start | bytes 393224 | tf_op jit(solution)/shard_map/ppermute | solution.py:176
  37.0 0.9 %outer_swap.1 = bf16[256,512]{1,0:T(8,128)(2,1)} custom-call(bf16[272,512]{1,0:T(8,128)(2,1)S(1)} %front.1.v0_ref, bf16[256,512]{1,0:T(8,128)(2,1)S(1)} %get-tuple-element.43.rows_ref, bf16[32,512]{1,0:T(8,128)(2,1)S(1)} %collective-permute-done.4.window_ref), custom_call_target="tpu_custom_call" | custom-call | tf_op jit(solution)/shard_map/outer_swap/pallas_call | solution.py:265
  37.9 2.3 %collective-permute-done.17 = bf16[128,512]{1,0:T(8,128)(2,1)S(1)} collective-permute-done((bf16[128,512]{1,0:T(8,128)(2,1)S(1)}, bf16[128,512]{1,0:T(8,128)(2,1)S(1)}, u32[]{:S(2)}, u32[]{:S(2)}) %collective-permute-start.17) | collective-permute-done | bytes 131104 | tf_op jit(solution)/shard_map/ppermute | solution.py:176
  40.3 0.1 collective-permute-start.18
  40.3 0.8 %place.2.rest_0_ = f32[512,512]{1,0:T(8,128)} custom-call(bf16[2,128,512]{2,1,0:T(8,128)(2,1)S(1)} %pad_maximum_fusion.1.pair_ref), custom_call_target="tpu_custom_call" | custom-call | tf_op jit(solution)/shard_map/place/pallas_call | solution.py:289
  41.2 0.7 %collective-permute-done.18.pair_ref = bf16[2,128,512]{2,1,0:T(8,128)(2,1)S(1)} collective-permute-done((bf16[2,128,512]{2,1,0:T(8,128)(2,1)S(1)}, bf16[2,128,512]{2,1,0:T(8,128)(2,1)S(1)}, u32[]{:S(2)}, u32[]{:S(2)}) %collective-permute-start.18) | collective-permute-done | bytes 262176 | tf_op jit(solution)/shard_map/ppermute | solution.py:176
  41.9 0.8 %place.3 = f32[512,512]{1,0:T(8,128)} custom-call(bf16[2,128,512]{2,1,0:T(8,128)(2,1)S(1)} %collective-permute-done.18.pair_ref, f32[512,512]{1,0:T(8,128)} %place.2.rest_0_), custom_call_target="tpu_custom_call", output_to_operand_aliasing={{}: (1, {})} | custom-call | tf_op jit(solution)/shard_map/place/pallas_call | solution.py:289
  (18 shorter events, 0.4 us)
Async XLA Ops:
  0.6 5.6 %copy-start = (bf16[256,4096]{1,0:T(8,128)(2,1)S(1)}, bf16[256,4096]{1,0:T(8,128)(2,1)}, u32[]{:S(2)}) copy-start(bf16[256,4096]{1,0:T(8,128)(2,1)} %own_ref.11) | copy-start | bytes 6291460
  0.6 5.5 %collective-permute-start = (bf16[256,4096]{1,0:T(8,128)(2,1)}, bf16[256,4096]{1,0:T(8,128)(2,1)S(1)}, u32[]{:S(2)}, u32[]{:S(2)}) collective-permute-start(bf16[256,4096]{1,0:T(8,128)(2,1)} %own_ref.11), channel_id=1, source_target_pairs={{0,8},{1,9},{2,10},{3,11},{4,12},{5,13},{6,14},{7,15},{8,0},{9,1},... | collective-permute-start | bytes 6291464 | tf_op jit(solution)/shard_map/ppermute | solution.py:176
  4.6 1.6 %collective-permute-start.1 = (bf16[272,512]{1,0:T(8,128)(2,1)S(1)}, bf16[272,512]{1,0:T(8,128)(2,1)S(1)}, u32[]{:S(2)}, u32[]{:S(2)}) collective-permute-start(bf16[272,512]{1,0:T(8,128)(2,1)S(1)} %front.1.v0_ref), channel_id=1, source_target_pairs={{0,8},{1,9},{2,10},{3,11},{4,12},{5,13},{6,14},{7,15},{8,0},{9,1},... | collective-permute-start | bytes 835592 | tf_op jit(solution)/shard_map/ppermute | solution.py:176
  6.5 9.3 %collective-permute-start.3 = (bf16[128,512]{1,0:T(8,128)(2,1)S(1)}, bf16[128,512]{1,0:T(8,128)(2,1)S(1)}, u32[]{:S(2)}, u32[]{:S(2)}) collective-permute-start(bf16[128,512]{1,0:T(8,128)(2,1)S(1)} %partial_sums.10), channel_id=1, source_target_pairs={{0,1},{1,0},{2,3},{3,2},{4,5},{5,4},{6,7},{7,6},{8,9},{9,8},{10,11... | collective-permute-start | bytes 393224 | tf_op jit(solution)/shard_map/ppermute | solution.py:176
  9.4 8.6 %collective-permute-start.9 = (bf16[256,512]{1,0:T(8,128)(2,1)S(1)}, bf16[256,512]{1,0:T(8,128)(2,1)S(1)}, u32[]{:S(2)}, u32[]{:S(2)}) collective-permute-start(bf16[256,512]{1,0:T(8,128)(2,1)S(1)} %partial_sums.11), channel_id=1, source_target_pairs={{0,16},{1,17},{2,18},{3,19},{4,20},{5,21},{6,22},{7,23},{8,24},{9,... | collective-permute-start | bytes 786440 | tf_op jit(solution)/shard_map/ppermute | solution.py:176
  11.4 11.5 %collective-permute-start.2 = (bf16[384,256]{1,0:T(8,128)(2,1)S(1)}, bf16[384,256]{1,0:T(8,128)(2,1)S(1)}, u32[]{:S(2)}, u32[]{:S(2)}) collective-permute-start(bf16[384,256]{1,0:T(8,128)(2,1)S(1)} %get-tuple-element.27), channel_id=1, source_target_pairs={{0,2},{1,3},{2,0},{3,1},{4,6},{5,7},{6,4},{7,5},{8,10},{9,11},{10,... | collective-permute-start | bytes 589832 | tf_op jit(solution)/shard_map/ppermute | solution.py:176
  13.4 10.8 %collective-permute-start.12 = (bf16[384,256]{1,0:T(8,128)(2,1)S(1)}, bf16[384,256]{1,0:T(8,128)(2,1)S(1)}, u32[]{:S(2)}, u32[]{:S(2)}) collective-permute-start(bf16[384,256]{1,0:T(8,128)(2,1)S(1)} %get-tuple-element.29), channel_id=1, source_target_pairs={{0,2},{1,3},{2,0},{3,1},{4,6},{5,7},{6,4},{7,5},{8,10},{9,11},{10,... | collective-permute-start | bytes 589832 | tf_op jit(solution)/shard_map/ppermute | solution.py:176
  14.0 6.2 %collective-permute-start.5 = (bf16[128,512]{1,0:T(8,128)(2,1)S(1)}, bf16[128,512]{1,0:T(8,128)(2,1)S(1)}, u32[]{:S(2)}, u32[]{:S(2)}) collective-permute-start(bf16[128,512]{1,0:T(8,128)(2,1)S(1)} %get-tuple-element.35), channel_id=1, source_target_pairs={{0,1},{1,0},{2,3},{3,2},{4,5},{5,4},{6,7},{7,6},{8,9},{9,8},{10,11... | collective-permute-start | bytes 393224 | tf_op jit(solution)/shard_map/ppermute | solution.py:176
  15.8 5.4 %collective-permute-start.6 = (bf16[128,512]{1,0:T(8,128)(2,1)S(1)}, bf16[128,512]{1,0:T(8,128)(2,1)S(1)}, u32[]{:S(2)}, u32[]{:S(2)}) collective-permute-start(bf16[128,512]{1,0:T(8,128)(2,1)S(1)} %add_convert_fusion.4), channel_id=1, source_target_pairs={{0,16},{1,17},{2,18},{3,19},{4,20},{5,21},{6,22},{7,23},{8,24},{9,... | collective-permute-start | bytes 393224 | tf_op jit(solution)/shard_map/ppermute | solution.py:176
  18.0 4.9 %collective-permute-start.4 = (bf16[32,512]{1,0:T(8,128)(2,1)S(1)}, bf16[32,512]{1,0:T(8,128)(2,1)S(1)}, u32[]{:S(2)}, u32[]{:S(2)}) collective-permute-start(bf16[32,512]{1,0:T(8,128)(2,1)S(1)} %get-tuple-element.33), channel_id=1, source_target_pairs={{0,16},{1,17},{2,18},{3,19},{4,20},{5,21},{6,22},{7,23},{8,24},{9,... | collective-permute-start | bytes 98312 | tf_op jit(solution)/shard_map/ppermute | solution.py:176
  20.2 5.8 %collective-permute-start.10 = (bf16[128,512]{1,0:T(8,128)(2,1)S(1)}, bf16[128,512]{1,0:T(8,128)(2,1)S(1)}, u32[]{:S(2)}, u32[]{:S(2)}) collective-permute-start(bf16[128,512]{1,0:T(8,128)(2,1)S(1)} %add_convert_fusion.2), channel_id=1, source_target_pairs={{0,1},{1,0},{2,3},{3,2},{4,5},{5,4},{6,7},{7,6},{8,9},{9,8},{10,11... | collective-permute-start | bytes 393224 | tf_op jit(solution)/shard_map/ppermute | solution.py:176
  21.3 6.0 %collective-permute-start.11 = (bf16[128,512]{1,0:T(8,128)(2,1)S(1)}, bf16[128,512]{1,0:T(8,128)(2,1)S(1)}, u32[]{:S(2)}, u32[]{:S(2)}) collective-permute-start(bf16[128,512]{1,0:T(8,128)(2,1)S(1)} %add_convert_fusion.3), channel_id=1, source_target_pairs={{0,2},{1,3},{2,0},{3,1},{4,6},{5,7},{6,4},{7,5},{8,10},{9,11},{10,... | collective-permute-start | bytes 393224 | tf_op jit(solution)/shard_map/ppermute | solution.py:176
  23.0 7.0 %collective-permute-start.8 = (bf16[256,256]{1,0:T(8,128)(2,1)S(1)}, bf16[256,256]{1,0:T(8,128)(2,1)S(1)}, u32[]{:S(2)}, u32[]{:S(2)}) collective-permute-start(bf16[256,256]{1,0:T(8,128)(2,1)S(1)} %slice.119), channel_id=1, source_target_pairs={{0,16},{1,17},{2,18},{3,19},{4,20},{5,21},{6,22},{7,23},{8,24},{9,... | collective-permute-start | bytes 393224 | tf_op jit(solution)/shard_map/ppermute | solution.py:176
  24.4 6.4 %collective-permute-start.13 = (bf16[256,256]{1,0:T(8,128)(2,1)S(1)}, bf16[256,256]{1,0:T(8,128)(2,1)S(1)}, u32[]{:S(2)}, u32[]{:S(2)}) collective-permute-start(bf16[256,256]{1,0:T(8,128)(2,1)S(1)} %pad_maximum_fusion.2), channel_id=1, source_target_pairs={{0,1},{1,0},{2,3},{3,2},{4,5},{5,4},{6,7},{7,6},{8,9},{9,8},{10,11... | collective-permute-start | bytes 393224 | tf_op jit(solution)/shard_map/ppermute | solution.py:176
  25.2 5.6 %collective-permute-start.7 = (bf16[128,512]{1,0:T(8,128)(2,1)S(1)}, bf16[128,512]{1,0:T(8,128)(2,1)S(1)}, u32[]{:S(2)}, u32[]{:S(2)}) collective-permute-start(bf16[128,512]{1,0:T(8,128)(2,1)S(1)} %get-tuple-element.36), channel_id=1, source_target_pairs={{0,2},{1,3},{2,0},{3,1},{4,6},{5,7},{6,4},{7,5},{8,10},{9,11},{10,... | collective-permute-start | bytes 393224 | tf_op jit(solution)/shard_map/ppermute | solution.py:176
  27.3 5.9 %collective-permute-start.14 = (bf16[128,512]{1,0:T(8,128)(2,1)S(1)}, bf16[128,512]{1,0:T(8,128)(2,1)S(1)}, u32[]{:S(2)}, u32[]{:S(2)}) collective-permute-start(bf16[128,512]{1,0:T(8,128)(2,1)S(1)} %add_convert_fusion.1), channel_id=1, source_target_pairs={{0,4},{1,5},{2,6},{3,7},{4,0},{5,1},{6,2},{7,3},{8,12},{9,13},{10,... | collective-permute-start | bytes 393224 | tf_op jit(solution)/shard_map/ppermute | solution.py:176
  30.0 5.2 %collective-permute-start.15 = (bf16[128,256]{1,0:T(8,128)(2,1)S(1)}, bf16[128,256]{1,0:T(8,128)(2,1)S(1)}, u32[]{:S(2)}, u32[]{:S(2)}) collective-permute-start(bf16[128,256]{1,0:T(8,128)(2,1)S(1)} %fusion.1), channel_id=1, source_target_pairs={{0,1},{1,0},{2,3},{3,2},{4,5},{5,4},{6,7},{7,6},{8,9},{9,8},{10,11... | collective-permute-start | bytes 196616 | tf_op jit(solution)/shard_map/ppermute | solution.py:176
  30.8 4.3 %collective-permute-start.16 = (bf16[128,256]{1,0:T(8,128)(2,1)S(1)}, bf16[128,256]{1,0:T(8,128)(2,1)S(1)}, u32[]{:S(2)}, u32[]{:S(2)}) collective-permute-start(bf16[128,256]{1,0:T(8,128)(2,1)S(1)} %get-tuple-element.54), channel_id=1, source_target_pairs={{0,16},{1,17},{2,18},{3,19},{4,20},{5,21},{6,22},{7,23},{8,24},{9,... | collective-permute-start | bytes 196616 | tf_op jit(solution)/shard_map/ppermute | solution.py:176
  35.2 5.0 %collective-permute-start.17 = (bf16[128,512]{1,0:T(8,128)(2,1)S(1)}, bf16[128,512]{1,0:T(8,128)(2,1)S(1)}, u32[]{:S(2)}, u32[]{:S(2)}) collective-permute-start(bf16[128,512]{1,0:T(8,128)(2,1)S(1)} %add_convert_fusion), channel_id=1, source_target_pairs={{0,16},{1,17},{2,18},{3,19},{4,20},{5,21},{6,22},{7,23},{8,24},{9,... | collective-permute-start | bytes 393224 | tf_op jit(solution)/shard_map/ppermute | solution.py:176
  40.3 1.6 %collective-permute-start.18 = (bf16[2,128,512]{2,1,0:T(8,128)(2,1)S(1)}, bf16[2,128,512]{2,1,0:T(8,128)(2,1)S(1)}, u32[]{:S(2)}, u32[]{:S(2)}) collective-permute-start(bf16[2,128,512]{2,1,0:T(8,128)(2,1)S(1)} %pad_maximum_fusion.1.pair_ref), channel_id=1, source_target_pairs={{0,8},{1,9},{2,10},{3,11},{4,12},{5,13},{6,14},{7,15},{8,0},{9,1},... | collective-permute-start | bytes 786440 | tf_op jit(solution)/shard_map/ppermute | solution.py:176

commit v18 on v17

--- a/solution.py
+++ b/solution.py
@@ -333,30 +333,33 @@
         return total
 
     far_b, = sums([(((3, 1, 1),), 0, 512)], BF16)
-    first_a, = sums([(((2, 1, 1), (2, 1, 0)), 0, 512)], BF16)
+    far_a, = sums([(((2, 1, 1),), 0, 512)], BF16)
     every = ((1, 1), (1, 0), (0, 1), (0, 0))
     side_b, pair_some = sums([(((3, 0, 1),), 0, 512), (tuple((1, *at) for at in every[:3]), 0, 256)], BF16)
-    pair_rest, pair_own = sums(
-        [(tuple((1, *at) for at in every[:3]), 256, 256), (((1, 0, 0),), 0, 512)], BF16, after_all(v0, pair_some)[0]
+    pair_rest, side_a = sums(
+        [(tuple((1, *at) for at in every[:3]), 256, 256), (((2, 1, 0),), 0, 512)], BF16, after_all(v0, pair_some)[0]
     )
     keep_b, keep_a = sums([(((3, 1, 0), (3, 0, 0)), 0, 512), (((2, 0, 1), (2, 0, 0)), 0, 512)], F32)
-    own_some, own_rest = sums([(tuple((0, *at) for at in every), start, 256) for start in (0, 256)], F32)
     far_b = xor_permute(far_b, X)
     side_b = xor_permute(side_b, X)
-    first_a = xor_permute(first_a, Y)
-    pair_sent = pair_rest
+    far_a = xor_permute(far_a, Y)
     pair_some = xor_permute(pair_some, Z1)
     pair_rest = xor_permute(pair_rest, Z1)
+    far_b, far_a = after_all(far_b, far_a)
     on_b = add(keep_b[:LANE], far_b).astype(BF16)
-    rows, window = inner_swap(after_all(v0, pair_sent)[0], v1)
-    window = xor_permute(after_all(window, on_b)[0], Y)
+    v0_late = after_all(v0, on_b)[0]
+    rows, window = inner_swap(v0_late, v1)
+    own_some, own_rest = sums([(tuple((0, *at) for at in every), start, 256) for start in (0, 256)], F32, v0_late)
+    pair_own, = sums([(((1, 0, 0),), 0, 512)], BF16, v0_late)
     on_b = xor_permute(on_b, Y)
-    on_a = xor_permute(add(keep_a[:LANE], first_a[:LANE]).astype(BF16), X)
+    side_a = xor_permute(jnp.concatenate([side_a, window]), Y)
+    side_a, window = side_a[:LANE], side_a[LANE:]
+    on_a = xor_permute(add(keep_a[:LANE], far_a).astype(BF16), X)
     z3 = add(keep_b[LANE:], side_b, on_b).astype(BF16)
-    pair_some, window, pair_own = after_all(pair_some, window, pair_own, z3)[:3]
+    pair_some, pair_own = after_all(pair_some, pair_own, z3)[:2]
     z3 = xor_permute(z3, Z1)
     pair_own = xor_permute(pair_own, Z1)
-    z2 = add(keep_a[LANE:], first_a[LANE:], on_a, z3).astype(BF16)
+    z2 = add(keep_a[LANE:], side_a, on_a, z3).astype(BF16)
 
     some = add(own_some[:3 * LANE], pair_some)
     some_in = xor_permute(some[:2 * LANE].astype(BF16), Y)

time: 42.9 us -> 44 us (1.026)
  starting transfers between devices: 21.2 us -> 22.3 us
    ppermute x19, starting transfers between devices: 21.2 us -> 22.3 us  [xor_permute(): lax.ppermute(value, ('dp', 'fsdp'), [(i, i ^ mask) for i in range(count)])]
    pallas_call x6 -> x7, Pallas kernels: 2.37 us -> 2.55 us  [partial_sums(): pl.pallas_call(functools.partial(partial_kernel, parts), in_specs=[VMEM]...]
  transfers between devices with their start and end apart: 19 -> 19, of which waited for: 8 -> 7; matrix products, arithmetic and copies ran while one was open for 1% -> 1% of each run, Pallas kernels for 16% -> 16%
where the time goes in v18:
time: 44 us; the launch traced here: 43.8 us
  starting transfers between devices  22.3 us (51%)
  waiting for transfers between devices  11.4 us (26%)
  Pallas kernels  8.1 us (18%)
  between operations  1.6 us (4%)
    ppermute x19, starting transfers between devices, xor_permute(): lax.ppermute(value, ('dp', 'fsdp'), [(i, i ^ mask) for i in range(count)])  22.3 us
    ppermute x19, waiting for transfers between devices, xor_permute(): lax.ppermute(value, ('dp', 'fsdp'), [(i, i ^ mask) for i in range(count)])  11.4 us
    pallas_call x1, Pallas kernels, front(): pl.pallas_call(functools.partial(front_kernel, per_group), in_specs=[HBM]...  2.64 us
    pallas_call x7, Pallas kernels, partial_sums(): pl.pallas_call(functools.partial(partial_kernel, parts), in_specs=[VMEM]...  2.55 us
    pallas_call x2, Pallas kernels, place(): pl.pallas_call(functools.partial(place_kernel, core), in_specs=[VMEM] + [...  1.65 us
    pallas_call x1, Pallas kernels, outer_swap(): pl.pallas_call(outer_swap_kernel, in_specs=[VMEM] * 3, out_specs=VMEM, ou...  0.92 us
  transfers between devices with their start and end apart: 19, of which 7 were waited for; matrix products, arithmetic and copies ran while one was open for 1% of the time, Pallas kernels for 16%

profile of v18, /device:TPU:0, one launch (start us, length us, event | category | flops | bytes accessed | tf_op | source)
XLA Modules:
  0.0 43.8 jit_solution(15840490771478310622)
XLA Ops:
  0.6 0.5 %collective-permute-start = (bf16[256,4096]{1,0:T(8,128)(2,1)}, bf16[256,4096]{1,0:T(8,128)(2,1)S(1)}, u32[]{:S(2)}, u32[]{:S(2)}) collective-permute-start(bf16[256,4096]{1,0:T(8,128)(2,1)} %own_ref.13), channel_id=1, source_target_pairs={{0,8},{1,9},{2,10},{3,11},{4,12},{5,13},{6,14},{7,15},{8,0},{9,1},... | collective-permute-start | bytes 6291464 | tf_op jit(solution)/shard_map/ppermute | solution.py:176
  1.9 2.6 %front.1.v0_ref = bf16[272,512]{1,0:T(8,128)(2,1)S(1)} custom-call(f32[16]{0:T(128)} %loss_hbm.1, s32[1]{0:T(128)S(6)} %copy.14.exponent_hbm, s32[1,2]{1,0:T(1,128)} %start_hbm.1, s32[1,2]{1,0:T(1,128)} %rows_hbm.1, bf16[256,2048]{1,0:T(8,128)(2,1)} %q_hbm.1, bf16[256,512]{1,0:T(8,128)(2,1)} %k_hbm.1, bf16[256,2048]{1,0:T(8,128)(2,1)} %g_hbm.1, ...), custom_call_target="tpu_custom_call" | custom-call | tf_op jit(solution)/shard_map/front/pallas_call | solution.py:153
  4.6 0.1 collective-permute-start.1
  4.7 1.5 %collective-permute-done.1.v1_ref = bf16[272,512]{1,0:T(8,128)(2,1)S(1)} collective-permute-done((bf16[272,512]{1,0:T(8,128)(2,1)S(1)}, bf16[272,512]{1,0:T(8,128)(2,1)S(1)}, u32[]{:S(2)}, u32[]{:S(2)}) %collective-permute-start.1) | collective-permute-done | bytes 278560 | tf_op jit(solution)/shard_map/ppermute | solution.py:176
  6.2 0.0 collective-permute-done.near_ref
  6.2 0.3 partial_sums.8
  6.5 2.6 %collective-permute-start.2 = (bf16[128,512]{1,0:T(8,128)(2,1)S(1)}, bf16[128,512]{1,0:T(8,128)(2,1)S(1)}, u32[]{:S(2)}, u32[]{:S(2)}) collective-permute-start(bf16[128,512]{1,0:T(8,128)(2,1)S(1)} %partial_sums.8), channel_id=1, source_target_pairs={{0,1},{1,0},{2,3},{3,2},{4,5},{5,4},{6,7},{7,6},{8,9},{9,8},{10,11... | collective-permute-start | bytes 393224 | tf_op jit(solution)/shard_map/ppermute | solution.py:176
  9.1 0.3 partial_sums.9
  9.3 1.6 %collective-permute-start.3 = (bf16[128,512]{1,0:T(8,128)(2,1)S(1)}, bf16[128,512]{1,0:T(8,128)(2,1)S(1)}, u32[]{:S(2)}, u32[]{:S(2)}) collective-permute-start(bf16[128,512]{1,0:T(8,128)(2,1)S(1)} %partial_sums.9), channel_id=1, source_target_pairs={{0,16},{1,17},{2,18},{3,19},{4,20},{5,21},{6,22},{7,23},{8,24},{9,... | collective-permute-start | bytes 393224 | tf_op jit(solution)/shard_map/ppermute | solution.py:176
  10.9 0.4 partial_sums.11
  11.3 1.6 %collective-permute-start.4 = (bf16[384,256]{1,0:T(8,128)(2,1)S(1)}, bf16[384,256]{1,0:T(8,128)(2,1)S(1)}, u32[]{:S(2)}, u32[]{:S(2)}) collective-permute-start(bf16[384,256]{1,0:T(8,128)(2,1)S(1)} %get-tuple-element.30), channel_id=1, source_target_pairs={{0,2},{1,3},{2,0},{3,1},{4,6},{5,7},{6,4},{7,5},{8,10},{9,11},{10,... | collective-permute-start | bytes 589832 | tf_op jit(solution)/shard_map/ppermute | solution.py:176
  13.0 0.5 %collective-permute-start.5 = (bf16[128,512]{1,0:T(8,128)(2,1)S(1)}, bf16[128,512]{1,0:T(8,128)(2,1)S(1)}, u32[]{:S(2)}, u32[]{:S(2)}) collective-permute-start(bf16[128,512]{1,0:T(8,128)(2,1)S(1)} %get-tuple-element.31), channel_id=1, source_target_pairs={{0,1},{1,0},{2,3},{3,2},{4,5},{5,4},{6,7},{7,6},{8,9},{9,8},{10,11... | collective-permute-start | bytes 393224 | tf_op jit(solution)/shard_map/ppermute | solution.py:176
  13.5 0.4 partial_sums.13
  13.9 0.5 %collective-permute-start.12 = (bf16[384,256]{1,0:T(8,128)(2,1)S(1)}, bf16[384,256]{1,0:T(8,128)(2,1)S(1)}, u32[]{:S(2)}, u32[]{:S(2)}) collective-permute-start(bf16[384,256]{1,0:T(8,128)(2,1)S(1)} %get-tuple-element.41), channel_id=1, source_target_pairs={{0,2},{1,3},{2,0},{3,1},{4,6},{5,7},{6,4},{7,5},{8,10},{9,11},{10,... | collective-permute-start | bytes 589832 | tf_op jit(solution)/shard_map/ppermute | solution.py:176
  14.4 0.5 %partial_sums.7 = (f32[256,512]{1,0:T(8,128)S(1)}, f32[256,512]{1,0:T(8,128)S(1)}) custom-call(bf16[256,4096]{1,0:T(8,128)(2,1)S(1)} %copy-done, bf16[256,4096]{1,0:T(8,128)(2,1)S(1)} %collective-permute-done.near_ref, bf16[272,512]{1,0:T(8,128)(2,1)S(1)} %front.1.v0_ref, bf16[272,512]{1,0:T(8,128)(2,1)S(1)} %collective-permute-done.1.v1_ref), custom_call_target="tpu_custom_call" | custom-call | tf_op jit(solution)/shard_map/partial_sums/pallas_call | solution.py:201
  14.9 0.0 collective-permute-done.2
  14.9 0.0 collective-permute-done.3
  15.0 1.5 %collective-permute-start.6 = (bf16[128,512]{1,0:T(8,128)(2,1)S(1)}, bf16[128,512]{1,0:T(8,128)(2,1)S(1)}, u32[]{:S(2)}, u32[]{:S(2)}) collective-permute-start(bf16[128,512]{1,0:T(8,128)(2,1)S(1)} %add_convert_fusion.4), channel_id=1, source_target_pairs={{0,16},{1,17},{2,18},{3,19},{4,20},{5,21},{6,22},{7,23},{8,24},{9,... | collective-permute-start | bytes 393224 | tf_op jit(solution)/shard_map/ppermute | solution.py:176
  16.5 0.3 inner_swap.1
  16.9 0.6 %collective-permute-start.9 = (bf16[160,512]{1,0:T(8,128)(2,1)S(1)}, bf16[160,512]{1,0:T(8,128)(2,1)S(1)}, u32[]{:S(2)}, u32[]{:S(2)}) collective-permute-start(bf16[160,512]{1,0:T(8,128)(2,1)S(1)} %pad_maximum_fusion.2), channel_id=1, source_target_pairs={{0,16},{1,17},{2,18},{3,19},{4,20},{5,21},{6,22},{7,23},{8,24},{9,... | collective-permute-start | bytes 491528 | tf_op jit(solution)/shard_map/ppermute | solution.py:176
  17.5 0.3 partial_sums.12
  17.7 0.5 %partial_sums.10 = (f32[512,256]{1,0:T(8,128)S(1)}, f32[512,256]{1,0:T(8,128)S(1)}) custom-call(bf16[256,4096]{1,0:T(8,128)(2,1)S(1)} %copy-done, bf16[256,4096]{1,0:T(8,128)(2,1)S(1)} %collective-permute-done.near_ref, bf16[272,512]{1,0:T(8,128)(2,1)S(1)} %front.1.v0_ref, bf16[272,512]{1,0:T(8,128)(2,1)S(1)} %collective-permute-done.1.v1_ref), custom_call_target="tpu_custom_call" | custom-call | tf_op jit(solution)/shard_map/partial_sums/pallas_call | solution.py:201
  18.3 0.0 collective-permute-done.5
  18.3 1.6 %collective-permute-start.10 = (bf16[128,512]{1,0:T(8,128)(2,1)S(1)}, bf16[128,512]{1,0:T(8,128)(2,1)S(1)}, u32[]{:S(2)}, u32[]{:S(2)}) collective-permute-start(bf16[128,512]{1,0:T(8,128)(2,1)S(1)} %add_convert_fusion.2), channel_id=1, source_target_pairs={{0,1},{1,0},{2,3},{3,2},{4,5},{5,4},{6,7},{7,6},{8,9},{9,8},{10,11... | collective-permute-start | bytes 393224 | tf_op jit(solution)/shard_map/ppermute | solution.py:176
  19.8 1.6 %collective-permute-done.6 = bf16[128,512]{1,0:T(8,128)(2,1)S(1)} collective-permute-done((bf16[128,512]{1,0:T(8,128)(2,1)S(1)}, bf16[128,512]{1,0:T(8,128)(2,1)S(1)}, u32[]{:S(2)}, u32[]{:S(2)}) %collective-permute-start.6) | collective-permute-done | bytes 131104 | tf_op jit(solution)/shard_map/ppermute | solution.py:176
  21.4 1.6 %collective-permute-start.11 = (bf16[128,512]{1,0:T(8,128)(2,1)S(1)}, bf16[128,512]{1,0:T(8,128)(2,1)S(1)}, u32[]{:S(2)}, u32[]{:S(2)}) collective-permute-start(bf16[128,512]{1,0:T(8,128)(2,1)S(1)} %add_convert_fusion.3), channel_id=1, source_target_pairs={{0,2},{1,3},{2,0},{3,1},{4,6},{5,7},{6,4},{7,5},{8,10},{9,11},{10,... | collective-permute-start | bytes 393224 | tf_op jit(solution)/shard_map/ppermute | solution.py:176
  23.1 0.0 collective-permute-done.4
  23.1 1.6 %collective-permute-start.8 = (bf16[256,256]{1,0:T(8,128)(2,1)S(1)}, bf16[256,256]{1,0:T(8,128)(2,1)S(1)}, u32[]{:S(2)}, u32[]{:S(2)}) collective-permute-start(bf16[256,256]{1,0:T(8,128)(2,1)S(1)} %slice.118), channel_id=1, source_target_pairs={{0,16},{1,17},{2,18},{3,19},{4,20},{5,21},{6,22},{7,23},{8,24},{9,... | collective-permute-start | bytes 393224 | tf_op jit(solution)/shard_map/ppermute | solution.py:176
  24.8 0.6 %collective-permute-start.13 = (bf16[256,256]{1,0:T(8,128)(2,1)S(1)}, bf16[256,256]{1,0:T(8,128)(2,1)S(1)}, u32[]{:S(2)}, u32[]{:S(2)}) collective-permute-start(bf16[256,256]{1,0:T(8,128)(2,1)S(1)} %pad_maximum_fusion.3), channel_id=1, source_target_pairs={{0,1},{1,0},{2,3},{3,2},{4,5},{5,4},{6,7},{7,6},{8,9},{9,8},{10,11... | collective-permute-start | bytes 393224 | tf_op jit(solution)/shard_map/ppermute | solution.py:176
  25.4 0.5 %collective-permute-start.7 = (bf16[128,512]{1,0:T(8,128)(2,1)S(1)}, bf16[128,512]{1,0:T(8,128)(2,1)S(1)}, u32[]{:S(2)}, u32[]{:S(2)}) collective-permute-start(bf16[128,512]{1,0:T(8,128)(2,1)S(1)} %partial_sums.12), channel_id=1, source_target_pairs={{0,2},{1,3},{2,0},{3,1},{4,6},{5,7},{6,4},{7,5},{8,10},{9,11},{10,... | collective-permute-start | bytes 393224 | tf_op jit(solution)/shard_map/ppermute | solution.py:176
  25.9 1.1 %collective-permute-done.11 = bf16[128,512]{1,0:T(8,128)(2,1)S(1)} collective-permute-done((bf16[128,512]{1,0:T(8,128)(2,1)S(1)}, bf16[128,512]{1,0:T(8,128)(2,1)S(1)}, u32[]{:S(2)}, u32[]{:S(2)}) %collective-permute-start.11) | collective-permute-done | bytes 131104 | tf_op jit(solution)/shard_map/ppermute | solution.py:176
  26.9 0.1 add_convert_fusion.1
  27.0 3.2 %collective-permute-start.14 = (bf16[128,512]{1,0:T(8,128)(2,1)S(1)}, bf16[128,512]{1,0:T(8,128)(2,1)S(1)}, u32[]{:S(2)}, u32[]{:S(2)}) collective-permute-start(bf16[128,512]{1,0:T(8,128)(2,1)S(1)} %add_convert_fusion.1), channel_id=1, source_target_pairs={{0,4},{1,5},{2,6},{3,7},{4,0},{5,1},{6,2},{7,3},{8,12},{9,13},{10,... | collective-permute-start | bytes 393224 | tf_op jit(solution)/shard_map/ppermute | solution.py:176
  30.2 0.0 collective-permute-done.8
  30.3 1.6 %collective-permute-start.15 = (bf16[128,256]{1,0:T(8,128)(2,1)S(1)}, bf16[128,256]{1,0:T(8,128)(2,1)S(1)}, u32[]{:S(2)}, u32[]{:S(2)}) collective-permute-start(bf16[128,256]{1,0:T(8,128)(2,1)S(1)} %fusion.1), channel_id=1, source_target_pairs={{0,1},{1,0},{2,3},{3,2},{4,5},{5,4},{6,7},{7,6},{8,9},{9,8},{10,11... | collective-permute-start | bytes 196616 | tf_op jit(solution)/shard_map/ppermute | solution.py:176
  31.9 0.0 collective-permute-done.13
  31.9 0.0 collective-permute-done.7
  31.9 0.1 fusion
  31.9 0.9 %collective-permute-start.16 = (bf16[128,256]{1,0:T(8,128)(2,1)S(1)}, bf16[128,256]{1,0:T(8,128)(2,1)S(1)}, u32[]{:S(2)}, u32[]{:S(2)}) collective-permute-start(bf16[128,256]{1,0:T(8,128)(2,1)S(1)} %get-tuple-element.54), channel_id=1, source_target_pairs={{0,16},{1,17},{2,18},{3,19},{4,20},{5,21},{6,22},{7,23},{8,24},{9,... | collective-permute-start | bytes 196616 | tf_op jit(solution)/shard_map/ppermute | solution.py:176
  32.9 1.7 %collective-permute-done.14.arrived_ref = bf16[128,512]{1,0:T(8,128)(2,1)S(1)} collective-permute-done((bf16[128,512]{1,0:T(8,128)(2,1)S(1)}, bf16[128,512]{1,0:T(8,128)(2,1)S(1)}, u32[]{:S(2)}, u32[]{:S(2)}) %collective-permute-start.14) | collective-permute-done | bytes 131104 | tf_op jit(solution)/shard_map/ppermute | solution.py:176
  34.6 1.7 %collective-permute-done.16 = bf16[128,256]{1,0:T(8,128)(2,1)S(1)} collective-permute-done((bf16[128,256]{1,0:T(8,128)(2,1)S(1)}, bf16[128,256]{1,0:T(8,128)(2,1)S(1)}, u32[]{:S(2)}, u32[]{:S(2)}) %collective-permute-start.16) | collective-permute-done | bytes 65568 | tf_op jit(solution)/shard_map/ppermute | solution.py:176
  36.3 0.9 %collective-permute-start.17 = (bf16[128,512]{1,0:T(8,128)(2,1)S(1)}, bf16[128,512]{1,0:T(8,128)(2,1)S(1)}, u32[]{:S(2)}, u32[]{:S(2)}) collective-permute-start(bf16[128,512]{1,0:T(8,128)(2,1)S(1)} %add_convert_fusion), channel_id=1, source_target_pairs={{0,16},{1,17},{2,18},{3,19},{4,20},{5,21},{6,22},{7,23},{8,24},{9,... | collective-permute-start | bytes 393224 | tf_op jit(solution)/shard_map/ppermute | solution.py:176
  37.2 0.9 %outer_swap.1 = bf16[256,512]{1,0:T(8,128)(2,1)} custom-call(bf16[272,512]{1,0:T(8,128)(2,1)S(1)} %front.1.v0_ref, bf16[256,512]{1,0:T(8,128)(2,1)S(1)} %get-tuple-element.44.rows_ref, bf16[32,512]{1,0:T(8,128)(2,1)S(1)} %slice.95.window_ref), custom_call_target="tpu_custom_call" | custom-call | tf_op jit(solution)/shard_map/outer_swap/pallas_call | solution.py:265
  38.1 3.2 %collective-permute-done.17 = bf16[128,512]{1,0:T(8,128)(2,1)S(1)} collective-permute-done((bf16[128,512]{1,0:T(8,128)(2,1)S(1)}, bf16[128,512]{1,0:T(8,128)(2,1)S(1)}, u32[]{:S(2)}, u32[]{:S(2)}) %collective-permute-start.17) | collective-permute-done | bytes 131104 | tf_op jit(solution)/shard_map/ppermute | solution.py:176
  41.4 0.1 collective-permute-start.18
  41.4 0.8 %place.2.rest_0_ = f32[512,512]{1,0:T(8,128)} custom-call(bf16[2,128,512]{2,1,0:T(8,128)(2,1)S(1)} %pad_maximum_fusion.1.pair_ref), custom_call_target="tpu_custom_call" | custom-call | tf_op jit(solution)/shard_map/place/pallas_call | solution.py:289
  42.3 0.7 %collective-permute-done.18.pair_ref = bf16[2,128,512]{2,1,0:T(8,128)(2,1)S(1)} collective-permute-done((bf16[2,128,512]{2,1,0:T(8,128)(2,1)S(1)}, bf16[2,128,512]{2,1,0:T(8,128)(2,1)S(1)}, u32[]{:S(2)}, u32[]{:S(2)}) %collective-permute-start.18) | collective-permute-done | bytes 262176 | tf_op jit(solution)/shard_map/ppermute | solution.py:176
  43.0 0.8 %place.3 = f32[512,512]{1,0:T(8,128)} custom-call(bf16[2,128,512]{2,1,0:T(8,128)(2,1)S(1)} %collective-permute-done.18.pair_ref, f32[512,512]{1,0:T(8,128)} %place.2.rest_0_), custom_call_target="tpu_custom_call", output_to_operand_aliasing={{}: (1, {})} | custom-call | tf_op jit(solution)/shard_map/place/pallas_call | solution.py:289
  (21 shorter events, 0.4 us)
Async XLA Ops:
  0.6 5.6 %copy-start = (bf16[256,4096]{1,0:T(8,128)(2,1)S(1)}, bf16[256,4096]{1,0:T(8,128)(2,1)}, u32[]{:S(2)}) copy-start(bf16[256,4096]{1,0:T(8,128)(2,1)} %own_ref.13) | copy-start | bytes 6291460
  0.6 5.5 %collective-permute-start = (bf16[256,4096]{1,0:T(8,128)(2,1)}, bf16[256,4096]{1,0:T(8,128)(2,1)S(1)}, u32[]{:S(2)}, u32[]{:S(2)}) collective-permute-start(bf16[256,4096]{1,0:T(8,128)(2,1)} %own_ref.13), channel_id=1, source_target_pairs={{0,8},{1,9},{2,10},{3,11},{4,12},{5,13},{6,14},{7,15},{8,0},{9,1},... | collective-permute-start | bytes 6291464 | tf_op jit(solution)/shard_map/ppermute | solution.py:176
  4.6 1.6 %collective-permute-start.1 = (bf16[272,512]{1,0:T(8,128)(2,1)S(1)}, bf16[272,512]{1,0:T(8,128)(2,1)S(1)}, u32[]{:S(2)}, u32[]{:S(2)}) collective-permute-start(bf16[272,512]{1,0:T(8,128)(2,1)S(1)} %front.1.v0_ref), channel_id=1, source_target_pairs={{0,8},{1,9},{2,10},{3,11},{4,12},{5,13},{6,14},{7,15},{8,0},{9,1},... | collective-permute-start | bytes 835592 | tf_op jit(solution)/shard_map/ppermute | solution.py:176
  6.5 8.4 %collective-permute-start.2 = (bf16[128,512]{1,0:T(8,128)(2,1)S(1)}, bf16[128,512]{1,0:T(8,128)(2,1)S(1)}, u32[]{:S(2)}, u32[]{:S(2)}) collective-permute-start(bf16[128,512]{1,0:T(8,128)(2,1)S(1)} %partial_sums.8), channel_id=1, source_target_pairs={{0,1},{1,0},{2,3},{3,2},{4,5},{5,4},{6,7},{7,6},{8,9},{9,8},{10,11... | collective-permute-start | bytes 393224 | tf_op jit(solution)/shard_map/ppermute | solution.py:176
  9.3 5.6 %collective-permute-start.3 = (bf16[128,512]{1,0:T(8,128)(2,1)S(1)}, bf16[128,512]{1,0:T(8,128)(2,1)S(1)}, u32[]{:S(2)}, u32[]{:S(2)}) collective-permute-start(bf16[128,512]{1,0:T(8,128)(2,1)S(1)} %partial_sums.9), channel_id=1, source_target_pairs={{0,16},{1,17},{2,18},{3,19},{4,20},{5,21},{6,22},{7,23},{8,24},{9,... | collective-permute-start | bytes 393224 | tf_op jit(solution)/shard_map/ppermute | solution.py:176
  11.3 11.8 %collective-permute-start.4 = (bf16[384,256]{1,0:T(8,128)(2,1)S(1)}, bf16[384,256]{1,0:T(8,128)(2,1)S(1)}, u32[]{:S(2)}, u32[]{:S(2)}) collective-permute-start(bf16[384,256]{1,0:T(8,128)(2,1)S(1)} %get-tuple-element.30), channel_id=1, source_target_pairs={{0,2},{1,3},{2,0},{3,1},{4,6},{5,7},{6,4},{7,5},{8,10},{9,11},{10,... | collective-permute-start | bytes 589832 | tf_op jit(solution)/shard_map/ppermute | solution.py:176
  13.0 5.3 %collective-permute-start.5 = (bf16[128,512]{1,0:T(8,128)(2,1)S(1)}, bf16[128,512]{1,0:T(8,128)(2,1)S(1)}, u32[]{:S(2)}, u32[]{:S(2)}) collective-permute-start(bf16[128,512]{1,0:T(8,128)(2,1)S(1)} %get-tuple-element.31), channel_id=1, source_target_pairs={{0,1},{1,0},{2,3},{3,2},{4,5},{5,4},{6,7},{7,6},{8,9},{9,8},{10,11... | collective-permute-start | bytes 393224 | tf_op jit(solution)/shard_map/ppermute | solution.py:176
  13.9 10.8 %collective-permute-start.12 = (bf16[384,256]{1,0:T(8,128)(2,1)S(1)}, bf16[384,256]{1,0:T(8,128)(2,1)S(1)}, u32[]{:S(2)}, u32[]{:S(2)}) collective-permute-start(bf16[384,256]{1,0:T(8,128)(2,1)S(1)} %get-tuple-element.41), channel_id=1, source_target_pairs={{0,2},{1,3},{2,0},{3,1},{4,6},{5,7},{6,4},{7,5},{8,10},{9,11},{10,... | collective-permute-start | bytes 589832 | tf_op jit(solution)/shard_map/ppermute | solution.py:176
  15.0 6.4 %collective-permute-start.6 = (bf16[128,512]{1,0:T(8,128)(2,1)S(1)}, bf16[128,512]{1,0:T(8,128)(2,1)S(1)}, u32[]{:S(2)}, u32[]{:S(2)}) collective-permute-start(bf16[128,512]{1,0:T(8,128)(2,1)S(1)} %add_convert_fusion.4), channel_id=1, source_target_pairs={{0,16},{1,17},{2,18},{3,19},{4,20},{5,21},{6,22},{7,23},{8,24},{9,... | collective-permute-start | bytes 393224 | tf_op jit(solution)/shard_map/ppermute | solution.py:176
  16.9 9.0 %collective-permute-start.9 = (bf16[160,512]{1,0:T(8,128)(2,1)S(1)}, bf16[160,512]{1,0:T(8,128)(2,1)S(1)}, u32[]{:S(2)}, u32[]{:S(2)}) collective-permute-start(bf16[160,512]{1,0:T(8,128)(2,1)S(1)} %pad_maximum_fusion.2), channel_id=1, source_target_pairs={{0,16},{1,17},{2,18},{3,19},{4,20},{5,21},{6,22},{7,23},{8,24},{9,... | collective-permute-start | bytes 491528 | tf_op jit(solution)/shard_map/ppermute | solution.py:176
  18.3 7.1 %collective-permute-start.10 = (bf16[128,512]{1,0:T(8,128)(2,1)S(1)}, bf16[128,512]{1,0:T(8,128)(2,1)S(1)}, u32[]{:S(2)}, u32[]{:S(2)}) collective-permute-start(bf16[128,512]{1,0:T(8,128)(2,1)S(1)} %add_convert_fusion.2), channel_id=1, source_target_pairs={{0,1},{1,0},{2,3},{3,2},{4,5},{5,4},{6,7},{7,6},{8,9},{9,8},{10,11... | collective-permute-start | bytes 393224 | tf_op jit(solution)/shard_map/ppermute | solution.py:176
  21.4 5.5 %collective-permute-start.11 = (bf16[128,512]{1,0:T(8,128)(2,1)S(1)}, bf16[128,512]{1,0:T(8,128)(2,1)S(1)}, u32[]{:S(2)}, u32[]{:S(2)}) collective-permute-start(bf16[128,512]{1,0:T(8,128)(2,1)S(1)} %add_convert_fusion.3), channel_id=1, source_target_pairs={{0,2},{1,3},{2,0},{3,1},{4,6},{5,7},{6,4},{7,5},{8,10},{9,11},{10,... | collective-permute-start | bytes 393224 | tf_op jit(solution)/shard_map/ppermute | solution.py:176
  23.1 7.1 %collective-permute-start.8 = (bf16[256,256]{1,0:T(8,128)(2,1)S(1)}, bf16[256,256]{1,0:T(8,128)(2,1)S(1)}, u32[]{:S(2)}, u32[]{:S(2)}) collective-permute-start(bf16[256,256]{1,0:T(8,128)(2,1)S(1)} %slice.118), channel_id=1, source_target_pairs={{0,16},{1,17},{2,18},{3,19},{4,20},{5,21},{6,22},{7,23},{8,24},{9,... | collective-permute-start | bytes 393224 | tf_op jit(solution)/shard_map/ppermute | solution.py:176
  24.8 7.1 %collective-permute-start.13 = (bf16[256,256]{1,0:T(8,128)(2,1)S(1)}, bf16[256,256]{1,0:T(8,128)(2,1)S(1)}, u32[]{:S(2)}, u32[]{:S(2)}) collective-permute-start(bf16[256,256]{1,0:T(8,128)(2,1)S(1)} %pad_maximum_fusion.3), channel_id=1, source_target_pairs={{0,1},{1,0},{2,3},{3,2},{4,5},{5,4},{6,7},{7,6},{8,9},{9,8},{10,11... | collective-permute-start | bytes 393224 | tf_op jit(solution)/shard_map/ppermute | solution.py:176
  25.4 6.5 %collective-permute-start.7 = (bf16[128,512]{1,0:T(8,128)(2,1)S(1)}, bf16[128,512]{1,0:T(8,128)(2,1)S(1)}, u32[]{:S(2)}, u32[]{:S(2)}) collective-permute-start(bf16[128,512]{1,0:T(8,128)(2,1)S(1)} %partial_sums.12), channel_id=1, source_target_pairs={{0,2},{1,3},{2,0},{3,1},{4,6},{5,7},{6,4},{7,5},{8,10},{9,11},{10,... | collective-permute-start | bytes 393224 | tf_op jit(solution)/shard_map/ppermute | solution.py:176
  27.0 7.6 %collective-permute-start.14 = (bf16[128,512]{1,0:T(8,128)(2,1)S(1)}, bf16[128,512]{1,0:T(8,128)(2,1)S(1)}, u32[]{:S(2)}, u32[]{:S(2)}) collective-permute-start(bf16[128,512]{1,0:T(8,128)(2,1)S(1)} %add_convert_fusion.1), channel_id=1, source_target_pairs={{0,4},{1,5},{2,6},{3,7},{4,0},{5,1},{6,2},{7,3},{8,12},{9,13},{10,... | collective-permute-start | bytes 393224 | tf_op jit(solution)/shard_map/ppermute | solution.py:176
  30.3 6.0 %collective-permute-start.15 = (bf16[128,256]{1,0:T(8,128)(2,1)S(1)}, bf16[128,256]{1,0:T(8,128)(2,1)S(1)}, u32[]{:S(2)}, u32[]{:S(2)}) collective-permute-start(bf16[128,256]{1,0:T(8,128)(2,1)S(1)} %fusion.1), channel_id=1, source_target_pairs={{0,1},{1,0},{2,3},{3,2},{4,5},{5,4},{6,7},{7,6},{8,9},{9,8},{10,11... | collective-permute-start | bytes 196616 | tf_op jit(solution)/shard_map/ppermute | solution.py:176
  31.9 4.3 %collective-permute-start.16 = (bf16[128,256]{1,0:T(8,128)(2,1)S(1)}, bf16[128,256]{1,0:T(8,128)(2,1)S(1)}, u32[]{:S(2)}, u32[]{:S(2)}) collective-permute-start(bf16[128,256]{1,0:T(8,128)(2,1)S(1)} %get-tuple-element.54), channel_id=1, source_target_pairs={{0,16},{1,17},{2,18},{3,19},{4,20},{5,21},{6,22},{7,23},{8,24},{9,... | collective-permute-start | bytes 196616 | tf_op jit(solution)/shard_map/ppermute | solution.py:176
  36.3 5.0 %collective-permute-start.17 = (bf16[128,512]{1,0:T(8,128)(2,1)S(1)}, bf16[128,512]{1,0:T(8,128)(2,1)S(1)}, u32[]{:S(2)}, u32[]{:S(2)}) collective-permute-start(bf16[128,512]{1,0:T(8,128)(2,1)S(1)} %add_convert_fusion), channel_id=1, source_target_pairs={{0,16},{1,17},{2,18},{3,19},{4,20},{5,21},{6,22},{7,23},{8,24},{9,... | collective-permute-start | bytes 393224 | tf_op jit(solution)/shard_map/ppermute | solution.py:176
  41.4 1.6 %collective-permute-start.18 = (bf16[2,128,512]{2,1,0:T(8,128)(2,1)S(1)}, bf16[2,128,512]{2,1,0:T(8,128)(2,1)S(1)}, u32[]{:S(2)}, u32[]{:S(2)}) collective-permute-start(bf16[2,128,512]{2,1,0:T(8,128)(2,1)S(1)} %pad_maximum_fusion.1.pair_ref), channel_id=1, source_target_pairs={{0,8},{1,9},{2,10},{3,11},{4,12},{5,13},{6,14},{7,15},{8,0},{9,1},... | collective-permute-start | bytes 786440 | tf_op jit(solution)/shard_map/ppermute | solution.py:176

commit v19 on v18

--- a/solution.py
+++ b/solution.py
@@ -352,10 +352,11 @@
     own_some, own_rest = sums([(tuple((0, *at) for at in every), start, 256) for start in (0, 256)], F32, v0_late)
     pair_own, = sums([(((1, 0, 0),), 0, 512)], BF16, v0_late)
     on_b = xor_permute(on_b, Y)
-    side_a = xor_permute(jnp.concatenate([side_a, window]), Y)
-    side_a, window = side_a[:LANE], side_a[LANE:]
     on_a = xor_permute(add(keep_a[:LANE], far_a).astype(BF16), X)
     z3 = add(keep_b[LANE:], side_b, on_b).astype(BF16)
+    side_a = after_all(jnp.concatenate([side_a, window]), z3)[0]
+    side_a = xor_permute(side_a, Y)
+    side_a, window = side_a[:LANE], side_a[LANE:]
     pair_some, pair_own = after_all(pair_some, pair_own, z3)[:2]
     z3 = xor_permute(z3, Z1)
     pair_own = xor_permute(pair_own, Z1)

time: 44 us -> 43.7 us (level)
  starting transfers between devices: 22.3 us -> 21.2 us
  waiting for transfers between devices: 11.4 us -> 12.2 us
    ppermute x19, starting transfers between devices: 22.3 us -> 21.2 us  [xor_permute(): lax.ppermute(value, ('dp', 'fsdp'), [(i, i ^ mask) for i in range(count)])]
    ppermute x19, waiting for transfers between devices: 11.4 us -> 12.2 us  [xor_permute(): lax.ppermute(value, ('dp', 'fsdp'), [(i, i ^ mask) for i in range(count)])]
where the time goes in v19:
time: 43.7 us; the launch traced here: 43.5 us
  starting transfers between devices  21.2 us (49%)
  waiting for transfers between devices  12.2 us (28%)
  Pallas kernels  8.11 us (19%)
  between operations  1.59 us (4%)
    ppermute x19, starting transfers between devices, xor_permute(): lax.ppermute(value, ('dp', 'fsdp'), [(i, i ^ mask) for i in range(count)])  21.2 us
    ppermute x19, waiting for transfers between devices, xor_permute(): lax.ppermute(value, ('dp', 'fsdp'), [(i, i ^ mask) for i in range(count)])  12.2 us
    pallas_call x1, Pallas kernels, front(): pl.pallas_call(functools.partial(front_kernel, per_group), in_specs=[HBM]...  2.64 us
    pallas_call x7, Pallas kernels, partial_sums(): pl.pallas_call(functools.partial(partial_kernel, parts), in_specs=[VMEM]...  2.56 us
    pallas_call x2, Pallas kernels, place(): pl.pallas_call(functools.partial(place_kernel, core), in_specs=[VMEM] + [...  1.65 us
    pallas_call x1, Pallas kernels, outer_swap(): pl.pallas_call(outer_swap_kernel, in_specs=[VMEM] * 3, out_specs=VMEM, ou...  0.91 us
  transfers between devices with their start and end apart: 19, of which 7 were waited for; matrix products, arithmetic and copies ran while one was open for 1% of the time, Pallas kernels for 16%

profile of v19, /device:TPU:0, one launch (start us, length us, event | category | flops | bytes accessed | tf_op | source)
XLA Modules:
  0.0 43.5 jit_solution(13533741978126285078)
XLA Ops:
  0.6 0.5 %collective-permute-start = (bf16[256,4096]{1,0:T(8,128)(2,1)}, bf16[256,4096]{1,0:T(8,128)(2,1)S(1)}, u32[]{:S(2)}, u32[]{:S(2)}) collective-permute-start(bf16[256,4096]{1,0:T(8,128)(2,1)} %own_ref.13), channel_id=1, source_target_pairs={{0,8},{1,9},{2,10},{3,11},{4,12},{5,13},{6,14},{7,15},{8,0},{9,1},... | collective-permute-start | bytes 6291464 | tf_op jit(solution)/shard_map/ppermute | solution.py:176
  1.9 2.6 %front.1.v0_ref = bf16[272,512]{1,0:T(8,128)(2,1)S(1)} custom-call(f32[16]{0:T(128)} %loss_hbm.1, s32[1]{0:T(128)S(6)} %copy.14.exponent_hbm, s32[1,2]{1,0:T(1,128)} %start_hbm.1, s32[1,2]{1,0:T(1,128)} %rows_hbm.1, bf16[256,2048]{1,0:T(8,128)(2,1)} %q_hbm.1, bf16[256,512]{1,0:T(8,128)(2,1)} %k_hbm.1, bf16[256,2048]{1,0:T(8,128)(2,1)} %g_hbm.1, ...), custom_call_target="tpu_custom_call" | custom-call | tf_op jit(solution)/shard_map/front/pallas_call | solution.py:153
  4.6 0.1 collective-permute-start.1
  4.7 1.5 %collective-permute-done.1.v1_ref = bf16[272,512]{1,0:T(8,128)(2,1)S(1)} collective-permute-done((bf16[272,512]{1,0:T(8,128)(2,1)S(1)}, bf16[272,512]{1,0:T(8,128)(2,1)S(1)}, u32[]{:S(2)}, u32[]{:S(2)}) %collective-permute-start.1) | collective-permute-done | bytes 278560 | tf_op jit(solution)/shard_map/ppermute | solution.py:176
  6.2 0.0 collective-permute-done.near_ref
  6.2 0.3 partial_sums.8
  6.5 2.6 %collective-permute-start.2 = (bf16[128,512]{1,0:T(8,128)(2,1)S(1)}, bf16[128,512]{1,0:T(8,128)(2,1)S(1)}, u32[]{:S(2)}, u32[]{:S(2)}) collective-permute-start(bf16[128,512]{1,0:T(8,128)(2,1)S(1)} %partial_sums.8), channel_id=1, source_target_pairs={{0,1},{1,0},{2,3},{3,2},{4,5},{5,4},{6,7},{7,6},{8,9},{9,8},{10,11... | collective-permute-start | bytes 393224 | tf_op jit(solution)/shard_map/ppermute | solution.py:176
  9.1 0.3 partial_sums.9
  9.3 1.6 %collective-permute-start.3 = (bf16[128,512]{1,0:T(8,128)(2,1)S(1)}, bf16[128,512]{1,0:T(8,128)(2,1)S(1)}, u32[]{:S(2)}, u32[]{:S(2)}) collective-permute-start(bf16[128,512]{1,0:T(8,128)(2,1)S(1)} %partial_sums.9), channel_id=1, source_target_pairs={{0,16},{1,17},{2,18},{3,19},{4,20},{5,21},{6,22},{7,23},{8,24},{9,... | collective-permute-start | bytes 393224 | tf_op jit(solution)/shard_map/ppermute | solution.py:176
  10.9 0.4 partial_sums.11
  11.3 1.6 %collective-permute-start.4 = (bf16[384,256]{1,0:T(8,128)(2,1)S(1)}, bf16[384,256]{1,0:T(8,128)(2,1)S(1)}, u32[]{:S(2)}, u32[]{:S(2)}) collective-permute-start(bf16[384,256]{1,0:T(8,128)(2,1)S(1)} %get-tuple-element.31), channel_id=1, source_target_pairs={{0,2},{1,3},{2,0},{3,1},{4,6},{5,7},{6,4},{7,5},{8,10},{9,11},{10,... | collective-permute-start | bytes 589832 | tf_op jit(solution)/shard_map/ppermute | solution.py:176
  13.0 0.5 %collective-permute-start.5 = (bf16[128,512]{1,0:T(8,128)(2,1)S(1)}, bf16[128,512]{1,0:T(8,128)(2,1)S(1)}, u32[]{:S(2)}, u32[]{:S(2)}) collective-permute-start(bf16[128,512]{1,0:T(8,128)(2,1)S(1)} %get-tuple-element.32), channel_id=1, source_target_pairs={{0,1},{1,0},{2,3},{3,2},{4,5},{5,4},{6,7},{7,6},{8,9},{9,8},{10,11... | collective-permute-start | bytes 393224 | tf_op jit(solution)/shard_map/ppermute | solution.py:176
  13.5 0.4 partial_sums.13
  13.9 0.5 %collective-permute-start.12 = (bf16[384,256]{1,0:T(8,128)(2,1)S(1)}, bf16[384,256]{1,0:T(8,128)(2,1)S(1)}, u32[]{:S(2)}, u32[]{:S(2)}) collective-permute-start(bf16[384,256]{1,0:T(8,128)(2,1)S(1)} %get-tuple-element.43), channel_id=1, source_target_pairs={{0,2},{1,3},{2,0},{3,1},{4,6},{5,7},{6,4},{7,5},{8,10},{9,11},{10,... | collective-permute-start | bytes 589832 | tf_op jit(solution)/shard_map/ppermute | solution.py:176
  14.4 0.5 %partial_sums.7 = (f32[256,512]{1,0:T(8,128)S(1)}, f32[256,512]{1,0:T(8,128)S(1)}) custom-call(bf16[256,4096]{1,0:T(8,128)(2,1)S(1)} %copy-done, bf16[256,4096]{1,0:T(8,128)(2,1)S(1)} %collective-permute-done.near_ref, bf16[272,512]{1,0:T(8,128)(2,1)S(1)} %front.1.v0_ref, bf16[272,512]{1,0:T(8,128)(2,1)S(1)} %collective-permute-done.1.v1_ref), custom_call_target="tpu_custom_call" | custom-call | tf_op jit(solution)/shard_map/partial_sums/pallas_call | solution.py:201
  14.9 0.0 collective-permute-done.3
  15.0 1.5 %collective-permute-start.6 = (bf16[128,512]{1,0:T(8,128)(2,1)S(1)}, bf16[128,512]{1,0:T(8,128)(2,1)S(1)}, u32[]{:S(2)}, u32[]{:S(2)}) collective-permute-start(bf16[128,512]{1,0:T(8,128)(2,1)S(1)} %add_convert_fusion.4), channel_id=1, source_target_pairs={{0,16},{1,17},{2,18},{3,19},{4,20},{5,21},{6,22},{7,23},{8,24},{9,... | collective-permute-start | bytes 393224 | tf_op jit(solution)/shard_map/ppermute | solution.py:176
  16.5 0.6 %collective-permute-start.10 = (bf16[128,512]{1,0:T(8,128)(2,1)S(1)}, bf16[128,512]{1,0:T(8,128)(2,1)S(1)}, u32[]{:S(2)}, u32[]{:S(2)}) collective-permute-start(bf16[128,512]{1,0:T(8,128)(2,1)S(1)} %add_convert_fusion.2), channel_id=1, source_target_pairs={{0,1},{1,0},{2,3},{3,2},{4,5},{5,4},{6,7},{7,6},{8,9},{9,8},{10,11... | collective-permute-start | bytes 393224 | tf_op jit(solution)/shard_map/ppermute | solution.py:176
  17.1 0.3 inner_swap.1
  17.5 0.3 partial_sums.12
  17.7 0.5 %partial_sums.10 = (f32[512,256]{1,0:T(8,128)S(1)}, f32[512,256]{1,0:T(8,128)S(1)}) custom-call(bf16[256,4096]{1,0:T(8,128)(2,1)S(1)} %copy-done, bf16[256,4096]{1,0:T(8,128)(2,1)S(1)} %collective-permute-done.near_ref, bf16[272,512]{1,0:T(8,128)(2,1)S(1)} %front.1.v0_ref, bf16[272,512]{1,0:T(8,128)(2,1)S(1)} %collective-permute-done.1.v1_ref), custom_call_target="tpu_custom_call" | custom-call | tf_op jit(solution)/shard_map/partial_sums/pallas_call | solution.py:201
  18.2 0.0 collective-permute-done.5
  18.3 1.7 %collective-permute-done.6 = bf16[128,512]{1,0:T(8,128)(2,1)S(1)} collective-permute-done((bf16[128,512]{1,0:T(8,128)(2,1)S(1)}, bf16[128,512]{1,0:T(8,128)(2,1)S(1)}, u32[]{:S(2)}, u32[]{:S(2)}) %collective-permute-start.6) | collective-permute-done | bytes 131104 | tf_op jit(solution)/shard_map/ppermute | solution.py:176
  20.0 1.6 %collective-permute-start.11 = (bf16[128,512]{1,0:T(8,128)(2,1)S(1)}, bf16[128,512]{1,0:T(8,128)(2,1)S(1)}, u32[]{:S(2)}, u32[]{:S(2)}) collective-permute-start(bf16[128,512]{1,0:T(8,128)(2,1)S(1)} %add_convert_fusion.3), channel_id=1, source_target_pairs={{0,2},{1,3},{2,0},{3,1},{4,6},{5,7},{6,4},{7,5},{8,10},{9,11},{10,... | collective-permute-start | bytes 393224 | tf_op jit(solution)/shard_map/ppermute | solution.py:176
  21.7 1.5 %collective-permute-start.9 = (bf16[160,512]{1,0:T(8,128)(2,1)S(1)}, bf16[160,512]{1,0:T(8,128)(2,1)S(1)}, u32[]{:S(2)}, u32[]{:S(2)}) collective-permute-start(bf16[160,512]{1,0:T(8,128)(2,1)S(1)} %pad_maximum_fusion.2), channel_id=1, source_target_pairs={{0,16},{1,17},{2,18},{3,19},{4,20},{5,21},{6,22},{7,23},{8,24},{9,... | collective-permute-start | bytes 491528 | tf_op jit(solution)/shard_map/ppermute | solution.py:176
  23.2 0.6 %collective-permute-start.8 = (bf16[256,256]{1,0:T(8,128)(2,1)S(1)}, bf16[256,256]{1,0:T(8,128)(2,1)S(1)}, u32[]{:S(2)}, u32[]{:S(2)}) collective-permute-start(bf16[256,256]{1,0:T(8,128)(2,1)S(1)} %slice.118), channel_id=1, source_target_pairs={{0,16},{1,17},{2,18},{3,19},{4,20},{5,21},{6,22},{7,23},{8,24},{9,... | collective-permute-start | bytes 393224 | tf_op jit(solution)/shard_map/ppermute | solution.py:176
  23.9 1.6 %collective-permute-start.13 = (bf16[256,256]{1,0:T(8,128)(2,1)S(1)}, bf16[256,256]{1,0:T(8,128)(2,1)S(1)}, u32[]{:S(2)}, u32[]{:S(2)}) collective-permute-start(bf16[256,256]{1,0:T(8,128)(2,1)S(1)} %pad_maximum_fusion.3), channel_id=1, source_target_pairs={{0,1},{1,0},{2,3},{3,2},{4,5},{5,4},{6,7},{7,6},{8,9},{9,8},{10,11... | collective-permute-start | bytes 393224 | tf_op jit(solution)/shard_map/ppermute | solution.py:176
  25.5 0.0 collective-permute-done.10
  25.5 0.5 %collective-permute-start.7 = (bf16[128,512]{1,0:T(8,128)(2,1)S(1)}, bf16[128,512]{1,0:T(8,128)(2,1)S(1)}, u32[]{:S(2)}, u32[]{:S(2)}) collective-permute-start(bf16[128,512]{1,0:T(8,128)(2,1)S(1)} %partial_sums.12), channel_id=1, source_target_pairs={{0,2},{1,3},{2,0},{3,1},{4,6},{5,7},{6,4},{7,5},{8,10},{9,11},{10,... | collective-permute-start | bytes 393224 | tf_op jit(solution)/shard_map/ppermute | solution.py:176
  25.9 0.0 collective-permute-done.11
  25.9 1.3 %collective-permute-done.9 = bf16[160,512]{1,0:T(8,128)(2,1)S(1)} collective-permute-done((bf16[160,512]{1,0:T(8,128)(2,1)S(1)}, bf16[160,512]{1,0:T(8,128)(2,1)S(1)}, u32[]{:S(2)}, u32[]{:S(2)}) %collective-permute-start.9) | collective-permute-done | bytes 163872 | tf_op jit(solution)/shard_map/ppermute | solution.py:176
  27.3 0.1 add_convert_fusion.1
  27.3 2.7 %collective-permute-start.14 = (bf16[128,512]{1,0:T(8,128)(2,1)S(1)}, bf16[128,512]{1,0:T(8,128)(2,1)S(1)}, u32[]{:S(2)}, u32[]{:S(2)}) collective-permute-start(bf16[128,512]{1,0:T(8,128)(2,1)S(1)} %add_convert_fusion.1), channel_id=1, source_target_pairs={{0,4},{1,5},{2,6},{3,7},{4,0},{5,1},{6,2},{7,3},{8,12},{9,13},{10,... | collective-permute-start | bytes 393224 | tf_op jit(solution)/shard_map/ppermute | solution.py:176
  30.0 1.3 %collective-permute-start.15 = (bf16[128,256]{1,0:T(8,128)(2,1)S(1)}, bf16[128,256]{1,0:T(8,128)(2,1)S(1)}, u32[]{:S(2)}, u32[]{:S(2)}) collective-permute-start(bf16[128,256]{1,0:T(8,128)(2,1)S(1)} %fusion.1), channel_id=1, source_target_pairs={{0,1},{1,0},{2,3},{3,2},{4,5},{5,4},{6,7},{7,6},{8,9},{9,8},{10,11... | collective-permute-start | bytes 196616 | tf_op jit(solution)/shard_map/ppermute | solution.py:176
  31.3 0.0 collective-permute-done.13
  31.3 0.0 collective-permute-done.7
  31.3 0.1 fusion
  31.4 0.9 %collective-permute-start.16 = (bf16[128,256]{1,0:T(8,128)(2,1)S(1)}, bf16[128,256]{1,0:T(8,128)(2,1)S(1)}, u32[]{:S(2)}, u32[]{:S(2)}) collective-permute-start(bf16[128,256]{1,0:T(8,128)(2,1)S(1)} %get-tuple-element.56), channel_id=1, source_target_pairs={{0,16},{1,17},{2,18},{3,19},{4,20},{5,21},{6,22},{7,23},{8,24},{9,... | collective-permute-start | bytes 196616 | tf_op jit(solution)/shard_map/ppermute | solution.py:176
  32.3 2.4 %collective-permute-done.14.arrived_ref = bf16[128,512]{1,0:T(8,128)(2,1)S(1)} collective-permute-done((bf16[128,512]{1,0:T(8,128)(2,1)S(1)}, bf16[128,512]{1,0:T(8,128)(2,1)S(1)}, u32[]{:S(2)}, u32[]{:S(2)}) %collective-permute-start.14) | collective-permute-done | bytes 131104 | tf_op jit(solution)/shard_map/ppermute | solution.py:176
  34.7 1.3 %collective-permute-done.16 = bf16[128,256]{1,0:T(8,128)(2,1)S(1)} collective-permute-done((bf16[128,256]{1,0:T(8,128)(2,1)S(1)}, bf16[128,256]{1,0:T(8,128)(2,1)S(1)}, u32[]{:S(2)}, u32[]{:S(2)}) %collective-permute-start.16) | collective-permute-done | bytes 65568 | tf_op jit(solution)/shard_map/ppermute | solution.py:176
  36.0 0.0 collective-permute-done.15
  36.0 0.9 %collective-permute-start.17 = (bf16[128,512]{1,0:T(8,128)(2,1)S(1)}, bf16[128,512]{1,0:T(8,128)(2,1)S(1)}, u32[]{:S(2)}, u32[]{:S(2)}) collective-permute-start(bf16[128,512]{1,0:T(8,128)(2,1)S(1)} %add_convert_fusion), channel_id=1, source_target_pairs={{0,16},{1,17},{2,18},{3,19},{4,20},{5,21},{6,22},{7,23},{8,24},{9,... | collective-permute-start | bytes 393224 | tf_op jit(solution)/shard_map/ppermute | solution.py:176
  36.9 0.9 %outer_swap.1 = bf16[256,512]{1,0:T(8,128)(2,1)} custom-call(bf16[272,512]{1,0:T(8,128)(2,1)S(1)} %front.1.v0_ref, bf16[256,512]{1,0:T(8,128)(2,1)S(1)} %get-tuple-element.46.rows_ref, bf16[32,512]{1,0:T(8,128)(2,1)S(1)} %slice.95.window_ref), custom_call_target="tpu_custom_call" | custom-call | tf_op jit(solution)/shard_map/outer_swap/pallas_call | solution.py:265
  37.8 3.2 %collective-permute-done.17 = bf16[128,512]{1,0:T(8,128)(2,1)S(1)} collective-permute-done((bf16[128,512]{1,0:T(8,128)(2,1)S(1)}, bf16[128,512]{1,0:T(8,128)(2,1)S(1)}, u32[]{:S(2)}, u32[]{:S(2)}) %collective-permute-start.17) | collective-permute-done | bytes 131104 | tf_op jit(solution)/shard_map/ppermute | solution.py:176
  41.1 0.1 collective-permute-start.18
  41.2 0.8 %place.2.rest_0_ = f32[512,512]{1,0:T(8,128)} custom-call(bf16[2,128,512]{2,1,0:T(8,128)(2,1)S(1)} %pad_maximum_fusion.1.pair_ref), custom_call_target="tpu_custom_call" | custom-call | tf_op jit(solution)/shard_map/place/pallas_call | solution.py:289
  42.0 0.7 %collective-permute-done.18.pair_ref = bf16[2,128,512]{2,1,0:T(8,128)(2,1)S(1)} collective-permute-done((bf16[2,128,512]{2,1,0:T(8,128)(2,1)S(1)}, bf16[2,128,512]{2,1,0:T(8,128)(2,1)S(1)}, u32[]{:S(2)}, u32[]{:S(2)}) %collective-permute-start.18) | collective-permute-done | bytes 262176 | tf_op jit(solution)/shard_map/ppermute | solution.py:176
  42.7 0.8 %place.3 = f32[512,512]{1,0:T(8,128)} custom-call(bf16[2,128,512]{2,1,0:T(8,128)(2,1)S(1)} %collective-permute-done.18.pair_ref, f32[512,512]{1,0:T(8,128)} %place.2.rest_0_), custom_call_target="tpu_custom_call", output_to_operand_aliasing={{}: (1, {})} | custom-call | tf_op jit(solution)/shard_map/place/pallas_call | solution.py:289
  (21 shorter events, 0.4 us)
Async XLA Ops:
  0.6 5.6 %copy-start = (bf16[256,4096]{1,0:T(8,128)(2,1)S(1)}, bf16[256,4096]{1,0:T(8,128)(2,1)}, u32[]{:S(2)}) copy-start(bf16[256,4096]{1,0:T(8,128)(2,1)} %own_ref.13) | copy-start | bytes 6291460
  0.6 5.5 %collective-permute-start = (bf16[256,4096]{1,0:T(8,128)(2,1)}, bf16[256,4096]{1,0:T(8,128)(2,1)S(1)}, u32[]{:S(2)}, u32[]{:S(2)}) collective-permute-start(bf16[256,4096]{1,0:T(8,128)(2,1)} %own_ref.13), channel_id=1, source_target_pairs={{0,8},{1,9},{2,10},{3,11},{4,12},{5,13},{6,14},{7,15},{8,0},{9,1},... | collective-permute-start | bytes 6291464 | tf_op jit(solution)/shard_map/ppermute | solution.py:176
  4.6 1.6 %collective-permute-start.1 = (bf16[272,512]{1,0:T(8,128)(2,1)S(1)}, bf16[272,512]{1,0:T(8,128)(2,1)S(1)}, u32[]{:S(2)}, u32[]{:S(2)}) collective-permute-start(bf16[272,512]{1,0:T(8,128)(2,1)S(1)} %front.1.v0_ref), channel_id=1, source_target_pairs={{0,8},{1,9},{2,10},{3,11},{4,12},{5,13},{6,14},{7,15},{8,0},{9,1},... | collective-permute-start | bytes 835592 | tf_op jit(solution)/shard_map/ppermute | solution.py:176
  6.5 8.4 %collective-permute-start.2 = (bf16[128,512]{1,0:T(8,128)(2,1)S(1)}, bf16[128,512]{1,0:T(8,128)(2,1)S(1)}, u32[]{:S(2)}, u32[]{:S(2)}) collective-permute-start(bf16[128,512]{1,0:T(8,128)(2,1)S(1)} %partial_sums.8), channel_id=1, source_target_pairs={{0,1},{1,0},{2,3},{3,2},{4,5},{5,4},{6,7},{7,6},{8,9},{9,8},{10,11... | collective-permute-start | bytes 393224 | tf_op jit(solution)/shard_map/ppermute | solution.py:176
  9.3 5.6 %collective-permute-start.3 = (bf16[128,512]{1,0:T(8,128)(2,1)S(1)}, bf16[128,512]{1,0:T(8,128)(2,1)S(1)}, u32[]{:S(2)}, u32[]{:S(2)}) collective-permute-start(bf16[128,512]{1,0:T(8,128)(2,1)S(1)} %partial_sums.9), channel_id=1, source_target_pairs={{0,16},{1,17},{2,18},{3,19},{4,20},{5,21},{6,22},{7,23},{8,24},{9,... | collective-permute-start | bytes 393224 | tf_op jit(solution)/shard_map/ppermute | solution.py:176
  11.3 11.8 %collective-permute-start.4 = (bf16[384,256]{1,0:T(8,128)(2,1)S(1)}, bf16[384,256]{1,0:T(8,128)(2,1)S(1)}, u32[]{:S(2)}, u32[]{:S(2)}) collective-permute-start(bf16[384,256]{1,0:T(8,128)(2,1)S(1)} %get-tuple-element.31), channel_id=1, source_target_pairs={{0,2},{1,3},{2,0},{3,1},{4,6},{5,7},{6,4},{7,5},{8,10},{9,11},{10,... | collective-permute-start | bytes 589832 | tf_op jit(solution)/shard_map/ppermute | solution.py:176
  13.0 5.3 %collective-permute-start.5 = (bf16[128,512]{1,0:T(8,128)(2,1)S(1)}, bf16[128,512]{1,0:T(8,128)(2,1)S(1)}, u32[]{:S(2)}, u32[]{:S(2)}) collective-permute-start(bf16[128,512]{1,0:T(8,128)(2,1)S(1)} %get-tuple-element.32), channel_id=1, source_target_pairs={{0,1},{1,0},{2,3},{3,2},{4,5},{5,4},{6,7},{7,6},{8,9},{9,8},{10,11... | collective-permute-start | bytes 393224 | tf_op jit(solution)/shard_map/ppermute | solution.py:176
  13.9 9.9 %collective-permute-start.12 = (bf16[384,256]{1,0:T(8,128)(2,1)S(1)}, bf16[384,256]{1,0:T(8,128)(2,1)S(1)}, u32[]{:S(2)}, u32[]{:S(2)}) collective-permute-start(bf16[384,256]{1,0:T(8,128)(2,1)S(1)} %get-tuple-element.43), channel_id=1, source_target_pairs={{0,2},{1,3},{2,0},{3,1},{4,6},{5,7},{6,4},{7,5},{8,10},{9,11},{10,... | collective-permute-start | bytes 589832 | tf_op jit(solution)/shard_map/ppermute | solution.py:176
  15.0 5.0 %collective-permute-start.6 = (bf16[128,512]{1,0:T(8,128)(2,1)S(1)}, bf16[128,512]{1,0:T(8,128)(2,1)S(1)}, u32[]{:S(2)}, u32[]{:S(2)}) collective-permute-start(bf16[128,512]{1,0:T(8,128)(2,1)S(1)} %add_convert_fusion.4), channel_id=1, source_target_pairs={{0,16},{1,17},{2,18},{3,19},{4,20},{5,21},{6,22},{7,23},{8,24},{9,... | collective-permute-start | bytes 393224 | tf_op jit(solution)/shard_map/ppermute | solution.py:176
  16.5 9.0 %collective-permute-start.10 = (bf16[128,512]{1,0:T(8,128)(2,1)S(1)}, bf16[128,512]{1,0:T(8,128)(2,1)S(1)}, u32[]{:S(2)}, u32[]{:S(2)}) collective-permute-start(bf16[128,512]{1,0:T(8,128)(2,1)S(1)} %add_convert_fusion.2), channel_id=1, source_target_pairs={{0,1},{1,0},{2,3},{3,2},{4,5},{5,4},{6,7},{7,6},{8,9},{9,8},{10,11... | collective-permute-start | bytes 393224 | tf_op jit(solution)/shard_map/ppermute | solution.py:176
  20.0 5.9 %collective-permute-start.11 = (bf16[128,512]{1,0:T(8,128)(2,1)S(1)}, bf16[128,512]{1,0:T(8,128)(2,1)S(1)}, u32[]{:S(2)}, u32[]{:S(2)}) collective-permute-start(bf16[128,512]{1,0:T(8,128)(2,1)S(1)} %add_convert_fusion.3), channel_id=1, source_target_pairs={{0,2},{1,3},{2,0},{3,1},{4,6},{5,7},{6,4},{7,5},{8,10},{9,11},{10,... | collective-permute-start | bytes 393224 | tf_op jit(solution)/shard_map/ppermute | solution.py:176
  21.7 5.6 %collective-permute-start.9 = (bf16[160,512]{1,0:T(8,128)(2,1)S(1)}, bf16[160,512]{1,0:T(8,128)(2,1)S(1)}, u32[]{:S(2)}, u32[]{:S(2)}) collective-permute-start(bf16[160,512]{1,0:T(8,128)(2,1)S(1)} %pad_maximum_fusion.2), channel_id=1, source_target_pairs={{0,16},{1,17},{2,18},{3,19},{4,20},{5,21},{6,22},{7,23},{8,24},{9,... | collective-permute-start | bytes 491528 | tf_op jit(solution)/shard_map/ppermute | solution.py:176
  23.2 6.8 %collective-permute-start.8 = (bf16[256,256]{1,0:T(8,128)(2,1)S(1)}, bf16[256,256]{1,0:T(8,128)(2,1)S(1)}, u32[]{:S(2)}, u32[]{:S(2)}) collective-permute-start(bf16[256,256]{1,0:T(8,128)(2,1)S(1)} %slice.118), channel_id=1, source_target_pairs={{0,16},{1,17},{2,18},{3,19},{4,20},{5,21},{6,22},{7,23},{8,24},{9,... | collective-permute-start | bytes 393224 | tf_op jit(solution)/shard_map/ppermute | solution.py:176
  23.9 7.4 %collective-permute-start.13 = (bf16[256,256]{1,0:T(8,128)(2,1)S(1)}, bf16[256,256]{1,0:T(8,128)(2,1)S(1)}, u32[]{:S(2)}, u32[]{:S(2)}) collective-permute-start(bf16[256,256]{1,0:T(8,128)(2,1)S(1)} %pad_maximum_fusion.3), channel_id=1, source_target_pairs={{0,1},{1,0},{2,3},{3,2},{4,5},{5,4},{6,7},{7,6},{8,9},{9,8},{10,11... | collective-permute-start | bytes 393224 | tf_op jit(solution)/shard_map/ppermute | solution.py:176
  25.5 5.8 %collective-permute-start.7 = (bf16[128,512]{1,0:T(8,128)(2,1)S(1)}, bf16[128,512]{1,0:T(8,128)(2,1)S(1)}, u32[]{:S(2)}, u32[]{:S(2)}) collective-permute-start(bf16[128,512]{1,0:T(8,128)(2,1)S(1)} %partial_sums.12), channel_id=1, source_target_pairs={{0,2},{1,3},{2,0},{3,1},{4,6},{5,7},{6,4},{7,5},{8,10},{9,11},{10,... | collective-permute-start | bytes 393224 | tf_op jit(solution)/shard_map/ppermute | solution.py:176
  27.3 7.3 %collective-permute-start.14 = (bf16[128,512]{1,0:T(8,128)(2,1)S(1)}, bf16[128,512]{1,0:T(8,128)(2,1)S(1)}, u32[]{:S(2)}, u32[]{:S(2)}) collective-permute-start(bf16[128,512]{1,0:T(8,128)(2,1)S(1)} %add_convert_fusion.1), channel_id=1, source_target_pairs={{0,4},{1,5},{2,6},{3,7},{4,0},{5,1},{6,2},{7,3},{8,12},{9,13},{10,... | collective-permute-start | bytes 393224 | tf_op jit(solution)/shard_map/ppermute | solution.py:176
  30.0 6.0 %collective-permute-start.15 = (bf16[128,256]{1,0:T(8,128)(2,1)S(1)}, bf16[128,256]{1,0:T(8,128)(2,1)S(1)}, u32[]{:S(2)}, u32[]{:S(2)}) collective-permute-start(bf16[128,256]{1,0:T(8,128)(2,1)S(1)} %fusion.1), channel_id=1, source_target_pairs={{0,1},{1,0},{2,3},{3,2},{4,5},{5,4},{6,7},{7,6},{8,9},{9,8},{10,11... | collective-permute-start | bytes 196616 | tf_op jit(solution)/shard_map/ppermute | solution.py:176
  31.4 4.6 %collective-permute-start.16 = (bf16[128,256]{1,0:T(8,128)(2,1)S(1)}, bf16[128,256]{1,0:T(8,128)(2,1)S(1)}, u32[]{:S(2)}, u32[]{:S(2)}) collective-permute-start(bf16[128,256]{1,0:T(8,128)(2,1)S(1)} %get-tuple-element.56), channel_id=1, source_target_pairs={{0,16},{1,17},{2,18},{3,19},{4,20},{5,21},{6,22},{7,23},{8,24},{9,... | collective-permute-start | bytes 196616 | tf_op jit(solution)/shard_map/ppermute | solution.py:176
  36.0 5.0 %collective-permute-start.17 = (bf16[128,512]{1,0:T(8,128)(2,1)S(1)}, bf16[128,512]{1,0:T(8,128)(2,1)S(1)}, u32[]{:S(2)}, u32[]{:S(2)}) collective-permute-start(bf16[128,512]{1,0:T(8,128)(2,1)S(1)} %add_convert_fusion), channel_id=1, source_target_pairs={{0,16},{1,17},{2,18},{3,19},{4,20},{5,21},{6,22},{7,23},{8,24},{9,... | collective-permute-start | bytes 393224 | tf_op jit(solution)/shard_map/ppermute | solution.py:176
  41.1 1.6 %collective-permute-start.18 = (bf16[2,128,512]{2,1,0:T(8,128)(2,1)S(1)}, bf16[2,128,512]{2,1,0:T(8,128)(2,1)S(1)}, u32[]{:S(2)}, u32[]{:S(2)}) collective-permute-start(bf16[2,128,512]{2,1,0:T(8,128)(2,1)S(1)} %pad_maximum_fusion.1.pair_ref), channel_id=1, source_target_pairs={{0,8},{1,9},{2,10},{3,11},{4,12},{5,13},{6,14},{7,15},{8,0},{9,1},... | collective-permute-start | bytes 786440 | tf_op jit(solution)/shard_map/ppermute | solution.py:176

commit v20 on v19

--- a/solution.py
+++ b/solution.py
@@ -354,12 +354,10 @@
     on_b = xor_permute(on_b, Y)
     on_a = xor_permute(add(keep_a[:LANE], far_a).astype(BF16), X)
     z3 = add(keep_b[LANE:], side_b, on_b).astype(BF16)
-    side_a = after_all(jnp.concatenate([side_a, window]), z3)[0]
-    side_a = xor_permute(side_a, Y)
+    side_a = xor_permute(after_all(jnp.concatenate([side_a, window]), own_some)[0], Y)
     side_a, window = side_a[:LANE], side_a[LANE:]
-    pair_some, pair_own = after_all(pair_some, pair_own, z3)[:2]
+    pair_some = after_all(pair_some, z3)[0]
     z3 = xor_permute(z3, Z1)
-    pair_own = xor_permute(pair_own, Z1)
     z2 = add(keep_a[LANE:], side_a, on_a, z3).astype(BF16)
 
     some = add(own_some[:3 * LANE], pair_some)
@@ -367,12 +365,15 @@
     rest = add(own_rest[:3 * LANE], after_all(pair_rest, some)[0])
     rest_far, rest_y, rest_x = (rest[row:row + LANE] for row in range(0, 3 * LANE, LANE))
     rest_in = xor_permute(jnp.concatenate([rest_far, rest_x]).astype(BF16), X)
-    some_in = after_all(some_in, z2)[0]
+    some_in, pair_own = after_all(some_in, pair_own, z2)[:2]
     z2 = xor_permute(z2, Z2)
+    pair_own = xor_permute(pair_own, Z1)
     some_on = add(some[2 * LANE:], some_in[:LANE]).astype(BF16)
     rest_in = after_all(rest_in, some_on)[0]
     some_on = xor_permute(some_on, X)
-    rest_on = xor_permute(add(rest_y, rest_in[:LANE]).astype(BF16), Y)
+    rest_on = add(rest_y, rest_in[:LANE]).astype(BF16)
+    pair_own = after_all(pair_own, rest_on)[0]
+    rest_on = xor_permute(rest_on, Y)
     base = jnp.concatenate([
         add(own_some[3 * LANE:], pair_own[:, :256], some_in[LANE:]),
         add(own_rest[3 * LANE:], pair_own[:, 256:], rest_in[LANE:]),

time: 43.7 us -> 44 us (level)
  starting transfers between devices: 21.2 us -> 22.1 us
  waiting for transfers between devices: 12.2 us -> 11.5 us
    ppermute x19, starting transfers between devices: 21.2 us -> 22.1 us  [xor_permute(): lax.ppermute(value, ('dp', 'fsdp'), [(i, i ^ mask) for i in range(count)])]
    ppermute x19, waiting for transfers between devices: 12.2 us -> 11.5 us  [xor_permute(): lax.ppermute(value, ('dp', 'fsdp'), [(i, i ^ mask) for i in range(count)])]
  transfers between devices with their start and end apart: 19 -> 19, of which waited for: 7 -> 8; matrix products, arithmetic and copies ran while one was open for 1% -> 1% of each run, Pallas kernels for 16% -> 16%
where the time goes in v20:
time: 44 us; the launch traced here: 43.8 us
  starting transfers between devices  22.1 us (50%)
  waiting for transfers between devices  11.5 us (26%)
  Pallas kernels  8.1 us (18%)
  between operations  1.61 us (4%)
    ppermute x19, starting transfers between devices, xor_permute(): lax.ppermute(value, ('dp', 'fsdp'), [(i, i ^ mask) for i in range(count)])  22.1 us
    ppermute x19, waiting for transfers between devices, xor_permute(): lax.ppermute(value, ('dp', 'fsdp'), [(i, i ^ mask) for i in range(count)])  11.5 us
    pallas_call x1, Pallas kernels, front(): pl.pallas_call(functools.partial(front_kernel, per_group), in_specs=[HBM]...  2.64 us
    pallas_call x7, Pallas kernels, partial_sums(): pl.pallas_call(functools.partial(partial_kernel, parts), in_specs=[VMEM]...  2.55 us
    pallas_call x2, Pallas kernels, place(): pl.pallas_call(functools.partial(place_kernel, core), in_specs=[VMEM] + [...  1.65 us
    pallas_call x1, Pallas kernels, outer_swap(): pl.pallas_call(outer_swap_kernel, in_specs=[VMEM] * 3, out_specs=VMEM, ou...  0.92 us
  transfers between devices with their start and end apart: 19, of which 8 were waited for; matrix products, arithmetic and copies ran while one was open for 1% of the time, Pallas kernels for 16%

profile of v20, /device:TPU:0, one launch (start us, length us, event | category | flops | bytes accessed | tf_op | source)
XLA Modules:
  0.0 43.8 jit_solution(1468069864649469818)
XLA Ops:
  0.6 0.5 %collective-permute-start = (bf16[256,4096]{1,0:T(8,128)(2,1)}, bf16[256,4096]{1,0:T(8,128)(2,1)S(1)}, u32[]{:S(2)}, u32[]{:S(2)}) collective-permute-start(bf16[256,4096]{1,0:T(8,128)(2,1)} %own_ref.13), channel_id=1, source_target_pairs={{0,8},{1,9},{2,10},{3,11},{4,12},{5,13},{6,14},{7,15},{8,0},{9,1},... | collective-permute-start | bytes 6291464 | tf_op jit(solution)/shard_map/ppermute | solution.py:176
  1.9 2.6 %front.1.v0_ref = bf16[272,512]{1,0:T(8,128)(2,1)S(1)} custom-call(f32[16]{0:T(128)} %loss_hbm.1, s32[1]{0:T(128)S(6)} %copy.14.exponent_hbm, s32[1,2]{1,0:T(1,128)} %start_hbm.1, s32[1,2]{1,0:T(1,128)} %rows_hbm.1, bf16[256,2048]{1,0:T(8,128)(2,1)} %q_hbm.1, bf16[256,512]{1,0:T(8,128)(2,1)} %k_hbm.1, bf16[256,2048]{1,0:T(8,128)(2,1)} %g_hbm.1, ...), custom_call_target="tpu_custom_call" | custom-call | tf_op jit(solution)/shard_map/front/pallas_call | solution.py:153
  4.6 0.1 collective-permute-start.1
  4.7 1.5 %collective-permute-done.1.v1_ref = bf16[272,512]{1,0:T(8,128)(2,1)S(1)} collective-permute-done((bf16[272,512]{1,0:T(8,128)(2,1)S(1)}, bf16[272,512]{1,0:T(8,128)(2,1)S(1)}, u32[]{:S(2)}, u32[]{:S(2)}) %collective-permute-start.1) | collective-permute-done | bytes 278560 | tf_op jit(solution)/shard_map/ppermute | solution.py:176
  6.2 0.0 collective-permute-done.near_ref
  6.2 0.3 partial_sums.8
  6.5 2.6 %collective-permute-start.2 = (bf16[128,512]{1,0:T(8,128)(2,1)S(1)}, bf16[128,512]{1,0:T(8,128)(2,1)S(1)}, u32[]{:S(2)}, u32[]{:S(2)}) collective-permute-start(bf16[128,512]{1,0:T(8,128)(2,1)S(1)} %partial_sums.8), channel_id=1, source_target_pairs={{0,1},{1,0},{2,3},{3,2},{4,5},{5,4},{6,7},{7,6},{8,9},{9,8},{10,11... | collective-permute-start | bytes 393224 | tf_op jit(solution)/shard_map/ppermute | solution.py:176
  9.1 0.3 partial_sums.9
  9.3 1.6 %collective-permute-start.3 = (bf16[128,512]{1,0:T(8,128)(2,1)S(1)}, bf16[128,512]{1,0:T(8,128)(2,1)S(1)}, u32[]{:S(2)}, u32[]{:S(2)}) collective-permute-start(bf16[128,512]{1,0:T(8,128)(2,1)S(1)} %partial_sums.9), channel_id=1, source_target_pairs={{0,16},{1,17},{2,18},{3,19},{4,20},{5,21},{6,22},{7,23},{8,24},{9,... | collective-permute-start | bytes 393224 | tf_op jit(solution)/shard_map/ppermute | solution.py:176
  10.9 0.4 partial_sums.11
  11.3 1.6 %collective-permute-start.4 = (bf16[384,256]{1,0:T(8,128)(2,1)S(1)}, bf16[384,256]{1,0:T(8,128)(2,1)S(1)}, u32[]{:S(2)}, u32[]{:S(2)}) collective-permute-start(bf16[384,256]{1,0:T(8,128)(2,1)S(1)} %get-tuple-element.32), channel_id=1, source_target_pairs={{0,2},{1,3},{2,0},{3,1},{4,6},{5,7},{6,4},{7,5},{8,10},{9,11},{10,... | collective-permute-start | bytes 589832 | tf_op jit(solution)/shard_map/ppermute | solution.py:176
  13.0 0.5 %collective-permute-start.5 = (bf16[128,512]{1,0:T(8,128)(2,1)S(1)}, bf16[128,512]{1,0:T(8,128)(2,1)S(1)}, u32[]{:S(2)}, u32[]{:S(2)}) collective-permute-start(bf16[128,512]{1,0:T(8,128)(2,1)S(1)} %get-tuple-element.33), channel_id=1, source_target_pairs={{0,1},{1,0},{2,3},{3,2},{4,5},{5,4},{6,7},{7,6},{8,9},{9,8},{10,11... | collective-permute-start | bytes 393224 | tf_op jit(solution)/shard_map/ppermute | solution.py:176
  13.5 0.4 partial_sums.13
  13.9 0.5 %collective-permute-start.12 = (bf16[384,256]{1,0:T(8,128)(2,1)S(1)}, bf16[384,256]{1,0:T(8,128)(2,1)S(1)}, u32[]{:S(2)}, u32[]{:S(2)}) collective-permute-start(bf16[384,256]{1,0:T(8,128)(2,1)S(1)} %get-tuple-element.43), channel_id=1, source_target_pairs={{0,2},{1,3},{2,0},{3,1},{4,6},{5,7},{6,4},{7,5},{8,10},{9,11},{10,... | collective-permute-start | bytes 589832 | tf_op jit(solution)/shard_map/ppermute | solution.py:176
  14.4 0.5 %partial_sums.7 = (f32[256,512]{1,0:T(8,128)S(1)}, f32[256,512]{1,0:T(8,128)S(1)}) custom-call(bf16[256,4096]{1,0:T(8,128)(2,1)S(1)} %copy-done, bf16[256,4096]{1,0:T(8,128)(2,1)S(1)} %collective-permute-done.near_ref, bf16[272,512]{1,0:T(8,128)(2,1)S(1)} %front.1.v0_ref, bf16[272,512]{1,0:T(8,128)(2,1)S(1)} %collective-permute-done.1.v1_ref), custom_call_target="tpu_custom_call" | custom-call | tf_op jit(solution)/shard_map/partial_sums/pallas_call | solution.py:201
  14.9 0.0 collective-permute-done.3
  15.0 1.5 %collective-permute-start.6 = (bf16[128,512]{1,0:T(8,128)(2,1)S(1)}, bf16[128,512]{1,0:T(8,128)(2,1)S(1)}, u32[]{:S(2)}, u32[]{:S(2)}) collective-permute-start(bf16[128,512]{1,0:T(8,128)(2,1)S(1)} %add_convert_fusion.4), channel_id=1, source_target_pairs={{0,16},{1,17},{2,18},{3,19},{4,20},{5,21},{6,22},{7,23},{8,24},{9,... | collective-permute-start | bytes 393224 | tf_op jit(solution)/shard_map/ppermute | solution.py:176
  16.5 0.6 %collective-permute-start.9 = (bf16[128,512]{1,0:T(8,128)(2,1)S(1)}, bf16[128,512]{1,0:T(8,128)(2,1)S(1)}, u32[]{:S(2)}, u32[]{:S(2)}) collective-permute-start(bf16[128,512]{1,0:T(8,128)(2,1)S(1)} %add_convert_fusion.2), channel_id=1, source_target_pairs={{0,1},{1,0},{2,3},{3,2},{4,5},{5,4},{6,7},{7,6},{8,9},{9,8},{10,11... | collective-permute-start | bytes 393224 | tf_op jit(solution)/shard_map/ppermute | solution.py:176
  17.1 0.5 %partial_sums.10 = (f32[512,256]{1,0:T(8,128)S(1)}, f32[512,256]{1,0:T(8,128)S(1)}) custom-call(bf16[256,4096]{1,0:T(8,128)(2,1)S(1)} %copy-done, bf16[256,4096]{1,0:T(8,128)(2,1)S(1)} %collective-permute-done.near_ref, bf16[272,512]{1,0:T(8,128)(2,1)S(1)} %front.1.v0_ref, bf16[272,512]{1,0:T(8,128)(2,1)S(1)} %collective-permute-done.1.v1_ref), custom_call_target="tpu_custom_call" | custom-call | tf_op jit(solution)/shard_map/partial_sums/pallas_call | solution.py:201
  17.6 0.3 inner_swap.1
  18.0 0.3 partial_sums.12
  18.2 0.0 collective-permute-done.5
  18.3 1.6 %collective-permute-start.8 = (bf16[160,512]{1,0:T(8,128)(2,1)S(1)}, bf16[160,512]{1,0:T(8,128)(2,1)S(1)}, u32[]{:S(2)}, u32[]{:S(2)}) collective-permute-start(bf16[160,512]{1,0:T(8,128)(2,1)S(1)} %pad_maximum_fusion.2), channel_id=1, source_target_pairs={{0,16},{1,17},{2,18},{3,19},{4,20},{5,21},{6,22},{7,23},{8,24},{9,... | collective-permute-start | bytes 491528 | tf_op jit(solution)/shard_map/ppermute | solution.py:176
  19.8 0.6 %collective-permute-done.6 = bf16[128,512]{1,0:T(8,128)(2,1)S(1)} collective-permute-done((bf16[128,512]{1,0:T(8,128)(2,1)S(1)}, bf16[128,512]{1,0:T(8,128)(2,1)S(1)}, u32[]{:S(2)}, u32[]{:S(2)}) %collective-permute-start.6) | collective-permute-done | bytes 131104 | tf_op jit(solution)/shard_map/ppermute | solution.py:176
  20.4 1.6 %collective-permute-start.10 = (bf16[128,512]{1,0:T(8,128)(2,1)S(1)}, bf16[128,512]{1,0:T(8,128)(2,1)S(1)}, u32[]{:S(2)}, u32[]{:S(2)}) collective-permute-start(bf16[128,512]{1,0:T(8,128)(2,1)S(1)} %add_convert_fusion.3), channel_id=1, source_target_pairs={{0,2},{1,3},{2,0},{3,1},{4,6},{5,7},{6,4},{7,5},{8,10},{9,11},{10,... | collective-permute-start | bytes 393224 | tf_op jit(solution)/shard_map/ppermute | solution.py:176
  22.1 0.0 collective-permute-done.4
  22.1 1.9 %collective-permute-start.7 = (bf16[256,256]{1,0:T(8,128)(2,1)S(1)}, bf16[256,256]{1,0:T(8,128)(2,1)S(1)}, u32[]{:S(2)}, u32[]{:S(2)}) collective-permute-start(bf16[256,256]{1,0:T(8,128)(2,1)S(1)} %slice.116), channel_id=1, source_target_pairs={{0,16},{1,17},{2,18},{3,19},{4,20},{5,21},{6,22},{7,23},{8,24},{9,... | collective-permute-start | bytes 393224 | tf_op jit(solution)/shard_map/ppermute | solution.py:176
  24.1 0.3 collective-permute-start.13
  24.4 0.0 collective-permute-done.9
  24.4 0.5 %collective-permute-done.8 = bf16[160,512]{1,0:T(8,128)(2,1)S(1)} collective-permute-done((bf16[160,512]{1,0:T(8,128)(2,1)S(1)}, bf16[160,512]{1,0:T(8,128)(2,1)S(1)}, u32[]{:S(2)}, u32[]{:S(2)}) %collective-permute-start.8) | collective-permute-done | bytes 163872 | tf_op jit(solution)/shard_map/ppermute | solution.py:176
  24.9 0.6 %collective-permute-done.10 = bf16[128,512]{1,0:T(8,128)(2,1)S(1)} collective-permute-done((bf16[128,512]{1,0:T(8,128)(2,1)S(1)}, bf16[128,512]{1,0:T(8,128)(2,1)S(1)}, u32[]{:S(2)}, u32[]{:S(2)}) %collective-permute-start.10) | collective-permute-done | bytes 131104 | tf_op jit(solution)/shard_map/ppermute | solution.py:176
  25.5 0.1 add_convert_fusion.1
  25.5 2.7 %collective-permute-start.14 = (bf16[128,512]{1,0:T(8,128)(2,1)S(1)}, bf16[128,512]{1,0:T(8,128)(2,1)S(1)}, u32[]{:S(2)}, u32[]{:S(2)}) collective-permute-start(bf16[128,512]{1,0:T(8,128)(2,1)S(1)} %add_convert_fusion.1), channel_id=1, source_target_pairs={{0,4},{1,5},{2,6},{3,7},{4,0},{5,1},{6,2},{7,3},{8,12},{9,13},{10,... | collective-permute-start | bytes 393224 | tf_op jit(solution)/shard_map/ppermute | solution.py:176
  28.2 0.0 collective-permute-done.7
  28.2 1.6 %collective-permute-start.11 = (bf16[128,512]{1,0:T(8,128)(2,1)S(1)}, bf16[128,512]{1,0:T(8,128)(2,1)S(1)}, u32[]{:S(2)}, u32[]{:S(2)}) collective-permute-start(bf16[128,512]{1,0:T(8,128)(2,1)S(1)} %partial_sums.12), channel_id=1, source_target_pairs={{0,2},{1,3},{2,0},{3,1},{4,6},{5,7},{6,4},{7,5},{8,10},{9,11},{10,... | collective-permute-start | bytes 393224 | tf_op jit(solution)/shard_map/ppermute | solution.py:176
  29.8 1.5 %collective-permute-start.15 = (bf16[128,256]{1,0:T(8,128)(2,1)S(1)}, bf16[128,256]{1,0:T(8,128)(2,1)S(1)}, u32[]{:S(2)}, u32[]{:S(2)}) collective-permute-start(bf16[128,256]{1,0:T(8,128)(2,1)S(1)} %fusion), channel_id=1, source_target_pairs={{0,1},{1,0},{2,3},{3,2},{4,5},{5,4},{6,7},{7,6},{8,9},{9,8},{10,11... | collective-permute-start | bytes 196616 | tf_op jit(solution)/shard_map/ppermute | solution.py:176
  31.3 0.0 collective-permute-done.13
  31.4 0.6 %collective-permute-start.16 = (bf16[128,256]{1,0:T(8,128)(2,1)S(1)}, bf16[128,256]{1,0:T(8,128)(2,1)S(1)}, u32[]{:S(2)}, u32[]{:S(2)}) collective-permute-start(bf16[128,256]{1,0:T(8,128)(2,1)S(1)} %fusion.1), channel_id=1, source_target_pairs={{0,16},{1,17},{2,18},{3,19},{4,20},{5,21},{6,22},{7,23},{8,24},{9,... | collective-permute-start | bytes 196616 | tf_op jit(solution)/shard_map/ppermute | solution.py:176
  32.0 1.5 %collective-permute-done.11 = bf16[128,512]{1,0:T(8,128)(2,1)S(1)} collective-permute-done((bf16[128,512]{1,0:T(8,128)(2,1)S(1)}, bf16[128,512]{1,0:T(8,128)(2,1)S(1)}, u32[]{:S(2)}, u32[]{:S(2)}) %collective-permute-start.11) | collective-permute-done | bytes 131104 | tf_op jit(solution)/shard_map/ppermute | solution.py:176
  33.5 0.0 collective-permute-done.14.arrived_ref
  33.6 2.7 %collective-permute-done.16 = bf16[128,256]{1,0:T(8,128)(2,1)S(1)} collective-permute-done((bf16[128,256]{1,0:T(8,128)(2,1)S(1)}, bf16[128,256]{1,0:T(8,128)(2,1)S(1)}, u32[]{:S(2)}, u32[]{:S(2)}) %collective-permute-start.16) | collective-permute-done | bytes 65568 | tf_op jit(solution)/shard_map/ppermute | solution.py:176
  36.3 0.6 %collective-permute-start.17 = (bf16[128,512]{1,0:T(8,128)(2,1)S(1)}, bf16[128,512]{1,0:T(8,128)(2,1)S(1)}, u32[]{:S(2)}, u32[]{:S(2)}) collective-permute-start(bf16[128,512]{1,0:T(8,128)(2,1)S(1)} %add_convert_fusion), channel_id=1, source_target_pairs={{0,16},{1,17},{2,18},{3,19},{4,20},{5,21},{6,22},{7,23},{8,24},{9,... | collective-permute-start | bytes 393224 | tf_op jit(solution)/shard_map/ppermute | solution.py:176
  37.0 0.9 %outer_swap.1 = bf16[256,512]{1,0:T(8,128)(2,1)} custom-call(bf16[272,512]{1,0:T(8,128)(2,1)S(1)} %front.1.v0_ref, bf16[256,512]{1,0:T(8,128)(2,1)S(1)} %get-tuple-element.48.rows_ref, bf16[32,512]{1,0:T(8,128)(2,1)S(1)} %slice.93.window_ref), custom_call_target="tpu_custom_call" | custom-call | tf_op jit(solution)/shard_map/outer_swap/pallas_call | solution.py:265
  37.9 3.5 %collective-permute-done.17 = bf16[128,512]{1,0:T(8,128)(2,1)S(1)} collective-permute-done((bf16[128,512]{1,0:T(8,128)(2,1)S(1)}, bf16[128,512]{1,0:T(8,128)(2,1)S(1)}, u32[]{:S(2)}, u32[]{:S(2)}) %collective-permute-start.17) | collective-permute-done | bytes 131104 | tf_op jit(solution)/shard_map/ppermute | solution.py:176
  41.4 0.1 collective-permute-start.18
  41.5 0.8 %place.2.rest_0_ = f32[512,512]{1,0:T(8,128)} custom-call(bf16[2,128,512]{2,1,0:T(8,128)(2,1)S(1)} %pad_maximum_fusion.1.pair_ref), custom_call_target="tpu_custom_call" | custom-call | tf_op jit(solution)/shard_map/place/pallas_call | solution.py:289
  42.3 0.7 %collective-permute-done.18.pair_ref = bf16[2,128,512]{2,1,0:T(8,128)(2,1)S(1)} collective-permute-done((bf16[2,128,512]{2,1,0:T(8,128)(2,1)S(1)}, bf16[2,128,512]{2,1,0:T(8,128)(2,1)S(1)}, u32[]{:S(2)}, u32[]{:S(2)}) %collective-permute-start.18) | collective-permute-done | bytes 262176 | tf_op jit(solution)/shard_map/ppermute | solution.py:176
  43.0 0.8 %place.3 = f32[512,512]{1,0:T(8,128)} custom-call(bf16[2,128,512]{2,1,0:T(8,128)(2,1)S(1)} %collective-permute-done.18.pair_ref, f32[512,512]{1,0:T(8,128)} %place.2.rest_0_), custom_call_target="tpu_custom_call", output_to_operand_aliasing={{}: (1, {})} | custom-call | tf_op jit(solution)/shard_map/place/pallas_call | solution.py:289
  (22 shorter events, 0.4 us)
Async XLA Ops:
  0.6 5.6 %copy-start = (bf16[256,4096]{1,0:T(8,128)(2,1)S(1)}, bf16[256,4096]{1,0:T(8,128)(2,1)}, u32[]{:S(2)}) copy-start(bf16[256,4096]{1,0:T(8,128)(2,1)} %own_ref.13) | copy-start | bytes 6291460
  0.6 5.5 %collective-permute-start = (bf16[256,4096]{1,0:T(8,128)(2,1)}, bf16[256,4096]{1,0:T(8,128)(2,1)S(1)}, u32[]{:S(2)}, u32[]{:S(2)}) collective-permute-start(bf16[256,4096]{1,0:T(8,128)(2,1)} %own_ref.13), channel_id=1, source_target_pairs={{0,8},{1,9},{2,10},{3,11},{4,12},{5,13},{6,14},{7,15},{8,0},{9,1},... | collective-permute-start | bytes 6291464 | tf_op jit(solution)/shard_map/ppermute | solution.py:176
  4.6 1.6 %collective-permute-start.1 = (bf16[272,512]{1,0:T(8,128)(2,1)S(1)}, bf16[272,512]{1,0:T(8,128)(2,1)S(1)}, u32[]{:S(2)}, u32[]{:S(2)}) collective-permute-start(bf16[272,512]{1,0:T(8,128)(2,1)S(1)} %front.1.v0_ref), channel_id=1, source_target_pairs={{0,8},{1,9},{2,10},{3,11},{4,12},{5,13},{6,14},{7,15},{8,0},{9,1},... | collective-permute-start | bytes 835592 | tf_op jit(solution)/shard_map/ppermute | solution.py:176
  6.5 8.4 %collective-permute-start.2 = (bf16[128,512]{1,0:T(8,128)(2,1)S(1)}, bf16[128,512]{1,0:T(8,128)(2,1)S(1)}, u32[]{:S(2)}, u32[]{:S(2)}) collective-permute-start(bf16[128,512]{1,0:T(8,128)(2,1)S(1)} %partial_sums.8), channel_id=1, source_target_pairs={{0,1},{1,0},{2,3},{3,2},{4,5},{5,4},{6,7},{7,6},{8,9},{9,8},{10,11... | collective-permute-start | bytes 393224 | tf_op jit(solution)/shard_map/ppermute | solution.py:176
  9.3 5.6 %collective-permute-start.3 = (bf16[128,512]{1,0:T(8,128)(2,1)S(1)}, bf16[128,512]{1,0:T(8,128)(2,1)S(1)}, u32[]{:S(2)}, u32[]{:S(2)}) collective-permute-start(bf16[128,512]{1,0:T(8,128)(2,1)S(1)} %partial_sums.9), channel_id=1, source_target_pairs={{0,16},{1,17},{2,18},{3,19},{4,20},{5,21},{6,22},{7,23},{8,24},{9,... | collective-permute-start | bytes 393224 | tf_op jit(solution)/shard_map/ppermute | solution.py:176
  11.3 10.7 %collective-permute-start.4 = (bf16[384,256]{1,0:T(8,128)(2,1)S(1)}, bf16[384,256]{1,0:T(8,128)(2,1)S(1)}, u32[]{:S(2)}, u32[]{:S(2)}) collective-permute-start(bf16[384,256]{1,0:T(8,128)(2,1)S(1)} %get-tuple-element.32), channel_id=1, source_target_pairs={{0,2},{1,3},{2,0},{3,1},{4,6},{5,7},{6,4},{7,5},{8,10},{9,11},{10,... | collective-permute-start | bytes 589832 | tf_op jit(solution)/shard_map/ppermute | solution.py:176
  13.0 5.3 %collective-permute-start.5 = (bf16[128,512]{1,0:T(8,128)(2,1)S(1)}, bf16[128,512]{1,0:T(8,128)(2,1)S(1)}, u32[]{:S(2)}, u32[]{:S(2)}) collective-permute-start(bf16[128,512]{1,0:T(8,128)(2,1)S(1)} %get-tuple-element.33), channel_id=1, source_target_pairs={{0,1},{1,0},{2,3},{3,2},{4,5},{5,4},{6,7},{7,6},{8,9},{9,8},{10,11... | collective-permute-start | bytes 393224 | tf_op jit(solution)/shard_map/ppermute | solution.py:176
  13.9 10.1 %collective-permute-start.12 = (bf16[384,256]{1,0:T(8,128)(2,1)S(1)}, bf16[384,256]{1,0:T(8,128)(2,1)S(1)}, u32[]{:S(2)}, u32[]{:S(2)}) collective-permute-start(bf16[384,256]{1,0:T(8,128)(2,1)S(1)} %get-tuple-element.43), channel_id=1, source_target_pairs={{0,2},{1,3},{2,0},{3,1},{4,6},{5,7},{6,4},{7,5},{8,10},{9,11},{10,... | collective-permute-start | bytes 589832 | tf_op jit(solution)/shard_map/ppermute | solution.py:176
  15.0 5.4 %collective-permute-start.6 = (bf16[128,512]{1,0:T(8,128)(2,1)S(1)}, bf16[128,512]{1,0:T(8,128)(2,1)S(1)}, u32[]{:S(2)}, u32[]{:S(2)}) collective-permute-start(bf16[128,512]{1,0:T(8,128)(2,1)S(1)} %add_convert_fusion.4), channel_id=1, source_target_pairs={{0,16},{1,17},{2,18},{3,19},{4,20},{5,21},{6,22},{7,23},{8,24},{9,... | collective-permute-start | bytes 393224 | tf_op jit(solution)/shard_map/ppermute | solution.py:176
  16.5 7.9 %collective-permute-start.9 = (bf16[128,512]{1,0:T(8,128)(2,1)S(1)}, bf16[128,512]{1,0:T(8,128)(2,1)S(1)}, u32[]{:S(2)}, u32[]{:S(2)}) collective-permute-start(bf16[128,512]{1,0:T(8,128)(2,1)S(1)} %add_convert_fusion.2), channel_id=1, source_target_pairs={{0,1},{1,0},{2,3},{3,2},{4,5},{5,4},{6,7},{7,6},{8,9},{9,8},{10,11... | collective-permute-start | bytes 393224 | tf_op jit(solution)/shard_map/ppermute | solution.py:176
  18.3 6.6 %collective-permute-start.8 = (bf16[160,512]{1,0:T(8,128)(2,1)S(1)}, bf16[160,512]{1,0:T(8,128)(2,1)S(1)}, u32[]{:S(2)}, u32[]{:S(2)}) collective-permute-start(bf16[160,512]{1,0:T(8,128)(2,1)S(1)} %pad_maximum_fusion.2), channel_id=1, source_target_pairs={{0,16},{1,17},{2,18},{3,19},{4,20},{5,21},{6,22},{7,23},{8,24},{9,... | collective-permute-start | bytes 491528 | tf_op jit(solution)/shard_map/ppermute | solution.py:176
  20.4 5.0 %collective-permute-start.10 = (bf16[128,512]{1,0:T(8,128)(2,1)S(1)}, bf16[128,512]{1,0:T(8,128)(2,1)S(1)}, u32[]{:S(2)}, u32[]{:S(2)}) collective-permute-start(bf16[128,512]{1,0:T(8,128)(2,1)S(1)} %add_convert_fusion.3), channel_id=1, source_target_pairs={{0,2},{1,3},{2,0},{3,1},{4,6},{5,7},{6,4},{7,5},{8,10},{9,11},{10,... | collective-permute-start | bytes 393224 | tf_op jit(solution)/shard_map/ppermute | solution.py:176
  22.1 6.1 %collective-permute-start.7 = (bf16[256,256]{1,0:T(8,128)(2,1)S(1)}, bf16[256,256]{1,0:T(8,128)(2,1)S(1)}, u32[]{:S(2)}, u32[]{:S(2)}) collective-permute-start(bf16[256,256]{1,0:T(8,128)(2,1)S(1)} %slice.116), channel_id=1, source_target_pairs={{0,16},{1,17},{2,18},{3,19},{4,20},{5,21},{6,22},{7,23},{8,24},{9,... | collective-permute-start | bytes 393224 | tf_op jit(solution)/shard_map/ppermute | solution.py:176
  24.1 7.3 %collective-permute-start.13 = (bf16[256,256]{1,0:T(8,128)(2,1)S(1)}, bf16[256,256]{1,0:T(8,128)(2,1)S(1)}, u32[]{:S(2)}, u32[]{:S(2)}) collective-permute-start(bf16[256,256]{1,0:T(8,128)(2,1)S(1)} %pad_maximum_fusion.3), channel_id=1, source_target_pairs={{0,1},{1,0},{2,3},{3,2},{4,5},{5,4},{6,7},{7,6},{8,9},{9,8},{10,11... | collective-permute-start | bytes 393224 | tf_op jit(solution)/shard_map/ppermute | solution.py:176
  25.5 8.0 %collective-permute-start.14 = (bf16[128,512]{1,0:T(8,128)(2,1)S(1)}, bf16[128,512]{1,0:T(8,128)(2,1)S(1)}, u32[]{:S(2)}, u32[]{:S(2)}) collective-permute-start(bf16[128,512]{1,0:T(8,128)(2,1)S(1)} %add_convert_fusion.1), channel_id=1, source_target_pairs={{0,4},{1,5},{2,6},{3,7},{4,0},{5,1},{6,2},{7,3},{8,12},{9,13},{10,... | collective-permute-start | bytes 393224 | tf_op jit(solution)/shard_map/ppermute | solution.py:176
  28.2 5.3 %collective-permute-start.11 = (bf16[128,512]{1,0:T(8,128)(2,1)S(1)}, bf16[128,512]{1,0:T(8,128)(2,1)S(1)}, u32[]{:S(2)}, u32[]{:S(2)}) collective-permute-start(bf16[128,512]{1,0:T(8,128)(2,1)S(1)} %partial_sums.12), channel_id=1, source_target_pairs={{0,2},{1,3},{2,0},{3,1},{4,6},{5,7},{6,4},{7,5},{8,10},{9,11},{10,... | collective-permute-start | bytes 393224 | tf_op jit(solution)/shard_map/ppermute | solution.py:176
  29.8 6.5 %collective-permute-start.15 = (bf16[128,256]{1,0:T(8,128)(2,1)S(1)}, bf16[128,256]{1,0:T(8,128)(2,1)S(1)}, u32[]{:S(2)}, u32[]{:S(2)}) collective-permute-start(bf16[128,256]{1,0:T(8,128)(2,1)S(1)} %fusion), channel_id=1, source_target_pairs={{0,1},{1,0},{2,3},{3,2},{4,5},{5,4},{6,7},{7,6},{8,9},{9,8},{10,11... | collective-permute-start | bytes 196616 | tf_op jit(solution)/shard_map/ppermute | solution.py:176
  31.4 5.0 %collective-permute-start.16 = (bf16[128,256]{1,0:T(8,128)(2,1)S(1)}, bf16[128,256]{1,0:T(8,128)(2,1)S(1)}, u32[]{:S(2)}, u32[]{:S(2)}) collective-permute-start(bf16[128,256]{1,0:T(8,128)(2,1)S(1)} %fusion.1), channel_id=1, source_target_pairs={{0,16},{1,17},{2,18},{3,19},{4,20},{5,21},{6,22},{7,23},{8,24},{9,... | collective-permute-start | bytes 196616 | tf_op jit(solution)/shard_map/ppermute | solution.py:176
  36.3 5.0 %collective-permute-start.17 = (bf16[128,512]{1,0:T(8,128)(2,1)S(1)}, bf16[128,512]{1,0:T(8,128)(2,1)S(1)}, u32[]{:S(2)}, u32[]{:S(2)}) collective-permute-start(bf16[128,512]{1,0:T(8,128)(2,1)S(1)} %add_convert_fusion), channel_id=1, source_target_pairs={{0,16},{1,17},{2,18},{3,19},{4,20},{5,21},{6,22},{7,23},{8,24},{9,... | collective-permute-start | bytes 393224 | tf_op jit(solution)/shard_map/ppermute | solution.py:176
  41.4 1.6 %collective-permute-start.18 = (bf16[2,128,512]{2,1,0:T(8,128)(2,1)S(1)}, bf16[2,128,512]{2,1,0:T(8,128)(2,1)S(1)}, u32[]{:S(2)}, u32[]{:S(2)}) collective-permute-start(bf16[2,128,512]{2,1,0:T(8,128)(2,1)S(1)} %pad_maximum_fusion.1.pair_ref), channel_id=1, source_target_pairs={{0,8},{1,9},{2,10},{3,11},{4,12},{5,13},{6,14},{7,15},{8,0},{9,1},... | collective-permute-start | bytes 786440 | tf_op jit(solution)/shard_map/ppermute | solution.py:176

commit v21 on v20

--- a/solution.py
+++ b/solution.py
@@ -361,19 +361,19 @@
     z2 = add(keep_a[LANE:], side_a, on_a, z3).astype(BF16)
 
     some = add(own_some[:3 * LANE], pair_some)
-    some_in = xor_permute(some[:2 * LANE].astype(BF16), Y)
+    some_far, some_y, some_x = (some[row:row + LANE] for row in range(0, 3 * LANE, LANE))
+    some_in = xor_permute(jnp.concatenate([some_far, some_x]).astype(BF16), X)
     rest = add(own_rest[:3 * LANE], after_all(pair_rest, some)[0])
-    rest_far, rest_y, rest_x = (rest[row:row + LANE] for row in range(0, 3 * LANE, LANE))
-    rest_in = xor_permute(jnp.concatenate([rest_far, rest_x]).astype(BF16), X)
+    rest_in = xor_permute(rest[:2 * LANE].astype(BF16), Y)
     some_in, pair_own = after_all(some_in, pair_own, z2)[:2]
     z2 = xor_permute(z2, Z2)
     pair_own = xor_permute(pair_own, Z1)
-    some_on = add(some[2 * LANE:], some_in[:LANE]).astype(BF16)
+    some_on = add(some_y, some_in[:LANE]).astype(BF16)
     rest_in = after_all(rest_in, some_on)[0]
-    some_on = xor_permute(some_on, X)
-    rest_on = add(rest_y, rest_in[:LANE]).astype(BF16)
+    some_on = xor_permute(some_on, Y)
+    rest_on = add(rest[2 * LANE:], rest_in[:LANE]).astype(BF16)
     pair_own = after_all(pair_own, rest_on)[0]
-    rest_on = xor_permute(rest_on, Y)
+    rest_on = xor_permute(rest_on, X)
     base = jnp.concatenate([
         add(own_some[3 * LANE:], pair_own[:, :256], some_in[LANE:]),
         add(own_rest[3 * LANE:], pair_own[:, 256:], rest_in[LANE:]),

time: 44 us -> 43.9 us (level)
  transfers between devices with their start and end apart: 19 -> 19, of which waited for: 8 -> 7; matrix products, arithmetic and copies ran while one was open for 1% -> 1% of each run, Pallas kernels for 16% -> 16%
where the time goes in v21:
time: 43.9 us; the launch traced here: 43.7 us
  starting transfers between devices  22.1 us (50%)
  waiting for transfers between devices  11.5 us (26%)
  Pallas kernels  8.1 us (18%)
  between operations  1.61 us (4%)
    ppermute x19, starting transfers between devices, xor_permute(): lax.ppermute(value, ('dp', 'fsdp'), [(i, i ^ mask) for i in range(count)])  22.1 us
    ppermute x19, waiting for transfers between devices, xor_permute(): lax.ppermute(value, ('dp', 'fsdp'), [(i, i ^ mask) for i in range(count)])  11.5 us
    pallas_call x1, Pallas kernels, front(): pl.pallas_call(functools.partial(front_kernel, per_group), in_specs=[HBM]...  2.64 us
    pallas_call x7, Pallas kernels, partial_sums(): pl.pallas_call(functools.partial(partial_kernel, parts), in_specs=[VMEM]...  2.55 us
    pallas_call x2, Pallas kernels, place(): pl.pallas_call(functools.partial(place_kernel, core), in_specs=[VMEM] + [...  1.65 us
    pallas_call x1, Pallas kernels, outer_swap(): pl.pallas_call(outer_swap_kernel, in_specs=[VMEM] * 3, out_specs=VMEM, ou...  0.91 us
  transfers between devices with their start and end apart: 19, of which 7 were waited for; matrix products, arithmetic and copies ran while one was open for 1% of the time, Pallas kernels for 16%

profile of v21, /device:TPU:0, one launch (start us, length us, event | category | flops | bytes accessed | tf_op | source)
XLA Modules:
  0.0 43.7 jit_solution(7161459423955182588)
XLA Ops:
  0.6 0.5 %collective-permute-start = (bf16[256,4096]{1,0:T(8,128)(2,1)}, bf16[256,4096]{1,0:T(8,128)(2,1)S(1)}, u32[]{:S(2)}, u32[]{:S(2)}) collective-permute-start(bf16[256,4096]{1,0:T(8,128)(2,1)} %own_ref.13), channel_id=1, source_target_pairs={{0,8},{1,9},{2,10},{3,11},{4,12},{5,13},{6,14},{7,15},{8,0},{9,1},... | collective-permute-start | bytes 6291464 | tf_op jit(solution)/shard_map/ppermute | solution.py:176
  1.9 2.6 %front.1.v0_ref = bf16[272,512]{1,0:T(8,128)(2,1)S(1)} custom-call(f32[16]{0:T(128)} %loss_hbm.1, s32[1]{0:T(128)S(6)} %copy.14.exponent_hbm, s32[1,2]{1,0:T(1,128)} %start_hbm.1, s32[1,2]{1,0:T(1,128)} %rows_hbm.1, bf16[256,2048]{1,0:T(8,128)(2,1)} %q_hbm.1, bf16[256,512]{1,0:T(8,128)(2,1)} %k_hbm.1, bf16[256,2048]{1,0:T(8,128)(2,1)} %g_hbm.1, ...), custom_call_target="tpu_custom_call" | custom-call | tf_op jit(solution)/shard_map/front/pallas_call | solution.py:153
  4.6 0.1 collective-permute-start.1
  4.7 1.5 %collective-permute-done.1.v1_ref = bf16[272,512]{1,0:T(8,128)(2,1)S(1)} collective-permute-done((bf16[272,512]{1,0:T(8,128)(2,1)S(1)}, bf16[272,512]{1,0:T(8,128)(2,1)S(1)}, u32[]{:S(2)}, u32[]{:S(2)}) %collective-permute-start.1) | collective-permute-done | bytes 278560 | tf_op jit(solution)/shard_map/ppermute | solution.py:176
  6.2 0.0 collective-permute-done.near_ref
  6.2 0.3 partial_sums.8
  6.5 2.6 %collective-permute-start.2 = (bf16[128,512]{1,0:T(8,128)(2,1)S(1)}, bf16[128,512]{1,0:T(8,128)(2,1)S(1)}, u32[]{:S(2)}, u32[]{:S(2)}) collective-permute-start(bf16[128,512]{1,0:T(8,128)(2,1)S(1)} %partial_sums.8), channel_id=1, source_target_pairs={{0,1},{1,0},{2,3},{3,2},{4,5},{5,4},{6,7},{7,6},{8,9},{9,8},{10,11... | collective-permute-start | bytes 393224 | tf_op jit(solution)/shard_map/ppermute | solution.py:176
  9.1 0.3 partial_sums.9
  9.3 1.6 %collective-permute-start.3 = (bf16[128,512]{1,0:T(8,128)(2,1)S(1)}, bf16[128,512]{1,0:T(8,128)(2,1)S(1)}, u32[]{:S(2)}, u32[]{:S(2)}) collective-permute-start(bf16[128,512]{1,0:T(8,128)(2,1)S(1)} %partial_sums.9), channel_id=1, source_target_pairs={{0,16},{1,17},{2,18},{3,19},{4,20},{5,21},{6,22},{7,23},{8,24},{9,... | collective-permute-start | bytes 393224 | tf_op jit(solution)/shard_map/ppermute | solution.py:176
  10.9 0.4 partial_sums.11
  11.3 1.6 %collective-permute-start.4 = (bf16[384,256]{1,0:T(8,128)(2,1)S(1)}, bf16[384,256]{1,0:T(8,128)(2,1)S(1)}, u32[]{:S(2)}, u32[]{:S(2)}) collective-permute-start(bf16[384,256]{1,0:T(8,128)(2,1)S(1)} %get-tuple-element.32), channel_id=1, source_target_pairs={{0,2},{1,3},{2,0},{3,1},{4,6},{5,7},{6,4},{7,5},{8,10},{9,11},{10,... | collective-permute-start | bytes 589832 | tf_op jit(solution)/shard_map/ppermute | solution.py:176
  13.0 0.5 %collective-permute-start.5 = (bf16[128,512]{1,0:T(8,128)(2,1)S(1)}, bf16[128,512]{1,0:T(8,128)(2,1)S(1)}, u32[]{:S(2)}, u32[]{:S(2)}) collective-permute-start(bf16[128,512]{1,0:T(8,128)(2,1)S(1)} %get-tuple-element.33), channel_id=1, source_target_pairs={{0,1},{1,0},{2,3},{3,2},{4,5},{5,4},{6,7},{7,6},{8,9},{9,8},{10,11... | collective-permute-start | bytes 393224 | tf_op jit(solution)/shard_map/ppermute | solution.py:176
  13.5 0.4 partial_sums.13
  13.9 0.5 %collective-permute-start.12 = (bf16[384,256]{1,0:T(8,128)(2,1)S(1)}, bf16[384,256]{1,0:T(8,128)(2,1)S(1)}, u32[]{:S(2)}, u32[]{:S(2)}) collective-permute-start(bf16[384,256]{1,0:T(8,128)(2,1)S(1)} %get-tuple-element.43), channel_id=1, source_target_pairs={{0,2},{1,3},{2,0},{3,1},{4,6},{5,7},{6,4},{7,5},{8,10},{9,11},{10,... | collective-permute-start | bytes 589832 | tf_op jit(solution)/shard_map/ppermute | solution.py:176
  14.4 0.5 %partial_sums.7 = (f32[256,512]{1,0:T(8,128)S(1)}, f32[256,512]{1,0:T(8,128)S(1)}) custom-call(bf16[256,4096]{1,0:T(8,128)(2,1)S(1)} %copy-done, bf16[256,4096]{1,0:T(8,128)(2,1)S(1)} %collective-permute-done.near_ref, bf16[272,512]{1,0:T(8,128)(2,1)S(1)} %front.1.v0_ref, bf16[272,512]{1,0:T(8,128)(2,1)S(1)} %collective-permute-done.1.v1_ref), custom_call_target="tpu_custom_call" | custom-call | tf_op jit(solution)/shard_map/partial_sums/pallas_call | solution.py:201
  14.9 0.0 collective-permute-done.2
  14.9 0.0 collective-permute-done.3
  15.0 1.5 %collective-permute-start.6 = (bf16[128,512]{1,0:T(8,128)(2,1)S(1)}, bf16[128,512]{1,0:T(8,128)(2,1)S(1)}, u32[]{:S(2)}, u32[]{:S(2)}) collective-permute-start(bf16[128,512]{1,0:T(8,128)(2,1)S(1)} %add_convert_fusion.4), channel_id=1, source_target_pairs={{0,16},{1,17},{2,18},{3,19},{4,20},{5,21},{6,22},{7,23},{8,24},{9,... | collective-permute-start | bytes 393224 | tf_op jit(solution)/shard_map/ppermute | solution.py:176
  16.5 0.6 %collective-permute-start.9 = (bf16[128,512]{1,0:T(8,128)(2,1)S(1)}, bf16[128,512]{1,0:T(8,128)(2,1)S(1)}, u32[]{:S(2)}, u32[]{:S(2)}) collective-permute-start(bf16[128,512]{1,0:T(8,128)(2,1)S(1)} %add_convert_fusion.2), channel_id=1, source_target_pairs={{0,1},{1,0},{2,3},{3,2},{4,5},{5,4},{6,7},{7,6},{8,9},{9,8},{10,11... | collective-permute-start | bytes 393224 | tf_op jit(solution)/shard_map/ppermute | solution.py:176
  17.1 0.5 %partial_sums.10 = (f32[512,256]{1,0:T(8,128)S(1)}, f32[512,256]{1,0:T(8,128)S(1)}) custom-call(bf16[256,4096]{1,0:T(8,128)(2,1)S(1)} %copy-done, bf16[256,4096]{1,0:T(8,128)(2,1)S(1)} %collective-permute-done.near_ref, bf16[272,512]{1,0:T(8,128)(2,1)S(1)} %front.1.v0_ref, bf16[272,512]{1,0:T(8,128)(2,1)S(1)} %collective-permute-done.1.v1_ref), custom_call_target="tpu_custom_call" | custom-call | tf_op jit(solution)/shard_map/partial_sums/pallas_call | solution.py:201
  17.6 0.3 inner_swap.1
  18.0 0.3 partial_sums.12
  18.2 0.0 collective-permute-done.5
  18.3 1.6 %collective-permute-start.8 = (bf16[160,512]{1,0:T(8,128)(2,1)S(1)}, bf16[160,512]{1,0:T(8,128)(2,1)S(1)}, u32[]{:S(2)}, u32[]{:S(2)}) collective-permute-start(bf16[160,512]{1,0:T(8,128)(2,1)S(1)} %pad_maximum_fusion.2), channel_id=1, source_target_pairs={{0,16},{1,17},{2,18},{3,19},{4,20},{5,21},{6,22},{7,23},{8,24},{9,... | collective-permute-start | bytes 491528 | tf_op jit(solution)/shard_map/ppermute | solution.py:176
  19.8 0.6 %collective-permute-done.6 = bf16[128,512]{1,0:T(8,128)(2,1)S(1)} collective-permute-done((bf16[128,512]{1,0:T(8,128)(2,1)S(1)}, bf16[128,512]{1,0:T(8,128)(2,1)S(1)}, u32[]{:S(2)}, u32[]{:S(2)}) %collective-permute-start.6) | collective-permute-done | bytes 131104 | tf_op jit(solution)/shard_map/ppermute | solution.py:176
  20.4 1.6 %collective-permute-start.10 = (bf16[128,512]{1,0:T(8,128)(2,1)S(1)}, bf16[128,512]{1,0:T(8,128)(2,1)S(1)}, u32[]{:S(2)}, u32[]{:S(2)}) collective-permute-start(bf16[128,512]{1,0:T(8,128)(2,1)S(1)} %add_convert_fusion.3), channel_id=1, source_target_pairs={{0,2},{1,3},{2,0},{3,1},{4,6},{5,7},{6,4},{7,5},{8,10},{9,11},{10,... | collective-permute-start | bytes 393224 | tf_op jit(solution)/shard_map/ppermute | solution.py:176
  22.1 0.0 collective-permute-done.4
  22.2 1.6 %collective-permute-start.7 = (bf16[256,256]{1,0:T(8,128)(2,1)S(1)}, bf16[256,256]{1,0:T(8,128)(2,1)S(1)}, u32[]{:S(2)}, u32[]{:S(2)}) collective-permute-start(bf16[256,256]{1,0:T(8,128)(2,1)S(1)} %pad_maximum_fusion.3), channel_id=1, source_target_pairs={{0,1},{1,0},{2,3},{3,2},{4,5},{5,4},{6,7},{7,6},{8,9},{9,8},{10,11... | collective-permute-start | bytes 393224 | tf_op jit(solution)/shard_map/ppermute | solution.py:176
  23.8 0.6 %collective-permute-start.13 = (bf16[256,256]{1,0:T(8,128)(2,1)S(1)}, bf16[256,256]{1,0:T(8,128)(2,1)S(1)}, u32[]{:S(2)}, u32[]{:S(2)}) collective-permute-start(bf16[256,256]{1,0:T(8,128)(2,1)S(1)} %slice.116), channel_id=1, source_target_pairs={{0,16},{1,17},{2,18},{3,19},{4,20},{5,21},{6,22},{7,23},{8,24},{9,... | collective-permute-start | bytes 393224 | tf_op jit(solution)/shard_map/ppermute | solution.py:176
  24.4 0.0 collective-permute-done.9
  24.4 0.0 collective-permute-done.8
  24.4 1.1 %collective-permute-done.10 = bf16[128,512]{1,0:T(8,128)(2,1)S(1)} collective-permute-done((bf16[128,512]{1,0:T(8,128)(2,1)S(1)}, bf16[128,512]{1,0:T(8,128)(2,1)S(1)}, u32[]{:S(2)}, u32[]{:S(2)}) %collective-permute-start.10) | collective-permute-done | bytes 131104 | tf_op jit(solution)/shard_map/ppermute | solution.py:176
  25.5 0.1 add_convert_fusion.1
  25.5 2.7 %collective-permute-start.14 = (bf16[128,512]{1,0:T(8,128)(2,1)S(1)}, bf16[128,512]{1,0:T(8,128)(2,1)S(1)}, u32[]{:S(2)}, u32[]{:S(2)}) collective-permute-start(bf16[128,512]{1,0:T(8,128)(2,1)S(1)} %add_convert_fusion.1), channel_id=1, source_target_pairs={{0,4},{1,5},{2,6},{3,7},{4,0},{5,1},{6,2},{7,3},{8,12},{9,13},{10,... | collective-permute-start | bytes 393224 | tf_op jit(solution)/shard_map/ppermute | solution.py:176
  28.2 0.0 collective-permute-done.7
  28.2 1.6 %collective-permute-start.11 = (bf16[128,512]{1,0:T(8,128)(2,1)S(1)}, bf16[128,512]{1,0:T(8,128)(2,1)S(1)}, u32[]{:S(2)}, u32[]{:S(2)}) collective-permute-start(bf16[128,512]{1,0:T(8,128)(2,1)S(1)} %partial_sums.12), channel_id=1, source_target_pairs={{0,2},{1,3},{2,0},{3,1},{4,6},{5,7},{6,4},{7,5},{8,10},{9,11},{10,... | collective-permute-start | bytes 393224 | tf_op jit(solution)/shard_map/ppermute | solution.py:176
  29.8 2.0 %collective-permute-start.15 = (bf16[128,256]{1,0:T(8,128)(2,1)S(1)}, bf16[128,256]{1,0:T(8,128)(2,1)S(1)}, u32[]{:S(2)}, u32[]{:S(2)}) collective-permute-start(bf16[128,256]{1,0:T(8,128)(2,1)S(1)} %fusion), channel_id=1, source_target_pairs={{0,16},{1,17},{2,18},{3,19},{4,20},{5,21},{6,22},{7,23},{8,24},{9,... | collective-permute-start | bytes 196616 | tf_op jit(solution)/shard_map/ppermute | solution.py:176
  31.8 0.1 collective-permute-start.16
  32.0 1.5 %collective-permute-done.11 = bf16[128,512]{1,0:T(8,128)(2,1)S(1)} collective-permute-done((bf16[128,512]{1,0:T(8,128)(2,1)S(1)}, bf16[128,512]{1,0:T(8,128)(2,1)S(1)}, u32[]{:S(2)}, u32[]{:S(2)}) %collective-permute-start.11) | collective-permute-done | bytes 131104 | tf_op jit(solution)/shard_map/ppermute | solution.py:176
  33.6 2.6 %collective-permute-done.16 = bf16[128,256]{1,0:T(8,128)(2,1)S(1)} collective-permute-done((bf16[128,256]{1,0:T(8,128)(2,1)S(1)}, bf16[128,256]{1,0:T(8,128)(2,1)S(1)}, u32[]{:S(2)}, u32[]{:S(2)}) %collective-permute-start.16) | collective-permute-done | bytes 65568 | tf_op jit(solution)/shard_map/ppermute | solution.py:176
  36.2 0.0 collective-permute-done.15
  36.2 0.6 %collective-permute-start.17 = (bf16[128,512]{1,0:T(8,128)(2,1)S(1)}, bf16[128,512]{1,0:T(8,128)(2,1)S(1)}, u32[]{:S(2)}, u32[]{:S(2)}) collective-permute-start(bf16[128,512]{1,0:T(8,128)(2,1)S(1)} %add_convert_fusion), channel_id=1, source_target_pairs={{0,16},{1,17},{2,18},{3,19},{4,20},{5,21},{6,22},{7,23},{8,24},{9,... | collective-permute-start | bytes 393224 | tf_op jit(solution)/shard_map/ppermute | solution.py:176
  36.8 0.9 %outer_swap.1 = bf16[256,512]{1,0:T(8,128)(2,1)} custom-call(bf16[272,512]{1,0:T(8,128)(2,1)S(1)} %front.1.v0_ref, bf16[256,512]{1,0:T(8,128)(2,1)S(1)} %get-tuple-element.48.rows_ref, bf16[32,512]{1,0:T(8,128)(2,1)S(1)} %slice.93.window_ref), custom_call_target="tpu_custom_call" | custom-call | tf_op jit(solution)/shard_map/outer_swap/pallas_call | solution.py:265
  37.7 3.6 %collective-permute-done.17 = bf16[128,512]{1,0:T(8,128)(2,1)S(1)} collective-permute-done((bf16[128,512]{1,0:T(8,128)(2,1)S(1)}, bf16[128,512]{1,0:T(8,128)(2,1)S(1)}, u32[]{:S(2)}, u32[]{:S(2)}) %collective-permute-start.17) | collective-permute-done | bytes 131104 | tf_op jit(solution)/shard_map/ppermute | solution.py:176
  41.3 0.1 collective-permute-start.18
  41.3 0.8 %place.2.rest_0_ = f32[512,512]{1,0:T(8,128)} custom-call(bf16[2,128,512]{2,1,0:T(8,128)(2,1)S(1)} %pad_maximum_fusion.1.pair_ref), custom_call_target="tpu_custom_call" | custom-call | tf_op jit(solution)/shard_map/place/pallas_call | solution.py:289
  42.2 0.7 %collective-permute-done.18.pair_ref = bf16[2,128,512]{2,1,0:T(8,128)(2,1)S(1)} collective-permute-done((bf16[2,128,512]{2,1,0:T(8,128)(2,1)S(1)}, bf16[2,128,512]{2,1,0:T(8,128)(2,1)S(1)}, u32[]{:S(2)}, u32[]{:S(2)}) %collective-permute-start.18) | collective-permute-done | bytes 262176 | tf_op jit(solution)/shard_map/ppermute | solution.py:176
  42.9 0.8 %place.3 = f32[512,512]{1,0:T(8,128)} custom-call(bf16[2,128,512]{2,1,0:T(8,128)(2,1)S(1)} %collective-permute-done.18.pair_ref, f32[512,512]{1,0:T(8,128)} %place.2.rest_0_), custom_call_target="tpu_custom_call", output_to_operand_aliasing={{}: (1, {})} | custom-call | tf_op jit(solution)/shard_map/place/pallas_call | solution.py:289
  (22 shorter events, 0.4 us)
Async XLA Ops:
  0.6 5.6 %copy-start = (bf16[256,4096]{1,0:T(8,128)(2,1)S(1)}, bf16[256,4096]{1,0:T(8,128)(2,1)}, u32[]{:S(2)}) copy-start(bf16[256,4096]{1,0:T(8,128)(2,1)} %own_ref.13) | copy-start | bytes 6291460
  0.6 5.5 %collective-permute-start = (bf16[256,4096]{1,0:T(8,128)(2,1)}, bf16[256,4096]{1,0:T(8,128)(2,1)S(1)}, u32[]{:S(2)}, u32[]{:S(2)}) collective-permute-start(bf16[256,4096]{1,0:T(8,128)(2,1)} %own_ref.13), channel_id=1, source_target_pairs={{0,8},{1,9},{2,10},{3,11},{4,12},{5,13},{6,14},{7,15},{8,0},{9,1},... | collective-permute-start | bytes 6291464 | tf_op jit(solution)/shard_map/ppermute | solution.py:176
  4.6 1.6 %collective-permute-start.1 = (bf16[272,512]{1,0:T(8,128)(2,1)S(1)}, bf16[272,512]{1,0:T(8,128)(2,1)S(1)}, u32[]{:S(2)}, u32[]{:S(2)}) collective-permute-start(bf16[272,512]{1,0:T(8,128)(2,1)S(1)} %front.1.v0_ref), channel_id=1, source_target_pairs={{0,8},{1,9},{2,10},{3,11},{4,12},{5,13},{6,14},{7,15},{8,0},{9,1},... | collective-permute-start | bytes 835592 | tf_op jit(solution)/shard_map/ppermute | solution.py:176
  6.5 8.4 %collective-permute-start.2 = (bf16[128,512]{1,0:T(8,128)(2,1)S(1)}, bf16[128,512]{1,0:T(8,128)(2,1)S(1)}, u32[]{:S(2)}, u32[]{:S(2)}) collective-permute-start(bf16[128,512]{1,0:T(8,128)(2,1)S(1)} %partial_sums.8), channel_id=1, source_target_pairs={{0,1},{1,0},{2,3},{3,2},{4,5},{5,4},{6,7},{7,6},{8,9},{9,8},{10,11... | collective-permute-start | bytes 393224 | tf_op jit(solution)/shard_map/ppermute | solution.py:176
  9.3 5.6 %collective-permute-start.3 = (bf16[128,512]{1,0:T(8,128)(2,1)S(1)}, bf16[128,512]{1,0:T(8,128)(2,1)S(1)}, u32[]{:S(2)}, u32[]{:S(2)}) collective-permute-start(bf16[128,512]{1,0:T(8,128)(2,1)S(1)} %partial_sums.9), channel_id=1, source_target_pairs={{0,16},{1,17},{2,18},{3,19},{4,20},{5,21},{6,22},{7,23},{8,24},{9,... | collective-permute-start | bytes 393224 | tf_op jit(solution)/shard_map/ppermute | solution.py:176
  11.3 10.7 %collective-permute-start.4 = (bf16[384,256]{1,0:T(8,128)(2,1)S(1)}, bf16[384,256]{1,0:T(8,128)(2,1)S(1)}, u32[]{:S(2)}, u32[]{:S(2)}) collective-permute-start(bf16[384,256]{1,0:T(8,128)(2,1)S(1)} %get-tuple-element.32), channel_id=1, source_target_pairs={{0,2},{1,3},{2,0},{3,1},{4,6},{5,7},{6,4},{7,5},{8,10},{9,11},{10,... | collective-permute-start | bytes 589832 | tf_op jit(solution)/shard_map/ppermute | solution.py:176
  13.0 5.3 %collective-permute-start.5 = (bf16[128,512]{1,0:T(8,128)(2,1)S(1)}, bf16[128,512]{1,0:T(8,128)(2,1)S(1)}, u32[]{:S(2)}, u32[]{:S(2)}) collective-permute-start(bf16[128,512]{1,0:T(8,128)(2,1)S(1)} %get-tuple-element.33), channel_id=1, source_target_pairs={{0,1},{1,0},{2,3},{3,2},{4,5},{5,4},{6,7},{7,6},{8,9},{9,8},{10,11... | collective-permute-start | bytes 393224 | tf_op jit(solution)/shard_map/ppermute | solution.py:176
  13.9 9.8 %collective-permute-start.12 = (bf16[384,256]{1,0:T(8,128)(2,1)S(1)}, bf16[384,256]{1,0:T(8,128)(2,1)S(1)}, u32[]{:S(2)}, u32[]{:S(2)}) collective-permute-start(bf16[384,256]{1,0:T(8,128)(2,1)S(1)} %get-tuple-element.43), channel_id=1, source_target_pairs={{0,2},{1,3},{2,0},{3,1},{4,6},{5,7},{6,4},{7,5},{8,10},{9,11},{10,... | collective-permute-start | bytes 589832 | tf_op jit(solution)/shard_map/ppermute | solution.py:176
  15.0 5.4 %collective-permute-start.6 = (bf16[128,512]{1,0:T(8,128)(2,1)S(1)}, bf16[128,512]{1,0:T(8,128)(2,1)S(1)}, u32[]{:S(2)}, u32[]{:S(2)}) collective-permute-start(bf16[128,512]{1,0:T(8,128)(2,1)S(1)} %add_convert_fusion.4), channel_id=1, source_target_pairs={{0,16},{1,17},{2,18},{3,19},{4,20},{5,21},{6,22},{7,23},{8,24},{9,... | collective-permute-start | bytes 393224 | tf_op jit(solution)/shard_map/ppermute | solution.py:176
  16.5 7.9 %collective-permute-start.9 = (bf16[128,512]{1,0:T(8,128)(2,1)S(1)}, bf16[128,512]{1,0:T(8,128)(2,1)S(1)}, u32[]{:S(2)}, u32[]{:S(2)}) collective-permute-start(bf16[128,512]{1,0:T(8,128)(2,1)S(1)} %add_convert_fusion.2), channel_id=1, source_target_pairs={{0,1},{1,0},{2,3},{3,2},{4,5},{5,4},{6,7},{7,6},{8,9},{9,8},{10,11... | collective-permute-start | bytes 393224 | tf_op jit(solution)/shard_map/ppermute | solution.py:176
  18.3 6.1 %collective-permute-start.8 = (bf16[160,512]{1,0:T(8,128)(2,1)S(1)}, bf16[160,512]{1,0:T(8,128)(2,1)S(1)}, u32[]{:S(2)}, u32[]{:S(2)}) collective-permute-start(bf16[160,512]{1,0:T(8,128)(2,1)S(1)} %pad_maximum_fusion.2), channel_id=1, source_target_pairs={{0,16},{1,17},{2,18},{3,19},{4,20},{5,21},{6,22},{7,23},{8,24},{9,... | collective-permute-start | bytes 491528 | tf_op jit(solution)/shard_map/ppermute | solution.py:176
  20.4 5.0 %collective-permute-start.10 = (bf16[128,512]{1,0:T(8,128)(2,1)S(1)}, bf16[128,512]{1,0:T(8,128)(2,1)S(1)}, u32[]{:S(2)}, u32[]{:S(2)}) collective-permute-start(bf16[128,512]{1,0:T(8,128)(2,1)S(1)} %add_convert_fusion.3), channel_id=1, source_target_pairs={{0,2},{1,3},{2,0},{3,1},{4,6},{5,7},{6,4},{7,5},{8,10},{9,11},{10,... | collective-permute-start | bytes 393224 | tf_op jit(solution)/shard_map/ppermute | solution.py:176
  22.2 6.0 %collective-permute-start.7 = (bf16[256,256]{1,0:T(8,128)(2,1)S(1)}, bf16[256,256]{1,0:T(8,128)(2,1)S(1)}, u32[]{:S(2)}, u32[]{:S(2)}) collective-permute-start(bf16[256,256]{1,0:T(8,128)(2,1)S(1)} %pad_maximum_fusion.3), channel_id=1, source_target_pairs={{0,1},{1,0},{2,3},{3,2},{4,5},{5,4},{6,7},{7,6},{8,9},{9,8},{10,11... | collective-permute-start | bytes 393224 | tf_op jit(solution)/shard_map/ppermute | solution.py:176
  23.8 8.0 %collective-permute-start.13 = (bf16[256,256]{1,0:T(8,128)(2,1)S(1)}, bf16[256,256]{1,0:T(8,128)(2,1)S(1)}, u32[]{:S(2)}, u32[]{:S(2)}) collective-permute-start(bf16[256,256]{1,0:T(8,128)(2,1)S(1)} %slice.116), channel_id=1, source_target_pairs={{0,16},{1,17},{2,18},{3,19},{4,20},{5,21},{6,22},{7,23},{8,24},{9,... | collective-permute-start | bytes 393224 | tf_op jit(solution)/shard_map/ppermute | solution.py:176
  25.5 8.0 %collective-permute-start.14 = (bf16[128,512]{1,0:T(8,128)(2,1)S(1)}, bf16[128,512]{1,0:T(8,128)(2,1)S(1)}, u32[]{:S(2)}, u32[]{:S(2)}) collective-permute-start(bf16[128,512]{1,0:T(8,128)(2,1)S(1)} %add_convert_fusion.1), channel_id=1, source_target_pairs={{0,4},{1,5},{2,6},{3,7},{4,0},{5,1},{6,2},{7,3},{8,12},{9,13},{10,... | collective-permute-start | bytes 393224 | tf_op jit(solution)/shard_map/ppermute | solution.py:176
  28.2 5.3 %collective-permute-start.11 = (bf16[128,512]{1,0:T(8,128)(2,1)S(1)}, bf16[128,512]{1,0:T(8,128)(2,1)S(1)}, u32[]{:S(2)}, u32[]{:S(2)}) collective-permute-start(bf16[128,512]{1,0:T(8,128)(2,1)S(1)} %partial_sums.12), channel_id=1, source_target_pairs={{0,2},{1,3},{2,0},{3,1},{4,6},{5,7},{6,4},{7,5},{8,10},{9,11},{10,... | collective-permute-start | bytes 393224 | tf_op jit(solution)/shard_map/ppermute | solution.py:176
  29.8 6.4 %collective-permute-start.15 = (bf16[128,256]{1,0:T(8,128)(2,1)S(1)}, bf16[128,256]{1,0:T(8,128)(2,1)S(1)}, u32[]{:S(2)}, u32[]{:S(2)}) collective-permute-start(bf16[128,256]{1,0:T(8,128)(2,1)S(1)} %fusion), channel_id=1, source_target_pairs={{0,16},{1,17},{2,18},{3,19},{4,20},{5,21},{6,22},{7,23},{8,24},{9,... | collective-permute-start | bytes 196616 | tf_op jit(solution)/shard_map/ppermute | solution.py:176
  31.8 4.3 %collective-permute-start.16 = (bf16[128,256]{1,0:T(8,128)(2,1)S(1)}, bf16[128,256]{1,0:T(8,128)(2,1)S(1)}, u32[]{:S(2)}, u32[]{:S(2)}) collective-permute-start(bf16[128,256]{1,0:T(8,128)(2,1)S(1)} %fusion.1), channel_id=1, source_target_pairs={{0,1},{1,0},{2,3},{3,2},{4,5},{5,4},{6,7},{7,6},{8,9},{9,8},{10,11... | collective-permute-start | bytes 196616 | tf_op jit(solution)/shard_map/ppermute | solution.py:176
  36.2 5.0 %collective-permute-start.17 = (bf16[128,512]{1,0:T(8,128)(2,1)S(1)}, bf16[128,512]{1,0:T(8,128)(2,1)S(1)}, u32[]{:S(2)}, u32[]{:S(2)}) collective-permute-start(bf16[128,512]{1,0:T(8,128)(2,1)S(1)} %add_convert_fusion), channel_id=1, source_target_pairs={{0,16},{1,17},{2,18},{3,19},{4,20},{5,21},{6,22},{7,23},{8,24},{9,... | collective-permute-start | bytes 393224 | tf_op jit(solution)/shard_map/ppermute | solution.py:176
  41.3 1.6 %collective-permute-start.18 = (bf16[2,128,512]{2,1,0:T(8,128)(2,1)S(1)}, bf16[2,128,512]{2,1,0:T(8,128)(2,1)S(1)}, u32[]{:S(2)}, u32[]{:S(2)}) collective-permute-start(bf16[2,128,512]{2,1,0:T(8,128)(2,1)S(1)} %pad_maximum_fusion.1.pair_ref), channel_id=1, source_target_pairs={{0,8},{1,9},{2,10},{3,11},{4,12},{5,13},{6,14},{7,15},{8,0},{9,1},... | collective-permute-start | bytes 786440 | tf_op jit(solution)/shard_map/ppermute | solution.py:176

commit v22 on v21

--- a/solution.py
+++ b/solution.py
@@ -356,8 +356,9 @@
     z3 = add(keep_b[LANE:], side_b, on_b).astype(BF16)
     side_a = xor_permute(after_all(jnp.concatenate([side_a, window]), own_some)[0], Y)
     side_a, window = side_a[:LANE], side_a[LANE:]
-    pair_some = after_all(pair_some, z3)[0]
+    pair_some, pair_own = after_all(pair_some, pair_own, z3)[:2]
     z3 = xor_permute(z3, Z1)
+    pair_own = xor_permute(pair_own, Z1)
     z2 = add(keep_a[LANE:], side_a, on_a, z3).astype(BF16)
 
     some = add(own_some[:3 * LANE], pair_some)
@@ -365,14 +366,12 @@
     some_in = xor_permute(jnp.concatenate([some_far, some_x]).astype(BF16), X)
     rest = add(own_rest[:3 * LANE], after_all(pair_rest, some)[0])
     rest_in = xor_permute(rest[:2 * LANE].astype(BF16), Y)
-    some_in, pair_own = after_all(some_in, pair_own, z2)[:2]
+    some_in = after_all(some_in, z2)[0]
     z2 = xor_permute(z2, Z2)
-    pair_own = xor_permute(pair_own, Z1)
     some_on = add(some_y, some_in[:LANE]).astype(BF16)
     rest_in = after_all(rest_in, some_on)[0]
     some_on = xor_permute(some_on, Y)
     rest_on = add(rest[2 * LANE:], rest_in[:LANE]).astype(BF16)
-    pair_own = after_all(pair_own, rest_on)[0]
     rest_on = xor_permute(rest_on, X)
     base = jnp.concatenate([
         add(own_some[3 * LANE:], pair_own[:, :256], some_in[LANE:]),

time: 43.9 us -> 43.4 us (0.989)
  starting transfers between devices: 22.1 us -> 20.9 us
  waiting for transfers between devices: 11.5 us -> 12.3 us
    ppermute x19, starting transfers between devices: 22.1 us -> 20.9 us  [xor_permute(): lax.ppermute(value, ('dp', 'fsdp'), [(i, i ^ mask) for i in range(count)])]
    ppermute x19, waiting for transfers between devices: 11.5 us -> 12.3 us  [xor_permute(): lax.ppermute(value, ('dp', 'fsdp'), [(i, i ^ mask) for i in range(count)])]
  transfers between devices with their start and end apart: 19 -> 19, of which waited for: 7 -> 9; matrix products, arithmetic and copies ran while one was open for 1% -> 1% of each run, Pallas kernels for 16% -> 16%
where the time goes in v22:
time: 43.4 us; the launch traced here: 43.3 us
  starting transfers between devices  20.9 us (48%)
  waiting for transfers between devices  12.3 us (28%)
  Pallas kernels  8.1 us (19%)
  between operations  1.58 us (4%)
    ppermute x19, starting transfers between devices, xor_permute(): lax.ppermute(value, ('dp', 'fsdp'), [(i, i ^ mask) for i in range(count)])  20.9 us
    ppermute x19, waiting for transfers between devices, xor_permute(): lax.ppermute(value, ('dp', 'fsdp'), [(i, i ^ mask) for i in range(count)])  12.3 us
    pallas_call x1, Pallas kernels, front(): pl.pallas_call(functools.partial(front_kernel, per_group), in_specs=[HBM]...  2.64 us
    pallas_call x7, Pallas kernels, partial_sums(): pl.pallas_call(functools.partial(partial_kernel, parts), in_specs=[VMEM]...  2.55 us
    pallas_call x2, Pallas kernels, place(): pl.pallas_call(functools.partial(place_kernel, core), in_specs=[VMEM] + [...  1.65 us
    pallas_call x1, Pallas kernels, outer_swap(): pl.pallas_call(outer_swap_kernel, in_specs=[VMEM] * 3, out_specs=VMEM, ou...  0.91 us
  transfers between devices with their start and end apart: 19, of which 9 were waited for; matrix products, arithmetic and copies ran while one was open for 1% of the time, Pallas kernels for 16%

profile of v22, /device:TPU:0, one launch (start us, length us, event | category | flops | bytes accessed | tf_op | source)
XLA Modules:
  0.0 43.3 jit_solution(6766756853534167323)
XLA Ops:
  0.6 0.5 %collective-permute-start = (bf16[256,4096]{1,0:T(8,128)(2,1)}, bf16[256,4096]{1,0:T(8,128)(2,1)S(1)}, u32[]{:S(2)}, u32[]{:S(2)}) collective-permute-start(bf16[256,4096]{1,0:T(8,128)(2,1)} %own_ref.13), channel_id=1, source_target_pairs={{0,8},{1,9},{2,10},{3,11},{4,12},{5,13},{6,14},{7,15},{8,0},{9,1},... | collective-permute-start | bytes 6291464 | tf_op jit(solution)/shard_map/ppermute | solution.py:176
  1.9 2.6 %front.1.v0_ref = bf16[272,512]{1,0:T(8,128)(2,1)S(1)} custom-call(f32[16]{0:T(128)} %loss_hbm.1, s32[1]{0:T(128)S(6)} %copy.14.exponent_hbm, s32[1,2]{1,0:T(1,128)} %start_hbm.1, s32[1,2]{1,0:T(1,128)} %rows_hbm.1, bf16[256,2048]{1,0:T(8,128)(2,1)} %q_hbm.1, bf16[256,512]{1,0:T(8,128)(2,1)} %k_hbm.1, bf16[256,2048]{1,0:T(8,128)(2,1)} %g_hbm.1, ...), custom_call_target="tpu_custom_call" | custom-call | tf_op jit(solution)/shard_map/front/pallas_call | solution.py:153
  4.6 0.1 collective-permute-start.1
  4.7 1.5 %collective-permute-done.1.v1_ref = bf16[272,512]{1,0:T(8,128)(2,1)S(1)} collective-permute-done((bf16[272,512]{1,0:T(8,128)(2,1)S(1)}, bf16[272,512]{1,0:T(8,128)(2,1)S(1)}, u32[]{:S(2)}, u32[]{:S(2)}) %collective-permute-start.1) | collective-permute-done | bytes 278560 | tf_op jit(solution)/shard_map/ppermute | solution.py:176
  6.2 0.0 collective-permute-done.near_ref
  6.2 0.3 partial_sums.8
  6.5 2.6 %collective-permute-start.2 = (bf16[128,512]{1,0:T(8,128)(2,1)S(1)}, bf16[128,512]{1,0:T(8,128)(2,1)S(1)}, u32[]{:S(2)}, u32[]{:S(2)}) collective-permute-start(bf16[128,512]{1,0:T(8,128)(2,1)S(1)} %partial_sums.8), channel_id=1, source_target_pairs={{0,1},{1,0},{2,3},{3,2},{4,5},{5,4},{6,7},{7,6},{8,9},{9,8},{10,11... | collective-permute-start | bytes 393224 | tf_op jit(solution)/shard_map/ppermute | solution.py:176
  9.1 0.3 partial_sums.9
  9.3 1.6 %collective-permute-start.3 = (bf16[128,512]{1,0:T(8,128)(2,1)S(1)}, bf16[128,512]{1,0:T(8,128)(2,1)S(1)}, u32[]{:S(2)}, u32[]{:S(2)}) collective-permute-start(bf16[128,512]{1,0:T(8,128)(2,1)S(1)} %partial_sums.9), channel_id=1, source_target_pairs={{0,16},{1,17},{2,18},{3,19},{4,20},{5,21},{6,22},{7,23},{8,24},{9,... | collective-permute-start | bytes 393224 | tf_op jit(solution)/shard_map/ppermute | solution.py:176
  10.9 0.4 partial_sums.11
  11.3 1.6 %collective-permute-start.4 = (bf16[384,256]{1,0:T(8,128)(2,1)S(1)}, bf16[384,256]{1,0:T(8,128)(2,1)S(1)}, u32[]{:S(2)}, u32[]{:S(2)}) collective-permute-start(bf16[384,256]{1,0:T(8,128)(2,1)S(1)} %get-tuple-element.31), channel_id=1, source_target_pairs={{0,2},{1,3},{2,0},{3,1},{4,6},{5,7},{6,4},{7,5},{8,10},{9,11},{10,... | collective-permute-start | bytes 589832 | tf_op jit(solution)/shard_map/ppermute | solution.py:176
  13.0 0.4 partial_sums.13
  13.4 0.5 %collective-permute-start.12 = (bf16[384,256]{1,0:T(8,128)(2,1)S(1)}, bf16[384,256]{1,0:T(8,128)(2,1)S(1)}, u32[]{:S(2)}, u32[]{:S(2)}) collective-permute-start(bf16[384,256]{1,0:T(8,128)(2,1)S(1)} %get-tuple-element.43), channel_id=1, source_target_pairs={{0,2},{1,3},{2,0},{3,1},{4,6},{5,7},{6,4},{7,5},{8,10},{9,11},{10,... | collective-permute-start | bytes 589832 | tf_op jit(solution)/shard_map/ppermute | solution.py:176
  13.9 0.5 %collective-permute-start.5 = (bf16[128,512]{1,0:T(8,128)(2,1)S(1)}, bf16[128,512]{1,0:T(8,128)(2,1)S(1)}, u32[]{:S(2)}, u32[]{:S(2)}) collective-permute-start(bf16[128,512]{1,0:T(8,128)(2,1)S(1)} %get-tuple-element.32), channel_id=1, source_target_pairs={{0,1},{1,0},{2,3},{3,2},{4,5},{5,4},{6,7},{7,6},{8,9},{9,8},{10,11... | collective-permute-start | bytes 393224 | tf_op jit(solution)/shard_map/ppermute | solution.py:176
  14.4 0.5 %partial_sums.7 = (f32[256,512]{1,0:T(8,128)S(1)}, f32[256,512]{1,0:T(8,128)S(1)}) custom-call(bf16[256,4096]{1,0:T(8,128)(2,1)S(1)} %copy-done, bf16[256,4096]{1,0:T(8,128)(2,1)S(1)} %collective-permute-done.near_ref, bf16[272,512]{1,0:T(8,128)(2,1)S(1)} %front.1.v0_ref, bf16[272,512]{1,0:T(8,128)(2,1)S(1)} %collective-permute-done.1.v1_ref), custom_call_target="tpu_custom_call" | custom-call | tf_op jit(solution)/shard_map/partial_sums/pallas_call | solution.py:201
  14.9 0.0 collective-permute-done.2
  14.9 0.0 collective-permute-done.3
  15.0 1.5 %collective-permute-start.6 = (bf16[128,512]{1,0:T(8,128)(2,1)S(1)}, bf16[128,512]{1,0:T(8,128)(2,1)S(1)}, u32[]{:S(2)}, u32[]{:S(2)}) collective-permute-start(bf16[128,512]{1,0:T(8,128)(2,1)S(1)} %add_convert_fusion.4), channel_id=1, source_target_pairs={{0,16},{1,17},{2,18},{3,19},{4,20},{5,21},{6,22},{7,23},{8,24},{9,... | collective-permute-start | bytes 393224 | tf_op jit(solution)/shard_map/ppermute | solution.py:176
  16.5 0.6 %collective-permute-start.10 = (bf16[128,512]{1,0:T(8,128)(2,1)S(1)}, bf16[128,512]{1,0:T(8,128)(2,1)S(1)}, u32[]{:S(2)}, u32[]{:S(2)}) collective-permute-start(bf16[128,512]{1,0:T(8,128)(2,1)S(1)} %add_convert_fusion.2), channel_id=1, source_target_pairs={{0,1},{1,0},{2,3},{3,2},{4,5},{5,4},{6,7},{7,6},{8,9},{9,8},{10,11... | collective-permute-start | bytes 393224 | tf_op jit(solution)/shard_map/ppermute | solution.py:176
  17.1 0.5 %partial_sums.10 = (f32[512,256]{1,0:T(8,128)S(1)}, f32[512,256]{1,0:T(8,128)S(1)}) custom-call(bf16[256,4096]{1,0:T(8,128)(2,1)S(1)} %copy-done, bf16[256,4096]{1,0:T(8,128)(2,1)S(1)} %collective-permute-done.near_ref, bf16[272,512]{1,0:T(8,128)(2,1)S(1)} %front.1.v0_ref, bf16[272,512]{1,0:T(8,128)(2,1)S(1)} %collective-permute-done.1.v1_ref), custom_call_target="tpu_custom_call" | custom-call | tf_op jit(solution)/shard_map/partial_sums/pallas_call | solution.py:201
  17.6 0.3 inner_swap.1
  18.0 0.3 partial_sums.12
  18.2 1.4 %collective-permute-done.5 = bf16[128,512]{1,0:T(8,128)(2,1)S(1)} collective-permute-done((bf16[128,512]{1,0:T(8,128)(2,1)S(1)}, bf16[128,512]{1,0:T(8,128)(2,1)S(1)}, u32[]{:S(2)}, u32[]{:S(2)}) %collective-permute-start.5) | collective-permute-done | bytes 131104 | tf_op jit(solution)/shard_map/ppermute | solution.py:176
  19.6 0.5 %collective-permute-start.9 = (bf16[160,512]{1,0:T(8,128)(2,1)S(1)}, bf16[160,512]{1,0:T(8,128)(2,1)S(1)}, u32[]{:S(2)}, u32[]{:S(2)}) collective-permute-start(bf16[160,512]{1,0:T(8,128)(2,1)S(1)} %pad_maximum_fusion.2), channel_id=1, source_target_pairs={{0,16},{1,17},{2,18},{3,19},{4,20},{5,21},{6,22},{7,23},{8,24},{9,... | collective-permute-start | bytes 491528 | tf_op jit(solution)/shard_map/ppermute | solution.py:176
  20.1 0.0 collective-permute-done.6
  20.2 1.7 %collective-permute-start.11 = (bf16[128,512]{1,0:T(8,128)(2,1)S(1)}, bf16[128,512]{1,0:T(8,128)(2,1)S(1)}, u32[]{:S(2)}, u32[]{:S(2)}) collective-permute-start(bf16[128,512]{1,0:T(8,128)(2,1)S(1)} %add_convert_fusion.3), channel_id=1, source_target_pairs={{0,2},{1,3},{2,0},{3,1},{4,6},{5,7},{6,4},{7,5},{8,10},{9,11},{10,... | collective-permute-start | bytes 393224 | tf_op jit(solution)/shard_map/ppermute | solution.py:176
  21.8 0.0 collective-permute-done.4
  21.9 1.4 %collective-permute-done.12 = bf16[384,256]{1,0:T(8,128)(2,1)S(1)} collective-permute-done((bf16[384,256]{1,0:T(8,128)(2,1)S(1)}, bf16[384,256]{1,0:T(8,128)(2,1)S(1)}, u32[]{:S(2)}, u32[]{:S(2)}) %collective-permute-start.12) | collective-permute-done | bytes 196640 | tf_op jit(solution)/shard_map/ppermute | solution.py:176
  23.3 0.7 %collective-permute-start.13 = (bf16[256,256]{1,0:T(8,128)(2,1)S(1)}, bf16[256,256]{1,0:T(8,128)(2,1)S(1)}, u32[]{:S(2)}, u32[]{:S(2)}) collective-permute-start(bf16[256,256]{1,0:T(8,128)(2,1)S(1)} %slice.118), channel_id=1, source_target_pairs={{0,16},{1,17},{2,18},{3,19},{4,20},{5,21},{6,22},{7,23},{8,24},{9,... | collective-permute-start | bytes 393224 | tf_op jit(solution)/shard_map/ppermute | solution.py:176
  24.1 0.3 collective-permute-start.8
  24.4 0.0 collective-permute-done.10
  24.4 0.8 %collective-permute-start.7 = (bf16[128,512]{1,0:T(8,128)(2,1)S(1)}, bf16[128,512]{1,0:T(8,128)(2,1)S(1)}, u32[]{:S(2)}, u32[]{:S(2)}) collective-permute-start(bf16[128,512]{1,0:T(8,128)(2,1)S(1)} %partial_sums.12), channel_id=1, source_target_pairs={{0,2},{1,3},{2,0},{3,1},{4,6},{5,7},{6,4},{7,5},{8,10},{9,11},{10,... | collective-permute-start | bytes 393224 | tf_op jit(solution)/shard_map/ppermute | solution.py:176
  25.2 0.9 %collective-permute-done.9 = bf16[160,512]{1,0:T(8,128)(2,1)S(1)} collective-permute-done((bf16[160,512]{1,0:T(8,128)(2,1)S(1)}, bf16[160,512]{1,0:T(8,128)(2,1)S(1)}, u32[]{:S(2)}, u32[]{:S(2)}) %collective-permute-start.9) | collective-permute-done | bytes 163872 | tf_op jit(solution)/shard_map/ppermute | solution.py:176
  26.1 0.0 collective-permute-done.11
  26.1 0.1 add_convert_fusion.1
  26.1 2.6 %collective-permute-start.14 = (bf16[128,512]{1,0:T(8,128)(2,1)S(1)}, bf16[128,512]{1,0:T(8,128)(2,1)S(1)}, u32[]{:S(2)}, u32[]{:S(2)}) collective-permute-start(bf16[128,512]{1,0:T(8,128)(2,1)S(1)} %add_convert_fusion.1), channel_id=1, source_target_pairs={{0,4},{1,5},{2,6},{3,7},{4,0},{5,1},{6,2},{7,3},{8,12},{9,13},{10,... | collective-permute-start | bytes 393224 | tf_op jit(solution)/shard_map/ppermute | solution.py:176
  28.8 0.4 collective-permute-done.8
  29.1 2.2 %collective-permute-start.15 = (bf16[128,256]{1,0:T(8,128)(2,1)S(1)}, bf16[128,256]{1,0:T(8,128)(2,1)S(1)}, u32[]{:S(2)}, u32[]{:S(2)}) collective-permute-start(bf16[128,256]{1,0:T(8,128)(2,1)S(1)} %fusion.1), channel_id=1, source_target_pairs={{0,16},{1,17},{2,18},{3,19},{4,20},{5,21},{6,22},{7,23},{8,24},{9,... | collective-permute-start | bytes 196616 | tf_op jit(solution)/shard_map/ppermute | solution.py:176
  31.4 0.7 %collective-permute-start.16 = (bf16[128,256]{1,0:T(8,128)(2,1)S(1)}, bf16[128,256]{1,0:T(8,128)(2,1)S(1)}, u32[]{:S(2)}, u32[]{:S(2)}) collective-permute-start(bf16[128,256]{1,0:T(8,128)(2,1)S(1)} %get-tuple-element.56), channel_id=1, source_target_pairs={{0,1},{1,0},{2,3},{3,2},{4,5},{5,4},{6,7},{7,6},{8,9},{9,8},{10,11... | collective-permute-start | bytes 196616 | tf_op jit(solution)/shard_map/ppermute | solution.py:176
  32.1 1.4 %collective-permute-done.14.arrived_ref = bf16[128,512]{1,0:T(8,128)(2,1)S(1)} collective-permute-done((bf16[128,512]{1,0:T(8,128)(2,1)S(1)}, bf16[128,512]{1,0:T(8,128)(2,1)S(1)}, u32[]{:S(2)}, u32[]{:S(2)}) %collective-permute-start.14) | collective-permute-done | bytes 131104 | tf_op jit(solution)/shard_map/ppermute | solution.py:176
  33.5 2.2 %collective-permute-done.16 = bf16[128,256]{1,0:T(8,128)(2,1)S(1)} collective-permute-done((bf16[128,256]{1,0:T(8,128)(2,1)S(1)}, bf16[128,256]{1,0:T(8,128)(2,1)S(1)}, u32[]{:S(2)}, u32[]{:S(2)}) %collective-permute-start.16) | collective-permute-done | bytes 65568 | tf_op jit(solution)/shard_map/ppermute | solution.py:176
  35.8 1.7 %collective-permute-start.17 = (bf16[128,512]{1,0:T(8,128)(2,1)S(1)}, bf16[128,512]{1,0:T(8,128)(2,1)S(1)}, u32[]{:S(2)}, u32[]{:S(2)}) collective-permute-start(bf16[128,512]{1,0:T(8,128)(2,1)S(1)} %add_convert_fusion), channel_id=1, source_target_pairs={{0,16},{1,17},{2,18},{3,19},{4,20},{5,21},{6,22},{7,23},{8,24},{9,... | collective-permute-start | bytes 393224 | tf_op jit(solution)/shard_map/ppermute | solution.py:176
  37.4 0.9 %outer_swap.1 = bf16[256,512]{1,0:T(8,128)(2,1)} custom-call(bf16[272,512]{1,0:T(8,128)(2,1)S(1)} %front.1.v0_ref, bf16[256,512]{1,0:T(8,128)(2,1)S(1)} %get-tuple-element.46.rows_ref, bf16[32,512]{1,0:T(8,128)(2,1)S(1)} %slice.95.window_ref), custom_call_target="tpu_custom_call" | custom-call | tf_op jit(solution)/shard_map/outer_swap/pallas_call | solution.py:265
  38.4 2.4 %collective-permute-done.17 = bf16[128,512]{1,0:T(8,128)(2,1)S(1)} collective-permute-done((bf16[128,512]{1,0:T(8,128)(2,1)S(1)}, bf16[128,512]{1,0:T(8,128)(2,1)S(1)}, u32[]{:S(2)}, u32[]{:S(2)}) %collective-permute-start.17) | collective-permute-done | bytes 131104 | tf_op jit(solution)/shard_map/ppermute | solution.py:176
  40.8 0.1 collective-permute-start.18
  40.9 0.8 %place.2.rest_0_ = f32[512,512]{1,0:T(8,128)} custom-call(bf16[2,128,512]{2,1,0:T(8,128)(2,1)S(1)} %pad_maximum_fusion.1.pair_ref), custom_call_target="tpu_custom_call" | custom-call | tf_op jit(solution)/shard_map/place/pallas_call | solution.py:289
  41.7 0.7 %collective-permute-done.18.pair_ref = bf16[2,128,512]{2,1,0:T(8,128)(2,1)S(1)} collective-permute-done((bf16[2,128,512]{2,1,0:T(8,128)(2,1)S(1)}, bf16[2,128,512]{2,1,0:T(8,128)(2,1)S(1)}, u32[]{:S(2)}, u32[]{:S(2)}) %collective-permute-start.18) | collective-permute-done | bytes 262176 | tf_op jit(solution)/shard_map/ppermute | solution.py:176
  42.4 0.8 %place.3 = f32[512,512]{1,0:T(8,128)} custom-call(bf16[2,128,512]{2,1,0:T(8,128)(2,1)S(1)} %collective-permute-done.18.pair_ref, f32[512,512]{1,0:T(8,128)} %place.2.rest_0_), custom_call_target="tpu_custom_call", output_to_operand_aliasing={{}: (1, {})} | custom-call | tf_op jit(solution)/shard_map/place/pallas_call | solution.py:289
  (21 shorter events, 0.4 us)
Async XLA Ops:
  0.6 5.6 %copy-start = (bf16[256,4096]{1,0:T(8,128)(2,1)S(1)}, bf16[256,4096]{1,0:T(8,128)(2,1)}, u32[]{:S(2)}) copy-start(bf16[256,4096]{1,0:T(8,128)(2,1)} %own_ref.13) | copy-start | bytes 6291460
  0.6 5.5 %collective-permute-start = (bf16[256,4096]{1,0:T(8,128)(2,1)}, bf16[256,4096]{1,0:T(8,128)(2,1)S(1)}, u32[]{:S(2)}, u32[]{:S(2)}) collective-permute-start(bf16[256,4096]{1,0:T(8,128)(2,1)} %own_ref.13), channel_id=1, source_target_pairs={{0,8},{1,9},{2,10},{3,11},{4,12},{5,13},{6,14},{7,15},{8,0},{9,1},... | collective-permute-start | bytes 6291464 | tf_op jit(solution)/shard_map/ppermute | solution.py:176
  4.6 1.6 %collective-permute-start.1 = (bf16[272,512]{1,0:T(8,128)(2,1)S(1)}, bf16[272,512]{1,0:T(8,128)(2,1)S(1)}, u32[]{:S(2)}, u32[]{:S(2)}) collective-permute-start(bf16[272,512]{1,0:T(8,128)(2,1)S(1)} %front.1.v0_ref), channel_id=1, source_target_pairs={{0,8},{1,9},{2,10},{3,11},{4,12},{5,13},{6,14},{7,15},{8,0},{9,1},... | collective-permute-start | bytes 835592 | tf_op jit(solution)/shard_map/ppermute | solution.py:176
  6.5 8.4 %collective-permute-start.2 = (bf16[128,512]{1,0:T(8,128)(2,1)S(1)}, bf16[128,512]{1,0:T(8,128)(2,1)S(1)}, u32[]{:S(2)}, u32[]{:S(2)}) collective-permute-start(bf16[128,512]{1,0:T(8,128)(2,1)S(1)} %partial_sums.8), channel_id=1, source_target_pairs={{0,1},{1,0},{2,3},{3,2},{4,5},{5,4},{6,7},{7,6},{8,9},{9,8},{10,11... | collective-permute-start | bytes 393224 | tf_op jit(solution)/shard_map/ppermute | solution.py:176
  9.3 5.6 %collective-permute-start.3 = (bf16[128,512]{1,0:T(8,128)(2,1)S(1)}, bf16[128,512]{1,0:T(8,128)(2,1)S(1)}, u32[]{:S(2)}, u32[]{:S(2)}) collective-permute-start(bf16[128,512]{1,0:T(8,128)(2,1)S(1)} %partial_sums.9), channel_id=1, source_target_pairs={{0,16},{1,17},{2,18},{3,19},{4,20},{5,21},{6,22},{7,23},{8,24},{9,... | collective-permute-start | bytes 393224 | tf_op jit(solution)/shard_map/ppermute | solution.py:176
  11.3 10.5 %collective-permute-start.4 = (bf16[384,256]{1,0:T(8,128)(2,1)S(1)}, bf16[384,256]{1,0:T(8,128)(2,1)S(1)}, u32[]{:S(2)}, u32[]{:S(2)}) collective-permute-start(bf16[384,256]{1,0:T(8,128)(2,1)S(1)} %get-tuple-element.31), channel_id=1, source_target_pairs={{0,2},{1,3},{2,0},{3,1},{4,6},{5,7},{6,4},{7,5},{8,10},{9,11},{10,... | collective-permute-start | bytes 589832 | tf_op jit(solution)/shard_map/ppermute | solution.py:176
  13.4 9.9 %collective-permute-start.12 = (bf16[384,256]{1,0:T(8,128)(2,1)S(1)}, bf16[384,256]{1,0:T(8,128)(2,1)S(1)}, u32[]{:S(2)}, u32[]{:S(2)}) collective-permute-start(bf16[384,256]{1,0:T(8,128)(2,1)S(1)} %get-tuple-element.43), channel_id=1, source_target_pairs={{0,2},{1,3},{2,0},{3,1},{4,6},{5,7},{6,4},{7,5},{8,10},{9,11},{10,... | collective-permute-start | bytes 589832 | tf_op jit(solution)/shard_map/ppermute | solution.py:176
  13.9 5.7 %collective-permute-start.5 = (bf16[128,512]{1,0:T(8,128)(2,1)S(1)}, bf16[128,512]{1,0:T(8,128)(2,1)S(1)}, u32[]{:S(2)}, u32[]{:S(2)}) collective-permute-start(bf16[128,512]{1,0:T(8,128)(2,1)S(1)} %get-tuple-element.32), channel_id=1, source_target_pairs={{0,1},{1,0},{2,3},{3,2},{4,5},{5,4},{6,7},{7,6},{8,9},{9,8},{10,11... | collective-permute-start | bytes 393224 | tf_op jit(solution)/shard_map/ppermute | solution.py:176
  15.0 5.2 %collective-permute-start.6 = (bf16[128,512]{1,0:T(8,128)(2,1)S(1)}, bf16[128,512]{1,0:T(8,128)(2,1)S(1)}, u32[]{:S(2)}, u32[]{:S(2)}) collective-permute-start(bf16[128,512]{1,0:T(8,128)(2,1)S(1)} %add_convert_fusion.4), channel_id=1, source_target_pairs={{0,16},{1,17},{2,18},{3,19},{4,20},{5,21},{6,22},{7,23},{8,24},{9,... | collective-permute-start | bytes 393224 | tf_op jit(solution)/shard_map/ppermute | solution.py:176
  16.5 7.9 %collective-permute-start.10 = (bf16[128,512]{1,0:T(8,128)(2,1)S(1)}, bf16[128,512]{1,0:T(8,128)(2,1)S(1)}, u32[]{:S(2)}, u32[]{:S(2)}) collective-permute-start(bf16[128,512]{1,0:T(8,128)(2,1)S(1)} %add_convert_fusion.2), channel_id=1, source_target_pairs={{0,1},{1,0},{2,3},{3,2},{4,5},{5,4},{6,7},{7,6},{8,9},{9,8},{10,11... | collective-permute-start | bytes 393224 | tf_op jit(solution)/shard_map/ppermute | solution.py:176
  19.6 6.5 %collective-permute-start.9 = (bf16[160,512]{1,0:T(8,128)(2,1)S(1)}, bf16[160,512]{1,0:T(8,128)(2,1)S(1)}, u32[]{:S(2)}, u32[]{:S(2)}) collective-permute-start(bf16[160,512]{1,0:T(8,128)(2,1)S(1)} %pad_maximum_fusion.2), channel_id=1, source_target_pairs={{0,16},{1,17},{2,18},{3,19},{4,20},{5,21},{6,22},{7,23},{8,24},{9,... | collective-permute-start | bytes 491528 | tf_op jit(solution)/shard_map/ppermute | solution.py:176
  20.2 5.9 %collective-permute-start.11 = (bf16[128,512]{1,0:T(8,128)(2,1)S(1)}, bf16[128,512]{1,0:T(8,128)(2,1)S(1)}, u32[]{:S(2)}, u32[]{:S(2)}) collective-permute-start(bf16[128,512]{1,0:T(8,128)(2,1)S(1)} %add_convert_fusion.3), channel_id=1, source_target_pairs={{0,2},{1,3},{2,0},{3,1},{4,6},{5,7},{6,4},{7,5},{8,10},{9,11},{10,... | collective-permute-start | bytes 393224 | tf_op jit(solution)/shard_map/ppermute | solution.py:176
  23.3 8.0 %collective-permute-start.13 = (bf16[256,256]{1,0:T(8,128)(2,1)S(1)}, bf16[256,256]{1,0:T(8,128)(2,1)S(1)}, u32[]{:S(2)}, u32[]{:S(2)}) collective-permute-start(bf16[256,256]{1,0:T(8,128)(2,1)S(1)} %slice.118), channel_id=1, source_target_pairs={{0,16},{1,17},{2,18},{3,19},{4,20},{5,21},{6,22},{7,23},{8,24},{9,... | collective-permute-start | bytes 393224 | tf_op jit(solution)/shard_map/ppermute | solution.py:176
  24.1 5.0 %collective-permute-start.8 = (bf16[256,256]{1,0:T(8,128)(2,1)S(1)}, bf16[256,256]{1,0:T(8,128)(2,1)S(1)}, u32[]{:S(2)}, u32[]{:S(2)}) collective-permute-start(bf16[256,256]{1,0:T(8,128)(2,1)S(1)} %pad_maximum_fusion.3), channel_id=1, source_target_pairs={{0,1},{1,0},{2,3},{3,2},{4,5},{5,4},{6,7},{7,6},{8,9},{9,8},{10,11... | collective-permute-start | bytes 393224 | tf_op jit(solution)/shard_map/ppermute | solution.py:176
  24.4 7.0 %collective-permute-start.7 = (bf16[128,512]{1,0:T(8,128)(2,1)S(1)}, bf16[128,512]{1,0:T(8,128)(2,1)S(1)}, u32[]{:S(2)}, u32[]{:S(2)}) collective-permute-start(bf16[128,512]{1,0:T(8,128)(2,1)S(1)} %partial_sums.12), channel_id=1, source_target_pairs={{0,2},{1,3},{2,0},{3,1},{4,6},{5,7},{6,4},{7,5},{8,10},{9,11},{10,... | collective-permute-start | bytes 393224 | tf_op jit(solution)/shard_map/ppermute | solution.py:176
  26.1 7.3 %collective-permute-start.14 = (bf16[128,512]{1,0:T(8,128)(2,1)S(1)}, bf16[128,512]{1,0:T(8,128)(2,1)S(1)}, u32[]{:S(2)}, u32[]{:S(2)}) collective-permute-start(bf16[128,512]{1,0:T(8,128)(2,1)S(1)} %add_convert_fusion.1), channel_id=1, source_target_pairs={{0,4},{1,5},{2,6},{3,7},{4,0},{5,1},{6,2},{7,3},{8,12},{9,13},{10,... | collective-permute-start | bytes 393224 | tf_op jit(solution)/shard_map/ppermute | solution.py:176
  29.1 6.6 %collective-permute-start.15 = (bf16[128,256]{1,0:T(8,128)(2,1)S(1)}, bf16[128,256]{1,0:T(8,128)(2,1)S(1)}, u32[]{:S(2)}, u32[]{:S(2)}) collective-permute-start(bf16[128,256]{1,0:T(8,128)(2,1)S(1)} %fusion.1), channel_id=1, source_target_pairs={{0,16},{1,17},{2,18},{3,19},{4,20},{5,21},{6,22},{7,23},{8,24},{9,... | collective-permute-start | bytes 196616 | tf_op jit(solution)/shard_map/ppermute | solution.py:176
  31.4 4.3 %collective-permute-start.16 = (bf16[128,256]{1,0:T(8,128)(2,1)S(1)}, bf16[128,256]{1,0:T(8,128)(2,1)S(1)}, u32[]{:S(2)}, u32[]{:S(2)}) collective-permute-start(bf16[128,256]{1,0:T(8,128)(2,1)S(1)} %get-tuple-element.56), channel_id=1, source_target_pairs={{0,1},{1,0},{2,3},{3,2},{4,5},{5,4},{6,7},{7,6},{8,9},{9,8},{10,11... | collective-permute-start | bytes 196616 | tf_op jit(solution)/shard_map/ppermute | solution.py:176
  35.8 5.0 %collective-permute-start.17 = (bf16[128,512]{1,0:T(8,128)(2,1)S(1)}, bf16[128,512]{1,0:T(8,128)(2,1)S(1)}, u32[]{:S(2)}, u32[]{:S(2)}) collective-permute-start(bf16[128,512]{1,0:T(8,128)(2,1)S(1)} %add_convert_fusion), channel_id=1, source_target_pairs={{0,16},{1,17},{2,18},{3,19},{4,20},{5,21},{6,22},{7,23},{8,24},{9,... | collective-permute-start | bytes 393224 | tf_op jit(solution)/shard_map/ppermute | solution.py:176
  40.8 1.6 %collective-permute-start.18 = (bf16[2,128,512]{2,1,0:T(8,128)(2,1)S(1)}, bf16[2,128,512]{2,1,0:T(8,128)(2,1)S(1)}, u32[]{:S(2)}, u32[]{:S(2)}) collective-permute-start(bf16[2,128,512]{2,1,0:T(8,128)(2,1)S(1)} %pad_maximum_fusion.1.pair_ref), channel_id=1, source_target_pairs={{0,8},{1,9},{2,10},{3,11},{4,12},{5,13},{6,14},{7,15},{8,0},{9,1},... | collective-permute-start | bytes 786440 | tf_op jit(solution)/shard_map/ppermute | solution.py:176

commit v23 on v17

--- a/solution.py
+++ b/solution.py
@@ -353,9 +353,8 @@
     on_b = xor_permute(on_b, Y)
     on_a = xor_permute(add(keep_a[:LANE], first_a[:LANE]).astype(BF16), X)
     z3 = add(keep_b[LANE:], side_b, on_b).astype(BF16)
-    pair_some, window, pair_own = after_all(pair_some, window, pair_own, z3)[:3]
+    pair_some, window = after_all(pair_some, window, z3)[:2]
     z3 = xor_permute(z3, Z1)
-    pair_own = xor_permute(pair_own, Z1)
     z2 = add(keep_a[LANE:], first_a[LANE:], on_a, z3).astype(BF16)
 
     some = add(own_some[:3 * LANE], pair_some)
@@ -363,8 +362,9 @@
     rest = add(own_rest[:3 * LANE], after_all(pair_rest, some)[0])
     rest_far, rest_y, rest_x = (rest[row:row + LANE] for row in range(0, 3 * LANE, LANE))
     rest_in = xor_permute(jnp.concatenate([rest_far, rest_x]).astype(BF16), X)
-    some_in = after_all(some_in, z2)[0]
+    some_in, pair_own = after_all(some_in, pair_own, z2)[:2]
     z2 = xor_permute(z2, Z2)
+    pair_own = xor_permute(pair_own, Z1)
     some_on = add(some[2 * LANE:], some_in[:LANE]).astype(BF16)
     rest_in = after_all(rest_in, some_on)[0]
     some_on = xor_permute(some_on, X)

time: 42.9 us -> 46.5 us (1.084)
  waiting for transfers between devices: 11.6 us -> 14.8 us
    ppermute x19, waiting for transfers between devices: 11.6 us -> 14.8 us  [xor_permute(): lax.ppermute(value, ('dp', 'fsdp'), [(i, i ^ mask) for i in range(count)])]
  transfers between devices with their start and end apart: 19 -> 19, of which waited for: 8 -> 8; matrix products, arithmetic and copies ran while one was open for 1% -> 1% of each run, Pallas kernels for 16% -> 15%
where the time goes in v23:
time: 46.5 us; the launch traced here: 46.4 us
  starting transfers between devices  21.6 us (46%)
  waiting for transfers between devices  14.8 us (32%)
  Pallas kernels  7.92 us (17%)
  between operations  1.59 us (3%)
    ppermute x19, starting transfers between devices, xor_permute(): lax.ppermute(value, ('dp', 'fsdp'), [(i, i ^ mask) for i in range(count)])  21.6 us
    ppermute x19, waiting for transfers between devices, xor_permute(): lax.ppermute(value, ('dp', 'fsdp'), [(i, i ^ mask) for i in range(count)])  14.8 us
    pallas_call x1, Pallas kernels, front(): pl.pallas_call(functools.partial(front_kernel, per_group), in_specs=[HBM]...  2.64 us
    pallas_call x6, Pallas kernels, partial_sums(): pl.pallas_call(functools.partial(partial_kernel, parts), in_specs=[VMEM]...  2.37 us
    pallas_call x2, Pallas kernels, place(): pl.pallas_call(functools.partial(place_kernel, core), in_specs=[VMEM] + [...  1.65 us
  transfers between devices with their start and end apart: 19, of which 8 were waited for; matrix products, arithmetic and copies ran while one was open for 1% of the time, Pallas kernels for 15%

profile of v23, /device:TPU:0, one launch (start us, length us, event | category | flops | bytes accessed | tf_op | source)
XLA Modules:
  0.0 46.4 jit_solution(17283247323445826565)
XLA Ops:
  0.6 0.5 %collective-permute-start = (bf16[256,4096]{1,0:T(8,128)(2,1)}, bf16[256,4096]{1,0:T(8,128)(2,1)S(1)}, u32[]{:S(2)}, u32[]{:S(2)}) collective-permute-start(bf16[256,4096]{1,0:T(8,128)(2,1)} %own_ref.11), channel_id=1, source_target_pairs={{0,8},{1,9},{2,10},{3,11},{4,12},{5,13},{6,14},{7,15},{8,0},{9,1},... | collective-permute-start | bytes 6291464 | tf_op jit(solution)/shard_map/ppermute | solution.py:176
  1.9 2.6 %front.1.v0_ref = bf16[272,512]{1,0:T(8,128)(2,1)S(1)} custom-call(f32[16]{0:T(128)} %loss_hbm.1, s32[1]{0:T(128)S(6)} %copy.14.exponent_hbm, s32[1,2]{1,0:T(1,128)} %start_hbm.1, s32[1,2]{1,0:T(1,128)} %rows_hbm.1, bf16[256,2048]{1,0:T(8,128)(2,1)} %q_hbm.1, bf16[256,512]{1,0:T(8,128)(2,1)} %k_hbm.1, bf16[256,2048]{1,0:T(8,128)(2,1)} %g_hbm.1, ...), custom_call_target="tpu_custom_call" | custom-call | tf_op jit(solution)/shard_map/front/pallas_call | solution.py:153
  4.6 0.1 collective-permute-start.1
  4.7 1.5 %collective-permute-done.1.v1_ref = bf16[272,512]{1,0:T(8,128)(2,1)S(1)} collective-permute-done((bf16[272,512]{1,0:T(8,128)(2,1)S(1)}, bf16[272,512]{1,0:T(8,128)(2,1)S(1)}, u32[]{:S(2)}, u32[]{:S(2)}) %collective-permute-start.1) | collective-permute-done | bytes 278560 | tf_op jit(solution)/shard_map/ppermute | solution.py:176
  6.2 0.0 collective-permute-done.near_ref
  6.2 0.3 partial_sums.10
  6.5 2.6 %collective-permute-start.3 = (bf16[128,512]{1,0:T(8,128)(2,1)S(1)}, bf16[128,512]{1,0:T(8,128)(2,1)S(1)}, u32[]{:S(2)}, u32[]{:S(2)}) collective-permute-start(bf16[128,512]{1,0:T(8,128)(2,1)S(1)} %partial_sums.10), channel_id=1, source_target_pairs={{0,1},{1,0},{2,3},{3,2},{4,5},{5,4},{6,7},{7,6},{8,9},{9,8},{10,11... | collective-permute-start | bytes 393224 | tf_op jit(solution)/shard_map/ppermute | solution.py:176
  9.1 0.3 partial_sums.11
  9.4 1.6 %collective-permute-start.8 = (bf16[256,512]{1,0:T(8,128)(2,1)S(1)}, bf16[256,512]{1,0:T(8,128)(2,1)S(1)}, u32[]{:S(2)}, u32[]{:S(2)}) collective-permute-start(bf16[256,512]{1,0:T(8,128)(2,1)S(1)} %partial_sums.11), channel_id=1, source_target_pairs={{0,16},{1,17},{2,18},{3,19},{4,20},{5,21},{6,22},{7,23},{8,24},{9,... | collective-permute-start | bytes 786440 | tf_op jit(solution)/shard_map/ppermute | solution.py:176
  11.0 0.4 partial_sums.7
  11.4 1.6 %collective-permute-start.2 = (bf16[384,256]{1,0:T(8,128)(2,1)S(1)}, bf16[384,256]{1,0:T(8,128)(2,1)S(1)}, u32[]{:S(2)}, u32[]{:S(2)}) collective-permute-start(bf16[384,256]{1,0:T(8,128)(2,1)S(1)} %get-tuple-element.27), channel_id=1, source_target_pairs={{0,2},{1,3},{2,0},{3,1},{4,6},{5,7},{6,4},{7,5},{8,10},{9,11},{10,... | collective-permute-start | bytes 589832 | tf_op jit(solution)/shard_map/ppermute | solution.py:176
  13.0 0.4 partial_sums.8
  13.4 0.5 %collective-permute-start.12 = (bf16[384,256]{1,0:T(8,128)(2,1)S(1)}, bf16[384,256]{1,0:T(8,128)(2,1)S(1)}, u32[]{:S(2)}, u32[]{:S(2)}) collective-permute-start(bf16[384,256]{1,0:T(8,128)(2,1)S(1)} %get-tuple-element.29), channel_id=1, source_target_pairs={{0,2},{1,3},{2,0},{3,1},{4,6},{5,7},{6,4},{7,5},{8,10},{9,11},{10,... | collective-permute-start | bytes 589832 | tf_op jit(solution)/shard_map/ppermute | solution.py:176
  14.0 0.5 %collective-permute-start.5 = (bf16[128,512]{1,0:T(8,128)(2,1)S(1)}, bf16[128,512]{1,0:T(8,128)(2,1)S(1)}, u32[]{:S(2)}, u32[]{:S(2)}) collective-permute-start(bf16[128,512]{1,0:T(8,128)(2,1)S(1)} %get-tuple-element.34), channel_id=1, source_target_pairs={{0,1},{1,0},{2,3},{3,2},{4,5},{5,4},{6,7},{7,6},{8,9},{9,8},{10,11... | collective-permute-start | bytes 393224 | tf_op jit(solution)/shard_map/ppermute | solution.py:176
  14.5 0.5 %partial_sums.9 = (f32[256,512]{1,0:T(8,128)S(1)}, f32[256,512]{1,0:T(8,128)S(1)}) custom-call(bf16[256,4096]{1,0:T(8,128)(2,1)S(1)} %copy-done, bf16[256,4096]{1,0:T(8,128)(2,1)S(1)} %collective-permute-done.near_ref, bf16[272,512]{1,0:T(8,128)(2,1)S(1)} %front.1.v0_ref, bf16[272,512]{1,0:T(8,128)(2,1)S(1)} %collective-permute-done.1.v1_ref), custom_call_target="tpu_custom_call" | custom-call | tf_op jit(solution)/shard_map/partial_sums/pallas_call | solution.py:201
  15.0 0.5 %partial_sums.6 = (f32[512,256]{1,0:T(8,128)S(1)}, f32[512,256]{1,0:T(8,128)S(1)}) custom-call(bf16[256,4096]{1,0:T(8,128)(2,1)S(1)} %copy-done, bf16[256,4096]{1,0:T(8,128)(2,1)S(1)} %collective-permute-done.near_ref, bf16[272,512]{1,0:T(8,128)(2,1)S(1)} %front.1.v0_ref, bf16[272,512]{1,0:T(8,128)(2,1)S(1)} %collective-permute-done.1.v1_ref), custom_call_target="tpu_custom_call" | custom-call | tf_op jit(solution)/shard_map/partial_sums/pallas_call | solution.py:201
  15.5 0.3 inner_swap.1
  15.8 0.0 collective-permute-done.3
  15.8 0.2 collective-permute-start.6
  16.0 2.0 %collective-permute-done.8 = bf16[256,512]{1,0:T(8,128)(2,1)S(1)} collective-permute-done((bf16[256,512]{1,0:T(8,128)(2,1)S(1)}, bf16[256,512]{1,0:T(8,128)(2,1)S(1)}, u32[]{:S(2)}, u32[]{:S(2)}) %collective-permute-start.8) | collective-permute-done | bytes 262176 | tf_op jit(solution)/shard_map/ppermute | solution.py:176
  18.0 2.1 %collective-permute-start.4 = (bf16[32,512]{1,0:T(8,128)(2,1)S(1)}, bf16[32,512]{1,0:T(8,128)(2,1)S(1)}, u32[]{:S(2)}, u32[]{:S(2)}) collective-permute-start(bf16[32,512]{1,0:T(8,128)(2,1)S(1)} %get-tuple-element.33), channel_id=1, source_target_pairs={{0,16},{1,17},{2,18},{3,19},{4,20},{5,21},{6,22},{7,23},{8,24},{9,... | collective-permute-start | bytes 98312 | tf_op jit(solution)/shard_map/ppermute | solution.py:176
  20.2 0.0 collective-permute-done.5
  20.2 0.1 collective-permute-start.9
  20.3 0.9 %collective-permute-done.6 = bf16[128,512]{1,0:T(8,128)(2,1)S(1)} collective-permute-done((bf16[128,512]{1,0:T(8,128)(2,1)S(1)}, bf16[128,512]{1,0:T(8,128)(2,1)S(1)}, u32[]{:S(2)}, u32[]{:S(2)}) %collective-permute-start.6) | collective-permute-done | bytes 131104 | tf_op jit(solution)/shard_map/ppermute | solution.py:176
  21.3 1.6 %collective-permute-start.10 = (bf16[128,512]{1,0:T(8,128)(2,1)S(1)}, bf16[128,512]{1,0:T(8,128)(2,1)S(1)}, u32[]{:S(2)}, u32[]{:S(2)}) collective-permute-start(bf16[128,512]{1,0:T(8,128)(2,1)S(1)} %add_convert_fusion.3), channel_id=1, source_target_pairs={{0,2},{1,3},{2,0},{3,1},{4,6},{5,7},{6,4},{7,5},{8,10},{9,11},{10,... | collective-permute-start | bytes 393224 | tf_op jit(solution)/shard_map/ppermute | solution.py:176
  22.9 0.0 collective-permute-done.4.window_ref
  23.0 1.3 %collective-permute-start.7 = (bf16[256,256]{1,0:T(8,128)(2,1)S(1)}, bf16[256,256]{1,0:T(8,128)(2,1)S(1)}, u32[]{:S(2)}, u32[]{:S(2)}) collective-permute-start(bf16[256,256]{1,0:T(8,128)(2,1)S(1)} %slice.119), channel_id=1, source_target_pairs={{0,16},{1,17},{2,18},{3,19},{4,20},{5,21},{6,22},{7,23},{8,24},{9,... | collective-permute-start | bytes 393224 | tf_op jit(solution)/shard_map/ppermute | solution.py:176
  24.3 0.0 collective-permute-done.12
  24.4 0.8 %collective-permute-start.13 = (bf16[256,256]{1,0:T(8,128)(2,1)S(1)}, bf16[256,256]{1,0:T(8,128)(2,1)S(1)}, u32[]{:S(2)}, u32[]{:S(2)}) collective-permute-start(bf16[256,256]{1,0:T(8,128)(2,1)S(1)} %pad_maximum_fusion.2), channel_id=1, source_target_pairs={{0,1},{1,0},{2,3},{3,2},{4,5},{5,4},{6,7},{7,6},{8,9},{9,8},{10,11... | collective-permute-start | bytes 393224 | tf_op jit(solution)/shard_map/ppermute | solution.py:176
  25.2 0.0 collective-permute-done.9
  25.2 1.1 %collective-permute-done.10 = bf16[128,512]{1,0:T(8,128)(2,1)S(1)} collective-permute-done((bf16[128,512]{1,0:T(8,128)(2,1)S(1)}, bf16[128,512]{1,0:T(8,128)(2,1)S(1)}, u32[]{:S(2)}, u32[]{:S(2)}) %collective-permute-start.10) | collective-permute-done | bytes 131104 | tf_op jit(solution)/shard_map/ppermute | solution.py:176
  26.3 0.1 add_convert_fusion.1
  26.4 2.8 %collective-permute-start.14 = (bf16[128,512]{1,0:T(8,128)(2,1)S(1)}, bf16[128,512]{1,0:T(8,128)(2,1)S(1)}, u32[]{:S(2)}, u32[]{:S(2)}) collective-permute-start(bf16[128,512]{1,0:T(8,128)(2,1)S(1)} %add_convert_fusion.1), channel_id=1, source_target_pairs={{0,4},{1,5},{2,6},{3,7},{4,0},{5,1},{6,2},{7,3},{8,12},{9,13},{10,... | collective-permute-start | bytes 393224 | tf_op jit(solution)/shard_map/ppermute | solution.py:176
  29.2 0.0 collective-permute-done.7
  29.2 1.4 %collective-permute-start.11 = (bf16[128,512]{1,0:T(8,128)(2,1)S(1)}, bf16[128,512]{1,0:T(8,128)(2,1)S(1)}, u32[]{:S(2)}, u32[]{:S(2)}) collective-permute-start(bf16[128,512]{1,0:T(8,128)(2,1)S(1)} %get-tuple-element.38), channel_id=1, source_target_pairs={{0,2},{1,3},{2,0},{3,1},{4,6},{5,7},{6,4},{7,5},{8,10},{9,11},{10,... | collective-permute-start | bytes 393224 | tf_op jit(solution)/shard_map/ppermute | solution.py:176
  30.6 1.2 %collective-permute-start.15 = (bf16[128,256]{1,0:T(8,128)(2,1)S(1)}, bf16[128,256]{1,0:T(8,128)(2,1)S(1)}, u32[]{:S(2)}, u32[]{:S(2)}) collective-permute-start(bf16[128,256]{1,0:T(8,128)(2,1)S(1)} %fusion.1), channel_id=1, source_target_pairs={{0,1},{1,0},{2,3},{3,2},{4,5},{5,4},{6,7},{7,6},{8,9},{9,8},{10,11... | collective-permute-start | bytes 196616 | tf_op jit(solution)/shard_map/ppermute | solution.py:176
  31.8 0.0 collective-permute-done.13
  31.8 2.6 %collective-permute-done.11 = bf16[128,512]{1,0:T(8,128)(2,1)S(1)} collective-permute-done((bf16[128,512]{1,0:T(8,128)(2,1)S(1)}, bf16[128,512]{1,0:T(8,128)(2,1)S(1)}, u32[]{:S(2)}, u32[]{:S(2)}) %collective-permute-start.11) | collective-permute-done | bytes 131104 | tf_op jit(solution)/shard_map/ppermute | solution.py:176
  34.5 1.1 %collective-permute-start.16 = (bf16[128,256]{1,0:T(8,128)(2,1)S(1)}, bf16[128,256]{1,0:T(8,128)(2,1)S(1)}, u32[]{:S(2)}, u32[]{:S(2)}) collective-permute-start(bf16[128,256]{1,0:T(8,128)(2,1)S(1)} %get-tuple-element.54), channel_id=1, source_target_pairs={{0,16},{1,17},{2,18},{3,19},{4,20},{5,21},{6,22},{7,23},{8,24},{9,... | collective-permute-start | bytes 196616 | tf_op jit(solution)/shard_map/ppermute | solution.py:176
  35.7 0.0 collective-permute-done.14.arrived_ref
  35.7 3.1 %collective-permute-done.16 = bf16[128,256]{1,0:T(8,128)(2,1)S(1)} collective-permute-done((bf16[128,256]{1,0:T(8,128)(2,1)S(1)}, bf16[128,256]{1,0:T(8,128)(2,1)S(1)}, u32[]{:S(2)}, u32[]{:S(2)}) %collective-permute-start.16) | collective-permute-done | bytes 65568 | tf_op jit(solution)/shard_map/ppermute | solution.py:176
  38.9 1.3 %collective-permute-start.17 = (bf16[128,512]{1,0:T(8,128)(2,1)S(1)}, bf16[128,512]{1,0:T(8,128)(2,1)S(1)}, u32[]{:S(2)}, u32[]{:S(2)}) collective-permute-start(bf16[128,512]{1,0:T(8,128)(2,1)S(1)} %add_convert_fusion), channel_id=1, source_target_pairs={{0,16},{1,17},{2,18},{3,19},{4,20},{5,21},{6,22},{7,23},{8,24},{9,... | collective-permute-start | bytes 393224 | tf_op jit(solution)/shard_map/ppermute | solution.py:176
  40.2 0.9 %outer_swap.1 = bf16[256,512]{1,0:T(8,128)(2,1)} custom-call(bf16[272,512]{1,0:T(8,128)(2,1)S(1)} %front.1.v0_ref, bf16[256,512]{1,0:T(8,128)(2,1)S(1)} %get-tuple-element.43.rows_ref, bf16[32,512]{1,0:T(8,128)(2,1)S(1)} %collective-permute-done.4.window_ref), custom_call_target="tpu_custom_call" | custom-call | tf_op jit(solution)/shard_map/outer_swap/pallas_call | solution.py:265
  41.1 2.8 %collective-permute-done.17 = bf16[128,512]{1,0:T(8,128)(2,1)S(1)} collective-permute-done((bf16[128,512]{1,0:T(8,128)(2,1)S(1)}, bf16[128,512]{1,0:T(8,128)(2,1)S(1)}, u32[]{:S(2)}, u32[]{:S(2)}) %collective-permute-start.17) | collective-permute-done | bytes 131104 | tf_op jit(solution)/shard_map/ppermute | solution.py:176
  43.9 0.1 collective-permute-start.18
  44.0 0.8 %place.2.rest_0_ = f32[512,512]{1,0:T(8,128)} custom-call(bf16[2,128,512]{2,1,0:T(8,128)(2,1)S(1)} %pad_maximum_fusion.1.pair_ref), custom_call_target="tpu_custom_call" | custom-call | tf_op jit(solution)/shard_map/place/pallas_call | solution.py:289
  44.9 0.7 %collective-permute-done.18.pair_ref = bf16[2,128,512]{2,1,0:T(8,128)(2,1)S(1)} collective-permute-done((bf16[2,128,512]{2,1,0:T(8,128)(2,1)S(1)}, bf16[2,128,512]{2,1,0:T(8,128)(2,1)S(1)}, u32[]{:S(2)}, u32[]{:S(2)}) %collective-permute-start.18) | collective-permute-done | bytes 262176 | tf_op jit(solution)/shard_map/ppermute | solution.py:176
  45.5 0.8 %place.3 = f32[512,512]{1,0:T(8,128)} custom-call(bf16[2,128,512]{2,1,0:T(8,128)(2,1)S(1)} %collective-permute-done.18.pair_ref, f32[512,512]{1,0:T(8,128)} %place.2.rest_0_), custom_call_target="tpu_custom_call", output_to_operand_aliasing={{}: (1, {})} | custom-call | tf_op jit(solution)/shard_map/place/pallas_call | solution.py:289
  (18 shorter events, 0.4 us)
Async XLA Ops:
  0.6 5.6 %copy-start = (bf16[256,4096]{1,0:T(8,128)(2,1)S(1)}, bf16[256,4096]{1,0:T(8,128)(2,1)}, u32[]{:S(2)}) copy-start(bf16[256,4096]{1,0:T(8,128)(2,1)} %own_ref.11) | copy-start | bytes 6291460
  0.6 5.5 %collective-permute-start = (bf16[256,4096]{1,0:T(8,128)(2,1)}, bf16[256,4096]{1,0:T(8,128)(2,1)S(1)}, u32[]{:S(2)}, u32[]{:S(2)}) collective-permute-start(bf16[256,4096]{1,0:T(8,128)(2,1)} %own_ref.11), channel_id=1, source_target_pairs={{0,8},{1,9},{2,10},{3,11},{4,12},{5,13},{6,14},{7,15},{8,0},{9,1},... | collective-permute-start | bytes 6291464 | tf_op jit(solution)/shard_map/ppermute | solution.py:176
  4.6 1.6 %collective-permute-start.1 = (bf16[272,512]{1,0:T(8,128)(2,1)S(1)}, bf16[272,512]{1,0:T(8,128)(2,1)S(1)}, u32[]{:S(2)}, u32[]{:S(2)}) collective-permute-start(bf16[272,512]{1,0:T(8,128)(2,1)S(1)} %front.1.v0_ref), channel_id=1, source_target_pairs={{0,8},{1,9},{2,10},{3,11},{4,12},{5,13},{6,14},{7,15},{8,0},{9,1},... | collective-permute-start | bytes 835592 | tf_op jit(solution)/shard_map/ppermute | solution.py:176
  6.5 9.3 %collective-permute-start.3 = (bf16[128,512]{1,0:T(8,128)(2,1)S(1)}, bf16[128,512]{1,0:T(8,128)(2,1)S(1)}, u32[]{:S(2)}, u32[]{:S(2)}) collective-permute-start(bf16[128,512]{1,0:T(8,128)(2,1)S(1)} %partial_sums.10), channel_id=1, source_target_pairs={{0,1},{1,0},{2,3},{3,2},{4,5},{5,4},{6,7},{7,6},{8,9},{9,8},{10,11... | collective-permute-start | bytes 393224 | tf_op jit(solution)/shard_map/ppermute | solution.py:176
  9.4 8.6 %collective-permute-start.8 = (bf16[256,512]{1,0:T(8,128)(2,1)S(1)}, bf16[256,512]{1,0:T(8,128)(2,1)S(1)}, u32[]{:S(2)}, u32[]{:S(2)}) collective-permute-start(bf16[256,512]{1,0:T(8,128)(2,1)S(1)} %partial_sums.11), channel_id=1, source_target_pairs={{0,16},{1,17},{2,18},{3,19},{4,20},{5,21},{6,22},{7,23},{8,24},{9,... | collective-permute-start | bytes 786440 | tf_op jit(solution)/shard_map/ppermute | solution.py:176
  11.4 11.5 %collective-permute-start.2 = (bf16[384,256]{1,0:T(8,128)(2,1)S(1)}, bf16[384,256]{1,0:T(8,128)(2,1)S(1)}, u32[]{:S(2)}, u32[]{:S(2)}) collective-permute-start(bf16[384,256]{1,0:T(8,128)(2,1)S(1)} %get-tuple-element.27), channel_id=1, source_target_pairs={{0,2},{1,3},{2,0},{3,1},{4,6},{5,7},{6,4},{7,5},{8,10},{9,11},{10,... | collective-permute-start | bytes 589832 | tf_op jit(solution)/shard_map/ppermute | solution.py:176
  13.4 10.8 %collective-permute-start.12 = (bf16[384,256]{1,0:T(8,128)(2,1)S(1)}, bf16[384,256]{1,0:T(8,128)(2,1)S(1)}, u32[]{:S(2)}, u32[]{:S(2)}) collective-permute-start(bf16[384,256]{1,0:T(8,128)(2,1)S(1)} %get-tuple-element.29), channel_id=1, source_target_pairs={{0,2},{1,3},{2,0},{3,1},{4,6},{5,7},{6,4},{7,5},{8,10},{9,11},{10,... | collective-permute-start | bytes 589832 | tf_op jit(solution)/shard_map/ppermute | solution.py:176
  14.0 6.2 %collective-permute-start.5 = (bf16[128,512]{1,0:T(8,128)(2,1)S(1)}, bf16[128,512]{1,0:T(8,128)(2,1)S(1)}, u32[]{:S(2)}, u32[]{:S(2)}) collective-permute-start(bf16[128,512]{1,0:T(8,128)(2,1)S(1)} %get-tuple-element.34), channel_id=1, source_target_pairs={{0,1},{1,0},{2,3},{3,2},{4,5},{5,4},{6,7},{7,6},{8,9},{9,8},{10,11... | collective-permute-start | bytes 393224 | tf_op jit(solution)/shard_map/ppermute | solution.py:176
  15.8 5.4 %collective-permute-start.6 = (bf16[128,512]{1,0:T(8,128)(2,1)S(1)}, bf16[128,512]{1,0:T(8,128)(2,1)S(1)}, u32[]{:S(2)}, u32[]{:S(2)}) collective-permute-start(bf16[128,512]{1,0:T(8,128)(2,1)S(1)} %add_convert_fusion.4), channel_id=1, source_target_pairs={{0,16},{1,17},{2,18},{3,19},{4,20},{5,21},{6,22},{7,23},{8,24},{9,... | collective-permute-start | bytes 393224 | tf_op jit(solution)/shard_map/ppermute | solution.py:176
  18.0 4.9 %collective-permute-start.4 = (bf16[32,512]{1,0:T(8,128)(2,1)S(1)}, bf16[32,512]{1,0:T(8,128)(2,1)S(1)}, u32[]{:S(2)}, u32[]{:S(2)}) collective-permute-start(bf16[32,512]{1,0:T(8,128)(2,1)S(1)} %get-tuple-element.33), channel_id=1, source_target_pairs={{0,16},{1,17},{2,18},{3,19},{4,20},{5,21},{6,22},{7,23},{8,24},{9,... | collective-permute-start | bytes 98312 | tf_op jit(solution)/shard_map/ppermute | solution.py:176
  20.2 5.0 %collective-permute-start.9 = (bf16[128,512]{1,0:T(8,128)(2,1)S(1)}, bf16[128,512]{1,0:T(8,128)(2,1)S(1)}, u32[]{:S(2)}, u32[]{:S(2)}) collective-permute-start(bf16[128,512]{1,0:T(8,128)(2,1)S(1)} %add_convert_fusion.2), channel_id=1, source_target_pairs={{0,1},{1,0},{2,3},{3,2},{4,5},{5,4},{6,7},{7,6},{8,9},{9,8},{10,11... | collective-permute-start | bytes 393224 | tf_op jit(solution)/shard_map/ppermute | solution.py:176
  21.3 5.0 %collective-permute-start.10 = (bf16[128,512]{1,0:T(8,128)(2,1)S(1)}, bf16[128,512]{1,0:T(8,128)(2,1)S(1)}, u32[]{:S(2)}, u32[]{:S(2)}) collective-permute-start(bf16[128,512]{1,0:T(8,128)(2,1)S(1)} %add_convert_fusion.3), channel_id=1, source_target_pairs={{0,2},{1,3},{2,0},{3,1},{4,6},{5,7},{6,4},{7,5},{8,10},{9,11},{10,... | collective-permute-start | bytes 393224 | tf_op jit(solution)/shard_map/ppermute | solution.py:176
  23.0 6.2 %collective-permute-start.7 = (bf16[256,256]{1,0:T(8,128)(2,1)S(1)}, bf16[256,256]{1,0:T(8,128)(2,1)S(1)}, u32[]{:S(2)}, u32[]{:S(2)}) collective-permute-start(bf16[256,256]{1,0:T(8,128)(2,1)S(1)} %slice.119), channel_id=1, source_target_pairs={{0,16},{1,17},{2,18},{3,19},{4,20},{5,21},{6,22},{7,23},{8,24},{9,... | collective-permute-start | bytes 393224 | tf_op jit(solution)/shard_map/ppermute | solution.py:176
  24.4 7.5 %collective-permute-start.13 = (bf16[256,256]{1,0:T(8,128)(2,1)S(1)}, bf16[256,256]{1,0:T(8,128)(2,1)S(1)}, u32[]{:S(2)}, u32[]{:S(2)}) collective-permute-start(bf16[256,256]{1,0:T(8,128)(2,1)S(1)} %pad_maximum_fusion.2), channel_id=1, source_target_pairs={{0,1},{1,0},{2,3},{3,2},{4,5},{5,4},{6,7},{7,6},{8,9},{9,8},{10,11... | collective-permute-start | bytes 393224 | tf_op jit(solution)/shard_map/ppermute | solution.py:176
  26.4 9.3 %collective-permute-start.14 = (bf16[128,512]{1,0:T(8,128)(2,1)S(1)}, bf16[128,512]{1,0:T(8,128)(2,1)S(1)}, u32[]{:S(2)}, u32[]{:S(2)}) collective-permute-start(bf16[128,512]{1,0:T(8,128)(2,1)S(1)} %add_convert_fusion.1), channel_id=1, source_target_pairs={{0,4},{1,5},{2,6},{3,7},{4,0},{5,1},{6,2},{7,3},{8,12},{9,13},{10,... | collective-permute-start | bytes 393224 | tf_op jit(solution)/shard_map/ppermute | solution.py:176
  29.2 5.3 %collective-permute-start.11 = (bf16[128,512]{1,0:T(8,128)(2,1)S(1)}, bf16[128,512]{1,0:T(8,128)(2,1)S(1)}, u32[]{:S(2)}, u32[]{:S(2)}) collective-permute-start(bf16[128,512]{1,0:T(8,128)(2,1)S(1)} %get-tuple-element.38), channel_id=1, source_target_pairs={{0,2},{1,3},{2,0},{3,1},{4,6},{5,7},{6,4},{7,5},{8,10},{9,11},{10,... | collective-permute-start | bytes 393224 | tf_op jit(solution)/shard_map/ppermute | solution.py:176
  30.6 5.1 %collective-permute-start.15 = (bf16[128,256]{1,0:T(8,128)(2,1)S(1)}, bf16[128,256]{1,0:T(8,128)(2,1)S(1)}, u32[]{:S(2)}, u32[]{:S(2)}) collective-permute-start(bf16[128,256]{1,0:T(8,128)(2,1)S(1)} %fusion.1), channel_id=1, source_target_pairs={{0,1},{1,0},{2,3},{3,2},{4,5},{5,4},{6,7},{7,6},{8,9},{9,8},{10,11... | collective-permute-start | bytes 196616 | tf_op jit(solution)/shard_map/ppermute | solution.py:176
  34.5 4.3 %collective-permute-start.16 = (bf16[128,256]{1,0:T(8,128)(2,1)S(1)}, bf16[128,256]{1,0:T(8,128)(2,1)S(1)}, u32[]{:S(2)}, u32[]{:S(2)}) collective-permute-start(bf16[128,256]{1,0:T(8,128)(2,1)S(1)} %get-tuple-element.54), channel_id=1, source_target_pairs={{0,16},{1,17},{2,18},{3,19},{4,20},{5,21},{6,22},{7,23},{8,24},{9,... | collective-permute-start | bytes 196616 | tf_op jit(solution)/shard_map/ppermute | solution.py:176
  38.9 5.0 %collective-permute-start.17 = (bf16[128,512]{1,0:T(8,128)(2,1)S(1)}, bf16[128,512]{1,0:T(8,128)(2,1)S(1)}, u32[]{:S(2)}, u32[]{:S(2)}) collective-permute-start(bf16[128,512]{1,0:T(8,128)(2,1)S(1)} %add_convert_fusion), channel_id=1, source_target_pairs={{0,16},{1,17},{2,18},{3,19},{4,20},{5,21},{6,22},{7,23},{8,24},{9,... | collective-permute-start | bytes 393224 | tf_op jit(solution)/shard_map/ppermute | solution.py:176
  43.9 1.6 %collective-permute-start.18 = (bf16[2,128,512]{2,1,0:T(8,128)(2,1)S(1)}, bf16[2,128,512]{2,1,0:T(8,128)(2,1)S(1)}, u32[]{:S(2)}, u32[]{:S(2)}) collective-permute-start(bf16[2,128,512]{2,1,0:T(8,128)(2,1)S(1)} %pad_maximum_fusion.1.pair_ref), channel_id=1, source_target_pairs={{0,8},{1,9},{2,10},{3,11},{4,12},{5,13},{6,14},{7,15},{8,0},{9,1},... | collective-permute-start | bytes 786440 | tf_op jit(solution)/shard_map/ppermute | solution.py:176

commit v24 on v20

--- a/solution.py
+++ b/solution.py
@@ -365,20 +365,19 @@
     rest = add(own_rest[:3 * LANE], after_all(pair_rest, some)[0])
     rest_far, rest_y, rest_x = (rest[row:row + LANE] for row in range(0, 3 * LANE, LANE))
     rest_in = xor_permute(jnp.concatenate([rest_far, rest_x]).astype(BF16), X)
-    some_in, pair_own = after_all(some_in, pair_own, z2)[:2]
+    some_in = after_all(some_in, z2)[0]
     z2 = xor_permute(z2, Z2)
-    pair_own = xor_permute(pair_own, Z1)
     some_on = add(some[2 * LANE:], some_in[:LANE]).astype(BF16)
     rest_in = after_all(rest_in, some_on)[0]
     some_on = xor_permute(some_on, X)
     rest_on = add(rest_y, rest_in[:LANE]).astype(BF16)
-    pair_own = after_all(pair_own, rest_on)[0]
+    pair_own = xor_permute(after_all(pair_own, rest_on)[0], Z1)
     rest_on = xor_permute(rest_on, Y)
     base = jnp.concatenate([
-        add(own_some[3 * LANE:], pair_own[:, :256], some_in[LANE:]),
-        add(own_rest[3 * LANE:], pair_own[:, 256:], rest_in[LANE:]),
+        add(own_some[3 * LANE:], some_in[LANE:]),
+        add(own_rest[3 * LANE:], rest_in[LANE:]),
     ], axis=1)
-    mine = add(fold(base, z2), jnp.concatenate([some_on, rest_on], axis=1)).astype(BF16)
+    mine = add(fold(base, z2), jnp.concatenate([some_on, rest_on], axis=1), pair_own).astype(BF16)
     from_y = xor_permute(mine, Y)
     value_grad = outer_swap(v0, rows, after_all(window, mine)[0])
     from_y, value_grad = after_all(from_y, value_grad)

time: 44 us -> 43.9 us (level)
  transfers between devices with their start and end apart: 19 -> 19, of which waited for: 8 -> 9; matrix products, arithmetic and copies ran while one was open for 1% -> 1% of each run, Pallas kernels for 16% -> 16%
where the time goes in v24:
time: 43.9 us; the launch traced here: 43.7 us
  starting transfers between devices  21.9 us (50%)
  waiting for transfers between devices  11.7 us (27%)
  Pallas kernels  8.1 us (18%)
  between operations  1.61 us (4%)
    ppermute x19, starting transfers between devices, xor_permute(): lax.ppermute(value, ('dp', 'fsdp'), [(i, i ^ mask) for i in range(count)])  21.9 us
    ppermute x19, waiting for transfers between devices, xor_permute(): lax.ppermute(value, ('dp', 'fsdp'), [(i, i ^ mask) for i in range(count)])  11.7 us
    pallas_call x1, Pallas kernels, front(): pl.pallas_call(functools.partial(front_kernel, per_group), in_specs=[HBM]...  2.64 us
    pallas_call x7, Pallas kernels, partial_sums(): pl.pallas_call(functools.partial(partial_kernel, parts), in_specs=[VMEM]...  2.55 us
    pallas_call x2, Pallas kernels, place(): pl.pallas_call(functools.partial(place_kernel, core), in_specs=[VMEM] + [...  1.65 us
    pallas_call x1, Pallas kernels, outer_swap(): pl.pallas_call(outer_swap_kernel, in_specs=[VMEM] * 3, out_specs=VMEM, ou...  0.91 us
  transfers between devices with their start and end apart: 19, of which 9 were waited for; matrix products, arithmetic and copies ran while one was open for 1% of the time, Pallas kernels for 16%

profile of v24, /device:TPU:0, one launch (start us, length us, event | category | flops | bytes accessed | tf_op | source)
XLA Modules:
  0.0 43.7 jit_solution(9401709368085687400)
XLA Ops:
  0.6 0.5 %collective-permute-start = (bf16[256,4096]{1,0:T(8,128)(2,1)}, bf16[256,4096]{1,0:T(8,128)(2,1)S(1)}, u32[]{:S(2)}, u32[]{:S(2)}) collective-permute-start(bf16[256,4096]{1,0:T(8,128)(2,1)} %own_ref.13), channel_id=1, source_target_pairs={{0,8},{1,9},{2,10},{3,11},{4,12},{5,13},{6,14},{7,15},{8,0},{9,1},... | collective-permute-start | bytes 6291464 | tf_op jit(solution)/shard_map/ppermute | solution.py:176
  1.9 2.6 %front.1.v0_ref = bf16[272,512]{1,0:T(8,128)(2,1)S(1)} custom-call(f32[16]{0:T(128)} %loss_hbm.1, s32[1]{0:T(128)S(6)} %copy.14.exponent_hbm, s32[1,2]{1,0:T(1,128)} %start_hbm.1, s32[1,2]{1,0:T(1,128)} %rows_hbm.1, bf16[256,2048]{1,0:T(8,128)(2,1)} %q_hbm.1, bf16[256,512]{1,0:T(8,128)(2,1)} %k_hbm.1, bf16[256,2048]{1,0:T(8,128)(2,1)} %g_hbm.1, ...), custom_call_target="tpu_custom_call" | custom-call | tf_op jit(solution)/shard_map/front/pallas_call | solution.py:153
  4.6 0.1 collective-permute-start.1
  4.7 1.5 %collective-permute-done.1.v1_ref = bf16[272,512]{1,0:T(8,128)(2,1)S(1)} collective-permute-done((bf16[272,512]{1,0:T(8,128)(2,1)S(1)}, bf16[272,512]{1,0:T(8,128)(2,1)S(1)}, u32[]{:S(2)}, u32[]{:S(2)}) %collective-permute-start.1) | collective-permute-done | bytes 278560 | tf_op jit(solution)/shard_map/ppermute | solution.py:176
  6.2 0.0 collective-permute-done.near_ref
  6.2 0.3 partial_sums.8
  6.5 2.6 %collective-permute-start.2 = (bf16[128,512]{1,0:T(8,128)(2,1)S(1)}, bf16[128,512]{1,0:T(8,128)(2,1)S(1)}, u32[]{:S(2)}, u32[]{:S(2)}) collective-permute-start(bf16[128,512]{1,0:T(8,128)(2,1)S(1)} %partial_sums.8), channel_id=1, source_target_pairs={{0,1},{1,0},{2,3},{3,2},{4,5},{5,4},{6,7},{7,6},{8,9},{9,8},{10,11... | collective-permute-start | bytes 393224 | tf_op jit(solution)/shard_map/ppermute | solution.py:176
  9.1 0.3 partial_sums.9
  9.3 1.6 %collective-permute-start.3 = (bf16[128,512]{1,0:T(8,128)(2,1)S(1)}, bf16[128,512]{1,0:T(8,128)(2,1)S(1)}, u32[]{:S(2)}, u32[]{:S(2)}) collective-permute-start(bf16[128,512]{1,0:T(8,128)(2,1)S(1)} %partial_sums.9), channel_id=1, source_target_pairs={{0,16},{1,17},{2,18},{3,19},{4,20},{5,21},{6,22},{7,23},{8,24},{9,... | collective-permute-start | bytes 393224 | tf_op jit(solution)/shard_map/ppermute | solution.py:176
  10.9 0.4 partial_sums.11
  11.3 1.6 %collective-permute-start.4 = (bf16[384,256]{1,0:T(8,128)(2,1)S(1)}, bf16[384,256]{1,0:T(8,128)(2,1)S(1)}, u32[]{:S(2)}, u32[]{:S(2)}) collective-permute-start(bf16[384,256]{1,0:T(8,128)(2,1)S(1)} %get-tuple-element.31), channel_id=1, source_target_pairs={{0,2},{1,3},{2,0},{3,1},{4,6},{5,7},{6,4},{7,5},{8,10},{9,11},{10,... | collective-permute-start | bytes 589832 | tf_op jit(solution)/shard_map/ppermute | solution.py:176
  13.0 0.5 %collective-permute-start.5 = (bf16[128,512]{1,0:T(8,128)(2,1)S(1)}, bf16[128,512]{1,0:T(8,128)(2,1)S(1)}, u32[]{:S(2)}, u32[]{:S(2)}) collective-permute-start(bf16[128,512]{1,0:T(8,128)(2,1)S(1)} %get-tuple-element.32), channel_id=1, source_target_pairs={{0,1},{1,0},{2,3},{3,2},{4,5},{5,4},{6,7},{7,6},{8,9},{9,8},{10,11... | collective-permute-start | bytes 393224 | tf_op jit(solution)/shard_map/ppermute | solution.py:176
  13.5 0.4 partial_sums.12
  13.9 0.5 %collective-permute-start.11 = (bf16[384,256]{1,0:T(8,128)(2,1)S(1)}, bf16[384,256]{1,0:T(8,128)(2,1)S(1)}, u32[]{:S(2)}, u32[]{:S(2)}) collective-permute-start(bf16[384,256]{1,0:T(8,128)(2,1)S(1)} %get-tuple-element.42), channel_id=1, source_target_pairs={{0,2},{1,3},{2,0},{3,1},{4,6},{5,7},{6,4},{7,5},{8,10},{9,11},{10,... | collective-permute-start | bytes 589832 | tf_op jit(solution)/shard_map/ppermute | solution.py:176
  14.4 0.5 %partial_sums.7 = (f32[256,512]{1,0:T(8,128)S(1)}, f32[256,512]{1,0:T(8,128)S(1)}) custom-call(bf16[256,4096]{1,0:T(8,128)(2,1)S(1)} %copy-done, bf16[256,4096]{1,0:T(8,128)(2,1)S(1)} %collective-permute-done.near_ref, bf16[272,512]{1,0:T(8,128)(2,1)S(1)} %front.1.v0_ref, bf16[272,512]{1,0:T(8,128)(2,1)S(1)} %collective-permute-done.1.v1_ref), custom_call_target="tpu_custom_call" | custom-call | tf_op jit(solution)/shard_map/partial_sums/pallas_call | solution.py:201
  14.9 0.0 collective-permute-done.2
  15.0 1.5 %collective-permute-start.6 = (bf16[128,512]{1,0:T(8,128)(2,1)S(1)}, bf16[128,512]{1,0:T(8,128)(2,1)S(1)}, u32[]{:S(2)}, u32[]{:S(2)}) collective-permute-start(bf16[128,512]{1,0:T(8,128)(2,1)S(1)} %add_convert_fusion.4), channel_id=1, source_target_pairs={{0,16},{1,17},{2,18},{3,19},{4,20},{5,21},{6,22},{7,23},{8,24},{9,... | collective-permute-start | bytes 393224 | tf_op jit(solution)/shard_map/ppermute | solution.py:176
  16.5 0.3 inner_swap.1
  16.9 0.5 %partial_sums.10 = (f32[512,256]{1,0:T(8,128)S(1)}, f32[512,256]{1,0:T(8,128)S(1)}) custom-call(bf16[256,4096]{1,0:T(8,128)(2,1)S(1)} %copy-done, bf16[256,4096]{1,0:T(8,128)(2,1)S(1)} %collective-permute-done.near_ref, bf16[272,512]{1,0:T(8,128)(2,1)S(1)} %front.1.v0_ref, bf16[272,512]{1,0:T(8,128)(2,1)S(1)} %collective-permute-done.1.v1_ref), custom_call_target="tpu_custom_call" | custom-call | tf_op jit(solution)/shard_map/partial_sums/pallas_call | solution.py:201
  17.4 0.6 %collective-permute-start.9 = (bf16[128,512]{1,0:T(8,128)(2,1)S(1)}, bf16[128,512]{1,0:T(8,128)(2,1)S(1)}, u32[]{:S(2)}, u32[]{:S(2)}) collective-permute-start(bf16[128,512]{1,0:T(8,128)(2,1)S(1)} %add_convert_fusion.2), channel_id=1, source_target_pairs={{0,1},{1,0},{2,3},{3,2},{4,5},{5,4},{6,7},{7,6},{8,9},{9,8},{10,11... | collective-permute-start | bytes 393224 | tf_op jit(solution)/shard_map/ppermute | solution.py:176
  18.0 0.3 partial_sums.13
  18.2 0.0 collective-permute-done.5
  18.3 1.6 %collective-permute-start.8 = (bf16[160,512]{1,0:T(8,128)(2,1)S(1)}, bf16[160,512]{1,0:T(8,128)(2,1)S(1)}, u32[]{:S(2)}, u32[]{:S(2)}) collective-permute-start(bf16[160,512]{1,0:T(8,128)(2,1)S(1)} %pad_maximum_fusion.2), channel_id=1, source_target_pairs={{0,16},{1,17},{2,18},{3,19},{4,20},{5,21},{6,22},{7,23},{8,24},{9,... | collective-permute-start | bytes 491528 | tf_op jit(solution)/shard_map/ppermute | solution.py:176
  19.8 0.5 %collective-permute-done.6 = bf16[128,512]{1,0:T(8,128)(2,1)S(1)} collective-permute-done((bf16[128,512]{1,0:T(8,128)(2,1)S(1)}, bf16[128,512]{1,0:T(8,128)(2,1)S(1)}, u32[]{:S(2)}, u32[]{:S(2)}) %collective-permute-start.6) | collective-permute-done | bytes 131104 | tf_op jit(solution)/shard_map/ppermute | solution.py:176
  20.4 1.6 %collective-permute-start.10 = (bf16[128,512]{1,0:T(8,128)(2,1)S(1)}, bf16[128,512]{1,0:T(8,128)(2,1)S(1)}, u32[]{:S(2)}, u32[]{:S(2)}) collective-permute-start(bf16[128,512]{1,0:T(8,128)(2,1)S(1)} %add_convert_fusion.3), channel_id=1, source_target_pairs={{0,2},{1,3},{2,0},{3,1},{4,6},{5,7},{6,4},{7,5},{8,10},{9,11},{10,... | collective-permute-start | bytes 393224 | tf_op jit(solution)/shard_map/ppermute | solution.py:176
  22.1 0.0 collective-permute-done.4
  22.1 1.1 %collective-permute-done.11 = bf16[384,256]{1,0:T(8,128)(2,1)S(1)} collective-permute-done((bf16[384,256]{1,0:T(8,128)(2,1)S(1)}, bf16[384,256]{1,0:T(8,128)(2,1)S(1)}, u32[]{:S(2)}, u32[]{:S(2)}) %collective-permute-start.11) | collective-permute-done | bytes 196640 | tf_op jit(solution)/shard_map/ppermute | solution.py:176
  23.3 0.7 %collective-permute-start.7 = (bf16[256,256]{1,0:T(8,128)(2,1)S(1)}, bf16[256,256]{1,0:T(8,128)(2,1)S(1)}, u32[]{:S(2)}, u32[]{:S(2)}) collective-permute-start(bf16[256,256]{1,0:T(8,128)(2,1)S(1)} %slice.106), channel_id=1, source_target_pairs={{0,16},{1,17},{2,18},{3,19},{4,20},{5,21},{6,22},{7,23},{8,24},{9,... | collective-permute-start | bytes 393224 | tf_op jit(solution)/shard_map/ppermute | solution.py:176
  24.1 0.3 collective-permute-start.12
  24.4 0.0 collective-permute-done.9
  24.4 1.1 %collective-permute-done.10 = bf16[128,512]{1,0:T(8,128)(2,1)S(1)} collective-permute-done((bf16[128,512]{1,0:T(8,128)(2,1)S(1)}, bf16[128,512]{1,0:T(8,128)(2,1)S(1)}, u32[]{:S(2)}, u32[]{:S(2)}) %collective-permute-start.10) | collective-permute-done | bytes 131104 | tf_op jit(solution)/shard_map/ppermute | solution.py:176
  25.5 0.1 add_convert_fusion.1
  25.5 2.6 %collective-permute-start.13 = (bf16[128,512]{1,0:T(8,128)(2,1)S(1)}, bf16[128,512]{1,0:T(8,128)(2,1)S(1)}, u32[]{:S(2)}, u32[]{:S(2)}) collective-permute-start(bf16[128,512]{1,0:T(8,128)(2,1)S(1)} %add_convert_fusion.1), channel_id=1, source_target_pairs={{0,4},{1,5},{2,6},{3,7},{4,0},{5,1},{6,2},{7,3},{8,12},{9,13},{10,... | collective-permute-start | bytes 393224 | tf_op jit(solution)/shard_map/ppermute | solution.py:176
  28.2 0.1 collective-permute-done.7
  28.3 1.5 %collective-permute-start.14 = (bf16[128,256]{1,0:T(8,128)(2,1)S(1)}, bf16[128,256]{1,0:T(8,128)(2,1)S(1)}, u32[]{:S(2)}, u32[]{:S(2)}) collective-permute-start(bf16[128,256]{1,0:T(8,128)(2,1)S(1)} %get-tuple-element.57), channel_id=1, source_target_pairs={{0,1},{1,0},{2,3},{3,2},{4,5},{5,4},{6,7},{7,6},{8,9},{9,8},{10,11... | collective-permute-start | bytes 196616 | tf_op jit(solution)/shard_map/ppermute | solution.py:176
  29.8 0.0 collective-permute-done.12
  29.8 1.4 %collective-permute-start.15 = (bf16[128,256]{1,0:T(8,128)(2,1)S(1)}, bf16[128,256]{1,0:T(8,128)(2,1)S(1)}, u32[]{:S(2)}, u32[]{:S(2)}) collective-permute-start(bf16[128,256]{1,0:T(8,128)(2,1)S(1)} %get-tuple-element.59), channel_id=1, source_target_pairs={{0,16},{1,17},{2,18},{3,19},{4,20},{5,21},{6,22},{7,23},{8,24},{9,... | collective-permute-start | bytes 196616 | tf_op jit(solution)/shard_map/ppermute | solution.py:176
  31.2 1.6 %collective-permute-start.16 = (bf16[128,512]{1,0:T(8,128)(2,1)S(1)}, bf16[128,512]{1,0:T(8,128)(2,1)S(1)}, u32[]{:S(2)}, u32[]{:S(2)}) collective-permute-start(bf16[128,512]{1,0:T(8,128)(2,1)S(1)} %partial_sums.13), channel_id=1, source_target_pairs={{0,2},{1,3},{2,0},{3,1},{4,6},{5,7},{6,4},{7,5},{8,10},{9,11},{10,... | collective-permute-start | bytes 393224 | tf_op jit(solution)/shard_map/ppermute | solution.py:176
  32.8 0.0 collective-permute-done.13.arrived_ref
  32.9 1.3 %collective-permute-done.15 = bf16[128,256]{1,0:T(8,128)(2,1)S(1)} collective-permute-done((bf16[128,256]{1,0:T(8,128)(2,1)S(1)}, bf16[128,256]{1,0:T(8,128)(2,1)S(1)}, u32[]{:S(2)}, u32[]{:S(2)}) %collective-permute-start.15) | collective-permute-done | bytes 65568 | tf_op jit(solution)/shard_map/ppermute | solution.py:176
  34.2 2.0 %collective-permute-done.16 = bf16[128,512]{1,0:T(8,128)(2,1)S(1)} collective-permute-done((bf16[128,512]{1,0:T(8,128)(2,1)S(1)}, bf16[128,512]{1,0:T(8,128)(2,1)S(1)}, u32[]{:S(2)}, u32[]{:S(2)}) %collective-permute-start.16) | collective-permute-done | bytes 131104 | tf_op jit(solution)/shard_map/ppermute | solution.py:176
  36.2 0.8 %collective-permute-start.17 = (bf16[128,512]{1,0:T(8,128)(2,1)S(1)}, bf16[128,512]{1,0:T(8,128)(2,1)S(1)}, u32[]{:S(2)}, u32[]{:S(2)}) collective-permute-start(bf16[128,512]{1,0:T(8,128)(2,1)S(1)} %add_convert_fusion), channel_id=1, source_target_pairs={{0,16},{1,17},{2,18},{3,19},{4,20},{5,21},{6,22},{7,23},{8,24},{9,... | collective-permute-start | bytes 393224 | tf_op jit(solution)/shard_map/ppermute | solution.py:176
  37.0 0.9 %outer_swap.1 = bf16[256,512]{1,0:T(8,128)(2,1)} custom-call(bf16[272,512]{1,0:T(8,128)(2,1)S(1)} %front.1.v0_ref, bf16[256,512]{1,0:T(8,128)(2,1)S(1)} %get-tuple-element.46.rows_ref, bf16[32,512]{1,0:T(8,128)(2,1)S(1)} %slice.85.window_ref), custom_call_target="tpu_custom_call" | custom-call | tf_op jit(solution)/shard_map/outer_swap/pallas_call | solution.py:265
  37.9 3.3 %collective-permute-done.17 = bf16[128,512]{1,0:T(8,128)(2,1)S(1)} collective-permute-done((bf16[128,512]{1,0:T(8,128)(2,1)S(1)}, bf16[128,512]{1,0:T(8,128)(2,1)S(1)}, u32[]{:S(2)}, u32[]{:S(2)}) %collective-permute-start.17) | collective-permute-done | bytes 131104 | tf_op jit(solution)/shard_map/ppermute | solution.py:176
  41.3 0.1 collective-permute-start.18
  41.4 0.8 %place.2.rest_0_ = f32[512,512]{1,0:T(8,128)} custom-call(bf16[2,128,512]{2,1,0:T(8,128)(2,1)S(1)} %pad_maximum_fusion.1.pair_ref), custom_call_target="tpu_custom_call" | custom-call | tf_op jit(solution)/shard_map/place/pallas_call | solution.py:289
  42.2 0.7 %collective-permute-done.18.pair_ref = bf16[2,128,512]{2,1,0:T(8,128)(2,1)S(1)} collective-permute-done((bf16[2,128,512]{2,1,0:T(8,128)(2,1)S(1)}, bf16[2,128,512]{2,1,0:T(8,128)(2,1)S(1)}, u32[]{:S(2)}, u32[]{:S(2)}) %collective-permute-start.18) | collective-permute-done | bytes 262176 | tf_op jit(solution)/shard_map/ppermute | solution.py:176
  42.9 0.8 %place.3 = f32[512,512]{1,0:T(8,128)} custom-call(bf16[2,128,512]{2,1,0:T(8,128)(2,1)S(1)} %collective-permute-done.18.pair_ref, f32[512,512]{1,0:T(8,128)} %place.2.rest_0_), custom_call_target="tpu_custom_call", output_to_operand_aliasing={{}: (1, {})} | custom-call | tf_op jit(solution)/shard_map/place/pallas_call | solution.py:289
  (21 shorter events, 0.4 us)
Async XLA Ops:
  0.6 5.6 %copy-start = (bf16[256,4096]{1,0:T(8,128)(2,1)S(1)}, bf16[256,4096]{1,0:T(8,128)(2,1)}, u32[]{:S(2)}) copy-start(bf16[256,4096]{1,0:T(8,128)(2,1)} %own_ref.13) | copy-start | bytes 6291460
  0.6 5.5 %collective-permute-start = (bf16[256,4096]{1,0:T(8,128)(2,1)}, bf16[256,4096]{1,0:T(8,128)(2,1)S(1)}, u32[]{:S(2)}, u32[]{:S(2)}) collective-permute-start(bf16[256,4096]{1,0:T(8,128)(2,1)} %own_ref.13), channel_id=1, source_target_pairs={{0,8},{1,9},{2,10},{3,11},{4,12},{5,13},{6,14},{7,15},{8,0},{9,1},... | collective-permute-start | bytes 6291464 | tf_op jit(solution)/shard_map/ppermute | solution.py:176
  4.6 1.6 %collective-permute-start.1 = (bf16[272,512]{1,0:T(8,128)(2,1)S(1)}, bf16[272,512]{1,0:T(8,128)(2,1)S(1)}, u32[]{:S(2)}, u32[]{:S(2)}) collective-permute-start(bf16[272,512]{1,0:T(8,128)(2,1)S(1)} %front.1.v0_ref), channel_id=1, source_target_pairs={{0,8},{1,9},{2,10},{3,11},{4,12},{5,13},{6,14},{7,15},{8,0},{9,1},... | collective-permute-start | bytes 835592 | tf_op jit(solution)/shard_map/ppermute | solution.py:176
  6.5 8.4 %collective-permute-start.2 = (bf16[128,512]{1,0:T(8,128)(2,1)S(1)}, bf16[128,512]{1,0:T(8,128)(2,1)S(1)}, u32[]{:S(2)}, u32[]{:S(2)}) collective-permute-start(bf16[128,512]{1,0:T(8,128)(2,1)S(1)} %partial_sums.8), channel_id=1, source_target_pairs={{0,1},{1,0},{2,3},{3,2},{4,5},{5,4},{6,7},{7,6},{8,9},{9,8},{10,11... | collective-permute-start | bytes 393224 | tf_op jit(solution)/shard_map/ppermute | solution.py:176
  9.3 5.6 %collective-permute-start.3 = (bf16[128,512]{1,0:T(8,128)(2,1)S(1)}, bf16[128,512]{1,0:T(8,128)(2,1)S(1)}, u32[]{:S(2)}, u32[]{:S(2)}) collective-permute-start(bf16[128,512]{1,0:T(8,128)(2,1)S(1)} %partial_sums.9), channel_id=1, source_target_pairs={{0,16},{1,17},{2,18},{3,19},{4,20},{5,21},{6,22},{7,23},{8,24},{9,... | collective-permute-start | bytes 393224 | tf_op jit(solution)/shard_map/ppermute | solution.py:176
  11.3 10.7 %collective-permute-start.4 = (bf16[384,256]{1,0:T(8,128)(2,1)S(1)}, bf16[384,256]{1,0:T(8,128)(2,1)S(1)}, u32[]{:S(2)}, u32[]{:S(2)}) collective-permute-start(bf16[384,256]{1,0:T(8,128)(2,1)S(1)} %get-tuple-element.31), channel_id=1, source_target_pairs={{0,2},{1,3},{2,0},{3,1},{4,6},{5,7},{6,4},{7,5},{8,10},{9,11},{10,... | collective-permute-start | bytes 589832 | tf_op jit(solution)/shard_map/ppermute | solution.py:176
  13.0 5.3 %collective-permute-start.5 = (bf16[128,512]{1,0:T(8,128)(2,1)S(1)}, bf16[128,512]{1,0:T(8,128)(2,1)S(1)}, u32[]{:S(2)}, u32[]{:S(2)}) collective-permute-start(bf16[128,512]{1,0:T(8,128)(2,1)S(1)} %get-tuple-element.32), channel_id=1, source_target_pairs={{0,1},{1,0},{2,3},{3,2},{4,5},{5,4},{6,7},{7,6},{8,9},{9,8},{10,11... | collective-permute-start | bytes 393224 | tf_op jit(solution)/shard_map/ppermute | solution.py:176
  13.9 9.4 %collective-permute-start.11 = (bf16[384,256]{1,0:T(8,128)(2,1)S(1)}, bf16[384,256]{1,0:T(8,128)(2,1)S(1)}, u32[]{:S(2)}, u32[]{:S(2)}) collective-permute-start(bf16[384,256]{1,0:T(8,128)(2,1)S(1)} %get-tuple-element.42), channel_id=1, source_target_pairs={{0,2},{1,3},{2,0},{3,1},{4,6},{5,7},{6,4},{7,5},{8,10},{9,11},{10,... | collective-permute-start | bytes 589832 | tf_op jit(solution)/shard_map/ppermute | solution.py:176
  15.0 5.4 %collective-permute-start.6 = (bf16[128,512]{1,0:T(8,128)(2,1)S(1)}, bf16[128,512]{1,0:T(8,128)(2,1)S(1)}, u32[]{:S(2)}, u32[]{:S(2)}) collective-permute-start(bf16[128,512]{1,0:T(8,128)(2,1)S(1)} %add_convert_fusion.4), channel_id=1, source_target_pairs={{0,16},{1,17},{2,18},{3,19},{4,20},{5,21},{6,22},{7,23},{8,24},{9,... | collective-permute-start | bytes 393224 | tf_op jit(solution)/shard_map/ppermute | solution.py:176
  17.4 7.0 %collective-permute-start.9 = (bf16[128,512]{1,0:T(8,128)(2,1)S(1)}, bf16[128,512]{1,0:T(8,128)(2,1)S(1)}, u32[]{:S(2)}, u32[]{:S(2)}) collective-permute-start(bf16[128,512]{1,0:T(8,128)(2,1)S(1)} %add_convert_fusion.2), channel_id=1, source_target_pairs={{0,1},{1,0},{2,3},{3,2},{4,5},{5,4},{6,7},{7,6},{8,9},{9,8},{10,11... | collective-permute-start | bytes 393224 | tf_op jit(solution)/shard_map/ppermute | solution.py:176
  18.3 6.1 %collective-permute-start.8 = (bf16[160,512]{1,0:T(8,128)(2,1)S(1)}, bf16[160,512]{1,0:T(8,128)(2,1)S(1)}, u32[]{:S(2)}, u32[]{:S(2)}) collective-permute-start(bf16[160,512]{1,0:T(8,128)(2,1)S(1)} %pad_maximum_fusion.2), channel_id=1, source_target_pairs={{0,16},{1,17},{2,18},{3,19},{4,20},{5,21},{6,22},{7,23},{8,24},{9,... | collective-permute-start | bytes 491528 | tf_op jit(solution)/shard_map/ppermute | solution.py:176
  20.4 5.0 %collective-permute-start.10 = (bf16[128,512]{1,0:T(8,128)(2,1)S(1)}, bf16[128,512]{1,0:T(8,128)(2,1)S(1)}, u32[]{:S(2)}, u32[]{:S(2)}) collective-permute-start(bf16[128,512]{1,0:T(8,128)(2,1)S(1)} %add_convert_fusion.3), channel_id=1, source_target_pairs={{0,2},{1,3},{2,0},{3,1},{4,6},{5,7},{6,4},{7,5},{8,10},{9,11},{10,... | collective-permute-start | bytes 393224 | tf_op jit(solution)/shard_map/ppermute | solution.py:176
  23.3 5.0 %collective-permute-start.7 = (bf16[256,256]{1,0:T(8,128)(2,1)S(1)}, bf16[256,256]{1,0:T(8,128)(2,1)S(1)}, u32[]{:S(2)}, u32[]{:S(2)}) collective-permute-start(bf16[256,256]{1,0:T(8,128)(2,1)S(1)} %slice.106), channel_id=1, source_target_pairs={{0,16},{1,17},{2,18},{3,19},{4,20},{5,21},{6,22},{7,23},{8,24},{9,... | collective-permute-start | bytes 393224 | tf_op jit(solution)/shard_map/ppermute | solution.py:176
  24.1 5.7 %collective-permute-start.12 = (bf16[256,256]{1,0:T(8,128)(2,1)S(1)}, bf16[256,256]{1,0:T(8,128)(2,1)S(1)}, u32[]{:S(2)}, u32[]{:S(2)}) collective-permute-start(bf16[256,256]{1,0:T(8,128)(2,1)S(1)} %pad_maximum_fusion.3), channel_id=1, source_target_pairs={{0,1},{1,0},{2,3},{3,2},{4,5},{5,4},{6,7},{7,6},{8,9},{9,8},{10,11... | collective-permute-start | bytes 393224 | tf_op jit(solution)/shard_map/ppermute | solution.py:176
  25.5 7.3 %collective-permute-start.13 = (bf16[128,512]{1,0:T(8,128)(2,1)S(1)}, bf16[128,512]{1,0:T(8,128)(2,1)S(1)}, u32[]{:S(2)}, u32[]{:S(2)}) collective-permute-start(bf16[128,512]{1,0:T(8,128)(2,1)S(1)} %add_convert_fusion.1), channel_id=1, source_target_pairs={{0,4},{1,5},{2,6},{3,7},{4,0},{5,1},{6,2},{7,3},{8,12},{9,13},{10,... | collective-permute-start | bytes 393224 | tf_op jit(solution)/shard_map/ppermute | solution.py:176
  28.3 4.6 %collective-permute-start.14 = (bf16[128,256]{1,0:T(8,128)(2,1)S(1)}, bf16[128,256]{1,0:T(8,128)(2,1)S(1)}, u32[]{:S(2)}, u32[]{:S(2)}) collective-permute-start(bf16[128,256]{1,0:T(8,128)(2,1)S(1)} %get-tuple-element.57), channel_id=1, source_target_pairs={{0,1},{1,0},{2,3},{3,2},{4,5},{5,4},{6,7},{7,6},{8,9},{9,8},{10,11... | collective-permute-start | bytes 196616 | tf_op jit(solution)/shard_map/ppermute | solution.py:176
  29.8 4.3 %collective-permute-start.15 = (bf16[128,256]{1,0:T(8,128)(2,1)S(1)}, bf16[128,256]{1,0:T(8,128)(2,1)S(1)}, u32[]{:S(2)}, u32[]{:S(2)}) collective-permute-start(bf16[128,256]{1,0:T(8,128)(2,1)S(1)} %get-tuple-element.59), channel_id=1, source_target_pairs={{0,16},{1,17},{2,18},{3,19},{4,20},{5,21},{6,22},{7,23},{8,24},{9,... | collective-permute-start | bytes 196616 | tf_op jit(solution)/shard_map/ppermute | solution.py:176
  31.2 5.0 %collective-permute-start.16 = (bf16[128,512]{1,0:T(8,128)(2,1)S(1)}, bf16[128,512]{1,0:T(8,128)(2,1)S(1)}, u32[]{:S(2)}, u32[]{:S(2)}) collective-permute-start(bf16[128,512]{1,0:T(8,128)(2,1)S(1)} %partial_sums.13), channel_id=1, source_target_pairs={{0,2},{1,3},{2,0},{3,1},{4,6},{5,7},{6,4},{7,5},{8,10},{9,11},{10,... | collective-permute-start | bytes 393224 | tf_op jit(solution)/shard_map/ppermute | solution.py:176
  36.2 5.0 %collective-permute-start.17 = (bf16[128,512]{1,0:T(8,128)(2,1)S(1)}, bf16[128,512]{1,0:T(8,128)(2,1)S(1)}, u32[]{:S(2)}, u32[]{:S(2)}) collective-permute-start(bf16[128,512]{1,0:T(8,128)(2,1)S(1)} %add_convert_fusion), channel_id=1, source_target_pairs={{0,16},{1,17},{2,18},{3,19},{4,20},{5,21},{6,22},{7,23},{8,24},{9,... | collective-permute-start | bytes 393224 | tf_op jit(solution)/shard_map/ppermute | solution.py:176
  41.3 1.6 %collective-permute-start.18 = (bf16[2,128,512]{2,1,0:T(8,128)(2,1)S(1)}, bf16[2,128,512]{2,1,0:T(8,128)(2,1)S(1)}, u32[]{:S(2)}, u32[]{:S(2)}) collective-permute-start(bf16[2,128,512]{2,1,0:T(8,128)(2,1)S(1)} %pad_maximum_fusion.1.pair_ref), channel_id=1, source_target_pairs={{0,8},{1,9},{2,10},{3,11},{4,12},{5,13},{6,14},{7,15},{8,0},{9,1},... | collective-permute-start | bytes 786440 | tf_op jit(solution)/shard_map/ppermute | solution.py:176
